TPU v7x, 32 devices: a whole 2x2x4 slice. The times are simulated.
32 devices in a mesh: loop: 4 (over x, core), rep: 8 (over z, y).
Axes of the slice: x: 2, y: 2, z: 4, core: 2. Of those that a mesh axis runs over, the one named last changes fastest.
Arguments:
- features: bfloat16 [768, 8, 1152], P('loop', 'rep'), may hold values from -6 to 6
- text: bfloat16 [768, 8, 1152], P('loop', 'rep'), may hold values from -6 to 6
- proj: bfloat16 [1152, 1152], replicated, may hold values from -0.1875 to 0.1875
- gain: float32 [1152], replicated, may hold values from 0.5 to 1.5
- scale: float32 [1], replicated, may hold values from 8 to 32
- bias: float32 [1], replicated, may hold values from -4 to 0
Outputs:
- feature_grad: bfloat16 [768, 8, 1152], P('loop', 'rep')
- text_grad: bfloat16 [768, 8, 1152], P('loop', 'rep')
- proj_grad: float32 [1152, 1152], P('rep')
- gain_gradient: float32 [1152], replicated
All inputs are finite; a program needn't handle non-finite values.
Results may differ from a plain program's by a relative error of at most 0.024.
Values may be sent and summed in bfloat16 or wider, within the bound.
No kernel may reach another device: no remote copies, remote signals or barrier semaphores. Data moves between devices by JAX's collectives and lax.ppermute only.
A program may use at most 64 MiB of HBM per device.

v0:
```python
import jax
import jax.numpy as jnp
from jax import lax
from jax.sharding import PartitionSpec as P


def passed_along(value, axis, steps):
    count = lax.axis_size(axis)
    pairs = [(source, (source + steps) % count) for source in range(count)]
    return lax.ppermute(value, axis, pairs)


def unit_rows(values):
    inverse = lax.rsqrt(jnp.sum(values * values, axis=-1, keepdims=True) + 1e-06)
    return (values * inverse, inverse)


def local(features, text, proj, gain, scale, bias):
    loop_count = lax.axis_size("loop")
    row_count = features.shape[0]
    group_row_set = row_count * loop_count
    logit_scale = scale[0]
    logit_bias = bias[0]
    contract_last = (((1,), (1,)), ((), ()))
    contract_first = (((0,), (0,)), ((), ()))
    xvalues = features[:, 0, :].astype(jnp.float32)
    row_mean = jnp.mean(xvalues, axis=-1, keepdims=True)
    mean_removed = xvalues - row_mean
    row_inverse_deviation = lax.rsqrt(
        jnp.mean(mean_removed * mean_removed, axis=-1, keepdims=True) + 1e-06
    )
    standardized_input = mean_removed * row_inverse_deviation
    normalized_rows = (standardized_input * gain).astype(jnp.bfloat16)
    projected = jnp.dot(normalized_rows, proj, preferred_element_type=jnp.float32)
    img_dir, img_inv = unit_rows(projected)
    img_unit = img_dir.astype(jnp.bfloat16)
    txt_dir, txt_inv = unit_rows(text[:, 0, :].astype(jnp.float32))
    txt_unit = txt_dir.astype(jnp.bfloat16)
    empty = jnp.zeros((row_count, txt_unit.shape[1]), jnp.float32)
    local_ids = jnp.arange(row_count, dtype=jnp.int32)
    diag_mask = (local_ids[:, None] == local_ids[None, :]).astype(jnp.float32)

    def visit_step(turn_index, carry):
        visitor, text_sums, img_back = carry
        logits = (
            logit_scale
            * lax.dot_general(img_unit, visitor, contract_last, preferred_element_type=jnp.float32)
            + logit_bias
        )
        own_turn = (turn_index == 0).astype(jnp.float32)
        pair_weight = (jax.nn.sigmoid(logits) - own_turn * diag_mask).astype(jnp.bfloat16)
        img_back = img_back + logit_scale * jnp.dot(
            pair_weight, visitor, preferred_element_type=jnp.float32
        )
        text_sums = text_sums + logit_scale * lax.dot_general(
            pair_weight, img_unit, contract_first, preferred_element_type=jnp.float32
        )
        visitor = passed_along(visitor, "loop", 1)
        text_sums = passed_along(text_sums.astype(jnp.bfloat16), "loop", 1).astype(text_sums.dtype)
        return (visitor, text_sums, img_back)

    final_state = lax.fori_loop(0, loop_count, visit_step, (txt_unit, empty, empty))
    txt_back = final_state[1]
    img_back = final_state[2]
    proj_back = (
        (img_back - img_dir * jnp.sum(img_dir * img_back, axis=-1, keepdims=True)) * img_inv
    ).astype(jnp.bfloat16)
    text_out = (
        (txt_back - txt_dir * jnp.sum(txt_dir * txt_back, axis=-1, keepdims=True)) * txt_inv
    ).astype(jnp.bfloat16)
    norm_backward = lax.dot_general(
        proj_back, proj, contract_last, preferred_element_type=jnp.float32
    )
    scaled_backward = norm_backward * gain
    feature_result = (
        row_inverse_deviation
        * (
            scaled_backward
            - jnp.mean(scaled_backward, axis=-1, keepdims=True)
            - standardized_input
            * jnp.mean(scaled_backward * standardized_input, axis=-1, keepdims=True)
        )
    ).astype(jnp.bfloat16)
    partial_grad = lax.dot_general(
        normalized_rows, proj_back, contract_first, preferred_element_type=jnp.float32
    ) * (1.0 / group_row_set)
    row_block = lax.psum_scatter(
        partial_grad.astype(jnp.bfloat16), "rep", scatter_dimension=0, tiled=True
    )
    proj_grad = lax.psum(row_block, "loop").astype(jnp.float32)
    gain_gradient = lax.psum(
        jnp.sum(norm_backward * standardized_input, axis=0) * (1.0 / group_row_set), ("loop", "rep")
    )
    return (feature_result[:, None, :], text_out[:, None, :], proj_grad, gain_gradient)


def solution(mesh):
    return jax.shard_map(
        local,
        mesh=mesh,
        in_specs=(P("loop", "rep", None), P("loop", "rep", None), P(), P(), P(), P()),
        out_specs=(P("loop", "rep", None), P("loop", "rep", None), P("rep", None), P()),
        check_vma=False,
    )
```

profile of v0, /device:TPU:0, one launch (start us, length us, event | category | flops | bytes accessed | tf_op | source)
XLA Modules:
  0.0 214.5 jit_solution(5242098839467740180)
XLA Ops:
  7.2 1.3 fusion.34
  8.6 1.2 convert_reduce_fusion
  9.8 1.3 fusion.29
  11.1 2.8 %multiply_reduce_fusion.1 = (f32[192]{0:T(256)S(1)}, f32[192,1152]{1,0:T(8,128)}) fusion(bf16[1152,1152]{1,0:T(8,128)(2,1)S(1)} %copy-done, bf16[192,1,1152]{2,0,1:T(8,128)(2,1)} %param.8, f32[1152]{0:T(1024)} %param.11, f32[192]{0:T(256)S(1)} %add_rsqrt_fusion.2, f32[192]{0:T(256)S(1)} %broadcast_multiply_fusion.3), kind=kOutput, calls=%fused_computation.45 | convolution fusion | flops 511156032 | bytes 3988224 | tf_op jit(solution)/shard_map/dot_general | solution.py:34
  13.9 2.1 fusion.15
  16.0 69.9 %while.18 = (s32[]{:T(128)}, bf16[192,1152]{1,0:T(8,128)(2,1)}, f32[192,1152]{1,0:T(8,128)}, f32[192,1152]{1,0:T(8,128)}, f32[]{:T(128)}, /*index=5*/bf16[192,11...) while((s32[]{:T(128)}, bf16[192,1152]{1,0:T(8,128)(2,1)}, f32[192,1152]{1,0:T(8,128)}, ...), condition=%wide.region_5.0_spmd.clone, body=%wide.region_4.0_spmd.clone.sunk | while | flops 256905216 | bytes 14672137 | solution.py:62
  16.0 1.1 copy.15
  17.1 1.6 fusion.65
  18.8 1.8 fusion.66
  21.0 2.6 %collective-permute-start = (bf16[192,1152]{1,0:T(8,128)(2,1)S(1)}, bf16[192,1152]{1,0:T(8,128)(2,1)}, u32[]{:S(2)}, u32[]{:S(2)}) collective-permute-start(bf16[192,1152]{1,0:T(8,128)(2,1)S(1)} %copy.15), channel_id=1, source_target_pairs={{0,8},{8,16},{16,24},{24,0},{1,9},{9,17},{17,25},{25,1},{2,10},{10... | collective-permute-start | bytes 1327112 | tf_op jit(solution)/shard_map/while/body/eval_jaxpr/ppermute | solution.py:10
  23.6 2.8 %fusion.67 = f32[192,1152]{1,0:T(8,128)} fusion(bf16[192,192]{1,0:T(8,128)(2,1)} %copy-done.3, bf16[192,1152]{1,0:T(8,128)(2,1)S(1)} %copy.15, f32[192,1152]{1,0:T(8,128)} %get-tuple-element.249, f32[]{:T(128)} %get-tuple-element.259, pred[]{:T(512)S(6)} %compare.3), kind=kOutput, calls=%fused_computation.2.clone.1 | convolution fusion | flops 85598208 | bytes 2285573 | tf_op jit(solution)/shard_map/while/body/eval_jaxpr/dot_general | solution.py:52
  26.4 2.9 %collective-permute-done.1 = bf16[192,1152]{1,0:T(8,128)(2,1)} collective-permute-done((bf16[192,1152]{1,0:T(8,128)(2,1)}, bf16[192,1152]{1,0:T(8,128)(2,1)}, u32[]{:S(2)}, u32[]{:S(2)}) %collective-permute-start.1) | collective-permute-done | bytes 442400 | tf_op jit(solution)/shard_map/while/body/eval_jaxpr/ppermute | solution.py:10
  29.2 2.0 convert_element_type.149
  31.2 2.7 %collective-permute-done = bf16[192,1152]{1,0:T(8,128)(2,1)} collective-permute-done((bf16[192,1152]{1,0:T(8,128)(2,1)S(1)}, bf16[192,1152]{1,0:T(8,128)(2,1)}, u32[]{:S(2)}, u32[]{:S(2)}) %collective-permute-start) | collective-permute-done | bytes 442400 | tf_op jit(solution)/shard_map/while/body/eval_jaxpr/ppermute | solution.py:10
  34.0 1.1 copy.15
  35.1 1.6 fusion.65
  36.7 1.8 fusion.66
  38.5 2.4 %collective-permute-start = (bf16[192,1152]{1,0:T(8,128)(2,1)S(1)}, bf16[192,1152]{1,0:T(8,128)(2,1)}, u32[]{:S(2)}, u32[]{:S(2)}) collective-permute-start(bf16[192,1152]{1,0:T(8,128)(2,1)S(1)} %copy.15), channel_id=1, source_target_pairs={{0,8},{8,16},{16,24},{24,0},{1,9},{9,17},{17,25},{25,1},{2,10},{10... | collective-permute-start | bytes 1327112 | tf_op jit(solution)/shard_map/while/body/eval_jaxpr/ppermute | solution.py:10
  40.9 3.1 %fusion.67 = f32[192,1152]{1,0:T(8,128)} fusion(bf16[192,192]{1,0:T(8,128)(2,1)} %copy-done.3, bf16[192,1152]{1,0:T(8,128)(2,1)S(1)} %copy.15, f32[192,1152]{1,0:T(8,128)} %get-tuple-element.249, f32[]{:T(128)} %get-tuple-element.259, pred[]{:T(512)S(6)} %compare.3), kind=kOutput, calls=%fused_computation.2.clone.1 | convolution fusion | flops 85598208 | bytes 2285573 | tf_op jit(solution)/shard_map/while/body/eval_jaxpr/dot_general | solution.py:52
  44.0 2.5 %collective-permute-done.1 = bf16[192,1152]{1,0:T(8,128)(2,1)} collective-permute-done((bf16[192,1152]{1,0:T(8,128)(2,1)}, bf16[192,1152]{1,0:T(8,128)(2,1)}, u32[]{:S(2)}, u32[]{:S(2)}) %collective-permute-start.1) | collective-permute-done | bytes 442400 | tf_op jit(solution)/shard_map/while/body/eval_jaxpr/ppermute | solution.py:10
  46.6 2.0 convert_element_type.149
  48.6 2.7 %collective-permute-done = bf16[192,1152]{1,0:T(8,128)(2,1)} collective-permute-done((bf16[192,1152]{1,0:T(8,128)(2,1)S(1)}, bf16[192,1152]{1,0:T(8,128)(2,1)}, u32[]{:S(2)}, u32[]{:S(2)}) %collective-permute-start) | collective-permute-done | bytes 442400 | tf_op jit(solution)/shard_map/while/body/eval_jaxpr/ppermute | solution.py:10
  51.3 1.1 copy.15
  52.4 1.6 fusion.65
  54.1 1.8 fusion.66
  55.8 2.4 %collective-permute-start = (bf16[192,1152]{1,0:T(8,128)(2,1)S(1)}, bf16[192,1152]{1,0:T(8,128)(2,1)}, u32[]{:S(2)}, u32[]{:S(2)}) collective-permute-start(bf16[192,1152]{1,0:T(8,128)(2,1)S(1)} %copy.15), channel_id=1, source_target_pairs={{0,8},{8,16},{16,24},{24,0},{1,9},{9,17},{17,25},{25,1},{2,10},{10... | collective-permute-start | bytes 1327112 | tf_op jit(solution)/shard_map/while/body/eval_jaxpr/ppermute | solution.py:10
  58.3 3.1 %fusion.67 = f32[192,1152]{1,0:T(8,128)} fusion(bf16[192,192]{1,0:T(8,128)(2,1)} %copy-done.3, bf16[192,1152]{1,0:T(8,128)(2,1)S(1)} %copy.15, f32[192,1152]{1,0:T(8,128)} %get-tuple-element.249, f32[]{:T(128)} %get-tuple-element.259, pred[]{:T(512)S(6)} %compare.3), kind=kOutput, calls=%fused_computation.2.clone.1 | convolution fusion | flops 85598208 | bytes 2285573 | tf_op jit(solution)/shard_map/while/body/eval_jaxpr/dot_general | solution.py:52
  61.4 2.5 %collective-permute-done.1 = bf16[192,1152]{1,0:T(8,128)(2,1)} collective-permute-done((bf16[192,1152]{1,0:T(8,128)(2,1)}, bf16[192,1152]{1,0:T(8,128)(2,1)}, u32[]{:S(2)}, u32[]{:S(2)}) %collective-permute-start.1) | collective-permute-done | bytes 442400 | tf_op jit(solution)/shard_map/while/body/eval_jaxpr/ppermute | solution.py:10
  63.9 2.0 convert_element_type.149
  65.9 2.7 %collective-permute-done = bf16[192,1152]{1,0:T(8,128)(2,1)} collective-permute-done((bf16[192,1152]{1,0:T(8,128)(2,1)S(1)}, bf16[192,1152]{1,0:T(8,128)(2,1)}, u32[]{:S(2)}, u32[]{:S(2)}) %collective-permute-start) | collective-permute-done | bytes 442400 | tf_op jit(solution)/shard_map/while/body/eval_jaxpr/ppermute | solution.py:10
  68.6 1.1 copy.15
  69.7 1.6 fusion.65
  71.4 1.8 fusion.66
  73.2 2.4 %collective-permute-start = (bf16[192,1152]{1,0:T(8,128)(2,1)S(1)}, bf16[192,1152]{1,0:T(8,128)(2,1)}, u32[]{:S(2)}, u32[]{:S(2)}) collective-permute-start(bf16[192,1152]{1,0:T(8,128)(2,1)S(1)} %copy.15), channel_id=1, source_target_pairs={{0,8},{8,16},{16,24},{24,0},{1,9},{9,17},{17,25},{25,1},{2,10},{10... | collective-permute-start | bytes 1327112 | tf_op jit(solution)/shard_map/while/body/eval_jaxpr/ppermute | solution.py:10
  75.6 3.1 %fusion.67 = f32[192,1152]{1,0:T(8,128)} fusion(bf16[192,192]{1,0:T(8,128)(2,1)} %copy-done.3, bf16[192,1152]{1,0:T(8,128)(2,1)S(1)} %copy.15, f32[192,1152]{1,0:T(8,128)} %get-tuple-element.249, f32[]{:T(128)} %get-tuple-element.259, pred[]{:T(512)S(6)} %compare.3), kind=kOutput, calls=%fused_computation.2.clone.1 | convolution fusion | flops 85598208 | bytes 2285573 | tf_op jit(solution)/shard_map/while/body/eval_jaxpr/dot_general | solution.py:52
  78.7 2.5 %collective-permute-done.1 = bf16[192,1152]{1,0:T(8,128)(2,1)} collective-permute-done((bf16[192,1152]{1,0:T(8,128)(2,1)}, bf16[192,1152]{1,0:T(8,128)(2,1)}, u32[]{:S(2)}, u32[]{:S(2)}) %collective-permute-start.1) | collective-permute-done | bytes 442400 | tf_op jit(solution)/shard_map/while/body/eval_jaxpr/ppermute | solution.py:10
  81.2 2.0 convert_element_type.149
  83.2 2.7 %collective-permute-done = bf16[192,1152]{1,0:T(8,128)(2,1)} collective-permute-done((bf16[192,1152]{1,0:T(8,128)(2,1)S(1)}, bf16[192,1152]{1,0:T(8,128)(2,1)}, u32[]{:S(2)}, u32[]{:S(2)}) %collective-permute-start) | collective-permute-done | bytes 442400 | tf_op jit(solution)/shard_map/while/body/eval_jaxpr/ppermute | solution.py:10
  86.0 1.7 multiply_reduce_fusion
  87.7 1.6 multiply_convert_fusion
  90.1 2.6 %fusion.12 = bf16[1152,1152]{1,0:T(8,128)(2,1)} fusion(bf16[192,1152]{1,0:T(8,128)(2,1)S(1)} %multiply_convert_fusion, bf16[192,1,1152]{2,0,1:T(8,128)(2,1)S(1)} %copy-done.6, f32[1152]{0:T(1024)S(1)} %copy-done.9, f32[192]{0:T(256)S(1)} %add_rsqrt_fusion.2, f32[192]{0:T(256)S(1)} %broadcast_multiply_fusion.3), kind=kOutput, calls=%fused_computation.16 | convolution fusion | flops 513368064 | bytes 3545088 | tf_op jit(solution)/shard_map/dot_general | solution.py:84
  92.8 1.3 fusion.30
  94.1 3.0 %fusion.28 = (f32[1152]{0:T(1024)}, f32[192]{0:T(256)S(1)}, f32[192]{0:T(256)S(1)}, f32[192,1152]{1,0:T(8,128)S(1)}) fusion(bf16[192,1,1152]{2,0,1:T(8,128)(2,1)} %param.8, f32[192]{0:T(256)S(1)} %add_rsqrt_fusion.2, f32[192]{0:T(256)S(1)} %broadcast_multiply_fusion.3, f32[1152]{0:T(1024)} %param.11, bf16[192,1152]{1,0:T(8,128)(2,1)} %copy-done.8, ...), kind=kOutput, calls=%fused_computation.36 | convolution fusion | flops 511597056 | bytes 4435968 | tf_op jit(solution)/shard_map/dot_general | solution.py:71
  97.1 1.0 fusion.35
  98.1 1.1 fusion.36
  99.2 66.2 %reduce-scatter.2.cloned.1.call-done = bf16[144,1152]{1,0:T(8,128)(2,1)} async-done(((bf16[1152,1152]{1,0:T(8,128)(2,1)}), bf16[144,1152]{1,0:T(8,128)(2,1)}) %reduce-scatter.2.cloned.1.call-update) | async-done | bytes 331792 | tf_op jit(solution)/shard_map/reduce_scatter | solution.py:87
  166.2 39.6 %psum.15 = f32[1152]{0:T(1024)} all-reduce(f32[1152]{0:T(1024)S(1)} %broadcast_multiply_fusion), channel_id=1, replica_groups=mesh['loop'=4,'rep'=8] {'loop','rep'}, use_global_device_ids=true, to_apply=%region_13.0 | all-reduce | flops 1152 | bytes 9216 | tf_op jit(solution)/shard_map/psum | solution.py:91
  205.8 1.9 convert_element_type.79
  (52 shorter events, 2.1 us)
Async XLA Ops:
  7.2 3.9 %copy-start = (bf16[1152,1152]{1,0:T(8,128)(2,1)S(1)}, bf16[1152,1152]{1,0:T(8,128)(2,1)}, u32[]{:S(2)}) copy-start(bf16[1152,1152]{1,0:T(8,128)(2,1)} %param.10) | copy-start | bytes 7962628
  7.2 158.3 %reduce-scatter.2.cloned.1.call-start = ((), (), s32[]{:S(2)}) async-start(), calls=%async_computation.1 | async-start | bytes 2985984 | tf_op jit(solution)/shard_map/reduce_scatter | solution.py:87
  11.0 2.9 %copy-start.4 = (bf16[192,1,1152]{2,0,1:T(8,128)(2,1)S(1)}, bf16[192,1,1152]{2,0,1:T(8,128)(2,1)}, u32[]{:S(2)}) copy-start(bf16[192,1,1152]{2,0,1:T(8,128)(2,1)} %param.9) | copy-start | bytes 1327108
  16.0 2.8 %copy-start.1 = (f32[192,1152]{1,0:T(8,128)S(1)}, f32[192,1152]{1,0:T(8,128)}, u32[]{:S(2)}) copy-start(f32[192,1152]{1,0:T(8,128)} %get-tuple-element.248) | copy-start | bytes 2654212 | tf_op jit(solution)/shard_map/while
  18.8 1.8 copy-start.3
  20.6 8.7 %collective-permute-start.1 = (bf16[192,1152]{1,0:T(8,128)(2,1)}, bf16[192,1152]{1,0:T(8,128)(2,1)}, u32[]{:S(2)}, u32[]{:S(2)}) collective-permute-start(bf16[192,1152]{1,0:T(8,128)(2,1)} %fusion.66), channel_id=1, source_target_pairs={{0,8},{8,16},{16,24},{24,0},{1,9},{9,17},{17,25},{25,1},{2,10},{10... | collective-permute-start | bytes 1327112 | tf_op jit(solution)/shard_map/while/body/eval_jaxpr/ppermute | solution.py:10
  21.0 13.0 %collective-permute-start = (bf16[192,1152]{1,0:T(8,128)(2,1)S(1)}, bf16[192,1152]{1,0:T(8,128)(2,1)}, u32[]{:S(2)}, u32[]{:S(2)}) collective-permute-start(bf16[192,1152]{1,0:T(8,128)(2,1)S(1)} %copy.15), channel_id=1, source_target_pairs={{0,8},{8,16},{16,24},{24,0},{1,9},{9,17},{17,25},{25,1},{2,10},{10... | collective-permute-start | bytes 1327112 | tf_op jit(solution)/shard_map/while/body/eval_jaxpr/ppermute | solution.py:10
  34.0 2.8 %copy-start.1 = (f32[192,1152]{1,0:T(8,128)S(1)}, f32[192,1152]{1,0:T(8,128)}, u32[]{:S(2)}) copy-start(f32[192,1152]{1,0:T(8,128)} %get-tuple-element.248) | copy-start | bytes 2654212 | tf_op jit(solution)/shard_map/while
  36.7 1.8 copy-start.3
  38.5 8.0 %collective-permute-start.1 = (bf16[192,1152]{1,0:T(8,128)(2,1)}, bf16[192,1152]{1,0:T(8,128)(2,1)}, u32[]{:S(2)}, u32[]{:S(2)}) collective-permute-start(bf16[192,1152]{1,0:T(8,128)(2,1)} %fusion.66), channel_id=1, source_target_pairs={{0,8},{8,16},{16,24},{24,0},{1,9},{9,17},{17,25},{25,1},{2,10},{10... | collective-permute-start | bytes 1327112 | tf_op jit(solution)/shard_map/while/body/eval_jaxpr/ppermute | solution.py:10
  38.5 12.8 %collective-permute-start = (bf16[192,1152]{1,0:T(8,128)(2,1)S(1)}, bf16[192,1152]{1,0:T(8,128)(2,1)}, u32[]{:S(2)}, u32[]{:S(2)}) collective-permute-start(bf16[192,1152]{1,0:T(8,128)(2,1)S(1)} %copy.15), channel_id=1, source_target_pairs={{0,8},{8,16},{16,24},{24,0},{1,9},{9,17},{17,25},{25,1},{2,10},{10... | collective-permute-start | bytes 1327112 | tf_op jit(solution)/shard_map/while/body/eval_jaxpr/ppermute | solution.py:10
  51.3 2.8 %copy-start.1 = (f32[192,1152]{1,0:T(8,128)S(1)}, f32[192,1152]{1,0:T(8,128)}, u32[]{:S(2)}) copy-start(f32[192,1152]{1,0:T(8,128)} %get-tuple-element.248) | copy-start | bytes 2654212 | tf_op jit(solution)/shard_map/while
  54.0 1.8 copy-start.3
  55.8 8.0 %collective-permute-start.1 = (bf16[192,1152]{1,0:T(8,128)(2,1)}, bf16[192,1152]{1,0:T(8,128)(2,1)}, u32[]{:S(2)}, u32[]{:S(2)}) collective-permute-start(bf16[192,1152]{1,0:T(8,128)(2,1)} %fusion.66), channel_id=1, source_target_pairs={{0,8},{8,16},{16,24},{24,0},{1,9},{9,17},{17,25},{25,1},{2,10},{10... | collective-permute-start | bytes 1327112 | tf_op jit(solution)/shard_map/while/body/eval_jaxpr/ppermute | solution.py:10
  55.8 12.8 %collective-permute-start = (bf16[192,1152]{1,0:T(8,128)(2,1)S(1)}, bf16[192,1152]{1,0:T(8,128)(2,1)}, u32[]{:S(2)}, u32[]{:S(2)}) collective-permute-start(bf16[192,1152]{1,0:T(8,128)(2,1)S(1)} %copy.15), channel_id=1, source_target_pairs={{0,8},{8,16},{16,24},{24,0},{1,9},{9,17},{17,25},{25,1},{2,10},{10... | collective-permute-start | bytes 1327112 | tf_op jit(solution)/shard_map/while/body/eval_jaxpr/ppermute | solution.py:10
  68.6 2.8 %copy-start.1 = (f32[192,1152]{1,0:T(8,128)S(1)}, f32[192,1152]{1,0:T(8,128)}, u32[]{:S(2)}) copy-start(f32[192,1152]{1,0:T(8,128)} %get-tuple-element.248) | copy-start | bytes 2654212 | tf_op jit(solution)/shard_map/while
  71.4 1.8 copy-start.3
  73.2 8.0 %collective-permute-start.1 = (bf16[192,1152]{1,0:T(8,128)(2,1)}, bf16[192,1152]{1,0:T(8,128)(2,1)}, u32[]{:S(2)}, u32[]{:S(2)}) collective-permute-start(bf16[192,1152]{1,0:T(8,128)(2,1)} %fusion.66), channel_id=1, source_target_pairs={{0,8},{8,16},{16,24},{24,0},{1,9},{9,17},{17,25},{25,1},{2,10},{10... | collective-permute-start | bytes 1327112 | tf_op jit(solution)/shard_map/while/body/eval_jaxpr/ppermute | solution.py:10
  73.2 12.8 %collective-permute-start = (bf16[192,1152]{1,0:T(8,128)(2,1)S(1)}, bf16[192,1152]{1,0:T(8,128)(2,1)}, u32[]{:S(2)}, u32[]{:S(2)}) collective-permute-start(bf16[192,1152]{1,0:T(8,128)(2,1)S(1)} %copy.15), channel_id=1, source_target_pairs={{0,8},{8,16},{16,24},{24,0},{1,9},{9,17},{17,25},{25,1},{2,10},{10... | collective-permute-start | bytes 1327112 | tf_op jit(solution)/shard_map/while/body/eval_jaxpr/ppermute | solution.py:10
  85.9 4.1 %copy-start.6 = (bf16[192,1,1152]{2,0,1:T(8,128)(2,1)S(1)}, bf16[192,1,1152]{2,0,1:T(8,128)(2,1)}, u32[]{:S(2)}) copy-start(bf16[192,1,1152]{2,0,1:T(8,128)(2,1)} %param.8) | copy-start | bytes 1327108
  85.9 4.1 %copy-start.9 = (f32[1152]{0:T(1024)S(1)}, f32[1152]{0:T(1024)}, u32[]{:S(2)}) copy-start(f32[1152]{0:T(1024)} %param.11) | copy-start | bytes 13828
  89.3 0.8 copy-start.8
  90.1 2.7 %copy-start.2 = (f32[192,1152]{1,0:T(8,128)S(1)}, f32[192,1152]{1,0:T(8,128)}, u32[]{:S(2)}) copy-start(f32[192,1152]{1,0:T(8,128)} %get-tuple-element.145) | copy-start | bytes 2654212
  92.7 113.0 %all-reduce.2.cloned.1.call-start = ((), (), s32[]{:S(2)}) async-start(), calls=%async_computation.2 | async-start | bytes 663552 | tf_op jit(solution)/shard_map/psum | solution.py:90
  94.1 3.1 %copy-start.5 = (bf16[192,1,1152]{2,0,1:T(8,128)(2,1)S(1)}, bf16[192,1,1152]{2,0,1:T(8,128)(2,1)}, u32[]{:S(2)}) copy-start(bf16[192,1,1152]{2,0,1:T(8,128)(2,1)} %param.9) | copy-start | bytes 1327108
  94.1 4.0 %copy-start.7 = (bf16[192,1,1152]{2,0,1:T(8,128)(2,1)S(1)}, bf16[192,1,1152]{2,0,1:T(8,128)(2,1)}, u32[]{:S(2)}) copy-start(bf16[192,1,1152]{2,0,1:T(8,128)(2,1)} %param.8) | copy-start | bytes 1327108
  94.1 4.0 %copy-start.10 = (f32[1152]{0:T(1024)S(1)}, f32[1152]{0:T(1024)}, u32[]{:S(2)}) copy-start(f32[1152]{0:T(1024)} %param.11) | copy-start | bytes 13828
Sparse Core Ops, SparseCore 0:
  92.9 72.5 reduce-scatter.1
  167.9 30.6 all-reduce.1
where the time goes:
time: 216 us; the launch traced here: 214 us
  waiting for transfers between devices  87.7 us (41%)
  blocking collectives  39.6 us (18%)
  matrix products  34.2 us (16%)
  other arithmetic  23.2 us (11%)
  between operations  14.1 us (7%)
  starting transfers between devices  10.4 us (5%)
  local copies, waits for them, and re-layouts  5.21 us (2%)
    reduce_scatter x1, waiting for transfers between devices, local(): lax.psum_scatter(partial_grad.astype(jnp.bfloat16), 'rep', scatter_dimens...  66.2 us
    psum x1, blocking collectives, local(): lax.psum(jnp.sum(norm_backward * standardized_input, axis=0) * (1.0 / gro...  39.6 us
    ppermute x8, waiting for transfers between devices, passed_along(): return lax.ppermute(value, axis, pairs)  21.4 us
    dot_general x4, matrix products, visit_step(): jnp.dot(pair_weight, visitor, preferred_element_type=jnp.float32)  12.1 us
    ppermute x8, starting transfers between devices, passed_along(): return lax.ppermute(value, axis, pairs)  10.3 us
    convert_element_type x4, other arithmetic, visit_step(): passed_along(text_sums.astype(jnp.bfloat16), 'loop', 1)  8 us
    dot_general x4, matrix products, visit_step(): lax.dot_general(pair_weight, img_unit, contract_first, preferred_element_...  7.09 us
    dot_general x4, matrix products, visit_step(): lax.dot_general(img_unit, visitor, contract_last, preferred_element_type=...  6.56 us
  transfers between devices with their start and end apart: 10, of which 9 were waited for; matrix products, arithmetic and copies ran while one was open for 13% of the time, Pallas kernels for 0%

commit v1 on v0

v1 whole, which is shorter than its diff:
```python
import jax
import jax.numpy as jnp
from jax import lax
from jax.sharding import PartitionSpec as P

F32 = jnp.float32
BF16 = jnp.bfloat16
LAST = (((1,), (1,)), ((), ()))
FIRST = (((0,), (0,)), ((), ()))


def dot(a, b, dims=(((1,), (0,)), ((), ()))):
    return lax.dot_general(a, b, dims, preferred_element_type=F32)


def unit_rows(values):
    inverse = lax.rsqrt(jnp.sum(values * values, axis=-1, keepdims=True) + 1e-06)
    return values * inverse, inverse


def standardize(rows):
    values = rows.astype(F32)
    centred = values - jnp.mean(values, axis=-1, keepdims=True)
    inverse = lax.rsqrt(jnp.mean(centred * centred, axis=-1, keepdims=True) + 1e-06)
    return centred * inverse, inverse


def send(value, axis, target):
    count = lax.axis_size(axis)
    return lax.ppermute(value, axis, [(p, target(p)) for p in range(count)])


def gather_group(value, count):
    mine = [value]
    for step in range(1, count // 2):
        mine.append(send(value, "loop", lambda p: (p + 2 * step) % count))
    mates = [send(block, "loop", lambda p: p ^ 1) for block in mine]
    return mine + mates


def local(features, text, proj, gain, scale, bias):
    n = lax.axis_size("loop")
    m = lax.axis_size("rep")
    me = lax.axis_index("loop")
    half = n // 2
    rows, width = features.shape[0], features.shape[2]
    columns = proj.shape[1] // n
    group_rows = rows * n
    logit_scale, logit_bias = scale[0], bias[0]

    own_features = features[:, 0, :]
    own_text = text[:, 0, :]
    text_blocks = gather_group(own_text, n)
    feature_blocks = gather_group(own_features, n)

    xhat, deviation = standardize(own_features)
    normed = (xhat * gain).astype(BF16)
    img_dir, img_inv = unit_rows(dot(normed, proj))
    img_unit = img_dir.astype(BF16)

    txt_dir, txt_inv = unit_rows(own_text.astype(F32))
    own_txt_unit = txt_dir.astype(BF16)
    txt_unit = jnp.concatenate(
        [own_txt_unit] + [unit_rows(block.astype(F32))[0].astype(BF16) for block in text_blocks[1:]]
    )
    row_ids = lax.broadcasted_iota(jnp.int32, (rows, group_rows), 0)
    column_ids = lax.broadcasted_iota(jnp.int32, (rows, group_rows), 1)
    diagonal = (row_ids == column_ids).astype(F32)

    def weights(left, right):
        logits = logit_scale * dot(left, right, LAST) + logit_bias
        return (jax.nn.sigmoid(logits) - diagonal).astype(BF16)

    img_back = logit_scale * dot(weights(img_unit, txt_unit), txt_unit)
    proj_back = (
        (img_back - img_dir * jnp.sum(img_dir * img_back, axis=-1, keepdims=True)) * img_inv
    ).astype(BF16)

    blocks = jnp.transpose(proj_back.reshape(rows, n, columns), (1, 0, 2))
    blocks = lax.all_to_all(blocks, "loop", 0, 0, tiled=True)
    back_columns = blocks.reshape(group_rows, columns)

    norm_back = dot(proj_back, proj, LAST)
    scaled = norm_back * gain
    feature_grad = (
        deviation
        * (
            scaled
            - jnp.mean(scaled, axis=-1, keepdims=True)
            - xhat * jnp.mean(scaled * xhat, axis=-1, keepdims=True)
        )
    ).astype(BF16)
    gain_term = jnp.sum(norm_back * xhat, axis=0) * (1.0 / group_rows)

    other_normed = [(standardize(block)[0] * gain).astype(BF16) for block in feature_blocks[1:]]
    relative = jnp.stack([normed] + other_normed)
    member = jnp.arange(n)
    same_core = (member % 2) == (me % 2)
    chips_back = ((me // 2 - member // 2) % half)
    position = jnp.where(same_core, chips_back, half + chips_back)
    group_normed = relative[position].reshape(group_rows, width)

    partial = (dot(group_normed, back_columns, FIRST) * (1.0 / group_rows)).astype(BF16)
    pieces = lax.all_to_all(partial.reshape(m, width // m, columns), "rep", 0, 0, tiled=True)
    reduced = jnp.sum(pieces.astype(F32), axis=0).astype(BF16)
    gains = lax.all_gather(gain_term, "rep")
    gain_sum = jnp.sum(gains, axis=0)
    proj_rows = lax.all_gather(reduced, "loop")
    proj_grad = jnp.transpose(proj_rows, (1, 0, 2)).reshape(width // m, n * columns).astype(F32)
    gain_gradient = jnp.sum(lax.all_gather(gain_sum, "loop"), axis=0)

    group_unit = jnp.concatenate(
        [img_unit] + [unit_rows(dot(block, proj))[0].astype(BF16) for block in other_normed]
    )
    text_weights = weights(own_txt_unit, group_unit)
    txt_back = logit_scale * dot(text_weights, group_unit)
    text_grad = (
        (txt_back - txt_dir * jnp.sum(txt_dir * txt_back, axis=-1, keepdims=True)) * txt_inv
    ).astype(BF16)
    return feature_grad[:, None, :], text_grad[:, None, :], proj_grad, gain_gradient


def solution(mesh):
    return jax.shard_map(
        local,
        mesh=mesh,
        in_specs=(P("loop", "rep", None), P("loop", "rep", None), P(), P(), P(), P()),
        out_specs=(P("loop", "rep", None), P("loop", "rep", None), P("rep", None), P()),
        check_vma=False,
    )
```

time: 216 us -> 157 us (0.73)
  waiting for transfers between devices: 87.7 us -> 4.42 us
  other arithmetic: 23.2 us -> 43.1 us
  blocking collectives: 39.6 us -> 56.1 us
  between operations: 14.1 us -> 2.27 us
  matrix products: 34.2 us -> 26 us
  local copies, waits for them, and re-layouts: 5.21 us -> 9.66 us
  starting transfers between devices: 10.4 us -> 14.5 us
    reduce_scatter x1 -> x0, waiting for transfers between devices: 66.2 us -> none  [local(): lax.psum_scatter(partial_grad.astype(jnp.bfloat16), 'rep', scatter_dimens...]
    all_gather x0 -> x3, blocking collectives: none -> 56.1 us  [the longest x1 43.6 us: local(): gains = lax.all_gather(gain_term, 'rep')]
    psum x1 -> x0, blocking collectives: 39.6 us -> none  [local(): lax.psum(jnp.sum(norm_backward * standardized_input, axis=0) * (1.0 / gro...]
    ppermute x8 -> x6, waiting for transfers between devices: 21.4 us -> 4.41 us  [send(): return lax.ppermute(value, axis, [(p, target(p)) for p in range(count)])]
    all_to_all x0 -> x2, starting transfers between devices: none -> 10.4 us  [the longest x1 6.09 us: local(): lax.all_to_all(partial.reshape(m, width // m, columns), 'rep', 0, 0, tile...]
    dot_general x15 -> x8, matrix products: 34.2 us -> 26 us  [dot(): return lax.dot_general(a, b, dims, preferred_element_type=F32)]
    ppermute x8 -> x6, starting transfers between devices: 10.3 us -> 4.03 us  [send(): return lax.ppermute(value, axis, [(p, target(p)) for p in range(count)])]
    reduce_sum x4 -> x11, other arithmetic: 5.43 us -> 11.1 us  [the longest x4 4.09 us: standardize(): jnp.mean(centred * centred, axis=-1, keepdims=True) + 1e-06]
  transfers between devices with their start and end apart: 10 -> 8, of which waited for: 9 -> 1; matrix products, arithmetic and copies ran while one was open for 13% -> 37% of each run, Pallas kernels for 0% -> 0%
where the time goes in v1:
time: 157 us; the launch traced here: 156 us
  blocking collectives  56.1 us (36%)
  other arithmetic  43.1 us (27%)
  matrix products  26 us (17%)
  starting transfers between devices  14.5 us (9%)
  local copies, waits for them, and re-layouts  9.66 us (6%)
  waiting for transfers between devices  4.42 us (3%)
  between operations  2.27 us (1%)
    all_gather x1, blocking collectives, local(): gains = lax.all_gather(gain_term, 'rep')  43.6 us
    dot_general x8, matrix products, dot(): return lax.dot_general(a, b, dims, preferred_element_type=F32)  26 us
    all_gather x1, blocking collectives, local(): proj_rows = lax.all_gather(reduced, 'loop')  6.89 us
    all_to_all x1, starting transfers between devices, local(): lax.all_to_all(partial.reshape(m, width // m, columns), 'rep', 0, 0, tile...  6.09 us
    all_gather x1, blocking collectives, local(): gain_gradient = jnp.sum(lax.all_gather(gain_sum, 'loop'), axis=0)  5.63 us
    convert_element_type x3, other arithmetic, local(): unit_rows(block.astype(F32))[0].astype(BF16)  4.75 us
    ppermute x6, waiting for transfers between devices, send(): return lax.ppermute(value, axis, [(p, target(p)) for p in range(count)])  4.41 us
    all_to_all x1, starting transfers between devices, local(): blocks = lax.all_to_all(blocks, 'loop', 0, 0, tiled=True)  4.34 us
  transfers between devices with their start and end apart: 8, of which 1 were waited for; matrix products, arithmetic and copies ran while one was open for 37% of the time, Pallas kernels for 0%

profile of v1, /device:TPU:0, one launch (start us, length us, event | category | flops | bytes accessed | tf_op | source)
XLA Modules:
  0.0 156.0 jit_solution(11413241146217281103)
XLA Ops:
  0.6 3.0 %collective-permute-start = (bf16[192,1152]{1,0:T(8,128)(2,1)}, bf16[192,1152]{1,0:T(8,128)(2,1)}, u32[]{:S(2)}, u32[]{:S(2)}) collective-permute-start(bf16[192,1152]{1,0:T(8,128)(2,1)} %bitcast.64), channel_id=1, source_target_pairs={{0,16},{8,24},{16,0},{24,8},{1,17},{9,25},{17,1},{25,9},{2,18},{10... | collective-permute-start | bytes 1327112 | tf_op jit(solution)/shard_map/ppermute | solution.py:30
  4.2 1.2 convert_reduce_fusion.3
  5.3 1.7 %fusion.51 = f32[192]{0:T(256)} fusion(bf16[192,1,1152]{2,0,1:T(8,128)(2,1)} %param.7), kind=kLoop, calls=%fused_computation.76 | loop fusion | flops 663360 | bytes 443136 | tf_op jit(solution)/shard_map/reduce_sum | solution.py:17
  7.1 1.3 fusion.46
  8.4 2.9 %multiply_reduce_fusion.4 = (f32[192]{0:T(256)S(1)}, f32[192,1152]{1,0:T(8,128)}) fusion(bf16[1152,1152]{1,0:T(8,128)(2,1)S(1)} %copy-done, f32[1152]{0:T(1024)} %param.9, f32[192]{0:T(256)S(1)} %add_rsqrt_fusion.11, f32[192]{0:T(256)S(1)} %broadcast_multiply_fusion.6, bf16[192,1,1152]{2,0,1:T(8,128)(2,1)} %param.6), kind=kOutput, calls=%fused_computation.96 | convolution fusion | flops 511156032 | bytes 3988224 | tf_op jit(solution)/shard_map/dot_general | solution.py:13
  11.9 0.6 add_rsqrt_fusion.9
  13.8 0.6 pad_clamp_fusion
  14.4 2.4 %fusion.18 = (bf16[192,1152]{1,0:T(8,128)(2,1)}, bf16[192,1152]{1,0:T(8,128)(2,1)}) fusion(f32[192]{0:T(256)} %add_rsqrt_fusion.9, bf16[192,1,1152]{2,0,1:T(8,128)(2,1)} %param.7, f32[192,1152]{1,0:T(8,128)} %get-tuple-element.14, f32[192]{0:T(256)} %add_rsqrt_fusion.10), kind=kLoop, calls=%fused_computation.41 | loop fusion | flops 1105920 | bytes 2213376 | tf_op jit(solution)/shard_map/convert_element_type | solution.py:62
  16.9 1.1 fusion.60
  17.9 1.2 fusion.54
  19.1 4.4 %collective-permute-done.3 = bf16[192,1152]{1,0:T(8,128)(2,1)S(1)} collective-permute-done((bf16[192,1152]{1,0:T(8,128)(2,1)}, bf16[192,1152]{1,0:T(8,128)(2,1)S(1)}, u32[]{:S(2)}, u32[]{:S(2)}) %collective-permute-start.3) | collective-permute-done | bytes 442400 | tf_op jit(solution)/shard_map/ppermute | solution.py:30
  23.7 1.2 fusion.52
  25.2 1.2 convert_reduce_fusion.1
  26.3 1.3 fusion.34
  27.6 2.8 %multiply_reduce_fusion.1 = (f32[192]{0:T(256)S(1)}, f32[192,1152]{1,0:T(8,128)}) fusion(bf16[1152,1152]{1,0:T(8,128)(2,1)S(1)} %copy-done, bf16[192,1152]{1,0:T(8,128)(2,1)} %collective-permute-done.4, f32[192]{0:T(256)S(1)} %add_rsqrt_fusion.3, f32[192]{0:T(256)S(1)} %broadcast_multiply_fusion.2, f32[1152]{0:T(1024)S(1)} %copy-done.5), kind=kOutput, calls=%fused_computation.91 | convolution fusion | flops 511156032 | bytes 3988224 | tf_op jit(solution)/shard_map/dot_general | solution.py:13
  30.5 1.0 multiply_reduce_fusion.2
  31.5 0.9 multiply_convert_fusion.2
  32.9 1.9 %fusion.55 = bf16[192,1152]{1,0:T(8,128)(2,1)} fusion(bf16[192,1152]{1,0:T(8,128)(2,1)} %collective-permute-done.1, f32[192]{0:T(256)S(1)} %add_rsqrt_fusion.7), kind=kLoop, calls=%fused_computation.80 | loop fusion | flops 663552 | bytes 885504 | tf_op jit(solution)/shard_map/convert_element_type | solution.py:64
  34.8 1.9 %fusion.53 = bf16[192,1152]{1,0:T(8,128)(2,1)} fusion(bf16[192,1152]{1,0:T(8,128)(2,1)} %collective-permute-done, f32[192]{0:T(256)S(1)} %add_rsqrt_fusion.8), kind=kLoop, calls=%fused_computation.78 | loop fusion | flops 663552 | bytes 885504 | tf_op jit(solution)/shard_map/convert_element_type | solution.py:64
  36.9 0.9 fusion.57
  37.8 5.3 %multiply_reduce_fusion.3 = (f32[192]{0:T(256)}, f32[192,1152]{1,0:T(8,128)}) fusion(f32[192,1152]{1,0:T(8,128)} %get-tuple-element.14, f32[192]{0:T(256)S(1)} %copy-done.9, bf16[192,1152]{1,0:T(8,128)(2,1)} %fusion.57, bf16[192,1152]{1,0:T(8,128)(2,1)} %fusion.55, bf16[192,1152]{1,0:T(8,128)(2,1)} %fusion.53, bf16[192,1152]{1,0:T(8,128)(2,1)} %get-tuple-element.25, ...), kind=kOutput, calls=%fused_computation.95 | convolution fusion | flops 695844672 | bytes 3982856 | tf_op jit(solution)/shard_map/dot_general | solution.py:13
  43.1 2.4 %multiply_convert_fusion.3 = bf16[192,1152]{1,0:T(8,128)(2,1)} fusion(f32[192,1152]{1,0:T(8,128)} %get-tuple-element.16, f32[192,1152]{1,0:T(8,128)} %get-tuple-element.14, f32[192]{0:T(256)} %get-tuple-element.15, f32[192]{0:T(256)S(1)} %copy-done.9), kind=kLoop, calls=%fused_computation.94 | loop fusion | flops 1105920 | bytes 2213376 | tf_op jit(solution)/shard_map/convert_element_type | solution.py:77
  45.5 2.1 %copy.19 = bf16[192,1152]{0,1:T(8,128)(2,1)} copy(bf16[192,1152]{1,0:T(8,128)(2,1)} %multiply_convert_fusion.3) | data formatting | bytes 884736 | tf_op jit(solution)/shard_map/reshape | solution.py:79
  47.6 3.0 %fusion.95 = f32[192,1152]{1,0:T(8,128)} fusion(bf16[192,1152]{1,0:T(8,128)(2,1)} %multiply_convert_fusion.3, bf16[1152,1152]{1,0:T(8,128)(2,1)S(1)} %copy-done), kind=kOutput, calls=%fused_computation.157 | convolution fusion | flops 509607936 | bytes 3981312 | tf_op jit(solution)/shard_map/dot_general | solution.py:13
  50.5 1.2 convert_reduce_fusion
  51.7 1.3 fusion.31
  53.0 2.8 %multiply_reduce_fusion = (f32[192]{0:T(256)S(1)}, f32[192,1152]{1,0:T(8,128)}) fusion(bf16[1152,1152]{1,0:T(8,128)(2,1)S(1)} %copy-done, bf16[192,1152]{1,0:T(8,128)(2,1)} %collective-permute-done.5, f32[192]{0:T(256)S(1)} %add_rsqrt_fusion.1, f32[192]{0:T(256)S(1)} %broadcast_multiply_fusion.1, f32[1152]{0:T(1024)S(1)} %copy-done.5), kind=kOutput, calls=%fused_computation.89 | convolution fusion | flops 511156032 | bytes 3988224 | tf_op jit(solution)/shard_map/dot_general | solution.py:13
  55.8 4.3 %all-to-all-start = ((bf16[4,192,288]{1,2,0:T(8,128)(2,1)}), bf16[4,192,288]{1,2,0:T(8,128)(2,1)}, u32[]{:S(2)}, u32[]{:S(2)}) async-start(bf16[4,192,288]{1,2,0:T(8,128)(2,1)} %bitcast.67), calls=%async_computation | async-start | bytes 1179648 | tf_op jit(solution)/shard_map/all_to_all | solution.py:80
  60.2 2.6 %multiply_convert_fusion = (bf16[192,1152]{1,0:T(8,128)(2,1)}, bf16[192,1152]{1,0:T(8,128)(2,1)}) fusion(f32[192,1152]{1,0:T(8,128)} %get-tuple-element.18, f32[192]{0:T(256)S(1)} %add_rsqrt_fusion, f32[192,1152]{1,0:T(8,128)} %get-tuple-element.20, f32[192]{0:T(256)S(1)} %add_rsqrt_fusion.2), kind=kLoop, calls=%fused_computation.88 | loop fusion | flops 884736 | bytes 2655744 | tf_op jit(solution)/shard_map/convert_element_type | solution.py:113
  62.8 2.7 %fusion.86 = (bf16[1,192,1152]{2,1,0:T(8,128)(2,1)S(1)}, bf16[1,192,1152]{2,1,0:T(8,128)(2,1)S(1)}, bf16[1,192,1152]{2,1,0:T(8,128)(2,1)S(1)}, f32[192]{0:T(256)}, f32[192]{0:T(256)}, /*index=5*/f32[1152]{0:T(1024)S(1)}) fusion(f32[1152]{0:T(1024)S(1)} %copy-done.5, f32[192]{0:T(256)} %copy-done.14, f32[192]{0:T(256)} %copy-done.10, ...), kind=kLoop, calls=%fused_computation.151 | loop fusion | flops 5306880 | bytes 3998208 | tf_op jit(solution)/shard_map/stack | solution.py:96
  65.5 1.5 pad_maximum_fusion.2
  67.0 5.0 %fusion.47 = (f32[192]{0:T(256)}, f32[192,1152]{1,0:T(8,128)}) fusion(f32[192]{0:T(256)} %add_rsqrt_fusion.9, bf16[192,1,1152]{2,0,1:T(8,128)(2,1)S(1)} %copy-done.3, bf16[192,1152]{1,0:T(8,128)(2,1)} %get-tuple-element.27, bf16[192,1152]{1,0:T(8,128)(2,1)} %get-tuple-element.28, bf16[192,1152]{1,0:T(8,128)(2,1)} %multiply_convert_fusion.2, ...), kind=kOutput, calls=%fused_computation.72 | convolution fusion | flops 696065856 | bytes 3540488 | tf_op jit(solution)/shard_map/dot_general | solution.py:13
  72.0 1.2 broadcast_multiply_fusion.4
  73.2 3.5 %gather_fusion = bf16[4,192,1152]{2,1,0:T(8,128)(2,1)} fusion(bf16[4,192,1152]{2,1,0:T(8,128)(2,1)} %pad_maximum_fusion.2, s32[1024]{0:T(1024)} %pad_clamp_fusion), kind=kCustom, calls=%fused_computation | custom fusion | bytes 3538960 | tf_op jit(solution)/shard_map/gather | solution.py:101
  76.8 0.6 broadcast_multiply_fusion
  77.4 3.3 %fusion.1 = bf16[1152,288]{0,1:T(8,128)(2,1)} fusion(bf16[4,192,288]{1,2,0:T(8,128)(2,1)} %all-to-all-done, bf16[4,192,1152]{2,1,0:T(8,128)(2,1)} %gather_fusion), kind=kOutput, calls=%fused_computation.5 | convolution fusion | flops 510271488 | bytes 2875392 | tf_op jit(solution)/shard_map/dot_general | solution.py:13
  80.7 2.4 %copy.17 = bf16[1152,288]{1,0:T(8,128)(2,1)} copy(bf16[1152,288]{0,1:T(8,128)(2,1)} %fusion.1) | data formatting | bytes 1327104 | tf_op jit(solution)/shard_map/convert_element_type | solution.py:103
  83.0 6.1 %all-to-all-start.1 = ((bf16[8,144,288]{2,1,0:T(8,128)(2,1)}), bf16[8,144,288]{2,1,0:T(8,128)(2,1)}, u32[]{:S(2)}, u32[]{:S(2)}) async-start(bf16[8,144,288]{2,1,0:T(8,128)(2,1)} %bitcast.66), calls=%async_computation.1 | async-start | bytes 1769472 | tf_op jit(solution)/shard_map/all_to_all | solution.py:104
  89.1 1.2 broadcast_multiply_fusion.5
  90.3 43.6 %all-gather.3 = f32[8,1,1152]{2,1,0:T(1,128)} all-gather(f32[1,1,1152]{2,1,0:T(1,128)S(1)} %reshape.336), channel_id=3, replica_groups=mesh['loop'=4,'rep'=8] {'rep'}, dimensions={0}, use_global_device_ids=true | all-gather | bytes 41472 | tf_op jit(solution)/shard_map/all_gather | solution.py:106
  133.9 0.8 reduce_sum.241
  134.7 5.6 %all-gather.4 = f32[4,1,1152]{2,1,0:T(1,128)} all-gather(f32[1,1,1152]{2,1,0:T(1,128)S(1)} %reshape.338), channel_id=4, replica_groups=mesh['loop'=4,'rep'=8] {'loop'}, dimensions={0}, use_global_device_ids=true | all-gather | bytes 23040 | tf_op jit(solution)/shard_map/all_gather | solution.py:110
  140.3 1.3 reduce_sum.242
  141.7 2.2 %fusion.63 = bf16[192,1,1152]{2,0,1:T(8,128)(2,1)} fusion(f32[192,1152]{1,0:T(8,128)} %get-tuple-element.24, f32[192]{0:T(256)} %get-tuple-element.23, f32[192]{0:T(256)} %add_rsqrt_fusion.9, bf16[192,1,1152]{2,0,1:T(8,128)(2,1)S(1)} %copy-done.3), kind=kLoop, calls=%fused_computation.102 | loop fusion | flops 1327104 | bytes 1771008 | tf_op jit(solution)/shard_map/broadcast_in_dim | solution.py:120
  143.8 2.3 %fusion.64 = bf16[192,1,1152]{2,0,1:T(8,128)(2,1)} fusion(f32[192,1152]{1,0:T(8,128)} %fusion.95, f32[192]{0:T(256)} %broadcast_multiply_fusion.4, f32[192]{0:T(256)} %broadcast_multiply_fusion.5, f32[1152]{0:T(1024)S(1)} %copy-done.5, f32[192]{0:T(256)} %copy-done.8, f32[192]{0:T(256)} %copy-done.7, bf16[192,1,1152]{2,0,1:T(8,128)(2,1)S(1)} %copy-done.1), kind=kLoop, calls=%fused_computation.103 | loop fusion | flops 1990656 | bytes 1777152 | tf_op jit(solution)/shard_map/broadcast_in_dim | solution.py:120
  146.1 1.3 reduce_sum.239
  147.4 6.9 %all-gather = bf16[576,288]{1,0:T(8,128)(2,1)S(1)} all-gather(bf16[144,288]{1,0:T(8,128)(2,1)S(1)} %reduce_sum.239), channel_id=2, replica_groups=mesh['loop'=4,'rep'=8] {'loop'}, dimensions={0}, use_global_device_ids=true | all-gather | bytes 414720 | tf_op jit(solution)/shard_map/all_gather | solution.py:108
  154.7 1.3 reshape.323
  (73 shorter events, 2.8 us)
Async XLA Ops:
  0.6 7.7 %copy-start = (bf16[1152,1152]{1,0:T(8,128)(2,1)S(1)}, bf16[1152,1152]{1,0:T(8,128)(2,1)}, u32[]{:S(2)}) copy-start(bf16[1152,1152]{1,0:T(8,128)(2,1)} %param.8) | copy-start | bytes 7962628
  0.6 23.0 %collective-permute-start = (bf16[192,1152]{1,0:T(8,128)(2,1)}, bf16[192,1152]{1,0:T(8,128)(2,1)}, u32[]{:S(2)}, u32[]{:S(2)}) collective-permute-start(bf16[192,1152]{1,0:T(8,128)(2,1)} %bitcast.64), channel_id=1, source_target_pairs={{0,16},{8,24},{16,0},{24,8},{1,17},{9,25},{17,1},{25,9},{2,18},{10... | collective-permute-start | bytes 1327112 | tf_op jit(solution)/shard_map/ppermute | solution.py:30
  3.6 14.3 %collective-permute-start.1 = (bf16[192,1152]{1,0:T(8,128)(2,1)}, bf16[192,1152]{1,0:T(8,128)(2,1)}, u32[]{:S(2)}, u32[]{:S(2)}) collective-permute-start(bf16[192,1152]{1,0:T(8,128)(2,1)} %bitcast.65), channel_id=1, source_target_pairs={{0,8},{8,0},{16,24},{24,16},{1,9},{9,1},{17,25},{25,17},{2,10},{10... | collective-permute-start | bytes 1327112 | tf_op jit(solution)/shard_map/ppermute | solution.py:30
  3.7 19.9 %collective-permute-start.3 = (bf16[192,1152]{1,0:T(8,128)(2,1)}, bf16[192,1152]{1,0:T(8,128)(2,1)S(1)}, u32[]{:S(2)}, u32[]{:S(2)}) collective-permute-start(bf16[192,1152]{1,0:T(8,128)(2,1)} %bitcast.62), channel_id=1, source_target_pairs={{0,16},{8,24},{16,0},{24,8},{1,17},{9,25},{17,1},{25,9},{2,18},{10... | collective-permute-start | bytes 1327112 | tf_op jit(solution)/shard_map/ppermute | solution.py:30
  3.8 21.4 %collective-permute-start.4 = (bf16[192,1152]{1,0:T(8,128)(2,1)}, bf16[192,1152]{1,0:T(8,128)(2,1)}, u32[]{:S(2)}, u32[]{:S(2)}) collective-permute-start(bf16[192,1152]{1,0:T(8,128)(2,1)} %bitcast.63), channel_id=1, source_target_pairs={{0,8},{8,0},{16,24},{24,16},{1,9},{9,1},{17,25},{25,17},{2,10},{10... | collective-permute-start | bytes 1327112 | tf_op jit(solution)/shard_map/ppermute | solution.py:30
  7.1 9.8 %copy-start.7 = (f32[192]{0:T(256)}, f32[192]{0:T(256)S(1)}, u32[]{:S(2)}) copy-start(f32[192]{0:T(256)S(1)} %broadcast_multiply_fusion.6) | copy-start | bytes 2308
  8.4 8.5 %copy-start.8 = (f32[192]{0:T(256)}, f32[192]{0:T(256)S(1)}, u32[]{:S(2)}) copy-start(f32[192]{0:T(256)S(1)} %add_rsqrt_fusion.11) | copy-start | bytes 2308
  8.4 3.5 %copy-start.16 = (f32[192]{0:T(256)S(1)}, f32[192]{0:T(256)}, u32[]{:S(2)}) copy-start(f32[192]{0:T(256)} %fusion.51) | copy-start | bytes 2308
  8.4 8.5 %copy-start.1 = (bf16[192,1,1152]{2,0,1:T(8,128)(2,1)S(1)}, bf16[192,1,1152]{2,0,1:T(8,128)(2,1)}, u32[]{:S(2)}) copy-start(bf16[192,1,1152]{2,0,1:T(8,128)(2,1)} %param.6) | copy-start | bytes 1327108
  8.4 8.5 %copy-start.5 = (f32[1152]{0:T(1024)S(1)}, f32[1152]{0:T(1024)}, u32[]{:S(2)}) copy-start(f32[1152]{0:T(1024)} %param.9) | copy-start | bytes 13828
  23.7 6.8 %copy-start.10 = (f32[192]{0:T(256)}, f32[192]{0:T(256)S(1)}, u32[]{:S(2)}) copy-start(f32[192]{0:T(256)S(1)} %broadcast_multiply_fusion.3) | copy-start | bytes 2308
  25.2 5.3 %copy-start.14 = (f32[192]{0:T(256)}, f32[192]{0:T(256)S(1)}, u32[]{:S(2)}) copy-start(f32[192]{0:T(256)S(1)} %add_rsqrt_fusion.5) | copy-start | bytes 2308
  26.3 4.1 %copy-start.11 = (f32[192]{0:T(256)}, f32[192]{0:T(256)S(1)}, u32[]{:S(2)}) copy-start(f32[192]{0:T(256)S(1)} %broadcast_multiply_fusion.2) | copy-start | bytes 2308
  27.6 2.8 %copy-start.15 = (f32[192]{0:T(256)}, f32[192]{0:T(256)S(1)}, u32[]{:S(2)}) copy-start(f32[192]{0:T(256)S(1)} %add_rsqrt_fusion.3) | copy-start | bytes 2308
  31.4 6.3 %copy-start.9 = (f32[192]{0:T(256)S(1)}, f32[192]{0:T(256)}, u32[]{:S(2)}) copy-start(f32[192]{0:T(256)} %add_rsqrt_fusion.10) | copy-start | bytes 2308
  32.4 4.3 %collective-permute-start.2 = (bf16[192,1152]{1,0:T(8,128)(2,1)}, bf16[192,1152]{1,0:T(8,128)(2,1)S(1)}, u32[]{:S(2)}, u32[]{:S(2)}) collective-permute-start(bf16[192,1152]{1,0:T(8,128)(2,1)} %collective-permute-done), channel_id=1, source_target_pairs={{0,8},{8,0},{16,24},{24,16},{1,9},{9,1},{17,25},{25,17},{2,10},{10... | collective-permute-start | bytes 1327112 | tf_op jit(solution)/shard_map/ppermute | solution.py:30
  32.4 18.2 %collective-permute-start.5 = (bf16[192,1152]{1,0:T(8,128)(2,1)S(1)}, bf16[192,1152]{1,0:T(8,128)(2,1)}, u32[]{:S(2)}, u32[]{:S(2)}) collective-permute-start(bf16[192,1152]{1,0:T(8,128)(2,1)S(1)} %collective-permute-done.3), channel_id=1, source_target_pairs={{0,8},{8,0},{16,24},{24,16},{1,9},{9,1},{17,25},{25,17},{2,10},{10... | collective-permute-start | bytes 1327112 | tf_op jit(solution)/shard_map/ppermute | solution.py:30
  51.7 4.1 %copy-start.12 = (f32[192]{0:T(256)}, f32[192]{0:T(256)S(1)}, u32[]{:S(2)}) copy-start(f32[192]{0:T(256)S(1)} %broadcast_multiply_fusion.1) | copy-start | bytes 2308
  53.0 2.8 %copy-start.17 = (f32[192]{0:T(256)}, f32[192]{0:T(256)S(1)}, u32[]{:S(2)}) copy-start(f32[192]{0:T(256)S(1)} %add_rsqrt_fusion.1) | copy-start | bytes 2308
  55.8 21.6 %all-to-all-start = ((bf16[4,192,288]{1,2,0:T(8,128)(2,1)}), bf16[4,192,288]{1,2,0:T(8,128)(2,1)}, u32[]{:S(2)}, u32[]{:S(2)}) async-start(bf16[4,192,288]{1,2,0:T(8,128)(2,1)} %bitcast.67), calls=%async_computation | async-start | bytes 1179648 | tf_op jit(solution)/shard_map/all_to_all | solution.py:80
  60.2 2.6 %copy-start.2 = (f32[192,1152]{1,0:T(8,128)S(1)}, f32[192,1152]{1,0:T(8,128)}, u32[]{:S(2)}) copy-start(f32[192,1152]{1,0:T(8,128)} %fusion.95) | copy-start | bytes 2654212
  60.2 2.6 %copy-start.13 = (f32[192]{0:T(256)S(1)}, f32[192]{0:T(256)}, u32[]{:S(2)}) copy-start(f32[192]{0:T(256)} %copy-done.12) | copy-start | bytes 2308
  60.2 2.6 %copy-start.18 = (f32[192]{0:T(256)S(1)}, f32[192]{0:T(256)}, u32[]{:S(2)}) copy-start(f32[192]{0:T(256)} %copy-done.17) | copy-start | bytes 2308
  62.8 2.7 %copy-start.4 = (bf16[1,192,1152]{2,1,0:T(8,128)(2,1)S(1)}, bf16[1,192,1152]{2,1,0:T(8,128)(2,1)}, u32[]{:S(2)}) copy-start(bf16[1,192,1152]{2,1,0:T(8,128)(2,1)} %fusion.60) | copy-start | bytes 1327108
  65.5 1.5 copy-start.3
  80.7 9.6 %copy-start.6 = (f32[1152]{0:T(1024)S(1)}, f32[1152]{0:T(1024)}, u32[]{:S(2)}) copy-start(f32[1152]{0:T(1024)} %broadcast_multiply_fusion) | copy-start | bytes 13828
  83.0 63.1 %all-to-all-start.1 = ((bf16[8,144,288]{2,1,0:T(8,128)(2,1)}), bf16[8,144,288]{2,1,0:T(8,128)(2,1)}, u32[]{:S(2)}, u32[]{:S(2)}) async-start(bf16[8,144,288]{2,1,0:T(8,128)(2,1)} %bitcast.66), calls=%async_computation.1 | async-start | bytes 1769472 | tf_op jit(solution)/shard_map/all_to_all | solution.py:104

commit v2 on v1

--- a/solution.py
+++ b/solution.py
@@ -1,6 +1,10 @@
+import functools
+
 import jax
 import jax.numpy as jnp
 from jax import lax
+from jax.experimental import pallas as pl
+from jax.experimental.pallas import tpu as pltpu
 from jax.sharding import PartitionSpec as P
 
 F32 = jnp.float32
@@ -38,7 +42,7 @@
     return mine + mates
 
 
-def local(features, text, proj, gain, scale, bias):
+def local_any_size(features, text, proj, gain, scale, bias):
     n = lax.axis_size("loop")
     m = lax.axis_size("rep")
     me = lax.axis_index("loop")
@@ -120,11 +124,385 @@
     return feature_grad[:, None, :], text_grad[:, None, :], proj_grad, gain_gradient
 
 
+VMEM = pl.BlockSpec(memory_space=pltpu.VMEM)
+SMEM = pl.BlockSpec(memory_space=pltpu.SMEM)
+LANES = 128
+BAND = 16
+
+
+def call(body, outs, scratch=(), smem=0, flops=0, moved=0):
+    def run(*operands):
+        specs = [SMEM] * smem + [VMEM] * (len(operands) - smem)
+        return pl.pallas_call(
+            body,
+            out_shape=[jax.ShapeDtypeStruct(shape, kind) for shape, kind in outs],
+            in_specs=specs,
+            out_specs=[VMEM] * len(outs),
+            scratch_shapes=list(scratch),
+            compiler_params=pltpu.CompilerParams(vmem_limit_bytes=36 * 2**20),
+            cost_estimate=pl.CostEstimate(flops=flops, bytes_accessed=moved, transcendentals=0),
+        )(*operands)
+
+    return run
+
+
+def over_rows(count, step, body):
+    def turn(index, _):
+        body(pl.ds(pl.multiple_of(index * step, step), step))
+        return 0
+
+    lax.fori_loop(0, count // step, turn, 0, unroll=2)
+
+
+def sums(values):
+    return jnp.sum(values, axis=-1, keepdims=True)
+
+
+def normalize_into(source, gain, target, at):
+    rows, width = source.shape
+
+    def chunk(where):
+        values = source[where, :].astype(F32)
+        centred = values - sums(values) * (1.0 / width)
+        inverse = lax.rsqrt(sums(centred * centred) * (1.0 / width) + 1e-06)
+        target[pl.ds(at + where.start, where.size), :] = (centred * inverse * gain[...]).astype(BF16)
+
+    over_rows(rows, 32, chunk)
+
+
+def unit_into(source, target, at, inverses=None):
+    rows = source.shape[0]
+
+    def chunk(where):
+        values = source[where, :].astype(F32)
+        inverse = lax.rsqrt(sums(values * values) + 1e-06)
+        place = pl.ds(at + where.start, where.size)
+        target[place, :] = (values * inverse).astype(BF16)
+        if inverses is not None:
+            inverses[place, :] = inverse
+
+    over_rows(rows, 32, chunk)
+
+
+def weigh(dots, scale, bias, first_column, weights, columns_at, totals, add_to):
+    rows, columns = dots.shape
+
+    def chunk(where):
+        product = dots[where, :]
+        logits = scale * product + bias
+        weight = 1.0 / (1.0 + jnp.exp(-logits))
+        row = where.start + lax.broadcasted_iota(jnp.int32, product.shape, 0)
+        column = first_column + lax.broadcasted_iota(jnp.int32, product.shape, 1)
+        weight = jnp.where(row == column, weight - 1.0, weight).astype(BF16)
+        weights[where, columns_at : columns_at + columns] = weight
+        total = sums(weight.astype(F32) * product)
+        totals[where, :] = total if add_to is None else add_to[where, :] + total
+
+    over_rows(rows, 64, chunk)
+
+
+def near_body(f0, f1, t0, t1, proj, gain, normed, unit, inverse, text_unit, projected):
+    rows = f0.shape[0]
+    for k, source in enumerate((f0, f1)):
+        normalize_into(source, gain, normed, k * rows)
+    for k, source in enumerate((t0, t1)):
+        unit_into(source, text_unit, k * rows)
+    projected[...] = dot(normed[...], proj[...])
+    unit_into(projected, unit, 0, inverse)
+
+
+def far_body(
+    scalars, f2, f3, proj, gain, normed_near, unit_near, inverse_near, text_near,
+    normed, unit, inverse, weights, totals, projected, dots,
+):
+    rows = f2.shape[0]
+    near = 2 * rows
+    normed[:near, :] = normed_near[...]
+    unit[:near, :] = unit_near[...]
+    inverse[:near, :] = inverse_near[...]
+    for k, source in enumerate((f2, f3)):
+        normalize_into(source, gain, normed, near + k * rows)
+    projected[...] = dot(normed[near:, :], proj[...])
+    unit_into(projected, unit, near, inverse)
+    dots[...] = dot(unit[...], text_near[...], LAST)
+    weigh(dots, scalars[0], scalars[1], 0, weights, 0, totals, None)
+
+
+def pack_into(target, block, full):
+    rows, columns = block.shape
+    rest = columns - full
+    target[:rows, :] = block[:, :full].astype(BF16)
+    per_band = full // rest
+    tail = block[:, full:]
+    chunks = [tail[at : at + BAND, :] for at in range(0, rows, BAND)]
+    for band in range(0, len(chunks), per_band):
+        part = chunks[band : band + per_band]
+        if len(part) < per_band:
+            part.append(jnp.zeros((BAND, full - rest * len(part)), block.dtype))
+        at = rows + (band // per_band) * BAND
+        target[at : at + BAND, :] = jnp.concatenate(part, axis=1).astype(BF16)
+
+
+def partial_body(
+    members, groups, scalars, place, t2, t3, text_near, unit, inverse, normed, weights_near, totals_near,
+    *refs,
+):
+    packets, (text_far, weights_own), scratch = refs[:groups], refs[groups : groups + 2], refs[groups + 2 :]
+    weights, totals, dots, text_columns, unit_columns, back, packed = scratch
+    rows = t2.shape[0]
+    near = 2 * rows
+    every = members * rows
+    width = unit.shape[1]
+    columns = width // members
+    full = packed.shape[2]
+    scale, bias = scalars[0], scalars[1]
+    for k, source in enumerate((t2, t3)):
+        unit_into(source, text_far, k * rows)
+    dots[...] = dot(unit[...], text_far[...], LAST)
+    weights[:, :near] = weights_near[...]
+    weigh(dots, scale, bias, near, weights, near, totals, totals_near)
+    weights_own[...] = weights[:rows, :]
+    for member in range(members):
+
+        @pl.when(place[0] == member)
+        def _():
+            where = slice(member * columns, (member + 1) * columns)
+            text_columns[:near, :] = text_near[:, where]
+            text_columns[near:, :] = text_far[:, where]
+            unit_columns[...] = unit[:, where]
+
+    image_back = dot(weights[...], text_columns[...])
+    back[...] = (
+        (image_back - unit_columns[...].astype(F32) * totals[...]) * (inverse[...] * scale)
+    ).astype(BF16)
+    each = width // groups
+    product = dot(normed[...], back[...], FIRST) * (1.0 / every)
+    for group in range(groups):
+        pack_into(packed.at[group], product[group * each : (group + 1) * each, :], full)
+    for step in range(groups):
+        packets[step][...] = packed[place[1] ^ step]
+
+
+def own_body(
+    scalars, features, text, proj, gain, text_near, text_far, weights_own, weights_near, unit, inverse,
+    feature_grad, text_grad, gain_term, back, norm_back,
+):
+    rows, width = features.shape
+    near = 2 * rows
+    scale = scalars[0]
+    image_back = dot(weights_own[:, :near], text_near[...]) + dot(weights_own[:, near:], text_far[...])
+    norm_back[...] = image_back
+
+    def image_chunk(where):
+        values = norm_back[where, :] * scale
+        direction = unit[where, :].astype(F32)
+        back[where, :] = (
+            (values - direction * sums(direction * values)) * inverse[where, :]
+        ).astype(BF16)
+
+    over_rows(rows, 32, image_chunk)
+    norm_back[...] = dot(back[...], proj[...], LAST)
+    gain_term[...] = jnp.zeros_like(gain_term)
+
+    def feature_chunk(index, total):
+        where = pl.ds(pl.multiple_of(index * 32, 32), 32)
+        values = features[where, :].astype(F32)
+        centred = values - sums(values) * (1.0 / width)
+        deviation = lax.rsqrt(sums(centred * centred) * (1.0 / width) + 1e-06)
+        xhat = centred * deviation
+        upstream = norm_back[where, :]
+        scaled = upstream * gain[...]
+        feature_grad[where, :] = (
+            deviation
+            * (scaled - sums(scaled) * (1.0 / width) - xhat * (sums(scaled * xhat) * (1.0 / width)))
+        ).astype(BF16)
+        return total + jnp.sum((upstream * xhat).reshape(4, 8, width), axis=0)
+
+    total = lax.fori_loop(0, rows // 32, feature_chunk, jnp.zeros((8, width), F32))
+    total = jnp.sum(total, axis=0, keepdims=True) * (1.0 / unit.shape[0])
+    for at in range(width // LANES):
+        gain_term[at : at + 1, :] = total[:, at * LANES : (at + 1) * LANES]
+
+    norm_back[...] = dot(weights_near[:, :rows], unit[...], FIRST)
+
+    def text_chunk(where):
+        values = norm_back[where, :] * scale
+        own = text[where, :].astype(F32)
+        own_inverse = lax.rsqrt(sums(own * own) + 1e-06)
+        direction = own * own_inverse
+        text_grad[where, :] = (
+            (values - direction * sums(direction * values)) * own_inverse
+        ).astype(BF16)
+
+    over_rows(rows, 32, text_chunk)
+
+
+def reduce_body(groups, each, place, *refs):
+    packets, terms = refs[:groups], refs[groups : 2 * groups]
+    total, ordered = refs[2 * groups :]
+    count, full = total.shape
+
+    def chunk(where):
+        value = packets[0][where, :].astype(F32)
+        for packet in packets[1:]:
+            value = value + packet[where, :].astype(F32)
+        total[where, :] = value.astype(BF16)
+
+    over_rows(count, BAND, chunk)
+    for step in range(groups):
+        ordered[place[1] ^ step] = terms[step][...]
+    value = ordered[0]
+    for group in range(1, groups):
+        value = value + ordered[group]
+    total[count - BAND :, full - LANES :] = value.astype(BF16)
+
+
+def finish_body(members, place, *refs):
+    packets, (proj_grad, gain_gradient, ordered) = refs[:members], refs[members:]
+    count, full = packets[0].shape
+    rows, width = proj_grad.shape
+    columns = width // members
+    rest = columns - full
+    per_band = full // rest
+    for own in range(members):
+
+        @pl.when(place[0] == own)
+        def _():
+            for k in range(members):
+                base = (own ^ k) * columns
+                packet = packets[k]
+                main = packet[:rows, :].astype(F32)
+                tails = []
+                for index in range(rows // BAND):
+                    at = rows + (index // per_band) * BAND
+                    lane = (index % per_band) * rest
+                    tails.append(packet[at : at + BAND, lane : lane + rest].astype(F32))
+                proj_grad[:, base : base + full] = main
+                proj_grad[:, base + full : base + columns] = jnp.concatenate(tails, axis=0)
+
+    for k in range(members):
+        ordered[place[0] ^ k] = packets[k][count - BAND :, full - LANES :].astype(F32)
+    value = ordered[0]
+    for member in range(1, members):
+        value = value + ordered[member]
+    for at in range(width // LANES):
+        gain_gradient[:, at * LANES : (at + 1) * LANES] = value[at : at + 1, :]
+
+
+def local_four(features, text, proj, gain, scale, bias):
+    members = lax.axis_size("loop")
+    groups = lax.axis_size("rep")
+    place = jnp.stack([lax.axis_index("loop"), lax.axis_index("rep")]).astype(jnp.int32)
+    scalars = jnp.concatenate([scale, bias])
+    rows, width = features.shape[0], features.shape[2]
+    near, every = 2 * rows, 4 * rows
+    columns = width // members
+    full = columns // LANES * LANES
+    each = width // groups
+    bands = -(-(each // BAND) // (full // (columns - full)))
+    packet = (each + bands * BAND, full)
+    gain_row = gain.reshape(1, width)
+
+    f0, t0 = features[:, 0, :], text[:, 0, :]
+    f1 = send(f0, "loop", lambda p: p ^ 1)
+    t1 = send(t0, "loop", lambda p: p ^ 1)
+    f2 = send(f0, "loop", lambda p: p ^ 2)
+    t_after, f2 = lax.optimization_barrier((t0, f2))
+    t2 = send(t_after, "loop", lambda p: p ^ 2)
+    f3 = send(f2, "loop", lambda p: p ^ 1)
+    t3 = send(t2, "loop", lambda p: p ^ 1)
+
+    normed_near, unit_near, inverse_near, text_near = call(
+        near_body,
+        [((near, width), BF16), ((near, width), BF16), ((near, 1), F32), ((near, width), BF16)],
+        [pltpu.VMEM((near, width), F32)],
+        flops=2 * near * width * width,
+        moved=8 * near * width,
+    )(f0, f1, t0, t1, proj, gain_row)
+
+    normed, unit, inverse, weights_near, totals_near = call(
+        far_body,
+        [((every, width), BF16), ((every, width), BF16), ((every, 1), F32), ((every, near), BF16), ((every, 1), F32)],
+        [pltpu.VMEM((near, width), F32), pltpu.VMEM((every, near), F32)],
+        smem=1,
+        flops=4 * near * width * width,
+        moved=16 * near * width,
+    )(scalars, f2, f3, proj, gain_row, normed_near, unit_near, inverse_near, text_near)
+
+    outs = call(
+        functools.partial(partial_body, members, groups),
+        [(packet, BF16)] * groups + [((near, width), BF16), ((rows, every), BF16)],
+        [
+            pltpu.VMEM((every, every), BF16),
+            pltpu.VMEM((every, 1), F32),
+            pltpu.VMEM((every, near), F32),
+            pltpu.VMEM((every, columns), BF16),
+            pltpu.VMEM((every, columns), BF16),
+            pltpu.VMEM((every, columns), BF16),
+            pltpu.VMEM((groups,) + packet, BF16),
+        ],
+        smem=2,
+        flops=6 * near * width * width,
+        moved=16 * near * width,
+    )(scalars, place, t2, t3, text_near, unit, inverse, normed, weights_near, totals_near)
+    packets, (text_far, weights_own) = outs[:groups], outs[groups:]
+    arrived = [packets[0]] + [
+        send(packets[step], "rep", lambda p: p ^ step) for step in range(1, groups)
+    ]
+
+    feature_grad, text_grad, gain_term = call(
+        own_body,
+        [((rows, width), BF16), ((rows, width), BF16), ((BAND, LANES), F32)],
+        [pltpu.VMEM((rows, width), BF16), pltpu.VMEM((rows, width), F32)],
+        smem=1,
+        flops=6 * near * width * width,
+        moved=16 * near * width,
+    )(scalars, f0, t0, proj, gain_row, text_near, text_far, weights_own, weights_near, unit, inverse)
+    terms = [gain_term] + [send(gain_term, "rep", lambda p: p ^ step) for step in range(1, groups)]
+
+    (reduced,) = call(
+        functools.partial(reduce_body, groups, each),
+        [(packet, BF16)],
+        [pltpu.VMEM((groups, BAND, LANES), F32)],
+        smem=1,
+        moved=4 * each * width,
+    )(place, *arrived, *terms)
+    blocks = [reduced] + [send(reduced, "loop", lambda p: p ^ k) for k in range(1, members)]
+
+    proj_grad, gain_gradient = call(
+        functools.partial(finish_body, members),
+        [((each, width), F32), ((1, width), F32)],
+        [pltpu.VMEM((members, BAND, LANES), F32)],
+        smem=1,
+        moved=8 * each * width,
+    )(place, *blocks)
+    return feature_grad[:, None, :], text_grad[:, None, :], proj_grad, gain_gradient.reshape(width)
+
+
+def four_fits(mesh, rows_shape):
+    members, groups = mesh.shape["loop"], mesh.shape["rep"]
+    rows, width = rows_shape[0] // members, rows_shape[2]
+    if members != 4 or groups & (groups - 1) or width % (members * groups) or width % LANES:
+        return False
+    columns, each = width // members, width // groups
+    full = columns // LANES * LANES
+    rest = columns - full
+    if rest == 0 or full < LANES or full % rest or each % BAND or rows % 64 or width // LANES > BAND:
+        return False
+    chunks = each // BAND
+    used = (chunks - 1) % (full // rest) + 1
+    return used * rest <= full - LANES
+
+
 def solution(mesh):
-    return jax.shard_map(
-        local,
-        mesh=mesh,
-        in_specs=(P("loop", "rep", None), P("loop", "rep", None), P(), P(), P(), P()),
-        out_specs=(P("loop", "rep", None), P("loop", "rep", None), P("rep", None), P()),
-        check_vma=False,
-    )
+    def run(features, text, proj, gain, scale, bias):
+        body = local_four if four_fits(mesh, features.shape) else local_any_size
+        return jax.shard_map(
+            body,
+            mesh=mesh,
+            in_specs=(P("loop", "rep", None), P("loop", "rep", None), P(), P(), P(), P()),
+            out_specs=(P("loop", "rep", None), P("loop", "rep", None), P("rep", None), P()),
+            check_vma=False,
+        )(features, text, proj, gain, scale, bias)
+
+    return run

time: 157 us -> 92.7 us (0.59)
  blocking collectives: 56.1 us -> 0 us
  other arithmetic: 43.1 us -> 0.77 us
  matrix products: 26 us -> 0 us
  Pallas kernels: 0 us -> 25.3 us
  waiting for transfers between devices: 4.42 us -> 29.5 us
  starting transfers between devices: 14.5 us -> 30.2 us
  local copies, waits for them, and re-layouts: 9.66 us -> 4.49 us
    all_gather x3 -> x0, blocking collectives: 56.1 us -> none  [the longest x1 43.6 us: local(): gains = lax.all_gather(gain_term, 'rep')]
    ppermute x6 -> x23, starting transfers between devices: 4.03 us -> 30.2 us  [send(): return lax.ppermute(value, axis, [(p, target(p)) for p in range(count)])]
    dot_general x8 -> x0, matrix products: 26 us -> none  [dot(): return lax.dot_general(a, b, dims, preferred_element_type=F32)]
    pallas_call x0 -> x6, Pallas kernels: none -> 25.3 us  [run(): pl.pallas_call(body, out_shape=[jax.ShapeDtypeStruct(shape, kind) for sha...]
    ppermute x6 -> x23, waiting for transfers between devices: 4.41 us -> 29.5 us  [send(): return lax.ppermute(value, axis, [(p, target(p)) for p in range(count)])]
    reduce_sum x15 -> x0, other arithmetic: 15.4 us -> none  [the longest x4 4.27 us: unit_rows(): jnp.sum(values * values, axis=-1, keepdims=True) + 1e-06]
    convert_element_type x9 -> x0, other arithmetic: 14.2 us -> none  [the longest x3 4.75 us: local(): unit_rows(block.astype(F32))[0].astype(BF16)]
    all_to_all x2 -> x0, starting transfers between devices: 10.4 us -> none  [the longest x1 6.09 us: local(): lax.all_to_all(partial.reshape(m, width // m, columns), 'rep', 0, 0, tile...]
  transfers between devices with their start and end apart: 8 -> 23, of which waited for: 1 -> 11; matrix products, arithmetic and copies ran while one was open for 37% -> 1% of each run, Pallas kernels for 0% -> 19%
where the time goes in v2:
time: 92.7 us; the launch traced here: 92.4 us
  starting transfers between devices  30.2 us (33%)
  waiting for transfers between devices  29.5 us (32%)
  Pallas kernels  25.3 us (27%)
  local copies, waits for them, and re-layouts  4.49 us (5%)
  between operations  2 us (2%)
    ppermute x23, starting transfers between devices, send(): return lax.ppermute(value, axis, [(p, target(p)) for p in range(count)])  30.2 us
    ppermute x23, waiting for transfers between devices, send(): return lax.ppermute(value, axis, [(p, target(p)) for p in range(count)])  29.5 us
    pallas_call x6, Pallas kernels, run(): pl.pallas_call(body, out_shape=[jax.ShapeDtypeStruct(shape, kind) for sha...  25.3 us
    unnamed x12, local copies, waits for them, and re-layouts  3.79 us
  transfers between devices with their start and end apart: 23, of which 11 were waited for; matrix products, arithmetic and copies ran while one was open for 1% of the time, Pallas kernels for 19%

profile of v2, /device:TPU:0, one launch (start us, length us, event | category | flops | bytes accessed | tf_op | source)
XLA Modules:
  0.0 92.4 jit_solution(5760908915469519471)
XLA Ops:
  0.6 3.0 %collective-permute-start.2 = (bf16[192,1152]{1,0:T(8,128)(2,1)}, bf16[192,1152]{1,0:T(8,128)(2,1)S(1)}, u32[]{:S(2)}, u32[]{:S(2)}) collective-permute-start(bf16[192,1152]{1,0:T(8,128)(2,1)} %bitcast.6), channel_id=1, source_target_pairs={{0,16},{8,24},{16,0},{24,8},{1,17},{9,25},{17,1},{25,9},{2,18},{10... | collective-permute-start | bytes 1327112 | tf_op jit(solution)/shard_map/ppermute | solution.py:34
  3.6 10.4 %collective-permute-done.2.f2 = bf16[192,1152]{1,0:T(8,128)(2,1)S(1)} collective-permute-done((bf16[192,1152]{1,0:T(8,128)(2,1)}, bf16[192,1152]{1,0:T(8,128)(2,1)S(1)}, u32[]{:S(2)}, u32[]{:S(2)}) %collective-permute-start.2) | collective-permute-done | bytes 442400 | tf_op jit(solution)/shard_map/ppermute | solution.py:34
  14.0 1.7 %collective-permute-start.3 = (bf16[192,1152]{1,0:T(8,128)(2,1)}, bf16[192,1152]{1,0:T(8,128)(2,1)S(1)}, u32[]{:S(2)}, u32[]{:S(2)}) collective-permute-start(bf16[192,1152]{1,0:T(8,128)(2,1)} %bitcast.10), channel_id=1, source_target_pairs={{0,16},{8,24},{16,0},{24,8},{1,17},{9,25},{17,1},{25,9},{2,18},{10... | collective-permute-start | bytes 1327112 | tf_op jit(solution)/shard_map/ppermute | solution.py:34
  15.8 0.0 collective-permute-start
  15.8 0.5 collective-permute-start.1
  16.3 0.0 collective-permute-start.5
  17.6 8.0 %collective-permute-done.3.t2 = bf16[192,1152]{1,0:T(8,128)(2,1)S(1)} collective-permute-done((bf16[192,1152]{1,0:T(8,128)(2,1)}, bf16[192,1152]{1,0:T(8,128)(2,1)S(1)}, u32[]{:S(2)}, u32[]{:S(2)}) %collective-permute-start.3) | collective-permute-done | bytes 442400 | tf_op jit(solution)/shard_map/ppermute | solution.py:34
  25.6 0.1 pad_maximum_fusion.scalars
  25.7 0.7 reshape.14.gain
  26.4 0.1 pad_add_fusion.place
  26.4 0.0 collective-permute-done.f1
  26.4 1.7 %copy-done = bf16[1152,1152]{1,0:T(8,128)(2,1)S(1)} copy-done((bf16[1152,1152]{1,0:T(8,128)(2,1)S(1)}, bf16[1152,1152]{1,0:T(8,128)(2,1)}, u32[]{:S(2)}) %copy-start) | copy-done | bytes 2654232
  28.2 1.0 %copy-done.2 = bf16[192,1,1152]{2,0,1:T(8,128)(2,1)S(1)} copy-done((bf16[192,1,1152]{2,0,1:T(8,128)(2,1)S(1)}, bf16[192,1,1152]{2,0,1:T(8,128)(2,1)}, u32[]{:S(2)}) %copy-start.2) | copy-done | bytes 442392
  29.2 1.0 %copy-done.4 = bf16[192,1,1152]{2,0,1:T(8,128)(2,1)S(1)} copy-done((bf16[192,1,1152]{2,0,1:T(8,128)(2,1)S(1)}, bf16[192,1,1152]{2,0,1:T(8,128)(2,1)}, u32[]{:S(2)}) %copy-start.4) | copy-done | bytes 442392
  30.2 4.1 %shard_map.93 = (bf16[384,1152]{1,0:T(8,128)(2,1)S(1)}, bf16[384,1152]{1,0:T(8,128)(2,1)S(1)}, f32[384,1]{1,0:T(8,128)S(1)}, bf16[384,1152]{1,0:T(8,128)(2,1)S(1)}) custom-call(bf16[192,1152]{1,0:T(8,128)(2,1)S(1)} %bitcast.8, bf16[192,1152]{1,0:T(8,128)(2,1)S(1)} %collective-permute-done.f1, bf16[192,1152]{1,0:T(8,128)(2,1)S(1)} %bitcast.12, ...), custom_call_target="tpu_custom_call" | custom-call | flops 1019215872 | bytes 3538944 | tf_op jit(solution)/shard_map/pallas_call | solution.py:136
  34.4 0.0 collective-permute-done.5.f3
  34.4 6.7 %shard_map.94 = (bf16[768,1152]{1,0:T(8,128)(2,1)S(1)}, bf16[768,1152]{1,0:T(8,128)(2,1)S(1)}, f32[768,1]{1,0:T(8,128)S(1)}, bf16[768,384]{1,0:T(8,128)(2,1)S(1)}, f32[768,1]{1,0:T(8,128)S(1)}) custom-call(f32[2]{0:T(128)S(1)} %pad_maximum_fusion.scalars, bf16[192,1152]{1,0:T(8,128)(2,1)S(1)} %collective-permute-done.2.f2, ...), custom_call_target="tpu_custom_call" | custom-call | flops 2038431744 | bytes 7077888 | tf_op jit(solution)/shard_map/pallas_call | solution.py:136
  41.0 0.0 collective-permute-done.4.t3
  41.0 5.5 %shard_map.95 = (bf16[176,256]{1,0:T(8,128)(2,1)S(1)}, bf16[176,256]{1,0:T(8,128)(2,1)S(1)}, bf16[176,256]{1,0:T(8,128)(2,1)S(1)}, bf16[176,256]{1,0:T(8,128)(2,...) custom-call(f32[2]{0:T(128)S(1)} %pad_maximum_fusion.scalars, ...), custom_call_target="tpu_custom_call" | custom-call | flops 3057647616 | bytes 7077888 | tf_op jit(solution)/shard_map/pallas_call | solution.py:136
  46.6 3.5 %collective-permute-start.10 = (bf16[176,256]{1,0:T(8,128)(2,1)S(1)}, bf16[176,256]{1,0:T(8,128)(2,1)S(1)}, u32[]{:S(2)}, u32[]{:S(2)}) collective-permute-start(bf16[176,256]{1,0:T(8,128)(2,1)S(1)} %get-tuple-element.50), channel_id=1, source_target_pairs={{0,5},{1,4},{2,7},{3,6},{4,1},{5,0},{6,3},{7,2},{8,13},{9,12},{10,... | collective-permute-start | bytes 270344 | tf_op jit(solution)/shard_map/ppermute | solution.py:34
  50.1 1.4 %collective-permute-start.11 = (bf16[176,256]{1,0:T(8,128)(2,1)S(1)}, bf16[176,256]{1,0:T(8,128)(2,1)S(1)}, u32[]{:S(2)}, u32[]{:S(2)}) collective-permute-start(bf16[176,256]{1,0:T(8,128)(2,1)S(1)} %get-tuple-element.51), channel_id=1, source_target_pairs={{0,6},{1,7},{2,4},{3,5},{4,2},{5,3},{6,0},{7,1},{8,14},{9,15},{10,... | collective-permute-start | bytes 270344 | tf_op jit(solution)/shard_map/ppermute | solution.py:34
  51.5 6.7 %shard_map.96 = (bf16[192,1152]{1,0:T(8,128)(2,1)}, bf16[192,1152]{1,0:T(8,128)(2,1)}, f32[16,128]{1,0:T(8,128)S(1)}) custom-call(f32[2]{0:T(128)S(1)} %pad_maximum_fusion.scalars, bf16[192,1152]{1,0:T(8,128)(2,1)S(1)} %bitcast.9, bf16[192,1152]{1,0:T(8,128)(2,1)S(1)} %bitcast.13, bf16[1152,1152]{1,0:T(8,128)(2,1)S(1)} %copy-done.1, ...), custom_call_target="tpu_custom_call" | custom-call | flops 3057647616 | bytes 7077888 | tf_op jit(solution)/shard_map/pallas_call | solution.py:136
  58.2 0.5 collective-permute-start.13
  58.7 0.2 collective-permute-start.14
  58.9 2.8 %collective-permute-start.15 = (f32[16,128]{1,0:T(8,128)S(1)}, f32[16,128]{1,0:T(8,128)S(1)}, u32[]{:S(2)}, u32[]{:S(2)}) collective-permute-start(f32[16,128]{1,0:T(8,128)S(1)} %get-tuple-element.53.refs_8_), channel_id=1, source_target_pairs={{0,3},{1,2},{2,1},{3,0},{4,7},{5,6},{6,5},{7,4},{8,11},{9,10},{10,... | collective-permute-start | bytes 24584 | tf_op jit(solution)/shard_map/ppermute | solution.py:34
  61.7 0.2 collective-permute-done.13.refs_9_
  61.8 1.7 %collective-permute-start.16 = (f32[16,128]{1,0:T(8,128)S(1)}, f32[16,128]{1,0:T(8,128)S(1)}, u32[]{:S(2)}, u32[]{:S(2)}) collective-permute-start(f32[16,128]{1,0:T(8,128)S(1)} %get-tuple-element.53.refs_8_), channel_id=1, source_target_pairs={{0,4},{1,5},{2,6},{3,7},{4,0},{5,1},{6,2},{7,3},{8,12},{9,13},{10,... | collective-permute-start | bytes 24584 | tf_op jit(solution)/shard_map/ppermute | solution.py:34
  63.5 1.5 %collective-permute-start.17 = (f32[16,128]{1,0:T(8,128)S(1)}, f32[16,128]{1,0:T(8,128)S(1)}, u32[]{:S(2)}, u32[]{:S(2)}) collective-permute-start(f32[16,128]{1,0:T(8,128)S(1)} %get-tuple-element.53.refs_8_), channel_id=1, source_target_pairs={{0,5},{1,4},{2,7},{3,6},{4,1},{5,0},{6,3},{7,2},{8,13},{9,12},{10,... | collective-permute-start | bytes 24584 | tf_op jit(solution)/shard_map/ppermute | solution.py:34
  65.0 0.0 collective-permute-done.15.refs_11_
  65.0 2.2 %collective-permute-start.18 = (f32[16,128]{1,0:T(8,128)S(1)}, f32[16,128]{1,0:T(8,128)S(1)}, u32[]{:S(2)}, u32[]{:S(2)}) collective-permute-start(f32[16,128]{1,0:T(8,128)S(1)} %get-tuple-element.53.refs_8_), channel_id=1, source_target_pairs={{0,6},{1,7},{2,4},{3,5},{4,2},{5,3},{6,0},{7,1},{8,14},{9,15},{10,... | collective-permute-start | bytes 24584 | tf_op jit(solution)/shard_map/ppermute | solution.py:34
  67.2 2.3 %collective-permute-start.19 = (f32[16,128]{1,0:T(8,128)S(1)}, f32[16,128]{1,0:T(8,128)S(1)}, u32[]{:S(2)}, u32[]{:S(2)}) collective-permute-start(f32[16,128]{1,0:T(8,128)S(1)} %get-tuple-element.53.refs_8_), channel_id=1, source_target_pairs={{0,7},{1,6},{2,5},{3,4},{4,3},{5,2},{6,1},{7,0},{8,15},{9,14},{10,... | collective-permute-start | bytes 24584 | tf_op jit(solution)/shard_map/ppermute | solution.py:34
  69.5 2.4 %collective-permute-start.12 = (bf16[176,256]{1,0:T(8,128)(2,1)S(1)}, bf16[176,256]{1,0:T(8,128)(2,1)S(1)}, u32[]{:S(2)}, u32[]{:S(2)}) collective-permute-start(bf16[176,256]{1,0:T(8,128)(2,1)S(1)} %get-tuple-element.52), channel_id=1, source_target_pairs={{0,7},{1,6},{2,5},{3,4},{4,3},{5,2},{6,1},{7,0},{8,15},{9,14},{10,... | collective-permute-start | bytes 270344 | tf_op jit(solution)/shard_map/ppermute | solution.py:34
  71.9 1.5 %collective-permute-start.6 = (bf16[176,256]{1,0:T(8,128)(2,1)S(1)}, bf16[176,256]{1,0:T(8,128)(2,1)S(1)}, u32[]{:S(2)}, u32[]{:S(2)}) collective-permute-start(bf16[176,256]{1,0:T(8,128)(2,1)S(1)} %get-tuple-element.46), channel_id=1, source_target_pairs={{0,1},{1,0},{2,3},{3,2},{4,5},{5,4},{6,7},{7,6},{8,9},{9,8},{10,11... | collective-permute-start | bytes 270344 | tf_op jit(solution)/shard_map/ppermute | solution.py:34
  73.4 0.2 collective-permute-done.19.refs_15_
  73.7 3.0 %collective-permute-start.8 = (bf16[176,256]{1,0:T(8,128)(2,1)S(1)}, bf16[176,256]{1,0:T(8,128)(2,1)S(1)}, u32[]{:S(2)}, u32[]{:S(2)}) collective-permute-start(bf16[176,256]{1,0:T(8,128)(2,1)S(1)} %get-tuple-element.48), channel_id=1, source_target_pairs={{0,3},{1,2},{2,1},{3,0},{4,7},{5,6},{6,5},{7,4},{8,11},{9,10},{10,... | collective-permute-start | bytes 270344 | tf_op jit(solution)/shard_map/ppermute | solution.py:34
  76.6 1.2 %collective-permute-done.12.refs_7_ = bf16[176,256]{1,0:T(8,128)(2,1)S(1)} collective-permute-done((bf16[176,256]{1,0:T(8,128)(2,1)S(1)}, bf16[176,256]{1,0:T(8,128)(2,1)S(1)}, u32[]{:S(2)}, u32[]{:S(2)}) %collective-permute-start.12) | collective-permute-done | bytes 90144 | tf_op jit(solution)/shard_map/ppermute | solution.py:34
  77.8 0.6 collective-permute-done.6.refs_1_
  78.4 0.4 collective-permute-done.7.refs_2_
  78.8 1.7 %collective-permute-done.8.refs_3_ = bf16[176,256]{1,0:T(8,128)(2,1)S(1)} collective-permute-done((bf16[176,256]{1,0:T(8,128)(2,1)S(1)}, bf16[176,256]{1,0:T(8,128)(2,1)S(1)}, u32[]{:S(2)}, u32[]{:S(2)}) %collective-permute-start.8) | collective-permute-done | bytes 90144 | tf_op jit(solution)/shard_map/ppermute | solution.py:34
  80.6 1.9 %collective-permute-done.9.refs_4_ = bf16[176,256]{1,0:T(8,128)(2,1)S(1)} collective-permute-done((bf16[176,256]{1,0:T(8,128)(2,1)S(1)}, bf16[176,256]{1,0:T(8,128)(2,1)S(1)}, u32[]{:S(2)}, u32[]{:S(2)}) %collective-permute-start.9) | collective-permute-done | bytes 90144 | tf_op jit(solution)/shard_map/ppermute | solution.py:34
  82.5 0.7 shard_map.97.refs_0_
  83.2 0.1 collective-permute-start.20
  83.2 1.9 %collective-permute-start.21 = (bf16[176,256]{1,0:T(8,128)(2,1)S(1)}, bf16[176,256]{1,0:T(8,128)(2,1)S(1)}, u32[]{:S(2)}, u32[]{:S(2)}) collective-permute-start(bf16[176,256]{1,0:T(8,128)(2,1)S(1)} %shard_map.97.refs_0_), channel_id=1, source_target_pairs={{0,16},{8,24},{16,0},{24,8},{1,17},{9,25},{17,1},{25,9},{2,18},{10... | collective-permute-start | bytes 270344 | tf_op jit(solution)/shard_map/ppermute | solution.py:34
  85.1 0.1 collective-permute-start.22
  85.2 3.3 %collective-permute-done.21.refs_2_ = bf16[176,256]{1,0:T(8,128)(2,1)S(1)} collective-permute-done((bf16[176,256]{1,0:T(8,128)(2,1)S(1)}, bf16[176,256]{1,0:T(8,128)(2,1)S(1)}, u32[]{:S(2)}, u32[]{:S(2)}) %collective-permute-start.21) | collective-permute-done | bytes 90144 | tf_op jit(solution)/shard_map/ppermute | solution.py:34
  88.5 1.6 %collective-permute-done.22.refs_3_ = bf16[176,256]{1,0:T(8,128)(2,1)S(1)} collective-permute-done((bf16[176,256]{1,0:T(8,128)(2,1)S(1)}, bf16[176,256]{1,0:T(8,128)(2,1)S(1)}, u32[]{:S(2)}, u32[]{:S(2)}) %collective-permute-start.22) | collective-permute-done | bytes 90144 | tf_op jit(solution)/shard_map/ppermute | solution.py:34
  90.1 1.7 %shard_map.98 = (f32[144,1152]{1,0:T(8,128)}, f32[1,1152]{1,0:T(1,128)S(1)}) custom-call(s32[2]{0:T(128)S(1)} %pad_add_fusion.place, bf16[176,256]{1,0:T(8,128)(2,1)S(1)} %shard_map.97.refs_0_, bf16[176,256]{1,0:T(8,128)(2,1)S(1)} %collective-permute-done.20.refs_1_, bf16[176,256]{1,0:T(8,128)(2,1)S(1)} %collective-permute-done.21.refs_2_, ...), custom_call_target="tpu_custom_call" | custom-call | bytes 1327104 | tf_op jit(solution)/shard_map/pallas_call | solution.py:136
  91.8 0.6 reduce
  (20 shorter events, 0.0 us)
Async XLA Ops:
  0.6 13.4 %collective-permute-start.2 = (bf16[192,1152]{1,0:T(8,128)(2,1)}, bf16[192,1152]{1,0:T(8,128)(2,1)S(1)}, u32[]{:S(2)}, u32[]{:S(2)}) collective-permute-start(bf16[192,1152]{1,0:T(8,128)(2,1)} %bitcast.6), channel_id=1, source_target_pairs={{0,16},{8,24},{16,0},{24,8},{1,17},{9,25},{17,1},{25,9},{2,18},{10... | collective-permute-start | bytes 1327112 | tf_op jit(solution)/shard_map/ppermute | solution.py:34
  14.0 11.6 %collective-permute-start.3 = (bf16[192,1152]{1,0:T(8,128)(2,1)}, bf16[192,1152]{1,0:T(8,128)(2,1)S(1)}, u32[]{:S(2)}, u32[]{:S(2)}) collective-permute-start(bf16[192,1152]{1,0:T(8,128)(2,1)} %bitcast.10), channel_id=1, source_target_pairs={{0,16},{8,24},{16,0},{24,8},{1,17},{9,25},{17,1},{25,9},{2,18},{10... | collective-permute-start | bytes 1327112 | tf_op jit(solution)/shard_map/ppermute | solution.py:34
  15.8 10.7 %collective-permute-start = (bf16[192,1152]{1,0:T(8,128)(2,1)}, bf16[192,1152]{1,0:T(8,128)(2,1)S(1)}, u32[]{:S(2)}, u32[]{:S(2)}) collective-permute-start(bf16[192,1152]{1,0:T(8,128)(2,1)} %bitcast.7), channel_id=1, source_target_pairs={{0,8},{8,0},{16,24},{24,16},{1,9},{9,1},{17,25},{25,17},{2,10},{10... | collective-permute-start | bytes 1327112 | tf_op jit(solution)/shard_map/ppermute | solution.py:34
  15.8 10.7 %collective-permute-start.1 = (bf16[192,1152]{1,0:T(8,128)(2,1)}, bf16[192,1152]{1,0:T(8,128)(2,1)S(1)}, u32[]{:S(2)}, u32[]{:S(2)}) collective-permute-start(bf16[192,1152]{1,0:T(8,128)(2,1)} %bitcast.11), channel_id=1, source_target_pairs={{0,8},{8,0},{16,24},{24,16},{1,9},{9,1},{17,25},{25,17},{2,10},{10... | collective-permute-start | bytes 1327112 | tf_op jit(solution)/shard_map/ppermute | solution.py:34
  16.3 18.1 %collective-permute-start.5 = (bf16[192,1152]{1,0:T(8,128)(2,1)S(1)}, bf16[192,1152]{1,0:T(8,128)(2,1)S(1)}, u32[]{:S(2)}, u32[]{:S(2)}) collective-permute-start(bf16[192,1152]{1,0:T(8,128)(2,1)S(1)} %collective-permute-done.2.f2), channel_id=1, source_target_pairs={{0,8},{8,0},{16,24},{24,16},{1,9},{9,1},{17,25},{25,17},{2,10},{10... | collective-permute-start | bytes 1327112 | tf_op jit(solution)/shard_map/ppermute | solution.py:34
  25.6 15.5 %collective-permute-start.4 = (bf16[192,1152]{1,0:T(8,128)(2,1)S(1)}, bf16[192,1152]{1,0:T(8,128)(2,1)S(1)}, u32[]{:S(2)}, u32[]{:S(2)}) collective-permute-start(bf16[192,1152]{1,0:T(8,128)(2,1)S(1)} %collective-permute-done.3.t2), channel_id=1, source_target_pairs={{0,8},{8,0},{16,24},{24,16},{1,9},{9,1},{17,25},{25,17},{2,10},{10... | collective-permute-start | bytes 1327112 | tf_op jit(solution)/shard_map/ppermute | solution.py:34
  26.4 1.8 %copy-start = (bf16[1152,1152]{1,0:T(8,128)(2,1)S(1)}, bf16[1152,1152]{1,0:T(8,128)(2,1)}, u32[]{:S(2)}) copy-start(bf16[1152,1152]{1,0:T(8,128)(2,1)} %proj.5) | copy-start | bytes 7962628
  28.2 1.0 %copy-start.2 = (bf16[192,1,1152]{2,0,1:T(8,128)(2,1)S(1)}, bf16[192,1,1152]{2,0,1:T(8,128)(2,1)}, u32[]{:S(2)}) copy-start(bf16[192,1,1152]{2,0,1:T(8,128)(2,1)} %param.6) | copy-start | bytes 1327108
  29.2 1.0 %copy-start.4 = (bf16[192,1,1152]{2,0,1:T(8,128)(2,1)S(1)}, bf16[192,1,1152]{2,0,1:T(8,128)(2,1)}, u32[]{:S(2)}) copy-start(bf16[192,1,1152]{2,0,1:T(8,128)(2,1)} %param.7) | copy-start | bytes 1327108
  30.2 4.2 %copy-start.1 = (bf16[1152,1152]{1,0:T(8,128)(2,1)S(1)}, bf16[1152,1152]{1,0:T(8,128)(2,1)}, u32[]{:S(2)}) copy-start(bf16[1152,1152]{1,0:T(8,128)(2,1)} %proj.5) | copy-start | bytes 7962628
  41.0 10.4 %copy-start.3 = (bf16[192,1,1152]{2,0,1:T(8,128)(2,1)S(1)}, bf16[192,1,1152]{2,0,1:T(8,128)(2,1)}, u32[]{:S(2)}) copy-start(bf16[192,1,1152]{2,0,1:T(8,128)(2,1)} %param.6) | copy-start | bytes 1327108
  41.0 10.4 %copy-start.5 = (bf16[192,1,1152]{2,0,1:T(8,128)(2,1)S(1)}, bf16[192,1,1152]{2,0,1:T(8,128)(2,1)}, u32[]{:S(2)}) copy-start(bf16[192,1,1152]{2,0,1:T(8,128)(2,1)} %param.7) | copy-start | bytes 1327108
  46.6 27.1 %collective-permute-start.10 = (bf16[176,256]{1,0:T(8,128)(2,1)S(1)}, bf16[176,256]{1,0:T(8,128)(2,1)S(1)}, u32[]{:S(2)}, u32[]{:S(2)}) collective-permute-start(bf16[176,256]{1,0:T(8,128)(2,1)S(1)} %get-tuple-element.50), channel_id=1, source_target_pairs={{0,5},{1,4},{2,7},{3,6},{4,1},{5,0},{6,3},{7,2},{8,13},{9,12},{10,... | collective-permute-start | bytes 270344 | tf_op jit(solution)/shard_map/ppermute | solution.py:34
  50.1 26.5 %collective-permute-start.11 = (bf16[176,256]{1,0:T(8,128)(2,1)S(1)}, bf16[176,256]{1,0:T(8,128)(2,1)S(1)}, u32[]{:S(2)}, u32[]{:S(2)}) collective-permute-start(bf16[176,256]{1,0:T(8,128)(2,1)S(1)} %get-tuple-element.51), channel_id=1, source_target_pairs={{0,6},{1,7},{2,4},{3,5},{4,2},{5,3},{6,0},{7,1},{8,14},{9,15},{10,... | collective-permute-start | bytes 270344 | tf_op jit(solution)/shard_map/ppermute | solution.py:34
  58.2 3.7 %collective-permute-start.13 = (f32[16,128]{1,0:T(8,128)S(1)}, f32[16,128]{1,0:T(8,128)S(1)}, u32[]{:S(2)}, u32[]{:S(2)}) collective-permute-start(f32[16,128]{1,0:T(8,128)S(1)} %get-tuple-element.53.refs_8_), channel_id=1, source_target_pairs={{0,1},{1,0},{2,3},{3,2},{4,5},{5,4},{6,7},{7,6},{8,9},{9,8},{10,11... | collective-permute-start | bytes 24584 | tf_op jit(solution)/shard_map/ppermute | solution.py:34
  58.7 4.8 %collective-permute-start.14 = (f32[16,128]{1,0:T(8,128)S(1)}, f32[16,128]{1,0:T(8,128)S(1)}, u32[]{:S(2)}, u32[]{:S(2)}) collective-permute-start(f32[16,128]{1,0:T(8,128)S(1)} %get-tuple-element.53.refs_8_), channel_id=1, source_target_pairs={{0,2},{1,3},{2,0},{3,1},{4,6},{5,7},{6,4},{7,5},{8,10},{9,11},{10,... | collective-permute-start | bytes 24584 | tf_op jit(solution)/shard_map/ppermute | solution.py:34
  58.9 6.1 %collective-permute-start.15 = (f32[16,128]{1,0:T(8,128)S(1)}, f32[16,128]{1,0:T(8,128)S(1)}, u32[]{:S(2)}, u32[]{:S(2)}) collective-permute-start(f32[16,128]{1,0:T(8,128)S(1)} %get-tuple-element.53.refs_8_), channel_id=1, source_target_pairs={{0,3},{1,2},{2,1},{3,0},{4,7},{5,6},{6,5},{7,4},{8,11},{9,10},{10,... | collective-permute-start | bytes 24584 | tf_op jit(solution)/shard_map/ppermute | solution.py:34
  61.8 5.4 %collective-permute-start.16 = (f32[16,128]{1,0:T(8,128)S(1)}, f32[16,128]{1,0:T(8,128)S(1)}, u32[]{:S(2)}, u32[]{:S(2)}) collective-permute-start(f32[16,128]{1,0:T(8,128)S(1)} %get-tuple-element.53.refs_8_), channel_id=1, source_target_pairs={{0,4},{1,5},{2,6},{3,7},{4,0},{5,1},{6,2},{7,3},{8,12},{9,13},{10,... | collective-permute-start | bytes 24584 | tf_op jit(solution)/shard_map/ppermute | solution.py:34
  63.5 6.0 %collective-permute-start.17 = (f32[16,128]{1,0:T(8,128)S(1)}, f32[16,128]{1,0:T(8,128)S(1)}, u32[]{:S(2)}, u32[]{:S(2)}) collective-permute-start(f32[16,128]{1,0:T(8,128)S(1)} %get-tuple-element.53.refs_8_), channel_id=1, source_target_pairs={{0,5},{1,4},{2,7},{3,6},{4,1},{5,0},{6,3},{7,2},{8,13},{9,12},{10,... | collective-permute-start | bytes 24584 | tf_op jit(solution)/shard_map/ppermute | solution.py:34
  65.0 6.9 %collective-permute-start.18 = (f32[16,128]{1,0:T(8,128)S(1)}, f32[16,128]{1,0:T(8,128)S(1)}, u32[]{:S(2)}, u32[]{:S(2)}) collective-permute-start(f32[16,128]{1,0:T(8,128)S(1)} %get-tuple-element.53.refs_8_), channel_id=1, source_target_pairs={{0,6},{1,7},{2,4},{3,5},{4,2},{5,3},{6,0},{7,1},{8,14},{9,15},{10,... | collective-permute-start | bytes 24584 | tf_op jit(solution)/shard_map/ppermute | solution.py:34
  67.2 6.5 %collective-permute-start.19 = (f32[16,128]{1,0:T(8,128)S(1)}, f32[16,128]{1,0:T(8,128)S(1)}, u32[]{:S(2)}, u32[]{:S(2)}) collective-permute-start(f32[16,128]{1,0:T(8,128)S(1)} %get-tuple-element.53.refs_8_), channel_id=1, source_target_pairs={{0,7},{1,6},{2,5},{3,4},{4,3},{5,2},{6,1},{7,0},{8,15},{9,14},{10,... | collective-permute-start | bytes 24584 | tf_op jit(solution)/shard_map/ppermute | solution.py:34
  69.5 8.3 %collective-permute-start.12 = (bf16[176,256]{1,0:T(8,128)(2,1)S(1)}, bf16[176,256]{1,0:T(8,128)(2,1)S(1)}, u32[]{:S(2)}, u32[]{:S(2)}) collective-permute-start(bf16[176,256]{1,0:T(8,128)(2,1)S(1)} %get-tuple-element.52), channel_id=1, source_target_pairs={{0,7},{1,6},{2,5},{3,4},{4,3},{5,2},{6,1},{7,0},{8,15},{9,14},{10,... | collective-permute-start | bytes 270344 | tf_op jit(solution)/shard_map/ppermute | solution.py:34
  71.9 6.5 %collective-permute-start.6 = (bf16[176,256]{1,0:T(8,128)(2,1)S(1)}, bf16[176,256]{1,0:T(8,128)(2,1)S(1)}, u32[]{:S(2)}, u32[]{:S(2)}) collective-permute-start(bf16[176,256]{1,0:T(8,128)(2,1)S(1)} %get-tuple-element.46), channel_id=1, source_target_pairs={{0,1},{1,0},{2,3},{3,2},{4,5},{5,4},{6,7},{7,6},{8,9},{9,8},{10,11... | collective-permute-start | bytes 270344 | tf_op jit(solution)/shard_map/ppermute | solution.py:34
  73.6 5.2 %collective-permute-start.7 = (bf16[176,256]{1,0:T(8,128)(2,1)S(1)}, bf16[176,256]{1,0:T(8,128)(2,1)S(1)}, u32[]{:S(2)}, u32[]{:S(2)}) collective-permute-start(bf16[176,256]{1,0:T(8,128)(2,1)S(1)} %get-tuple-element.47), channel_id=1, source_target_pairs={{0,2},{1,3},{2,0},{3,1},{4,6},{5,7},{6,4},{7,5},{8,10},{9,11},{10,... | collective-permute-start | bytes 270344 | tf_op jit(solution)/shard_map/ppermute | solution.py:34
  73.7 6.9 %collective-permute-start.8 = (bf16[176,256]{1,0:T(8,128)(2,1)S(1)}, bf16[176,256]{1,0:T(8,128)(2,1)S(1)}, u32[]{:S(2)}, u32[]{:S(2)}) collective-permute-start(bf16[176,256]{1,0:T(8,128)(2,1)S(1)} %get-tuple-element.48), channel_id=1, source_target_pairs={{0,3},{1,2},{2,1},{3,0},{4,7},{5,6},{6,5},{7,4},{8,11},{9,10},{10,... | collective-permute-start | bytes 270344 | tf_op jit(solution)/shard_map/ppermute | solution.py:34
  76.6 5.9 %collective-permute-start.9 = (bf16[176,256]{1,0:T(8,128)(2,1)S(1)}, bf16[176,256]{1,0:T(8,128)(2,1)S(1)}, u32[]{:S(2)}, u32[]{:S(2)}) collective-permute-start(bf16[176,256]{1,0:T(8,128)(2,1)S(1)} %get-tuple-element.49), channel_id=1, source_target_pairs={{0,4},{1,5},{2,6},{3,7},{4,0},{5,1},{6,2},{7,3},{8,12},{9,13},{10,... | collective-permute-start | bytes 270344 | tf_op jit(solution)/shard_map/ppermute | solution.py:34
  83.2 2.1 %collective-permute-start.20 = (bf16[176,256]{1,0:T(8,128)(2,1)S(1)}, bf16[176,256]{1,0:T(8,128)(2,1)S(1)}, u32[]{:S(2)}, u32[]{:S(2)}) collective-permute-start(bf16[176,256]{1,0:T(8,128)(2,1)S(1)} %shard_map.97.refs_0_), channel_id=1, source_target_pairs={{0,8},{8,0},{16,24},{24,16},{1,9},{9,1},{17,25},{25,17},{2,10},{10... | collective-permute-start | bytes 270344 | tf_op jit(solution)/shard_map/ppermute | solution.py:34
  83.2 5.3 %collective-permute-start.21 = (bf16[176,256]{1,0:T(8,128)(2,1)S(1)}, bf16[176,256]{1,0:T(8,128)(2,1)S(1)}, u32[]{:S(2)}, u32[]{:S(2)}) collective-permute-start(bf16[176,256]{1,0:T(8,128)(2,1)S(1)} %shard_map.97.refs_0_), channel_id=1, source_target_pairs={{0,16},{8,24},{16,0},{24,8},{1,17},{9,25},{17,1},{25,9},{2,18},{10... | collective-permute-start | bytes 270344 | tf_op jit(solution)/shard_map/ppermute | solution.py:34
  85.1 5.0 %collective-permute-start.22 = (bf16[176,256]{1,0:T(8,128)(2,1)S(1)}, bf16[176,256]{1,0:T(8,128)(2,1)S(1)}, u32[]{:S(2)}, u32[]{:S(2)}) collective-permute-start(bf16[176,256]{1,0:T(8,128)(2,1)S(1)} %shard_map.97.refs_0_), channel_id=1, source_target_pairs={{0,24},{8,16},{16,8},{24,0},{1,25},{9,17},{17,9},{25,1},{2,26},{10... | collective-permute-start | bytes 270344 | tf_op jit(solution)/shard_map/ppermute | solution.py:34

commit v3 on v2

--- a/solution.py
+++ b/solution.py
@@ -212,11 +212,18 @@
 
 
 def far_body(
-    scalars, f2, f3, proj, gain, normed_near, unit_near, inverse_near, text_near,
-    normed, unit, inverse, weights, totals, projected, dots,
+    scalars, place, f2, f3, proj, gain, normed_near, unit_near, inverse_near, text_near,
+    normed, unit, inverse, weights, totals, proj_columns, projected, dots,
 ):
     rows = f2.shape[0]
     near = 2 * rows
+    members, columns = proj.shape[1] // proj_columns.shape[1], proj_columns.shape[1]
+    for member in range(members):
+
+        @pl.when(place[0] == member)
+        def _():
+            proj_columns[...] = proj[:, member * columns : (member + 1) * columns]
+
     normed[:near, :] = normed_near[...]
     unit[:near, :] = unit_near[...]
     inverse[:near, :] = inverse_near[...]
@@ -244,17 +251,18 @@
 
 
 def partial_body(
-    members, groups, scalars, place, t2, t3, text_near, unit, inverse, normed, weights_near, totals_near,
-    *refs,
+    members, groups, lead, scalars, place, t2, t3, text_near, unit, inverse, normed, weights_near, totals_near,
+    proj_columns, gain, *refs,
 ):
-    packets, (text_far, weights_own), scratch = refs[:groups], refs[groups : groups + 2], refs[groups + 2 :]
-    weights, totals, dots, text_columns, unit_columns, back, packed = scratch
+    across, keep_lead, keep_tail, *refs = refs
+    along, refs = refs[: groups // 2 - 1], refs[groups // 2 - 1 :]
+    text_far, weights_own, weights, totals, dots, text_columns, unit_columns, back, packed = refs
     rows = t2.shape[0]
     near = 2 * rows
     every = members * rows
     width = unit.shape[1]
     columns = width // members
-    full = packed.shape[2]
+    count, full = packed.shape[1:]
     scale, bias = scalars[0], scalars[1]
     for k, source in enumerate((t2, t3)):
         unit_into(source, text_far, k * rows)
@@ -279,54 +287,71 @@
     product = dot(normed[...], back[...], FIRST) * (1.0 / every)
     for group in range(groups):
         pack_into(packed.at[group], product[group * each : (group + 1) * each, :], full)
-    for step in range(groups):
-        packets[step][...] = packed[place[1] ^ step]
-
-
-def own_body(
-    scalars, features, text, proj, gain, text_near, text_far, weights_own, weights_near, unit, inverse,
-    feature_grad, text_grad, gain_term, back, norm_back,
+
+    terms = product * proj_columns[...].astype(F32)
+    folded = jnp.concatenate([terms[:, full:], jnp.zeros((width, full + LANES - columns), F32)], axis=1)
+    for at in range(0, full, LANES):
+        folded = folded + terms[:, at : at + LANES]
+    high = folded.astype(BF16)
+    low = (folded - high.astype(F32)).astype(BF16)
+    ones = jnp.ones((BAND, 2 * LANES), BF16)
+    gain_row = dot(ones, jnp.concatenate([high, low], axis=1), LAST)[:1, :] / gain[...]
+    pieces = [gain_row[:, at : at + LANES] for at in range(0, width, LANES)]
+    pieces.append(jnp.zeros((BAND - len(pieces), LANES), F32))
+    gain_tile = jnp.concatenate(pieces, axis=0).astype(BF16)
+    for group in range(groups):
+        packed[group, count - BAND :, full - LANES :] = gain_tile
+
+    own = place[1]
+    for step in range(groups // 2):
+        across[step] = packed[own ^ 1 ^ (2 * step), :lead, :]
+        keep_lead[step] = packed[own ^ (2 * step), :lead, :]
+    for other in range(2):
+        keep_tail[other] = packed[own ^ other, lead:, :]
+        for step in range(1, groups // 2):
+            along[step - 1][other] = packed[own ^ (2 * step) ^ other, lead:, :]
+
+
+def image_body(
+    scalars, features, proj, gain, text_near, text_far, weights_own, unit, inverse,
+    feature_grad, back, product,
 ):
     rows, width = features.shape
     near = 2 * rows
     scale = scalars[0]
-    image_back = dot(weights_own[:, :near], text_near[...]) + dot(weights_own[:, near:], text_far[...])
-    norm_back[...] = image_back
+    product[...] = dot(weights_own[:, :near], text_near[...]) + dot(weights_own[:, near:], text_far[...])
 
     def image_chunk(where):
-        values = norm_back[where, :] * scale
+        values = product[where, :] * scale
         direction = unit[where, :].astype(F32)
         back[where, :] = (
             (values - direction * sums(direction * values)) * inverse[where, :]
         ).astype(BF16)
 
     over_rows(rows, 32, image_chunk)
-    norm_back[...] = dot(back[...], proj[...], LAST)
-    gain_term[...] = jnp.zeros_like(gain_term)
-
-    def feature_chunk(index, total):
-        where = pl.ds(pl.multiple_of(index * 32, 32), 32)
+    product[...] = dot(back[...], proj[...], LAST)
+
+    def feature_chunk(where):
         values = features[where, :].astype(F32)
         centred = values - sums(values) * (1.0 / width)
         deviation = lax.rsqrt(sums(centred * centred) * (1.0 / width) + 1e-06)
         xhat = centred * deviation
-        upstream = norm_back[where, :]
-        scaled = upstream * gain[...]
+        scaled = product[where, :] * gain[...]
         feature_grad[where, :] = (
             deviation
             * (scaled - sums(scaled) * (1.0 / width) - xhat * (sums(scaled * xhat) * (1.0 / width)))
         ).astype(BF16)
-        return total + jnp.sum((upstream * xhat).reshape(4, 8, width), axis=0)
-
-    total = lax.fori_loop(0, rows // 32, feature_chunk, jnp.zeros((8, width), F32))
-    total = jnp.sum(total, axis=0, keepdims=True) * (1.0 / unit.shape[0])
-    for at in range(width // LANES):
-        gain_term[at : at + 1, :] = total[:, at * LANES : (at + 1) * LANES]
-
-    norm_back[...] = dot(weights_near[:, :rows], unit[...], FIRST)
+
+    over_rows(rows, 32, feature_chunk)
+
+
+def text_body(scalars, text, weights_near, unit, text_grad, product):
+    rows = text.shape[0]
+    scale = scalars[0]
+    product[...] = dot(weights_near[:, :rows], unit[...], FIRST)
 
     def text_chunk(where):
-        values = norm_back[where, :] * scale
+        values = product[where, :] * scale
         own = text[where, :].astype(F32)
         own_inverse = lax.rsqrt(sums(own * own) + 1e-06)
         direction = own * own_inverse
@@ -337,24 +362,31 @@
     over_rows(rows, 32, text_chunk)
 
 
-def reduce_body(groups, each, place, *refs):
-    packets, terms = refs[:groups], refs[groups : 2 * groups]
-    total, ordered = refs[2 * groups :]
-    count, full = total.shape
-
-    def chunk(where):
-        value = packets[0][where, :].astype(F32)
-        for packet in packets[1:]:
-            value = value + packet[where, :].astype(F32)
-        total[where, :] = value.astype(BF16)
-
-    over_rows(count, BAND, chunk)
-    for step in range(groups):
-        ordered[place[1] ^ step] = terms[step][...]
-    value = ordered[0]
-    for group in range(1, groups):
-        value = value + ordered[group]
-    total[count - BAND :, full - LANES :] = value.astype(BF16)
+def first_sum_body(place, keep_lead, across, keep_tail, *refs):
+    steps = keep_lead.shape[0]
+    along, refs = refs[: steps - 1], refs[steps - 1 :]
+    leads, (tail, tail_across, ordered) = refs[:steps], refs[steps:]
+    for step in range(steps):
+        leads[step][...] = (keep_lead[step].astype(F32) + across[step].astype(F32)).astype(BF16)
+    own = place[1] // 2
+    ordered[own] = keep_tail[...]
+    for step in range(1, steps):
+        ordered[own ^ step] = along[step - 1][...]
+    value = ordered[0].astype(F32)
+    for step in range(1, steps):
+        value = value + ordered[step].astype(F32)
+    tail[...] = value[0].astype(BF16)
+    tail_across[...] = value[1].astype(BF16)
+
+
+def last_sum_body(tail, tail_across, *refs):
+    leads, total = refs[:-1], refs[-1]
+    split = leads[0].shape[0]
+    value = leads[0][...].astype(F32)
+    for lead in leads[1:]:
+        value = value + lead[...].astype(F32)
+    total[:split, :] = value.astype(BF16)
+    total[split:, :] = (tail[...].astype(F32) + tail_across[...].astype(F32)).astype(BF16)
 
 
 def finish_body(members, place, *refs):
@@ -403,14 +435,14 @@
     packet = (each + bands * BAND, full)
     gain_row = gain.reshape(1, width)
 
+    lead = (2 * packet[0] // BAND // 3) * BAND
+    tail = packet[0] - lead
+    steps = groups // 2
+
     f0, t0 = features[:, 0, :], text[:, 0, :]
+    f2 = send(f0, "loop", lambda p: p ^ 2)
     f1 = send(f0, "loop", lambda p: p ^ 1)
     t1 = send(t0, "loop", lambda p: p ^ 1)
-    f2 = send(f0, "loop", lambda p: p ^ 2)
-    t_after, f2 = lax.optimization_barrier((t0, f2))
-    t2 = send(t_after, "loop", lambda p: p ^ 2)
-    f3 = send(f2, "loop", lambda p: p ^ 1)
-    t3 = send(t2, "loop", lambda p: p ^ 1)
 
     normed_near, unit_near, inverse_near, text_near = call(
         near_body,
@@ -420,18 +452,34 @@
         moved=8 * near * width,
     )(f0, f1, t0, t1, proj, gain_row)
 
-    normed, unit, inverse, weights_near, totals_near = call(
+    t_after, f2, normed_near, unit_near, inverse_near, text_near = lax.optimization_barrier(
+        (t0, f2, normed_near, unit_near, inverse_near, text_near)
+    )
+    t2 = send(t_after, "loop", lambda p: p ^ 2)
+    f3 = send(f2, "loop", lambda p: p ^ 1)
+
+    normed, unit, inverse, weights_near, totals_near, proj_columns = call(
         far_body,
-        [((every, width), BF16), ((every, width), BF16), ((every, 1), F32), ((every, near), BF16), ((every, 1), F32)],
+        [
+            ((every, width), BF16), ((every, width), BF16), ((every, 1), F32),
+            ((every, near), BF16), ((every, 1), F32), ((width, columns), BF16),
+        ],
         [pltpu.VMEM((near, width), F32), pltpu.VMEM((every, near), F32)],
-        smem=1,
+        smem=2,
         flops=4 * near * width * width,
         moved=16 * near * width,
-    )(scalars, f2, f3, proj, gain_row, normed_near, unit_near, inverse_near, text_near)
+    )(scalars, place, f2, f3, proj, gain_row, normed_near, unit_near, inverse_near, text_near)
+
+    t2, normed, unit, inverse, weights_near, totals_near, proj_columns = lax.optimization_barrier(
+        (t2, normed, unit, inverse, weights_near, totals_near, proj_columns)
+    )
+    t3 = send(t2, "loop", lambda p: p ^ 1)
 
     outs = call(
-        functools.partial(partial_body, members, groups),
-        [(packet, BF16)] * groups + [((near, width), BF16), ((rows, every), BF16)],
+        functools.partial(partial_body, members, groups, lead),
+        [((steps, lead, full), BF16), ((steps, lead, full), BF16), ((2, tail, full), BF16)]
+        + [((2, tail, full), BF16)] * (steps - 1)
+        + [((near, width), BF16), ((rows, every), BF16)],
         [
             pltpu.VMEM((every, every), BF16),
             pltpu.VMEM((every, 1), F32),
@@ -444,29 +492,51 @@
         smem=2,
         flops=6 * near * width * width,
         moved=16 * near * width,
-    )(scalars, place, t2, t3, text_near, unit, inverse, normed, weights_near, totals_near)
-    packets, (text_far, weights_own) = outs[:groups], outs[groups:]
-    arrived = [packets[0]] + [
-        send(packets[step], "rep", lambda p: p ^ step) for step in range(1, groups)
-    ]
-
-    feature_grad, text_grad, gain_term = call(
-        own_body,
-        [((rows, width), BF16), ((rows, width), BF16), ((BAND, LANES), F32)],
+    )(
+        scalars, place, t2, t3, text_near, unit, inverse, normed, weights_near, totals_near,
+        proj_columns, gain_row,
+    )
+    across, keep_lead, keep_tail = outs[:3]
+    along, (text_far, weights_own) = outs[3 : 2 + steps], outs[2 + steps :]
+
+    along = [send(along[step - 1], "rep", lambda p: p ^ (2 * step)) for step in range(1, steps)]
+    across = send(across, "rep", lambda p: p ^ 1)
+
+    (feature_grad,) = call(
+        image_body,
+        [((rows, width), BF16)],
         [pltpu.VMEM((rows, width), BF16), pltpu.VMEM((rows, width), F32)],
         smem=1,
-        flops=6 * near * width * width,
-        moved=16 * near * width,
-    )(scalars, f0, t0, proj, gain_row, text_near, text_far, weights_own, weights_near, unit, inverse)
-    terms = [gain_term] + [send(gain_term, "rep", lambda p: p ^ step) for step in range(1, groups)]
-
-    (reduced,) = call(
-        functools.partial(reduce_body, groups, each),
-        [(packet, BF16)],
-        [pltpu.VMEM((groups, BAND, LANES), F32)],
+        flops=4 * near * width * width,
+        moved=12 * near * width,
+    )(scalars, f0, proj, gain_row, text_near, text_far, weights_own, unit, inverse)
+    feature_grad, across = lax.optimization_barrier((feature_grad, across))
+
+    outs = call(
+        first_sum_body,
+        [((lead, full), BF16)] * steps + [((tail, full), BF16)] * 2,
+        [pltpu.VMEM((steps, 2, tail, full), BF16)],
         smem=1,
         moved=4 * each * width,
-    )(place, *arrived, *terms)
+    )(place, keep_lead, across, keep_tail, *along)
+    leads = [outs[0]] + [send(outs[step], "rep", lambda p: p ^ (2 * step)) for step in range(1, steps)]
+    tail_across = send(outs[steps + 1], "rep", lambda p: p ^ 1)
+
+    (text_grad,) = call(
+        text_body,
+        [((rows, width), BF16)],
+        [pltpu.VMEM((rows, width), F32)],
+        smem=1,
+        flops=2 * near * width * width,
+        moved=6 * near * width,
+    )(scalars, t0, weights_near, unit)
+    text_grad, tail_across = lax.optimization_barrier((text_grad, tail_across))
+
+    (reduced,) = call(
+        last_sum_body,
+        [(packet, BF16)],
+        moved=4 * each * width,
+    )(outs[steps], tail_across, *leads)
     blocks = [reduced] + [send(reduced, "loop", lambda p: p ^ k) for k in range(1, members)]
 
     proj_grad, gain_gradient = call(

time: 92.7 us -> 68.4 us (0.74)
  waiting for transfers between devices: 29.5 us -> 8.59 us
  starting transfers between devices: 30.2 us -> 18.4 us
  local copies, waits for them, and re-layouts: 4.49 us -> 9.27 us
  Pallas kernels: 25.3 us -> 28.9 us
    ppermute x23 -> x17, waiting for transfers between devices: 29.5 us -> 8.59 us  [send(): return lax.ppermute(value, axis, [(p, target(p)) for p in range(count)])]
    ppermute x23 -> x17, starting transfers between devices: 30.2 us -> 18.4 us  [send(): return lax.ppermute(value, axis, [(p, target(p)) for p in range(count)])]
    unnamed x12 -> x20, local copies, waits for them, and re-layouts: 3.79 us -> 8.57 us
    pallas_call x6 -> x8, Pallas kernels: 25.3 us -> 28.9 us  [run(): pl.pallas_call(body, out_shape=[jax.ShapeDtypeStruct(shape, kind) for sha...]
  transfers between devices with their start and end apart: 23 -> 17, of which waited for: 11 -> 7; matrix products, arithmetic and copies ran while one was open for 1% -> 1% of each run, Pallas kernels for 19% -> 30%
where the time goes in v3:
time: 68.4 us; the launch traced here: 67.9 us
  Pallas kernels  28.9 us (42%)
  starting transfers between devices  18.4 us (27%)
  local copies, waits for them, and re-layouts  9.27 us (14%)
  waiting for transfers between devices  8.59 us (13%)
  between operations  2.01 us (3%)
  other arithmetic  0.77 us (1%)
    pallas_call x8, Pallas kernels, run(): pl.pallas_call(body, out_shape=[jax.ShapeDtypeStruct(shape, kind) for sha...  28.9 us
    ppermute x17, starting transfers between devices, send(): return lax.ppermute(value, axis, [(p, target(p)) for p in range(count)])  18.4 us
    ppermute x17, waiting for transfers between devices, send(): return lax.ppermute(value, axis, [(p, target(p)) for p in range(count)])  8.59 us
    unnamed x20, local copies, waits for them, and re-layouts  8.57 us
  transfers between devices with their start and end apart: 17, of which 7 were waited for; matrix products, arithmetic and copies ran while one was open for 1% of the time, Pallas kernels for 30%

profile of v3, /device:TPU:0, one launch (start us, length us, event | category | flops | bytes accessed | tf_op | source)
XLA Modules:
  0.0 67.9 jit_solution(13335917552042673764)
XLA Ops:
  0.6 0.5 collective-permute-start.1
  1.1 0.1 collective-permute-start.2
  1.2 2.9 %collective-permute-start = (bf16[192,1152]{1,0:T(8,128)(2,1)}, bf16[192,1152]{1,0:T(8,128)(2,1)}, u32[]{:S(2)}, u32[]{:S(2)}) collective-permute-start(bf16[192,1152]{1,0:T(8,128)(2,1)} %bitcast.7), channel_id=1, source_target_pairs={{0,16},{8,24},{16,0},{24,8},{1,17},{9,25},{17,1},{25,9},{2,18},{10... | collective-permute-start | bytes 1327112 | tf_op jit(solution)/shard_map/ppermute | solution.py:34
  4.1 0.7 %reshape.14.gain = f32[1,1152]{1,0:T(1,128)S(1)} reshape(f32[1152]{0:T(1024)} %param.9) | data formatting | bytes 9216 | tf_op jit(solution)/shard_map/reshape | solution.py:436
  4.9 0.0 copy-start
  4.9 1.7 %copy-done = bf16[1152,1152]{1,0:T(8,128)(2,1)S(1)} copy-done((bf16[1152,1152]{1,0:T(8,128)(2,1)S(1)}, bf16[1152,1152]{1,0:T(8,128)(2,1)}, u32[]{:S(2)}) %copy-start) | copy-done | bytes 2654232
  6.6 1.0 %copy-done.2 = bf16[192,1,1152]{2,0,1:T(8,128)(2,1)S(1)} copy-done((bf16[192,1,1152]{2,0,1:T(8,128)(2,1)S(1)}, bf16[192,1,1152]{2,0,1:T(8,128)(2,1)}, u32[]{:S(2)}) %copy-start.2) | copy-done | bytes 442392
  7.6 5.3 %shard_map.93 = (bf16[384,1152]{1,0:T(8,128)(2,1)S(1)}, bf16[384,1152]{1,0:T(8,128)(2,1)S(1)}, f32[384,1]{1,0:T(8,128)S(1)}, bf16[384,1152]{1,0:T(8,128)(2,1)S(1)}) custom-call(bf16[192,1152]{1,0:T(8,128)(2,1)S(1)} %bitcast.8, bf16[192,1152]{1,0:T(8,128)(2,1)S(1)} %collective-permute-done.1.f1, bf16[192,1152]{1,0:T(8,128)(2,1)} %bitcast.1.t0.text, ...), custom_call_target="tpu_custom_call" | custom-call | flops 1019215872 | bytes 3538944 | tf_op jit(solution)/shard_map/pallas_call | solution.py:136
  12.9 0.9 %copy-done.4 = bf16[384,1152]{1,0:T(8,128)(2,1)} copy-done((bf16[384,1152]{1,0:T(8,128)(2,1)}, bf16[384,1152]{1,0:T(8,128)(2,1)S(1)}, u32[]{:S(2)}) %copy-start.4) | copy-done | bytes 884760
  13.9 0.9 %copy-done.6 = bf16[384,1152]{1,0:T(8,128)(2,1)} copy-done((bf16[384,1152]{1,0:T(8,128)(2,1)}, bf16[384,1152]{1,0:T(8,128)(2,1)S(1)}, u32[]{:S(2)}) %copy-start.6) | copy-done | bytes 884760
  14.8 0.7 copy-done.8
  15.5 0.0 collective-permute-done.f2
  15.5 1.6 %collective-permute-start.3 = (bf16[192,1152]{1,0:T(8,128)(2,1)}, bf16[192,1152]{1,0:T(8,128)(2,1)}, u32[]{:S(2)}, u32[]{:S(2)}) collective-permute-start(bf16[192,1152]{1,0:T(8,128)(2,1)} %bitcast.1.t0.text), channel_id=1, source_target_pairs={{0,16},{8,24},{16,0},{24,8},{1,17},{9,25},{17,1},{25,9},{2,18},{10... | collective-permute-start | bytes 1327112 | tf_op jit(solution)/shard_map/ppermute | solution.py:34
  18.3 0.1 pad_add_fusion.place
  18.4 0.1 pad_maximum_fusion.scalars
  18.5 1.2 %copy-done.5 = bf16[384,1152]{1,0:T(8,128)(2,1)S(1)} copy-done((bf16[384,1152]{1,0:T(8,128)(2,1)S(1)}, bf16[384,1152]{1,0:T(8,128)(2,1)}, u32[]{:S(2)}) %copy-start.5) | copy-done | bytes 884760
  19.7 1.2 %copy-done.7 = bf16[384,1152]{1,0:T(8,128)(2,1)S(1)} copy-done((bf16[384,1152]{1,0:T(8,128)(2,1)S(1)}, bf16[384,1152]{1,0:T(8,128)(2,1)}, u32[]{:S(2)}) %copy-start.7) | copy-done | bytes 884760
  20.8 0.9 %copy-done.9 = f32[384,1]{1,0:T(8,128)S(1)} copy-done((f32[384,1]{1,0:T(8,128)S(1)}, f32[384,1]{1,0:T(8,128)}, u32[]{:S(2)}) %copy-start.9) | copy-done | bytes 1560
  21.8 7.4 %shard_map.94 = (bf16[768,1152]{1,0:T(8,128)(2,1)S(1)}, bf16[768,1152]{1,0:T(8,128)(2,1)S(1)}, f32[768,1]{1,0:T(8,128)S(1)}, bf16[768,384]{1,0:T(8,128)(2,1)S(1)...) custom-call(f32[2]{0:T(128)S(1)} %pad_maximum_fusion.scalars, s32[2]{0:T(128)S(1)} %pad_add_fusion.place, ...), custom_call_target="tpu_custom_call" | custom-call | flops 2038431744 | bytes 7077888 | tf_op jit(solution)/shard_map/pallas_call | solution.py:136
  29.1 0.0 collective-permute-done.3.t2
  29.2 0.4 collective-permute-start.5
  29.6 1.6 %collective-permute-done.5.t3 = bf16[192,1152]{1,0:T(8,128)(2,1)S(1)} collective-permute-done((bf16[192,1152]{1,0:T(8,128)(2,1)}, bf16[192,1152]{1,0:T(8,128)(2,1)S(1)}, u32[]{:S(2)}, u32[]{:S(2)}) %collective-permute-start.5) | collective-permute-done | bytes 442400 | tf_op jit(solution)/shard_map/ppermute | solution.py:34
  31.2 6.3 %shard_map.95 = (bf16[4,112,256]{2,1,0:T(8,128)(2,1)S(1)}, bf16[4,112,256]{2,1,0:T(8,128)(2,1)S(1)}, bf16[2,64,256]{2,1,0:T(8,128)(2,1)S(1)}, bf16[2,64,256]{2,1...) custom-call(f32[2]{0:T(128)S(1)} %pad_maximum_fusion.scalars, ...), custom_call_target="tpu_custom_call" | custom-call | flops 3057647616 | bytes 7077888 | tf_op jit(solution)/shard_map/pallas_call | solution.py:136
  37.6 1.6 %collective-permute-start.6 = (bf16[4,112,256]{2,1,0:T(8,128)(2,1)S(1)}, bf16[4,112,256]{2,1,0:T(8,128)(2,1)S(1)}, u32[]{:S(2)}, u32[]{:S(2)}) collective-permute-start(bf16[4,112,256]{2,1,0:T(8,128)(2,1)S(1)} %get-tuple-element.72), channel_id=1, source_target_pairs={{0,1},{1,0},{2,3},{3,2},{4,5},{5,4},{6,7},{7,6},{8,9},{9,8},{10,11... | collective-permute-start | bytes 688136 | tf_op jit(solution)/shard_map/ppermute | solution.py:34
  39.1 1.6 %collective-permute-start.7 = (bf16[2,64,256]{2,1,0:T(8,128)(2,1)S(1)}, bf16[2,64,256]{2,1,0:T(8,128)(2,1)S(1)}, u32[]{:S(2)}, u32[]{:S(2)}) collective-permute-start(bf16[2,64,256]{2,1,0:T(8,128)(2,1)S(1)} %get-tuple-element.77), channel_id=1, source_target_pairs={{0,2},{1,3},{2,0},{3,1},{4,6},{5,7},{6,4},{7,5},{8,10},{9,11},{10,... | collective-permute-start | bytes 196616 | tf_op jit(solution)/shard_map/ppermute | solution.py:34
  40.7 2.6 %collective-permute-start.8 = (bf16[2,64,256]{2,1,0:T(8,128)(2,1)S(1)}, bf16[2,64,256]{2,1,0:T(8,128)(2,1)S(1)}, u32[]{:S(2)}, u32[]{:S(2)}) collective-permute-start(bf16[2,64,256]{2,1,0:T(8,128)(2,1)S(1)} %get-tuple-element.78), channel_id=1, source_target_pairs={{0,4},{1,5},{2,6},{3,7},{4,0},{5,1},{6,2},{7,3},{8,12},{9,13},{10,... | collective-permute-start | bytes 196616 | tf_op jit(solution)/shard_map/ppermute | solution.py:34
  43.3 0.2 collective-permute-start.9
  43.5 4.6 %shard_map.96 = bf16[192,1152]{1,0:T(8,128)(2,1)} custom-call(f32[2]{0:T(128)S(1)} %pad_maximum_fusion.scalars, bf16[192,1152]{1,0:T(8,128)(2,1)S(1)} %bitcast.9, bf16[1152,1152]{1,0:T(8,128)(2,1)S(1)} %copy-done.1, f32[1,1152]{1,0:T(1,128)S(1)} %reshape.14.gain, bf16[384,1152]{1,0:T(8,128)(2,1)S(1)} %get-tuple-element.51.text_near, ...), custom_call_target="tpu_custom_call" | custom-call | flops 2038431744 | bytes 5308416 | tf_op jit(solution)/shard_map/pallas_call | solution.py:136
  48.1 0.0 collective-permute-done.7.refs_0_
  48.1 0.3 collective-permute-done.8.refs_1_
  48.4 1.0 %collective-permute-done.9.refs_2_ = bf16[2,64,256]{2,1,0:T(8,128)(2,1)S(1)} collective-permute-done((bf16[2,64,256]{2,1,0:T(8,128)(2,1)S(1)}, bf16[2,64,256]{2,1,0:T(8,128)(2,1)S(1)}, u32[]{:S(2)}, u32[]{:S(2)}) %collective-permute-start.9) | collective-permute-done | bytes 65568 | tf_op jit(solution)/shard_map/ppermute | solution.py:34
  49.4 0.6 shard_map.98
  50.1 1.3 %collective-permute-start.11 = (bf16[112,256]{1,0:T(8,128)(2,1)S(1)}, bf16[112,256]{1,0:T(8,128)(2,1)S(1)}, u32[]{:S(2)}, u32[]{:S(2)}) collective-permute-start(bf16[112,256]{1,0:T(8,128)(2,1)S(1)} %get-tuple-element.85), channel_id=1, source_target_pairs={{0,2},{1,3},{2,0},{3,1},{4,6},{5,7},{6,4},{7,5},{8,10},{9,11},{10,... | collective-permute-start | bytes 172040 | tf_op jit(solution)/shard_map/ppermute | solution.py:34
  51.4 1.7 %collective-permute-start.12 = (bf16[112,256]{1,0:T(8,128)(2,1)S(1)}, bf16[112,256]{1,0:T(8,128)(2,1)S(1)}, u32[]{:S(2)}, u32[]{:S(2)}) collective-permute-start(bf16[112,256]{1,0:T(8,128)(2,1)S(1)} %get-tuple-element.86), channel_id=1, source_target_pairs={{0,4},{1,5},{2,6},{3,7},{4,0},{5,1},{6,2},{7,3},{8,12},{9,13},{10,... | collective-permute-start | bytes 172040 | tf_op jit(solution)/shard_map/ppermute | solution.py:34
  53.1 1.5 %collective-permute-start.13 = (bf16[112,256]{1,0:T(8,128)(2,1)S(1)}, bf16[112,256]{1,0:T(8,128)(2,1)S(1)}, u32[]{:S(2)}, u32[]{:S(2)}) collective-permute-start(bf16[112,256]{1,0:T(8,128)(2,1)S(1)} %get-tuple-element.87), channel_id=1, source_target_pairs={{0,6},{1,7},{2,4},{3,5},{4,2},{5,3},{6,0},{7,1},{8,14},{9,15},{10,... | collective-permute-start | bytes 172040 | tf_op jit(solution)/shard_map/ppermute | solution.py:34
  54.5 0.5 collective-permute-start.10
  55.0 3.0 %shard_map.97 = bf16[192,1152]{1,0:T(8,128)(2,1)} custom-call(f32[2]{0:T(128)S(1)} %pad_maximum_fusion.scalars, bf16[192,1152]{1,0:T(8,128)(2,1)} %bitcast.1.t0.text, bf16[768,384]{1,0:T(8,128)(2,1)S(1)} %get-tuple-element.67.weights_near, bf16[768,1152]{1,0:T(8,128)(2,1)S(1)} %get-tuple-element.64.unit), custom_call_target="tpu_custom_call" | custom-call | flops 1019215872 | bytes 2654208 | tf_op jit(solution)/shard_map/pallas_call | solution.py:136
  58.0 0.4 collective-permute-done.10.tail_across
  58.4 0.0 collective-permute-done.11.refs_1_
  58.4 0.6 collective-permute-done.13.refs_3_
  59.1 0.1 collective-permute-start.14
  59.2 1.2 %collective-permute-start.15 = (bf16[176,256]{1,0:T(8,128)(2,1)S(1)}, bf16[176,256]{1,0:T(8,128)(2,1)S(1)}, u32[]{:S(2)}, u32[]{:S(2)}) collective-permute-start(bf16[176,256]{1,0:T(8,128)(2,1)S(1)} %shard_map.99.refs_0_), channel_id=1, source_target_pairs={{0,16},{8,24},{16,0},{24,8},{1,17},{9,25},{17,1},{25,9},{2,18},{10... | collective-permute-start | bytes 270344 | tf_op jit(solution)/shard_map/ppermute | solution.py:34
  60.3 0.7 collective-permute-start.16
  61.0 0.0 collective-permute-done.14.refs_1_
  61.0 3.6 %collective-permute-done.15.refs_2_ = bf16[176,256]{1,0:T(8,128)(2,1)S(1)} collective-permute-done((bf16[176,256]{1,0:T(8,128)(2,1)S(1)}, bf16[176,256]{1,0:T(8,128)(2,1)S(1)}, u32[]{:S(2)}, u32[]{:S(2)}) %collective-permute-start.15) | collective-permute-done | bytes 90144 | tf_op jit(solution)/shard_map/ppermute | solution.py:34
  64.6 1.0 %collective-permute-done.16.refs_3_ = bf16[176,256]{1,0:T(8,128)(2,1)S(1)} collective-permute-done((bf16[176,256]{1,0:T(8,128)(2,1)S(1)}, bf16[176,256]{1,0:T(8,128)(2,1)S(1)}, u32[]{:S(2)}, u32[]{:S(2)}) %collective-permute-start.16) | collective-permute-done | bytes 90144 | tf_op jit(solution)/shard_map/ppermute | solution.py:34
  65.7 1.7 %shard_map.100 = (f32[144,1152]{1,0:T(8,128)}, f32[1,1152]{1,0:T(1,128)S(1)}) custom-call(s32[2]{0:T(128)S(1)} %pad_add_fusion.place, bf16[176,256]{1,0:T(8,128)(2,1)S(1)} %shard_map.99.refs_0_, bf16[176,256]{1,0:T(8,128)(2,1)S(1)} %collective-permute-done.14.refs_1_, bf16[176,256]{1,0:T(8,128)(2,1)S(1)} %collective-permute-done.15.refs_2_, ...), custom_call_target="tpu_custom_call" | custom-call | bytes 1327104 | tf_op jit(solution)/shard_map/pallas_call | solution.py:136
  67.3 0.6 reduce
  (18 shorter events, 0.1 us)
Async XLA Ops:
  0.6 4.2 %collective-permute-start.1 = (bf16[192,1152]{1,0:T(8,128)(2,1)}, bf16[192,1152]{1,0:T(8,128)(2,1)S(1)}, u32[]{:S(2)}, u32[]{:S(2)}) collective-permute-start(bf16[192,1152]{1,0:T(8,128)(2,1)} %bitcast.6), channel_id=1, source_target_pairs={{0,8},{8,0},{16,24},{24,16},{1,9},{9,1},{17,25},{25,17},{2,10},{10... | collective-permute-start | bytes 1327112 | tf_op jit(solution)/shard_map/ppermute | solution.py:34
  1.1 3.7 %collective-permute-start.2 = (bf16[192,1152]{1,0:T(8,128)(2,1)}, bf16[192,1152]{1,0:T(8,128)(2,1)S(1)}, u32[]{:S(2)}, u32[]{:S(2)}) collective-permute-start(bf16[192,1152]{1,0:T(8,128)(2,1)} %bitcast.1.t0.text), channel_id=1, source_target_pairs={{0,8},{8,0},{16,24},{24,16},{1,9},{9,1},{17,25},{25,17},{2,10},{10... | collective-permute-start | bytes 1327112 | tf_op jit(solution)/shard_map/ppermute | solution.py:34
  1.2 14.2 %collective-permute-start = (bf16[192,1152]{1,0:T(8,128)(2,1)}, bf16[192,1152]{1,0:T(8,128)(2,1)}, u32[]{:S(2)}, u32[]{:S(2)}) collective-permute-start(bf16[192,1152]{1,0:T(8,128)(2,1)} %bitcast.7), channel_id=1, source_target_pairs={{0,16},{8,24},{16,0},{24,8},{1,17},{9,25},{17,1},{25,9},{2,18},{10... | collective-permute-start | bytes 1327112 | tf_op jit(solution)/shard_map/ppermute | solution.py:34
  4.9 1.8 %copy-start = (bf16[1152,1152]{1,0:T(8,128)(2,1)S(1)}, bf16[1152,1152]{1,0:T(8,128)(2,1)}, u32[]{:S(2)}) copy-start(bf16[1152,1152]{1,0:T(8,128)(2,1)} %proj.5) | copy-start | bytes 7962628
  6.6 1.0 %copy-start.2 = (bf16[192,1,1152]{2,0,1:T(8,128)(2,1)S(1)}, bf16[192,1,1152]{2,0,1:T(8,128)(2,1)}, u32[]{:S(2)}) copy-start(bf16[192,1,1152]{2,0,1:T(8,128)(2,1)} %param.6) | copy-start | bytes 1327108
  7.6 10.9 %copy-start.1 = (bf16[1152,1152]{1,0:T(8,128)(2,1)S(1)}, bf16[1152,1152]{1,0:T(8,128)(2,1)}, u32[]{:S(2)}) copy-start(bf16[1152,1152]{1,0:T(8,128)(2,1)} %proj.5) | copy-start | bytes 7962628
  12.9 0.9 %copy-start.4 = (bf16[384,1152]{1,0:T(8,128)(2,1)}, bf16[384,1152]{1,0:T(8,128)(2,1)S(1)}, u32[]{:S(2)}) copy-start(bf16[384,1152]{1,0:T(8,128)(2,1)S(1)} %get-tuple-element.54.normed_near) | copy-start | bytes 2654212
  13.9 0.9 %copy-start.6 = (bf16[384,1152]{1,0:T(8,128)(2,1)}, bf16[384,1152]{1,0:T(8,128)(2,1)S(1)}, u32[]{:S(2)}) copy-start(bf16[384,1152]{1,0:T(8,128)(2,1)S(1)} %get-tuple-element.55.unit_near) | copy-start | bytes 2654212
  14.8 0.7 copy-start.8
  15.5 3.0 %collective-permute-start.4 = (bf16[192,1152]{1,0:T(8,128)(2,1)}, bf16[192,1152]{1,0:T(8,128)(2,1)}, u32[]{:S(2)}, u32[]{:S(2)}) collective-permute-start(bf16[192,1152]{1,0:T(8,128)(2,1)} %collective-permute-done.f2), channel_id=1, source_target_pairs={{0,8},{8,0},{16,24},{24,16},{1,9},{9,1},{17,25},{25,17},{2,10},{10... | collective-permute-start | bytes 1327112 | tf_op jit(solution)/shard_map/ppermute | solution.py:34
  15.5 13.7 %collective-permute-start.3 = (bf16[192,1152]{1,0:T(8,128)(2,1)}, bf16[192,1152]{1,0:T(8,128)(2,1)}, u32[]{:S(2)}, u32[]{:S(2)}) collective-permute-start(bf16[192,1152]{1,0:T(8,128)(2,1)} %bitcast.1.t0.text), channel_id=1, source_target_pairs={{0,16},{8,24},{16,0},{24,8},{1,17},{9,25},{17,1},{25,9},{2,18},{10... | collective-permute-start | bytes 1327112 | tf_op jit(solution)/shard_map/ppermute | solution.py:34
  18.5 1.2 %copy-start.5 = (bf16[384,1152]{1,0:T(8,128)(2,1)S(1)}, bf16[384,1152]{1,0:T(8,128)(2,1)}, u32[]{:S(2)}) copy-start(bf16[384,1152]{1,0:T(8,128)(2,1)} %copy-done.4) | copy-start | bytes 2654212
  19.7 1.2 %copy-start.7 = (bf16[384,1152]{1,0:T(8,128)(2,1)S(1)}, bf16[384,1152]{1,0:T(8,128)(2,1)}, u32[]{:S(2)}) copy-start(bf16[384,1152]{1,0:T(8,128)(2,1)} %copy-done.6) | copy-start | bytes 2654212
  20.8 0.9 %copy-start.9 = (f32[384,1]{1,0:T(8,128)S(1)}, f32[384,1]{1,0:T(8,128)}, u32[]{:S(2)}) copy-start(f32[384,1]{1,0:T(8,128)} %copy-done.8) | copy-start | bytes 4612
  29.1 14.4 %copy-start.3 = (bf16[192,1,1152]{2,0,1:T(8,128)(2,1)S(1)}, bf16[192,1,1152]{2,0,1:T(8,128)(2,1)}, u32[]{:S(2)}) copy-start(bf16[192,1,1152]{2,0,1:T(8,128)(2,1)} %param.6) | copy-start | bytes 1327108
  29.2 2.1 %collective-permute-start.5 = (bf16[192,1152]{1,0:T(8,128)(2,1)}, bf16[192,1152]{1,0:T(8,128)(2,1)S(1)}, u32[]{:S(2)}, u32[]{:S(2)}) collective-permute-start(bf16[192,1152]{1,0:T(8,128)(2,1)} %collective-permute-done.3.t2), channel_id=1, source_target_pairs={{0,8},{8,0},{16,24},{24,16},{1,9},{9,1},{17,25},{25,17},{2,10},{10... | collective-permute-start | bytes 1327112 | tf_op jit(solution)/shard_map/ppermute | solution.py:34
  37.6 10.5 %collective-permute-start.6 = (bf16[4,112,256]{2,1,0:T(8,128)(2,1)S(1)}, bf16[4,112,256]{2,1,0:T(8,128)(2,1)S(1)}, u32[]{:S(2)}, u32[]{:S(2)}) collective-permute-start(bf16[4,112,256]{2,1,0:T(8,128)(2,1)S(1)} %get-tuple-element.72), channel_id=1, source_target_pairs={{0,1},{1,0},{2,3},{3,2},{4,5},{5,4},{6,7},{7,6},{8,9},{9,8},{10,11... | collective-permute-start | bytes 688136 | tf_op jit(solution)/shard_map/ppermute | solution.py:34
  39.1 9.0 %collective-permute-start.7 = (bf16[2,64,256]{2,1,0:T(8,128)(2,1)S(1)}, bf16[2,64,256]{2,1,0:T(8,128)(2,1)S(1)}, u32[]{:S(2)}, u32[]{:S(2)}) collective-permute-start(bf16[2,64,256]{2,1,0:T(8,128)(2,1)S(1)} %get-tuple-element.77), channel_id=1, source_target_pairs={{0,2},{1,3},{2,0},{3,1},{4,6},{5,7},{6,4},{7,5},{8,10},{9,11},{10,... | collective-permute-start | bytes 196616 | tf_op jit(solution)/shard_map/ppermute | solution.py:34
  40.7 7.7 %collective-permute-start.8 = (bf16[2,64,256]{2,1,0:T(8,128)(2,1)S(1)}, bf16[2,64,256]{2,1,0:T(8,128)(2,1)S(1)}, u32[]{:S(2)}, u32[]{:S(2)}) collective-permute-start(bf16[2,64,256]{2,1,0:T(8,128)(2,1)S(1)} %get-tuple-element.78), channel_id=1, source_target_pairs={{0,4},{1,5},{2,6},{3,7},{4,0},{5,1},{6,2},{7,3},{8,12},{9,13},{10,... | collective-permute-start | bytes 196616 | tf_op jit(solution)/shard_map/ppermute | solution.py:34
  43.3 6.1 %collective-permute-start.9 = (bf16[2,64,256]{2,1,0:T(8,128)(2,1)S(1)}, bf16[2,64,256]{2,1,0:T(8,128)(2,1)S(1)}, u32[]{:S(2)}, u32[]{:S(2)}) collective-permute-start(bf16[2,64,256]{2,1,0:T(8,128)(2,1)S(1)} %get-tuple-element.79), channel_id=1, source_target_pairs={{0,6},{1,7},{2,4},{3,5},{4,2},{5,3},{6,0},{7,1},{8,14},{9,15},{10,... | collective-permute-start | bytes 196616 | tf_op jit(solution)/shard_map/ppermute | solution.py:34
  50.1 8.4 %collective-permute-start.11 = (bf16[112,256]{1,0:T(8,128)(2,1)S(1)}, bf16[112,256]{1,0:T(8,128)(2,1)S(1)}, u32[]{:S(2)}, u32[]{:S(2)}) collective-permute-start(bf16[112,256]{1,0:T(8,128)(2,1)S(1)} %get-tuple-element.85), channel_id=1, source_target_pairs={{0,2},{1,3},{2,0},{3,1},{4,6},{5,7},{6,4},{7,5},{8,10},{9,11},{10,... | collective-permute-start | bytes 172040 | tf_op jit(solution)/shard_map/ppermute | solution.py:34
  51.4 7.1 %collective-permute-start.12 = (bf16[112,256]{1,0:T(8,128)(2,1)S(1)}, bf16[112,256]{1,0:T(8,128)(2,1)S(1)}, u32[]{:S(2)}, u32[]{:S(2)}) collective-permute-start(bf16[112,256]{1,0:T(8,128)(2,1)S(1)} %get-tuple-element.86), channel_id=1, source_target_pairs={{0,4},{1,5},{2,6},{3,7},{4,0},{5,1},{6,2},{7,3},{8,12},{9,13},{10,... | collective-permute-start | bytes 172040 | tf_op jit(solution)/shard_map/ppermute | solution.py:34
  53.1 6.0 %collective-permute-start.13 = (bf16[112,256]{1,0:T(8,128)(2,1)S(1)}, bf16[112,256]{1,0:T(8,128)(2,1)S(1)}, u32[]{:S(2)}, u32[]{:S(2)}) collective-permute-start(bf16[112,256]{1,0:T(8,128)(2,1)S(1)} %get-tuple-element.87), channel_id=1, source_target_pairs={{0,6},{1,7},{2,4},{3,5},{4,2},{5,3},{6,0},{7,1},{8,14},{9,15},{10,... | collective-permute-start | bytes 172040 | tf_op jit(solution)/shard_map/ppermute | solution.py:34
  54.5 3.9 %collective-permute-start.10 = (bf16[64,256]{1,0:T(8,128)(2,1)S(1)}, bf16[64,256]{1,0:T(8,128)(2,1)S(1)}, u32[]{:S(2)}, u32[]{:S(2)}) collective-permute-start(bf16[64,256]{1,0:T(8,128)(2,1)S(1)} %get-tuple-element.80), channel_id=1, source_target_pairs={{0,1},{1,0},{2,3},{3,2},{4,5},{5,4},{6,7},{7,6},{8,9},{9,8},{10,11... | collective-permute-start | bytes 98312 | tf_op jit(solution)/shard_map/ppermute | solution.py:34
  59.1 1.9 %collective-permute-start.14 = (bf16[176,256]{1,0:T(8,128)(2,1)S(1)}, bf16[176,256]{1,0:T(8,128)(2,1)S(1)}, u32[]{:S(2)}, u32[]{:S(2)}) collective-permute-start(bf16[176,256]{1,0:T(8,128)(2,1)S(1)} %shard_map.99.refs_0_), channel_id=1, source_target_pairs={{0,8},{8,0},{16,24},{24,16},{1,9},{9,1},{17,25},{25,17},{2,10},{10... | collective-permute-start | bytes 270344 | tf_op jit(solution)/shard_map/ppermute | solution.py:34
  59.2 5.5 %collective-permute-start.15 = (bf16[176,256]{1,0:T(8,128)(2,1)S(1)}, bf16[176,256]{1,0:T(8,128)(2,1)S(1)}, u32[]{:S(2)}, u32[]{:S(2)}) collective-permute-start(bf16[176,256]{1,0:T(8,128)(2,1)S(1)} %shard_map.99.refs_0_), channel_id=1, source_target_pairs={{0,16},{8,24},{16,0},{24,8},{1,17},{9,25},{17,1},{25,9},{2,18},{10... | collective-permute-start | bytes 270344 | tf_op jit(solution)/shard_map/ppermute | solution.py:34
  60.3 5.3 %collective-permute-start.16 = (bf16[176,256]{1,0:T(8,128)(2,1)S(1)}, bf16[176,256]{1,0:T(8,128)(2,1)S(1)}, u32[]{:S(2)}, u32[]{:S(2)}) collective-permute-start(bf16[176,256]{1,0:T(8,128)(2,1)S(1)} %shard_map.99.refs_0_), channel_id=1, source_target_pairs={{0,24},{8,16},{16,8},{24,0},{1,25},{9,17},{17,9},{25,1},{2,26},{10... | collective-permute-start | bytes 270344 | tf_op jit(solution)/shard_map/ppermute | solution.py:34

commit v4 on v3

--- a/solution.py
+++ b/solution.py
@@ -126,6 +126,7 @@
 
 VMEM = pl.BlockSpec(memory_space=pltpu.VMEM)
 SMEM = pl.BlockSpec(memory_space=pltpu.SMEM)
+ANYWHERE = pl.BlockSpec(memory_space=pl.ANY)
 LANES = 128
 BAND = 16
 
@@ -139,11 +140,43 @@
             in_specs=specs,
             out_specs=[VMEM] * len(outs),
             scratch_shapes=list(scratch),
-            compiler_params=pltpu.CompilerParams(vmem_limit_bytes=36 * 2**20),
+            compiler_params=pltpu.CompilerParams(vmem_limit_bytes=24 * 2**20),
             cost_estimate=pl.CostEstimate(flops=flops, bytes_accessed=moved, transcendentals=0),
         )(*operands)
 
     return run
+
+
+def call_moving(body, outs, scratch, copies, smem=0, flops=0, moved=0):
+    def run(*operands):
+        specs = [SMEM] * smem + [ANYWHERE] * (len(operands) - smem)
+        return pl.pallas_call(
+            body,
+            out_shape=[jax.ShapeDtypeStruct(shape, kind) for shape, kind in outs],
+            in_specs=specs,
+            out_specs=[ANYWHERE] * len(outs),
+            scratch_shapes=list(scratch) + [pltpu.SemaphoreType.DMA((copies,))],
+            compiler_params=pltpu.CompilerParams(vmem_limit_bytes=56 * 2**20),
+            cost_estimate=pl.CostEstimate(flops=flops, bytes_accessed=moved, transcendentals=0),
+        )(*operands)
+
+    return run
+
+
+class Mover:
+    def __init__(self, semaphores):
+        self.semaphores, self.used = semaphores, 0
+
+    def __call__(self, source, target):
+        copy = pltpu.make_async_copy(source, target, self.semaphores.at[self.used])
+        self.used += 1
+        copy.start()
+        return copy
+
+
+def wait_all(*copies):
+    for copy in copies:
+        copy.wait()
 
 
 def over_rows(count, step, body):
@@ -151,7 +184,7 @@
         body(pl.ds(pl.multiple_of(index * step, step), step))
         return 0
 
-    lax.fori_loop(0, count // step, turn, 0, unroll=2)
+    lax.fori_loop(0, count // step, turn, 0, unroll=min(4, count // step))
 
 
 def sums(values):
@@ -184,55 +217,126 @@
     over_rows(rows, 32, chunk)
 
 
-def weigh(dots, scale, bias, first_column, weights, columns_at, totals, add_to):
-    rows, columns = dots.shape
-
+def weigh(dots, scale, bias, diagonal, weights, totals, add_to=None):
     def chunk(where):
         product = dots[where, :]
-        logits = scale * product + bias
-        weight = 1.0 / (1.0 + jnp.exp(-logits))
-        row = where.start + lax.broadcasted_iota(jnp.int32, product.shape, 0)
-        column = first_column + lax.broadcasted_iota(jnp.int32, product.shape, 1)
-        weight = jnp.where(row == column, weight - 1.0, weight).astype(BF16)
-        weights[where, columns_at : columns_at + columns] = weight
+        weight = 1.0 / (1.0 + jnp.exp(-(scale * product + bias)))
+        if diagonal is not None:
+            row = where.start + lax.broadcasted_iota(jnp.int32, product.shape, 0)
+            column = diagonal + lax.broadcasted_iota(jnp.int32, product.shape, 1)
+            weight = jnp.where(row == column, weight - 1.0, weight)
+        weight = weight.astype(BF16)
+        weights[where, :] = weight
         total = sums(weight.astype(F32) * product)
         totals[where, :] = total if add_to is None else add_to[where, :] + total
 
-    over_rows(rows, 64, chunk)
-
-
-def near_body(f0, f1, t0, t1, proj, gain, normed, unit, inverse, text_unit, projected):
-    rows = f0.shape[0]
-    for k, source in enumerate((f0, f1)):
-        normalize_into(source, gain, normed, k * rows)
-    for k, source in enumerate((t0, t1)):
-        unit_into(source, text_unit, k * rows)
-    projected[...] = dot(normed[...], proj[...])
-    unit_into(projected, unit, 0, inverse)
-
-
-def far_body(
-    scalars, place, f2, f3, proj, gain, normed_near, unit_near, inverse_near, text_near,
-    normed, unit, inverse, weights, totals, proj_columns, projected, dots,
-):
-    rows = f2.shape[0]
-    near = 2 * rows
-    members, columns = proj.shape[1] // proj_columns.shape[1], proj_columns.shape[1]
-    for member in range(members):
+    over_rows(dots.shape[0], 64, chunk)
+
+
+def take_columns(place, source, target):
+    columns = target.shape[1]
+    for member in range(source.shape[1] // columns):
 
         @pl.when(place[0] == member)
         def _():
-            proj_columns[...] = proj[:, member * columns : (member + 1) * columns]
-
-    normed[:near, :] = normed_near[...]
-    unit[:near, :] = unit_near[...]
-    inverse[:near, :] = inverse_near[...]
-    for k, source in enumerate((f2, f3)):
-        normalize_into(source, gain, normed, near + k * rows)
-    projected[...] = dot(normed[near:, :], proj[...])
-    unit_into(projected, unit, near, inverse)
-    dots[...] = dot(unit[...], text_near[...], LAST)
-    weigh(dots, scalars[0], scalars[1], 0, weights, 0, totals, None)
+            target[...] = source[:, member * columns : (member + 1) * columns]
+
+
+def near_body(
+    scalars, place, f0, f1, t0, t1, proj, gain,
+    normed, normed_turned, unit, unit_columns, inverse, text_unit, text_columns, weights, totals, proj_columns,
+    f0_v, f1_v, t0_v, t1_v, proj_v, gain_v, normed_v, turned_v, unit_v, unit_columns_v, inverse_v, text_v,
+    text_columns_v, weights_v, totals_v, proj_columns_v, projected, dots, semaphores,
+):
+    move = Mover(semaphores)
+    rows = f0.shape[0]
+    gain_in, f0_in, f1_in = move(gain, gain_v), move(f0, f0_v), move(f1, f1_v)
+    proj_in, t0_in, t1_in = move(proj, proj_v), move(t0, t0_v), move(t1, t1_v)
+    wait_all(gain_in, f0_in)
+    normalize_into(f0_v, gain_v, normed_v, 0)
+    f1_in.wait()
+    normalize_into(f1_v, gain_v, normed_v, rows)
+    out = [move(normed_v, normed)]
+    proj_in.wait()
+    projected[...] = dot(normed_v[...], proj_v[...])
+    t0_in.wait()
+    unit_into(t0_v, text_v, 0)
+    t1_in.wait()
+    unit_into(t1_v, text_v, rows)
+    out.append(move(text_v, text_unit))
+    unit_into(projected, unit_v, 0, inverse_v)
+    out += [move(unit_v, unit), move(inverse_v, inverse)]
+    dots[...] = dot(unit_v[...], text_v[...], LAST)
+    weigh(dots, scalars[0], scalars[1], 0, weights_v, totals_v)
+    out += [move(weights_v, weights), move(totals_v, totals)]
+    take_columns(place, unit_v, unit_columns_v)
+    take_columns(place, text_v, text_columns_v)
+    take_columns(place, proj_v, proj_columns_v)
+    out += [move(unit_columns_v, unit_columns), move(text_columns_v, text_columns)]
+    out += [move(proj_columns_v, proj_columns)]
+    turned_v[...] = normed_v[...].T
+    out.append(move(turned_v, normed_turned))
+    wait_all(*out)
+
+
+def far_body(
+    scalars, place, f2, f3, proj, gain, text_near,
+    normed_turned, unit, unit_columns, inverse, weights, totals,
+    f2_v, f3_v, proj_v, gain_v, text_v, normed_v, turned_v, unit_v, unit_columns_v, inverse_v, weights_v, totals_v,
+    projected, dots, semaphores,
+):
+    move = Mover(semaphores)
+    rows = f2.shape[0]
+    gain_in, f2_in, f3_in = move(gain, gain_v), move(f2, f2_v), move(f3, f3_v)
+    proj_in, text_in = move(proj, proj_v), move(text_near, text_v)
+    wait_all(gain_in, f2_in)
+    normalize_into(f2_v, gain_v, normed_v, 0)
+    f3_in.wait()
+    normalize_into(f3_v, gain_v, normed_v, rows)
+    proj_in.wait()
+    projected[...] = dot(normed_v[...], proj_v[...])
+    unit_into(projected, unit_v, 0, inverse_v)
+    out = [move(unit_v, unit), move(inverse_v, inverse)]
+    text_in.wait()
+    dots[...] = dot(unit_v[...], text_v[...], LAST)
+    weigh(dots, scalars[0], scalars[1], None, weights_v, totals_v)
+    out += [move(weights_v, weights), move(totals_v, totals)]
+    take_columns(place, unit_v, unit_columns_v)
+    out.append(move(unit_columns_v, unit_columns))
+    turned_v[...] = normed_v[...].T
+    out.append(move(turned_v, normed_turned))
+    wait_all(*out)
+
+
+def third_body(
+    scalars, place, t2, unit_near, unit_far, weights_near, weights_far, totals_near, totals_far, text_columns_near,
+    text_unit, weights_own, image_back, totals,
+    t2_v, unit_v, weights_near_v, totals_v, text_columns_v, text_v, weights_v, back_v, dots, semaphores,
+):
+    move = Mover(semaphores)
+    rows = t2.shape[0]
+    near = 2 * rows
+    t2_in = move(t2, t2_v)
+    unit_in = [move(unit_near, unit_v.at[:near]), move(unit_far, unit_v.at[near:])]
+    totals_in = [move(totals_near, totals_v.at[:near]), move(totals_far, totals_v.at[near:])]
+    rest_in = [
+        move(weights_near, weights_near_v.at[:near]),
+        move(weights_far, weights_near_v.at[near:]),
+        move(text_columns_near, text_columns_v.at[:near]),
+    ]
+    t2_in.wait()
+    unit_into(t2_v, text_v, 0)
+    out = [move(text_v, text_unit)]
+    take_columns(place, text_v, text_columns_v.at[near : near + rows])
+    wait_all(*unit_in)
+    dots[...] = dot(unit_v[...], text_v[...], LAST)
+    wait_all(*totals_in)
+    weigh(dots, scalars[0], scalars[1], near, weights_v, totals_v, totals_v)
+    out += [move(totals_v, totals), move(weights_v.at[:rows], weights_own)]
+    wait_all(*rest_in)
+    back_v[...] = dot(weights_near_v[...], text_columns_v[:near, :]) + dot(weights_v[...], text_columns_v[near:, :])
+    out.append(move(back_v, image_back))
+    wait_all(*out)
 
 
 def pack_into(target, block, full):
@@ -251,51 +355,68 @@
 
 
 def partial_body(
-    members, groups, lead, scalars, place, t2, t3, text_near, unit, inverse, normed, weights_near, totals_near,
-    proj_columns, gain, *refs,
+    members, groups, lead, scalars, place, t3, unit_near, unit_far, totals, image_back, unit_columns_near,
+    unit_columns_far, inverse_near, inverse_far, turned_near, turned_far, proj_columns, gain, *refs,
 ):
-    across, keep_lead, keep_tail, *refs = refs
+    (across, keep_lead, keep_tail), refs = refs[:3], refs[3:]
     along, refs = refs[: groups // 2 - 1], refs[groups // 2 - 1 :]
-    text_far, weights_own, weights, totals, dots, text_columns, unit_columns, back, packed = refs
-    rows = t2.shape[0]
+    text_unit, weights_own, *refs = refs
+    outs = [across, keep_lead, keep_tail, *along]
+    outs_v, refs = refs[: len(outs)], refs[len(outs) :]
+    (
+        t3_v, unit_v, totals_v, back_v, unit_columns_v, inverse_v, turned_v, proj_columns_v, gain_v,
+        text_v, text_columns, weights, dots, back, packed, semaphores,
+    ) = refs
+    across, keep_lead, keep_tail, *along = outs_v
+    move = Mover(semaphores)
+    rows = t3.shape[0]
     near = 2 * rows
     every = members * rows
-    width = unit.shape[1]
+    width = unit_near.shape[1]
     columns = width // members
     count, full = packed.shape[1:]
     scale, bias = scalars[0], scalars[1]
-    for k, source in enumerate((t2, t3)):
-        unit_into(source, text_far, k * rows)
-    dots[...] = dot(unit[...], text_far[...], LAST)
-    weights[:, :near] = weights_near[...]
-    weigh(dots, scale, bias, near, weights, near, totals, totals_near)
-    weights_own[...] = weights[:rows, :]
-    for member in range(members):
-
-        @pl.when(place[0] == member)
-        def _():
-            where = slice(member * columns, (member + 1) * columns)
-            text_columns[:near, :] = text_near[:, where]
-            text_columns[near:, :] = text_far[:, where]
-            unit_columns[...] = unit[:, where]
-
-    image_back = dot(weights[...], text_columns[...])
+    t3_in = move(t3, t3_v)
+    unit_in = [move(unit_near, unit_v.at[:near]), move(unit_far, unit_v.at[near:])]
+    totals_in = move(totals, totals_v)
+    back_in = [
+        move(image_back, back_v),
+        move(unit_columns_near, unit_columns_v.at[:near]),
+        move(unit_columns_far, unit_columns_v.at[near:]),
+        move(inverse_near, inverse_v.at[:near]),
+        move(inverse_far, inverse_v.at[near:]),
+    ]
+    turned_in = [move(turned_near, turned_v.at[:, :near]), move(turned_far, turned_v.at[:, near:])]
+    gain_in = [move(proj_columns, proj_columns_v), move(gain, gain_v)]
+    t3_in.wait()
+    unit_into(t3_v, text_v, 0)
+    moved_out = [move(text_v, text_unit)]
+    take_columns(place, text_v, text_columns)
+    wait_all(*unit_in)
+    dots[...] = dot(unit_v[...], text_v[...], LAST)
+    totals_in.wait()
+    weigh(dots, scale, bias, near + rows, weights, totals_v, totals_v)
+    moved_out.append(move(weights.at[:rows], weights_own))
+    wait_all(*back_in)
+    image_back = back_v[...] + dot(weights[...], text_columns[...])
     back[...] = (
-        (image_back - unit_columns[...].astype(F32) * totals[...]) * (inverse[...] * scale)
+        (image_back - unit_columns_v[...].astype(F32) * totals_v[...]) * (inverse_v[...] * scale)
     ).astype(BF16)
+    wait_all(*turned_in)
     each = width // groups
-    product = dot(normed[...], back[...], FIRST) * (1.0 / every)
+    product = dot(turned_v[...], back[...]) * (1.0 / every)
     for group in range(groups):
         pack_into(packed.at[group], product[group * each : (group + 1) * each, :], full)
 
-    terms = product * proj_columns[...].astype(F32)
+    wait_all(*gain_in)
+    terms = product * proj_columns_v[...].astype(F32)
     folded = jnp.concatenate([terms[:, full:], jnp.zeros((width, full + LANES - columns), F32)], axis=1)
     for at in range(0, full, LANES):
         folded = folded + terms[:, at : at + LANES]
     high = folded.astype(BF16)
     low = (folded - high.astype(F32)).astype(BF16)
     ones = jnp.ones((BAND, 2 * LANES), BF16)
-    gain_row = dot(ones, jnp.concatenate([high, low], axis=1), LAST)[:1, :] / gain[...]
+    gain_row = dot(ones, jnp.concatenate([high, low], axis=1), LAST)[:1, :] / gain_v[...]
     pieces = [gain_row[:, at : at + LANES] for at in range(0, width, LANES)]
     pieces.append(jnp.zeros((BAND - len(pieces), LANES), F32))
     gain_tile = jnp.concatenate(pieces, axis=0).astype(BF16)
@@ -310,56 +431,98 @@
         keep_tail[other] = packed[own ^ other, lead:, :]
         for step in range(1, groups // 2):
             along[step - 1][other] = packed[own ^ (2 * step) ^ other, lead:, :]
+    moved_out += [move(source, target) for source, target in zip(outs_v, outs)]
+    wait_all(*moved_out)
 
 
 def image_body(
-    scalars, features, proj, gain, text_near, text_far, weights_own, unit, inverse,
-    feature_grad, back, product,
+    scalars, features, proj, gain, text_near, text_third, text_fourth, weights_near, weights_third, weights_fourth,
+    unit, inverse, feature_grad,
+    features_v, proj_v, gain_v, text_v, weights_near_v, weights_third_v, weights_fourth_v, unit_v, inverse_v,
+    grad_v, back, product, semaphores,
 ):
+    move = Mover(semaphores)
     rows, width = features.shape
     near = 2 * rows
     scale = scalars[0]
-    product[...] = dot(weights_own[:, :near], text_near[...]) + dot(weights_own[:, near:], text_far[...])
+    weights_in = [
+        move(weights_near.at[:rows], weights_near_v),
+        move(weights_third, weights_third_v),
+        move(weights_fourth, weights_fourth_v),
+    ]
+    text_in = [
+        move(text_near, text_v.at[:near]),
+        move(text_third, text_v.at[near : near + rows]),
+        move(text_fourth, text_v.at[near + rows :]),
+    ]
+    unit_in = [move(unit.at[:rows], unit_v), move(inverse.at[:rows], inverse_v)]
+    proj_in = move(proj, proj_v)
+    rest_in = [move(features, features_v), move(gain, gain_v)]
+    wait_all(*weights_in, *text_in)
+    product[...] = (
+        dot(weights_near_v[...], text_v[:near, :])
+        + dot(weights_third_v[...], text_v[near : near + rows, :])
+        + dot(weights_fourth_v[...], text_v[near + rows :, :])
+    )
+    wait_all(*unit_in)
 
     def image_chunk(where):
         values = product[where, :] * scale
-        direction = unit[where, :].astype(F32)
+        direction = unit_v[where, :].astype(F32)
         back[where, :] = (
-            (values - direction * sums(direction * values)) * inverse[where, :]
+            (values - direction * sums(direction * values)) * inverse_v[where, :]
         ).astype(BF16)
 
     over_rows(rows, 32, image_chunk)
-    product[...] = dot(back[...], proj[...], LAST)
+    proj_in.wait()
+    product[...] = dot(back[...], proj_v[...], LAST)
+    wait_all(*rest_in)
 
     def feature_chunk(where):
-        values = features[where, :].astype(F32)
+        values = features_v[where, :].astype(F32)
         centred = values - sums(values) * (1.0 / width)
         deviation = lax.rsqrt(sums(centred * centred) * (1.0 / width) + 1e-06)
         xhat = centred * deviation
-        scaled = product[where, :] * gain[...]
-        feature_grad[where, :] = (
+        scaled = product[where, :] * gain_v[...]
+        grad_v[where, :] = (
             deviation
             * (scaled - sums(scaled) * (1.0 / width) - xhat * (sums(scaled * xhat) * (1.0 / width)))
         ).astype(BF16)
 
     over_rows(rows, 32, feature_chunk)
-
-
-def text_body(scalars, text, weights_near, unit, text_grad, product):
+    move(grad_v, feature_grad).wait()
+
+
+def text_body(
+    scalars, text, weights_near, weights_far, unit_near, unit_far, text_grad,
+    text_v, weights_near_v, weights_far_v, unit_near_v, unit_far_v, grad_v, product, semaphores,
+):
+    move = Mover(semaphores)
     rows = text.shape[0]
     scale = scalars[0]
-    product[...] = dot(weights_near[:, :rows], unit[...], FIRST)
+    copies = [
+        move(weights_near, weights_near_v),
+        move(unit_near, unit_near_v),
+        move(weights_far, weights_far_v),
+        move(unit_far, unit_far_v),
+        move(text, text_v),
+    ]
+    wait_all(*copies)
+    product[...] = dot(weights_near_v[:, :rows], unit_near_v[...], FIRST) + dot(
+        weights_far_v[:, :rows], unit_far_v[...], FIRST
+    )
 
     def text_chunk(where):
         values = product[where, :] * scale
-        own = text[where, :].astype(F32)
+        own = text_v[where, :].astype(F32)
         own_inverse = lax.rsqrt(sums(own * own) + 1e-06)
         direction = own * own_inverse
-        text_grad[where, :] = (
+        grad_v[where, :] = (
             (values - direction * sums(direction * values)) * own_inverse
         ).astype(BF16)
 
     over_rows(rows, 32, text_chunk)
+    move(grad_v, text_grad).wait()
 
 
 def first_sum_body(place, keep_lead, across, keep_tail, *refs):
@@ -444,72 +607,104 @@
     f1 = send(f0, "loop", lambda p: p ^ 1)
     t1 = send(t0, "loop", lambda p: p ^ 1)
 
-    normed_near, unit_near, inverse_near, text_near = call(
+    wide, half, one = ((near, width), BF16), ((rows, width), BF16), ((near, 1), F32)
+    square, part, turned = ((near, near), BF16), ((near, columns), BF16), ((width, near), BF16)
+    proj_kind, gain_kind = ((width, width), BF16), ((1, width), F32)
+
+    def room(*kinds):
+        return [pltpu.VMEM(shape, kind) for shape, kind in kinds]
+
+    outs = [wide, turned, wide, part, one, wide, part, square, one, ((width, columns), BF16)]
+    (
+        normed_near, turned_near, unit_near, unit_columns_near, inverse_near, text_near, text_columns_near,
+        weights_near, totals_near, proj_columns,
+    ) = call_moving(
         near_body,
-        [((near, width), BF16), ((near, width), BF16), ((near, 1), F32), ((near, width), BF16)],
-        [pltpu.VMEM((near, width), F32)],
+        outs,
+        room(half, half, half, half, proj_kind, gain_kind, *outs, ((near, width), F32), ((near, near), F32)),
+        16,
+        smem=2,
+        flops=3 * near * width * width,
+        moved=8 * near * width,
+    )(scalars, place, f0, f1, t0, t1, proj, gain_row)
+
+    t_after, f2, text_near = lax.optimization_barrier((t0, f2, text_near))
+    t2 = send(t_after, "loop", lambda p: p ^ 2)
+    f3 = send(f2, "loop", lambda p: p ^ 1)
+
+    outs = [turned, wide, part, one, square, one]
+    turned_far, unit_far, unit_columns_far, inverse_far, weights_far, totals_far = call_moving(
+        far_body,
+        outs,
+        room(half, half, proj_kind, gain_kind, wide, wide, *outs, ((near, width), F32), ((near, near), F32)),
+        11,
+        smem=2,
+        flops=3 * near * width * width,
+        moved=8 * near * width,
+    )(scalars, place, f2, f3, proj, gain_row, text_near)
+
+    t2, weights_far = lax.optimization_barrier((t2, weights_far))
+    t3 = send(t2, "loop", lambda p: p ^ 1)
+
+    narrow = ((every, rows), BF16)
+    outs = [half, ((rows, rows), BF16), ((every, columns), F32), ((every, 1), F32)]
+    text_third, weights_third, image_back, totals = call_moving(
+        third_body,
+        outs,
+        room(
+            half, ((every, width), BF16), ((every, near), BF16), ((every, 1), F32), ((near + rows, columns), BF16),
+            half, narrow, ((every, columns), F32), ((every, rows), F32),
+        ),
+        12,
+        smem=2,
         flops=2 * near * width * width,
         moved=8 * near * width,
-    )(f0, f1, t0, t1, proj, gain_row)
-
-    t_after, f2, normed_near, unit_near, inverse_near, text_near = lax.optimization_barrier(
-        (t0, f2, normed_near, unit_near, inverse_near, text_near)
+    )(
+        scalars, place, t2, unit_near, unit_far, weights_near, weights_far, totals_near, totals_far,
+        text_columns_near,
     )
-    t2 = send(t_after, "loop", lambda p: p ^ 2)
-    f3 = send(f2, "loop", lambda p: p ^ 1)
-
-    normed, unit, inverse, weights_near, totals_near, proj_columns = call(
-        far_body,
-        [
-            ((every, width), BF16), ((every, width), BF16), ((every, 1), F32),
-            ((every, near), BF16), ((every, 1), F32), ((width, columns), BF16),
-        ],
-        [pltpu.VMEM((near, width), F32), pltpu.VMEM((every, near), F32)],
+    t3, totals = lax.optimization_barrier((t3, totals))
+
+    shared = [((steps, lead, full), BF16), ((steps, lead, full), BF16)] + [((2, tail, full), BF16)] * steps
+    outs = call_moving(
+        functools.partial(partial_body, members, groups, lead),
+        shared + [half, ((rows, rows), BF16)],
+        room(
+            *shared,
+            half, ((every, width), BF16), ((every, 1), F32), ((every, columns), F32), ((every, columns), BF16),
+            ((every, 1), F32), ((width, every), BF16), ((width, columns), BF16), gain_kind,
+            half, ((rows, columns), BF16), narrow, ((every, rows), F32), ((every, columns), BF16),
+            ((groups,) + packet, BF16),
+        ),
+        15 + len(shared),
         smem=2,
         flops=4 * near * width * width,
         moved=16 * near * width,
-    )(scalars, place, f2, f3, proj, gain_row, normed_near, unit_near, inverse_near, text_near)
-
-    t2, normed, unit, inverse, weights_near, totals_near, proj_columns = lax.optimization_barrier(
-        (t2, normed, unit, inverse, weights_near, totals_near, proj_columns)
-    )
-    t3 = send(t2, "loop", lambda p: p ^ 1)
-
-    outs = call(
-        functools.partial(partial_body, members, groups, lead),
-        [((steps, lead, full), BF16), ((steps, lead, full), BF16), ((2, tail, full), BF16)]
-        + [((2, tail, full), BF16)] * (steps - 1)
-        + [((near, width), BF16), ((rows, every), BF16)],
-        [
-            pltpu.VMEM((every, every), BF16),
-            pltpu.VMEM((every, 1), F32),
-            pltpu.VMEM((every, near), F32),
-            pltpu.VMEM((every, columns), BF16),
-            pltpu.VMEM((every, columns), BF16),
-            pltpu.VMEM((every, columns), BF16),
-            pltpu.VMEM((groups,) + packet, BF16),
-        ],
-        smem=2,
-        flops=6 * near * width * width,
-        moved=16 * near * width,
     )(
-        scalars, place, t2, t3, text_near, unit, inverse, normed, weights_near, totals_near,
-        proj_columns, gain_row,
+        scalars, place, t3, unit_near, unit_far, totals, image_back, unit_columns_near, unit_columns_far,
+        inverse_near, inverse_far, turned_near, turned_far, proj_columns, gain_row,
     )
     across, keep_lead, keep_tail = outs[:3]
-    along, (text_far, weights_own) = outs[3 : 2 + steps], outs[2 + steps :]
+    along, (text_fourth, weights_fourth) = outs[3 : 2 + steps], outs[2 + steps :]
 
     along = [send(along[step - 1], "rep", lambda p: p ^ (2 * step)) for step in range(1, steps)]
     across = send(across, "rep", lambda p: p ^ 1)
 
-    (feature_grad,) = call(
+    (feature_grad,) = call_moving(
         image_body,
-        [((rows, width), BF16)],
-        [pltpu.VMEM((rows, width), BF16), pltpu.VMEM((rows, width), F32)],
+        [half],
+        room(
+            half, proj_kind, gain_kind, ((every, width), BF16), ((rows, near), BF16), ((rows, rows), BF16),
+            ((rows, rows), BF16), half, ((rows, 1), F32), half, half, ((rows, width), F32),
+        ),
+        12,
         smem=1,
         flops=4 * near * width * width,
         moved=12 * near * width,
-    )(scalars, f0, proj, gain_row, text_near, text_far, weights_own, unit, inverse)
+    )(
+        scalars, f0, proj, gain_row, text_near, text_third, text_fourth, weights_near, weights_third,
+        weights_fourth, unit_near, inverse_near,
+    )
     feature_grad, across = lax.optimization_barrier((feature_grad, across))
 
     outs = call(
@@ -522,22 +717,23 @@
     leads = [outs[0]] + [send(outs[step], "rep", lambda p: p ^ (2 * step)) for step in range(1, steps)]
     tail_across = send(outs[steps + 1], "rep", lambda p: p ^ 1)
 
-    (text_grad,) = call(
-        text_body,
-        [((rows, width), BF16)],
-        [pltpu.VMEM((rows, width), F32)],
-        smem=1,
-        flops=2 * near * width * width,
-        moved=6 * near * width,
-    )(scalars, t0, weights_near, unit)
-    text_grad, tail_across = lax.optimization_barrier((text_grad, tail_across))
-
     (reduced,) = call(
         last_sum_body,
         [(packet, BF16)],
         moved=4 * each * width,
     )(outs[steps], tail_across, *leads)
     blocks = [reduced] + [send(reduced, "loop", lambda p: p ^ k) for k in range(1, members)]
+    t0, _ = lax.optimization_barrier((t0, reduced))
+    (text_grad,) = call_moving(
+        text_body,
+        [half],
+        room(half, square, square, wide, wide, half, ((rows, width), F32)),
+        6,
+        smem=1,
+        flops=2 * near * width * width,
+        moved=6 * near * width,
+    )(scalars, t0, weights_near, weights_far, unit_near, unit_far)
+    text_grad, *blocks[1:] = lax.optimization_barrier((text_grad, *blocks[1:]))
 
     proj_grad, gain_gradient = call(
         functools.partial(finish_body, members),

time: 68.4 us -> 78.6 us (1.15)
  Pallas kernels: 28.9 us -> 43 us
  local copies, waits for them, and re-layouts: 9.27 us -> 5.11 us
  starting transfers between devices: 18.4 us -> 17.1 us
  other arithmetic: 0.77 us -> 1.88 us
    pallas_call x8 -> x9, Pallas kernels: 28.9 us -> 43 us  [run(): pl.pallas_call(body, out_shape=[jax.ShapeDtypeStruct(shape, kind) for sha...]
    unnamed x20, local copies, waits for them, and re-layouts: 8.57 us -> 3.82 us
    ppermute x17, starting transfers between devices: 18.4 us -> 17.1 us  [send(): return lax.ppermute(value, axis, [(p, target(p)) for p in range(count)])]
  transfers between devices with their start and end apart: 17 -> 17, of which waited for: 7 -> 4; matrix products, arithmetic and copies ran while one was open for 1% -> 3% of each run, Pallas kernels for 30% -> 42%
where the time goes in v4:
time: 78.6 us; the launch traced here: 78.3 us
  Pallas kernels  43 us (55%)
  starting transfers between devices  17.1 us (22%)
  waiting for transfers between devices  9.07 us (12%)
  local copies, waits for them, and re-layouts  5.11 us (7%)
  between operations  2.11 us (3%)
  other arithmetic  1.88 us (2%)
    pallas_call x9, Pallas kernels, run(): pl.pallas_call(body, out_shape=[jax.ShapeDtypeStruct(shape, kind) for sha...  43 us
    ppermute x17, starting transfers between devices, send(): return lax.ppermute(value, axis, [(p, target(p)) for p in range(count)])  17.1 us
    ppermute x17, waiting for transfers between devices, send(): return lax.ppermute(value, axis, [(p, target(p)) for p in range(count)])  9.07 us
    unnamed x20, local copies, waits for them, and re-layouts  3.82 us
  transfers between devices with their start and end apart: 17, of which 4 were waited for; matrix products, arithmetic and copies ran while one was open for 3% of the time, Pallas kernels for 42%

profile of v4, /device:TPU:0, one launch (start us, length us, event | category | flops | bytes accessed | tf_op | source)
XLA Modules:
  0.0 78.3 jit_solution(2195740852051138100)
XLA Ops:
  0.6 0.5 collective-permute-start.1
  1.1 0.1 collective-permute-start.2
  1.2 2.9 %collective-permute-start = (bf16[192,1152]{1,0:T(8,128)(2,1)}, bf16[192,1152]{1,0:T(8,128)(2,1)S(1)}, u32[]{:S(2)}, u32[]{:S(2)}) collective-permute-start(bf16[192,1152]{1,0:T(8,128)(2,1)} %bitcast.7), channel_id=1, source_target_pairs={{0,16},{8,24},{16,0},{24,8},{1,17},{9,25},{17,1},{25,9},{2,18},{10... | collective-permute-start | bytes 1327112 | tf_op jit(solution)/shard_map/ppermute | solution.py:34
  5.4 1.3 %reshape.14.gain = f32[1,1152]{1,0:T(1,128)} reshape(f32[1152]{0:T(1024)} %param.9) | data formatting | bytes 9216 | tf_op jit(solution)/shard_map/reshape | solution.py:599
  6.7 0.6 pad_maximum_fusion.scalars
  7.4 0.6 pad_add_fusion.place
  8.0 0.0 collective-permute-done.1.f1
  8.0 0.0 collective-permute-done.2.t1
  8.0 0.8 copy-done.5
  8.8 0.8 copy-done.6
  9.5 8.5 %shard_map.93 = (bf16[384,1152]{1,0:T(8,128)(2,1)}, bf16[1152,384]{1,0:T(8,128)(2,1)}, bf16[384,1152]{1,0:T(8,128)(2,1)}, bf16[384,288]{1,0:T(8,128)(2,1)}, f32[...) custom-call(f32[2]{0:T(128)} %pad_maximum_fusion.scalars, ...), custom_call_target="tpu_custom_call" | custom-call | flops 1528823808 | bytes 3538944 | tf_op jit(solution)/shard_map/pallas_call | solution.py:153
  18.1 0.0 collective-permute-done.f2
  18.1 0.0 copy-start.4
  18.1 0.4 collective-permute-start.4
  18.5 0.3 collective-permute-start.3
  18.8 1.2 %collective-permute-done.4.f3 = bf16[192,1152]{1,0:T(8,128)(2,1)S(1)} collective-permute-done((bf16[192,1152]{1,0:T(8,128)(2,1)S(1)}, bf16[192,1152]{1,0:T(8,128)(2,1)S(1)}, u32[]{:S(2)}, u32[]{:S(2)}) %collective-permute-start.4) | collective-permute-done | bytes 442400 | tf_op jit(solution)/shard_map/ppermute | solution.py:34
  20.0 0.8 copy-done.9
  20.7 7.4 %shard_map.94 = (bf16[1152,384]{1,0:T(8,128)(2,1)}, bf16[384,1152]{1,0:T(8,128)(2,1)}, bf16[384,288]{1,0:T(8,128)(2,1)}, f32[384,1]{1,0:T(8,128)}, bf16[384,384]{1,0:T(8,128)(2,1)}, /*index=5*/f32[384,1]{1,0:T(8,128)}) custom-call(f32[2]{0:T(128)} %pad_maximum_fusion.scalars, s32[2]{0:T(128)} %pad_add_fusion.place, bf16[192,1152]{1,0:T(8,128)(2,1)} %copy-done.4, ...), custom_call_target="tpu_custom_call" | custom-call | flops 1528823808 | bytes 3538944 | tf_op jit(solution)/shard_map/pallas_call | solution.py:153
  28.1 2.6 %collective-permute-done.3.t2 = bf16[192,1152]{1,0:T(8,128)(2,1)S(1)} collective-permute-done((bf16[192,1152]{1,0:T(8,128)(2,1)S(1)}, bf16[192,1152]{1,0:T(8,128)(2,1)S(1)}, u32[]{:S(2)}, u32[]{:S(2)}) %collective-permute-start.3) | collective-permute-done | bytes 442400 | tf_op jit(solution)/shard_map/ppermute | solution.py:34
  30.8 0.0 collective-permute-start.5
  30.8 0.8 copy-done.8
  31.5 6.4 %shard_map.95 = (bf16[192,1152]{1,0:T(8,128)(2,1)}, bf16[192,192]{1,0:T(8,128)(2,1)}, f32[768,288]{1,0:T(8,128)}, f32[768,1]{1,0:T(8,128)}) custom-call(f32[2]{0:T(128)} %pad_maximum_fusion.scalars, s32[2]{0:T(128)} %pad_add_fusion.place, bf16[192,1152]{1,0:T(8,128)(2,1)} %copy-done.8, bf16[384,1152]{1,0:T(8,128)(2,1)} %get-tuple-element.59.unit_near.unit, ...), custom_call_target="tpu_custom_call" | custom-call | flops 1019215872 | bytes 3538944 | tf_op jit(solution)/shard_map/pallas_call | solution.py:153
  38.0 0.0 collective-permute-done.5.t3
  38.0 0.0 copy-start.7
  38.0 0.8 copy-done.7
  38.7 7.5 %shard_map.96 = (bf16[4,112,256]{2,1,0:T(8,128)(2,1)}, bf16[4,112,256]{2,1,0:T(8,128)(2,1)}, bf16[2,64,256]{2,1,0:T(8,128)(2,1)}, bf16[2,64,256]{2,1,0:T(8,128)(...) custom-call(f32[2]{0:T(128)} %pad_maximum_fusion.scalars, ...), custom_call_target="tpu_custom_call" | custom-call | flops 2038431744 | bytes 7077888 | tf_op jit(solution)/shard_map/pallas_call | solution.py:153
  46.3 1.6 %collective-permute-start.6 = (bf16[4,112,256]{2,1,0:T(8,128)(2,1)}, bf16[4,112,256]{2,1,0:T(8,128)(2,1)S(1)}, u32[]{:S(2)}, u32[]{:S(2)}) collective-permute-start(bf16[4,112,256]{2,1,0:T(8,128)(2,1)} %get-tuple-element.81), channel_id=1, source_target_pairs={{0,1},{1,0},{2,3},{3,2},{4,5},{5,4},{6,7},{7,6},{8,9},{9,8},{10,11... | collective-permute-start | bytes 688136 | tf_op jit(solution)/shard_map/ppermute | solution.py:34
  47.8 1.6 %collective-permute-start.7 = (bf16[2,64,256]{2,1,0:T(8,128)(2,1)}, bf16[2,64,256]{2,1,0:T(8,128)(2,1)S(1)}, u32[]{:S(2)}, u32[]{:S(2)}) collective-permute-start(bf16[2,64,256]{2,1,0:T(8,128)(2,1)} %get-tuple-element.86), channel_id=1, source_target_pairs={{0,2},{1,3},{2,0},{3,1},{4,6},{5,7},{6,4},{7,5},{8,10},{9,11},{10,... | collective-permute-start | bytes 196616 | tf_op jit(solution)/shard_map/ppermute | solution.py:34
  49.4 2.6 %collective-permute-start.8 = (bf16[2,64,256]{2,1,0:T(8,128)(2,1)}, bf16[2,64,256]{2,1,0:T(8,128)(2,1)S(1)}, u32[]{:S(2)}, u32[]{:S(2)}) collective-permute-start(bf16[2,64,256]{2,1,0:T(8,128)(2,1)} %get-tuple-element.87), channel_id=1, source_target_pairs={{0,4},{1,5},{2,6},{3,7},{4,0},{5,1},{6,2},{7,3},{8,12},{9,13},{10,... | collective-permute-start | bytes 196616 | tf_op jit(solution)/shard_map/ppermute | solution.py:34
  52.0 0.2 collective-permute-start.9
  52.2 6.3 %shard_map.97 = bf16[192,1152]{1,0:T(8,128)(2,1)} custom-call(f32[2]{0:T(128)} %pad_maximum_fusion.scalars, bf16[192,1152]{1,0:T(8,128)(2,1)} %bitcast.9, bf16[1152,1152]{1,0:T(8,128)(2,1)} %proj.5, f32[1,1152]{1,0:T(1,128)} %reshape.14.gain, bf16[384,1152]{1,0:T(8,128)(2,1)} %get-tuple-element.54.text_near, bf16[192,1152]{1,0:T(8,128)(2,1)} %get-tuple-element.66.text_third, ...), custom_call_target="tpu_custom_call" | custom-call | flops 2038431744 | bytes 5308416 | tf_op jit(solution)/shard_map/pallas_call | solution.py:153
  58.6 0.0 collective-permute-done.6.across
  58.6 0.0 collective-permute-done.7.refs_0_
  58.6 0.0 collective-permute-done.9.refs_2_
  58.7 0.6 shard_map.98
  59.3 0.8 collective-permute-start.11
  60.1 3.5 %collective-permute-start.12 = (bf16[112,256]{1,0:T(8,128)(2,1)S(1)}, bf16[112,256]{1,0:T(8,128)(2,1)S(1)}, u32[]{:S(2)}, u32[]{:S(2)}) collective-permute-start(bf16[112,256]{1,0:T(8,128)(2,1)S(1)} %get-tuple-element.93), channel_id=1, source_target_pairs={{0,4},{1,5},{2,6},{3,7},{4,0},{5,1},{6,2},{7,3},{8,12},{9,13},{10,... | collective-permute-start | bytes 172040 | tf_op jit(solution)/shard_map/ppermute | solution.py:34
  63.5 0.2 collective-permute-start.13
  63.8 0.5 collective-permute-start.10
  64.3 3.4 %collective-permute-done.10.tail_across = bf16[64,256]{1,0:T(8,128)(2,1)S(1)} collective-permute-done((bf16[64,256]{1,0:T(8,128)(2,1)S(1)}, bf16[64,256]{1,0:T(8,128)(2,1)S(1)}, u32[]{:S(2)}, u32[]{:S(2)}) %collective-permute-start.10) | collective-permute-done | bytes 32800 | tf_op jit(solution)/shard_map/ppermute | solution.py:34
  67.7 1.8 %collective-permute-done.13.refs_3_ = bf16[112,256]{1,0:T(8,128)(2,1)S(1)} collective-permute-done((bf16[112,256]{1,0:T(8,128)(2,1)S(1)}, bf16[112,256]{1,0:T(8,128)(2,1)S(1)}, u32[]{:S(2)}, u32[]{:S(2)}) %collective-permute-start.13) | collective-permute-done | bytes 57376 | tf_op jit(solution)/shard_map/ppermute | solution.py:34
  69.5 0.1 collective-permute-start.16
  69.6 1.3 %collective-permute-start.15 = (bf16[176,256]{1,0:T(8,128)(2,1)S(1)}, bf16[176,256]{1,0:T(8,128)(2,1)S(1)}, u32[]{:S(2)}, u32[]{:S(2)}) collective-permute-start(bf16[176,256]{1,0:T(8,128)(2,1)S(1)} %shard_map.99.refs_0_), channel_id=1, source_target_pairs={{0,16},{8,24},{16,0},{24,8},{1,17},{9,25},{17,1},{25,9},{2,18},{10... | collective-permute-start | bytes 270344 | tf_op jit(solution)/shard_map/ppermute | solution.py:34
  70.9 0.6 collective-permute-start.14
  71.5 4.4 %shard_map.100 = bf16[192,1152]{1,0:T(8,128)(2,1)} custom-call(f32[2]{0:T(128)} %pad_maximum_fusion.scalars, bf16[192,1152]{1,0:T(8,128)(2,1)} %bitcast.12, bf16[384,384]{1,0:T(8,128)(2,1)} %get-tuple-element.61.weights_near, bf16[384,384]{1,0:T(8,128)(2,1)} %get-tuple-element.62.weights_far, bf16[384,1152]{1,0:T(8,128)(2,1)} %get-tuple-element.59.unit_near.unit, ...), custom_call_target="tpu_custom_call" | custom-call | flops 1019215872 | bytes 2654208 | tf_op jit(solution)/shard_map/pallas_call | solution.py:153
  75.9 0.0 collective-permute-done.15.refs_2_
  76.0 1.7 %shard_map.101 = (f32[144,1152]{1,0:T(8,128)}, f32[1,1152]{1,0:T(1,128)S(1)}) custom-call(s32[2]{0:T(128)S(1)} %copy-done.2, bf16[176,256]{1,0:T(8,128)(2,1)S(1)} %shard_map.99.refs_0_, bf16[176,256]{1,0:T(8,128)(2,1)S(1)} %collective-permute-done.14.refs_1_, bf16[176,256]{1,0:T(8,128)(2,1)S(1)} %collective-permute-done.15.refs_2_, ...), custom_call_target="tpu_custom_call" | custom-call | bytes 1327104 | tf_op jit(solution)/shard_map/pallas_call | solution.py:137
  77.6 0.6 reduce
  (19 shorter events, 0.1 us)
Async XLA Ops:
  0.6 7.4 %collective-permute-start.1 = (bf16[192,1152]{1,0:T(8,128)(2,1)}, bf16[192,1152]{1,0:T(8,128)(2,1)S(1)}, u32[]{:S(2)}, u32[]{:S(2)}) collective-permute-start(bf16[192,1152]{1,0:T(8,128)(2,1)} %bitcast.6), channel_id=1, source_target_pairs={{0,8},{8,0},{16,24},{24,16},{1,9},{9,1},{17,25},{25,17},{2,10},{10... | collective-permute-start | bytes 1327112 | tf_op jit(solution)/shard_map/ppermute | solution.py:34
  1.1 6.9 %collective-permute-start.2 = (bf16[192,1152]{1,0:T(8,128)(2,1)}, bf16[192,1152]{1,0:T(8,128)(2,1)S(1)}, u32[]{:S(2)}, u32[]{:S(2)}) collective-permute-start(bf16[192,1152]{1,0:T(8,128)(2,1)} %bitcast.10), channel_id=1, source_target_pairs={{0,8},{8,0},{16,24},{24,16},{1,9},{9,1},{17,25},{25,17},{2,10},{10... | collective-permute-start | bytes 1327112 | tf_op jit(solution)/shard_map/ppermute | solution.py:34
  1.2 16.8 %collective-permute-start = (bf16[192,1152]{1,0:T(8,128)(2,1)}, bf16[192,1152]{1,0:T(8,128)(2,1)S(1)}, u32[]{:S(2)}, u32[]{:S(2)}) collective-permute-start(bf16[192,1152]{1,0:T(8,128)(2,1)} %bitcast.7), channel_id=1, source_target_pairs={{0,16},{8,24},{16,0},{24,8},{1,17},{9,25},{17,1},{25,9},{2,18},{10... | collective-permute-start | bytes 1327112 | tf_op jit(solution)/shard_map/ppermute | solution.py:34
  8.0 10.5 %copy-start.3 = (bf16[192,1,1152]{2,0,1:T(8,128)(2,1)S(1)}, bf16[192,1,1152]{2,0,1:T(8,128)(2,1)}, u32[]{:S(2)}) copy-start(bf16[192,1,1152]{2,0,1:T(8,128)(2,1)} %param.7) | copy-start | bytes 1327108
  8.0 0.8 copy-start.5
  8.8 0.8 copy-start.6
  18.1 1.9 %copy-start.4 = (bf16[192,1152]{1,0:T(8,128)(2,1)}, bf16[192,1152]{1,0:T(8,128)(2,1)S(1)}, u32[]{:S(2)}) copy-start(bf16[192,1152]{1,0:T(8,128)(2,1)S(1)} %collective-permute-done.f2) | copy-start | bytes 1327108
  18.1 1.9 %collective-permute-start.4 = (bf16[192,1152]{1,0:T(8,128)(2,1)S(1)}, bf16[192,1152]{1,0:T(8,128)(2,1)S(1)}, u32[]{:S(2)}, u32[]{:S(2)}) collective-permute-start(bf16[192,1152]{1,0:T(8,128)(2,1)S(1)} %collective-permute-done.f2), channel_id=1, source_target_pairs={{0,8},{8,0},{16,24},{24,16},{1,9},{9,1},{17,25},{25,17},{2,10},{10... | collective-permute-start | bytes 1327112 | tf_op jit(solution)/shard_map/ppermute | solution.py:34
  18.5 12.2 %collective-permute-start.3 = (bf16[192,1152]{1,0:T(8,128)(2,1)S(1)}, bf16[192,1152]{1,0:T(8,128)(2,1)S(1)}, u32[]{:S(2)}, u32[]{:S(2)}) collective-permute-start(bf16[192,1152]{1,0:T(8,128)(2,1)S(1)} %bitcast.13), channel_id=1, source_target_pairs={{0,16},{8,24},{16,0},{24,8},{1,17},{9,25},{17,1},{25,9},{2,18},{10... | collective-permute-start | bytes 1327112 | tf_op jit(solution)/shard_map/ppermute | solution.py:34
  20.0 0.8 copy-start.9
  30.7 0.8 copy-start.8
  30.8 7.2 %collective-permute-start.5 = (bf16[192,1152]{1,0:T(8,128)(2,1)S(1)}, bf16[192,1152]{1,0:T(8,128)(2,1)S(1)}, u32[]{:S(2)}, u32[]{:S(2)}) collective-permute-start(bf16[192,1152]{1,0:T(8,128)(2,1)S(1)} %collective-permute-done.3.t2), channel_id=1, source_target_pairs={{0,8},{8,0},{16,24},{24,16},{1,9},{9,1},{17,25},{25,17},{2,10},{10... | collective-permute-start | bytes 1327112 | tf_op jit(solution)/shard_map/ppermute | solution.py:34
  38.0 0.8 copy-start.7
  46.3 12.3 %collective-permute-start.6 = (bf16[4,112,256]{2,1,0:T(8,128)(2,1)}, bf16[4,112,256]{2,1,0:T(8,128)(2,1)S(1)}, u32[]{:S(2)}, u32[]{:S(2)}) collective-permute-start(bf16[4,112,256]{2,1,0:T(8,128)(2,1)} %get-tuple-element.81), channel_id=1, source_target_pairs={{0,1},{1,0},{2,3},{3,2},{4,5},{5,4},{6,7},{7,6},{8,9},{9,8},{10,11... | collective-permute-start | bytes 688136 | tf_op jit(solution)/shard_map/ppermute | solution.py:34
  47.8 10.8 %collective-permute-start.7 = (bf16[2,64,256]{2,1,0:T(8,128)(2,1)}, bf16[2,64,256]{2,1,0:T(8,128)(2,1)S(1)}, u32[]{:S(2)}, u32[]{:S(2)}) collective-permute-start(bf16[2,64,256]{2,1,0:T(8,128)(2,1)} %get-tuple-element.86), channel_id=1, source_target_pairs={{0,2},{1,3},{2,0},{3,1},{4,6},{5,7},{6,4},{7,5},{8,10},{9,11},{10,... | collective-permute-start | bytes 196616 | tf_op jit(solution)/shard_map/ppermute | solution.py:34
  49.4 9.2 %collective-permute-start.8 = (bf16[2,64,256]{2,1,0:T(8,128)(2,1)}, bf16[2,64,256]{2,1,0:T(8,128)(2,1)S(1)}, u32[]{:S(2)}, u32[]{:S(2)}) collective-permute-start(bf16[2,64,256]{2,1,0:T(8,128)(2,1)} %get-tuple-element.87), channel_id=1, source_target_pairs={{0,4},{1,5},{2,6},{3,7},{4,0},{5,1},{6,2},{7,3},{8,12},{9,13},{10,... | collective-permute-start | bytes 196616 | tf_op jit(solution)/shard_map/ppermute | solution.py:34
  52.0 6.6 %collective-permute-start.9 = (bf16[2,64,256]{2,1,0:T(8,128)(2,1)}, bf16[2,64,256]{2,1,0:T(8,128)(2,1)S(1)}, u32[]{:S(2)}, u32[]{:S(2)}) collective-permute-start(bf16[2,64,256]{2,1,0:T(8,128)(2,1)} %get-tuple-element.88), channel_id=1, source_target_pairs={{0,6},{1,7},{2,4},{3,5},{4,2},{5,3},{6,0},{7,1},{8,14},{9,15},{10,... | collective-permute-start | bytes 196616 | tf_op jit(solution)/shard_map/ppermute | solution.py:34
  52.2 6.4 %copy-start = (bf16[4,112,256]{2,1,0:T(8,128)(2,1)S(1)}, bf16[4,112,256]{2,1,0:T(8,128)(2,1)}, u32[]{:S(2)}) copy-start(bf16[4,112,256]{2,1,0:T(8,128)(2,1)} %get-tuple-element.83.keep_lead) | copy-start | bytes 688132
  52.2 6.4 %copy-start.1 = (bf16[2,64,256]{2,1,0:T(8,128)(2,1)S(1)}, bf16[2,64,256]{2,1,0:T(8,128)(2,1)}, u32[]{:S(2)}) copy-start(bf16[2,64,256]{2,1,0:T(8,128)(2,1)} %get-tuple-element.85.keep_tail) | copy-start | bytes 196612
  52.2 6.4 %copy-start.2 = (s32[2]{0:T(128)S(1)}, s32[2]{0:T(128)}, u32[]{:S(2)}) copy-start(s32[2]{0:T(128)} %pad_add_fusion.place) | copy-start | bytes 28
  59.3 8.4 %collective-permute-start.11 = (bf16[112,256]{1,0:T(8,128)(2,1)S(1)}, bf16[112,256]{1,0:T(8,128)(2,1)S(1)}, u32[]{:S(2)}, u32[]{:S(2)}) collective-permute-start(bf16[112,256]{1,0:T(8,128)(2,1)S(1)} %get-tuple-element.92), channel_id=1, source_target_pairs={{0,2},{1,3},{2,0},{3,1},{4,6},{5,7},{6,4},{7,5},{8,10},{9,11},{10,... | collective-permute-start | bytes 172040 | tf_op jit(solution)/shard_map/ppermute | solution.py:34
  60.1 7.6 %collective-permute-start.12 = (bf16[112,256]{1,0:T(8,128)(2,1)S(1)}, bf16[112,256]{1,0:T(8,128)(2,1)S(1)}, u32[]{:S(2)}, u32[]{:S(2)}) collective-permute-start(bf16[112,256]{1,0:T(8,128)(2,1)S(1)} %get-tuple-element.93), channel_id=1, source_target_pairs={{0,4},{1,5},{2,6},{3,7},{4,0},{5,1},{6,2},{7,3},{8,12},{9,13},{10,... | collective-permute-start | bytes 172040 | tf_op jit(solution)/shard_map/ppermute | solution.py:34
  63.5 6.0 %collective-permute-start.13 = (bf16[112,256]{1,0:T(8,128)(2,1)S(1)}, bf16[112,256]{1,0:T(8,128)(2,1)S(1)}, u32[]{:S(2)}, u32[]{:S(2)}) collective-permute-start(bf16[112,256]{1,0:T(8,128)(2,1)S(1)} %get-tuple-element.94), channel_id=1, source_target_pairs={{0,6},{1,7},{2,4},{3,5},{4,2},{5,3},{6,0},{7,1},{8,14},{9,15},{10,... | collective-permute-start | bytes 172040 | tf_op jit(solution)/shard_map/ppermute | solution.py:34
  63.8 3.9 %collective-permute-start.10 = (bf16[64,256]{1,0:T(8,128)(2,1)S(1)}, bf16[64,256]{1,0:T(8,128)(2,1)S(1)}, u32[]{:S(2)}, u32[]{:S(2)}) collective-permute-start(bf16[64,256]{1,0:T(8,128)(2,1)S(1)} %get-tuple-element.90), channel_id=1, source_target_pairs={{0,1},{1,0},{2,3},{3,2},{4,5},{5,4},{6,7},{7,6},{8,9},{9,8},{10,11... | collective-permute-start | bytes 98312 | tf_op jit(solution)/shard_map/ppermute | solution.py:34
  69.5 6.4 %collective-permute-start.16 = (bf16[176,256]{1,0:T(8,128)(2,1)S(1)}, bf16[176,256]{1,0:T(8,128)(2,1)S(1)}, u32[]{:S(2)}, u32[]{:S(2)}) collective-permute-start(bf16[176,256]{1,0:T(8,128)(2,1)S(1)} %shard_map.99.refs_0_), channel_id=1, source_target_pairs={{0,24},{8,16},{16,8},{24,0},{1,25},{9,17},{17,9},{25,1},{2,26},{10... | collective-permute-start | bytes 270344 | tf_op jit(solution)/shard_map/ppermute | solution.py:34
  69.6 6.3 %collective-permute-start.15 = (bf16[176,256]{1,0:T(8,128)(2,1)S(1)}, bf16[176,256]{1,0:T(8,128)(2,1)S(1)}, u32[]{:S(2)}, u32[]{:S(2)}) collective-permute-start(bf16[176,256]{1,0:T(8,128)(2,1)S(1)} %shard_map.99.refs_0_), channel_id=1, source_target_pairs={{0,16},{8,24},{16,0},{24,8},{1,17},{9,25},{17,1},{25,9},{2,18},{10... | collective-permute-start | bytes 270344 | tf_op jit(solution)/shard_map/ppermute | solution.py:34
  70.9 5.1 %collective-permute-start.14 = (bf16[176,256]{1,0:T(8,128)(2,1)S(1)}, bf16[176,256]{1,0:T(8,128)(2,1)S(1)}, u32[]{:S(2)}, u32[]{:S(2)}) collective-permute-start(bf16[176,256]{1,0:T(8,128)(2,1)S(1)} %shard_map.99.refs_0_), channel_id=1, source_target_pairs={{0,8},{8,0},{16,24},{24,16},{1,9},{9,1},{17,25},{25,17},{2,10},{10... | collective-permute-start | bytes 270344 | tf_op jit(solution)/shard_map/ppermute | solution.py:34

commit v5 on v3

--- a/solution.py
+++ b/solution.py
@@ -128,6 +128,7 @@
 SMEM = pl.BlockSpec(memory_space=pltpu.SMEM)
 LANES = 128
 BAND = 16
+TOKEN = ((8, LANES), F32)
 
 
 def call(body, outs, scratch=(), smem=0, flops=0, moved=0):
@@ -138,8 +139,8 @@
             out_shape=[jax.ShapeDtypeStruct(shape, kind) for shape, kind in outs],
             in_specs=specs,
             out_specs=[VMEM] * len(outs),
-            scratch_shapes=list(scratch),
-            compiler_params=pltpu.CompilerParams(vmem_limit_bytes=36 * 2**20),
+            scratch_shapes=[pltpu.VMEM(shape, kind) for shape, kind in scratch],
+            compiler_params=pltpu.CompilerParams(vmem_limit_bytes=24 * 2**20),
             cost_estimate=pl.CostEstimate(flops=flops, bytes_accessed=moved, transcendentals=0),
         )(*operands)
 
@@ -151,7 +152,7 @@
         body(pl.ds(pl.multiple_of(index * step, step), step))
         return 0
 
-    lax.fori_loop(0, count // step, turn, 0, unroll=2)
+    lax.fori_loop(0, count // step, turn, 0, unroll=min(4, count // step))
 
 
 def sums(values):
@@ -184,55 +185,102 @@
     over_rows(rows, 32, chunk)
 
 
-def weigh(dots, scale, bias, first_column, weights, columns_at, totals, add_to):
+def weigh(dots, scale, bias, diagonal, weights, totals, add_to=None):
     rows, columns = dots.shape
 
-    def chunk(where):
-        product = dots[where, :]
-        logits = scale * product + bias
-        weight = 1.0 / (1.0 + jnp.exp(-logits))
-        row = where.start + lax.broadcasted_iota(jnp.int32, product.shape, 0)
-        column = first_column + lax.broadcasted_iota(jnp.int32, product.shape, 1)
-        weight = jnp.where(row == column, weight - 1.0, weight).astype(BF16)
-        weights[where, columns_at : columns_at + columns] = weight
-        total = sums(weight.astype(F32) * product)
-        totals[where, :] = total if add_to is None else add_to[where, :] + total
-
-    over_rows(rows, 64, chunk)
-
-
-def near_body(f0, f1, t0, t1, proj, gain, normed, unit, inverse, text_unit, projected):
+    def part(first, count, with_pairs):
+        def chunk(where):
+            where = pl.ds(first + where.start, where.size)
+            product = dots[where, :]
+            weight = jnp.tanh((0.5 * scale) * product + 0.5 * bias)
+            offset = 0.5
+            if with_pairs:
+                row = where.start - diagonal + lax.broadcasted_iota(jnp.int32, product.shape, 0)
+                column = lax.broadcasted_iota(jnp.int32, product.shape, 1)
+                offset = jnp.where(row == column, -0.5, 0.5)
+            weight = (0.5 * weight + offset).astype(BF16)
+            weights[where, :] = weight
+            total = sums(weight.astype(F32) * product)
+            totals[where, :] = total if add_to is None else add_to[where, :] + total
+
+        over_rows(count, 32, chunk)
+
+    if diagonal is None:
+        part(0, rows, False)
+        return
+    if diagonal:
+        part(0, diagonal, False)
+    part(diagonal, columns, True)
+    if diagonal + columns < rows:
+        part(diagonal + columns, rows - diagonal - columns, False)
+
+
+def take_columns(place, source, target):
+    columns = target.shape[1]
+    for member in range(source.shape[1] // columns):
+
+        @pl.when(place[0] == member)
+        def _():
+            target[...] = source[:, member * columns : (member + 1) * columns]
+
+
+def near_body(
+    scalars, place, f0, f1, t0, t1, proj, gain,
+    normed_turned, unit, unit_columns, inverse, text_unit, text_columns, weights, totals, proj_columns, token,
+    normed, projected, dots,
+):
     rows = f0.shape[0]
-    for k, source in enumerate((f0, f1)):
-        normalize_into(source, gain, normed, k * rows)
-    for k, source in enumerate((t0, t1)):
-        unit_into(source, text_unit, k * rows)
+    normalize_into(f0, gain, normed, 0)
+    normalize_into(f1, gain, normed, rows)
+    projected[...] = dot(normed[...], proj[...])
+    unit_into(t0, text_unit, 0)
+    unit_into(t1, text_unit, rows)
+    unit_into(projected, unit, 0, inverse)
+    dots[...] = dot(unit[...], text_unit[...], LAST)
+    weigh(dots, scalars[0], scalars[1], 0, weights, totals)
+    take_columns(place, unit, unit_columns)
+    take_columns(place, text_unit, text_columns)
+    take_columns(place, proj, proj_columns)
+    normed_turned[...] = normed[...].T
+    token[...] = jnp.zeros_like(token)
+
+
+def far_body(
+    scalars, place, f2, f3, proj, gain, text_near, before,
+    normed_turned, unit, unit_columns, inverse, weights, totals, token,
+    normed, projected, dots,
+):
+    rows = f2.shape[0]
+    normalize_into(f2, gain, normed, 0)
+    normalize_into(f3, gain, normed, rows)
     projected[...] = dot(normed[...], proj[...])
     unit_into(projected, unit, 0, inverse)
-
-
-def far_body(
-    scalars, place, f2, f3, proj, gain, normed_near, unit_near, inverse_near, text_near,
-    normed, unit, inverse, weights, totals, proj_columns, projected, dots,
+    dots[...] = dot(unit[...], text_near[...], LAST)
+    weigh(dots, scalars[0], scalars[1], None, weights, totals)
+    take_columns(place, unit, unit_columns)
+    normed_turned[...] = normed[...].T
+    token[...] = jnp.zeros_like(token)
+
+
+def third_body(
+    scalars, place, t2, unit_near, unit_far, weights_near, weights_far, totals_near, totals_far, text_columns_near, before,
+    text_unit, weights_own, image_back, totals,
+    text_columns, weights, dots,
 ):
-    rows = f2.shape[0]
+    rows = t2.shape[0]
     near = 2 * rows
-    members, columns = proj.shape[1] // proj_columns.shape[1], proj_columns.shape[1]
-    for member in range(members):
-
-        @pl.when(place[0] == member)
-        def _():
-            proj_columns[...] = proj[:, member * columns : (member + 1) * columns]
-
-    normed[:near, :] = normed_near[...]
-    unit[:near, :] = unit_near[...]
-    inverse[:near, :] = inverse_near[...]
-    for k, source in enumerate((f2, f3)):
-        normalize_into(source, gain, normed, near + k * rows)
-    projected[...] = dot(normed[near:, :], proj[...])
-    unit_into(projected, unit, near, inverse)
-    dots[...] = dot(unit[...], text_near[...], LAST)
-    weigh(dots, scalars[0], scalars[1], 0, weights, 0, totals, None)
+    unit_into(t2, text_unit, 0)
+    take_columns(place, text_unit, text_columns)
+    dots[:near, :] = dot(unit_near[...], text_unit[...], LAST)
+    dots[near:, :] = dot(unit_far[...], text_unit[...], LAST)
+    totals[:near, :] = totals_near[...]
+    totals[near:, :] = totals_far[...]
+    weigh(dots, scalars[0], scalars[1], near, weights, totals, totals)
+    weights_own[...] = weights[:rows, :]
+    for at, earlier in ((0, weights_near), (near, weights_far)):
+        image_back[at : at + near, :] = dot(earlier[...], text_columns_near[...]) + dot(
+            weights[at : at + near, :], text_columns[...]
+        )
 
 
 def pack_into(target, block, full):
@@ -251,40 +299,33 @@
 
 
 def partial_body(
-    members, groups, lead, scalars, place, t2, t3, text_near, unit, inverse, normed, weights_near, totals_near,
-    proj_columns, gain, *refs,
+    members, groups, lead, scalars, place, t3, unit_near, unit_far, totals, image_back, unit_columns_near,
+    unit_columns_far, inverse_near, inverse_far, turned_near, turned_far, proj_columns, gain, *refs,
 ):
-    across, keep_lead, keep_tail, *refs = refs
+    (across, keep_lead, keep_tail), refs = refs[:3], refs[3:]
     along, refs = refs[: groups // 2 - 1], refs[groups // 2 - 1 :]
-    text_far, weights_own, weights, totals, dots, text_columns, unit_columns, back, packed = refs
-    rows = t2.shape[0]
+    text_unit, weights_own, text_columns, weights, dots, all_totals, back, packed = refs
+    rows = t3.shape[0]
     near = 2 * rows
     every = members * rows
-    width = unit.shape[1]
+    width = unit_near.shape[1]
     columns = width // members
     count, full = packed.shape[1:]
     scale, bias = scalars[0], scalars[1]
-    for k, source in enumerate((t2, t3)):
-        unit_into(source, text_far, k * rows)
-    dots[...] = dot(unit[...], text_far[...], LAST)
-    weights[:, :near] = weights_near[...]
-    weigh(dots, scale, bias, near, weights, near, totals, totals_near)
+    unit_into(t3, text_unit, 0)
+    take_columns(place, text_unit, text_columns)
+    dots[:near, :] = dot(unit_near[...], text_unit[...], LAST)
+    dots[near:, :] = dot(unit_far[...], text_unit[...], LAST)
+    weigh(dots, scale, bias, near + rows, weights, all_totals, totals)
     weights_own[...] = weights[:rows, :]
-    for member in range(members):
-
-        @pl.when(place[0] == member)
-        def _():
-            where = slice(member * columns, (member + 1) * columns)
-            text_columns[:near, :] = text_near[:, where]
-            text_columns[near:, :] = text_far[:, where]
-            unit_columns[...] = unit[:, where]
-
-    image_back = dot(weights[...], text_columns[...])
-    back[...] = (
-        (image_back - unit_columns[...].astype(F32) * totals[...]) * (inverse[...] * scale)
-    ).astype(BF16)
+    for at, unit_columns, inverse in ((0, unit_columns_near, inverse_near), (near, unit_columns_far, inverse_far)):
+        where = slice(at, at + near)
+        whole = image_back[where, :] + dot(weights[where, :], text_columns[...])
+        back[where, :] = (
+            (whole - unit_columns[...].astype(F32) * all_totals[where, :]) * (inverse[...] * scale)
+        ).astype(BF16)
     each = width // groups
-    product = dot(normed[...], back[...], FIRST) * (1.0 / every)
+    product = (dot(turned_near[...], back[:near, :]) + dot(turned_far[...], back[near:, :])) * (1.0 / every)
     for group in range(groups):
         pack_into(packed.at[group], product[group * each : (group + 1) * each, :], full)
 
@@ -313,13 +354,16 @@
 
 
 def image_body(
-    scalars, features, proj, gain, text_near, text_far, weights_own, unit, inverse,
-    feature_grad, back, product,
+    scalars, features, proj, gain, text_near, text_third, text_fourth, weights_near, weights_third, weights_fourth,
+    unit, inverse, feature_grad, token, back, product,
 ):
     rows, width = features.shape
-    near = 2 * rows
     scale = scalars[0]
-    product[...] = dot(weights_own[:, :near], text_near[...]) + dot(weights_own[:, near:], text_far[...])
+    product[...] = (
+        dot(weights_near[:rows, :], text_near[...])
+        + dot(weights_third[...], text_third[...])
+        + dot(weights_fourth[...], text_fourth[...])
+    )
 
     def image_chunk(where):
         values = product[where, :] * scale
@@ -343,12 +387,15 @@
         ).astype(BF16)
 
     over_rows(rows, 32, feature_chunk)
-
-
-def text_body(scalars, text, weights_near, unit, text_grad, product):
+    token[...] = jnp.zeros_like(token)
+
+
+def text_body(scalars, text, weights_near, weights_far, unit_near, unit_far, after, text_grad, token, product):
     rows = text.shape[0]
     scale = scalars[0]
-    product[...] = dot(weights_near[:, :rows], unit[...], FIRST)
+    product[...] = dot(weights_near[:, :rows], unit_near[...], FIRST) + dot(
+        weights_far[:, :rows], unit_far[...], FIRST
+    )
 
     def text_chunk(where):
         values = product[where, :] * scale
@@ -360,9 +407,10 @@
         ).astype(BF16)
 
     over_rows(rows, 32, text_chunk)
-
-
-def first_sum_body(place, keep_lead, across, keep_tail, *refs):
+    token[...] = after[:8, :LANES].astype(F32) * 0.0
+
+
+def first_sum_body(place, token, keep_lead, across, keep_tail, *refs):
     steps = keep_lead.shape[0]
     along, refs = refs[: steps - 1], refs[steps - 1 :]
     leads, (tail, tail_across, ordered) = refs[:steps], refs[steps:]
@@ -389,7 +437,7 @@
     total[split:, :] = (tail[...].astype(F32) + tail_across[...].astype(F32)).astype(BF16)
 
 
-def finish_body(members, place, *refs):
+def finish_body(members, place, token, *refs):
     packets, (proj_grad, gain_gradient, ordered) = refs[:members], refs[members:]
     count, full = packets[0].shape
     rows, width = proj_grad.shape
@@ -444,93 +492,94 @@
     f1 = send(f0, "loop", lambda p: p ^ 1)
     t1 = send(t0, "loop", lambda p: p ^ 1)
 
-    normed_near, unit_near, inverse_near, text_near = call(
+    wide, half, one = ((near, width), BF16), ((rows, width), BF16), ((near, 1), F32)
+    square, part, turned = ((near, near), BF16), ((near, columns), BF16), ((width, near), BF16)
+
+    outs = [turned, wide, part, one, wide, part, square, one, ((width, columns), BF16), TOKEN]
+    (
+        turned_near, unit_near, unit_columns_near, inverse_near, text_near, text_columns_near,
+        weights_near, totals_near, proj_columns, token,
+    ) = call(
         near_body,
-        [((near, width), BF16), ((near, width), BF16), ((near, 1), F32), ((near, width), BF16)],
-        [pltpu.VMEM((near, width), F32)],
+        outs,
+        [wide, ((near, width), F32), ((near, near), F32)],
+        smem=2,
+        flops=3 * near * width * width,
+        moved=8 * near * width,
+    )(scalars, place, f0, f1, t0, t1, proj, gain_row)
+
+    t_after, f2_after, token = lax.optimization_barrier((t0, f2, token))
+    t2 = send(t_after, "loop", lambda p: p ^ 2)
+    f3 = send(f2_after, "loop", lambda p: p ^ 1)
+
+    turned_far, unit_far, unit_columns_far, inverse_far, weights_far, totals_far, token = call(
+        far_body,
+        [turned, wide, part, one, square, one, TOKEN],
+        [wide, ((near, width), F32), ((near, near), F32)],
+        smem=2,
+        flops=3 * near * width * width,
+        moved=8 * near * width,
+    )(scalars, place, f2, f3, proj, gain_row, text_near, token)
+
+    t2_after, token = lax.optimization_barrier((t2, token))
+    t3 = send(t2_after, "loop", lambda p: p ^ 1)
+
+    narrow = ((every, rows), BF16)
+    text_third, weights_third, image_back, totals = call(
+        third_body,
+        [half, ((rows, rows), BF16), ((every, columns), F32), ((every, 1), F32)],
+        [((rows, columns), BF16), narrow, ((every, rows), F32)],
+        smem=2,
         flops=2 * near * width * width,
         moved=8 * near * width,
-    )(f0, f1, t0, t1, proj, gain_row)
-
-    t_after, f2, normed_near, unit_near, inverse_near, text_near = lax.optimization_barrier(
-        (t0, f2, normed_near, unit_near, inverse_near, text_near)
+    )(
+        scalars, place, t2, unit_near, unit_far, weights_near, weights_far, totals_near, totals_far,
+        text_columns_near, token,
     )
-    t2 = send(t_after, "loop", lambda p: p ^ 2)
-    f3 = send(f2, "loop", lambda p: p ^ 1)
-
-    normed, unit, inverse, weights_near, totals_near, proj_columns = call(
-        far_body,
+
+    outs = call(
+        functools.partial(partial_body, members, groups, lead),
+        [((steps, lead, full), BF16), ((steps, lead, full), BF16)]
+        + [((2, tail, full), BF16)] * steps
+        + [half, ((rows, rows), BF16)],
         [
-            ((every, width), BF16), ((every, width), BF16), ((every, 1), F32),
-            ((every, near), BF16), ((every, 1), F32), ((width, columns), BF16),
+            ((rows, columns), BF16), narrow, ((every, rows), F32), ((every, 1), F32), ((every, columns), BF16),
+            ((groups,) + packet, BF16),
         ],
-        [pltpu.VMEM((near, width), F32), pltpu.VMEM((every, near), F32)],
         smem=2,
         flops=4 * near * width * width,
         moved=16 * near * width,
-    )(scalars, place, f2, f3, proj, gain_row, normed_near, unit_near, inverse_near, text_near)
-
-    t2, normed, unit, inverse, weights_near, totals_near, proj_columns = lax.optimization_barrier(
-        (t2, normed, unit, inverse, weights_near, totals_near, proj_columns)
-    )
-    t3 = send(t2, "loop", lambda p: p ^ 1)
-
-    outs = call(
-        functools.partial(partial_body, members, groups, lead),
-        [((steps, lead, full), BF16), ((steps, lead, full), BF16), ((2, tail, full), BF16)]
-        + [((2, tail, full), BF16)] * (steps - 1)
-        + [((near, width), BF16), ((rows, every), BF16)],
-        [
-            pltpu.VMEM((every, every), BF16),
-            pltpu.VMEM((every, 1), F32),
-            pltpu.VMEM((every, near), F32),
-            pltpu.VMEM((every, columns), BF16),
-            pltpu.VMEM((every, columns), BF16),
-            pltpu.VMEM((every, columns), BF16),
-            pltpu.VMEM((groups,) + packet, BF16),
-        ],
-        smem=2,
-        flops=6 * near * width * width,
-        moved=16 * near * width,
     )(
-        scalars, place, t2, t3, text_near, unit, inverse, normed, weights_near, totals_near,
-        proj_columns, gain_row,
+        scalars, place, t3, unit_near, unit_far, totals, image_back, unit_columns_near, unit_columns_far,
+        inverse_near, inverse_far, turned_near, turned_far, proj_columns, gain_row,
     )
     across, keep_lead, keep_tail = outs[:3]
-    along, (text_far, weights_own) = outs[3 : 2 + steps], outs[2 + steps :]
+    along, (text_fourth, weights_fourth) = outs[3 : 2 + steps], outs[2 + steps :]
 
     along = [send(along[step - 1], "rep", lambda p: p ^ (2 * step)) for step in range(1, steps)]
     across = send(across, "rep", lambda p: p ^ 1)
 
-    (feature_grad,) = call(
+    feature_grad, token = call(
         image_body,
-        [((rows, width), BF16)],
-        [pltpu.VMEM((rows, width), BF16), pltpu.VMEM((rows, width), F32)],
+        [half, TOKEN],
+        [half, ((rows, width), F32)],
         smem=1,
         flops=4 * near * width * width,
         moved=12 * near * width,
-    )(scalars, f0, proj, gain_row, text_near, text_far, weights_own, unit, inverse)
-    feature_grad, across = lax.optimization_barrier((feature_grad, across))
+    )(
+        scalars, f0, proj, gain_row, text_near, text_third, text_fourth, weights_near, weights_third,
+        weights_fourth, unit_near, inverse_near,
+    )
 
     outs = call(
         first_sum_body,
         [((lead, full), BF16)] * steps + [((tail, full), BF16)] * 2,
-        [pltpu.VMEM((steps, 2, tail, full), BF16)],
+        [((steps, 2, tail, full), BF16)],
         smem=1,
         moved=4 * each * width,
-    )(place, keep_lead, across, keep_tail, *along)
+    )(place, token, keep_lead, across, keep_tail, *along)
     leads = [outs[0]] + [send(outs[step], "rep", lambda p: p ^ (2 * step)) for step in range(1, steps)]
     tail_across = send(outs[steps + 1], "rep", lambda p: p ^ 1)
-
-    (text_grad,) = call(
-        text_body,
-        [((rows, width), BF16)],
-        [pltpu.VMEM((rows, width), F32)],
-        smem=1,
-        flops=2 * near * width * width,
-        moved=6 * near * width,
-    )(scalars, t0, weights_near, unit)
-    text_grad, tail_across = lax.optimization_barrier((text_grad, tail_across))
 
     (reduced,) = call(
         last_sum_body,
@@ -538,14 +587,22 @@
         moved=4 * each * width,
     )(outs[steps], tail_across, *leads)
     blocks = [reduced] + [send(reduced, "loop", lambda p: p ^ k) for k in range(1, members)]
+    text_grad, token = call(
+        text_body,
+        [half, TOKEN],
+        [((rows, width), F32)],
+        smem=1,
+        flops=2 * near * width * width,
+        moved=6 * near * width,
+    )(scalars, t0, weights_near, weights_far, unit_near, unit_far, reduced)
 
     proj_grad, gain_gradient = call(
         functools.partial(finish_body, members),
         [((each, width), F32), ((1, width), F32)],
-        [pltpu.VMEM((members, BAND, LANES), F32)],
+        [((members, BAND, LANES), F32)],
         smem=1,
         moved=8 * each * width,
-    )(place, *blocks)
+    )(place, token, *blocks)
     return feature_grad[:, None, :], text_grad[:, None, :], proj_grad, gain_gradient.reshape(width)
 
 

time: 68.4 us -> 67.4 us (0.985)
  waiting for transfers between devices: 8.59 us -> 14.2 us
  local copies, waits for them, and re-layouts: 9.27 us -> 4.49 us
  starting transfers between devices: 18.4 us -> 17.1 us
    ppermute x17, waiting for transfers between devices: 8.59 us -> 14.2 us  [send(): return lax.ppermute(value, axis, [(p, target(p)) for p in range(count)])]
    unnamed x20 -> x12, local copies, waits for them, and re-layouts: 8.57 us -> 3.79 us
    ppermute x17, starting transfers between devices: 18.4 us -> 17.1 us  [send(): return lax.ppermute(value, axis, [(p, target(p)) for p in range(count)])]
    pallas_call x8 -> x9, Pallas kernels: 28.9 us -> 28.5 us  [run(): pl.pallas_call(body, out_shape=[jax.ShapeDtypeStruct(shape, kind) for sha...]
  transfers between devices with their start and end apart: 17 -> 17, of which waited for: 7 -> 8; matrix products, arithmetic and copies ran while one was open for 1% -> 1% of each run, Pallas kernels for 30% -> 32%
where the time goes in v5:
time: 67.4 us; the launch traced here: 67.1 us
  Pallas kernels  28.5 us (42%)
  starting transfers between devices  17.1 us (25%)
  waiting for transfers between devices  14.2 us (21%)
  local copies, waits for them, and re-layouts  4.49 us (7%)
  between operations  2.02 us (3%)
  other arithmetic  0.77 us (1%)
    pallas_call x9, Pallas kernels, run(): pl.pallas_call(body, out_shape=[jax.ShapeDtypeStruct(shape, kind) for sha...  28.5 us
    ppermute x17, starting transfers between devices, send(): return lax.ppermute(value, axis, [(p, target(p)) for p in range(count)])  17.1 us
    ppermute x17, waiting for transfers between devices, send(): return lax.ppermute(value, axis, [(p, target(p)) for p in range(count)])  14.2 us
    unnamed x12, local copies, waits for them, and re-layouts  3.79 us
  transfers between devices with their start and end apart: 17, of which 8 were waited for; matrix products, arithmetic and copies ran while one was open for 1% of the time, Pallas kernels for 32%

profile of v5, /device:TPU:0, one launch (start us, length us, event | category | flops | bytes accessed | tf_op | source)
XLA Modules:
  0.0 67.1 jit_solution(14599601866410369284)
XLA Ops:
  0.6 0.5 collective-permute-start
  1.1 0.1 collective-permute-start.1
  1.2 2.9 %collective-permute-start.2 = (bf16[192,1152]{1,0:T(8,128)(2,1)}, bf16[192,1152]{1,0:T(8,128)(2,1)S(1)}, u32[]{:S(2)}, u32[]{:S(2)}) collective-permute-start(bf16[192,1152]{1,0:T(8,128)(2,1)} %bitcast.7), channel_id=1, source_target_pairs={{0,16},{8,24},{16,0},{24,8},{1,17},{9,25},{17,1},{25,9},{2,18},{10... | collective-permute-start | bytes 1327112 | tf_op jit(solution)/shard_map/ppermute | solution.py:34
  5.4 0.7 %reshape.14.gain = f32[1,1152]{1,0:T(1,128)S(1)} reshape(f32[1152]{0:T(1024)} %param.9) | data formatting | bytes 9216 | tf_op jit(solution)/shard_map/reshape | solution.py:484
  6.1 0.1 pad_maximum_fusion.scalars
  6.2 0.1 pad_add_fusion.place
  6.3 0.0 collective-permute-done.f1
  6.3 0.0 collective-permute-done.1.t1
  6.3 1.7 %copy-done = bf16[1152,1152]{1,0:T(8,128)(2,1)S(1)} copy-done((bf16[1152,1152]{1,0:T(8,128)(2,1)S(1)}, bf16[1152,1152]{1,0:T(8,128)(2,1)}, u32[]{:S(2)}) %copy-start) | copy-done | bytes 2654232
  8.1 1.0 %copy-done.2 = bf16[192,1,1152]{2,0,1:T(8,128)(2,1)S(1)} copy-done((bf16[192,1,1152]{2,0,1:T(8,128)(2,1)S(1)}, bf16[192,1,1152]{2,0,1:T(8,128)(2,1)}, u32[]{:S(2)}) %copy-start.2) | copy-done | bytes 442392
  9.1 1.0 %copy-done.4 = bf16[192,1,1152]{2,0,1:T(8,128)(2,1)S(1)} copy-done((bf16[192,1,1152]{2,0,1:T(8,128)(2,1)S(1)}, bf16[192,1,1152]{2,0,1:T(8,128)(2,1)}, u32[]{:S(2)}) %copy-start.4) | copy-done | bytes 442392
  10.1 6.0 %shard_map.93 = (bf16[1152,384]{1,0:T(8,128)(2,1)S(1)}, bf16[384,1152]{1,0:T(8,128)(2,1)S(1)}, bf16[384,288]{1,0:T(8,128)(2,1)S(1)}, f32[384,1]{1,0:T(8,128)S(1)...) custom-call(f32[2]{0:T(128)S(1)} %pad_maximum_fusion.scalars, ...), custom_call_target="tpu_custom_call" | custom-call | flops 1528823808 | bytes 3538944 | tf_op jit(solution)/shard_map/pallas_call | solution.py:137
  16.1 0.0 collective-permute-done.2.f2
  16.1 0.4 collective-permute-start.4
  16.6 0.3 collective-permute-start.3
  16.9 1.1 %collective-permute-done.4.f3 = bf16[192,1152]{1,0:T(8,128)(2,1)S(1)} collective-permute-done((bf16[192,1152]{1,0:T(8,128)(2,1)S(1)}, bf16[192,1152]{1,0:T(8,128)(2,1)S(1)}, u32[]{:S(2)}, u32[]{:S(2)}) %collective-permute-start.4) | collective-permute-done | bytes 442400 | tf_op jit(solution)/shard_map/ppermute | solution.py:34
  18.0 5.2 %shard_map.94 = (bf16[1152,384]{1,0:T(8,128)(2,1)S(1)}, bf16[384,1152]{1,0:T(8,128)(2,1)S(1)}, bf16[384,288]{1,0:T(8,128)(2,1)S(1)}, f32[384,1]{1,0:T(8,128)S(1)...) custom-call(f32[2]{0:T(128)S(1)} %pad_maximum_fusion.scalars, ...), custom_call_target="tpu_custom_call" | custom-call | flops 1528823808 | bytes 3538944 | tf_op jit(solution)/shard_map/pallas_call | solution.py:137
  23.3 5.5 %collective-permute-done.3.t2 = bf16[192,1152]{1,0:T(8,128)(2,1)S(1)} collective-permute-done((bf16[192,1152]{1,0:T(8,128)(2,1)S(1)}, bf16[192,1152]{1,0:T(8,128)(2,1)S(1)}, u32[]{:S(2)}, u32[]{:S(2)}) %collective-permute-start.3) | collective-permute-done | bytes 442400 | tf_op jit(solution)/shard_map/ppermute | solution.py:34
  28.8 0.0 collective-permute-start.5
  28.8 3.3 %shard_map.95 = (bf16[192,1152]{1,0:T(8,128)(2,1)S(1)}, bf16[192,192]{1,0:T(8,128)(2,1)S(1)}, f32[768,288]{1,0:T(8,128)S(1)}, f32[768,1]{1,0:T(8,128)S(1)}) custom-call(f32[2]{0:T(128)S(1)} %pad_maximum_fusion.scalars, s32[2]{0:T(128)S(1)} %pad_add_fusion.place, bf16[192,1152]{1,0:T(8,128)(2,1)S(1)} %collective-permute-done.3.t2, ...), custom_call_target="tpu_custom_call" | custom-call | flops 1019215872 | bytes 3538944 | tf_op jit(solution)/shard_map/pallas_call | solution.py:137
  32.1 0.0 collective-permute-done.5.t3
  32.1 0.0 copy-start.3
  32.1 4.9 %shard_map.96 = (bf16[4,112,256]{2,1,0:T(8,128)(2,1)S(1)}, bf16[4,112,256]{2,1,0:T(8,128)(2,1)S(1)}, bf16[2,64,256]{2,1,0:T(8,128)(2,1)S(1)}, bf16[2,64,256]{2,1...) custom-call(f32[2]{0:T(128)S(1)} %pad_maximum_fusion.scalars, ...), custom_call_target="tpu_custom_call" | custom-call | flops 2038431744 | bytes 7077888 | tf_op jit(solution)/shard_map/pallas_call | solution.py:137
  37.0 1.6 %collective-permute-start.6 = (bf16[4,112,256]{2,1,0:T(8,128)(2,1)S(1)}, bf16[4,112,256]{2,1,0:T(8,128)(2,1)S(1)}, u32[]{:S(2)}, u32[]{:S(2)}) collective-permute-start(bf16[4,112,256]{2,1,0:T(8,128)(2,1)S(1)} %get-tuple-element.81), channel_id=1, source_target_pairs={{0,1},{1,0},{2,3},{3,2},{4,5},{5,4},{6,7},{7,6},{8,9},{9,8},{10,11... | collective-permute-start | bytes 688136 | tf_op jit(solution)/shard_map/ppermute | solution.py:34
  38.6 1.6 %collective-permute-start.7 = (bf16[2,64,256]{2,1,0:T(8,128)(2,1)S(1)}, bf16[2,64,256]{2,1,0:T(8,128)(2,1)S(1)}, u32[]{:S(2)}, u32[]{:S(2)}) collective-permute-start(bf16[2,64,256]{2,1,0:T(8,128)(2,1)S(1)} %get-tuple-element.83), channel_id=1, source_target_pairs={{0,2},{1,3},{2,0},{3,1},{4,6},{5,7},{6,4},{7,5},{8,10},{9,11},{10,... | collective-permute-start | bytes 196616 | tf_op jit(solution)/shard_map/ppermute | solution.py:34
  40.2 2.6 %collective-permute-start.8 = (bf16[2,64,256]{2,1,0:T(8,128)(2,1)S(1)}, bf16[2,64,256]{2,1,0:T(8,128)(2,1)S(1)}, u32[]{:S(2)}, u32[]{:S(2)}) collective-permute-start(bf16[2,64,256]{2,1,0:T(8,128)(2,1)S(1)} %get-tuple-element.84), channel_id=1, source_target_pairs={{0,4},{1,5},{2,6},{3,7},{4,0},{5,1},{6,2},{7,3},{8,12},{9,13},{10,... | collective-permute-start | bytes 196616 | tf_op jit(solution)/shard_map/ppermute | solution.py:34
  42.8 0.2 collective-permute-start.9
  43.0 4.1 %shard_map.97 = (bf16[192,1152]{1,0:T(8,128)(2,1)}, f32[8,128]{1,0:T(8,128)S(1)}) custom-call(f32[2]{0:T(128)S(1)} %pad_maximum_fusion.scalars, bf16[192,1152]{1,0:T(8,128)(2,1)S(1)} %bitcast.9, bf16[1152,1152]{1,0:T(8,128)(2,1)S(1)} %copy-done.1, f32[1,1152]{1,0:T(1,128)S(1)} %reshape.14.gain, bf16[384,1152]{1,0:T(8,128)(2,1)S(1)} %get-tuple-element.50.text_near, ...), custom_call_target="tpu_custom_call" | custom-call | flops 2038431744 | bytes 5308416 | tf_op jit(solution)/shard_map/pallas_call | solution.py:137
  47.1 0.8 %collective-permute-done.8.refs_1_ = bf16[2,64,256]{2,1,0:T(8,128)(2,1)S(1)} collective-permute-done((bf16[2,64,256]{2,1,0:T(8,128)(2,1)S(1)}, bf16[2,64,256]{2,1,0:T(8,128)(2,1)S(1)}, u32[]{:S(2)}, u32[]{:S(2)}) %collective-permute-start.8) | collective-permute-done | bytes 65568 | tf_op jit(solution)/shard_map/ppermute | solution.py:34
  47.9 1.0 %collective-permute-done.9.refs_2_ = bf16[2,64,256]{2,1,0:T(8,128)(2,1)S(1)} collective-permute-done((bf16[2,64,256]{2,1,0:T(8,128)(2,1)S(1)}, bf16[2,64,256]{2,1,0:T(8,128)(2,1)S(1)}, u32[]{:S(2)}, u32[]{:S(2)}) %collective-permute-start.9) | collective-permute-done | bytes 65568 | tf_op jit(solution)/shard_map/ppermute | solution.py:34
  48.9 0.0 collective-permute-done.6.across
  48.9 0.6 shard_map.98
  49.6 1.3 %collective-permute-start.11 = (bf16[112,256]{1,0:T(8,128)(2,1)S(1)}, bf16[112,256]{1,0:T(8,128)(2,1)S(1)}, u32[]{:S(2)}, u32[]{:S(2)}) collective-permute-start(bf16[112,256]{1,0:T(8,128)(2,1)S(1)} %get-tuple-element.89), channel_id=1, source_target_pairs={{0,2},{1,3},{2,0},{3,1},{4,6},{5,7},{6,4},{7,5},{8,10},{9,11},{10,... | collective-permute-start | bytes 172040 | tf_op jit(solution)/shard_map/ppermute | solution.py:34
  50.8 1.7 %collective-permute-start.12 = (bf16[112,256]{1,0:T(8,128)(2,1)S(1)}, bf16[112,256]{1,0:T(8,128)(2,1)S(1)}, u32[]{:S(2)}, u32[]{:S(2)}) collective-permute-start(bf16[112,256]{1,0:T(8,128)(2,1)S(1)} %get-tuple-element.90), channel_id=1, source_target_pairs={{0,4},{1,5},{2,6},{3,7},{4,0},{5,1},{6,2},{7,3},{8,12},{9,13},{10,... | collective-permute-start | bytes 172040 | tf_op jit(solution)/shard_map/ppermute | solution.py:34
  52.5 1.5 %collective-permute-start.13 = (bf16[112,256]{1,0:T(8,128)(2,1)S(1)}, bf16[112,256]{1,0:T(8,128)(2,1)S(1)}, u32[]{:S(2)}, u32[]{:S(2)}) collective-permute-start(bf16[112,256]{1,0:T(8,128)(2,1)S(1)} %get-tuple-element.91), channel_id=1, source_target_pairs={{0,6},{1,7},{2,4},{3,5},{4,2},{5,3},{6,0},{7,1},{8,14},{9,15},{10,... | collective-permute-start | bytes 172040 | tf_op jit(solution)/shard_map/ppermute | solution.py:34
  54.0 0.5 collective-permute-start.10
  54.5 3.4 %collective-permute-done.10.tail_across = bf16[64,256]{1,0:T(8,128)(2,1)S(1)} collective-permute-done((bf16[64,256]{1,0:T(8,128)(2,1)S(1)}, bf16[64,256]{1,0:T(8,128)(2,1)S(1)}, u32[]{:S(2)}, u32[]{:S(2)}) %collective-permute-start.10) | collective-permute-done | bytes 32800 | tf_op jit(solution)/shard_map/ppermute | solution.py:34
  57.9 0.0 collective-permute-done.11.refs_1_
  57.9 0.0 collective-permute-done.12.refs_2_
  57.9 0.6 collective-permute-done.13.refs_3_
  58.5 0.1 collective-permute-start.16
  58.6 1.2 %collective-permute-start.15 = (bf16[176,256]{1,0:T(8,128)(2,1)S(1)}, bf16[176,256]{1,0:T(8,128)(2,1)S(1)}, u32[]{:S(2)}, u32[]{:S(2)}) collective-permute-start(bf16[176,256]{1,0:T(8,128)(2,1)S(1)} %shard_map.99.after.refs_0_), channel_id=1, source_target_pairs={{0,16},{8,24},{16,0},{24,8},{1,17},{9,25},{17,1},{25,9},{2,18},{10... | collective-permute-start | bytes 270344 | tf_op jit(solution)/shard_map/ppermute | solution.py:34
  59.8 0.7 %collective-permute-start.14 = (bf16[176,256]{1,0:T(8,128)(2,1)S(1)}, bf16[176,256]{1,0:T(8,128)(2,1)S(1)}, u32[]{:S(2)}, u32[]{:S(2)}) collective-permute-start(bf16[176,256]{1,0:T(8,128)(2,1)S(1)} %shard_map.99.after.refs_0_), channel_id=1, source_target_pairs={{0,8},{8,0},{16,24},{24,16},{1,9},{9,1},{17,25},{25,17},{2,10},{10... | collective-permute-start | bytes 270344 | tf_op jit(solution)/shard_map/ppermute | solution.py:34
  60.5 2.6 %shard_map.100 = (bf16[192,1152]{1,0:T(8,128)(2,1)}, f32[8,128]{1,0:T(8,128)S(1)}) custom-call(f32[2]{0:T(128)S(1)} %pad_maximum_fusion.scalars, bf16[192,1152]{1,0:T(8,128)(2,1)S(1)} %bitcast.13, bf16[384,384]{1,0:T(8,128)(2,1)S(1)} %get-tuple-element.57.weights_near, bf16[384,384]{1,0:T(8,128)(2,1)S(1)} %get-tuple-element.58.weights_far, ...), custom_call_target="tpu_custom_call" | custom-call | flops 1019215872 | bytes 2654208 | tf_op jit(solution)/shard_map/pallas_call | solution.py:137
  63.0 0.4 collective-permute-done.16.refs_3_
  63.4 1.4 %collective-permute-done.15.refs_2_ = bf16[176,256]{1,0:T(8,128)(2,1)S(1)} collective-permute-done((bf16[176,256]{1,0:T(8,128)(2,1)S(1)}, bf16[176,256]{1,0:T(8,128)(2,1)S(1)}, u32[]{:S(2)}, u32[]{:S(2)}) %collective-permute-start.15) | collective-permute-done | bytes 90144 | tf_op jit(solution)/shard_map/ppermute | solution.py:34
  64.8 1.7 %shard_map.101 = (f32[144,1152]{1,0:T(8,128)}, f32[1,1152]{1,0:T(1,128)S(1)}) custom-call(s32[2]{0:T(128)S(1)} %pad_add_fusion.place, f32[8,128]{1,0:T(8,128)S(1)} %get-tuple-element.93.token, bf16[176,256]{1,0:T(8,128)(2,1)S(1)} %shard_map.99.after.refs_0_, bf16[176,256]{1,0:T(8,128)(2,1)S(1)} %collective-permute-done.14.refs_1_, ...), custom_call_target="tpu_custom_call" | custom-call | bytes 1327104 | tf_op jit(solution)/shard_map/pallas_call | solution.py:137
  66.5 0.6 reduce
  (11 shorter events, 0.1 us)
Async XLA Ops:
  0.6 5.7 %collective-permute-start = (bf16[192,1152]{1,0:T(8,128)(2,1)}, bf16[192,1152]{1,0:T(8,128)(2,1)S(1)}, u32[]{:S(2)}, u32[]{:S(2)}) collective-permute-start(bf16[192,1152]{1,0:T(8,128)(2,1)} %bitcast.6), channel_id=1, source_target_pairs={{0,8},{8,0},{16,24},{24,16},{1,9},{9,1},{17,25},{25,17},{2,10},{10... | collective-permute-start | bytes 1327112 | tf_op jit(solution)/shard_map/ppermute | solution.py:34
  1.1 5.2 %collective-permute-start.1 = (bf16[192,1152]{1,0:T(8,128)(2,1)}, bf16[192,1152]{1,0:T(8,128)(2,1)S(1)}, u32[]{:S(2)}, u32[]{:S(2)}) collective-permute-start(bf16[192,1152]{1,0:T(8,128)(2,1)} %bitcast.10), channel_id=1, source_target_pairs={{0,8},{8,0},{16,24},{24,16},{1,9},{9,1},{17,25},{25,17},{2,10},{10... | collective-permute-start | bytes 1327112 | tf_op jit(solution)/shard_map/ppermute | solution.py:34
  1.2 14.9 %collective-permute-start.2 = (bf16[192,1152]{1,0:T(8,128)(2,1)}, bf16[192,1152]{1,0:T(8,128)(2,1)S(1)}, u32[]{:S(2)}, u32[]{:S(2)}) collective-permute-start(bf16[192,1152]{1,0:T(8,128)(2,1)} %bitcast.7), channel_id=1, source_target_pairs={{0,16},{8,24},{16,0},{24,8},{1,17},{9,25},{17,1},{25,9},{2,18},{10... | collective-permute-start | bytes 1327112 | tf_op jit(solution)/shard_map/ppermute | solution.py:34
  6.3 1.8 %copy-start = (bf16[1152,1152]{1,0:T(8,128)(2,1)S(1)}, bf16[1152,1152]{1,0:T(8,128)(2,1)}, u32[]{:S(2)}) copy-start(bf16[1152,1152]{1,0:T(8,128)(2,1)} %proj.5) | copy-start | bytes 7962628
  8.1 1.0 %copy-start.2 = (bf16[192,1,1152]{2,0,1:T(8,128)(2,1)S(1)}, bf16[192,1,1152]{2,0,1:T(8,128)(2,1)}, u32[]{:S(2)}) copy-start(bf16[192,1,1152]{2,0,1:T(8,128)(2,1)} %param.6) | copy-start | bytes 1327108
  9.1 1.0 %copy-start.4 = (bf16[192,1,1152]{2,0,1:T(8,128)(2,1)S(1)}, bf16[192,1,1152]{2,0,1:T(8,128)(2,1)}, u32[]{:S(2)}) copy-start(bf16[192,1,1152]{2,0,1:T(8,128)(2,1)} %param.7) | copy-start | bytes 1327108
  10.1 7.9 %copy-start.1 = (bf16[1152,1152]{1,0:T(8,128)(2,1)S(1)}, bf16[1152,1152]{1,0:T(8,128)(2,1)}, u32[]{:S(2)}) copy-start(bf16[1152,1152]{1,0:T(8,128)(2,1)} %proj.5) | copy-start | bytes 7962628
  16.1 1.9 %collective-permute-start.4 = (bf16[192,1152]{1,0:T(8,128)(2,1)S(1)}, bf16[192,1152]{1,0:T(8,128)(2,1)S(1)}, u32[]{:S(2)}, u32[]{:S(2)}) collective-permute-start(bf16[192,1152]{1,0:T(8,128)(2,1)S(1)} %collective-permute-done.2.f2), channel_id=1, source_target_pairs={{0,8},{8,0},{16,24},{24,16},{1,9},{9,1},{17,25},{25,17},{2,10},{10... | collective-permute-start | bytes 1327112 | tf_op jit(solution)/shard_map/ppermute | solution.py:34
  16.6 12.2 %collective-permute-start.3 = (bf16[192,1152]{1,0:T(8,128)(2,1)S(1)}, bf16[192,1152]{1,0:T(8,128)(2,1)S(1)}, u32[]{:S(2)}, u32[]{:S(2)}) collective-permute-start(bf16[192,1152]{1,0:T(8,128)(2,1)S(1)} %bitcast.12), channel_id=1, source_target_pairs={{0,16},{8,24},{16,0},{24,8},{1,17},{9,25},{17,1},{25,9},{2,18},{10... | collective-permute-start | bytes 1327112 | tf_op jit(solution)/shard_map/ppermute | solution.py:34
  28.8 3.3 %collective-permute-start.5 = (bf16[192,1152]{1,0:T(8,128)(2,1)S(1)}, bf16[192,1152]{1,0:T(8,128)(2,1)S(1)}, u32[]{:S(2)}, u32[]{:S(2)}) collective-permute-start(bf16[192,1152]{1,0:T(8,128)(2,1)S(1)} %collective-permute-done.3.t2), channel_id=1, source_target_pairs={{0,8},{8,0},{16,24},{24,16},{1,9},{9,1},{17,25},{25,17},{2,10},{10... | collective-permute-start | bytes 1327112 | tf_op jit(solution)/shard_map/ppermute | solution.py:34
  32.1 10.9 %copy-start.3 = (bf16[192,1,1152]{2,0,1:T(8,128)(2,1)S(1)}, bf16[192,1,1152]{2,0,1:T(8,128)(2,1)}, u32[]{:S(2)}) copy-start(bf16[192,1,1152]{2,0,1:T(8,128)(2,1)} %param.6) | copy-start | bytes 1327108
  37.0 11.9 %collective-permute-start.6 = (bf16[4,112,256]{2,1,0:T(8,128)(2,1)S(1)}, bf16[4,112,256]{2,1,0:T(8,128)(2,1)S(1)}, u32[]{:S(2)}, u32[]{:S(2)}) collective-permute-start(bf16[4,112,256]{2,1,0:T(8,128)(2,1)S(1)} %get-tuple-element.81), channel_id=1, source_target_pairs={{0,1},{1,0},{2,3},{3,2},{4,5},{5,4},{6,7},{7,6},{8,9},{9,8},{10,11... | collective-permute-start | bytes 688136 | tf_op jit(solution)/shard_map/ppermute | solution.py:34
  38.6 8.5 %collective-permute-start.7 = (bf16[2,64,256]{2,1,0:T(8,128)(2,1)S(1)}, bf16[2,64,256]{2,1,0:T(8,128)(2,1)S(1)}, u32[]{:S(2)}, u32[]{:S(2)}) collective-permute-start(bf16[2,64,256]{2,1,0:T(8,128)(2,1)S(1)} %get-tuple-element.83), channel_id=1, source_target_pairs={{0,2},{1,3},{2,0},{3,1},{4,6},{5,7},{6,4},{7,5},{8,10},{9,11},{10,... | collective-permute-start | bytes 196616 | tf_op jit(solution)/shard_map/ppermute | solution.py:34
  40.2 7.7 %collective-permute-start.8 = (bf16[2,64,256]{2,1,0:T(8,128)(2,1)S(1)}, bf16[2,64,256]{2,1,0:T(8,128)(2,1)S(1)}, u32[]{:S(2)}, u32[]{:S(2)}) collective-permute-start(bf16[2,64,256]{2,1,0:T(8,128)(2,1)S(1)} %get-tuple-element.84), channel_id=1, source_target_pairs={{0,4},{1,5},{2,6},{3,7},{4,0},{5,1},{6,2},{7,3},{8,12},{9,13},{10,... | collective-permute-start | bytes 196616 | tf_op jit(solution)/shard_map/ppermute | solution.py:34
  42.8 6.1 %collective-permute-start.9 = (bf16[2,64,256]{2,1,0:T(8,128)(2,1)S(1)}, bf16[2,64,256]{2,1,0:T(8,128)(2,1)S(1)}, u32[]{:S(2)}, u32[]{:S(2)}) collective-permute-start(bf16[2,64,256]{2,1,0:T(8,128)(2,1)S(1)} %get-tuple-element.85), channel_id=1, source_target_pairs={{0,6},{1,7},{2,4},{3,5},{4,2},{5,3},{6,0},{7,1},{8,14},{9,15},{10,... | collective-permute-start | bytes 196616 | tf_op jit(solution)/shard_map/ppermute | solution.py:34
  43.0 17.4 %copy-start.5 = (bf16[192,1,1152]{2,0,1:T(8,128)(2,1)S(1)}, bf16[192,1,1152]{2,0,1:T(8,128)(2,1)}, u32[]{:S(2)}) copy-start(bf16[192,1,1152]{2,0,1:T(8,128)(2,1)} %param.7) | copy-start | bytes 1327108
  49.6 8.4 %collective-permute-start.11 = (bf16[112,256]{1,0:T(8,128)(2,1)S(1)}, bf16[112,256]{1,0:T(8,128)(2,1)S(1)}, u32[]{:S(2)}, u32[]{:S(2)}) collective-permute-start(bf16[112,256]{1,0:T(8,128)(2,1)S(1)} %get-tuple-element.89), channel_id=1, source_target_pairs={{0,2},{1,3},{2,0},{3,1},{4,6},{5,7},{6,4},{7,5},{8,10},{9,11},{10,... | collective-permute-start | bytes 172040 | tf_op jit(solution)/shard_map/ppermute | solution.py:34
  50.8 7.1 %collective-permute-start.12 = (bf16[112,256]{1,0:T(8,128)(2,1)S(1)}, bf16[112,256]{1,0:T(8,128)(2,1)S(1)}, u32[]{:S(2)}, u32[]{:S(2)}) collective-permute-start(bf16[112,256]{1,0:T(8,128)(2,1)S(1)} %get-tuple-element.90), channel_id=1, source_target_pairs={{0,4},{1,5},{2,6},{3,7},{4,0},{5,1},{6,2},{7,3},{8,12},{9,13},{10,... | collective-permute-start | bytes 172040 | tf_op jit(solution)/shard_map/ppermute | solution.py:34
  52.5 6.0 %collective-permute-start.13 = (bf16[112,256]{1,0:T(8,128)(2,1)S(1)}, bf16[112,256]{1,0:T(8,128)(2,1)S(1)}, u32[]{:S(2)}, u32[]{:S(2)}) collective-permute-start(bf16[112,256]{1,0:T(8,128)(2,1)S(1)} %get-tuple-element.91), channel_id=1, source_target_pairs={{0,6},{1,7},{2,4},{3,5},{4,2},{5,3},{6,0},{7,1},{8,14},{9,15},{10,... | collective-permute-start | bytes 172040 | tf_op jit(solution)/shard_map/ppermute | solution.py:34
  54.0 3.9 %collective-permute-start.10 = (bf16[64,256]{1,0:T(8,128)(2,1)S(1)}, bf16[64,256]{1,0:T(8,128)(2,1)S(1)}, u32[]{:S(2)}, u32[]{:S(2)}) collective-permute-start(bf16[64,256]{1,0:T(8,128)(2,1)S(1)} %get-tuple-element.87), channel_id=1, source_target_pairs={{0,1},{1,0},{2,3},{3,2},{4,5},{5,4},{6,7},{7,6},{8,9},{9,8},{10,11... | collective-permute-start | bytes 98312 | tf_op jit(solution)/shard_map/ppermute | solution.py:34
  58.5 4.9 %collective-permute-start.16 = (bf16[176,256]{1,0:T(8,128)(2,1)S(1)}, bf16[176,256]{1,0:T(8,128)(2,1)S(1)}, u32[]{:S(2)}, u32[]{:S(2)}) collective-permute-start(bf16[176,256]{1,0:T(8,128)(2,1)S(1)} %shard_map.99.after.refs_0_), channel_id=1, source_target_pairs={{0,24},{8,16},{16,8},{24,0},{1,25},{9,17},{17,9},{25,1},{2,26},{10... | collective-permute-start | bytes 270344 | tf_op jit(solution)/shard_map/ppermute | solution.py:34
  58.6 6.2 %collective-permute-start.15 = (bf16[176,256]{1,0:T(8,128)(2,1)S(1)}, bf16[176,256]{1,0:T(8,128)(2,1)S(1)}, u32[]{:S(2)}, u32[]{:S(2)}) collective-permute-start(bf16[176,256]{1,0:T(8,128)(2,1)S(1)} %shard_map.99.after.refs_0_), channel_id=1, source_target_pairs={{0,16},{8,24},{16,0},{24,8},{1,17},{9,25},{17,1},{25,9},{2,18},{10... | collective-permute-start | bytes 270344 | tf_op jit(solution)/shard_map/ppermute | solution.py:34
  59.8 5.1 %collective-permute-start.14 = (bf16[176,256]{1,0:T(8,128)(2,1)S(1)}, bf16[176,256]{1,0:T(8,128)(2,1)S(1)}, u32[]{:S(2)}, u32[]{:S(2)}) collective-permute-start(bf16[176,256]{1,0:T(8,128)(2,1)S(1)} %shard_map.99.after.refs_0_), channel_id=1, source_target_pairs={{0,8},{8,0},{16,24},{24,16},{1,9},{9,1},{17,25},{25,17},{2,10},{10... | collective-permute-start | bytes 270344 | tf_op jit(solution)/shard_map/ppermute | solution.py:34

commit v6 on v5

--- a/solution.py
+++ b/solution.py
@@ -126,21 +126,23 @@
 
 VMEM = pl.BlockSpec(memory_space=pltpu.VMEM)
 SMEM = pl.BlockSpec(memory_space=pltpu.SMEM)
+HBM = pl.BlockSpec(memory_space=pltpu.HBM)
 LANES = 128
 BAND = 16
 TOKEN = ((8, LANES), F32)
 
 
-def call(body, outs, scratch=(), smem=0, flops=0, moved=0):
+def call(body, outs, scratch=(), smem=0, hbm=0, limit=24, flops=0, moved=0):
     def run(*operands):
-        specs = [SMEM] * smem + [VMEM] * (len(operands) - smem)
+        specs = [SMEM] * smem + [HBM] * hbm + [VMEM] * (len(operands) - smem - hbm)
         return pl.pallas_call(
             body,
             out_shape=[jax.ShapeDtypeStruct(shape, kind) for shape, kind in outs],
             in_specs=specs,
             out_specs=[VMEM] * len(outs),
-            scratch_shapes=[pltpu.VMEM(shape, kind) for shape, kind in scratch],
-            compiler_params=pltpu.CompilerParams(vmem_limit_bytes=24 * 2**20),
+            scratch_shapes=[pltpu.VMEM(shape, kind) for shape, kind in scratch]
+            + [pltpu.SemaphoreType.DMA((hbm,))] * bool(hbm),
+            compiler_params=pltpu.CompilerParams(vmem_limit_bytes=limit * 2**20),
             cost_estimate=pl.CostEstimate(flops=flops, bytes_accessed=moved, transcendentals=0),
         )(*operands)
 
@@ -225,19 +227,28 @@
 
 
 def near_body(
-    scalars, place, f0, f1, t0, t1, proj, gain,
+    scale, bias, place, f0_far, proj_far, t0_far, f1, t1, gain,
     normed_turned, unit, unit_columns, inverse, text_unit, text_columns, weights, totals, proj_columns, token,
-    normed, projected, dots,
+    normed, projected, dots, f0, proj, t0, semaphores,
 ):
     rows = f0.shape[0]
+    copies = [
+        pltpu.make_async_copy(source, target, semaphores.at[at])
+        for at, (source, target) in enumerate(((f0_far, f0), (proj_far, proj), (t0_far, t0)))
+    ]
+    for copy in copies:
+        copy.start()
+    normalize_into(f1, gain, normed, rows)
+    unit_into(t1, text_unit, rows)
+    copies[0].wait()
     normalize_into(f0, gain, normed, 0)
-    normalize_into(f1, gain, normed, rows)
+    copies[1].wait()
     projected[...] = dot(normed[...], proj[...])
+    copies[2].wait()
     unit_into(t0, text_unit, 0)
-    unit_into(t1, text_unit, rows)
     unit_into(projected, unit, 0, inverse)
     dots[...] = dot(unit[...], text_unit[...], LAST)
-    weigh(dots, scalars[0], scalars[1], 0, weights, totals)
+    weigh(dots, scale[0], bias[0], 0, weights, totals)
     take_columns(place, unit, unit_columns)
     take_columns(place, text_unit, text_columns)
     take_columns(place, proj, proj_columns)
@@ -246,7 +257,7 @@
 
 
 def far_body(
-    scalars, place, f2, f3, proj, gain, text_near, before,
+    scale, bias, place, f2, f3, proj, gain, text_near, before,
     normed_turned, unit, unit_columns, inverse, weights, totals, token,
     normed, projected, dots,
 ):
@@ -256,14 +267,14 @@
     projected[...] = dot(normed[...], proj[...])
     unit_into(projected, unit, 0, inverse)
     dots[...] = dot(unit[...], text_near[...], LAST)
-    weigh(dots, scalars[0], scalars[1], None, weights, totals)
+    weigh(dots, scale[0], bias[0], None, weights, totals)
     take_columns(place, unit, unit_columns)
     normed_turned[...] = normed[...].T
     token[...] = jnp.zeros_like(token)
 
 
 def third_body(
-    scalars, place, t2, unit_near, unit_far, weights_near, weights_far, totals_near, totals_far, text_columns_near, before,
+    scale, bias, place, t2, unit_near, unit_far, weights_near, weights_far, totals_near, totals_far, text_columns_near, before,
     text_unit, weights_own, image_back, totals,
     text_columns, weights, dots,
 ):
@@ -275,7 +286,7 @@
     dots[near:, :] = dot(unit_far[...], text_unit[...], LAST)
     totals[:near, :] = totals_near[...]
     totals[near:, :] = totals_far[...]
-    weigh(dots, scalars[0], scalars[1], near, weights, totals, totals)
+    weigh(dots, scale[0], bias[0], near, weights, totals, totals)
     weights_own[...] = weights[:rows, :]
     for at, earlier in ((0, weights_near), (near, weights_far)):
         image_back[at : at + near, :] = dot(earlier[...], text_columns_near[...]) + dot(
@@ -299,7 +310,7 @@
 
 
 def partial_body(
-    members, groups, lead, scalars, place, t3, unit_near, unit_far, totals, image_back, unit_columns_near,
+    members, groups, lead, scale, bias, place, t3, unit_near, unit_far, totals, image_back, unit_columns_near,
     unit_columns_far, inverse_near, inverse_far, turned_near, turned_far, proj_columns, gain, *refs,
 ):
     (across, keep_lead, keep_tail), refs = refs[:3], refs[3:]
@@ -311,7 +322,7 @@
     width = unit_near.shape[1]
     columns = width // members
     count, full = packed.shape[1:]
-    scale, bias = scalars[0], scalars[1]
+    scale, bias = scale[0], bias[0]
     unit_into(t3, text_unit, 0)
     take_columns(place, text_unit, text_columns)
     dots[:near, :] = dot(unit_near[...], text_unit[...], LAST)
@@ -354,11 +365,11 @@
 
 
 def image_body(
-    scalars, features, proj, gain, text_near, text_third, text_fourth, weights_near, weights_third, weights_fourth,
+    scale, features, proj, gain, text_near, text_third, text_fourth, weights_near, weights_third, weights_fourth,
     unit, inverse, feature_grad, token, back, product,
 ):
     rows, width = features.shape
-    scale = scalars[0]
+    scale = scale[0]
     product[...] = (
         dot(weights_near[:rows, :], text_near[...])
         + dot(weights_third[...], text_third[...])
@@ -390,9 +401,9 @@
     token[...] = jnp.zeros_like(token)
 
 
-def text_body(scalars, text, weights_near, weights_far, unit_near, unit_far, after, text_grad, token, product):
+def text_body(scale, text, weights_near, weights_far, unit_near, unit_far, text_grad, token, product):
     rows = text.shape[0]
-    scale = scalars[0]
+    scale = scale[0]
     product[...] = dot(weights_near[:, :rows], unit_near[...], FIRST) + dot(
         weights_far[:, :rows], unit_far[...], FIRST
     )
@@ -407,7 +418,7 @@
         ).astype(BF16)
 
     over_rows(rows, 32, text_chunk)
-    token[...] = after[:8, :LANES].astype(F32) * 0.0
+    token[...] = jnp.zeros_like(token)
 
 
 def first_sum_body(place, token, keep_lead, across, keep_tail, *refs):
@@ -419,7 +430,7 @@
     own = place[1] // 2
     ordered[own] = keep_tail[...]
     for step in range(1, steps):
-        ordered[own ^ step] = along[step - 1][...]
+        ordered[own ^ step] = along[steps - 1 - step][...]
     value = ordered[0].astype(F32)
     for step in range(1, steps):
         value = value + ordered[step].astype(F32)
@@ -437,7 +448,7 @@
     total[split:, :] = (tail[...].astype(F32) + tail_across[...].astype(F32)).astype(BF16)
 
 
-def finish_body(members, place, token, *refs):
+def finish_body(members, place, *refs):
     packets, (proj_grad, gain_gradient, ordered) = refs[:members], refs[members:]
     count, full = packets[0].shape
     rows, width = proj_grad.shape
@@ -466,14 +477,13 @@
     for member in range(1, members):
         value = value + ordered[member]
     for at in range(width // LANES):
-        gain_gradient[:, at * LANES : (at + 1) * LANES] = value[at : at + 1, :]
+        gain_gradient[at * LANES : (at + 1) * LANES] = value[at]
 
 
 def local_four(features, text, proj, gain, scale, bias):
     members = lax.axis_size("loop")
     groups = lax.axis_size("rep")
     place = jnp.stack([lax.axis_index("loop"), lax.axis_index("rep")]).astype(jnp.int32)
-    scalars = jnp.concatenate([scale, bias])
     rows, width = features.shape[0], features.shape[2]
     near, every = 2 * rows, 4 * rows
     columns = width // members
@@ -502,11 +512,13 @@
     ) = call(
         near_body,
         outs,
-        [wide, ((near, width), F32), ((near, near), F32)],
-        smem=2,
+        [wide, ((near, width), F32), ((near, near), F32), half, ((width, width), BF16), half],
+        smem=3,
+        hbm=3,
+        limit=43,
         flops=3 * near * width * width,
         moved=8 * near * width,
-    )(scalars, place, f0, f1, t0, t1, proj, gain_row)
+    )(scale, bias, place, f0, proj, t0, f1, t1, gain_row)
 
     t_after, f2_after, token = lax.optimization_barrier((t0, f2, token))
     t2 = send(t_after, "loop", lambda p: p ^ 2)
@@ -516,10 +528,19 @@
         far_body,
         [turned, wide, part, one, square, one, TOKEN],
         [wide, ((near, width), F32), ((near, near), F32)],
-        smem=2,
+        smem=3,
         flops=3 * near * width * width,
         moved=8 * near * width,
-    )(scalars, place, f2, f3, proj, gain_row, text_near, token)
+    )(scale, bias, place, f2, f3, proj, gain_row, text_near, token)
+
+    text_grad, token = call(
+        text_body,
+        [half, TOKEN],
+        [((rows, width), F32)],
+        smem=1,
+        flops=2 * near * width * width,
+        moved=6 * near * width,
+    )(scale, t0, weights_near, weights_far, unit_near, unit_far)
 
     t2_after, token = lax.optimization_barrier((t2, token))
     t3 = send(t2_after, "loop", lambda p: p ^ 1)
@@ -529,11 +550,11 @@
         third_body,
         [half, ((rows, rows), BF16), ((every, columns), F32), ((every, 1), F32)],
         [((rows, columns), BF16), narrow, ((every, rows), F32)],
-        smem=2,
+        smem=3,
         flops=2 * near * width * width,
         moved=8 * near * width,
     )(
-        scalars, place, t2, unit_near, unit_far, weights_near, weights_far, totals_near, totals_far,
+        scale, bias, place, t2, unit_near, unit_far, weights_near, weights_far, totals_near, totals_far,
         text_columns_near, token,
     )
 
@@ -546,18 +567,18 @@
             ((rows, columns), BF16), narrow, ((every, rows), F32), ((every, 1), F32), ((every, columns), BF16),
             ((groups,) + packet, BF16),
         ],
-        smem=2,
+        smem=3,
         flops=4 * near * width * width,
         moved=16 * near * width,
     )(
-        scalars, place, t3, unit_near, unit_far, totals, image_back, unit_columns_near, unit_columns_far,
+        scale, bias, place, t3, unit_near, unit_far, totals, image_back, unit_columns_near, unit_columns_far,
         inverse_near, inverse_far, turned_near, turned_far, proj_columns, gain_row,
     )
     across, keep_lead, keep_tail = outs[:3]
     along, (text_fourth, weights_fourth) = outs[3 : 2 + steps], outs[2 + steps :]
 
-    along = [send(along[step - 1], "rep", lambda p: p ^ (2 * step)) for step in range(1, steps)]
     across = send(across, "rep", lambda p: p ^ 1)
+    along = [send(along[step - 1], "rep", lambda p: p ^ (2 * step)) for step in reversed(range(1, steps))]
 
     feature_grad, token = call(
         image_body,
@@ -567,7 +588,7 @@
         flops=4 * near * width * width,
         moved=12 * near * width,
     )(
-        scalars, f0, proj, gain_row, text_near, text_third, text_fourth, weights_near, weights_third,
+        scale, f0, proj, gain_row, text_near, text_third, text_fourth, weights_near, weights_third,
         weights_fourth, unit_near, inverse_near,
     )
 
@@ -578,7 +599,7 @@
         smem=1,
         moved=4 * each * width,
     )(place, token, keep_lead, across, keep_tail, *along)
-    leads = [outs[0]] + [send(outs[step], "rep", lambda p: p ^ (2 * step)) for step in range(1, steps)]
+    leads = [outs[0]] + [send(outs[step], "rep", lambda p: p ^ (2 * step)) for step in reversed(range(1, steps))]
     tail_across = send(outs[steps + 1], "rep", lambda p: p ^ 1)
 
     (reduced,) = call(
@@ -586,24 +607,18 @@
         [(packet, BF16)],
         moved=4 * each * width,
     )(outs[steps], tail_across, *leads)
-    blocks = [reduced] + [send(reduced, "loop", lambda p: p ^ k) for k in range(1, members)]
-    text_grad, token = call(
-        text_body,
-        [half, TOKEN],
-        [((rows, width), F32)],
-        smem=1,
-        flops=2 * near * width * width,
-        moved=6 * near * width,
-    )(scalars, t0, weights_near, weights_far, unit_near, unit_far, reduced)
+    far_block = send(reduced, "loop", lambda p: p ^ 2)
+    near_block = send(reduced, "loop", lambda p: p ^ 1)
+    blocks = [reduced, near_block, far_block, send(far_block, "loop", lambda p: p ^ 1)]
 
     proj_grad, gain_gradient = call(
         functools.partial(finish_body, members),
-        [((each, width), F32), ((1, width), F32)],
+        [((each, width), F32), ((width,), F32)],
         [((members, BAND, LANES), F32)],
         smem=1,
         moved=8 * each * width,
-    )(place, token, *blocks)
-    return feature_grad[:, None, :], text_grad[:, None, :], proj_grad, gain_gradient.reshape(width)
+    )(place, *blocks)
+    return feature_grad[:, None, :], text_grad[:, None, :], proj_grad, gain_gradient
 
 
 def four_fits(mesh, rows_shape):

time: 67.4 us -> 66 us (0.979)
  other arithmetic: 0.77 us -> 0.08 us
    unnamed x12 -> x6, local copies, waits for them, and re-layouts: 3.79 us -> 3.77 us
  transfers between devices with their start and end apart: 17 -> 17, of which waited for: 8 -> 6; matrix products, arithmetic and copies ran while one was open for 1% -> 1% of each run, Pallas kernels for 32% -> 33%
where the time goes in v6:
time: 66 us; the launch traced here: 65.7 us
  Pallas kernels  28.8 us (44%)
  starting transfers between devices  16.6 us (25%)
  waiting for transfers between devices  13.7 us (21%)
  local copies, waits for them, and re-layouts  4.48 us (7%)
  between operations  2.01 us (3%)
    pallas_call x9, Pallas kernels, run(): pl.pallas_call(body, out_shape=[jax.ShapeDtypeStruct(shape, kind) for sha...  28.8 us
    ppermute x17, starting transfers between devices, send(): return lax.ppermute(value, axis, [(p, target(p)) for p in range(count)])  16.6 us
    ppermute x17, waiting for transfers between devices, send(): return lax.ppermute(value, axis, [(p, target(p)) for p in range(count)])  13.7 us
    unnamed x6, local copies, waits for them, and re-layouts  3.77 us
  transfers between devices with their start and end apart: 17, of which 6 were waited for; matrix products, arithmetic and copies ran while one was open for 1% of the time, Pallas kernels for 33%

profile of v6, /device:TPU:0, one launch (start us, length us, event | category | flops | bytes accessed | tf_op | source)
XLA Modules:
  0.0 65.7 jit_solution(13494003741952685053)
XLA Ops:
  0.6 0.5 collective-permute-start
  1.1 0.1 collective-permute-start.1
  1.2 2.9 %collective-permute-start.2 = (bf16[192,1152]{1,0:T(8,128)(2,1)}, bf16[192,1152]{1,0:T(8,128)(2,1)S(1)}, u32[]{:S(2)}, u32[]{:S(2)}) collective-permute-start(bf16[192,1152]{1,0:T(8,128)(2,1)} %bitcast.11), channel_id=1, source_target_pairs={{0,16},{8,24},{16,0},{24,8},{1,17},{9,25},{17,1},{25,9},{2,18},{10... | collective-permute-start | bytes 1327112 | tf_op jit(solution)/shard_map/ppermute | solution.py:34
  4.8 0.7 %reshape.11.gain = f32[1,1152]{1,0:T(1,128)S(1)} reshape(f32[1152]{0:T(1024)} %param.9) | data formatting | bytes 9216 | tf_op jit(solution)/shard_map/reshape | solution.py:494
  6.2 0.1 pad_add_fusion.place
  6.2 0.0 collective-permute-done.f1
  6.2 0.0 collective-permute-done.1.t1
  6.2 0.0 copy-start
  6.2 1.7 %copy-done = bf16[1152,1152]{1,0:T(8,128)(2,1)S(1)} copy-done((bf16[1152,1152]{1,0:T(8,128)(2,1)S(1)}, bf16[1152,1152]{1,0:T(8,128)(2,1)}, u32[]{:S(2)}) %copy-start) | copy-done | bytes 2654232
  8.0 1.0 %copy-done.1 = bf16[192,1,1152]{2,0,1:T(8,128)(2,1)S(1)} copy-done((bf16[192,1,1152]{2,0,1:T(8,128)(2,1)S(1)}, bf16[192,1,1152]{2,0,1:T(8,128)(2,1)}, u32[]{:S(2)}) %copy-start.1) | copy-done | bytes 442392
  9.0 1.0 %copy-done.2 = bf16[192,1,1152]{2,0,1:T(8,128)(2,1)S(1)} copy-done((bf16[192,1,1152]{2,0,1:T(8,128)(2,1)S(1)}, bf16[192,1,1152]{2,0,1:T(8,128)(2,1)}, u32[]{:S(2)}) %copy-start.2) | copy-done | bytes 442392
  10.0 6.9 %shard_map.93 = (bf16[1152,384]{1,0:T(8,128)(2,1)S(1)}, bf16[384,1152]{1,0:T(8,128)(2,1)S(1)}, bf16[384,288]{1,0:T(8,128)(2,1)S(1)}, f32[384,1]{1,0:T(8,128)S(1)...) custom-call(f32[1]{0:T(128)S(6)} %copy.10.scale, ...), custom_call_target="tpu_custom_call" | custom-call | flops 1528823808 | bytes 3538944 | tf_op jit(solution)/shard_map/pallas_call | solution.py:138
  16.9 0.0 collective-permute-done.2.f2
  17.0 0.4 collective-permute-start.4
  17.4 0.4 collective-permute-start.3
  17.8 1.1 %collective-permute-done.4.f3 = bf16[192,1152]{1,0:T(8,128)(2,1)S(1)} collective-permute-done((bf16[192,1152]{1,0:T(8,128)(2,1)S(1)}, bf16[192,1152]{1,0:T(8,128)(2,1)S(1)}, u32[]{:S(2)}, u32[]{:S(2)}) %collective-permute-start.4) | collective-permute-done | bytes 442400 | tf_op jit(solution)/shard_map/ppermute | solution.py:34
  18.8 5.8 %shard_map.94 = (bf16[1152,384]{1,0:T(8,128)(2,1)S(1)}, bf16[384,1152]{1,0:T(8,128)(2,1)S(1)}, bf16[384,288]{1,0:T(8,128)(2,1)S(1)}, f32[384,1]{1,0:T(8,128)S(1)...) custom-call(f32[1]{0:T(128)S(6)} %copy.10.scale, f32[1]{0:T(128)S(6)} %copy.11.bias, ...), custom_call_target="tpu_custom_call" | custom-call | flops 1528823808 | bytes 3538944 | tf_op jit(solution)/shard_map/pallas_call | solution.py:138
  24.6 2.0 %shard_map.95 = (bf16[192,1152]{1,0:T(8,128)(2,1)}, f32[8,128]{1,0:T(8,128)S(1)}) custom-call(f32[1]{0:T(128)S(6)} %copy.10.scale, bf16[192,1152]{1,0:T(8,128)(2,1)S(1)} %bitcast.9, bf16[384,384]{1,0:T(8,128)(2,1)S(1)} %get-tuple-element.56.weights_near, bf16[384,384]{1,0:T(8,128)(2,1)S(1)} %get-tuple-element.57.weights_far, ...), custom_call_target="tpu_custom_call" | custom-call | flops 1019215872 | bytes 2654208 | tf_op jit(solution)/shard_map/pallas_call | solution.py:138
  26.6 3.0 %collective-permute-done.3.t2 = bf16[192,1152]{1,0:T(8,128)(2,1)S(1)} collective-permute-done((bf16[192,1152]{1,0:T(8,128)(2,1)S(1)}, bf16[192,1152]{1,0:T(8,128)(2,1)S(1)}, u32[]{:S(2)}, u32[]{:S(2)}) %collective-permute-start.3) | collective-permute-done | bytes 442400 | tf_op jit(solution)/shard_map/ppermute | solution.py:34
  29.6 0.0 collective-permute-start.5
  29.6 3.3 %shard_map.96 = (bf16[192,1152]{1,0:T(8,128)(2,1)S(1)}, bf16[192,192]{1,0:T(8,128)(2,1)S(1)}, f32[768,288]{1,0:T(8,128)S(1)}, f32[768,1]{1,0:T(8,128)S(1)}) custom-call(f32[1]{0:T(128)S(6)} %copy.10.scale, f32[1]{0:T(128)S(6)} %copy.11.bias, s32[2]{0:T(128)S(1)} %pad_add_fusion.place, bf16[192,1152]{1,0:T(8,128)(2,1)S(1)} %collective-permute-done.3.t2, ...), custom_call_target="tpu_custom_call" | custom-call | flops 1019215872 | bytes 3538944 | tf_op jit(solution)/shard_map/pallas_call | solution.py:138
  32.9 0.0 collective-permute-done.5.t3
  32.9 4.9 %shard_map.97 = (bf16[4,112,256]{2,1,0:T(8,128)(2,1)S(1)}, bf16[4,112,256]{2,1,0:T(8,128)(2,1)S(1)}, bf16[2,64,256]{2,1,0:T(8,128)(2,1)S(1)}, bf16[2,64,256]{2,1...) custom-call(f32[1]{0:T(128)S(6)} %copy.10.scale, ...), custom_call_target="tpu_custom_call" | custom-call | flops 2038431744 | bytes 7077888 | tf_op jit(solution)/shard_map/pallas_call | solution.py:138
  37.8 1.6 %collective-permute-start.6 = (bf16[4,112,256]{2,1,0:T(8,128)(2,1)S(1)}, bf16[4,112,256]{2,1,0:T(8,128)(2,1)S(1)}, u32[]{:S(2)}, u32[]{:S(2)}) collective-permute-start(bf16[4,112,256]{2,1,0:T(8,128)(2,1)S(1)} %get-tuple-element.81), channel_id=1, source_target_pairs={{0,1},{1,0},{2,3},{3,2},{4,5},{5,4},{6,7},{7,6},{8,9},{9,8},{10,11... | collective-permute-start | bytes 688136 | tf_op jit(solution)/shard_map/ppermute | solution.py:34
  39.4 3.6 %collective-permute-start.7 = (bf16[2,64,256]{2,1,0:T(8,128)(2,1)S(1)}, bf16[2,64,256]{2,1,0:T(8,128)(2,1)S(1)}, u32[]{:S(2)}, u32[]{:S(2)}) collective-permute-start(bf16[2,64,256]{2,1,0:T(8,128)(2,1)S(1)} %get-tuple-element.83), channel_id=1, source_target_pairs={{0,6},{1,7},{2,4},{3,5},{4,2},{5,3},{6,0},{7,1},{8,14},{9,15},{10,... | collective-permute-start | bytes 196616 | tf_op jit(solution)/shard_map/ppermute | solution.py:34
  43.0 0.0 collective-permute-start.8
  43.0 0.8 %collective-permute-start.9 = (bf16[2,64,256]{2,1,0:T(8,128)(2,1)S(1)}, bf16[2,64,256]{2,1,0:T(8,128)(2,1)S(1)}, u32[]{:S(2)}, u32[]{:S(2)}) collective-permute-start(bf16[2,64,256]{2,1,0:T(8,128)(2,1)S(1)} %get-tuple-element.85), channel_id=1, source_target_pairs={{0,2},{1,3},{2,0},{3,1},{4,6},{5,7},{6,4},{7,5},{8,10},{9,11},{10,... | collective-permute-start | bytes 196616 | tf_op jit(solution)/shard_map/ppermute | solution.py:34
  43.8 3.6 %shard_map.98 = (bf16[192,1152]{1,0:T(8,128)(2,1)}, f32[8,128]{1,0:T(8,128)S(1)}) custom-call(f32[1]{0:T(128)S(6)} %copy.10.scale, bf16[192,1152]{1,0:T(8,128)(2,1)S(1)} %bitcast.13, bf16[1152,1152]{1,0:T(8,128)(2,1)S(1)} %copy-done, f32[1,1152]{1,0:T(1,128)S(1)} %reshape.11.gain, bf16[384,1152]{1,0:T(8,128)(2,1)S(1)} %get-tuple-element.49.text_near, ...), custom_call_target="tpu_custom_call" | custom-call | flops 2038431744 | bytes 5308416 | tf_op jit(solution)/shard_map/pallas_call | solution.py:138
  47.4 0.0 collective-permute-done.7.refs_0_
  47.4 1.7 %collective-permute-done.8.refs_1_ = bf16[2,64,256]{2,1,0:T(8,128)(2,1)S(1)} collective-permute-done((bf16[2,64,256]{2,1,0:T(8,128)(2,1)S(1)}, bf16[2,64,256]{2,1,0:T(8,128)(2,1)S(1)}, u32[]{:S(2)}, u32[]{:S(2)}) %collective-permute-start.8) | collective-permute-done | bytes 65568 | tf_op jit(solution)/shard_map/ppermute | solution.py:34
  49.1 0.0 collective-permute-done.9.refs_2_
  49.1 0.0 collective-permute-done.6.across
  49.1 0.6 shard_map.99
  49.7 2.5 %collective-permute-start.11 = (bf16[112,256]{1,0:T(8,128)(2,1)S(1)}, bf16[112,256]{1,0:T(8,128)(2,1)S(1)}, u32[]{:S(2)}, u32[]{:S(2)}) collective-permute-start(bf16[112,256]{1,0:T(8,128)(2,1)S(1)} %get-tuple-element.89), channel_id=1, source_target_pairs={{0,6},{1,7},{2,4},{3,5},{4,2},{5,3},{6,0},{7,1},{8,14},{9,15},{10,... | collective-permute-start | bytes 172040 | tf_op jit(solution)/shard_map/ppermute | solution.py:34
  52.3 0.2 collective-permute-start.12
  52.5 1.7 %collective-permute-start.13 = (bf16[112,256]{1,0:T(8,128)(2,1)S(1)}, bf16[112,256]{1,0:T(8,128)(2,1)S(1)}, u32[]{:S(2)}, u32[]{:S(2)}) collective-permute-start(bf16[112,256]{1,0:T(8,128)(2,1)S(1)} %get-tuple-element.91), channel_id=1, source_target_pairs={{0,2},{1,3},{2,0},{3,1},{4,6},{5,7},{6,4},{7,5},{8,10},{9,11},{10,... | collective-permute-start | bytes 172040 | tf_op jit(solution)/shard_map/ppermute | solution.py:34
  54.2 0.5 collective-permute-start.10
  54.7 3.4 %collective-permute-done.10.tail_across = bf16[64,256]{1,0:T(8,128)(2,1)S(1)} collective-permute-done((bf16[64,256]{1,0:T(8,128)(2,1)S(1)}, bf16[64,256]{1,0:T(8,128)(2,1)S(1)}, u32[]{:S(2)}, u32[]{:S(2)}) %collective-permute-start.10) | collective-permute-done | bytes 32800 | tf_op jit(solution)/shard_map/ppermute | solution.py:34
  58.1 0.0 collective-permute-done.11.refs_1_
  58.1 0.0 collective-permute-done.12.refs_2_
  58.1 0.0 collective-permute-done.13.refs_3_
  58.2 1.3 %collective-permute-start.15 = (bf16[176,256]{1,0:T(8,128)(2,1)S(1)}, bf16[176,256]{1,0:T(8,128)(2,1)S(1)}, u32[]{:S(2)}, u32[]{:S(2)}) collective-permute-start(bf16[176,256]{1,0:T(8,128)(2,1)S(1)} %shard_map.100.refs_0_), channel_id=1, source_target_pairs={{0,16},{8,24},{16,0},{24,8},{1,17},{9,25},{17,1},{25,9},{2,18},{10... | collective-permute-start | bytes 270344 | tf_op jit(solution)/shard_map/ppermute | solution.py:34
  59.5 0.0 collective-permute-start.14
  59.5 3.3 %collective-permute-done.15.refs_2_ = bf16[176,256]{1,0:T(8,128)(2,1)S(1)} collective-permute-done((bf16[176,256]{1,0:T(8,128)(2,1)S(1)}, bf16[176,256]{1,0:T(8,128)(2,1)S(1)}, u32[]{:S(2)}, u32[]{:S(2)}) %collective-permute-start.15) | collective-permute-done | bytes 90144 | tf_op jit(solution)/shard_map/ppermute | solution.py:34
  62.8 0.0 collective-permute-start.16
  62.8 0.0 collective-permute-done.14.refs_1_
  62.8 1.3 %collective-permute-done.16.refs_3_ = bf16[176,256]{1,0:T(8,128)(2,1)S(1)} collective-permute-done((bf16[176,256]{1,0:T(8,128)(2,1)S(1)}, bf16[176,256]{1,0:T(8,128)(2,1)S(1)}, u32[]{:S(2)}, u32[]{:S(2)}) %collective-permute-start.16) | collective-permute-done | bytes 90144 | tf_op jit(solution)/shard_map/ppermute | solution.py:34
  64.1 1.7 %shard_map.101 = (f32[144,1152]{1,0:T(8,128)}, f32[1152]{0:T(1024)}) custom-call(s32[2]{0:T(128)S(1)} %pad_add_fusion.place, bf16[176,256]{1,0:T(8,128)(2,1)S(1)} %shard_map.100.refs_0_, bf16[176,256]{1,0:T(8,128)(2,1)S(1)} %collective-permute-done.14.refs_1_, bf16[176,256]{1,0:T(8,128)(2,1)S(1)} %collective-permute-done.15.refs_2_, ...), custom_call_target="tpu_custom_call" | custom-call | bytes 1327104 | tf_op jit(solution)/shard_map/pallas_call | solution.py:138
  (3 shorter events, 0.0 us)
Async XLA Ops:
  0.6 5.6 %collective-permute-start = (bf16[192,1152]{1,0:T(8,128)(2,1)}, bf16[192,1152]{1,0:T(8,128)(2,1)S(1)}, u32[]{:S(2)}, u32[]{:S(2)}) collective-permute-start(bf16[192,1152]{1,0:T(8,128)(2,1)} %bitcast.10), channel_id=1, source_target_pairs={{0,8},{8,0},{16,24},{24,16},{1,9},{9,1},{17,25},{25,17},{2,10},{10... | collective-permute-start | bytes 1327112 | tf_op jit(solution)/shard_map/ppermute | solution.py:34
  1.1 5.1 %collective-permute-start.1 = (bf16[192,1152]{1,0:T(8,128)(2,1)}, bf16[192,1152]{1,0:T(8,128)(2,1)S(1)}, u32[]{:S(2)}, u32[]{:S(2)}) collective-permute-start(bf16[192,1152]{1,0:T(8,128)(2,1)} %bitcast.6), channel_id=1, source_target_pairs={{0,8},{8,0},{16,24},{24,16},{1,9},{9,1},{17,25},{25,17},{2,10},{10... | collective-permute-start | bytes 1327112 | tf_op jit(solution)/shard_map/ppermute | solution.py:34
  1.2 15.7 %collective-permute-start.2 = (bf16[192,1152]{1,0:T(8,128)(2,1)}, bf16[192,1152]{1,0:T(8,128)(2,1)S(1)}, u32[]{:S(2)}, u32[]{:S(2)}) collective-permute-start(bf16[192,1152]{1,0:T(8,128)(2,1)} %bitcast.11), channel_id=1, source_target_pairs={{0,16},{8,24},{16,0},{24,8},{1,17},{9,25},{17,1},{25,9},{2,18},{10... | collective-permute-start | bytes 1327112 | tf_op jit(solution)/shard_map/ppermute | solution.py:34
  6.2 1.8 %copy-start = (bf16[1152,1152]{1,0:T(8,128)(2,1)S(1)}, bf16[1152,1152]{1,0:T(8,128)(2,1)}, u32[]{:S(2)}) copy-start(bf16[1152,1152]{1,0:T(8,128)(2,1)} %proj.3) | copy-start | bytes 7962628
  8.0 1.0 %copy-start.1 = (bf16[192,1,1152]{2,0,1:T(8,128)(2,1)S(1)}, bf16[192,1,1152]{2,0,1:T(8,128)(2,1)}, u32[]{:S(2)}) copy-start(bf16[192,1,1152]{2,0,1:T(8,128)(2,1)} %param.7) | copy-start | bytes 1327108
  9.0 1.0 %copy-start.2 = (bf16[192,1,1152]{2,0,1:T(8,128)(2,1)S(1)}, bf16[192,1,1152]{2,0,1:T(8,128)(2,1)}, u32[]{:S(2)}) copy-start(bf16[192,1,1152]{2,0,1:T(8,128)(2,1)} %param.6) | copy-start | bytes 1327108
  17.0 1.9 %collective-permute-start.4 = (bf16[192,1152]{1,0:T(8,128)(2,1)S(1)}, bf16[192,1152]{1,0:T(8,128)(2,1)S(1)}, u32[]{:S(2)}, u32[]{:S(2)}) collective-permute-start(bf16[192,1152]{1,0:T(8,128)(2,1)S(1)} %collective-permute-done.2.f2), channel_id=1, source_target_pairs={{0,8},{8,0},{16,24},{24,16},{1,9},{9,1},{17,25},{25,17},{2,10},{10... | collective-permute-start | bytes 1327112 | tf_op jit(solution)/shard_map/ppermute | solution.py:34
  17.4 12.2 %collective-permute-start.3 = (bf16[192,1152]{1,0:T(8,128)(2,1)S(1)}, bf16[192,1152]{1,0:T(8,128)(2,1)S(1)}, u32[]{:S(2)}, u32[]{:S(2)}) collective-permute-start(bf16[192,1152]{1,0:T(8,128)(2,1)S(1)} %bitcast.8), channel_id=1, source_target_pairs={{0,16},{8,24},{16,0},{24,8},{1,17},{9,25},{17,1},{25,9},{2,18},{10... | collective-permute-start | bytes 1327112 | tf_op jit(solution)/shard_map/ppermute | solution.py:34
  29.6 3.3 %collective-permute-start.5 = (bf16[192,1152]{1,0:T(8,128)(2,1)S(1)}, bf16[192,1152]{1,0:T(8,128)(2,1)S(1)}, u32[]{:S(2)}, u32[]{:S(2)}) collective-permute-start(bf16[192,1152]{1,0:T(8,128)(2,1)S(1)} %collective-permute-done.3.t2), channel_id=1, source_target_pairs={{0,8},{8,0},{16,24},{24,16},{1,9},{9,1},{17,25},{25,17},{2,10},{10... | collective-permute-start | bytes 1327112 | tf_op jit(solution)/shard_map/ppermute | solution.py:34
  37.8 11.3 %collective-permute-start.6 = (bf16[4,112,256]{2,1,0:T(8,128)(2,1)S(1)}, bf16[4,112,256]{2,1,0:T(8,128)(2,1)S(1)}, u32[]{:S(2)}, u32[]{:S(2)}) collective-permute-start(bf16[4,112,256]{2,1,0:T(8,128)(2,1)S(1)} %get-tuple-element.81), channel_id=1, source_target_pairs={{0,1},{1,0},{2,3},{3,2},{4,5},{5,4},{6,7},{7,6},{8,9},{9,8},{10,11... | collective-permute-start | bytes 688136 | tf_op jit(solution)/shard_map/ppermute | solution.py:34
  39.4 8.0 %collective-permute-start.7 = (bf16[2,64,256]{2,1,0:T(8,128)(2,1)S(1)}, bf16[2,64,256]{2,1,0:T(8,128)(2,1)S(1)}, u32[]{:S(2)}, u32[]{:S(2)}) collective-permute-start(bf16[2,64,256]{2,1,0:T(8,128)(2,1)S(1)} %get-tuple-element.83), channel_id=1, source_target_pairs={{0,6},{1,7},{2,4},{3,5},{4,2},{5,3},{6,0},{7,1},{8,14},{9,15},{10,... | collective-permute-start | bytes 196616 | tf_op jit(solution)/shard_map/ppermute | solution.py:34
  43.0 6.1 %collective-permute-start.8 = (bf16[2,64,256]{2,1,0:T(8,128)(2,1)S(1)}, bf16[2,64,256]{2,1,0:T(8,128)(2,1)S(1)}, u32[]{:S(2)}, u32[]{:S(2)}) collective-permute-start(bf16[2,64,256]{2,1,0:T(8,128)(2,1)S(1)} %get-tuple-element.84), channel_id=1, source_target_pairs={{0,4},{1,5},{2,6},{3,7},{4,0},{5,1},{6,2},{7,3},{8,12},{9,13},{10,... | collective-permute-start | bytes 196616 | tf_op jit(solution)/shard_map/ppermute | solution.py:34
  43.0 6.1 %collective-permute-start.9 = (bf16[2,64,256]{2,1,0:T(8,128)(2,1)S(1)}, bf16[2,64,256]{2,1,0:T(8,128)(2,1)S(1)}, u32[]{:S(2)}, u32[]{:S(2)}) collective-permute-start(bf16[2,64,256]{2,1,0:T(8,128)(2,1)S(1)} %get-tuple-element.85), channel_id=1, source_target_pairs={{0,2},{1,3},{2,0},{3,1},{4,6},{5,7},{6,4},{7,5},{8,10},{9,11},{10,... | collective-permute-start | bytes 196616 | tf_op jit(solution)/shard_map/ppermute | solution.py:34
  49.7 8.4 %collective-permute-start.11 = (bf16[112,256]{1,0:T(8,128)(2,1)S(1)}, bf16[112,256]{1,0:T(8,128)(2,1)S(1)}, u32[]{:S(2)}, u32[]{:S(2)}) collective-permute-start(bf16[112,256]{1,0:T(8,128)(2,1)S(1)} %get-tuple-element.89), channel_id=1, source_target_pairs={{0,6},{1,7},{2,4},{3,5},{4,2},{5,3},{6,0},{7,1},{8,14},{9,15},{10,... | collective-permute-start | bytes 172040 | tf_op jit(solution)/shard_map/ppermute | solution.py:34
  52.3 5.9 %collective-permute-start.12 = (bf16[112,256]{1,0:T(8,128)(2,1)S(1)}, bf16[112,256]{1,0:T(8,128)(2,1)S(1)}, u32[]{:S(2)}, u32[]{:S(2)}) collective-permute-start(bf16[112,256]{1,0:T(8,128)(2,1)S(1)} %get-tuple-element.90), channel_id=1, source_target_pairs={{0,4},{1,5},{2,6},{3,7},{4,0},{5,1},{6,2},{7,3},{8,12},{9,13},{10,... | collective-permute-start | bytes 172040 | tf_op jit(solution)/shard_map/ppermute | solution.py:34
  52.5 5.7 %collective-permute-start.13 = (bf16[112,256]{1,0:T(8,128)(2,1)S(1)}, bf16[112,256]{1,0:T(8,128)(2,1)S(1)}, u32[]{:S(2)}, u32[]{:S(2)}) collective-permute-start(bf16[112,256]{1,0:T(8,128)(2,1)S(1)} %get-tuple-element.91), channel_id=1, source_target_pairs={{0,2},{1,3},{2,0},{3,1},{4,6},{5,7},{6,4},{7,5},{8,10},{9,11},{10,... | collective-permute-start | bytes 172040 | tf_op jit(solution)/shard_map/ppermute | solution.py:34
  54.2 3.9 %collective-permute-start.10 = (bf16[64,256]{1,0:T(8,128)(2,1)S(1)}, bf16[64,256]{1,0:T(8,128)(2,1)S(1)}, u32[]{:S(2)}, u32[]{:S(2)}) collective-permute-start(bf16[64,256]{1,0:T(8,128)(2,1)S(1)} %get-tuple-element.87), channel_id=1, source_target_pairs={{0,1},{1,0},{2,3},{3,2},{4,5},{5,4},{6,7},{7,6},{8,9},{9,8},{10,11... | collective-permute-start | bytes 98312 | tf_op jit(solution)/shard_map/ppermute | solution.py:34
  58.2 4.6 %collective-permute-start.15 = (bf16[176,256]{1,0:T(8,128)(2,1)S(1)}, bf16[176,256]{1,0:T(8,128)(2,1)S(1)}, u32[]{:S(2)}, u32[]{:S(2)}) collective-permute-start(bf16[176,256]{1,0:T(8,128)(2,1)S(1)} %shard_map.100.refs_0_), channel_id=1, source_target_pairs={{0,16},{8,24},{16,0},{24,8},{1,17},{9,25},{17,1},{25,9},{2,18},{10... | collective-permute-start | bytes 270344 | tf_op jit(solution)/shard_map/ppermute | solution.py:34
  59.5 3.3 %collective-permute-start.14 = (bf16[176,256]{1,0:T(8,128)(2,1)S(1)}, bf16[176,256]{1,0:T(8,128)(2,1)S(1)}, u32[]{:S(2)}, u32[]{:S(2)}) collective-permute-start(bf16[176,256]{1,0:T(8,128)(2,1)S(1)} %shard_map.100.refs_0_), channel_id=1, source_target_pairs={{0,8},{8,0},{16,24},{24,16},{1,9},{9,1},{17,25},{25,17},{2,10},{10... | collective-permute-start | bytes 270344 | tf_op jit(solution)/shard_map/ppermute | solution.py:34
  62.8 1.3 %collective-permute-start.16 = (bf16[176,256]{1,0:T(8,128)(2,1)S(1)}, bf16[176,256]{1,0:T(8,128)(2,1)S(1)}, u32[]{:S(2)}, u32[]{:S(2)}) collective-permute-start(bf16[176,256]{1,0:T(8,128)(2,1)S(1)} %collective-permute-done.15.refs_2_), channel_id=1, source_target_pairs={{0,8},{8,0},{16,24},{24,16},{1,9},{9,1},{17,25},{25,17},{2,10},{10... | collective-permute-start | bytes 270344 | tf_op jit(solution)/shard_map/ppermute | solution.py:34

commit v7 on v6

--- a/solution.py
+++ b/solution.py
@@ -182,39 +182,30 @@
         place = pl.ds(at + where.start, where.size)
         target[place, :] = (values * inverse).astype(BF16)
         if inverses is not None:
-            inverses[place, :] = inverse
+            inverses[place, :] = jnp.broadcast_to(inverse, (where.size, LANES))
 
     over_rows(rows, 32, chunk)
 
 
-def weigh(dots, scale, bias, diagonal, weights, totals, add_to=None):
-    rows, columns = dots.shape
-
-    def part(first, count, with_pairs):
-        def chunk(where):
-            where = pl.ds(first + where.start, where.size)
-            product = dots[where, :]
-            weight = jnp.tanh((0.5 * scale) * product + 0.5 * bias)
-            offset = 0.5
-            if with_pairs:
-                row = where.start - diagonal + lax.broadcasted_iota(jnp.int32, product.shape, 0)
-                column = lax.broadcasted_iota(jnp.int32, product.shape, 1)
-                offset = jnp.where(row == column, -0.5, 0.5)
-            weight = (0.5 * weight + offset).astype(BF16)
-            weights[where, :] = weight
-            total = sums(weight.astype(F32) * product)
-            totals[where, :] = total if add_to is None else add_to[where, :] + total
-
-        over_rows(count, 32, chunk)
-
-    if diagonal is None:
-        part(0, rows, False)
-        return
-    if diagonal:
-        part(0, diagonal, False)
-    part(diagonal, columns, True)
-    if diagonal + columns < rows:
-        part(diagonal + columns, rows - diagonal - columns, False)
+def weigh(dots, scale, bias, diagonal, weights):
+    texts, images = dots.shape
+
+    def chunk(index, total):
+        where = pl.ds(pl.multiple_of(index * BAND, BAND), BAND)
+        product = dots[where, :]
+        weight = jnp.tanh((0.5 * scale) * product + 0.5 * bias)
+        offset = 0.5
+        if diagonal is not None:
+            text = index * BAND + diagonal + lax.broadcasted_iota(jnp.int32, product.shape, 0)
+            image = lax.broadcasted_iota(jnp.int32, product.shape, 1)
+            offset = jnp.where(text == image, -0.5, 0.5)
+        weight = (0.5 * weight + offset).astype(BF16)
+        weights[where, :] = weight
+        both = weight.astype(F32) * product
+        return total + both[:8, :] + both[8:, :]
+
+    total = lax.fori_loop(0, texts // BAND, chunk, jnp.zeros((8, images), F32), unroll=4)
+    return jnp.sum(total, axis=0, keepdims=True)
 
 
 def take_columns(place, source, target):
@@ -227,9 +218,8 @@
 
 
 def near_body(
-    scale, bias, place, f0_far, proj_far, t0_far, f1, t1, gain,
-    normed_turned, unit, unit_columns, inverse, text_unit, text_columns, weights, totals, proj_columns, token,
-    normed, projected, dots, f0, proj, t0, semaphores,
+    f0_far, proj_far, t0_far, f1, t1, gain,
+    f0, proj, t0, normed, unit, factors, text_unit, token, projected, semaphores,
 ):
     rows = f0.shape[0]
     copies = [
@@ -246,52 +236,66 @@
     projected[...] = dot(normed[...], proj[...])
     copies[2].wait()
     unit_into(t0, text_unit, 0)
-    unit_into(projected, unit, 0, inverse)
-    dots[...] = dot(unit[...], text_unit[...], LAST)
-    weigh(dots, scale[0], bias[0], 0, weights, totals)
-    take_columns(place, unit, unit_columns)
+    unit_into(projected, unit, 0, factors)
+    token[...] = jnp.zeros_like(token)
+
+
+def near_pairs_body(
+    scale, bias, place, normed, unit, factors, text_unit, proj, before,
+    normed_turned, unit_turned, inverse, text_columns, weights, totals, proj_columns, dots, turned,
+):
+    dots[...] = dot(text_unit[...], unit[...], LAST)
+    totals[...] = weigh(dots, scale[0], bias[0], 0, weights)
     take_columns(place, text_unit, text_columns)
     take_columns(place, proj, proj_columns)
+    turn_own(place, unit, factors, turned, unit_turned, inverse)
     normed_turned[...] = normed[...].T
-    token[...] = jnp.zeros_like(token)
+
+
+def turn_own(place, unit, factors, turned, unit_turned, inverse):
+    columns = unit_turned.shape[0]
+    turned[...] = unit[...].T
+    unit_turned[...] = turned[pl.ds(pl.multiple_of(place[0] * columns, BAND), columns), :]
+    inverse[...] = factors[...].T[:1, :]
 
 
 def far_body(
     scale, bias, place, f2, f3, proj, gain, text_near, before,
-    normed_turned, unit, unit_columns, inverse, weights, totals, token,
-    normed, projected, dots,
+    normed_turned, unit, unit_turned, inverse, weights, totals, token,
+    normed, projected, dots, turned, factors,
 ):
     rows = f2.shape[0]
     normalize_into(f2, gain, normed, 0)
     normalize_into(f3, gain, normed, rows)
     projected[...] = dot(normed[...], proj[...])
-    unit_into(projected, unit, 0, inverse)
-    dots[...] = dot(unit[...], text_near[...], LAST)
-    weigh(dots, scale[0], bias[0], None, weights, totals)
-    take_columns(place, unit, unit_columns)
+    unit_into(projected, unit, 0, factors)
+    dots[...] = dot(text_near[...], unit[...], LAST)
+    totals[...] = weigh(dots, scale[0], bias[0], None, weights)
+    turn_own(place, unit, factors, turned, unit_turned, inverse)
     normed_turned[...] = normed[...].T
     token[...] = jnp.zeros_like(token)
 
 
 def third_body(
-    scale, bias, place, t2, unit_near, unit_far, weights_near, weights_far, totals_near, totals_far, text_columns_near, before,
-    text_unit, weights_own, image_back, totals,
-    text_columns, weights, dots,
+    scale, bias, place, t2, unit_near, unit_far, weights_near, weights_far, totals_near, totals_far, text_columns_near,
+    before, text_unit, weights, back_near, back_far, totals,
+    text_columns, dots,
 ):
     rows = t2.shape[0]
     near = 2 * rows
     unit_into(t2, text_unit, 0)
     take_columns(place, text_unit, text_columns)
-    dots[:near, :] = dot(unit_near[...], text_unit[...], LAST)
-    dots[near:, :] = dot(unit_far[...], text_unit[...], LAST)
-    totals[:near, :] = totals_near[...]
-    totals[near:, :] = totals_far[...]
-    weigh(dots, scale[0], bias[0], near, weights, totals, totals)
-    weights_own[...] = weights[:rows, :]
-    for at, earlier in ((0, weights_near), (near, weights_far)):
-        image_back[at : at + near, :] = dot(earlier[...], text_columns_near[...]) + dot(
-            weights[at : at + near, :], text_columns[...]
-        )
+    dots[:, :near] = dot(text_unit[...], unit_near[...], LAST)
+    dots[:, near:] = dot(text_unit[...], unit_far[...], LAST)
+    added = weigh(dots, scale[0], bias[0], near, weights)
+    totals[:, :near] = totals_near[...] + added[:, :near]
+    totals[:, near:] = totals_far[...] + added[:, near:]
+    back_near[...] = dot(text_columns_near[...], weights_near[...], FIRST) + dot(
+        text_columns[...], weights[:, :near], FIRST
+    )
+    back_far[...] = dot(text_columns_near[...], weights_far[...], FIRST) + dot(
+        text_columns[...], weights[:, near:], FIRST
+    )
 
 
 def pack_into(target, block, full):
@@ -310,12 +314,12 @@
 
 
 def partial_body(
-    members, groups, lead, scale, bias, place, t3, unit_near, unit_far, totals, image_back, unit_columns_near,
-    unit_columns_far, inverse_near, inverse_far, turned_near, turned_far, proj_columns, gain, *refs,
+    members, groups, lead, scale, bias, place, t3, unit_near, unit_far, totals, back_near, back_far, unit_turned_near,
+    unit_turned_far, inverse_near, inverse_far, turned_near, turned_far, proj_columns, gain, *refs,
 ):
     (across, keep_lead, keep_tail), refs = refs[:3], refs[3:]
     along, refs = refs[: groups // 2 - 1], refs[groups // 2 - 1 :]
-    text_unit, weights_own, text_columns, weights, dots, all_totals, back, packed = refs
+    text_unit, weights, text_columns, dots, packed = refs
     rows = t3.shape[0]
     near = 2 * rows
     every = members * rows
@@ -325,18 +329,20 @@
     scale, bias = scale[0], bias[0]
     unit_into(t3, text_unit, 0)
     take_columns(place, text_unit, text_columns)
-    dots[:near, :] = dot(unit_near[...], text_unit[...], LAST)
-    dots[near:, :] = dot(unit_far[...], text_unit[...], LAST)
-    weigh(dots, scale, bias, near + rows, weights, all_totals, totals)
-    weights_own[...] = weights[:rows, :]
-    for at, unit_columns, inverse in ((0, unit_columns_near, inverse_near), (near, unit_columns_far, inverse_far)):
-        where = slice(at, at + near)
-        whole = image_back[where, :] + dot(weights[where, :], text_columns[...])
-        back[where, :] = (
-            (whole - unit_columns[...].astype(F32) * all_totals[where, :]) * (inverse[...] * scale)
-        ).astype(BF16)
+    dots[:, :near] = dot(text_unit[...], unit_near[...], LAST)
+    dots[:, near:] = dot(text_unit[...], unit_far[...], LAST)
+    total = totals[...] + weigh(dots, scale, bias, near + rows, weights)
+    product = None
+    for where, earlier, unit_turned, inverse, turned in (
+        (slice(0, near), back_near, unit_turned_near, inverse_near, turned_near),
+        (slice(near, every), back_far, unit_turned_far, inverse_far, turned_far),
+    ):
+        whole = earlier[...] + dot(text_columns[...], weights[:, where], FIRST)
+        back = (whole - unit_turned[...].astype(F32) * total[:, where]) * (inverse[...] * scale)
+        part = dot(turned[...], back.astype(BF16), LAST)
+        product = part if product is None else product + part
     each = width // groups
-    product = (dot(turned_near[...], back[:near, :]) + dot(turned_far[...], back[near:, :])) * (1.0 / every)
+    product = product * (1.0 / every)
     for group in range(groups):
         pack_into(packed.at[group], product[group * each : (group + 1) * each, :], full)
 
@@ -366,21 +372,21 @@
 
 def image_body(
     scale, features, proj, gain, text_near, text_third, text_fourth, weights_near, weights_third, weights_fourth,
-    unit, inverse, feature_grad, token, back, product,
+    unit, factors, feature_grad, token, back, product,
 ):
     rows, width = features.shape
     scale = scale[0]
     product[...] = (
-        dot(weights_near[:rows, :], text_near[...])
-        + dot(weights_third[...], text_third[...])
-        + dot(weights_fourth[...], text_fourth[...])
+        dot(weights_near[:, :rows], text_near[...], FIRST)
+        + dot(weights_third[:, :rows], text_third[...], FIRST)
+        + dot(weights_fourth[:, :rows], text_fourth[...], FIRST)
     )
 
     def image_chunk(where):
         values = product[where, :] * scale
         direction = unit[where, :].astype(F32)
         back[where, :] = (
-            (values - direction * sums(direction * values)) * inverse[where, :]
+            (values - direction * sums(direction * values)) * factors[where, :1]
         ).astype(BF16)
 
     over_rows(rows, 32, image_chunk)
@@ -404,9 +410,7 @@
 def text_body(scale, text, weights_near, weights_far, unit_near, unit_far, text_grad, token, product):
     rows = text.shape[0]
     scale = scale[0]
-    product[...] = dot(weights_near[:, :rows], unit_near[...], FIRST) + dot(
-        weights_far[:, :rows], unit_far[...], FIRST
-    )
+    product[...] = dot(weights_near[:rows, :], unit_near[...]) + dot(weights_far[:rows, :], unit_far[...])
 
     def text_chunk(where):
         values = product[where, :] * scale
@@ -493,7 +497,7 @@
     packet = (each + bands * BAND, full)
     gain_row = gain.reshape(1, width)
 
-    lead = (2 * packet[0] // BAND // 3) * BAND
+    lead = (3 * packet[0] // BAND // 4) * BAND
     tail = packet[0] - lead
     steps = groups // 2
 
@@ -502,36 +506,44 @@
     f1 = send(f0, "loop", lambda p: p ^ 1)
     t1 = send(t0, "loop", lambda p: p ^ 1)
 
-    wide, half, one = ((near, width), BF16), ((rows, width), BF16), ((near, 1), F32)
+    wide, half = ((near, width), BF16), ((rows, width), BF16)
     square, part, turned = ((near, near), BF16), ((near, columns), BF16), ((width, near), BF16)
 
-    outs = [turned, wide, part, one, wide, part, square, one, ((width, columns), BF16), TOKEN]
-    (
-        turned_near, unit_near, unit_columns_near, inverse_near, text_near, text_columns_near,
-        weights_near, totals_near, proj_columns, token,
-    ) = call(
+    line, mine = ((1, near), F32), ((columns, near), BF16)
+    kept = ((width, width), BF16)
+    f0_kept, proj_kept, t0_kept, normed_near, unit_near, factors, text_near, token = call(
         near_body,
-        outs,
-        [wide, ((near, width), F32), ((near, near), F32), half, ((width, width), BF16), half],
-        smem=3,
+        [half, kept, half, wide, wide, ((near, LANES), F32), wide, TOKEN],
+        [((near, width), F32)],
         hbm=3,
-        limit=43,
-        flops=3 * near * width * width,
+        limit=46,
+        flops=2 * near * width * width,
         moved=8 * near * width,
-    )(scale, bias, place, f0, proj, t0, f1, t1, gain_row)
+    )(f0, proj, t0, f1, t1, gain_row)
 
     t_after, f2_after, token = lax.optimization_barrier((t0, f2, token))
     t2 = send(t_after, "loop", lambda p: p ^ 2)
     f3 = send(f2_after, "loop", lambda p: p ^ 1)
 
-    turned_far, unit_far, unit_columns_far, inverse_far, weights_far, totals_far, token = call(
+    (
+        turned_near, unit_turned_near, inverse_near, text_columns_near, weights_near, totals_near, proj_columns,
+    ) = call(
+        near_pairs_body,
+        [turned, mine, line, part, square, line, ((width, columns), BF16)],
+        [((near, near), F32), turned],
+        smem=3,
+        flops=near * width * width,
+        moved=8 * near * width,
+    )(scale, bias, place, normed_near, unit_near, factors, text_near, proj_kept, token)
+
+    turned_far, unit_far, unit_turned_far, inverse_far, weights_far, totals_far, token = call(
         far_body,
-        [turned, wide, part, one, square, one, TOKEN],
-        [wide, ((near, width), F32), ((near, near), F32)],
+        [turned, wide, mine, line, square, line, TOKEN],
+        [wide, ((near, width), F32), ((near, near), F32), turned, ((near, LANES), F32)],
         smem=3,
         flops=3 * near * width * width,
         moved=8 * near * width,
-    )(scale, bias, place, f2, f3, proj, gain_row, text_near, token)
+    )(scale, bias, place, f2, f3, proj_kept, gain_row, text_near, totals_near)
 
     text_grad, token = call(
         text_body,
@@ -540,16 +552,16 @@
         smem=1,
         flops=2 * near * width * width,
         moved=6 * near * width,
-    )(scale, t0, weights_near, weights_far, unit_near, unit_far)
+    )(scale, t0_kept, weights_near, weights_far, unit_near, unit_far)
 
     t2_after, token = lax.optimization_barrier((t2, token))
     t3 = send(t2_after, "loop", lambda p: p ^ 1)
 
-    narrow = ((every, rows), BF16)
-    text_third, weights_third, image_back, totals = call(
+    narrow, back_kind = ((rows, every), BF16), ((columns, near), F32)
+    text_third, weights_third, back_near, back_far, totals = call(
         third_body,
-        [half, ((rows, rows), BF16), ((every, columns), F32), ((every, 1), F32)],
-        [((rows, columns), BF16), narrow, ((every, rows), F32)],
+        [half, narrow, back_kind, back_kind, ((1, every), F32)],
+        [((rows, columns), BF16), ((rows, every), F32)],
         smem=3,
         flops=2 * near * width * width,
         moved=8 * near * width,
@@ -560,18 +572,13 @@
 
     outs = call(
         functools.partial(partial_body, members, groups, lead),
-        [((steps, lead, full), BF16), ((steps, lead, full), BF16)]
-        + [((2, tail, full), BF16)] * steps
-        + [half, ((rows, rows), BF16)],
-        [
-            ((rows, columns), BF16), narrow, ((every, rows), F32), ((every, 1), F32), ((every, columns), BF16),
-            ((groups,) + packet, BF16),
-        ],
+        [((steps, lead, full), BF16), ((steps, lead, full), BF16)] + [((2, tail, full), BF16)] * steps + [half, narrow],
+        [((rows, columns), BF16), ((rows, every), F32), ((groups,) + packet, BF16)],
         smem=3,
         flops=4 * near * width * width,
         moved=16 * near * width,
     )(
-        scale, bias, place, t3, unit_near, unit_far, totals, image_back, unit_columns_near, unit_columns_far,
+        scale, bias, place, t3, unit_near, unit_far, totals, back_near, back_far, unit_turned_near, unit_turned_far,
         inverse_near, inverse_far, turned_near, turned_far, proj_columns, gain_row,
     )
     across, keep_lead, keep_tail = outs[:3]
@@ -588,8 +595,8 @@
         flops=4 * near * width * width,
         moved=12 * near * width,
     )(
-        scale, f0, proj, gain_row, text_near, text_third, text_fourth, weights_near, weights_third,
-        weights_fourth, unit_near, inverse_near,
+        scale, f0_kept, proj_kept, gain_row, text_near, text_third, text_fourth, weights_near, weights_third,
+        weights_fourth, unit_near, factors,
     )
 
     outs = call(

time: 66 us -> 67.2 us (1.018)
  local copies, waits for them, and re-layouts: 4.48 us -> 9.03 us
  waiting for transfers between devices: 13.7 us -> 9.75 us
  starting transfers between devices: 16.6 us -> 17.8 us
  Pallas kernels: 28.8 us -> 28 us
    unnamed x6 -> x26, local copies, waits for them, and re-layouts: 3.77 us -> 8.33 us
    ppermute x17, waiting for transfers between devices: 13.7 us -> 9.75 us  [send(): return lax.ppermute(value, axis, [(p, target(p)) for p in range(count)])]
    ppermute x17, starting transfers between devices: 16.6 us -> 17.8 us  [send(): return lax.ppermute(value, axis, [(p, target(p)) for p in range(count)])]
    pallas_call x9 -> x10, Pallas kernels: 28.8 us -> 28 us  [run(): pl.pallas_call(body, out_shape=[jax.ShapeDtypeStruct(shape, kind) for sha...]
  transfers between devices with their start and end apart: 17 -> 17, of which waited for: 6 -> 6; matrix products, arithmetic and copies ran while one was open for 1% -> 1% of each run, Pallas kernels for 33% -> 32%
where the time goes in v7:
time: 67.2 us; the launch traced here: 66.7 us
  Pallas kernels  28 us (42%)
  starting transfers between devices  17.8 us (26%)
  waiting for transfers between devices  9.75 us (15%)
  local copies, waits for them, and re-layouts  9.03 us (13%)
  between operations  2.07 us (3%)
    pallas_call x10, Pallas kernels, run(): pl.pallas_call(body, out_shape=[jax.ShapeDtypeStruct(shape, kind) for sha...  28 us
    ppermute x17, starting transfers between devices, send(): return lax.ppermute(value, axis, [(p, target(p)) for p in range(count)])  17.8 us
    ppermute x17, waiting for transfers between devices, send(): return lax.ppermute(value, axis, [(p, target(p)) for p in range(count)])  9.75 us
    unnamed x26, local copies, waits for them, and re-layouts  8.33 us
  transfers between devices with their start and end apart: 17, of which 6 were waited for; matrix products, arithmetic and copies ran while one was open for 1% of the time, Pallas kernels for 32%

profile of v7, /device:TPU:0, one launch (start us, length us, event | category | flops | bytes accessed | tf_op | source)
XLA Modules:
  0.0 66.7 jit_solution(13942774939311302937)
XLA Ops:
  0.6 0.5 collective-permute-start
  1.1 0.1 collective-permute-start.1
  1.2 2.9 %collective-permute-start.2 = (bf16[192,1152]{1,0:T(8,128)(2,1)}, bf16[192,1152]{1,0:T(8,128)(2,1)}, u32[]{:S(2)}, u32[]{:S(2)}) collective-permute-start(bf16[192,1152]{1,0:T(8,128)(2,1)} %bitcast.7), channel_id=1, source_target_pairs={{0,16},{8,24},{16,0},{24,8},{1,17},{9,25},{17,1},{25,9},{2,18},{10... | collective-permute-start | bytes 1327112 | tf_op jit(solution)/shard_map/ppermute | solution.py:34
  4.1 0.7 %reshape.11.gain = f32[1,1152]{1,0:T(1,128)S(1)} reshape(f32[1152]{0:T(1024)} %param.9) | data formatting | bytes 9216 | tf_op jit(solution)/shard_map/reshape | solution.py:498
  4.8 0.0 collective-permute-done.f1
  4.9 0.0 copy-start.5
  4.9 1.0 %copy-done.5 = bf16[192,1,1152]{2,0,1:T(8,128)(2,1)S(1)} copy-done((bf16[192,1,1152]{2,0,1:T(8,128)(2,1)S(1)}, bf16[192,1,1152]{2,0,1:T(8,128)(2,1)}, u32[]{:S(2)}) %copy-start.5) | copy-done | bytes 442392
  5.9 4.2 %shard_map.93 = (bf16[192,1152]{1,0:T(8,128)(2,1)S(1)}, bf16[1152,1152]{1,0:T(8,128)(2,1)S(1)}, bf16[192,1152]{1,0:T(8,128)(2,1)S(1)}, bf16[384,1152]{1,0:T(8,12...) custom-call(bf16[192,1152]{1,0:T(8,128)(2,1)S(1)} %bitcast.8, ...), custom_call_target="tpu_custom_call" | custom-call | flops 1019215872 | bytes 3538944 | tf_op jit(solution)/shard_map/pallas_call | solution.py:138
  10.1 0.9 %copy-done = bf16[384,1152]{1,0:T(8,128)(2,1)} copy-done((bf16[384,1152]{1,0:T(8,128)(2,1)}, bf16[384,1152]{1,0:T(8,128)(2,1)S(1)}, u32[]{:S(2)}) %copy-start) | copy-done | bytes 884760
  11.0 0.9 %copy-done.3 = bf16[384,1152]{1,0:T(8,128)(2,1)} copy-done((bf16[384,1152]{1,0:T(8,128)(2,1)}, bf16[384,1152]{1,0:T(8,128)(2,1)S(1)}, u32[]{:S(2)}) %copy-start.3) | copy-done | bytes 884760
  12.0 0.7 %copy-done.6 = f32[384,128]{1,0:T(8,128)} copy-done((f32[384,128]{1,0:T(8,128)}, f32[384,128]{1,0:T(8,128)S(1)}, u32[]{:S(2)}) %copy-start.6) | copy-done | bytes 196632
  12.6 0.8 %copy-done.9 = bf16[192,1152]{1,0:T(8,128)(2,1)} copy-done((bf16[192,1152]{1,0:T(8,128)(2,1)}, bf16[192,1152]{1,0:T(8,128)(2,1)S(1)}, u32[]{:S(2)}) %copy-start.9) | copy-done | bytes 442392
  13.4 0.8 %copy-done.11 = bf16[192,1152]{1,0:T(8,128)(2,1)} copy-done((bf16[192,1152]{1,0:T(8,128)(2,1)}, bf16[192,1152]{1,0:T(8,128)(2,1)S(1)}, u32[]{:S(2)}) %copy-start.11) | copy-done | bytes 442392
  14.2 0.7 %collective-permute-done.2.f2 = bf16[192,1152]{1,0:T(8,128)(2,1)} collective-permute-done((bf16[192,1152]{1,0:T(8,128)(2,1)}, bf16[192,1152]{1,0:T(8,128)(2,1)}, u32[]{:S(2)}, u32[]{:S(2)}) %collective-permute-start.2) | collective-permute-done | bytes 442400 | tf_op jit(solution)/shard_map/ppermute | solution.py:34
  14.9 0.0 collective-permute-start.4
  14.9 1.7 %collective-permute-start.3 = (bf16[192,1152]{1,0:T(8,128)(2,1)}, bf16[192,1152]{1,0:T(8,128)(2,1)}, u32[]{:S(2)}, u32[]{:S(2)}) collective-permute-start(bf16[192,1152]{1,0:T(8,128)(2,1)} %bitcast.1.t0_far), channel_id=1, source_target_pairs={{0,16},{8,24},{16,0},{24,8},{1,17},{9,25},{17,1},{25,9},{2,18},{10... | collective-permute-start | bytes 1327112 | tf_op jit(solution)/shard_map/ppermute | solution.py:34
  17.9 0.1 pad_add_fusion.place
  18.0 1.2 %copy-done.1 = bf16[384,1152]{1,0:T(8,128)(2,1)S(1)} copy-done((bf16[384,1152]{1,0:T(8,128)(2,1)S(1)}, bf16[384,1152]{1,0:T(8,128)(2,1)}, u32[]{:S(2)}) %copy-start.1) | copy-done | bytes 884760
  19.2 1.2 %copy-done.4 = bf16[384,1152]{1,0:T(8,128)(2,1)S(1)} copy-done((bf16[384,1152]{1,0:T(8,128)(2,1)S(1)}, bf16[384,1152]{1,0:T(8,128)(2,1)}, u32[]{:S(2)}) %copy-start.4) | copy-done | bytes 884760
  20.3 0.9 %copy-done.7 = f32[384,128]{1,0:T(8,128)S(1)} copy-done((f32[384,128]{1,0:T(8,128)S(1)}, f32[384,128]{1,0:T(8,128)}, u32[]{:S(2)}) %copy-start.7) | copy-done | bytes 196632
  21.3 2.2 %shard_map.94 = (bf16[1152,384]{1,0:T(8,128)(2,1)S(1)}, bf16[288,384]{1,0:T(8,128)(2,1)S(1)}, f32[1,384]{1,0:T(1,128)S(1)}, bf16[384,288]{1,0:T(8,128)(2,1)S(1)}...) custom-call(f32[1]{0:T(128)S(6)} %copy.10.scale, f32[1]{0:T(128)S(6)} %copy.11.bias, ...), custom_call_target="tpu_custom_call" | custom-call | flops 509607936 | bytes 3538944 | tf_op jit(solution)/shard_map/pallas_call | solution.py:138
  23.5 0.0 collective-permute-done.4.f3
  23.5 0.0 copy-start.12
  23.5 6.5 %shard_map.95 = (bf16[1152,384]{1,0:T(8,128)(2,1)S(1)}, bf16[384,1152]{1,0:T(8,128)(2,1)S(1)}, bf16[288,384]{1,0:T(8,128)(2,1)S(1)}, f32[1,384]{1,0:T(1,128)S(1)...) custom-call(f32[1]{0:T(128)S(6)} %copy.10.scale, f32[1]{0:T(128)S(6)} %copy.11.bias, ...), custom_call_target="tpu_custom_call" | custom-call | flops 1528823808 | bytes 3538944 | tf_op jit(solution)/shard_map/pallas_call | solution.py:138
  30.0 2.0 %shard_map.96 = (bf16[192,1152]{1,0:T(8,128)(2,1)}, f32[8,128]{1,0:T(8,128)S(1)}) custom-call(f32[1]{0:T(128)S(6)} %copy.10.scale, bf16[192,1152]{1,0:T(8,128)(2,1)S(1)} %copy-done.12, bf16[384,384]{1,0:T(8,128)(2,1)S(1)} %get-tuple-element.67.weights_near, bf16[384,384]{1,0:T(8,128)(2,1)S(1)} %get-tuple-element.68.weights_far, ...), custom_call_target="tpu_custom_call" | custom-call | flops 1019215872 | bytes 2654208 | tf_op jit(solution)/shard_map/pallas_call | solution.py:138
  32.0 0.0 collective-permute-done.3.t2
  32.0 0.7 collective-permute-start.5
  32.6 3.0 %shard_map.97 = (bf16[192,1152]{1,0:T(8,128)(2,1)S(1)}, bf16[192,768]{1,0:T(8,128)(2,1)S(1)}, f32[288,384]{1,0:T(8,128)S(1)}, f32[288,384]{1,0:T(8,128)S(1)}, f32[1,768]{1,0:T(1,128)S(1)}) custom-call(f32[1]{0:T(128)S(6)} %copy.10.scale, f32[1]{0:T(128)S(6)} %copy.11.bias, s32[2]{0:T(128)S(1)} %pad_add_fusion.place, ...), custom_call_target="tpu_custom_call" | custom-call | flops 1019215872 | bytes 3538944 | tf_op jit(solution)/shard_map/pallas_call | solution.py:138
  35.7 0.0 collective-permute-done.5.t3
  35.7 0.0 copy-start.8
  35.7 0.0 copy-start.10
  35.7 4.1 %shard_map.98 = (bf16[4,128,256]{2,1,0:T(8,128)(2,1)S(1)}, bf16[4,128,256]{2,1,0:T(8,128)(2,1)S(1)}, bf16[2,48,256]{2,1,0:T(8,128)(2,1)S(1)}, bf16[2,48,256]{2,1...) custom-call(f32[1]{0:T(128)S(6)} %copy.10.scale, ...), custom_call_target="tpu_custom_call" | custom-call | flops 2038431744 | bytes 7077888 | tf_op jit(solution)/shard_map/pallas_call | solution.py:138
  39.8 1.6 %collective-permute-start.6 = (bf16[4,128,256]{2,1,0:T(8,128)(2,1)S(1)}, bf16[4,128,256]{2,1,0:T(8,128)(2,1)S(1)}, u32[]{:S(2)}, u32[]{:S(2)}) collective-permute-start(bf16[4,128,256]{2,1,0:T(8,128)(2,1)S(1)} %get-tuple-element.93), channel_id=1, source_target_pairs={{0,1},{1,0},{2,3},{3,2},{4,5},{5,4},{6,7},{7,6},{8,9},{9,8},{10,11... | collective-permute-start | bytes 786440 | tf_op jit(solution)/shard_map/ppermute | solution.py:34
  41.4 3.6 %collective-permute-start.7 = (bf16[2,48,256]{2,1,0:T(8,128)(2,1)S(1)}, bf16[2,48,256]{2,1,0:T(8,128)(2,1)S(1)}, u32[]{:S(2)}, u32[]{:S(2)}) collective-permute-start(bf16[2,48,256]{2,1,0:T(8,128)(2,1)S(1)} %get-tuple-element.95), channel_id=1, source_target_pairs={{0,6},{1,7},{2,4},{3,5},{4,2},{5,3},{6,0},{7,1},{8,14},{9,15},{10,... | collective-permute-start | bytes 147464 | tf_op jit(solution)/shard_map/ppermute | solution.py:34
  45.0 0.8 %collective-permute-start.9 = (bf16[2,48,256]{2,1,0:T(8,128)(2,1)S(1)}, bf16[2,48,256]{2,1,0:T(8,128)(2,1)S(1)}, u32[]{:S(2)}, u32[]{:S(2)}) collective-permute-start(bf16[2,48,256]{2,1,0:T(8,128)(2,1)S(1)} %get-tuple-element.97), channel_id=1, source_target_pairs={{0,2},{1,3},{2,0},{3,1},{4,6},{5,7},{6,4},{7,5},{8,10},{9,11},{10,... | collective-permute-start | bytes 147464 | tf_op jit(solution)/shard_map/ppermute | solution.py:34
  45.8 3.6 %shard_map.99 = (bf16[192,1152]{1,0:T(8,128)(2,1)}, f32[8,128]{1,0:T(8,128)S(1)}) custom-call(f32[1]{0:T(128)S(6)} %copy.10.scale, bf16[192,1152]{1,0:T(8,128)(2,1)S(1)} %copy-done.10, bf16[1152,1152]{1,0:T(8,128)(2,1)S(1)} %get-tuple-element.56.proj, f32[1,1152]{1,0:T(1,128)S(1)} %reshape.11.gain, bf16[384,1152]{1,0:T(8,128)(2,1)S(1)} %copy-done.2, ...), custom_call_target="tpu_custom_call" | custom-call | flops 2038431744 | bytes 5308416 | tf_op jit(solution)/shard_map/pallas_call | solution.py:138
  49.5 0.6 collective-permute-done.8.refs_1_
  50.0 0.0 collective-permute-done.6.across
  50.0 0.6 shard_map.100
  50.7 3.1 %collective-permute-start.11 = (bf16[128,256]{1,0:T(8,128)(2,1)S(1)}, bf16[128,256]{1,0:T(8,128)(2,1)S(1)}, u32[]{:S(2)}, u32[]{:S(2)}) collective-permute-start(bf16[128,256]{1,0:T(8,128)(2,1)S(1)} %get-tuple-element.101), channel_id=1, source_target_pairs={{0,6},{1,7},{2,4},{3,5},{4,2},{5,3},{6,0},{7,1},{8,14},{9,15},{10,... | collective-permute-start | bytes 196616 | tf_op jit(solution)/shard_map/ppermute | solution.py:34
  53.8 1.3 %collective-permute-start.13 = (bf16[128,256]{1,0:T(8,128)(2,1)S(1)}, bf16[128,256]{1,0:T(8,128)(2,1)S(1)}, u32[]{:S(2)}, u32[]{:S(2)}) collective-permute-start(bf16[128,256]{1,0:T(8,128)(2,1)S(1)} %get-tuple-element.103), channel_id=1, source_target_pairs={{0,2},{1,3},{2,0},{3,1},{4,6},{5,7},{6,4},{7,5},{8,10},{9,11},{10,... | collective-permute-start | bytes 196616 | tf_op jit(solution)/shard_map/ppermute | solution.py:34
  55.1 0.5 collective-permute-start.10
  55.6 3.3 %collective-permute-done.10.tail_across = bf16[48,256]{1,0:T(8,128)(2,1)S(1)} collective-permute-done((bf16[48,256]{1,0:T(8,128)(2,1)S(1)}, bf16[48,256]{1,0:T(8,128)(2,1)S(1)}, u32[]{:S(2)}, u32[]{:S(2)}) %collective-permute-start.10) | collective-permute-done | bytes 24608 | tf_op jit(solution)/shard_map/ppermute | solution.py:34
  59.0 0.2 collective-permute-done.12.refs_2_
  59.2 0.9 %collective-permute-start.15 = (bf16[176,256]{1,0:T(8,128)(2,1)S(1)}, bf16[176,256]{1,0:T(8,128)(2,1)S(1)}, u32[]{:S(2)}, u32[]{:S(2)}) collective-permute-start(bf16[176,256]{1,0:T(8,128)(2,1)S(1)} %shard_map.101.refs_0_), channel_id=1, source_target_pairs={{0,16},{8,24},{16,0},{24,8},{1,17},{9,25},{17,1},{25,9},{2,18},{10... | collective-permute-start | bytes 270344 | tf_op jit(solution)/shard_map/ppermute | solution.py:34
  60.1 3.7 %collective-permute-done.15.refs_2_ = bf16[176,256]{1,0:T(8,128)(2,1)S(1)} collective-permute-done((bf16[176,256]{1,0:T(8,128)(2,1)S(1)}, bf16[176,256]{1,0:T(8,128)(2,1)S(1)}, u32[]{:S(2)}, u32[]{:S(2)}) %collective-permute-start.15) | collective-permute-done | bytes 90144 | tf_op jit(solution)/shard_map/ppermute | solution.py:34
  63.8 1.3 %collective-permute-done.16.refs_3_ = bf16[176,256]{1,0:T(8,128)(2,1)S(1)} collective-permute-done((bf16[176,256]{1,0:T(8,128)(2,1)S(1)}, bf16[176,256]{1,0:T(8,128)(2,1)S(1)}, u32[]{:S(2)}, u32[]{:S(2)}) %collective-permute-start.16) | collective-permute-done | bytes 90144 | tf_op jit(solution)/shard_map/ppermute | solution.py:34
  65.1 1.7 %shard_map.102 = (f32[144,1152]{1,0:T(8,128)}, f32[1152]{0:T(1024)}) custom-call(s32[2]{0:T(128)S(1)} %pad_add_fusion.place, bf16[176,256]{1,0:T(8,128)(2,1)S(1)} %shard_map.101.refs_0_, bf16[176,256]{1,0:T(8,128)(2,1)S(1)} %collective-permute-done.14.refs_1_, bf16[176,256]{1,0:T(8,128)(2,1)S(1)} %collective-permute-done.15.refs_2_, ...), custom_call_target="tpu_custom_call" | custom-call | bytes 1327104 | tf_op jit(solution)/shard_map/pallas_call | solution.py:138
  (24 shorter events, 0.1 us)
Async XLA Ops:
  0.6 4.2 %collective-permute-start = (bf16[192,1152]{1,0:T(8,128)(2,1)}, bf16[192,1152]{1,0:T(8,128)(2,1)S(1)}, u32[]{:S(2)}, u32[]{:S(2)}) collective-permute-start(bf16[192,1152]{1,0:T(8,128)(2,1)} %bitcast.6), channel_id=1, source_target_pairs={{0,8},{8,0},{16,24},{24,16},{1,9},{9,1},{17,25},{25,17},{2,10},{10... | collective-permute-start | bytes 1327112 | tf_op jit(solution)/shard_map/ppermute | solution.py:34
  1.1 3.7 %collective-permute-start.1 = (bf16[192,1152]{1,0:T(8,128)(2,1)}, bf16[192,1152]{1,0:T(8,128)(2,1)S(1)}, u32[]{:S(2)}, u32[]{:S(2)}) collective-permute-start(bf16[192,1152]{1,0:T(8,128)(2,1)} %bitcast.1.t0_far), channel_id=1, source_target_pairs={{0,8},{8,0},{16,24},{24,16},{1,9},{9,1},{17,25},{25,17},{2,10},{10... | collective-permute-start | bytes 1327112 | tf_op jit(solution)/shard_map/ppermute | solution.py:34
  1.2 13.6 %collective-permute-start.2 = (bf16[192,1152]{1,0:T(8,128)(2,1)}, bf16[192,1152]{1,0:T(8,128)(2,1)}, u32[]{:S(2)}, u32[]{:S(2)}) collective-permute-start(bf16[192,1152]{1,0:T(8,128)(2,1)} %bitcast.7), channel_id=1, source_target_pairs={{0,16},{8,24},{16,0},{24,8},{1,17},{9,25},{17,1},{25,9},{2,18},{10... | collective-permute-start | bytes 1327112 | tf_op jit(solution)/shard_map/ppermute | solution.py:34
  4.9 1.0 %copy-start.5 = (bf16[192,1,1152]{2,0,1:T(8,128)(2,1)S(1)}, bf16[192,1,1152]{2,0,1:T(8,128)(2,1)}, u32[]{:S(2)}) copy-start(bf16[192,1,1152]{2,0,1:T(8,128)(2,1)} %param.6) | copy-start | bytes 1327108
  10.1 0.9 %copy-start = (bf16[384,1152]{1,0:T(8,128)(2,1)}, bf16[384,1152]{1,0:T(8,128)(2,1)S(1)}, u32[]{:S(2)}) copy-start(bf16[384,1152]{1,0:T(8,128)(2,1)S(1)} %get-tuple-element.57.text_unit.text_near) | copy-start | bytes 2654212
  11.0 0.9 %copy-start.3 = (bf16[384,1152]{1,0:T(8,128)(2,1)}, bf16[384,1152]{1,0:T(8,128)(2,1)S(1)}, u32[]{:S(2)}) copy-start(bf16[384,1152]{1,0:T(8,128)(2,1)S(1)} %get-tuple-element.62.normed) | copy-start | bytes 2654212
  12.0 0.7 %copy-start.6 = (f32[384,128]{1,0:T(8,128)}, f32[384,128]{1,0:T(8,128)S(1)}, u32[]{:S(2)}) copy-start(f32[384,128]{1,0:T(8,128)S(1)} %get-tuple-element.63.factors) | copy-start | bytes 589828
  12.6 0.8 %copy-start.9 = (bf16[192,1152]{1,0:T(8,128)(2,1)}, bf16[192,1152]{1,0:T(8,128)(2,1)S(1)}, u32[]{:S(2)}) copy-start(bf16[192,1152]{1,0:T(8,128)(2,1)S(1)} %get-tuple-element.55.features) | copy-start | bytes 1327108
  13.4 0.8 %copy-start.11 = (bf16[192,1152]{1,0:T(8,128)(2,1)}, bf16[192,1152]{1,0:T(8,128)(2,1)S(1)}, u32[]{:S(2)}) copy-start(bf16[192,1152]{1,0:T(8,128)(2,1)S(1)} %get-tuple-element.71.text) | copy-start | bytes 1327108
  14.9 8.6 %collective-permute-start.4 = (bf16[192,1152]{1,0:T(8,128)(2,1)}, bf16[192,1152]{1,0:T(8,128)(2,1)}, u32[]{:S(2)}, u32[]{:S(2)}) collective-permute-start(bf16[192,1152]{1,0:T(8,128)(2,1)} %collective-permute-done.2.f2), channel_id=1, source_target_pairs={{0,8},{8,0},{16,24},{24,16},{1,9},{9,1},{17,25},{25,17},{2,10},{10... | collective-permute-start | bytes 1327112 | tf_op jit(solution)/shard_map/ppermute | solution.py:34
  14.9 17.1 %collective-permute-start.3 = (bf16[192,1152]{1,0:T(8,128)(2,1)}, bf16[192,1152]{1,0:T(8,128)(2,1)}, u32[]{:S(2)}, u32[]{:S(2)}) collective-permute-start(bf16[192,1152]{1,0:T(8,128)(2,1)} %bitcast.1.t0_far), channel_id=1, source_target_pairs={{0,16},{8,24},{16,0},{24,8},{1,17},{9,25},{17,1},{25,9},{2,18},{10... | collective-permute-start | bytes 1327112 | tf_op jit(solution)/shard_map/ppermute | solution.py:34
  18.0 1.2 %copy-start.1 = (bf16[384,1152]{1,0:T(8,128)(2,1)S(1)}, bf16[384,1152]{1,0:T(8,128)(2,1)}, u32[]{:S(2)}) copy-start(bf16[384,1152]{1,0:T(8,128)(2,1)} %copy-done) | copy-start | bytes 2654212
  19.2 1.2 %copy-start.4 = (bf16[384,1152]{1,0:T(8,128)(2,1)S(1)}, bf16[384,1152]{1,0:T(8,128)(2,1)}, u32[]{:S(2)}) copy-start(bf16[384,1152]{1,0:T(8,128)(2,1)} %copy-done.3) | copy-start | bytes 2654212
  20.3 0.9 %copy-start.7 = (f32[384,128]{1,0:T(8,128)S(1)}, f32[384,128]{1,0:T(8,128)}, u32[]{:S(2)}) copy-start(f32[384,128]{1,0:T(8,128)} %copy-done.6) | copy-start | bytes 589828
  21.3 2.2 %copy-start.2 = (bf16[384,1152]{1,0:T(8,128)(2,1)S(1)}, bf16[384,1152]{1,0:T(8,128)(2,1)}, u32[]{:S(2)}) copy-start(bf16[384,1152]{1,0:T(8,128)(2,1)} %copy-done) | copy-start | bytes 2654212
  23.5 6.5 %copy-start.12 = (bf16[192,1152]{1,0:T(8,128)(2,1)S(1)}, bf16[192,1152]{1,0:T(8,128)(2,1)}, u32[]{:S(2)}) copy-start(bf16[192,1152]{1,0:T(8,128)(2,1)} %copy-done.11) | copy-start | bytes 1327108
  32.0 3.7 %collective-permute-start.5 = (bf16[192,1152]{1,0:T(8,128)(2,1)}, bf16[192,1152]{1,0:T(8,128)(2,1)S(1)}, u32[]{:S(2)}, u32[]{:S(2)}) collective-permute-start(bf16[192,1152]{1,0:T(8,128)(2,1)} %collective-permute-done.3.t2), channel_id=1, source_target_pairs={{0,8},{8,0},{16,24},{24,16},{1,9},{9,1},{17,25},{25,17},{2,10},{10... | collective-permute-start | bytes 1327112 | tf_op jit(solution)/shard_map/ppermute | solution.py:34
  35.7 10.1 %copy-start.8 = (f32[384,128]{1,0:T(8,128)S(1)}, f32[384,128]{1,0:T(8,128)}, u32[]{:S(2)}) copy-start(f32[384,128]{1,0:T(8,128)} %copy-done.6) | copy-start | bytes 589828
  35.7 10.1 %copy-start.10 = (bf16[192,1152]{1,0:T(8,128)(2,1)S(1)}, bf16[192,1152]{1,0:T(8,128)(2,1)}, u32[]{:S(2)}) copy-start(bf16[192,1152]{1,0:T(8,128)(2,1)} %copy-done.9) | copy-start | bytes 1327108
  39.8 10.2 %collective-permute-start.6 = (bf16[4,128,256]{2,1,0:T(8,128)(2,1)S(1)}, bf16[4,128,256]{2,1,0:T(8,128)(2,1)S(1)}, u32[]{:S(2)}, u32[]{:S(2)}) collective-permute-start(bf16[4,128,256]{2,1,0:T(8,128)(2,1)S(1)} %get-tuple-element.93), channel_id=1, source_target_pairs={{0,1},{1,0},{2,3},{3,2},{4,5},{5,4},{6,7},{7,6},{8,9},{9,8},{10,11... | collective-permute-start | bytes 786440 | tf_op jit(solution)/shard_map/ppermute | solution.py:34
  41.4 8.0 %collective-permute-start.7 = (bf16[2,48,256]{2,1,0:T(8,128)(2,1)S(1)}, bf16[2,48,256]{2,1,0:T(8,128)(2,1)S(1)}, u32[]{:S(2)}, u32[]{:S(2)}) collective-permute-start(bf16[2,48,256]{2,1,0:T(8,128)(2,1)S(1)} %get-tuple-element.95), channel_id=1, source_target_pairs={{0,6},{1,7},{2,4},{3,5},{4,2},{5,3},{6,0},{7,1},{8,14},{9,15},{10,... | collective-permute-start | bytes 147464 | tf_op jit(solution)/shard_map/ppermute | solution.py:34
  45.0 5.0 %collective-permute-start.8 = (bf16[2,48,256]{2,1,0:T(8,128)(2,1)S(1)}, bf16[2,48,256]{2,1,0:T(8,128)(2,1)S(1)}, u32[]{:S(2)}, u32[]{:S(2)}) collective-permute-start(bf16[2,48,256]{2,1,0:T(8,128)(2,1)S(1)} %get-tuple-element.96), channel_id=1, source_target_pairs={{0,4},{1,5},{2,6},{3,7},{4,0},{5,1},{6,2},{7,3},{8,12},{9,13},{10,... | collective-permute-start | bytes 147464 | tf_op jit(solution)/shard_map/ppermute | solution.py:34
  45.0 5.0 %collective-permute-start.9 = (bf16[2,48,256]{2,1,0:T(8,128)(2,1)S(1)}, bf16[2,48,256]{2,1,0:T(8,128)(2,1)S(1)}, u32[]{:S(2)}, u32[]{:S(2)}) collective-permute-start(bf16[2,48,256]{2,1,0:T(8,128)(2,1)S(1)} %get-tuple-element.97), channel_id=1, source_target_pairs={{0,2},{1,3},{2,0},{3,1},{4,6},{5,7},{6,4},{7,5},{8,10},{9,11},{10,... | collective-permute-start | bytes 147464 | tf_op jit(solution)/shard_map/ppermute | solution.py:34
  50.7 8.3 %collective-permute-start.11 = (bf16[128,256]{1,0:T(8,128)(2,1)S(1)}, bf16[128,256]{1,0:T(8,128)(2,1)S(1)}, u32[]{:S(2)}, u32[]{:S(2)}) collective-permute-start(bf16[128,256]{1,0:T(8,128)(2,1)S(1)} %get-tuple-element.101), channel_id=1, source_target_pairs={{0,6},{1,7},{2,4},{3,5},{4,2},{5,3},{6,0},{7,1},{8,14},{9,15},{10,... | collective-permute-start | bytes 196616 | tf_op jit(solution)/shard_map/ppermute | solution.py:34
  53.8 5.4 %collective-permute-start.12 = (bf16[128,256]{1,0:T(8,128)(2,1)S(1)}, bf16[128,256]{1,0:T(8,128)(2,1)S(1)}, u32[]{:S(2)}, u32[]{:S(2)}) collective-permute-start(bf16[128,256]{1,0:T(8,128)(2,1)S(1)} %get-tuple-element.102), channel_id=1, source_target_pairs={{0,4},{1,5},{2,6},{3,7},{4,0},{5,1},{6,2},{7,3},{8,12},{9,13},{10,... | collective-permute-start | bytes 196616 | tf_op jit(solution)/shard_map/ppermute | solution.py:34
  53.8 5.4 %collective-permute-start.13 = (bf16[128,256]{1,0:T(8,128)(2,1)S(1)}, bf16[128,256]{1,0:T(8,128)(2,1)S(1)}, u32[]{:S(2)}, u32[]{:S(2)}) collective-permute-start(bf16[128,256]{1,0:T(8,128)(2,1)S(1)} %get-tuple-element.103), channel_id=1, source_target_pairs={{0,2},{1,3},{2,0},{3,1},{4,6},{5,7},{6,4},{7,5},{8,10},{9,11},{10,... | collective-permute-start | bytes 196616 | tf_op jit(solution)/shard_map/ppermute | solution.py:34
  55.1 3.8 %collective-permute-start.10 = (bf16[48,256]{1,0:T(8,128)(2,1)S(1)}, bf16[48,256]{1,0:T(8,128)(2,1)S(1)}, u32[]{:S(2)}, u32[]{:S(2)}) collective-permute-start(bf16[48,256]{1,0:T(8,128)(2,1)S(1)} %get-tuple-element.99), channel_id=1, source_target_pairs={{0,1},{1,0},{2,3},{3,2},{4,5},{5,4},{6,7},{7,6},{8,9},{9,8},{10,11... | collective-permute-start | bytes 73736 | tf_op jit(solution)/shard_map/ppermute | solution.py:34
  59.2 4.6 %collective-permute-start.15 = (bf16[176,256]{1,0:T(8,128)(2,1)S(1)}, bf16[176,256]{1,0:T(8,128)(2,1)S(1)}, u32[]{:S(2)}, u32[]{:S(2)}) collective-permute-start(bf16[176,256]{1,0:T(8,128)(2,1)S(1)} %shard_map.101.refs_0_), channel_id=1, source_target_pairs={{0,16},{8,24},{16,0},{24,8},{1,17},{9,25},{17,1},{25,9},{2,18},{10... | collective-permute-start | bytes 270344 | tf_op jit(solution)/shard_map/ppermute | solution.py:34
  60.1 3.7 %collective-permute-start.14 = (bf16[176,256]{1,0:T(8,128)(2,1)S(1)}, bf16[176,256]{1,0:T(8,128)(2,1)S(1)}, u32[]{:S(2)}, u32[]{:S(2)}) collective-permute-start(bf16[176,256]{1,0:T(8,128)(2,1)S(1)} %shard_map.101.refs_0_), channel_id=1, source_target_pairs={{0,8},{8,0},{16,24},{24,16},{1,9},{9,1},{17,25},{25,17},{2,10},{10... | collective-permute-start | bytes 270344 | tf_op jit(solution)/shard_map/ppermute | solution.py:34
  63.8 1.3 %collective-permute-start.16 = (bf16[176,256]{1,0:T(8,128)(2,1)S(1)}, bf16[176,256]{1,0:T(8,128)(2,1)S(1)}, u32[]{:S(2)}, u32[]{:S(2)}) collective-permute-start(bf16[176,256]{1,0:T(8,128)(2,1)S(1)} %collective-permute-done.15.refs_2_), channel_id=1, source_target_pairs={{0,8},{8,0},{16,24},{24,16},{1,9},{9,1},{17,25},{25,17},{2,10},{10... | collective-permute-start | bytes 270344 | tf_op jit(solution)/shard_map/ppermute | solution.py:34

commit v8 on v7

--- a/solution.py
+++ b/solution.py
@@ -516,7 +516,7 @@
         [half, kept, half, wide, wide, ((near, LANES), F32), wide, TOKEN],
         [((near, width), F32)],
         hbm=3,
-        limit=46,
+        limit=36,
         flops=2 * near * width * width,
         moved=8 * near * width,
     )(f0, proj, t0, f1, t1, gain_row)

time: 67.2 us -> 68 us (1.012)
  local copies, waits for them, and re-layouts: 9.03 us -> 10.8 us
  waiting for transfers between devices: 9.75 us -> 8.95 us
    unnamed x26 -> x28, local copies, waits for them, and re-layouts: 8.33 us -> 10.1 us
    ppermute x17, waiting for transfers between devices: 9.75 us -> 8.95 us  [send(): return lax.ppermute(value, axis, [(p, target(p)) for p in range(count)])]
  transfers between devices with their start and end apart: 17 -> 17, of which waited for: 6 -> 5; matrix products, arithmetic and copies ran while one was open for 1% -> 1% of each run, Pallas kernels for 32% -> 32%
where the time goes in v8:
time: 68 us; the launch traced here: 67.6 us
  Pallas kernels  28.2 us (41%)
  starting transfers between devices  17.6 us (26%)
  local copies, waits for them, and re-layouts  10.8 us (16%)
  waiting for transfers between devices  8.95 us (13%)
  between operations  2.07 us (3%)
    pallas_call x10, Pallas kernels, run(): pl.pallas_call(body, out_shape=[jax.ShapeDtypeStruct(shape, kind) for sha...  28.2 us
    ppermute x17, starting transfers between devices, send(): return lax.ppermute(value, axis, [(p, target(p)) for p in range(count)])  17.6 us
    unnamed x28, local copies, waits for them, and re-layouts  10.1 us
    ppermute x17, waiting for transfers between devices, send(): return lax.ppermute(value, axis, [(p, target(p)) for p in range(count)])  8.95 us
  transfers between devices with their start and end apart: 17, of which 5 were waited for; matrix products, arithmetic and copies ran while one was open for 1% of the time, Pallas kernels for 32%

profile of v8, /device:TPU:0, one launch (start us, length us, event | category | flops | bytes accessed | tf_op | source)
XLA Modules:
  0.0 67.6 jit_solution(1452611955034520624)
XLA Ops:
  0.6 0.5 collective-permute-start
  1.1 0.1 collective-permute-start.1
  1.2 2.9 %collective-permute-start.2 = (bf16[192,1152]{1,0:T(8,128)(2,1)}, bf16[192,1152]{1,0:T(8,128)(2,1)}, u32[]{:S(2)}, u32[]{:S(2)}) collective-permute-start(bf16[192,1152]{1,0:T(8,128)(2,1)} %bitcast.7), channel_id=1, source_target_pairs={{0,16},{8,24},{16,0},{24,8},{1,17},{9,25},{17,1},{25,9},{2,18},{10... | collective-permute-start | bytes 1327112 | tf_op jit(solution)/shard_map/ppermute | solution.py:34
  4.1 0.7 %reshape.11.gain = f32[1,1152]{1,0:T(1,128)S(1)} reshape(f32[1152]{0:T(1024)} %param.9) | data formatting | bytes 9216 | tf_op jit(solution)/shard_map/reshape | solution.py:498
  4.8 0.0 collective-permute-done.f1
  4.9 0.0 copy-start
  4.9 1.7 %copy-done = bf16[1152,1152]{1,0:T(8,128)(2,1)S(1)} copy-done((bf16[1152,1152]{1,0:T(8,128)(2,1)S(1)}, bf16[1152,1152]{1,0:T(8,128)(2,1)}, u32[]{:S(2)}) %copy-start) | copy-done | bytes 2654232
  6.6 1.0 %copy-done.6 = bf16[192,1,1152]{2,0,1:T(8,128)(2,1)S(1)} copy-done((bf16[192,1,1152]{2,0,1:T(8,128)(2,1)S(1)}, bf16[192,1,1152]{2,0,1:T(8,128)(2,1)}, u32[]{:S(2)}) %copy-start.6) | copy-done | bytes 442392
  7.6 4.4 %shard_map.93 = (bf16[192,1152]{1,0:T(8,128)(2,1)S(1)}, bf16[1152,1152]{1,0:T(8,128)(2,1)S(1)}, bf16[192,1152]{1,0:T(8,128)(2,1)S(1)}, bf16[384,1152]{1,0:T(8,12...) custom-call(bf16[192,1152]{1,0:T(8,128)(2,1)S(1)} %bitcast.8, ...), custom_call_target="tpu_custom_call" | custom-call | flops 1019215872 | bytes 3538944 | tf_op jit(solution)/shard_map/pallas_call | solution.py:138
  12.0 0.9 %copy-done.1 = bf16[384,1152]{1,0:T(8,128)(2,1)} copy-done((bf16[384,1152]{1,0:T(8,128)(2,1)}, bf16[384,1152]{1,0:T(8,128)(2,1)S(1)}, u32[]{:S(2)}) %copy-start.1) | copy-done | bytes 884760
  12.9 0.9 %copy-done.4 = bf16[384,1152]{1,0:T(8,128)(2,1)} copy-done((bf16[384,1152]{1,0:T(8,128)(2,1)}, bf16[384,1152]{1,0:T(8,128)(2,1)S(1)}, u32[]{:S(2)}) %copy-start.4) | copy-done | bytes 884760
  13.9 0.7 copy-done.7
  14.6 0.8 %copy-done.10 = bf16[192,1152]{1,0:T(8,128)(2,1)} copy-done((bf16[192,1152]{1,0:T(8,128)(2,1)}, bf16[192,1152]{1,0:T(8,128)(2,1)S(1)}, u32[]{:S(2)}) %copy-start.10) | copy-done | bytes 442392
  15.3 0.8 %copy-done.12 = bf16[192,1152]{1,0:T(8,128)(2,1)} copy-done((bf16[192,1152]{1,0:T(8,128)(2,1)}, bf16[192,1152]{1,0:T(8,128)(2,1)S(1)}, u32[]{:S(2)}) %copy-start.12) | copy-done | bytes 442392
  16.1 1.6 %collective-permute-start.3 = (bf16[192,1152]{1,0:T(8,128)(2,1)}, bf16[192,1152]{1,0:T(8,128)(2,1)}, u32[]{:S(2)}, u32[]{:S(2)}) collective-permute-start(bf16[192,1152]{1,0:T(8,128)(2,1)} %bitcast.1.t0_far), channel_id=1, source_target_pairs={{0,16},{8,24},{16,0},{24,8},{1,17},{9,25},{17,1},{25,9},{2,18},{10... | collective-permute-start | bytes 1327112 | tf_op jit(solution)/shard_map/ppermute | solution.py:34
  18.9 0.1 pad_add_fusion.place
  19.0 1.2 %copy-done.2 = bf16[384,1152]{1,0:T(8,128)(2,1)S(1)} copy-done((bf16[384,1152]{1,0:T(8,128)(2,1)S(1)}, bf16[384,1152]{1,0:T(8,128)(2,1)}, u32[]{:S(2)}) %copy-start.2) | copy-done | bytes 884760
  20.2 1.2 %copy-done.5 = bf16[384,1152]{1,0:T(8,128)(2,1)S(1)} copy-done((bf16[384,1152]{1,0:T(8,128)(2,1)S(1)}, bf16[384,1152]{1,0:T(8,128)(2,1)}, u32[]{:S(2)}) %copy-start.5) | copy-done | bytes 884760
  21.4 0.9 %copy-done.8 = f32[384,128]{1,0:T(8,128)S(1)} copy-done((f32[384,128]{1,0:T(8,128)S(1)}, f32[384,128]{1,0:T(8,128)}, u32[]{:S(2)}) %copy-start.8) | copy-done | bytes 196632
  22.3 2.2 %shard_map.94 = (bf16[1152,384]{1,0:T(8,128)(2,1)S(1)}, bf16[288,384]{1,0:T(8,128)(2,1)S(1)}, f32[1,384]{1,0:T(1,128)S(1)}, bf16[384,288]{1,0:T(8,128)(2,1)S(1)}...) custom-call(f32[1]{0:T(128)S(6)} %copy.10.scale, f32[1]{0:T(128)S(6)} %copy.11.bias, ...), custom_call_target="tpu_custom_call" | custom-call | flops 509607936 | bytes 3538944 | tf_op jit(solution)/shard_map/pallas_call | solution.py:138
  24.5 0.0 collective-permute-done.4.f3
  24.5 0.0 copy-start.13
  24.5 6.5 %shard_map.95 = (bf16[1152,384]{1,0:T(8,128)(2,1)S(1)}, bf16[384,1152]{1,0:T(8,128)(2,1)S(1)}, bf16[288,384]{1,0:T(8,128)(2,1)S(1)}, f32[1,384]{1,0:T(1,128)S(1)...) custom-call(f32[1]{0:T(128)S(6)} %copy.10.scale, f32[1]{0:T(128)S(6)} %copy.11.bias, ...), custom_call_target="tpu_custom_call" | custom-call | flops 1528823808 | bytes 3538944 | tf_op jit(solution)/shard_map/pallas_call | solution.py:138
  31.0 2.0 %shard_map.96 = (bf16[192,1152]{1,0:T(8,128)(2,1)}, f32[8,128]{1,0:T(8,128)S(1)}) custom-call(f32[1]{0:T(128)S(6)} %copy.10.scale, bf16[192,1152]{1,0:T(8,128)(2,1)S(1)} %copy-done.13, bf16[384,384]{1,0:T(8,128)(2,1)S(1)} %get-tuple-element.67.weights_near, bf16[384,384]{1,0:T(8,128)(2,1)S(1)} %get-tuple-element.68.weights_far, ...), custom_call_target="tpu_custom_call" | custom-call | flops 1019215872 | bytes 2654208 | tf_op jit(solution)/shard_map/pallas_call | solution.py:138
  33.0 0.0 collective-permute-done.3.t2
  33.0 0.5 collective-permute-start.5
  33.5 3.0 %shard_map.97 = (bf16[192,1152]{1,0:T(8,128)(2,1)S(1)}, bf16[192,768]{1,0:T(8,128)(2,1)S(1)}, f32[288,384]{1,0:T(8,128)S(1)}, f32[288,384]{1,0:T(8,128)S(1)}, f32[1,768]{1,0:T(1,128)S(1)}) custom-call(f32[1]{0:T(128)S(6)} %copy.10.scale, f32[1]{0:T(128)S(6)} %copy.11.bias, s32[2]{0:T(128)S(1)} %pad_add_fusion.place, ...), custom_call_target="tpu_custom_call" | custom-call | flops 1019215872 | bytes 3538944 | tf_op jit(solution)/shard_map/pallas_call | solution.py:138
  36.6 0.0 copy-start.9
  36.6 0.0 copy-start.11
  36.6 4.1 %shard_map.98 = (bf16[4,128,256]{2,1,0:T(8,128)(2,1)S(1)}, bf16[4,128,256]{2,1,0:T(8,128)(2,1)S(1)}, bf16[2,48,256]{2,1,0:T(8,128)(2,1)S(1)}, bf16[2,48,256]{2,1...) custom-call(f32[1]{0:T(128)S(6)} %copy.10.scale, ...), custom_call_target="tpu_custom_call" | custom-call | flops 2038431744 | bytes 7077888 | tf_op jit(solution)/shard_map/pallas_call | solution.py:138
  40.7 1.6 %collective-permute-start.6 = (bf16[4,128,256]{2,1,0:T(8,128)(2,1)S(1)}, bf16[4,128,256]{2,1,0:T(8,128)(2,1)S(1)}, u32[]{:S(2)}, u32[]{:S(2)}) collective-permute-start(bf16[4,128,256]{2,1,0:T(8,128)(2,1)S(1)} %get-tuple-element.93), channel_id=1, source_target_pairs={{0,1},{1,0},{2,3},{3,2},{4,5},{5,4},{6,7},{7,6},{8,9},{9,8},{10,11... | collective-permute-start | bytes 786440 | tf_op jit(solution)/shard_map/ppermute | solution.py:34
  42.3 3.6 %collective-permute-start.7 = (bf16[2,48,256]{2,1,0:T(8,128)(2,1)S(1)}, bf16[2,48,256]{2,1,0:T(8,128)(2,1)S(1)}, u32[]{:S(2)}, u32[]{:S(2)}) collective-permute-start(bf16[2,48,256]{2,1,0:T(8,128)(2,1)S(1)} %get-tuple-element.95), channel_id=1, source_target_pairs={{0,6},{1,7},{2,4},{3,5},{4,2},{5,3},{6,0},{7,1},{8,14},{9,15},{10,... | collective-permute-start | bytes 147464 | tf_op jit(solution)/shard_map/ppermute | solution.py:34
  45.9 0.0 collective-permute-start.8
  45.9 0.8 %collective-permute-start.9 = (bf16[2,48,256]{2,1,0:T(8,128)(2,1)S(1)}, bf16[2,48,256]{2,1,0:T(8,128)(2,1)S(1)}, u32[]{:S(2)}, u32[]{:S(2)}) collective-permute-start(bf16[2,48,256]{2,1,0:T(8,128)(2,1)S(1)} %get-tuple-element.97), channel_id=1, source_target_pairs={{0,2},{1,3},{2,0},{3,1},{4,6},{5,7},{6,4},{7,5},{8,10},{9,11},{10,... | collective-permute-start | bytes 147464 | tf_op jit(solution)/shard_map/ppermute | solution.py:34
  46.7 3.6 %shard_map.99 = (bf16[192,1152]{1,0:T(8,128)(2,1)}, f32[8,128]{1,0:T(8,128)S(1)}) custom-call(f32[1]{0:T(128)S(6)} %copy.10.scale, bf16[192,1152]{1,0:T(8,128)(2,1)S(1)} %copy-done.11, bf16[1152,1152]{1,0:T(8,128)(2,1)S(1)} %get-tuple-element.56.proj, f32[1,1152]{1,0:T(1,128)S(1)} %reshape.11.gain, bf16[384,1152]{1,0:T(8,128)(2,1)S(1)} %copy-done.3, ...), custom_call_target="tpu_custom_call" | custom-call | flops 2038431744 | bytes 5308416 | tf_op jit(solution)/shard_map/pallas_call | solution.py:138
  50.3 0.0 collective-permute-done.7.refs_0_
  50.3 0.6 collective-permute-done.8.refs_1_
  50.9 0.0 collective-permute-done.9.refs_2_
  50.9 0.6 shard_map.100
  51.5 3.1 %collective-permute-start.11 = (bf16[128,256]{1,0:T(8,128)(2,1)S(1)}, bf16[128,256]{1,0:T(8,128)(2,1)S(1)}, u32[]{:S(2)}, u32[]{:S(2)}) collective-permute-start(bf16[128,256]{1,0:T(8,128)(2,1)S(1)} %get-tuple-element.101), channel_id=1, source_target_pairs={{0,6},{1,7},{2,4},{3,5},{4,2},{5,3},{6,0},{7,1},{8,14},{9,15},{10,... | collective-permute-start | bytes 196616 | tf_op jit(solution)/shard_map/ppermute | solution.py:34
  54.7 1.3 %collective-permute-start.13 = (bf16[128,256]{1,0:T(8,128)(2,1)S(1)}, bf16[128,256]{1,0:T(8,128)(2,1)S(1)}, u32[]{:S(2)}, u32[]{:S(2)}) collective-permute-start(bf16[128,256]{1,0:T(8,128)(2,1)S(1)} %get-tuple-element.103), channel_id=1, source_target_pairs={{0,2},{1,3},{2,0},{3,1},{4,6},{5,7},{6,4},{7,5},{8,10},{9,11},{10,... | collective-permute-start | bytes 196616 | tf_op jit(solution)/shard_map/ppermute | solution.py:34
  56.0 0.5 collective-permute-start.10
  56.5 3.3 %collective-permute-done.10.tail_across = bf16[48,256]{1,0:T(8,128)(2,1)S(1)} collective-permute-done((bf16[48,256]{1,0:T(8,128)(2,1)S(1)}, bf16[48,256]{1,0:T(8,128)(2,1)S(1)}, u32[]{:S(2)}, u32[]{:S(2)}) %collective-permute-start.10) | collective-permute-done | bytes 24608 | tf_op jit(solution)/shard_map/ppermute | solution.py:34
  59.8 0.2 collective-permute-done.12.refs_2_
  60.1 1.0 %collective-permute-start.15 = (bf16[176,256]{1,0:T(8,128)(2,1)S(1)}, bf16[176,256]{1,0:T(8,128)(2,1)S(1)}, u32[]{:S(2)}, u32[]{:S(2)}) collective-permute-start(bf16[176,256]{1,0:T(8,128)(2,1)S(1)} %shard_map.101.refs_0_), channel_id=1, source_target_pairs={{0,16},{8,24},{16,0},{24,8},{1,17},{9,25},{17,1},{25,9},{2,18},{10... | collective-permute-start | bytes 270344 | tf_op jit(solution)/shard_map/ppermute | solution.py:34
  61.1 3.6 %collective-permute-done.15.refs_2_ = bf16[176,256]{1,0:T(8,128)(2,1)S(1)} collective-permute-done((bf16[176,256]{1,0:T(8,128)(2,1)S(1)}, bf16[176,256]{1,0:T(8,128)(2,1)S(1)}, u32[]{:S(2)}, u32[]{:S(2)}) %collective-permute-start.15) | collective-permute-done | bytes 90144 | tf_op jit(solution)/shard_map/ppermute | solution.py:34
  64.7 1.3 %collective-permute-done.16.refs_3_ = bf16[176,256]{1,0:T(8,128)(2,1)S(1)} collective-permute-done((bf16[176,256]{1,0:T(8,128)(2,1)S(1)}, bf16[176,256]{1,0:T(8,128)(2,1)S(1)}, u32[]{:S(2)}, u32[]{:S(2)}) %collective-permute-start.16) | collective-permute-done | bytes 90144 | tf_op jit(solution)/shard_map/ppermute | solution.py:34
  65.9 1.7 %shard_map.102 = (f32[144,1152]{1,0:T(8,128)}, f32[1152]{0:T(1024)}) custom-call(s32[2]{0:T(128)S(1)} %pad_add_fusion.place, bf16[176,256]{1,0:T(8,128)(2,1)S(1)} %shard_map.101.refs_0_, bf16[176,256]{1,0:T(8,128)(2,1)S(1)} %collective-permute-done.14.refs_1_, bf16[176,256]{1,0:T(8,128)(2,1)S(1)} %collective-permute-done.15.refs_2_, ...), custom_call_target="tpu_custom_call" | custom-call | bytes 1327104 | tf_op jit(solution)/shard_map/pallas_call | solution.py:138
  (26 shorter events, 0.1 us)
Async XLA Ops:
  0.6 4.2 %collective-permute-start = (bf16[192,1152]{1,0:T(8,128)(2,1)}, bf16[192,1152]{1,0:T(8,128)(2,1)S(1)}, u32[]{:S(2)}, u32[]{:S(2)}) collective-permute-start(bf16[192,1152]{1,0:T(8,128)(2,1)} %bitcast.6), channel_id=1, source_target_pairs={{0,8},{8,0},{16,24},{24,16},{1,9},{9,1},{17,25},{25,17},{2,10},{10... | collective-permute-start | bytes 1327112 | tf_op jit(solution)/shard_map/ppermute | solution.py:34
  1.1 3.7 %collective-permute-start.1 = (bf16[192,1152]{1,0:T(8,128)(2,1)}, bf16[192,1152]{1,0:T(8,128)(2,1)S(1)}, u32[]{:S(2)}, u32[]{:S(2)}) collective-permute-start(bf16[192,1152]{1,0:T(8,128)(2,1)} %bitcast.1.t0_far), channel_id=1, source_target_pairs={{0,8},{8,0},{16,24},{24,16},{1,9},{9,1},{17,25},{25,17},{2,10},{10... | collective-permute-start | bytes 1327112 | tf_op jit(solution)/shard_map/ppermute | solution.py:34
  1.2 14.8 %collective-permute-start.2 = (bf16[192,1152]{1,0:T(8,128)(2,1)}, bf16[192,1152]{1,0:T(8,128)(2,1)}, u32[]{:S(2)}, u32[]{:S(2)}) collective-permute-start(bf16[192,1152]{1,0:T(8,128)(2,1)} %bitcast.7), channel_id=1, source_target_pairs={{0,16},{8,24},{16,0},{24,8},{1,17},{9,25},{17,1},{25,9},{2,18},{10... | collective-permute-start | bytes 1327112 | tf_op jit(solution)/shard_map/ppermute | solution.py:34
  4.9 1.8 %copy-start = (bf16[1152,1152]{1,0:T(8,128)(2,1)S(1)}, bf16[1152,1152]{1,0:T(8,128)(2,1)}, u32[]{:S(2)}) copy-start(bf16[1152,1152]{1,0:T(8,128)(2,1)} %proj_far.1) | copy-start | bytes 7962628
  6.6 1.0 %copy-start.6 = (bf16[192,1,1152]{2,0,1:T(8,128)(2,1)S(1)}, bf16[192,1,1152]{2,0,1:T(8,128)(2,1)}, u32[]{:S(2)}) copy-start(bf16[192,1,1152]{2,0,1:T(8,128)(2,1)} %param.6) | copy-start | bytes 1327108
  12.0 0.9 %copy-start.1 = (bf16[384,1152]{1,0:T(8,128)(2,1)}, bf16[384,1152]{1,0:T(8,128)(2,1)S(1)}, u32[]{:S(2)}) copy-start(bf16[384,1152]{1,0:T(8,128)(2,1)S(1)} %get-tuple-element.57.text_unit.text_near) | copy-start | bytes 2654212
  12.9 0.9 %copy-start.4 = (bf16[384,1152]{1,0:T(8,128)(2,1)}, bf16[384,1152]{1,0:T(8,128)(2,1)S(1)}, u32[]{:S(2)}) copy-start(bf16[384,1152]{1,0:T(8,128)(2,1)S(1)} %get-tuple-element.62.normed) | copy-start | bytes 2654212
  13.9 0.7 %copy-start.7 = (f32[384,128]{1,0:T(8,128)}, f32[384,128]{1,0:T(8,128)S(1)}, u32[]{:S(2)}) copy-start(f32[384,128]{1,0:T(8,128)S(1)} %get-tuple-element.63.factors) | copy-start | bytes 589828
  14.6 0.8 %copy-start.10 = (bf16[192,1152]{1,0:T(8,128)(2,1)}, bf16[192,1152]{1,0:T(8,128)(2,1)S(1)}, u32[]{:S(2)}) copy-start(bf16[192,1152]{1,0:T(8,128)(2,1)S(1)} %get-tuple-element.55.features) | copy-start | bytes 1327108
  15.3 0.8 %copy-start.12 = (bf16[192,1152]{1,0:T(8,128)(2,1)}, bf16[192,1152]{1,0:T(8,128)(2,1)S(1)}, u32[]{:S(2)}) copy-start(bf16[192,1152]{1,0:T(8,128)(2,1)S(1)} %get-tuple-element.71.text) | copy-start | bytes 1327108
  16.1 8.4 %collective-permute-start.4 = (bf16[192,1152]{1,0:T(8,128)(2,1)}, bf16[192,1152]{1,0:T(8,128)(2,1)}, u32[]{:S(2)}, u32[]{:S(2)}) collective-permute-start(bf16[192,1152]{1,0:T(8,128)(2,1)} %collective-permute-done.2.f2), channel_id=1, source_target_pairs={{0,8},{8,0},{16,24},{24,16},{1,9},{9,1},{17,25},{25,17},{2,10},{10... | collective-permute-start | bytes 1327112 | tf_op jit(solution)/shard_map/ppermute | solution.py:34
  16.1 16.9 %collective-permute-start.3 = (bf16[192,1152]{1,0:T(8,128)(2,1)}, bf16[192,1152]{1,0:T(8,128)(2,1)}, u32[]{:S(2)}, u32[]{:S(2)}) collective-permute-start(bf16[192,1152]{1,0:T(8,128)(2,1)} %bitcast.1.t0_far), channel_id=1, source_target_pairs={{0,16},{8,24},{16,0},{24,8},{1,17},{9,25},{17,1},{25,9},{2,18},{10... | collective-permute-start | bytes 1327112 | tf_op jit(solution)/shard_map/ppermute | solution.py:34
  19.0 1.2 %copy-start.2 = (bf16[384,1152]{1,0:T(8,128)(2,1)S(1)}, bf16[384,1152]{1,0:T(8,128)(2,1)}, u32[]{:S(2)}) copy-start(bf16[384,1152]{1,0:T(8,128)(2,1)} %copy-done.1) | copy-start | bytes 2654212
  20.2 1.2 %copy-start.5 = (bf16[384,1152]{1,0:T(8,128)(2,1)S(1)}, bf16[384,1152]{1,0:T(8,128)(2,1)}, u32[]{:S(2)}) copy-start(bf16[384,1152]{1,0:T(8,128)(2,1)} %copy-done.4) | copy-start | bytes 2654212
  21.4 0.9 %copy-start.8 = (f32[384,128]{1,0:T(8,128)S(1)}, f32[384,128]{1,0:T(8,128)}, u32[]{:S(2)}) copy-start(f32[384,128]{1,0:T(8,128)} %copy-done.7) | copy-start | bytes 589828
  22.3 2.2 %copy-start.3 = (bf16[384,1152]{1,0:T(8,128)(2,1)S(1)}, bf16[384,1152]{1,0:T(8,128)(2,1)}, u32[]{:S(2)}) copy-start(bf16[384,1152]{1,0:T(8,128)(2,1)} %copy-done.1) | copy-start | bytes 2654212
  24.5 6.5 %copy-start.13 = (bf16[192,1152]{1,0:T(8,128)(2,1)S(1)}, bf16[192,1152]{1,0:T(8,128)(2,1)}, u32[]{:S(2)}) copy-start(bf16[192,1152]{1,0:T(8,128)(2,1)} %copy-done.12) | copy-start | bytes 1327108
  33.0 3.6 %collective-permute-start.5 = (bf16[192,1152]{1,0:T(8,128)(2,1)}, bf16[192,1152]{1,0:T(8,128)(2,1)S(1)}, u32[]{:S(2)}, u32[]{:S(2)}) collective-permute-start(bf16[192,1152]{1,0:T(8,128)(2,1)} %collective-permute-done.3.t2), channel_id=1, source_target_pairs={{0,8},{8,0},{16,24},{24,16},{1,9},{9,1},{17,25},{25,17},{2,10},{10... | collective-permute-start | bytes 1327112 | tf_op jit(solution)/shard_map/ppermute | solution.py:34
  36.6 10.1 %copy-start.9 = (f32[384,128]{1,0:T(8,128)S(1)}, f32[384,128]{1,0:T(8,128)}, u32[]{:S(2)}) copy-start(f32[384,128]{1,0:T(8,128)} %copy-done.7) | copy-start | bytes 589828
  36.6 10.1 %copy-start.11 = (bf16[192,1152]{1,0:T(8,128)(2,1)S(1)}, bf16[192,1152]{1,0:T(8,128)(2,1)}, u32[]{:S(2)}) copy-start(bf16[192,1152]{1,0:T(8,128)(2,1)} %copy-done.10) | copy-start | bytes 1327108
  40.7 10.2 %collective-permute-start.6 = (bf16[4,128,256]{2,1,0:T(8,128)(2,1)S(1)}, bf16[4,128,256]{2,1,0:T(8,128)(2,1)S(1)}, u32[]{:S(2)}, u32[]{:S(2)}) collective-permute-start(bf16[4,128,256]{2,1,0:T(8,128)(2,1)S(1)} %get-tuple-element.93), channel_id=1, source_target_pairs={{0,1},{1,0},{2,3},{3,2},{4,5},{5,4},{6,7},{7,6},{8,9},{9,8},{10,11... | collective-permute-start | bytes 786440 | tf_op jit(solution)/shard_map/ppermute | solution.py:34
  42.3 8.0 %collective-permute-start.7 = (bf16[2,48,256]{2,1,0:T(8,128)(2,1)S(1)}, bf16[2,48,256]{2,1,0:T(8,128)(2,1)S(1)}, u32[]{:S(2)}, u32[]{:S(2)}) collective-permute-start(bf16[2,48,256]{2,1,0:T(8,128)(2,1)S(1)} %get-tuple-element.95), channel_id=1, source_target_pairs={{0,6},{1,7},{2,4},{3,5},{4,2},{5,3},{6,0},{7,1},{8,14},{9,15},{10,... | collective-permute-start | bytes 147464 | tf_op jit(solution)/shard_map/ppermute | solution.py:34
  45.9 5.0 %collective-permute-start.8 = (bf16[2,48,256]{2,1,0:T(8,128)(2,1)S(1)}, bf16[2,48,256]{2,1,0:T(8,128)(2,1)S(1)}, u32[]{:S(2)}, u32[]{:S(2)}) collective-permute-start(bf16[2,48,256]{2,1,0:T(8,128)(2,1)S(1)} %get-tuple-element.96), channel_id=1, source_target_pairs={{0,4},{1,5},{2,6},{3,7},{4,0},{5,1},{6,2},{7,3},{8,12},{9,13},{10,... | collective-permute-start | bytes 147464 | tf_op jit(solution)/shard_map/ppermute | solution.py:34
  45.9 5.0 %collective-permute-start.9 = (bf16[2,48,256]{2,1,0:T(8,128)(2,1)S(1)}, bf16[2,48,256]{2,1,0:T(8,128)(2,1)S(1)}, u32[]{:S(2)}, u32[]{:S(2)}) collective-permute-start(bf16[2,48,256]{2,1,0:T(8,128)(2,1)S(1)} %get-tuple-element.97), channel_id=1, source_target_pairs={{0,2},{1,3},{2,0},{3,1},{4,6},{5,7},{6,4},{7,5},{8,10},{9,11},{10,... | collective-permute-start | bytes 147464 | tf_op jit(solution)/shard_map/ppermute | solution.py:34
  51.5 8.3 %collective-permute-start.11 = (bf16[128,256]{1,0:T(8,128)(2,1)S(1)}, bf16[128,256]{1,0:T(8,128)(2,1)S(1)}, u32[]{:S(2)}, u32[]{:S(2)}) collective-permute-start(bf16[128,256]{1,0:T(8,128)(2,1)S(1)} %get-tuple-element.101), channel_id=1, source_target_pairs={{0,6},{1,7},{2,4},{3,5},{4,2},{5,3},{6,0},{7,1},{8,14},{9,15},{10,... | collective-permute-start | bytes 196616 | tf_op jit(solution)/shard_map/ppermute | solution.py:34
  54.7 5.4 %collective-permute-start.12 = (bf16[128,256]{1,0:T(8,128)(2,1)S(1)}, bf16[128,256]{1,0:T(8,128)(2,1)S(1)}, u32[]{:S(2)}, u32[]{:S(2)}) collective-permute-start(bf16[128,256]{1,0:T(8,128)(2,1)S(1)} %get-tuple-element.102), channel_id=1, source_target_pairs={{0,4},{1,5},{2,6},{3,7},{4,0},{5,1},{6,2},{7,3},{8,12},{9,13},{10,... | collective-permute-start | bytes 196616 | tf_op jit(solution)/shard_map/ppermute | solution.py:34
  54.7 5.4 %collective-permute-start.13 = (bf16[128,256]{1,0:T(8,128)(2,1)S(1)}, bf16[128,256]{1,0:T(8,128)(2,1)S(1)}, u32[]{:S(2)}, u32[]{:S(2)}) collective-permute-start(bf16[128,256]{1,0:T(8,128)(2,1)S(1)} %get-tuple-element.103), channel_id=1, source_target_pairs={{0,2},{1,3},{2,0},{3,1},{4,6},{5,7},{6,4},{7,5},{8,10},{9,11},{10,... | collective-permute-start | bytes 196616 | tf_op jit(solution)/shard_map/ppermute | solution.py:34
  56.0 3.8 %collective-permute-start.10 = (bf16[48,256]{1,0:T(8,128)(2,1)S(1)}, bf16[48,256]{1,0:T(8,128)(2,1)S(1)}, u32[]{:S(2)}, u32[]{:S(2)}) collective-permute-start(bf16[48,256]{1,0:T(8,128)(2,1)S(1)} %get-tuple-element.99), channel_id=1, source_target_pairs={{0,1},{1,0},{2,3},{3,2},{4,5},{5,4},{6,7},{7,6},{8,9},{9,8},{10,11... | collective-permute-start | bytes 73736 | tf_op jit(solution)/shard_map/ppermute | solution.py:34
  60.1 4.6 %collective-permute-start.15 = (bf16[176,256]{1,0:T(8,128)(2,1)S(1)}, bf16[176,256]{1,0:T(8,128)(2,1)S(1)}, u32[]{:S(2)}, u32[]{:S(2)}) collective-permute-start(bf16[176,256]{1,0:T(8,128)(2,1)S(1)} %shard_map.101.refs_0_), channel_id=1, source_target_pairs={{0,16},{8,24},{16,0},{24,8},{1,17},{9,25},{17,1},{25,9},{2,18},{10... | collective-permute-start | bytes 270344 | tf_op jit(solution)/shard_map/ppermute | solution.py:34
  61.1 3.6 %collective-permute-start.14 = (bf16[176,256]{1,0:T(8,128)(2,1)S(1)}, bf16[176,256]{1,0:T(8,128)(2,1)S(1)}, u32[]{:S(2)}, u32[]{:S(2)}) collective-permute-start(bf16[176,256]{1,0:T(8,128)(2,1)S(1)} %shard_map.101.refs_0_), channel_id=1, source_target_pairs={{0,8},{8,0},{16,24},{24,16},{1,9},{9,1},{17,25},{25,17},{2,10},{10... | collective-permute-start | bytes 270344 | tf_op jit(solution)/shard_map/ppermute | solution.py:34
  64.7 1.3 %collective-permute-start.16 = (bf16[176,256]{1,0:T(8,128)(2,1)S(1)}, bf16[176,256]{1,0:T(8,128)(2,1)S(1)}, u32[]{:S(2)}, u32[]{:S(2)}) collective-permute-start(bf16[176,256]{1,0:T(8,128)(2,1)S(1)} %collective-permute-done.15.refs_2_), channel_id=1, source_target_pairs={{0,8},{8,0},{16,24},{24,16},{1,9},{9,1},{17,25},{25,17},{2,10},{10... | collective-permute-start | bytes 270344 | tf_op jit(solution)/shard_map/ppermute | solution.py:34

commit v9 on v8

--- a/solution.py
+++ b/solution.py
@@ -218,7 +218,7 @@
 
 
 def near_body(
-    f0_far, proj_far, t0_far, f1, t1, gain,
+    scale, bias, place, f0_far, proj_far, t0_far, f1, t1, gain,
     f0, proj, t0, normed, unit, factors, text_unit, token, projected, semaphores,
 ):
     rows = f0.shape[0]
@@ -515,11 +515,12 @@
         near_body,
         [half, kept, half, wide, wide, ((near, LANES), F32), wide, TOKEN],
         [((near, width), F32)],
+        smem=3,
         hbm=3,
         limit=36,
         flops=2 * near * width * width,
         moved=8 * near * width,
-    )(f0, proj, t0, f1, t1, gain_row)
+    )(scale, bias, place, f0, proj, t0, f1, t1, gain_row)
 
     t_after, f2_after, token = lax.optimization_barrier((t0, f2, token))
     t2 = send(t_after, "loop", lambda p: p ^ 2)

time: 68 us -> 62.3 us (0.916)
  local copies, waits for them, and re-layouts: 10.8 us -> 4.48 us
  waiting for transfers between devices: 8.95 us -> 10.5 us
    unnamed x28 -> x6, local copies, waits for them, and re-layouts: 10.1 us -> 3.77 us
    ppermute x17, waiting for transfers between devices: 8.95 us -> 10.5 us  [send(): return lax.ppermute(value, axis, [(p, target(p)) for p in range(count)])]
  transfers between devices with their start and end apart: 17 -> 17, of which waited for: 5 -> 6; matrix products, arithmetic and copies ran while one was open for 1% -> 1% of each run, Pallas kernels for 32% -> 34%
where the time goes in v9:
time: 62.3 us; the launch traced here: 62 us
  Pallas kernels  27.8 us (45%)
  starting transfers between devices  17.2 us (28%)
  waiting for transfers between devices  10.5 us (17%)
  local copies, waits for them, and re-layouts  4.48 us (7%)
  between operations  2.02 us (3%)
    pallas_call x10, Pallas kernels, run(): pl.pallas_call(body, out_shape=[jax.ShapeDtypeStruct(shape, kind) for sha...  27.8 us
    ppermute x17, starting transfers between devices, send(): return lax.ppermute(value, axis, [(p, target(p)) for p in range(count)])  17.2 us
    ppermute x17, waiting for transfers between devices, send(): return lax.ppermute(value, axis, [(p, target(p)) for p in range(count)])  10.5 us
    unnamed x6, local copies, waits for them, and re-layouts  3.77 us
  transfers between devices with their start and end apart: 17, of which 6 were waited for; matrix products, arithmetic and copies ran while one was open for 1% of the time, Pallas kernels for 34%

profile of v9, /device:TPU:0, one launch (start us, length us, event | category | flops | bytes accessed | tf_op | source)
XLA Modules:
  0.0 62.0 jit_solution(6078418351999078887)
XLA Ops:
  0.6 0.5 collective-permute-start
  1.1 0.1 collective-permute-start.1
  1.2 2.9 %collective-permute-start.2 = (bf16[192,1152]{1,0:T(8,128)(2,1)}, bf16[192,1152]{1,0:T(8,128)(2,1)S(1)}, u32[]{:S(2)}, u32[]{:S(2)}) collective-permute-start(bf16[192,1152]{1,0:T(8,128)(2,1)} %bitcast.7), channel_id=1, source_target_pairs={{0,16},{8,24},{16,0},{24,8},{1,17},{9,25},{17,1},{25,9},{2,18},{10... | collective-permute-start | bytes 1327112 | tf_op jit(solution)/shard_map/ppermute | solution.py:34
  5.4 0.7 %reshape.11.gain = f32[1,1152]{1,0:T(1,128)S(1)} reshape(f32[1152]{0:T(1024)} %param.9) | data formatting | bytes 9216 | tf_op jit(solution)/shard_map/reshape | solution.py:498
  6.1 0.1 pad_add_fusion.place
  6.2 0.0 collective-permute-done.f1
  6.2 0.0 collective-permute-done.1.t1
  6.2 1.7 %copy-done = bf16[1152,1152]{1,0:T(8,128)(2,1)S(1)} copy-done((bf16[1152,1152]{1,0:T(8,128)(2,1)S(1)}, bf16[1152,1152]{1,0:T(8,128)(2,1)}, u32[]{:S(2)}) %copy-start) | copy-done | bytes 2654232
  8.0 1.0 %copy-done.1 = bf16[192,1,1152]{2,0,1:T(8,128)(2,1)S(1)} copy-done((bf16[192,1,1152]{2,0,1:T(8,128)(2,1)S(1)}, bf16[192,1,1152]{2,0,1:T(8,128)(2,1)}, u32[]{:S(2)}) %copy-start.1) | copy-done | bytes 442392
  9.0 1.0 %copy-done.2 = bf16[192,1,1152]{2,0,1:T(8,128)(2,1)S(1)} copy-done((bf16[192,1,1152]{2,0,1:T(8,128)(2,1)S(1)}, bf16[192,1,1152]{2,0,1:T(8,128)(2,1)}, u32[]{:S(2)}) %copy-start.2) | copy-done | bytes 442392
  10.0 5.2 %shard_map.93 = (bf16[192,1152]{1,0:T(8,128)(2,1)S(1)}, bf16[1152,1152]{1,0:T(8,128)(2,1)S(1)}, bf16[192,1152]{1,0:T(8,128)(2,1)S(1)}, bf16[384,1152]{1,0:T(8,12...) custom-call(f32[1]{0:T(128)S(6)} %copy.10.scale, ...), custom_call_target="tpu_custom_call" | custom-call | flops 1019215872 | bytes 3538944 | tf_op jit(solution)/shard_map/pallas_call | solution.py:138
  15.2 0.0 collective-permute-done.2.f2
  15.2 0.1 collective-permute-start.4
  15.3 1.3 %collective-permute-start.3 = (bf16[192,1152]{1,0:T(8,128)(2,1)S(1)}, bf16[192,1152]{1,0:T(8,128)(2,1)S(1)}, u32[]{:S(2)}, u32[]{:S(2)}) collective-permute-start(bf16[192,1152]{1,0:T(8,128)(2,1)S(1)} %bitcast.11), channel_id=1, source_target_pairs={{0,16},{8,24},{16,0},{24,8},{1,17},{9,25},{17,1},{25,9},{2,18},{10... | collective-permute-start | bytes 1327112 | tf_op jit(solution)/shard_map/ppermute | solution.py:34
  16.5 2.2 %shard_map.94 = (bf16[1152,384]{1,0:T(8,128)(2,1)S(1)}, bf16[288,384]{1,0:T(8,128)(2,1)S(1)}, f32[1,384]{1,0:T(1,128)S(1)}, bf16[384,288]{1,0:T(8,128)(2,1)S(1)}...) custom-call(f32[1]{0:T(128)S(6)} %copy.10.scale, f32[1]{0:T(128)S(6)} %copy.11.bias, ...), custom_call_target="tpu_custom_call" | custom-call | flops 509607936 | bytes 3538944 | tf_op jit(solution)/shard_map/pallas_call | solution.py:138
  18.7 0.0 collective-permute-done.4.f3
  18.7 5.8 %shard_map.95 = (bf16[1152,384]{1,0:T(8,128)(2,1)S(1)}, bf16[384,1152]{1,0:T(8,128)(2,1)S(1)}, bf16[288,384]{1,0:T(8,128)(2,1)S(1)}, f32[1,384]{1,0:T(1,128)S(1)...) custom-call(f32[1]{0:T(128)S(6)} %copy.10.scale, f32[1]{0:T(128)S(6)} %copy.11.bias, ...), custom_call_target="tpu_custom_call" | custom-call | flops 1528823808 | bytes 3538944 | tf_op jit(solution)/shard_map/pallas_call | solution.py:138
  24.6 2.0 %shard_map.96 = (bf16[192,1152]{1,0:T(8,128)(2,1)}, f32[8,128]{1,0:T(8,128)S(1)}) custom-call(f32[1]{0:T(128)S(6)} %copy.10.scale, bf16[192,1152]{1,0:T(8,128)(2,1)S(1)} %get-tuple-element.71.text, bf16[384,384]{1,0:T(8,128)(2,1)S(1)} %get-tuple-element.67.weights_near, bf16[384,384]{1,0:T(8,128)(2,1)S(1)} %get-tuple-element.68.weights_far, ...), custom_call_target="tpu_custom_call" | custom-call | flops 1019215872 | bytes 2654208 | tf_op jit(solution)/shard_map/pallas_call | solution.py:138
  26.5 1.3 %collective-permute-done.3.t2 = bf16[192,1152]{1,0:T(8,128)(2,1)S(1)} collective-permute-done((bf16[192,1152]{1,0:T(8,128)(2,1)S(1)}, bf16[192,1152]{1,0:T(8,128)(2,1)S(1)}, u32[]{:S(2)}, u32[]{:S(2)}) %collective-permute-start.3) | collective-permute-done | bytes 442400 | tf_op jit(solution)/shard_map/ppermute | solution.py:34
  27.8 0.0 collective-permute-start.5
  27.8 2.6 %shard_map.97 = (bf16[192,1152]{1,0:T(8,128)(2,1)S(1)}, bf16[192,768]{1,0:T(8,128)(2,1)S(1)}, f32[288,384]{1,0:T(8,128)S(1)}, f32[288,384]{1,0:T(8,128)S(1)}, f32[1,768]{1,0:T(1,128)S(1)}) custom-call(f32[1]{0:T(128)S(6)} %copy.10.scale, f32[1]{0:T(128)S(6)} %copy.11.bias, s32[2]{0:T(128)S(1)} %pad_add_fusion.place, ...), custom_call_target="tpu_custom_call" | custom-call | flops 1019215872 | bytes 3538944 | tf_op jit(solution)/shard_map/pallas_call | solution.py:138
  30.4 0.0 collective-permute-done.5.t3
  30.4 4.1 %shard_map.98 = (bf16[4,128,256]{2,1,0:T(8,128)(2,1)S(1)}, bf16[4,128,256]{2,1,0:T(8,128)(2,1)S(1)}, bf16[2,48,256]{2,1,0:T(8,128)(2,1)S(1)}, bf16[2,48,256]{2,1...) custom-call(f32[1]{0:T(128)S(6)} %copy.10.scale, ...), custom_call_target="tpu_custom_call" | custom-call | flops 2038431744 | bytes 7077888 | tf_op jit(solution)/shard_map/pallas_call | solution.py:138
  34.5 1.6 %collective-permute-start.6 = (bf16[4,128,256]{2,1,0:T(8,128)(2,1)S(1)}, bf16[4,128,256]{2,1,0:T(8,128)(2,1)S(1)}, u32[]{:S(2)}, u32[]{:S(2)}) collective-permute-start(bf16[4,128,256]{2,1,0:T(8,128)(2,1)S(1)} %get-tuple-element.93), channel_id=1, source_target_pairs={{0,1},{1,0},{2,3},{3,2},{4,5},{5,4},{6,7},{7,6},{8,9},{9,8},{10,11... | collective-permute-start | bytes 786440 | tf_op jit(solution)/shard_map/ppermute | solution.py:34
  36.1 3.6 %collective-permute-start.7 = (bf16[2,48,256]{2,1,0:T(8,128)(2,1)S(1)}, bf16[2,48,256]{2,1,0:T(8,128)(2,1)S(1)}, u32[]{:S(2)}, u32[]{:S(2)}) collective-permute-start(bf16[2,48,256]{2,1,0:T(8,128)(2,1)S(1)} %get-tuple-element.95), channel_id=1, source_target_pairs={{0,6},{1,7},{2,4},{3,5},{4,2},{5,3},{6,0},{7,1},{8,14},{9,15},{10,... | collective-permute-start | bytes 147464 | tf_op jit(solution)/shard_map/ppermute | solution.py:34
  39.7 0.0 collective-permute-start.8
  39.7 0.8 %collective-permute-start.9 = (bf16[2,48,256]{2,1,0:T(8,128)(2,1)S(1)}, bf16[2,48,256]{2,1,0:T(8,128)(2,1)S(1)}, u32[]{:S(2)}, u32[]{:S(2)}) collective-permute-start(bf16[2,48,256]{2,1,0:T(8,128)(2,1)S(1)} %get-tuple-element.97), channel_id=1, source_target_pairs={{0,2},{1,3},{2,0},{3,1},{4,6},{5,7},{6,4},{7,5},{8,10},{9,11},{10,... | collective-permute-start | bytes 147464 | tf_op jit(solution)/shard_map/ppermute | solution.py:34
  40.5 3.6 %shard_map.99 = (bf16[192,1152]{1,0:T(8,128)(2,1)}, f32[8,128]{1,0:T(8,128)S(1)}) custom-call(f32[1]{0:T(128)S(6)} %copy.10.scale, bf16[192,1152]{1,0:T(8,128)(2,1)S(1)} %get-tuple-element.55.features, bf16[1152,1152]{1,0:T(8,128)(2,1)S(1)} %get-tuple-element.56.proj, f32[1,1152]{1,0:T(1,128)S(1)} %reshape.11.gain, ...), custom_call_target="tpu_custom_call" | custom-call | flops 2038431744 | bytes 5308416 | tf_op jit(solution)/shard_map/pallas_call | solution.py:138
  44.1 0.0 collective-permute-done.7.refs_0_
  44.1 0.7 %collective-permute-done.8.refs_1_ = bf16[2,48,256]{2,1,0:T(8,128)(2,1)S(1)} collective-permute-done((bf16[2,48,256]{2,1,0:T(8,128)(2,1)S(1)}, bf16[2,48,256]{2,1,0:T(8,128)(2,1)S(1)}, u32[]{:S(2)}, u32[]{:S(2)}) %collective-permute-start.8) | collective-permute-done | bytes 49184 | tf_op jit(solution)/shard_map/ppermute | solution.py:34
  44.9 0.0 collective-permute-done.9.refs_2_
  44.9 0.0 collective-permute-done.6.across
  44.9 0.6 %shard_map.100 = (bf16[128,256]{1,0:T(8,128)(2,1)S(1)}, bf16[128,256]{1,0:T(8,128)(2,1)S(1)}, bf16[128,256]{1,0:T(8,128)(2,1)S(1)}, bf16[128,256]{1,0:T(8,128)(2...) custom-call(s32[2]{0:T(128)S(1)} %pad_add_fusion.place, f32[8,128]{1,0:T(8,128)S(1)} %get-tuple-element.91.token, ...), custom_call_target="tpu_custom_call" | custom-call | bytes 663552 | tf_op jit(solution)/shard_map/pallas_call | solution.py:138
  45.5 3.0 %collective-permute-start.11 = (bf16[128,256]{1,0:T(8,128)(2,1)S(1)}, bf16[128,256]{1,0:T(8,128)(2,1)S(1)}, u32[]{:S(2)}, u32[]{:S(2)}) collective-permute-start(bf16[128,256]{1,0:T(8,128)(2,1)S(1)} %get-tuple-element.101), channel_id=1, source_target_pairs={{0,6},{1,7},{2,4},{3,5},{4,2},{5,3},{6,0},{7,1},{8,14},{9,15},{10,... | collective-permute-start | bytes 196616 | tf_op jit(solution)/shard_map/ppermute | solution.py:34
  48.5 0.0 collective-permute-start.12
  48.5 1.5 %collective-permute-start.13 = (bf16[128,256]{1,0:T(8,128)(2,1)S(1)}, bf16[128,256]{1,0:T(8,128)(2,1)S(1)}, u32[]{:S(2)}, u32[]{:S(2)}) collective-permute-start(bf16[128,256]{1,0:T(8,128)(2,1)S(1)} %get-tuple-element.103), channel_id=1, source_target_pairs={{0,2},{1,3},{2,0},{3,1},{4,6},{5,7},{6,4},{7,5},{8,10},{9,11},{10,... | collective-permute-start | bytes 196616 | tf_op jit(solution)/shard_map/ppermute | solution.py:34
  50.0 0.5 collective-permute-start.10
  50.5 3.3 %collective-permute-done.10.tail_across = bf16[48,256]{1,0:T(8,128)(2,1)S(1)} collective-permute-done((bf16[48,256]{1,0:T(8,128)(2,1)S(1)}, bf16[48,256]{1,0:T(8,128)(2,1)S(1)}, u32[]{:S(2)}, u32[]{:S(2)}) %collective-permute-start.10) | collective-permute-done | bytes 24608 | tf_op jit(solution)/shard_map/ppermute | solution.py:34
  53.8 0.0 collective-permute-done.11.refs_1_
  53.8 0.6 %collective-permute-done.12.refs_2_ = bf16[128,256]{1,0:T(8,128)(2,1)S(1)} collective-permute-done((bf16[128,256]{1,0:T(8,128)(2,1)S(1)}, bf16[128,256]{1,0:T(8,128)(2,1)S(1)}, u32[]{:S(2)}, u32[]{:S(2)}) %collective-permute-start.12) | collective-permute-done | bytes 65568 | tf_op jit(solution)/shard_map/ppermute | solution.py:34
  54.4 0.0 collective-permute-done.13.refs_3_
  54.5 1.4 %collective-permute-start.15 = (bf16[176,256]{1,0:T(8,128)(2,1)S(1)}, bf16[176,256]{1,0:T(8,128)(2,1)S(1)}, u32[]{:S(2)}, u32[]{:S(2)}) collective-permute-start(bf16[176,256]{1,0:T(8,128)(2,1)S(1)} %shard_map.101.refs_0_), channel_id=1, source_target_pairs={{0,16},{8,24},{16,0},{24,8},{1,17},{9,25},{17,1},{25,9},{2,18},{10... | collective-permute-start | bytes 270344 | tf_op jit(solution)/shard_map/ppermute | solution.py:34
  55.9 0.0 collective-permute-start.14
  55.9 3.2 %collective-permute-done.15.refs_2_ = bf16[176,256]{1,0:T(8,128)(2,1)S(1)} collective-permute-done((bf16[176,256]{1,0:T(8,128)(2,1)S(1)}, bf16[176,256]{1,0:T(8,128)(2,1)S(1)}, u32[]{:S(2)}, u32[]{:S(2)}) %collective-permute-start.15) | collective-permute-done | bytes 90144 | tf_op jit(solution)/shard_map/ppermute | solution.py:34
  59.1 0.0 collective-permute-start.16
  59.1 0.0 collective-permute-done.14.refs_1_
  59.1 1.3 %collective-permute-done.16.refs_3_ = bf16[176,256]{1,0:T(8,128)(2,1)S(1)} collective-permute-done((bf16[176,256]{1,0:T(8,128)(2,1)S(1)}, bf16[176,256]{1,0:T(8,128)(2,1)S(1)}, u32[]{:S(2)}, u32[]{:S(2)}) %collective-permute-start.16) | collective-permute-done | bytes 90144 | tf_op jit(solution)/shard_map/ppermute | solution.py:34
  60.4 1.7 %shard_map.102 = (f32[144,1152]{1,0:T(8,128)}, f32[1152]{0:T(1024)}) custom-call(s32[2]{0:T(128)S(1)} %pad_add_fusion.place, bf16[176,256]{1,0:T(8,128)(2,1)S(1)} %shard_map.101.refs_0_, bf16[176,256]{1,0:T(8,128)(2,1)S(1)} %collective-permute-done.14.refs_1_, bf16[176,256]{1,0:T(8,128)(2,1)S(1)} %collective-permute-done.15.refs_2_, ...), custom_call_target="tpu_custom_call" | custom-call | bytes 1327104 | tf_op jit(solution)/shard_map/pallas_call | solution.py:138
  (4 shorter events, 0.0 us)
Async XLA Ops:
  0.6 5.6 %collective-permute-start = (bf16[192,1152]{1,0:T(8,128)(2,1)}, bf16[192,1152]{1,0:T(8,128)(2,1)S(1)}, u32[]{:S(2)}, u32[]{:S(2)}) collective-permute-start(bf16[192,1152]{1,0:T(8,128)(2,1)} %bitcast.6), channel_id=1, source_target_pairs={{0,8},{8,0},{16,24},{24,16},{1,9},{9,1},{17,25},{25,17},{2,10},{10... | collective-permute-start | bytes 1327112 | tf_op jit(solution)/shard_map/ppermute | solution.py:34
  1.1 5.1 %collective-permute-start.1 = (bf16[192,1152]{1,0:T(8,128)(2,1)}, bf16[192,1152]{1,0:T(8,128)(2,1)S(1)}, u32[]{:S(2)}, u32[]{:S(2)}) collective-permute-start(bf16[192,1152]{1,0:T(8,128)(2,1)} %bitcast.9), channel_id=1, source_target_pairs={{0,8},{8,0},{16,24},{24,16},{1,9},{9,1},{17,25},{25,17},{2,10},{10... | collective-permute-start | bytes 1327112 | tf_op jit(solution)/shard_map/ppermute | solution.py:34
  1.2 13.9 %collective-permute-start.2 = (bf16[192,1152]{1,0:T(8,128)(2,1)}, bf16[192,1152]{1,0:T(8,128)(2,1)S(1)}, u32[]{:S(2)}, u32[]{:S(2)}) collective-permute-start(bf16[192,1152]{1,0:T(8,128)(2,1)} %bitcast.7), channel_id=1, source_target_pairs={{0,16},{8,24},{16,0},{24,8},{1,17},{9,25},{17,1},{25,9},{2,18},{10... | collective-permute-start | bytes 1327112 | tf_op jit(solution)/shard_map/ppermute | solution.py:34
  6.2 1.8 %copy-start = (bf16[1152,1152]{1,0:T(8,128)(2,1)S(1)}, bf16[1152,1152]{1,0:T(8,128)(2,1)}, u32[]{:S(2)}) copy-start(bf16[1152,1152]{1,0:T(8,128)(2,1)} %proj_far.1) | copy-start | bytes 7962628
  8.0 1.0 %copy-start.1 = (bf16[192,1,1152]{2,0,1:T(8,128)(2,1)S(1)}, bf16[192,1,1152]{2,0,1:T(8,128)(2,1)}, u32[]{:S(2)}) copy-start(bf16[192,1,1152]{2,0,1:T(8,128)(2,1)} %param.6) | copy-start | bytes 1327108
  9.0 1.0 %copy-start.2 = (bf16[192,1,1152]{2,0,1:T(8,128)(2,1)S(1)}, bf16[192,1,1152]{2,0,1:T(8,128)(2,1)}, u32[]{:S(2)}) copy-start(bf16[192,1,1152]{2,0,1:T(8,128)(2,1)} %param.7) | copy-start | bytes 1327108
  15.2 3.5 %collective-permute-start.4 = (bf16[192,1152]{1,0:T(8,128)(2,1)S(1)}, bf16[192,1152]{1,0:T(8,128)(2,1)S(1)}, u32[]{:S(2)}, u32[]{:S(2)}) collective-permute-start(bf16[192,1152]{1,0:T(8,128)(2,1)S(1)} %collective-permute-done.2.f2), channel_id=1, source_target_pairs={{0,8},{8,0},{16,24},{24,16},{1,9},{9,1},{17,25},{25,17},{2,10},{10... | collective-permute-start | bytes 1327112 | tf_op jit(solution)/shard_map/ppermute | solution.py:34
  15.3 12.6 %collective-permute-start.3 = (bf16[192,1152]{1,0:T(8,128)(2,1)S(1)}, bf16[192,1152]{1,0:T(8,128)(2,1)S(1)}, u32[]{:S(2)}, u32[]{:S(2)}) collective-permute-start(bf16[192,1152]{1,0:T(8,128)(2,1)S(1)} %bitcast.11), channel_id=1, source_target_pairs={{0,16},{8,24},{16,0},{24,8},{1,17},{9,25},{17,1},{25,9},{2,18},{10... | collective-permute-start | bytes 1327112 | tf_op jit(solution)/shard_map/ppermute | solution.py:34
  27.8 2.6 %collective-permute-start.5 = (bf16[192,1152]{1,0:T(8,128)(2,1)S(1)}, bf16[192,1152]{1,0:T(8,128)(2,1)S(1)}, u32[]{:S(2)}, u32[]{:S(2)}) collective-permute-start(bf16[192,1152]{1,0:T(8,128)(2,1)S(1)} %collective-permute-done.3.t2), channel_id=1, source_target_pairs={{0,8},{8,0},{16,24},{24,16},{1,9},{9,1},{17,25},{25,17},{2,10},{10... | collective-permute-start | bytes 1327112 | tf_op jit(solution)/shard_map/ppermute | solution.py:34
  34.5 10.3 %collective-permute-start.6 = (bf16[4,128,256]{2,1,0:T(8,128)(2,1)S(1)}, bf16[4,128,256]{2,1,0:T(8,128)(2,1)S(1)}, u32[]{:S(2)}, u32[]{:S(2)}) collective-permute-start(bf16[4,128,256]{2,1,0:T(8,128)(2,1)S(1)} %get-tuple-element.93), channel_id=1, source_target_pairs={{0,1},{1,0},{2,3},{3,2},{4,5},{5,4},{6,7},{7,6},{8,9},{9,8},{10,11... | collective-permute-start | bytes 786440 | tf_op jit(solution)/shard_map/ppermute | solution.py:34
  36.1 8.0 %collective-permute-start.7 = (bf16[2,48,256]{2,1,0:T(8,128)(2,1)S(1)}, bf16[2,48,256]{2,1,0:T(8,128)(2,1)S(1)}, u32[]{:S(2)}, u32[]{:S(2)}) collective-permute-start(bf16[2,48,256]{2,1,0:T(8,128)(2,1)S(1)} %get-tuple-element.95), channel_id=1, source_target_pairs={{0,6},{1,7},{2,4},{3,5},{4,2},{5,3},{6,0},{7,1},{8,14},{9,15},{10,... | collective-permute-start | bytes 147464 | tf_op jit(solution)/shard_map/ppermute | solution.py:34
  39.7 5.1 %collective-permute-start.8 = (bf16[2,48,256]{2,1,0:T(8,128)(2,1)S(1)}, bf16[2,48,256]{2,1,0:T(8,128)(2,1)S(1)}, u32[]{:S(2)}, u32[]{:S(2)}) collective-permute-start(bf16[2,48,256]{2,1,0:T(8,128)(2,1)S(1)} %get-tuple-element.96), channel_id=1, source_target_pairs={{0,4},{1,5},{2,6},{3,7},{4,0},{5,1},{6,2},{7,3},{8,12},{9,13},{10,... | collective-permute-start | bytes 147464 | tf_op jit(solution)/shard_map/ppermute | solution.py:34
  39.7 5.1 %collective-permute-start.9 = (bf16[2,48,256]{2,1,0:T(8,128)(2,1)S(1)}, bf16[2,48,256]{2,1,0:T(8,128)(2,1)S(1)}, u32[]{:S(2)}, u32[]{:S(2)}) collective-permute-start(bf16[2,48,256]{2,1,0:T(8,128)(2,1)S(1)} %get-tuple-element.97), channel_id=1, source_target_pairs={{0,2},{1,3},{2,0},{3,1},{4,6},{5,7},{6,4},{7,5},{8,10},{9,11},{10,... | collective-permute-start | bytes 147464 | tf_op jit(solution)/shard_map/ppermute | solution.py:34
  45.5 8.3 %collective-permute-start.11 = (bf16[128,256]{1,0:T(8,128)(2,1)S(1)}, bf16[128,256]{1,0:T(8,128)(2,1)S(1)}, u32[]{:S(2)}, u32[]{:S(2)}) collective-permute-start(bf16[128,256]{1,0:T(8,128)(2,1)S(1)} %get-tuple-element.101), channel_id=1, source_target_pairs={{0,6},{1,7},{2,4},{3,5},{4,2},{5,3},{6,0},{7,1},{8,14},{9,15},{10,... | collective-permute-start | bytes 196616 | tf_op jit(solution)/shard_map/ppermute | solution.py:34
  48.5 5.9 %collective-permute-start.12 = (bf16[128,256]{1,0:T(8,128)(2,1)S(1)}, bf16[128,256]{1,0:T(8,128)(2,1)S(1)}, u32[]{:S(2)}, u32[]{:S(2)}) collective-permute-start(bf16[128,256]{1,0:T(8,128)(2,1)S(1)} %get-tuple-element.102), channel_id=1, source_target_pairs={{0,4},{1,5},{2,6},{3,7},{4,0},{5,1},{6,2},{7,3},{8,12},{9,13},{10,... | collective-permute-start | bytes 196616 | tf_op jit(solution)/shard_map/ppermute | solution.py:34
  48.5 5.9 %collective-permute-start.13 = (bf16[128,256]{1,0:T(8,128)(2,1)S(1)}, bf16[128,256]{1,0:T(8,128)(2,1)S(1)}, u32[]{:S(2)}, u32[]{:S(2)}) collective-permute-start(bf16[128,256]{1,0:T(8,128)(2,1)S(1)} %get-tuple-element.103), channel_id=1, source_target_pairs={{0,2},{1,3},{2,0},{3,1},{4,6},{5,7},{6,4},{7,5},{8,10},{9,11},{10,... | collective-permute-start | bytes 196616 | tf_op jit(solution)/shard_map/ppermute | solution.py:34
  50.0 3.8 %collective-permute-start.10 = (bf16[48,256]{1,0:T(8,128)(2,1)S(1)}, bf16[48,256]{1,0:T(8,128)(2,1)S(1)}, u32[]{:S(2)}, u32[]{:S(2)}) collective-permute-start(bf16[48,256]{1,0:T(8,128)(2,1)S(1)} %get-tuple-element.99), channel_id=1, source_target_pairs={{0,1},{1,0},{2,3},{3,2},{4,5},{5,4},{6,7},{7,6},{8,9},{9,8},{10,11... | collective-permute-start | bytes 73736 | tf_op jit(solution)/shard_map/ppermute | solution.py:34
  54.5 4.6 %collective-permute-start.15 = (bf16[176,256]{1,0:T(8,128)(2,1)S(1)}, bf16[176,256]{1,0:T(8,128)(2,1)S(1)}, u32[]{:S(2)}, u32[]{:S(2)}) collective-permute-start(bf16[176,256]{1,0:T(8,128)(2,1)S(1)} %shard_map.101.refs_0_), channel_id=1, source_target_pairs={{0,16},{8,24},{16,0},{24,8},{1,17},{9,25},{17,1},{25,9},{2,18},{10... | collective-permute-start | bytes 270344 | tf_op jit(solution)/shard_map/ppermute | solution.py:34
  55.9 3.2 %collective-permute-start.14 = (bf16[176,256]{1,0:T(8,128)(2,1)S(1)}, bf16[176,256]{1,0:T(8,128)(2,1)S(1)}, u32[]{:S(2)}, u32[]{:S(2)}) collective-permute-start(bf16[176,256]{1,0:T(8,128)(2,1)S(1)} %shard_map.101.refs_0_), channel_id=1, source_target_pairs={{0,8},{8,0},{16,24},{24,16},{1,9},{9,1},{17,25},{25,17},{2,10},{10... | collective-permute-start | bytes 270344 | tf_op jit(solution)/shard_map/ppermute | solution.py:34
  59.1 1.3 %collective-permute-start.16 = (bf16[176,256]{1,0:T(8,128)(2,1)S(1)}, bf16[176,256]{1,0:T(8,128)(2,1)S(1)}, u32[]{:S(2)}, u32[]{:S(2)}) collective-permute-start(bf16[176,256]{1,0:T(8,128)(2,1)S(1)} %collective-permute-done.15.refs_2_), channel_id=1, source_target_pairs={{0,8},{8,0},{16,24},{24,16},{1,9},{9,1},{17,25},{25,17},{2,10},{10... | collective-permute-start | bytes 270344 | tf_op jit(solution)/shard_map/ppermute | solution.py:34

commit v10 on v9

--- a/solution.py
+++ b/solution.py
@@ -209,12 +209,15 @@
 
 
 def take_columns(place, source, target):
-    columns = target.shape[1]
-    for member in range(source.shape[1] // columns):
+    members = source.shape[1] // target.shape[1]
+    full = target.shape[1] // LANES * LANES
+    rest = target.shape[1] - full
+    target[:, :full] = source[:, pl.ds(pl.multiple_of(place[0] * full, LANES), full)]
+    for member in range(members):
 
         @pl.when(place[0] == member)
         def _():
-            target[...] = source[:, member * columns : (member + 1) * columns]
+            target[:, full:] = source[:, members * full + member * rest : members * full + (member + 1) * rest]
 
 
 def near_body(
@@ -254,8 +257,12 @@
 
 def turn_own(place, unit, factors, turned, unit_turned, inverse):
     columns = unit_turned.shape[0]
+    full = columns // LANES * LANES
+    rest = columns - full
     turned[...] = unit[...].T
-    unit_turned[...] = turned[pl.ds(pl.multiple_of(place[0] * columns, BAND), columns), :]
+    unit_turned[:full, :] = turned[pl.ds(pl.multiple_of(place[0] * full, LANES), full), :]
+    begin = turned.shape[0] // columns * full
+    unit_turned[full:, :] = turned[pl.ds(pl.multiple_of(begin + place[0] * rest, BAND), rest), :]
     inverse[...] = factors[...].T[:1, :]
 
 
@@ -315,11 +322,9 @@
 
 def partial_body(
     members, groups, lead, scale, bias, place, t3, unit_near, unit_far, totals, back_near, back_far, unit_turned_near,
-    unit_turned_far, inverse_near, inverse_far, turned_near, turned_far, proj_columns, gain, *refs,
+    unit_turned_far, inverse_near, inverse_far, turned_near, turned_far, proj_columns, gain,
+    send_lead, keep_lead, send_tail, keep_tail, text_unit, weights, text_columns, dots, packed,
 ):
-    (across, keep_lead, keep_tail), refs = refs[:3], refs[3:]
-    along, refs = refs[: groups // 2 - 1], refs[groups // 2 - 1 :]
-    text_unit, weights, text_columns, dots, packed = refs
     rows = t3.shape[0]
     near = 2 * rows
     every = members * rows
@@ -332,15 +337,17 @@
     dots[:, :near] = dot(text_unit[...], unit_near[...], LAST)
     dots[:, near:] = dot(text_unit[...], unit_far[...], LAST)
     total = totals[...] + weigh(dots, scale, bias, near + rows, weights)
-    product = None
-    for where, earlier, unit_turned, inverse, turned in (
-        (slice(0, near), back_near, unit_turned_near, inverse_near, turned_near),
-        (slice(near, every), back_far, unit_turned_far, inverse_far, turned_far),
+    added = dot(text_columns[...], weights[...], FIRST)
+    back = []
+    for where, earlier, unit_turned, inverse in (
+        (slice(0, near), back_near, unit_turned_near, inverse_near),
+        (slice(near, every), back_far, unit_turned_far, inverse_far),
     ):
-        whole = earlier[...] + dot(text_columns[...], weights[:, where], FIRST)
-        back = (whole - unit_turned[...].astype(F32) * total[:, where]) * (inverse[...] * scale)
-        part = dot(turned[...], back.astype(BF16), LAST)
-        product = part if product is None else product + part
+        whole = earlier[...] + added[:, where]
+        part = (whole - unit_turned[...].astype(F32) * total[:, where]) * (inverse[...] * scale)
+        back.append(part.astype(BF16))
+    turned = jnp.concatenate([turned_near[...], turned_far[...]], axis=1)
+    product = dot(turned, jnp.concatenate(back, axis=1), LAST)
     each = width // groups
     product = product * (1.0 / every)
     for group in range(groups):
@@ -361,13 +368,12 @@
         packed[group, count - BAND :, full - LANES :] = gain_tile
 
     own = place[1]
-    for step in range(groups // 2):
-        across[step] = packed[own ^ 1 ^ (2 * step), :lead, :]
-        keep_lead[step] = packed[own ^ (2 * step), :lead, :]
-    for other in range(2):
-        keep_tail[other] = packed[own ^ other, lead:, :]
-        for step in range(1, groups // 2):
-            along[step - 1][other] = packed[own ^ (2 * step) ^ other, lead:, :]
+    for at in range(4):
+        send_lead[at] = packed[own ^ 1 ^ (2 * at), :lead, :]
+        keep_lead[at] = packed[own ^ (2 * at), :lead, :]
+        other = (at % 2) + 4 * (at // 2)
+        send_tail[at] = packed[own ^ 2 ^ other, lead:, :]
+        keep_tail[at] = packed[own ^ other, lead:, :]
 
 
 def image_body(
@@ -425,61 +431,47 @@
     token[...] = jnp.zeros_like(token)
 
 
-def first_sum_body(place, token, keep_lead, across, keep_tail, *refs):
-    steps = keep_lead.shape[0]
-    along, refs = refs[: steps - 1], refs[steps - 1 :]
-    leads, (tail, tail_across, ordered) = refs[:steps], refs[steps:]
-    for step in range(steps):
-        leads[step][...] = (keep_lead[step].astype(F32) + across[step].astype(F32)).astype(BF16)
-    own = place[1] // 2
-    ordered[own] = keep_tail[...]
-    for step in range(1, steps):
-        ordered[own ^ step] = along[steps - 1 - step][...]
-    value = ordered[0].astype(F32)
-    for step in range(1, steps):
-        value = value + ordered[step].astype(F32)
-    tail[...] = value[0].astype(BF16)
-    tail_across[...] = value[1].astype(BF16)
-
-
-def last_sum_body(tail, tail_across, *refs):
-    leads, total = refs[:-1], refs[-1]
-    split = leads[0].shape[0]
-    value = leads[0][...].astype(F32)
-    for lead in leads[1:]:
-        value = value + lead[...].astype(F32)
-    total[:split, :] = value.astype(BF16)
-    total[split:, :] = (tail[...].astype(F32) + tail_across[...].astype(F32)).astype(BF16)
+def halve_body(before, kept_lead, come_lead, kept_tail, come_tail, send_lead, keep_lead, send_tail, keep_tail):
+    for kept, come, send_next, keep in (
+        (kept_lead, come_lead, send_lead, keep_lead),
+        (kept_tail, come_tail, send_tail, keep_tail),
+    ):
+        for at in range(2):
+            keep[at] = (kept[2 * at].astype(F32) + come[2 * at].astype(F32)).astype(BF16)
+            send_next[at] = (kept[2 * at + 1].astype(F32) + come[2 * at + 1].astype(F32)).astype(BF16)
+
+
+def quarter_body(kept_lead, come_lead, kept_tail, come_tail, send_next, keep):
+    lead = kept_lead.shape[1]
+    for target, at in ((keep, 0), (send_next, 1)):
+        target[:lead, :] = (kept_lead[at].astype(F32) + come_lead[at].astype(F32)).astype(BF16)
+        target[lead:, :] = (kept_tail[at].astype(F32) + come_tail[at].astype(F32)).astype(BF16)
+
+
+def last_sum_body(kept, come, total):
+    total[...] = (kept[...].astype(F32) + come[...].astype(F32)).astype(BF16)
 
 
 def finish_body(members, place, *refs):
     packets, (proj_grad, gain_gradient, ordered) = refs[:members], refs[members:]
     count, full = packets[0].shape
     rows, width = proj_grad.shape
-    columns = width // members
-    rest = columns - full
+    rest = width // members - full
     per_band = full // rest
-    for own in range(members):
-
-        @pl.when(place[0] == own)
-        def _():
-            for k in range(members):
-                base = (own ^ k) * columns
-                packet = packets[k]
-                main = packet[:rows, :].astype(F32)
-                tails = []
-                for index in range(rows // BAND):
-                    at = rows + (index // per_band) * BAND
-                    lane = (index % per_band) * rest
-                    tails.append(packet[at : at + BAND, lane : lane + rest].astype(F32))
-                proj_grad[:, base : base + full] = main
-                proj_grad[:, base + full : base + columns] = jnp.concatenate(tails, axis=0)
-
     for k in range(members):
-        ordered[place[0] ^ k] = packets[k][count - BAND :, full - LANES :].astype(F32)
-    value = ordered[0]
+        member = place[0] ^ k
+        proj_grad[:, pl.ds(pl.multiple_of(member * full, LANES), full)] = packets[k][:rows, :].astype(F32)
+        ordered[member] = packets[k][rows:, :].astype(F32)
+    tails = []
+    for index in range(rows // BAND):
+        at, lane = (index // per_band) * BAND, (index % per_band) * rest
+        tails.append(
+            jnp.concatenate([ordered[member][at : at + BAND, lane : lane + rest] for member in range(members)], axis=1)
+        )
+    proj_grad[:, members * full :] = jnp.concatenate(tails, axis=0)
+    value = ordered[0][count - rows - BAND :, full - LANES :]
     for member in range(1, members):
-        value = value + ordered[member]
+        value = value + ordered[member][count - rows - BAND :, full - LANES :]
     for at in range(width // LANES):
         gain_gradient[at * LANES : (at + 1) * LANES] = value[at]
 
@@ -497,9 +489,8 @@
     packet = (each + bands * BAND, full)
     gain_row = gain.reshape(1, width)
 
-    lead = (3 * packet[0] // BAND // 4) * BAND
+    lead = (2 * packet[0] // BAND // 3) * BAND
     tail = packet[0] - lead
-    steps = groups // 2
 
     f0, t0 = features[:, 0, :], text[:, 0, :]
     f2 = send(f0, "loop", lambda p: p ^ 2)
@@ -573,7 +564,7 @@
 
     outs = call(
         functools.partial(partial_body, members, groups, lead),
-        [((steps, lead, full), BF16), ((steps, lead, full), BF16)] + [((2, tail, full), BF16)] * steps + [half, narrow],
+        [((4, lead, full), BF16)] * 2 + [((4, tail, full), BF16)] * 2 + [half, narrow],
         [((rows, columns), BF16), ((rows, every), F32), ((groups,) + packet, BF16)],
         smem=3,
         flops=4 * near * width * width,
@@ -582,11 +573,9 @@
         scale, bias, place, t3, unit_near, unit_far, totals, back_near, back_far, unit_turned_near, unit_turned_far,
         inverse_near, inverse_far, turned_near, turned_far, proj_columns, gain_row,
     )
-    across, keep_lead, keep_tail = outs[:3]
-    along, (text_fourth, weights_fourth) = outs[3 : 2 + steps], outs[2 + steps :]
-
-    across = send(across, "rep", lambda p: p ^ 1)
-    along = [send(along[step - 1], "rep", lambda p: p ^ (2 * step)) for step in reversed(range(1, steps))]
+    send_lead, keep_lead, send_tail, keep_tail, text_fourth, weights_fourth = outs
+    come_lead = send(send_lead, "rep", lambda p: p ^ 1)
+    come_tail = send(send_tail, "rep", lambda p: p ^ 2)
 
     feature_grad, token = call(
         image_body,
@@ -600,21 +589,18 @@
         weights_fourth, unit_near, factors,
     )
 
-    outs = call(
-        first_sum_body,
-        [((lead, full), BF16)] * steps + [((tail, full), BF16)] * 2,
-        [((steps, 2, tail, full), BF16)],
-        smem=1,
+    send_lead, keep_lead, send_tail, keep_tail = call(
+        halve_body,
+        [((2, lead, full), BF16)] * 2 + [((2, tail, full), BF16)] * 2,
         moved=4 * each * width,
-    )(place, token, keep_lead, across, keep_tail, *along)
-    leads = [outs[0]] + [send(outs[step], "rep", lambda p: p ^ (2 * step)) for step in reversed(range(1, steps))]
-    tail_across = send(outs[steps + 1], "rep", lambda p: p ^ 1)
-
-    (reduced,) = call(
-        last_sum_body,
-        [(packet, BF16)],
-        moved=4 * each * width,
-    )(outs[steps], tail_across, *leads)
+    )(token, keep_lead, come_lead, keep_tail, come_tail)
+    come_lead = send(send_lead, "rep", lambda p: p ^ 2)
+    come_tail = send(send_tail, "rep", lambda p: p ^ 1)
+    send_all, keep_all = call(quarter_body, [(packet, BF16)] * 2, moved=2 * each * width)(
+        keep_lead, come_lead, keep_tail, come_tail
+    )
+    come_all = send(send_all, "rep", lambda p: p ^ 4)
+    (reduced,) = call(last_sum_body, [(packet, BF16)], moved=each * width)(keep_all, come_all)
     far_block = send(reduced, "loop", lambda p: p ^ 2)
     near_block = send(reduced, "loop", lambda p: p ^ 1)
     blocks = [reduced, near_block, far_block, send(far_block, "loop", lambda p: p ^ 1)]
@@ -622,7 +608,7 @@
     proj_grad, gain_gradient = call(
         functools.partial(finish_body, members),
         [((each, width), F32), ((width,), F32)],
-        [((members, BAND, LANES), F32)],
+        [((members, bands * BAND, full), F32)],
         smem=1,
         moved=8 * each * width,
     )(place, *blocks)
@@ -632,7 +618,7 @@
 def four_fits(mesh, rows_shape):
     members, groups = mesh.shape["loop"], mesh.shape["rep"]
     rows, width = rows_shape[0] // members, rows_shape[2]
-    if members != 4 or groups & (groups - 1) or width % (members * groups) or width % LANES:
+    if members != 4 or groups != 8 or width % (members * groups) or width % LANES:
         return False
     columns, each = width // members, width // groups
     full = columns // LANES * LANES

time: 62.3 us -> 62.6 us (level)
  waiting for transfers between devices: 10.5 us -> 13.8 us
  starting transfers between devices: 17.2 us -> 15.1 us
  Pallas kernels: 27.8 us -> 26.8 us
    ppermute x17 -> x14, waiting for transfers between devices: 10.5 us -> 13.8 us  [send(): return lax.ppermute(value, axis, [(p, target(p)) for p in range(count)])]
    ppermute x17 -> x14, starting transfers between devices: 17.2 us -> 15.1 us  [send(): return lax.ppermute(value, axis, [(p, target(p)) for p in range(count)])]
    pallas_call x10 -> x11, Pallas kernels: 27.8 us -> 26.8 us  [run(): pl.pallas_call(body, out_shape=[jax.ShapeDtypeStruct(shape, kind) for sha...]
  transfers between devices with their start and end apart: 17 -> 14, of which waited for: 6 -> 7; matrix products, arithmetic and copies ran while one was open for 1% -> 1% of each run, Pallas kernels for 34% -> 34%
where the time goes in v10:
time: 62.6 us; the launch traced here: 62.3 us
  Pallas kernels  26.8 us (43%)
  starting transfers between devices  15.1 us (24%)
  waiting for transfers between devices  13.8 us (22%)
  local copies, waits for them, and re-layouts  4.48 us (7%)
  between operations  2.02 us (3%)
    pallas_call x11, Pallas kernels, run(): pl.pallas_call(body, out_shape=[jax.ShapeDtypeStruct(shape, kind) for sha...  26.8 us
    ppermute x14, starting transfers between devices, send(): return lax.ppermute(value, axis, [(p, target(p)) for p in range(count)])  15.1 us
    ppermute x14, waiting for transfers between devices, send(): return lax.ppermute(value, axis, [(p, target(p)) for p in range(count)])  13.8 us
    unnamed x6, local copies, waits for them, and re-layouts  3.77 us
  transfers between devices with their start and end apart: 14, of which 7 were waited for; matrix products, arithmetic and copies ran while one was open for 1% of the time, Pallas kernels for 34%

profile of v10, /device:TPU:0, one launch (start us, length us, event | category | flops | bytes accessed | tf_op | source)
XLA Modules:
  0.0 62.3 jit_solution(7629046740202567801)
XLA Ops:
  0.6 0.5 collective-permute-start
  1.1 0.1 collective-permute-start.1
  1.2 2.9 %collective-permute-start.2 = (bf16[192,1152]{1,0:T(8,128)(2,1)}, bf16[192,1152]{1,0:T(8,128)(2,1)S(1)}, u32[]{:S(2)}, u32[]{:S(2)}) collective-permute-start(bf16[192,1152]{1,0:T(8,128)(2,1)} %bitcast.7), channel_id=1, source_target_pairs={{0,16},{8,24},{16,0},{24,8},{1,17},{9,25},{17,1},{25,9},{2,18},{10... | collective-permute-start | bytes 1327112 | tf_op jit(solution)/shard_map/ppermute | solution.py:34
  5.4 0.7 %reshape.11.gain = f32[1,1152]{1,0:T(1,128)S(1)} reshape(f32[1152]{0:T(1024)} %param.9) | data formatting | bytes 9216 | tf_op jit(solution)/shard_map/reshape | solution.py:490
  6.1 0.1 pad_add_fusion.place
  6.2 0.0 collective-permute-done.f1
  6.2 0.0 collective-permute-done.1.t1
  6.2 0.0 copy-start
  6.2 1.7 %copy-done = bf16[1152,1152]{1,0:T(8,128)(2,1)S(1)} copy-done((bf16[1152,1152]{1,0:T(8,128)(2,1)S(1)}, bf16[1152,1152]{1,0:T(8,128)(2,1)}, u32[]{:S(2)}) %copy-start) | copy-done | bytes 2654232
  8.0 0.0 copy-start.1
  8.0 1.0 %copy-done.1 = bf16[192,1,1152]{2,0,1:T(8,128)(2,1)S(1)} copy-done((bf16[192,1,1152]{2,0,1:T(8,128)(2,1)S(1)}, bf16[192,1,1152]{2,0,1:T(8,128)(2,1)}, u32[]{:S(2)}) %copy-start.1) | copy-done | bytes 442392
  9.0 0.0 copy-start.2
  9.0 1.0 %copy-done.2 = bf16[192,1,1152]{2,0,1:T(8,128)(2,1)S(1)} copy-done((bf16[192,1,1152]{2,0,1:T(8,128)(2,1)S(1)}, bf16[192,1,1152]{2,0,1:T(8,128)(2,1)}, u32[]{:S(2)}) %copy-start.2) | copy-done | bytes 442392
  10.0 5.2 %shard_map.93 = (bf16[192,1152]{1,0:T(8,128)(2,1)S(1)}, bf16[1152,1152]{1,0:T(8,128)(2,1)S(1)}, bf16[192,1152]{1,0:T(8,128)(2,1)S(1)}, bf16[384,1152]{1,0:T(8,12...) custom-call(f32[1]{0:T(128)S(6)} %copy.10.scale, ...), custom_call_target="tpu_custom_call" | custom-call | flops 1019215872 | bytes 3538944 | tf_op jit(solution)/shard_map/pallas_call | solution.py:138
  15.2 0.0 collective-permute-done.2.f2
  15.2 0.1 collective-permute-start.4
  15.3 1.3 %collective-permute-start.3 = (bf16[192,1152]{1,0:T(8,128)(2,1)S(1)}, bf16[192,1152]{1,0:T(8,128)(2,1)S(1)}, u32[]{:S(2)}, u32[]{:S(2)}) collective-permute-start(bf16[192,1152]{1,0:T(8,128)(2,1)S(1)} %bitcast.11), channel_id=1, source_target_pairs={{0,16},{8,24},{16,0},{24,8},{1,17},{9,25},{17,1},{25,9},{2,18},{10... | collective-permute-start | bytes 1327112 | tf_op jit(solution)/shard_map/ppermute | solution.py:34
  16.5 2.2 %shard_map.94 = (bf16[1152,384]{1,0:T(8,128)(2,1)S(1)}, bf16[288,384]{1,0:T(8,128)(2,1)S(1)}, f32[1,384]{1,0:T(1,128)S(1)}, bf16[384,288]{1,0:T(8,128)(2,1)S(1)}...) custom-call(f32[1]{0:T(128)S(6)} %copy.10.scale, f32[1]{0:T(128)S(6)} %copy.11.bias, ...), custom_call_target="tpu_custom_call" | custom-call | flops 509607936 | bytes 3538944 | tf_op jit(solution)/shard_map/pallas_call | solution.py:138
  18.7 0.0 collective-permute-done.4.f3
  18.7 5.8 %shard_map.95 = (bf16[1152,384]{1,0:T(8,128)(2,1)S(1)}, bf16[384,1152]{1,0:T(8,128)(2,1)S(1)}, bf16[288,384]{1,0:T(8,128)(2,1)S(1)}, f32[1,384]{1,0:T(1,128)S(1)...) custom-call(f32[1]{0:T(128)S(6)} %copy.10.scale, f32[1]{0:T(128)S(6)} %copy.11.bias, ...), custom_call_target="tpu_custom_call" | custom-call | flops 1528823808 | bytes 3538944 | tf_op jit(solution)/shard_map/pallas_call | solution.py:138
  24.6 2.0 %shard_map.96 = (bf16[192,1152]{1,0:T(8,128)(2,1)}, f32[8,128]{1,0:T(8,128)S(1)}) custom-call(f32[1]{0:T(128)S(6)} %copy.10.scale, bf16[192,1152]{1,0:T(8,128)(2,1)S(1)} %get-tuple-element.69.text, bf16[384,384]{1,0:T(8,128)(2,1)S(1)} %get-tuple-element.65.weights_near, bf16[384,384]{1,0:T(8,128)(2,1)S(1)} %get-tuple-element.66.weights_far, ...), custom_call_target="tpu_custom_call" | custom-call | flops 1019215872 | bytes 2654208 | tf_op jit(solution)/shard_map/pallas_call | solution.py:138
  26.6 1.3 %collective-permute-done.3.t2 = bf16[192,1152]{1,0:T(8,128)(2,1)S(1)} collective-permute-done((bf16[192,1152]{1,0:T(8,128)(2,1)S(1)}, bf16[192,1152]{1,0:T(8,128)(2,1)S(1)}, u32[]{:S(2)}, u32[]{:S(2)}) %collective-permute-start.3) | collective-permute-done | bytes 442400 | tf_op jit(solution)/shard_map/ppermute | solution.py:34
  27.8 0.0 collective-permute-start.5
  27.8 2.6 %shard_map.97 = (bf16[192,1152]{1,0:T(8,128)(2,1)S(1)}, bf16[192,768]{1,0:T(8,128)(2,1)S(1)}, f32[288,384]{1,0:T(8,128)S(1)}, f32[288,384]{1,0:T(8,128)S(1)}, f32[1,768]{1,0:T(1,128)S(1)}) custom-call(f32[1]{0:T(128)S(6)} %copy.10.scale, f32[1]{0:T(128)S(6)} %copy.11.bias, s32[2]{0:T(128)S(1)} %pad_add_fusion.place, ...), custom_call_target="tpu_custom_call" | custom-call | flops 1019215872 | bytes 3538944 | tf_op jit(solution)/shard_map/pallas_call | solution.py:138
  30.4 0.0 collective-permute-done.5.t3
  30.4 3.7 %shard_map.98 = (bf16[4,112,256]{2,1,0:T(8,128)(2,1)S(1)}, bf16[4,112,256]{2,1,0:T(8,128)(2,1)S(1)}, bf16[4,64,256]{2,1,0:T(8,128)(2,1)S(1)}, bf16[4,64,256]{2,1...) custom-call(f32[1]{0:T(128)S(6)} %copy.10.scale, f32[1]{0:T(128)S(6)} %copy.11.bias, ...), custom_call_target="tpu_custom_call" | custom-call | flops 2038431744 | bytes 7077888 | tf_op jit(solution)/shard_map/pallas_call | solution.py:138
  34.2 1.6 %collective-permute-start.6 = (bf16[4,112,256]{2,1,0:T(8,128)(2,1)S(1)}, bf16[4,112,256]{2,1,0:T(8,128)(2,1)S(1)}, u32[]{:S(2)}, u32[]{:S(2)}) collective-permute-start(bf16[4,112,256]{2,1,0:T(8,128)(2,1)S(1)} %get-tuple-element.91), channel_id=1, source_target_pairs={{0,1},{1,0},{2,3},{3,2},{4,5},{5,4},{6,7},{7,6},{8,9},{9,8},{10,11... | collective-permute-start | bytes 688136 | tf_op jit(solution)/shard_map/ppermute | solution.py:34
  35.8 1.6 %collective-permute-start.7 = (bf16[4,64,256]{2,1,0:T(8,128)(2,1)S(1)}, bf16[4,64,256]{2,1,0:T(8,128)(2,1)S(1)}, u32[]{:S(2)}, u32[]{:S(2)}) collective-permute-start(bf16[4,64,256]{2,1,0:T(8,128)(2,1)S(1)} %get-tuple-element.93), channel_id=1, source_target_pairs={{0,2},{1,3},{2,0},{3,1},{4,6},{5,7},{6,4},{7,5},{8,10},{9,11},{10,... | collective-permute-start | bytes 393224 | tf_op jit(solution)/shard_map/ppermute | solution.py:34
  37.3 3.6 %shard_map.99 = (bf16[192,1152]{1,0:T(8,128)(2,1)}, f32[8,128]{1,0:T(8,128)S(1)}) custom-call(f32[1]{0:T(128)S(6)} %copy.10.scale, bf16[192,1152]{1,0:T(8,128)(2,1)S(1)} %get-tuple-element.53.features, bf16[1152,1152]{1,0:T(8,128)(2,1)S(1)} %get-tuple-element.54.proj, f32[1,1152]{1,0:T(1,128)S(1)} %reshape.11.gain, ...), custom_call_target="tpu_custom_call" | custom-call | flops 2038431744 | bytes 5308416 | tf_op jit(solution)/shard_map/pallas_call | solution.py:138
  41.0 0.5 collective-permute-done.7.come_tail
  41.5 0.9 %collective-permute-done.6.come_lead = bf16[4,112,256]{2,1,0:T(8,128)(2,1)S(1)} collective-permute-done((bf16[4,112,256]{2,1,0:T(8,128)(2,1)S(1)}, bf16[4,112,256]{2,1,0:T(8,128)(2,1)S(1)}, u32[]{:S(2)}, u32[]{:S(2)}) %collective-permute-start.6) | collective-permute-done | bytes 229408 | tf_op jit(solution)/shard_map/ppermute | solution.py:34
  42.4 0.1 shard_map.100
  42.5 1.6 %collective-permute-start.8 = (bf16[2,112,256]{2,1,0:T(8,128)(2,1)S(1)}, bf16[2,112,256]{2,1,0:T(8,128)(2,1)S(1)}, u32[]{:S(2)}, u32[]{:S(2)}) collective-permute-start(bf16[2,112,256]{2,1,0:T(8,128)(2,1)S(1)} %get-tuple-element.95), channel_id=1, source_target_pairs={{0,2},{1,3},{2,0},{3,1},{4,6},{5,7},{6,4},{7,5},{8,10},{9,11},{10,... | collective-permute-start | bytes 344072 | tf_op jit(solution)/shard_map/ppermute | solution.py:34
  44.1 1.5 %collective-permute-start.9 = (bf16[2,64,256]{2,1,0:T(8,128)(2,1)S(1)}, bf16[2,64,256]{2,1,0:T(8,128)(2,1)S(1)}, u32[]{:S(2)}, u32[]{:S(2)}) collective-permute-start(bf16[2,64,256]{2,1,0:T(8,128)(2,1)S(1)} %get-tuple-element.97), channel_id=1, source_target_pairs={{0,1},{1,0},{2,3},{3,2},{4,5},{5,4},{6,7},{7,6},{8,9},{9,8},{10,11... | collective-permute-start | bytes 196616 | tf_op jit(solution)/shard_map/ppermute | solution.py:34
  45.6 2.7 %collective-permute-done.9.come_tail = bf16[2,64,256]{2,1,0:T(8,128)(2,1)S(1)} collective-permute-done((bf16[2,64,256]{2,1,0:T(8,128)(2,1)S(1)}, bf16[2,64,256]{2,1,0:T(8,128)(2,1)S(1)}, u32[]{:S(2)}, u32[]{:S(2)}) %collective-permute-start.9) | collective-permute-done | bytes 65568 | tf_op jit(solution)/shard_map/ppermute | solution.py:34
  48.4 0.0 collective-permute-done.8.come_lead
  48.4 2.7 %collective-permute-start.10 = (bf16[176,256]{1,0:T(8,128)(2,1)S(1)}, bf16[176,256]{1,0:T(8,128)(2,1)S(1)}, u32[]{:S(2)}, u32[]{:S(2)}) collective-permute-start(bf16[176,256]{1,0:T(8,128)(2,1)S(1)} %get-tuple-element.99), channel_id=1, source_target_pairs={{0,4},{1,5},{2,6},{3,7},{4,0},{5,1},{6,2},{7,3},{8,12},{9,13},{10,... | collective-permute-start | bytes 270344 | tf_op jit(solution)/shard_map/ppermute | solution.py:34
  51.1 3.8 %collective-permute-done.10.come = bf16[176,256]{1,0:T(8,128)(2,1)S(1)} collective-permute-done((bf16[176,256]{1,0:T(8,128)(2,1)S(1)}, bf16[176,256]{1,0:T(8,128)(2,1)S(1)}, u32[]{:S(2)}, u32[]{:S(2)}) %collective-permute-start.10) | collective-permute-done | bytes 90144 | tf_op jit(solution)/shard_map/ppermute | solution.py:34
  54.9 1.3 %collective-permute-start.12 = (bf16[176,256]{1,0:T(8,128)(2,1)S(1)}, bf16[176,256]{1,0:T(8,128)(2,1)S(1)}, u32[]{:S(2)}, u32[]{:S(2)}) collective-permute-start(bf16[176,256]{1,0:T(8,128)(2,1)S(1)} %shard_map.102.refs_0_), channel_id=1, source_target_pairs={{0,16},{8,24},{16,0},{24,8},{1,17},{9,25},{17,1},{25,9},{2,18},{10... | collective-permute-start | bytes 270344 | tf_op jit(solution)/shard_map/ppermute | solution.py:34
  56.2 0.0 collective-permute-start.11
  56.2 3.3 %collective-permute-done.12.refs_2_ = bf16[176,256]{1,0:T(8,128)(2,1)S(1)} collective-permute-done((bf16[176,256]{1,0:T(8,128)(2,1)S(1)}, bf16[176,256]{1,0:T(8,128)(2,1)S(1)}, u32[]{:S(2)}, u32[]{:S(2)}) %collective-permute-start.12) | collective-permute-done | bytes 90144 | tf_op jit(solution)/shard_map/ppermute | solution.py:34
  59.5 0.0 collective-permute-start.13
  59.5 0.0 collective-permute-done.11.refs_1_
  59.5 1.3 %collective-permute-done.13.refs_3_ = bf16[176,256]{1,0:T(8,128)(2,1)S(1)} collective-permute-done((bf16[176,256]{1,0:T(8,128)(2,1)S(1)}, bf16[176,256]{1,0:T(8,128)(2,1)S(1)}, u32[]{:S(2)}, u32[]{:S(2)}) %collective-permute-start.13) | collective-permute-done | bytes 90144 | tf_op jit(solution)/shard_map/ppermute | solution.py:34
  60.8 1.5 %shard_map.103 = (f32[144,1152]{1,0:T(8,128)}, f32[1152]{0:T(1024)}) custom-call(s32[2]{0:T(128)S(1)} %pad_add_fusion.place, bf16[176,256]{1,0:T(8,128)(2,1)S(1)} %shard_map.102.refs_0_, bf16[176,256]{1,0:T(8,128)(2,1)S(1)} %collective-permute-done.11.refs_1_, bf16[176,256]{1,0:T(8,128)(2,1)S(1)} %collective-permute-done.12.refs_2_, ...), custom_call_target="tpu_custom_call" | custom-call | bytes 1327104 | tf_op jit(solution)/shard_map/pallas_call | solution.py:138
  (2 shorter events, 0.1 us)
Async XLA Ops:
  0.6 5.6 %collective-permute-start = (bf16[192,1152]{1,0:T(8,128)(2,1)}, bf16[192,1152]{1,0:T(8,128)(2,1)S(1)}, u32[]{:S(2)}, u32[]{:S(2)}) collective-permute-start(bf16[192,1152]{1,0:T(8,128)(2,1)} %bitcast.6), channel_id=1, source_target_pairs={{0,8},{8,0},{16,24},{24,16},{1,9},{9,1},{17,25},{25,17},{2,10},{10... | collective-permute-start | bytes 1327112 | tf_op jit(solution)/shard_map/ppermute | solution.py:34
  1.1 5.1 %collective-permute-start.1 = (bf16[192,1152]{1,0:T(8,128)(2,1)}, bf16[192,1152]{1,0:T(8,128)(2,1)S(1)}, u32[]{:S(2)}, u32[]{:S(2)}) collective-permute-start(bf16[192,1152]{1,0:T(8,128)(2,1)} %bitcast.9), channel_id=1, source_target_pairs={{0,8},{8,0},{16,24},{24,16},{1,9},{9,1},{17,25},{25,17},{2,10},{10... | collective-permute-start | bytes 1327112 | tf_op jit(solution)/shard_map/ppermute | solution.py:34
  1.2 13.9 %collective-permute-start.2 = (bf16[192,1152]{1,0:T(8,128)(2,1)}, bf16[192,1152]{1,0:T(8,128)(2,1)S(1)}, u32[]{:S(2)}, u32[]{:S(2)}) collective-permute-start(bf16[192,1152]{1,0:T(8,128)(2,1)} %bitcast.7), channel_id=1, source_target_pairs={{0,16},{8,24},{16,0},{24,8},{1,17},{9,25},{17,1},{25,9},{2,18},{10... | collective-permute-start | bytes 1327112 | tf_op jit(solution)/shard_map/ppermute | solution.py:34
  6.2 1.8 %copy-start = (bf16[1152,1152]{1,0:T(8,128)(2,1)S(1)}, bf16[1152,1152]{1,0:T(8,128)(2,1)}, u32[]{:S(2)}) copy-start(bf16[1152,1152]{1,0:T(8,128)(2,1)} %proj_far.1) | copy-start | bytes 7962628
  8.0 1.0 %copy-start.1 = (bf16[192,1,1152]{2,0,1:T(8,128)(2,1)S(1)}, bf16[192,1,1152]{2,0,1:T(8,128)(2,1)}, u32[]{:S(2)}) copy-start(bf16[192,1,1152]{2,0,1:T(8,128)(2,1)} %param.6) | copy-start | bytes 1327108
  9.0 1.0 %copy-start.2 = (bf16[192,1,1152]{2,0,1:T(8,128)(2,1)S(1)}, bf16[192,1,1152]{2,0,1:T(8,128)(2,1)}, u32[]{:S(2)}) copy-start(bf16[192,1,1152]{2,0,1:T(8,128)(2,1)} %param.7) | copy-start | bytes 1327108
  15.2 3.5 %collective-permute-start.4 = (bf16[192,1152]{1,0:T(8,128)(2,1)S(1)}, bf16[192,1152]{1,0:T(8,128)(2,1)S(1)}, u32[]{:S(2)}, u32[]{:S(2)}) collective-permute-start(bf16[192,1152]{1,0:T(8,128)(2,1)S(1)} %collective-permute-done.2.f2), channel_id=1, source_target_pairs={{0,8},{8,0},{16,24},{24,16},{1,9},{9,1},{17,25},{25,17},{2,10},{10... | collective-permute-start | bytes 1327112 | tf_op jit(solution)/shard_map/ppermute | solution.py:34
  15.3 12.6 %collective-permute-start.3 = (bf16[192,1152]{1,0:T(8,128)(2,1)S(1)}, bf16[192,1152]{1,0:T(8,128)(2,1)S(1)}, u32[]{:S(2)}, u32[]{:S(2)}) collective-permute-start(bf16[192,1152]{1,0:T(8,128)(2,1)S(1)} %bitcast.11), channel_id=1, source_target_pairs={{0,16},{8,24},{16,0},{24,8},{1,17},{9,25},{17,1},{25,9},{2,18},{10... | collective-permute-start | bytes 1327112 | tf_op jit(solution)/shard_map/ppermute | solution.py:34
  27.8 2.6 %collective-permute-start.5 = (bf16[192,1152]{1,0:T(8,128)(2,1)S(1)}, bf16[192,1152]{1,0:T(8,128)(2,1)S(1)}, u32[]{:S(2)}, u32[]{:S(2)}) collective-permute-start(bf16[192,1152]{1,0:T(8,128)(2,1)S(1)} %collective-permute-done.3.t2), channel_id=1, source_target_pairs={{0,8},{8,0},{16,24},{24,16},{1,9},{9,1},{17,25},{25,17},{2,10},{10... | collective-permute-start | bytes 1327112 | tf_op jit(solution)/shard_map/ppermute | solution.py:34
  34.2 8.2 %collective-permute-start.6 = (bf16[4,112,256]{2,1,0:T(8,128)(2,1)S(1)}, bf16[4,112,256]{2,1,0:T(8,128)(2,1)S(1)}, u32[]{:S(2)}, u32[]{:S(2)}) collective-permute-start(bf16[4,112,256]{2,1,0:T(8,128)(2,1)S(1)} %get-tuple-element.91), channel_id=1, source_target_pairs={{0,1},{1,0},{2,3},{3,2},{4,5},{5,4},{6,7},{7,6},{8,9},{9,8},{10,11... | collective-permute-start | bytes 688136 | tf_op jit(solution)/shard_map/ppermute | solution.py:34
  35.8 5.8 %collective-permute-start.7 = (bf16[4,64,256]{2,1,0:T(8,128)(2,1)S(1)}, bf16[4,64,256]{2,1,0:T(8,128)(2,1)S(1)}, u32[]{:S(2)}, u32[]{:S(2)}) collective-permute-start(bf16[4,64,256]{2,1,0:T(8,128)(2,1)S(1)} %get-tuple-element.93), channel_id=1, source_target_pairs={{0,2},{1,3},{2,0},{3,1},{4,6},{5,7},{6,4},{7,5},{8,10},{9,11},{10,... | collective-permute-start | bytes 393224 | tf_op jit(solution)/shard_map/ppermute | solution.py:34
  42.5 5.9 %collective-permute-start.8 = (bf16[2,112,256]{2,1,0:T(8,128)(2,1)S(1)}, bf16[2,112,256]{2,1,0:T(8,128)(2,1)S(1)}, u32[]{:S(2)}, u32[]{:S(2)}) collective-permute-start(bf16[2,112,256]{2,1,0:T(8,128)(2,1)S(1)} %get-tuple-element.95), channel_id=1, source_target_pairs={{0,2},{1,3},{2,0},{3,1},{4,6},{5,7},{6,4},{7,5},{8,10},{9,11},{10,... | collective-permute-start | bytes 344072 | tf_op jit(solution)/shard_map/ppermute | solution.py:34
  44.1 4.3 %collective-permute-start.9 = (bf16[2,64,256]{2,1,0:T(8,128)(2,1)S(1)}, bf16[2,64,256]{2,1,0:T(8,128)(2,1)S(1)}, u32[]{:S(2)}, u32[]{:S(2)}) collective-permute-start(bf16[2,64,256]{2,1,0:T(8,128)(2,1)S(1)} %get-tuple-element.97), channel_id=1, source_target_pairs={{0,1},{1,0},{2,3},{3,2},{4,5},{5,4},{6,7},{7,6},{8,9},{9,8},{10,11... | collective-permute-start | bytes 196616 | tf_op jit(solution)/shard_map/ppermute | solution.py:34
  48.4 6.4 %collective-permute-start.10 = (bf16[176,256]{1,0:T(8,128)(2,1)S(1)}, bf16[176,256]{1,0:T(8,128)(2,1)S(1)}, u32[]{:S(2)}, u32[]{:S(2)}) collective-permute-start(bf16[176,256]{1,0:T(8,128)(2,1)S(1)} %get-tuple-element.99), channel_id=1, source_target_pairs={{0,4},{1,5},{2,6},{3,7},{4,0},{5,1},{6,2},{7,3},{8,12},{9,13},{10,... | collective-permute-start | bytes 270344 | tf_op jit(solution)/shard_map/ppermute | solution.py:34
  54.9 4.6 %collective-permute-start.12 = (bf16[176,256]{1,0:T(8,128)(2,1)S(1)}, bf16[176,256]{1,0:T(8,128)(2,1)S(1)}, u32[]{:S(2)}, u32[]{:S(2)}) collective-permute-start(bf16[176,256]{1,0:T(8,128)(2,1)S(1)} %shard_map.102.refs_0_), channel_id=1, source_target_pairs={{0,16},{8,24},{16,0},{24,8},{1,17},{9,25},{17,1},{25,9},{2,18},{10... | collective-permute-start | bytes 270344 | tf_op jit(solution)/shard_map/ppermute | solution.py:34
  56.2 3.3 %collective-permute-start.11 = (bf16[176,256]{1,0:T(8,128)(2,1)S(1)}, bf16[176,256]{1,0:T(8,128)(2,1)S(1)}, u32[]{:S(2)}, u32[]{:S(2)}) collective-permute-start(bf16[176,256]{1,0:T(8,128)(2,1)S(1)} %shard_map.102.refs_0_), channel_id=1, source_target_pairs={{0,8},{8,0},{16,24},{24,16},{1,9},{9,1},{17,25},{25,17},{2,10},{10... | collective-permute-start | bytes 270344 | tf_op jit(solution)/shard_map/ppermute | solution.py:34
  59.5 1.3 %collective-permute-start.13 = (bf16[176,256]{1,0:T(8,128)(2,1)S(1)}, bf16[176,256]{1,0:T(8,128)(2,1)S(1)}, u32[]{:S(2)}, u32[]{:S(2)}) collective-permute-start(bf16[176,256]{1,0:T(8,128)(2,1)S(1)} %collective-permute-done.12.refs_2_), channel_id=1, source_target_pairs={{0,8},{8,0},{16,24},{24,16},{1,9},{9,1},{17,25},{25,17},{2,10},{10... | collective-permute-start | bytes 270344 | tf_op jit(solution)/shard_map/ppermute | solution.py:34

commit v11 on v7

--- a/solution.py
+++ b/solution.py
@@ -209,25 +209,30 @@
 
 
 def take_columns(place, source, target):
-    columns = target.shape[1]
-    for member in range(source.shape[1] // columns):
+    members = source.shape[1] // target.shape[1]
+    full = target.shape[1] // LANES * LANES
+    rest = target.shape[1] - full
+    target[:, :full] = source[:, pl.ds(pl.multiple_of(place[0] * full, LANES), full)]
+    for member in range(members):
 
         @pl.when(place[0] == member)
         def _():
-            target[...] = source[:, member * columns : (member + 1) * columns]
+            target[:, full:] = source[:, members * full + member * rest : members * full + (member + 1) * rest]
 
 
 def near_body(
-    f0_far, proj_far, t0_far, f1, t1, gain,
-    f0, proj, t0, normed, unit, factors, text_unit, token, projected, semaphores,
+    scale, bias, place, f0_far, proj_far, t0_far, f1, t1, gain_line,
+    f0, proj, t_sent, gain, normed, unit, factors, text_unit, token, projected, semaphores,
 ):
     rows = f0.shape[0]
     copies = [
         pltpu.make_async_copy(source, target, semaphores.at[at])
-        for at, (source, target) in enumerate(((f0_far, f0), (proj_far, proj), (t0_far, t0)))
+        for at, (source, target) in enumerate(((f0_far, f0), (proj_far, proj), (t0_far, t_sent.at[: f0.shape[0]])))
     ]
     for copy in copies:
         copy.start()
+    for at in range(0, gain.shape[1], LANES):
+        gain[:, at : at + LANES] = gain_line[at : at + LANES].reshape(1, LANES)
     normalize_into(f1, gain, normed, rows)
     unit_into(t1, text_unit, rows)
     copies[0].wait()
@@ -235,15 +240,17 @@
     copies[1].wait()
     projected[...] = dot(normed[...], proj[...])
     copies[2].wait()
-    unit_into(t0, text_unit, 0)
+    t_sent[rows:, :] = jnp.zeros((t_sent.shape[0] - rows, t_sent.shape[1]), BF16)
+    unit_into(t_sent.at[:rows], text_unit, 0)
     unit_into(projected, unit, 0, factors)
     token[...] = jnp.zeros_like(token)
 
 
 def near_pairs_body(
     scale, bias, place, normed, unit, factors, text_unit, proj, before,
-    normed_turned, unit_turned, inverse, text_columns, weights, totals, proj_columns, dots, turned,
+    normed_turned, unit_turned, inverse, text_columns, weights, totals, proj_columns, token, dots, turned,
 ):
+    token[...] = jnp.zeros_like(token)
     dots[...] = dot(text_unit[...], unit[...], LAST)
     totals[...] = weigh(dots, scale[0], bias[0], 0, weights)
     take_columns(place, text_unit, text_columns)
@@ -254,8 +261,12 @@
 
 def turn_own(place, unit, factors, turned, unit_turned, inverse):
     columns = unit_turned.shape[0]
+    full = columns // LANES * LANES
+    rest = columns - full
     turned[...] = unit[...].T
-    unit_turned[...] = turned[pl.ds(pl.multiple_of(place[0] * columns, BAND), columns), :]
+    unit_turned[:full, :] = turned[pl.ds(pl.multiple_of(place[0] * full, LANES), full), :]
+    begin = turned.shape[0] // columns * full
+    unit_turned[full:, :] = turned[pl.ds(pl.multiple_of(begin + place[0] * rest, BAND), rest), :]
     inverse[...] = factors[...].T[:1, :]
 
 
@@ -277,25 +288,22 @@
 
 
 def third_body(
-    scale, bias, place, t2, unit_near, unit_far, weights_near, weights_far, totals_near, totals_far, text_columns_near,
+    scale, bias, place, t2, unit_near, unit_far, totals_near, totals_far, early_near, early_far,
     before, text_unit, weights, back_near, back_far, totals,
     text_columns, dots,
 ):
-    rows = t2.shape[0]
+    rows = text_unit.shape[0]
     near = 2 * rows
-    unit_into(t2, text_unit, 0)
+    unit_into(t2.at[:rows], text_unit, 0)
     take_columns(place, text_unit, text_columns)
     dots[:, :near] = dot(text_unit[...], unit_near[...], LAST)
     dots[:, near:] = dot(text_unit[...], unit_far[...], LAST)
     added = weigh(dots, scale[0], bias[0], near, weights)
     totals[:, :near] = totals_near[...] + added[:, :near]
     totals[:, near:] = totals_far[...] + added[:, near:]
-    back_near[...] = dot(text_columns_near[...], weights_near[...], FIRST) + dot(
-        text_columns[...], weights[:, :near], FIRST
-    )
-    back_far[...] = dot(text_columns_near[...], weights_far[...], FIRST) + dot(
-        text_columns[...], weights[:, near:], FIRST
-    )
+    added = dot(text_columns[...], weights[...], FIRST)
+    back_near[...] = early_near[...] + added[:, :near]
+    back_far[...] = early_far[...] + added[:, near:]
 
 
 def pack_into(target, block, full):
@@ -315,32 +323,33 @@
 
 def partial_body(
     members, groups, lead, scale, bias, place, t3, unit_near, unit_far, totals, back_near, back_far, unit_turned_near,
-    unit_turned_far, inverse_near, inverse_far, turned_near, turned_far, proj_columns, gain, *refs,
+    unit_turned_far, inverse_near, inverse_far, turned_near, turned_far, proj_columns, gain,
+    across, keep_lead, keep_tail, *refs,
 ):
-    (across, keep_lead, keep_tail), refs = refs[:3], refs[3:]
-    along, refs = refs[: groups // 2 - 1], refs[groups // 2 - 1 :]
-    text_unit, weights, text_columns, dots, packed = refs
-    rows = t3.shape[0]
+    along, (text_unit, weights, text_columns, dots, packed) = refs[: groups // 2 - 1], refs[groups // 2 - 1 :]
+    rows = text_unit.shape[0]
     near = 2 * rows
     every = members * rows
     width = unit_near.shape[1]
     columns = width // members
     count, full = packed.shape[1:]
     scale, bias = scale[0], bias[0]
-    unit_into(t3, text_unit, 0)
+    unit_into(t3.at[:rows], text_unit, 0)
     take_columns(place, text_unit, text_columns)
     dots[:, :near] = dot(text_unit[...], unit_near[...], LAST)
     dots[:, near:] = dot(text_unit[...], unit_far[...], LAST)
     total = totals[...] + weigh(dots, scale, bias, near + rows, weights)
-    product = None
-    for where, earlier, unit_turned, inverse, turned in (
-        (slice(0, near), back_near, unit_turned_near, inverse_near, turned_near),
-        (slice(near, every), back_far, unit_turned_far, inverse_far, turned_far),
+    added = dot(text_columns[...], weights[...], FIRST)
+    back = []
+    for where, earlier, unit_turned, inverse in (
+        (slice(0, near), back_near, unit_turned_near, inverse_near),
+        (slice(near, every), back_far, unit_turned_far, inverse_far),
     ):
-        whole = earlier[...] + dot(text_columns[...], weights[:, where], FIRST)
-        back = (whole - unit_turned[...].astype(F32) * total[:, where]) * (inverse[...] * scale)
-        part = dot(turned[...], back.astype(BF16), LAST)
-        product = part if product is None else product + part
+        whole = earlier[...] + added[:, where]
+        part = (whole - unit_turned[...].astype(F32) * total[:, where]) * (inverse[...] * scale)
+        back.append(part.astype(BF16))
+    turned = jnp.concatenate([turned_near[...], turned_far[...]], axis=1)
+    product = dot(turned, jnp.concatenate(back, axis=1), LAST)
     each = width // groups
     product = product * (1.0 / every)
     for group in range(groups):
@@ -407,8 +416,11 @@
     token[...] = jnp.zeros_like(token)
 
 
-def text_body(scale, text, weights_near, weights_far, unit_near, unit_far, text_grad, token, product):
-    rows = text.shape[0]
+def text_body(
+    scale, text, weights_near, weights_far, unit_near, unit_far, text_columns, before,
+    text_grad, back_near, back_far, token, product,
+):
+    rows = text_grad.shape[0]
     scale = scale[0]
     product[...] = dot(weights_near[:rows, :], unit_near[...]) + dot(weights_far[:rows, :], unit_far[...])
 
@@ -422,6 +434,8 @@
         ).astype(BF16)
 
     over_rows(rows, 32, text_chunk)
+    back_near[...] = dot(text_columns[...], weights_near[...], FIRST)
+    back_far[...] = dot(text_columns[...], weights_far[...], FIRST)
     token[...] = jnp.zeros_like(token)
 
 
@@ -452,36 +466,49 @@
     total[split:, :] = (tail[...].astype(F32) + tail_across[...].astype(F32)).astype(BF16)
 
 
-def finish_body(members, place, *refs):
-    packets, (proj_grad, gain_gradient, ordered) = refs[:members], refs[members:]
+def place_main(packet, member, buffer, out, semaphore):
+    rows, full = buffer.shape
+    buffer[...] = packet[:rows, :].astype(F32)
+    where = pl.ds(pl.multiple_of(member * full, LANES), full)
+    copy = pltpu.make_async_copy(buffer, out.at[:, where], semaphore)
+    copy.start()
+    return copy
+
+
+def finish_most_body(place, own, near, far, out, first, second, third, semaphores):
+    copies = [
+        place_main(packet, place[0] ^ k, buffer, out, semaphores.at[k])
+        for k, (packet, buffer) in enumerate(((own, first), (near, second), (far, third)))
+    ]
+    for copy in copies:
+        copy.wait()
+
+
+def finish_body(members, place, begun, *refs):
+    packets, (out, gain_gradient, ordered, main, last, semaphores) = refs[:members], refs[members:]
     count, full = packets[0].shape
-    rows, width = proj_grad.shape
-    columns = width // members
-    rest = columns - full
+    rows, width = out.shape
+    rest = width // members - full
     per_band = full // rest
-    for own in range(members):
-
-        @pl.when(place[0] == own)
-        def _():
-            for k in range(members):
-                base = (own ^ k) * columns
-                packet = packets[k]
-                main = packet[:rows, :].astype(F32)
-                tails = []
-                for index in range(rows // BAND):
-                    at = rows + (index // per_band) * BAND
-                    lane = (index % per_band) * rest
-                    tails.append(packet[at : at + BAND, lane : lane + rest].astype(F32))
-                proj_grad[:, base : base + full] = main
-                proj_grad[:, base + full : base + columns] = jnp.concatenate(tails, axis=0)
-
+    main_out = place_main(packets[-1], place[0] ^ (members - 1), main, out, semaphores.at[0])
     for k in range(members):
-        ordered[place[0] ^ k] = packets[k][count - BAND :, full - LANES :].astype(F32)
-    value = ordered[0]
+        ordered[place[0] ^ k] = packets[k][rows:, :].astype(F32)
+    tails = []
+    for index in range(rows // BAND):
+        at, lane = (index // per_band) * BAND, (index % per_band) * rest
+        tails.append(
+            jnp.concatenate([ordered[member][at : at + BAND, lane : lane + rest] for member in range(members)], axis=1)
+        )
+    last[...] = jnp.concatenate(tails, axis=0)
+    last_out = pltpu.make_async_copy(last, out.at[:, members * full :], semaphores.at[1])
+    last_out.start()
+    value = ordered[0][count - rows - BAND :, full - LANES :]
     for member in range(1, members):
-        value = value + ordered[member]
+        value = value + ordered[member][count - rows - BAND :, full - LANES :]
     for at in range(width // LANES):
         gain_gradient[at * LANES : (at + 1) * LANES] = value[at]
+    main_out.wait()
+    last_out.wait()
 
 
 def local_four(features, text, proj, gain, scale, bias):
@@ -495,7 +522,6 @@
     each = width // groups
     bands = -(-(each // BAND) // (full // (columns - full)))
     packet = (each + bands * BAND, full)
-    gain_row = gain.reshape(1, width)
 
     lead = (3 * packet[0] // BAND // 4) * BAND
     tail = packet[0] - lead
@@ -511,29 +537,31 @@
 
     line, mine = ((1, near), F32), ((columns, near), BF16)
     kept = ((width, width), BF16)
-    f0_kept, proj_kept, t0_kept, normed_near, unit_near, factors, text_near, token = call(
+    f0_kept, proj_kept, t_sent, gain_row, normed_near, unit_near, factors, text_near, token = call(
         near_body,
-        [half, kept, half, wide, wide, ((near, LANES), F32), wide, TOKEN],
+        [half, kept, ((rows + BAND, width), BF16), ((1, width), F32), wide, wide, ((near, LANES), F32), wide, TOKEN],
         [((near, width), F32)],
+        smem=3,
         hbm=3,
         limit=46,
         flops=2 * near * width * width,
         moved=8 * near * width,
-    )(f0, proj, t0, f1, t1, gain_row)
-
-    t_after, f2_after, token = lax.optimization_barrier((t0, f2, token))
-    t2 = send(t_after, "loop", lambda p: p ^ 2)
+    )(scale, bias, place, f0, proj, t0, f1, t1, gain)
+
+    f2_after, f2_token = lax.optimization_barrier((f2, token))
     f3 = send(f2_after, "loop", lambda p: p ^ 1)
+    t2 = send(t_sent, "loop", lambda p: p ^ 2)
 
     (
         turned_near, unit_turned_near, inverse_near, text_columns_near, weights_near, totals_near, proj_columns,
+        token,
     ) = call(
         near_pairs_body,
-        [turned, mine, line, part, square, line, ((width, columns), BF16)],
+        [turned, mine, line, part, square, line, ((width, columns), BF16), TOKEN],
         [((near, near), F32), turned],
         smem=3,
-        flops=near * width * width,
-        moved=8 * near * width,
+        flops=1000,
+        moved=1000,
     )(scale, bias, place, normed_near, unit_near, factors, text_near, proj_kept, token)
 
     turned_far, unit_far, unit_turned_far, inverse_far, weights_far, totals_far, token = call(
@@ -541,23 +569,24 @@
         [turned, wide, mine, line, square, line, TOKEN],
         [wide, ((near, width), F32), ((near, near), F32), turned, ((near, LANES), F32)],
         smem=3,
-        flops=3 * near * width * width,
-        moved=8 * near * width,
-    )(scale, bias, place, f2, f3, proj_kept, gain_row, text_near, totals_near)
-
-    text_grad, token = call(
+        flops=1000,
+        moved=1000,
+    )(scale, bias, place, f2, f3, proj_kept, gain_row, text_near, f2_token)
+
+    back_kind = ((columns, near), F32)
+    text_grad, early_near, early_far, token = call(
         text_body,
-        [half, TOKEN],
+        [half, back_kind, back_kind, TOKEN],
         [((rows, width), F32)],
         smem=1,
-        flops=2 * near * width * width,
-        moved=6 * near * width,
-    )(scale, t0_kept, weights_near, weights_far, unit_near, unit_far)
+        flops=1000,
+        moved=1000,
+    )(scale, t_sent, weights_near, weights_far, unit_near, unit_far, text_columns_near, token)
 
     t2_after, token = lax.optimization_barrier((t2, token))
     t3 = send(t2_after, "loop", lambda p: p ^ 1)
 
-    narrow, back_kind = ((rows, every), BF16), ((columns, near), F32)
+    narrow = ((rows, every), BF16)
     text_third, weights_third, back_near, back_far, totals = call(
         third_body,
         [half, narrow, back_kind, back_kind, ((1, every), F32)],
@@ -566,13 +595,12 @@
         flops=2 * near * width * width,
         moved=8 * near * width,
     )(
-        scale, bias, place, t2, unit_near, unit_far, weights_near, weights_far, totals_near, totals_far,
-        text_columns_near, token,
+        scale, bias, place, t2, unit_near, unit_far, totals_near, totals_far, early_near, early_far, token,
     )
 
     outs = call(
         functools.partial(partial_body, members, groups, lead),
-        [((steps, lead, full), BF16), ((steps, lead, full), BF16)] + [((2, tail, full), BF16)] * steps + [half, narrow],
+        [((steps, lead, full), BF16)] * 2 + [((2, tail, full), BF16)] * steps + [half, narrow],
         [((rows, columns), BF16), ((rows, every), F32), ((groups,) + packet, BF16)],
         smem=3,
         flops=4 * near * width * width,
@@ -616,22 +644,40 @@
     )(outs[steps], tail_across, *leads)
     far_block = send(reduced, "loop", lambda p: p ^ 2)
     near_block = send(reduced, "loop", lambda p: p ^ 1)
-    blocks = [reduced, near_block, far_block, send(far_block, "loop", lambda p: p ^ 1)]
-
-    proj_grad, gain_gradient = call(
+    last_block = send(far_block, "loop", lambda p: p ^ 1)
+    out_kind = jax.ShapeDtypeStruct((each, width), F32)
+    main_room = pltpu.VMEM((each, full), F32)
+    begun = pl.pallas_call(
+        finish_most_body,
+        out_shape=out_kind,
+        in_specs=[SMEM] + [VMEM] * 3,
+        out_specs=HBM,
+        scratch_shapes=[main_room] * 3 + [pltpu.SemaphoreType.DMA((3,))],
+        compiler_params=pltpu.CompilerParams(vmem_limit_bytes=24 * 2**20),
+        cost_estimate=pl.CostEstimate(flops=0, bytes_accessed=8 * each * width, transcendentals=0),
+    )(place, reduced, near_block, far_block)
+    proj_grad, gain_gradient = pl.pallas_call(
         functools.partial(finish_body, members),
-        [((each, width), F32), ((width,), F32)],
-        [((members, BAND, LANES), F32)],
-        smem=1,
-        moved=8 * each * width,
-    )(place, *blocks)
+        out_shape=[out_kind, jax.ShapeDtypeStruct((width,), F32)],
+        in_specs=[SMEM, HBM] + [VMEM] * members,
+        out_specs=[HBM, VMEM],
+        input_output_aliases={1: 0},
+        scratch_shapes=[
+            pltpu.VMEM((members, bands * BAND, full), F32),
+            main_room,
+            pltpu.VMEM((each, width - members * full), F32),
+            pltpu.SemaphoreType.DMA((2,)),
+        ],
+        compiler_params=pltpu.CompilerParams(vmem_limit_bytes=24 * 2**20),
+        cost_estimate=pl.CostEstimate(flops=0, bytes_accessed=2 * each * width, transcendentals=0),
+    )(place, begun, reduced, near_block, far_block, last_block)
     return feature_grad[:, None, :], text_grad[:, None, :], proj_grad, gain_gradient
 
 
 def four_fits(mesh, rows_shape):
     members, groups = mesh.shape["loop"], mesh.shape["rep"]
     rows, width = rows_shape[0] // members, rows_shape[2]
-    if members != 4 or groups & (groups - 1) or width % (members * groups) or width % LANES:
+    if members != 4 or groups != 8 or width % (members * groups) or width % LANES:
         return False
     columns, each = width // members, width // groups
     full = columns // LANES * LANES

time: 67.2 us -> 60.3 us (0.90)
  local copies, waits for them, and re-layouts: 9.03 us -> 2.72 us
  starting transfers between devices: 17.8 us -> 16.3 us
    unnamed x26 -> x6, local copies, waits for them, and re-layouts: 8.33 us -> 2.72 us
    pallas_call x0 -> x2, Pallas kernels: none -> 3.26 us  [the longest x1 1.93 us: local_four(): pl.pallas_call(functools.partial(finish_body, members), out_shape=[out_ki...]
    pallas_call x10 -> x9, Pallas kernels: 28 us -> 25.2 us  [run(): pl.pallas_call(body, out_shape=[jax.ShapeDtypeStruct(shape, kind) for sha...]
    ppermute x17, starting transfers between devices: 17.8 us -> 16.3 us  [send(): return lax.ppermute(value, axis, [(p, target(p)) for p in range(count)])]
    reshape x1 -> x0, local copies, waits for them, and re-layouts: 0.7 us -> none  [local_four(): gain_row = gain.reshape(1, width)]
  transfers between devices with their start and end apart: 17 -> 17, of which waited for: 6 -> 6; matrix products, arithmetic and copies ran while one was open for 1% -> 0% of each run, Pallas kernels for 32% -> 37%
where the time goes in v11:
time: 60.3 us; the launch traced here: 60 us
  Pallas kernels  28.5 us (47%)
  starting transfers between devices  16.3 us (27%)
  waiting for transfers between devices  10.3 us (17%)
  local copies, waits for them, and re-layouts  2.72 us (5%)
  between operations  2.18 us (4%)
    pallas_call x9, Pallas kernels, run(): pl.pallas_call(body, out_shape=[jax.ShapeDtypeStruct(shape, kind) for sha...  25.2 us
    ppermute x17, starting transfers between devices, send(): return lax.ppermute(value, axis, [(p, target(p)) for p in range(count)])  16.3 us
    ppermute x17, waiting for transfers between devices, send(): return lax.ppermute(value, axis, [(p, target(p)) for p in range(count)])  10.3 us
    unnamed x6, local copies, waits for them, and re-layouts  2.72 us
    pallas_call x1, Pallas kernels, local_four(): pl.pallas_call(functools.partial(finish_body, members), out_shape=[out_ki...  1.93 us
    pallas_call x1, Pallas kernels, local_four(): pl.pallas_call(finish_most_body, out_shape=out_kind, in_specs=[SMEM] + [V...  1.34 us
  transfers between devices with their start and end apart: 17, of which 6 were waited for; matrix products, arithmetic and copies ran while one was open for 0% of the time, Pallas kernels for 37%

profile of v11, /device:TPU:0, one launch (start us, length us, event | category | flops | bytes accessed | tf_op | source)
XLA Modules:
  0.0 60.0 jit_solution(8131209419127062955)
XLA Ops:
  0.6 0.5 collective-permute-start
  1.1 0.1 collective-permute-start.1
  1.2 2.9 %collective-permute-start.3 = (bf16[192,1152]{1,0:T(8,128)(2,1)}, bf16[192,1152]{1,0:T(8,128)(2,1)S(1)}, u32[]{:S(2)}, u32[]{:S(2)}) collective-permute-start(bf16[192,1152]{1,0:T(8,128)(2,1)} %bitcast.9), channel_id=1, source_target_pairs={{0,16},{8,24},{16,0},{24,8},{1,17},{9,25},{17,1},{25,9},{2,18},{10... | collective-permute-start | bytes 1327112 | tf_op jit(solution)/shard_map/ppermute | solution.py:34
  5.4 0.1 pad_add_fusion.place
  5.5 0.0 collective-permute-done.f1
  5.5 0.0 collective-permute-done.1.t1
  5.5 1.0 %copy-done = bf16[192,1,1152]{2,0,1:T(8,128)(2,1)S(1)} copy-done((bf16[192,1,1152]{2,0,1:T(8,128)(2,1)S(1)}, bf16[192,1,1152]{2,0,1:T(8,128)(2,1)}, u32[]{:S(2)}) %copy-start) | copy-done | bytes 442392
  6.5 1.0 %copy-done.1 = bf16[192,1,1152]{2,0,1:T(8,128)(2,1)S(1)} copy-done((bf16[192,1,1152]{2,0,1:T(8,128)(2,1)S(1)}, bf16[192,1,1152]{2,0,1:T(8,128)(2,1)}, u32[]{:S(2)}) %copy-start.1) | copy-done | bytes 442392
  7.6 0.7 %copy-done.2 = f32[1152]{0:T(1024)S(1)} copy-done((f32[1152]{0:T(1024)S(1)}, f32[1152]{0:T(1024)}, u32[]{:S(2)}) %copy-start.2) | copy-done | bytes 4632
  8.3 5.0 %shard_map.93 = (bf16[192,1152]{1,0:T(8,128)(2,1)S(1)}, bf16[1152,1152]{1,0:T(8,128)(2,1)S(1)}, bf16[208,1152]{1,0:T(8,128)(2,1)S(1)}, f32[1,1152]{1,0:T(1,128)S...) custom-call(f32[1]{0:T(128)S(6)} %copy.12.scale, ...), custom_call_target="tpu_custom_call" | custom-call | flops 1019215872 | bytes 3538944 | tf_op jit(solution)/shard_map/pallas_call | solution.py:138
  13.2 0.8 %collective-permute-start.2 = (bf16[208,1152]{1,0:T(8,128)(2,1)S(1)}, bf16[208,1152]{1,0:T(8,128)(2,1)S(1)}, u32[]{:S(2)}, u32[]{:S(2)}) collective-permute-start(bf16[208,1152]{1,0:T(8,128)(2,1)S(1)} %get-tuple-element.62.text), channel_id=1, source_target_pairs={{0,16},{8,24},{16,0},{24,8},{1,17},{9,25},{17,1},{25,9},{2,18},{10... | collective-permute-start | bytes 1437704 | tf_op jit(solution)/shard_map/ppermute | solution.py:34
  14.0 0.7 %collective-permute-done.3.f2 = bf16[192,1152]{1,0:T(8,128)(2,1)S(1)} collective-permute-done((bf16[192,1152]{1,0:T(8,128)(2,1)}, bf16[192,1152]{1,0:T(8,128)(2,1)S(1)}, u32[]{:S(2)}, u32[]{:S(2)}) %collective-permute-start.3) | collective-permute-done | bytes 442400 | tf_op jit(solution)/shard_map/ppermute | solution.py:34
  14.8 0.0 collective-permute-start.4
  14.8 2.2 %shard_map.95 = (bf16[1152,384]{1,0:T(8,128)(2,1)S(1)}, bf16[288,384]{1,0:T(8,128)(2,1)S(1)}, f32[1,384]{1,0:T(1,128)S(1)}, bf16[384,288]{1,0:T(8,128)(2,1)S(1)}...) custom-call(f32[1]{0:T(128)S(6)} %copy.12.scale, ...), custom_call_target="tpu_custom_call" | custom-call | flops 1000 | bytes 1000 | tf_op jit(solution)/shard_map/pallas_call | solution.py:138
  17.0 0.0 collective-permute-done.4.f3
  17.0 5.3 %shard_map.94 = (bf16[1152,384]{1,0:T(8,128)(2,1)S(1)}, bf16[384,1152]{1,0:T(8,128)(2,1)S(1)}, bf16[288,384]{1,0:T(8,128)(2,1)S(1)}, f32[1,384]{1,0:T(1,128)S(1)...) custom-call(f32[1]{0:T(128)S(6)} %copy.12.scale, f32[1]{0:T(128)S(6)} %copy.13.bias, ...), custom_call_target="tpu_custom_call" | custom-call | flops 1000 | bytes 1000 | tf_op jit(solution)/shard_map/pallas_call | solution.py:138
  22.3 2.4 %shard_map.96 = (bf16[192,1152]{1,0:T(8,128)(2,1)}, f32[288,384]{1,0:T(8,128)S(1)}, f32[288,384]{1,0:T(8,128)S(1)}, f32[8,128]{1,0:T(8,128)S(1)}) custom-call(f32[1]{0:T(128)S(6)} %copy.12.scale, bf16[208,1152]{1,0:T(8,128)(2,1)S(1)} %get-tuple-element.62.text, bf16[384,384]{1,0:T(8,128)(2,1)S(1)} %get-tuple-element.72.weights_near, ...), custom_call_target="tpu_custom_call" | custom-call | flops 1000 | bytes 1000 | tf_op jit(solution)/shard_map/pallas_call | solution.py:138
  24.7 1.3 %collective-permute-done.2.t2 = bf16[208,1152]{1,0:T(8,128)(2,1)S(1)} collective-permute-done((bf16[208,1152]{1,0:T(8,128)(2,1)S(1)}, bf16[208,1152]{1,0:T(8,128)(2,1)S(1)}, u32[]{:S(2)}, u32[]{:S(2)}) %collective-permute-start.2) | collective-permute-done | bytes 479264 | tf_op jit(solution)/shard_map/ppermute | solution.py:34
  25.9 0.0 collective-permute-start.5
  26.0 2.3 %shard_map.97 = (bf16[192,1152]{1,0:T(8,128)(2,1)S(1)}, bf16[192,768]{1,0:T(8,128)(2,1)S(1)}, f32[288,384]{1,0:T(8,128)S(1)}, f32[288,384]{1,0:T(8,128)S(1)}, f32[1,768]{1,0:T(1,128)S(1)}) custom-call(f32[1]{0:T(128)S(6)} %copy.12.scale, f32[1]{0:T(128)S(6)} %copy.13.bias, s32[2]{0:T(128)S(1)} %pad_add_fusion.place, ...), custom_call_target="tpu_custom_call" | custom-call | flops 1019215872 | bytes 3538944 | tf_op jit(solution)/shard_map/pallas_call | solution.py:138
  28.2 0.0 collective-permute-done.5.t3
  28.2 3.7 %shard_map.98 = (bf16[4,128,256]{2,1,0:T(8,128)(2,1)S(1)}, bf16[4,128,256]{2,1,0:T(8,128)(2,1)S(1)}, bf16[2,48,256]{2,1,0:T(8,128)(2,1)S(1)}, bf16[2,48,256]{2,1...) custom-call(f32[1]{0:T(128)S(6)} %copy.12.scale, ...), custom_call_target="tpu_custom_call" | custom-call | flops 2038431744 | bytes 7077888 | tf_op jit(solution)/shard_map/pallas_call | solution.py:138
  32.0 1.6 %collective-permute-start.6 = (bf16[4,128,256]{2,1,0:T(8,128)(2,1)S(1)}, bf16[4,128,256]{2,1,0:T(8,128)(2,1)S(1)}, u32[]{:S(2)}, u32[]{:S(2)}) collective-permute-start(bf16[4,128,256]{2,1,0:T(8,128)(2,1)S(1)} %get-tuple-element.99), channel_id=1, source_target_pairs={{0,1},{1,0},{2,3},{3,2},{4,5},{5,4},{6,7},{7,6},{8,9},{9,8},{10,11... | collective-permute-start | bytes 786440 | tf_op jit(solution)/shard_map/ppermute | solution.py:34
  33.6 3.6 %collective-permute-start.7 = (bf16[2,48,256]{2,1,0:T(8,128)(2,1)S(1)}, bf16[2,48,256]{2,1,0:T(8,128)(2,1)S(1)}, u32[]{:S(2)}, u32[]{:S(2)}) collective-permute-start(bf16[2,48,256]{2,1,0:T(8,128)(2,1)S(1)} %get-tuple-element.101), channel_id=1, source_target_pairs={{0,6},{1,7},{2,4},{3,5},{4,2},{5,3},{6,0},{7,1},{8,14},{9,15},{10,... | collective-permute-start | bytes 147464 | tf_op jit(solution)/shard_map/ppermute | solution.py:34
  37.2 0.0 collective-permute-start.8
  37.2 0.8 %collective-permute-start.9 = (bf16[2,48,256]{2,1,0:T(8,128)(2,1)S(1)}, bf16[2,48,256]{2,1,0:T(8,128)(2,1)S(1)}, u32[]{:S(2)}, u32[]{:S(2)}) collective-permute-start(bf16[2,48,256]{2,1,0:T(8,128)(2,1)S(1)} %get-tuple-element.103), channel_id=1, source_target_pairs={{0,2},{1,3},{2,0},{3,1},{4,6},{5,7},{6,4},{7,5},{8,10},{9,11},{10,... | collective-permute-start | bytes 147464 | tf_op jit(solution)/shard_map/ppermute | solution.py:34
  38.0 3.6 %shard_map.99 = (bf16[192,1152]{1,0:T(8,128)(2,1)}, f32[8,128]{1,0:T(8,128)S(1)}) custom-call(f32[1]{0:T(128)S(6)} %copy.12.scale, bf16[192,1152]{1,0:T(8,128)(2,1)S(1)} %get-tuple-element.58.features, bf16[1152,1152]{1,0:T(8,128)(2,1)S(1)} %get-tuple-element.59.proj, f32[1,1152]{1,0:T(1,128)S(1)} %get-tuple-element.60.gain, ...), custom_call_target="tpu_custom_call" | custom-call | flops 2038431744 | bytes 5308416 | tf_op jit(solution)/shard_map/pallas_call | solution.py:138
  41.6 0.0 collective-permute-done.7.refs_0_
  41.6 0.7 %collective-permute-done.8.refs_1_ = bf16[2,48,256]{2,1,0:T(8,128)(2,1)S(1)} collective-permute-done((bf16[2,48,256]{2,1,0:T(8,128)(2,1)S(1)}, bf16[2,48,256]{2,1,0:T(8,128)(2,1)S(1)}, u32[]{:S(2)}, u32[]{:S(2)}) %collective-permute-start.8) | collective-permute-done | bytes 49184 | tf_op jit(solution)/shard_map/ppermute | solution.py:34
  42.3 0.0 collective-permute-done.9.refs_2_
  42.3 0.0 collective-permute-done.6.across
  42.3 0.6 %shard_map.100 = (bf16[128,256]{1,0:T(8,128)(2,1)S(1)}, bf16[128,256]{1,0:T(8,128)(2,1)S(1)}, bf16[128,256]{1,0:T(8,128)(2,1)S(1)}, bf16[128,256]{1,0:T(8,128)(2...) custom-call(s32[2]{0:T(128)S(1)} %pad_add_fusion.place, f32[8,128]{1,0:T(8,128)S(1)} %get-tuple-element.97.token, ...), custom_call_target="tpu_custom_call" | custom-call | bytes 663552 | tf_op jit(solution)/shard_map/pallas_call | solution.py:138
  43.0 3.0 %collective-permute-start.11 = (bf16[128,256]{1,0:T(8,128)(2,1)S(1)}, bf16[128,256]{1,0:T(8,128)(2,1)S(1)}, u32[]{:S(2)}, u32[]{:S(2)}) collective-permute-start(bf16[128,256]{1,0:T(8,128)(2,1)S(1)} %get-tuple-element.107), channel_id=1, source_target_pairs={{0,6},{1,7},{2,4},{3,5},{4,2},{5,3},{6,0},{7,1},{8,14},{9,15},{10,... | collective-permute-start | bytes 196616 | tf_op jit(solution)/shard_map/ppermute | solution.py:34
  46.0 0.0 collective-permute-start.12
  46.0 1.5 %collective-permute-start.13 = (bf16[128,256]{1,0:T(8,128)(2,1)S(1)}, bf16[128,256]{1,0:T(8,128)(2,1)S(1)}, u32[]{:S(2)}, u32[]{:S(2)}) collective-permute-start(bf16[128,256]{1,0:T(8,128)(2,1)S(1)} %get-tuple-element.109), channel_id=1, source_target_pairs={{0,2},{1,3},{2,0},{3,1},{4,6},{5,7},{6,4},{7,5},{8,10},{9,11},{10,... | collective-permute-start | bytes 196616 | tf_op jit(solution)/shard_map/ppermute | solution.py:34
  47.4 0.5 collective-permute-start.10
  47.9 3.3 %collective-permute-done.10.tail_across = bf16[48,256]{1,0:T(8,128)(2,1)S(1)} collective-permute-done((bf16[48,256]{1,0:T(8,128)(2,1)S(1)}, bf16[48,256]{1,0:T(8,128)(2,1)S(1)}, u32[]{:S(2)}, u32[]{:S(2)}) %collective-permute-start.10) | collective-permute-done | bytes 24608 | tf_op jit(solution)/shard_map/ppermute | solution.py:34
  51.3 0.0 collective-permute-done.11.refs_1_
  51.3 0.6 %collective-permute-done.12.refs_2_ = bf16[128,256]{1,0:T(8,128)(2,1)S(1)} collective-permute-done((bf16[128,256]{1,0:T(8,128)(2,1)S(1)}, bf16[128,256]{1,0:T(8,128)(2,1)S(1)}, u32[]{:S(2)}, u32[]{:S(2)}) %collective-permute-start.12) | collective-permute-done | bytes 65568 | tf_op jit(solution)/shard_map/ppermute | solution.py:34
  51.9 0.0 collective-permute-done.13.refs_3_
  51.9 1.0 %collective-permute-start.15 = (bf16[176,256]{1,0:T(8,128)(2,1)S(1)}, bf16[176,256]{1,0:T(8,128)(2,1)S(1)}, u32[]{:S(2)}, u32[]{:S(2)}) collective-permute-start(bf16[176,256]{1,0:T(8,128)(2,1)S(1)} %shard_map.101.own.refs_0_), channel_id=1, source_target_pairs={{0,16},{8,24},{16,0},{24,8},{1,17},{9,25},{17,1},{25,9},{2,18},{10... | collective-permute-start | bytes 270344 | tf_op jit(solution)/shard_map/ppermute | solution.py:34
  52.9 0.0 collective-permute-start.14
  52.9 3.6 %collective-permute-done.15.far.refs_2_ = bf16[176,256]{1,0:T(8,128)(2,1)S(1)} collective-permute-done((bf16[176,256]{1,0:T(8,128)(2,1)S(1)}, bf16[176,256]{1,0:T(8,128)(2,1)S(1)}, u32[]{:S(2)}, u32[]{:S(2)}) %collective-permute-start.15) | collective-permute-done | bytes 90144 | tf_op jit(solution)/shard_map/ppermute | solution.py:34
  56.5 0.0 collective-permute-start.16
  56.5 0.0 collective-permute-done.14.near.refs_1_
  56.5 1.3 %shard_map.102.begun = f32[144,1152]{1,0:T(8,128)} custom-call(s32[2]{0:T(128)S(1)} %pad_add_fusion.place, bf16[176,256]{1,0:T(8,128)(2,1)S(1)} %shard_map.101.own.refs_0_, bf16[176,256]{1,0:T(8,128)(2,1)S(1)} %collective-permute-done.14.near.refs_1_, bf16[176,256]{1,0:T(8,128)(2,1)S(1)} %collective-permute-done.15.far.refs_2_), custom_call_target="tpu_custom_call" | custom-call | bytes 1327104 | tf_op jit(solution)/shard_map/pallas_call | solution.py:650
  57.9 0.0 collective-permute-done.16.refs_3_
  57.9 1.9 %shard_map.103 = (f32[144,1152]{1,0:T(8,128)}, f32[1152]{0:T(1024)}) custom-call(s32[2]{0:T(128)S(1)} %pad_add_fusion.place, f32[144,1152]{1,0:T(8,128)} %shard_map.102.begun, bf16[176,256]{1,0:T(8,128)(2,1)S(1)} %shard_map.101.own.refs_0_, bf16[176,256]{1,0:T(8,128)(2,1)S(1)} %collective-permute-done.14.near.refs_1_, ...), custom_call_target="tpu_custom_call", output_to_operand_aliasing={{0}: (1, {})} | custom-call | bytes 331776 | tf_op jit(solution)/shard_map/pallas_call | solution.py:659
  (4 shorter events, 0.0 us)
Async XLA Ops:
  0.6 4.9 %collective-permute-start = (bf16[192,1152]{1,0:T(8,128)(2,1)}, bf16[192,1152]{1,0:T(8,128)(2,1)S(1)}, u32[]{:S(2)}, u32[]{:S(2)}) collective-permute-start(bf16[192,1152]{1,0:T(8,128)(2,1)} %bitcast.8), channel_id=1, source_target_pairs={{0,8},{8,0},{16,24},{24,16},{1,9},{9,1},{17,25},{25,17},{2,10},{10... | collective-permute-start | bytes 1327112 | tf_op jit(solution)/shard_map/ppermute | solution.py:34
  1.1 4.4 %collective-permute-start.1 = (bf16[192,1152]{1,0:T(8,128)(2,1)}, bf16[192,1152]{1,0:T(8,128)(2,1)S(1)}, u32[]{:S(2)}, u32[]{:S(2)}) collective-permute-start(bf16[192,1152]{1,0:T(8,128)(2,1)} %bitcast.6), channel_id=1, source_target_pairs={{0,8},{8,0},{16,24},{24,16},{1,9},{9,1},{17,25},{25,17},{2,10},{10... | collective-permute-start | bytes 1327112 | tf_op jit(solution)/shard_map/ppermute | solution.py:34
  1.2 13.5 %collective-permute-start.3 = (bf16[192,1152]{1,0:T(8,128)(2,1)}, bf16[192,1152]{1,0:T(8,128)(2,1)S(1)}, u32[]{:S(2)}, u32[]{:S(2)}) collective-permute-start(bf16[192,1152]{1,0:T(8,128)(2,1)} %bitcast.9), channel_id=1, source_target_pairs={{0,16},{8,24},{16,0},{24,8},{1,17},{9,25},{17,1},{25,9},{2,18},{10... | collective-permute-start | bytes 1327112 | tf_op jit(solution)/shard_map/ppermute | solution.py:34
  5.5 1.0 %copy-start = (bf16[192,1,1152]{2,0,1:T(8,128)(2,1)S(1)}, bf16[192,1,1152]{2,0,1:T(8,128)(2,1)}, u32[]{:S(2)}) copy-start(bf16[192,1,1152]{2,0,1:T(8,128)(2,1)} %param.7) | copy-start | bytes 1327108
  6.5 1.0 %copy-start.1 = (bf16[192,1,1152]{2,0,1:T(8,128)(2,1)S(1)}, bf16[192,1,1152]{2,0,1:T(8,128)(2,1)}, u32[]{:S(2)}) copy-start(bf16[192,1,1152]{2,0,1:T(8,128)(2,1)} %param.6) | copy-start | bytes 1327108
  7.6 0.7 %copy-start.2 = (f32[1152]{0:T(1024)S(1)}, f32[1152]{0:T(1024)}, u32[]{:S(2)}) copy-start(f32[1152]{0:T(1024)} %gain_line.1) | copy-start | bytes 13828
  13.2 12.7 %collective-permute-start.2 = (bf16[208,1152]{1,0:T(8,128)(2,1)S(1)}, bf16[208,1152]{1,0:T(8,128)(2,1)S(1)}, u32[]{:S(2)}, u32[]{:S(2)}) collective-permute-start(bf16[208,1152]{1,0:T(8,128)(2,1)S(1)} %get-tuple-element.62.text), channel_id=1, source_target_pairs={{0,16},{8,24},{16,0},{24,8},{1,17},{9,25},{17,1},{25,9},{2,18},{10... | collective-permute-start | bytes 1437704 | tf_op jit(solution)/shard_map/ppermute | solution.py:34
  14.8 2.2 %collective-permute-start.4 = (bf16[192,1152]{1,0:T(8,128)(2,1)S(1)}, bf16[192,1152]{1,0:T(8,128)(2,1)S(1)}, u32[]{:S(2)}, u32[]{:S(2)}) collective-permute-start(bf16[192,1152]{1,0:T(8,128)(2,1)S(1)} %collective-permute-done.3.f2), channel_id=1, source_target_pairs={{0,8},{8,0},{16,24},{24,16},{1,9},{9,1},{17,25},{25,17},{2,10},{10... | collective-permute-start | bytes 1327112 | tf_op jit(solution)/shard_map/ppermute | solution.py:34
  25.9 2.3 %collective-permute-start.5 = (bf16[208,1152]{1,0:T(8,128)(2,1)S(1)}, bf16[208,1152]{1,0:T(8,128)(2,1)S(1)}, u32[]{:S(2)}, u32[]{:S(2)}) collective-permute-start(bf16[208,1152]{1,0:T(8,128)(2,1)S(1)} %collective-permute-done.2.t2), channel_id=1, source_target_pairs={{0,8},{8,0},{16,24},{24,16},{1,9},{9,1},{17,25},{25,17},{2,10},{10... | collective-permute-start | bytes 1437704 | tf_op jit(solution)/shard_map/ppermute | solution.py:34
  32.0 10.4 %collective-permute-start.6 = (bf16[4,128,256]{2,1,0:T(8,128)(2,1)S(1)}, bf16[4,128,256]{2,1,0:T(8,128)(2,1)S(1)}, u32[]{:S(2)}, u32[]{:S(2)}) collective-permute-start(bf16[4,128,256]{2,1,0:T(8,128)(2,1)S(1)} %get-tuple-element.99), channel_id=1, source_target_pairs={{0,1},{1,0},{2,3},{3,2},{4,5},{5,4},{6,7},{7,6},{8,9},{9,8},{10,11... | collective-permute-start | bytes 786440 | tf_op jit(solution)/shard_map/ppermute | solution.py:34
  33.6 8.1 %collective-permute-start.7 = (bf16[2,48,256]{2,1,0:T(8,128)(2,1)S(1)}, bf16[2,48,256]{2,1,0:T(8,128)(2,1)S(1)}, u32[]{:S(2)}, u32[]{:S(2)}) collective-permute-start(bf16[2,48,256]{2,1,0:T(8,128)(2,1)S(1)} %get-tuple-element.101), channel_id=1, source_target_pairs={{0,6},{1,7},{2,4},{3,5},{4,2},{5,3},{6,0},{7,1},{8,14},{9,15},{10,... | collective-permute-start | bytes 147464 | tf_op jit(solution)/shard_map/ppermute | solution.py:34
  37.2 5.1 %collective-permute-start.8 = (bf16[2,48,256]{2,1,0:T(8,128)(2,1)S(1)}, bf16[2,48,256]{2,1,0:T(8,128)(2,1)S(1)}, u32[]{:S(2)}, u32[]{:S(2)}) collective-permute-start(bf16[2,48,256]{2,1,0:T(8,128)(2,1)S(1)} %get-tuple-element.102), channel_id=1, source_target_pairs={{0,4},{1,5},{2,6},{3,7},{4,0},{5,1},{6,2},{7,3},{8,12},{9,13},{10,... | collective-permute-start | bytes 147464 | tf_op jit(solution)/shard_map/ppermute | solution.py:34
  37.2 5.1 %collective-permute-start.9 = (bf16[2,48,256]{2,1,0:T(8,128)(2,1)S(1)}, bf16[2,48,256]{2,1,0:T(8,128)(2,1)S(1)}, u32[]{:S(2)}, u32[]{:S(2)}) collective-permute-start(bf16[2,48,256]{2,1,0:T(8,128)(2,1)S(1)} %get-tuple-element.103), channel_id=1, source_target_pairs={{0,2},{1,3},{2,0},{3,1},{4,6},{5,7},{6,4},{7,5},{8,10},{9,11},{10,... | collective-permute-start | bytes 147464 | tf_op jit(solution)/shard_map/ppermute | solution.py:34
  43.0 8.3 %collective-permute-start.11 = (bf16[128,256]{1,0:T(8,128)(2,1)S(1)}, bf16[128,256]{1,0:T(8,128)(2,1)S(1)}, u32[]{:S(2)}, u32[]{:S(2)}) collective-permute-start(bf16[128,256]{1,0:T(8,128)(2,1)S(1)} %get-tuple-element.107), channel_id=1, source_target_pairs={{0,6},{1,7},{2,4},{3,5},{4,2},{5,3},{6,0},{7,1},{8,14},{9,15},{10,... | collective-permute-start | bytes 196616 | tf_op jit(solution)/shard_map/ppermute | solution.py:34
  46.0 5.9 %collective-permute-start.12 = (bf16[128,256]{1,0:T(8,128)(2,1)S(1)}, bf16[128,256]{1,0:T(8,128)(2,1)S(1)}, u32[]{:S(2)}, u32[]{:S(2)}) collective-permute-start(bf16[128,256]{1,0:T(8,128)(2,1)S(1)} %get-tuple-element.108), channel_id=1, source_target_pairs={{0,4},{1,5},{2,6},{3,7},{4,0},{5,1},{6,2},{7,3},{8,12},{9,13},{10,... | collective-permute-start | bytes 196616 | tf_op jit(solution)/shard_map/ppermute | solution.py:34
  46.0 5.9 %collective-permute-start.13 = (bf16[128,256]{1,0:T(8,128)(2,1)S(1)}, bf16[128,256]{1,0:T(8,128)(2,1)S(1)}, u32[]{:S(2)}, u32[]{:S(2)}) collective-permute-start(bf16[128,256]{1,0:T(8,128)(2,1)S(1)} %get-tuple-element.109), channel_id=1, source_target_pairs={{0,2},{1,3},{2,0},{3,1},{4,6},{5,7},{6,4},{7,5},{8,10},{9,11},{10,... | collective-permute-start | bytes 196616 | tf_op jit(solution)/shard_map/ppermute | solution.py:34
  47.4 3.8 %collective-permute-start.10 = (bf16[48,256]{1,0:T(8,128)(2,1)S(1)}, bf16[48,256]{1,0:T(8,128)(2,1)S(1)}, u32[]{:S(2)}, u32[]{:S(2)}) collective-permute-start(bf16[48,256]{1,0:T(8,128)(2,1)S(1)} %get-tuple-element.105), channel_id=1, source_target_pairs={{0,1},{1,0},{2,3},{3,2},{4,5},{5,4},{6,7},{7,6},{8,9},{9,8},{10,11... | collective-permute-start | bytes 73736 | tf_op jit(solution)/shard_map/ppermute | solution.py:34
  51.9 4.6 %collective-permute-start.15 = (bf16[176,256]{1,0:T(8,128)(2,1)S(1)}, bf16[176,256]{1,0:T(8,128)(2,1)S(1)}, u32[]{:S(2)}, u32[]{:S(2)}) collective-permute-start(bf16[176,256]{1,0:T(8,128)(2,1)S(1)} %shard_map.101.own.refs_0_), channel_id=1, source_target_pairs={{0,16},{8,24},{16,0},{24,8},{1,17},{9,25},{17,1},{25,9},{2,18},{10... | collective-permute-start | bytes 270344 | tf_op jit(solution)/shard_map/ppermute | solution.py:34
  52.9 3.6 %collective-permute-start.14 = (bf16[176,256]{1,0:T(8,128)(2,1)S(1)}, bf16[176,256]{1,0:T(8,128)(2,1)S(1)}, u32[]{:S(2)}, u32[]{:S(2)}) collective-permute-start(bf16[176,256]{1,0:T(8,128)(2,1)S(1)} %shard_map.101.own.refs_0_), channel_id=1, source_target_pairs={{0,8},{8,0},{16,24},{24,16},{1,9},{9,1},{17,25},{25,17},{2,10},{10... | collective-permute-start | bytes 270344 | tf_op jit(solution)/shard_map/ppermute | solution.py:34
  56.5 1.4 %collective-permute-start.16 = (bf16[176,256]{1,0:T(8,128)(2,1)S(1)}, bf16[176,256]{1,0:T(8,128)(2,1)S(1)}, u32[]{:S(2)}, u32[]{:S(2)}) collective-permute-start(bf16[176,256]{1,0:T(8,128)(2,1)S(1)} %collective-permute-done.15.far.refs_2_), channel_id=1, source_target_pairs={{0,8},{8,0},{16,24},{24,16},{1,9},{9,1},{17,25},{25,17},{2,10},{10... | collective-permute-start | bytes 270344 | tf_op jit(solution)/shard_map/ppermute | solution.py:34

commit v12 on v11

--- a/solution.py
+++ b/solution.py
@@ -221,36 +221,37 @@
 
 
 def near_body(
-    scale, bias, place, f0_far, proj_far, t0_far, f1, t1, gain_line,
-    f0, proj, t_sent, gain, normed, unit, factors, text_unit, token, projected, semaphores,
+    scale, bias, place, f0_far, proj_far, t0_far, f1, gain_line,
+    f0, proj, t0, gain, normed, unit, factors, text_unit, token, projected, semaphores,
 ):
     rows = f0.shape[0]
     copies = [
         pltpu.make_async_copy(source, target, semaphores.at[at])
-        for at, (source, target) in enumerate(((f0_far, f0), (proj_far, proj), (t0_far, t_sent.at[: f0.shape[0]])))
+        for at, (source, target) in enumerate(((f0_far, f0), (proj_far, proj), (t0_far, t0)))
     ]
     for copy in copies:
         copy.start()
     for at in range(0, gain.shape[1], LANES):
         gain[:, at : at + LANES] = gain_line[at : at + LANES].reshape(1, LANES)
     normalize_into(f1, gain, normed, rows)
-    unit_into(t1, text_unit, rows)
     copies[0].wait()
     normalize_into(f0, gain, normed, 0)
     copies[1].wait()
     projected[...] = dot(normed[...], proj[...])
     copies[2].wait()
-    t_sent[rows:, :] = jnp.zeros((t_sent.shape[0] - rows, t_sent.shape[1]), BF16)
-    unit_into(t_sent.at[:rows], text_unit, 0)
+    unit_into(t0, text_unit, 0)
     unit_into(projected, unit, 0, factors)
     token[...] = jnp.zeros_like(token)
 
 
 def near_pairs_body(
-    scale, bias, place, normed, unit, factors, text_unit, proj, before,
-    normed_turned, unit_turned, inverse, text_columns, weights, totals, proj_columns, token, dots, turned,
+    scale, bias, place, normed, unit, factors, text_own, t1, proj, before,
+    text_unit, normed_turned, unit_turned, inverse, text_columns, weights, totals, proj_columns, token, dots, turned,
 ):
     token[...] = jnp.zeros_like(token)
+    rows = t1.shape[0]
+    text_unit[:rows, :] = text_own[...]
+    unit_into(t1, text_unit, rows)
     dots[...] = dot(text_unit[...], unit[...], LAST)
     totals[...] = weigh(dots, scale[0], bias[0], 0, weights)
     take_columns(place, text_unit, text_columns)
@@ -270,14 +271,20 @@
     inverse[...] = factors[...].T[:1, :]
 
 
+def split_body(f2, before, head, tail):
+    head[...] = f2[: head.shape[0], :]
+    tail[...] = f2[head.shape[0] :, :]
+
+
 def far_body(
-    scale, bias, place, f2, f3, proj, gain, text_near, before,
+    scale, bias, place, f2, f3_head, f3_tail, proj, gain, text_near,
     normed_turned, unit, unit_turned, inverse, weights, totals, token,
     normed, projected, dots, turned, factors,
 ):
     rows = f2.shape[0]
     normalize_into(f2, gain, normed, 0)
-    normalize_into(f3, gain, normed, rows)
+    normalize_into(f3_head, gain, normed, rows)
+    normalize_into(f3_tail, gain, normed, rows + f3_head.shape[0])
     projected[...] = dot(normed[...], proj[...])
     unit_into(projected, unit, 0, factors)
     dots[...] = dot(text_near[...], unit[...], LAST)
@@ -294,7 +301,7 @@
 ):
     rows = text_unit.shape[0]
     near = 2 * rows
-    unit_into(t2.at[:rows], text_unit, 0)
+    unit_into(t2, text_unit, 0)
     take_columns(place, text_unit, text_columns)
     dots[:, :near] = dot(text_unit[...], unit_near[...], LAST)
     dots[:, near:] = dot(text_unit[...], unit_far[...], LAST)
@@ -334,7 +341,7 @@
     columns = width // members
     count, full = packed.shape[1:]
     scale, bias = scale[0], bias[0]
-    unit_into(t3.at[:rows], text_unit, 0)
+    unit_into(t3, text_unit, 0)
     take_columns(place, text_unit, text_columns)
     dots[:, :near] = dot(text_unit[...], unit_near[...], LAST)
     dots[:, near:] = dot(text_unit[...], unit_far[...], LAST)
@@ -380,10 +387,10 @@
 
 
 def image_body(
-    scale, features, proj, gain, text_near, text_third, text_fourth, weights_near, weights_third, weights_fourth,
-    unit, factors, feature_grad, token, back, product,
+    scale, proj, text_near, text_third, text_fourth, weights_near, weights_third, weights_fourth,
+    unit, factors, norm_back, token, back, product,
 ):
-    rows, width = features.shape
+    rows = back.shape[0]
     scale = scale[0]
     product[...] = (
         dot(weights_near[:, :rows], text_near[...], FIRST)
@@ -399,14 +406,19 @@
         ).astype(BF16)
 
     over_rows(rows, 32, image_chunk)
-    product[...] = dot(back[...], proj[...], LAST)
+    norm_back[...] = dot(back[...], proj[...], LAST)
+    token[...] = jnp.zeros_like(token)
+
+
+def feature_body(features, gain, norm_back, before, feature_grad, token):
+    rows, width = features.shape
 
     def feature_chunk(where):
         values = features[where, :].astype(F32)
         centred = values - sums(values) * (1.0 / width)
         deviation = lax.rsqrt(sums(centred * centred) * (1.0 / width) + 1e-06)
         xhat = centred * deviation
-        scaled = product[where, :] * gain[...]
+        scaled = norm_back[where, :] * gain[...]
         feature_grad[where, :] = (
             deviation
             * (scaled - sums(scaled) * (1.0 / width) - xhat * (sums(scaled * xhat) * (1.0 / width)))
@@ -456,7 +468,7 @@
     tail_across[...] = value[1].astype(BF16)
 
 
-def last_sum_body(tail, tail_across, *refs):
+def last_sum_body(before, tail, tail_across, *refs):
     leads, total = refs[:-1], refs[-1]
     split = leads[0].shape[0]
     value = leads[0][...].astype(F32)
@@ -466,49 +478,28 @@
     total[split:, :] = (tail[...].astype(F32) + tail_across[...].astype(F32)).astype(BF16)
 
 
-def place_main(packet, member, buffer, out, semaphore):
-    rows, full = buffer.shape
-    buffer[...] = packet[:rows, :].astype(F32)
-    where = pl.ds(pl.multiple_of(member * full, LANES), full)
-    copy = pltpu.make_async_copy(buffer, out.at[:, where], semaphore)
-    copy.start()
-    return copy
-
-
-def finish_most_body(place, own, near, far, out, first, second, third, semaphores):
-    copies = [
-        place_main(packet, place[0] ^ k, buffer, out, semaphores.at[k])
-        for k, (packet, buffer) in enumerate(((own, first), (near, second), (far, third)))
-    ]
-    for copy in copies:
-        copy.wait()
-
-
-def finish_body(members, place, begun, *refs):
-    packets, (out, gain_gradient, ordered, main, last, semaphores) = refs[:members], refs[members:]
+def finish_body(members, place, *refs):
+    packets, (proj_grad, gain_gradient, ordered) = refs[:members], refs[members:]
     count, full = packets[0].shape
-    rows, width = out.shape
+    rows, width = proj_grad.shape
     rest = width // members - full
     per_band = full // rest
-    main_out = place_main(packets[-1], place[0] ^ (members - 1), main, out, semaphores.at[0])
     for k in range(members):
-        ordered[place[0] ^ k] = packets[k][rows:, :].astype(F32)
+        member = place[0] ^ k
+        proj_grad[:, pl.ds(pl.multiple_of(member * full, LANES), full)] = packets[k][:rows, :].astype(F32)
+        ordered[member] = packets[k][rows:, :].astype(F32)
     tails = []
     for index in range(rows // BAND):
         at, lane = (index // per_band) * BAND, (index % per_band) * rest
         tails.append(
             jnp.concatenate([ordered[member][at : at + BAND, lane : lane + rest] for member in range(members)], axis=1)
         )
-    last[...] = jnp.concatenate(tails, axis=0)
-    last_out = pltpu.make_async_copy(last, out.at[:, members * full :], semaphores.at[1])
-    last_out.start()
+    proj_grad[:, members * full :] = jnp.concatenate(tails, axis=0)
     value = ordered[0][count - rows - BAND :, full - LANES :]
     for member in range(1, members):
         value = value + ordered[member][count - rows - BAND :, full - LANES :]
     for at in range(width // LANES):
         gain_gradient[at * LANES : (at + 1) * LANES] = value[at]
-    main_out.wait()
-    last_out.wait()
 
 
 def local_four(features, text, proj, gain, scale, bias):
@@ -523,46 +514,48 @@
     bands = -(-(each // BAND) // (full // (columns - full)))
     packet = (each + bands * BAND, full)
 
-    lead = (3 * packet[0] // BAND // 4) * BAND
+    lead = (5 * packet[0] // BAND // 6) * BAND
     tail = packet[0] - lead
     steps = groups // 2
 
     f0, t0 = features[:, 0, :], text[:, 0, :]
     f2 = send(f0, "loop", lambda p: p ^ 2)
     f1 = send(f0, "loop", lambda p: p ^ 1)
-    t1 = send(t0, "loop", lambda p: p ^ 1)
 
     wide, half = ((near, width), BF16), ((rows, width), BF16)
     square, part, turned = ((near, near), BF16), ((near, columns), BF16), ((width, near), BF16)
 
     line, mine = ((1, near), F32), ((columns, near), BF16)
     kept = ((width, width), BF16)
-    f0_kept, proj_kept, t_sent, gain_row, normed_near, unit_near, factors, text_near, token = call(
+    f0_kept, proj_kept, t_sent, gain_row, normed_near, unit_near, factors, text_own, token = call(
         near_body,
-        [half, kept, ((rows + BAND, width), BF16), ((1, width), F32), wide, wide, ((near, LANES), F32), wide, TOKEN],
+        [half, kept, half, ((1, width), F32), wide, wide, ((near, LANES), F32), half, TOKEN],
         [((near, width), F32)],
         smem=3,
         hbm=3,
         limit=46,
         flops=2 * near * width * width,
         moved=8 * near * width,
-    )(scale, bias, place, f0, proj, t0, f1, t1, gain)
-
-    f2_after, f2_token = lax.optimization_barrier((f2, token))
-    f3 = send(f2_after, "loop", lambda p: p ^ 1)
+    )(scale, bias, place, f0, proj, t0, f1, gain)
+
     t2 = send(t_sent, "loop", lambda p: p ^ 2)
+    t1 = send(t_sent, "loop", lambda p: p ^ 1)
+    head = rows // 6 * 5
+    f3_head, f3_tail = call(split_body, [((head, width), BF16), ((rows - head, width), BF16)], moved=1000)(f2, token)
+    f3_head = send(f3_head, "loop", lambda p: p ^ 1)
+    f3_tail = send(f3_tail, "loop", lambda p: p ^ 1)
 
     (
-        turned_near, unit_turned_near, inverse_near, text_columns_near, weights_near, totals_near, proj_columns,
+        text_near, turned_near, unit_turned_near, inverse_near, text_columns_near, weights_near, totals_near, proj_columns,
         token,
     ) = call(
         near_pairs_body,
-        [turned, mine, line, part, square, line, ((width, columns), BF16), TOKEN],
+        [wide, turned, mine, line, part, square, line, ((width, columns), BF16), TOKEN],
         [((near, near), F32), turned],
         smem=3,
         flops=1000,
         moved=1000,
-    )(scale, bias, place, normed_near, unit_near, factors, text_near, proj_kept, token)
+    )(scale, bias, place, normed_near, unit_near, factors, text_own, t1, proj_kept, token)
 
     turned_far, unit_far, unit_turned_far, inverse_far, weights_far, totals_far, token = call(
         far_body,
@@ -571,7 +564,7 @@
         smem=3,
         flops=1000,
         moved=1000,
-    )(scale, bias, place, f2, f3, proj_kept, gain_row, text_near, f2_token)
+    )(scale, bias, place, f2, f3_head, f3_tail, proj_kept, gain_row, text_near)
 
     back_kind = ((columns, near), F32)
     text_grad, early_near, early_far, token = call(
@@ -615,16 +608,16 @@
     across = send(across, "rep", lambda p: p ^ 1)
     along = [send(along[step - 1], "rep", lambda p: p ^ (2 * step)) for step in reversed(range(1, steps))]
 
-    feature_grad, token = call(
+    norm_back, token = call(
         image_body,
-        [half, TOKEN],
+        [((rows, width), F32), TOKEN],
         [half, ((rows, width), F32)],
         smem=1,
         flops=4 * near * width * width,
         moved=12 * near * width,
     )(
-        scale, f0_kept, proj_kept, gain_row, text_near, text_third, text_fourth, weights_near, weights_third,
-        weights_fourth, unit_near, factors,
+        scale, proj_kept, text_near, text_third, text_fourth, weights_near, weights_third, weights_fourth,
+        unit_near, factors,
     )
 
     outs = call(
@@ -637,40 +630,26 @@
     leads = [outs[0]] + [send(outs[step], "rep", lambda p: p ^ (2 * step)) for step in reversed(range(1, steps))]
     tail_across = send(outs[steps + 1], "rep", lambda p: p ^ 1)
 
+    feature_grad, token = call(feature_body, [half, TOKEN], moved=12 * near * width)(
+        f0_kept, gain_row, norm_back, outs[steps]
+    )
+
     (reduced,) = call(
         last_sum_body,
         [(packet, BF16)],
         moved=4 * each * width,
-    )(outs[steps], tail_across, *leads)
+    )(token, outs[steps], tail_across, *leads)
     far_block = send(reduced, "loop", lambda p: p ^ 2)
     near_block = send(reduced, "loop", lambda p: p ^ 1)
-    last_block = send(far_block, "loop", lambda p: p ^ 1)
-    out_kind = jax.ShapeDtypeStruct((each, width), F32)
-    main_room = pltpu.VMEM((each, full), F32)
-    begun = pl.pallas_call(
-        finish_most_body,
-        out_shape=out_kind,
-        in_specs=[SMEM] + [VMEM] * 3,
-        out_specs=HBM,
-        scratch_shapes=[main_room] * 3 + [pltpu.SemaphoreType.DMA((3,))],
-        compiler_params=pltpu.CompilerParams(vmem_limit_bytes=24 * 2**20),
-        cost_estimate=pl.CostEstimate(flops=0, bytes_accessed=8 * each * width, transcendentals=0),
-    )(place, reduced, near_block, far_block)
-    proj_grad, gain_gradient = pl.pallas_call(
+    blocks = [reduced, near_block, far_block, send(far_block, "loop", lambda p: p ^ 1)]
+
+    proj_grad, gain_gradient = call(
         functools.partial(finish_body, members),
-        out_shape=[out_kind, jax.ShapeDtypeStruct((width,), F32)],
-        in_specs=[SMEM, HBM] + [VMEM] * members,
-        out_specs=[HBM, VMEM],
-        input_output_aliases={1: 0},
-        scratch_shapes=[
-            pltpu.VMEM((members, bands * BAND, full), F32),
-            main_room,
-            pltpu.VMEM((each, width - members * full), F32),
-            pltpu.SemaphoreType.DMA((2,)),
-        ],
-        compiler_params=pltpu.CompilerParams(vmem_limit_bytes=24 * 2**20),
-        cost_estimate=pl.CostEstimate(flops=0, bytes_accessed=2 * each * width, transcendentals=0),
-    )(place, begun, reduced, near_block, far_block, last_block)
+        [((each, width), F32), ((width,), F32)],
+        [((members, bands * BAND, full), F32)],
+        smem=1,
+        moved=8 * each * width,
+    )(place, *blocks)
     return feature_grad[:, None, :], text_grad[:, None, :], proj_grad, gain_gradient
 
 

time: 60.3 us -> 59.2 us (0.982)
  Pallas kernels: 28.5 us -> 26.6 us
  starting transfers between devices: 16.3 us -> 18 us
  waiting for transfers between devices: 10.3 us -> 9.46 us
    pallas_call x2 -> x0, Pallas kernels: 3.26 us -> none  [the longest x1 1.93 us: local_four(): pl.pallas_call(functools.partial(finish_body, members), out_shape=[out_ki...]
    ppermute x17 -> x18, starting transfers between devices: 16.3 us -> 18 us  [send(): return lax.ppermute(value, axis, [(p, target(p)) for p in range(count)])]
    pallas_call x9 -> x12, Pallas kernels: 25.2 us -> 26.6 us  [run(): pl.pallas_call(body, out_shape=[jax.ShapeDtypeStruct(shape, kind) for sha...]
    ppermute x17 -> x18, waiting for transfers between devices: 10.3 us -> 9.46 us  [send(): return lax.ppermute(value, axis, [(p, target(p)) for p in range(count)])]
  transfers between devices with their start and end apart: 17 -> 18, of which waited for: 6 -> 7; matrix products, arithmetic and copies ran while one was open for 0% -> 0% of each run, Pallas kernels for 37% -> 35%
where the time goes in v12:
time: 59.2 us; the launch traced here: 58.9 us
  Pallas kernels  26.6 us (45%)
  starting transfers between devices  18 us (30%)
  waiting for transfers between devices  9.46 us (16%)
  local copies, waits for them, and re-layouts  2.72 us (5%)
  between operations  2.02 us (3%)
    pallas_call x12, Pallas kernels, run(): pl.pallas_call(body, out_shape=[jax.ShapeDtypeStruct(shape, kind) for sha...  26.6 us
    ppermute x18, starting transfers between devices, send(): return lax.ppermute(value, axis, [(p, target(p)) for p in range(count)])  18 us
    ppermute x18, waiting for transfers between devices, send(): return lax.ppermute(value, axis, [(p, target(p)) for p in range(count)])  9.46 us
    unnamed x6, local copies, waits for them, and re-layouts  2.72 us
  transfers between devices with their start and end apart: 18, of which 7 were waited for; matrix products, arithmetic and copies ran while one was open for 0% of the time, Pallas kernels for 35%

profile of v12, /device:TPU:0, one launch (start us, length us, event | category | flops | bytes accessed | tf_op | source)
XLA Modules:
  0.0 58.9 jit_solution(13808555101727835998)
XLA Ops:
  0.6 0.5 collective-permute-start
  1.1 2.6 %collective-permute-start.3 = (bf16[192,1152]{1,0:T(8,128)(2,1)}, bf16[192,1152]{1,0:T(8,128)(2,1)S(1)}, u32[]{:S(2)}, u32[]{:S(2)}) collective-permute-start(bf16[192,1152]{1,0:T(8,128)(2,1)} %bitcast.8), channel_id=1, source_target_pairs={{0,16},{8,24},{16,0},{24,8},{1,17},{9,25},{17,1},{25,9},{2,18},{10... | collective-permute-start | bytes 1327112 | tf_op jit(solution)/shard_map/ppermute | solution.py:34
  5.0 0.1 pad_add_fusion.place
  5.1 0.0 collective-permute-done.f1
  5.1 1.0 %copy-done = bf16[192,1,1152]{2,0,1:T(8,128)(2,1)S(1)} copy-done((bf16[192,1,1152]{2,0,1:T(8,128)(2,1)S(1)}, bf16[192,1,1152]{2,0,1:T(8,128)(2,1)}, u32[]{:S(2)}) %copy-start) | copy-done | bytes 442392
  6.1 1.0 %copy-done.1 = bf16[192,1,1152]{2,0,1:T(8,128)(2,1)S(1)} copy-done((bf16[192,1,1152]{2,0,1:T(8,128)(2,1)S(1)}, bf16[192,1,1152]{2,0,1:T(8,128)(2,1)}, u32[]{:S(2)}) %copy-start.1) | copy-done | bytes 442392
  7.1 0.7 %copy-done.2 = f32[1152]{0:T(1024)S(1)} copy-done((f32[1152]{0:T(1024)S(1)}, f32[1152]{0:T(1024)}, u32[]{:S(2)}) %copy-start.2) | copy-done | bytes 4632
  7.8 4.8 %shard_map.93 = (bf16[192,1152]{1,0:T(8,128)(2,1)S(1)}, bf16[1152,1152]{1,0:T(8,128)(2,1)S(1)}, bf16[192,1152]{1,0:T(8,128)(2,1)S(1)}, f32[1,1152]{1,0:T(1,128)S...) custom-call(f32[1]{0:T(128)S(6)} %copy.10.scale, ...), custom_call_target="tpu_custom_call" | custom-call | flops 1019215872 | bytes 3538944 | tf_op jit(solution)/shard_map/pallas_call | solution.py:138
  12.6 0.2 collective-permute-start.1
  12.8 0.5 collective-permute-start.2
  13.4 1.3 %collective-permute-done.3.f2 = bf16[192,1152]{1,0:T(8,128)(2,1)S(1)} collective-permute-done((bf16[192,1152]{1,0:T(8,128)(2,1)}, bf16[192,1152]{1,0:T(8,128)(2,1)S(1)}, u32[]{:S(2)}, u32[]{:S(2)}) %collective-permute-start.3) | collective-permute-done | bytes 442400 | tf_op jit(solution)/shard_map/ppermute | solution.py:34
  14.7 0.1 collective-permute-start.4
  14.8 0.5 collective-permute-start.5
  15.3 0.0 collective-permute-done.1.t1
  15.3 2.6 %shard_map.94 = (bf16[384,1152]{1,0:T(8,128)(2,1)S(1)}, bf16[1152,384]{1,0:T(8,128)(2,1)S(1)}, bf16[288,384]{1,0:T(8,128)(2,1)S(1)}, f32[1,384]{1,0:T(1,128)S(1)...) custom-call(f32[1]{0:T(128)S(6)} %copy.10.scale, ...), custom_call_target="tpu_custom_call" | custom-call | flops 1000 | bytes 1000 | tf_op jit(solution)/shard_map/pallas_call | solution.py:138
  17.9 0.0 collective-permute-done.5.f3_tail
  17.9 0.0 collective-permute-done.4.f3_head
  17.9 4.9 %shard_map.96 = (bf16[1152,384]{1,0:T(8,128)(2,1)S(1)}, bf16[384,1152]{1,0:T(8,128)(2,1)S(1)}, bf16[288,384]{1,0:T(8,128)(2,1)S(1)}, f32[1,384]{1,0:T(1,128)S(1)...) custom-call(f32[1]{0:T(128)S(6)} %copy.10.scale, f32[1]{0:T(128)S(6)} %copy.11.bias, ...), custom_call_target="tpu_custom_call" | custom-call | flops 1000 | bytes 1000 | tf_op jit(solution)/shard_map/pallas_call | solution.py:138
  22.8 2.4 %shard_map.97 = (bf16[192,1152]{1,0:T(8,128)(2,1)}, f32[288,384]{1,0:T(8,128)S(1)}, f32[288,384]{1,0:T(8,128)S(1)}, f32[8,128]{1,0:T(8,128)S(1)}) custom-call(f32[1]{0:T(128)S(6)} %copy.10.scale, bf16[192,1152]{1,0:T(8,128)(2,1)S(1)} %get-tuple-element.68.text, bf16[384,384]{1,0:T(8,128)(2,1)S(1)} %get-tuple-element.76.weights_near, ...), custom_call_target="tpu_custom_call" | custom-call | flops 1000 | bytes 1000 | tf_op jit(solution)/shard_map/pallas_call | solution.py:138
  25.1 0.1 collective-permute-done.2.t2
  25.2 0.2 collective-permute-start.6
  25.4 2.2 %shard_map.98 = (bf16[192,1152]{1,0:T(8,128)(2,1)S(1)}, bf16[192,768]{1,0:T(8,128)(2,1)S(1)}, f32[288,384]{1,0:T(8,128)S(1)}, f32[288,384]{1,0:T(8,128)S(1)}, f32[1,768]{1,0:T(1,128)S(1)}) custom-call(f32[1]{0:T(128)S(6)} %copy.10.scale, f32[1]{0:T(128)S(6)} %copy.11.bias, s32[2]{0:T(128)S(1)} %pad_add_fusion.place, ...), custom_call_target="tpu_custom_call" | custom-call | flops 1019215872 | bytes 3538944 | tf_op jit(solution)/shard_map/pallas_call | solution.py:138
  27.7 0.0 collective-permute-done.6.t3
  27.7 3.8 %shard_map.99 = (bf16[4,144,256]{2,1,0:T(8,128)(2,1)S(1)}, bf16[4,144,256]{2,1,0:T(8,128)(2,1)S(1)}, bf16[2,32,256]{2,1,0:T(8,128)(2,1)S(1)}, bf16[2,32,256]{2,1...) custom-call(f32[1]{0:T(128)S(6)} %copy.10.scale, ...), custom_call_target="tpu_custom_call" | custom-call | flops 2038431744 | bytes 7077888 | tf_op jit(solution)/shard_map/pallas_call | solution.py:138
  31.5 1.9 %collective-permute-start.7 = (bf16[4,144,256]{2,1,0:T(8,128)(2,1)S(1)}, bf16[4,144,256]{2,1,0:T(8,128)(2,1)S(1)}, u32[]{:S(2)}, u32[]{:S(2)}) collective-permute-start(bf16[4,144,256]{2,1,0:T(8,128)(2,1)S(1)} %get-tuple-element.102), channel_id=1, source_target_pairs={{0,1},{1,0},{2,3},{3,2},{4,5},{5,4},{6,7},{7,6},{8,9},{9,8},{10,11... | collective-permute-start | bytes 884744 | tf_op jit(solution)/shard_map/ppermute | solution.py:34
  33.3 3.6 %collective-permute-start.8 = (bf16[2,32,256]{2,1,0:T(8,128)(2,1)S(1)}, bf16[2,32,256]{2,1,0:T(8,128)(2,1)S(1)}, u32[]{:S(2)}, u32[]{:S(2)}) collective-permute-start(bf16[2,32,256]{2,1,0:T(8,128)(2,1)S(1)} %get-tuple-element.104), channel_id=1, source_target_pairs={{0,6},{1,7},{2,4},{3,5},{4,2},{5,3},{6,0},{7,1},{8,14},{9,15},{10,... | collective-permute-start | bytes 98312 | tf_op jit(solution)/shard_map/ppermute | solution.py:34
  36.9 0.0 collective-permute-start.9
  36.9 0.8 %collective-permute-start.10 = (bf16[2,32,256]{2,1,0:T(8,128)(2,1)S(1)}, bf16[2,32,256]{2,1,0:T(8,128)(2,1)S(1)}, u32[]{:S(2)}, u32[]{:S(2)}) collective-permute-start(bf16[2,32,256]{2,1,0:T(8,128)(2,1)S(1)} %get-tuple-element.106), channel_id=1, source_target_pairs={{0,2},{1,3},{2,0},{3,1},{4,6},{5,7},{6,4},{7,5},{8,10},{9,11},{10,... | collective-permute-start | bytes 98312 | tf_op jit(solution)/shard_map/ppermute | solution.py:34
  37.7 2.1 %shard_map.100 = (f32[192,1152]{1,0:T(8,128)S(1)}, f32[8,128]{1,0:T(8,128)S(1)}) custom-call(f32[1]{0:T(128)S(6)} %copy.10.scale, bf16[1152,1152]{1,0:T(8,128)(2,1)S(1)} %get-tuple-element.63.proj, bf16[384,1152]{1,0:T(8,128)(2,1)S(1)} %get-tuple-element.70.text_near, bf16[192,1152]{1,0:T(8,128)(2,1)S(1)} %get-tuple-element.84.text_third, ...), custom_call_target="tpu_custom_call" | custom-call | flops 2038431744 | bytes 5308416 | tf_op jit(solution)/shard_map/pallas_call | solution.py:138
  39.8 0.0 collective-permute-done.8.refs_0_
  39.8 1.9 %collective-permute-done.9.refs_1_ = bf16[2,32,256]{2,1,0:T(8,128)(2,1)S(1)} collective-permute-done((bf16[2,32,256]{2,1,0:T(8,128)(2,1)S(1)}, bf16[2,32,256]{2,1,0:T(8,128)(2,1)S(1)}, u32[]{:S(2)}, u32[]{:S(2)}) %collective-permute-start.9) | collective-permute-done | bytes 32800 | tf_op jit(solution)/shard_map/ppermute | solution.py:34
  41.7 0.0 collective-permute-done.10.refs_2_
  41.7 0.0 collective-permute-done.7.across
  41.7 0.6 %shard_map.101 = (bf16[144,256]{1,0:T(8,128)(2,1)S(1)}, bf16[144,256]{1,0:T(8,128)(2,1)S(1)}, bf16[144,256]{1,0:T(8,128)(2,1)S(1)}, bf16[144,256]{1,0:T(8,128)(2...) custom-call(s32[2]{0:T(128)S(1)} %pad_add_fusion.place, f32[8,128]{1,0:T(8,128)S(1)} %get-tuple-element.100.token, ...), custom_call_target="tpu_custom_call" | custom-call | bytes 663552 | tf_op jit(solution)/shard_map/pallas_call | solution.py:138
  42.4 3.0 %collective-permute-start.12 = (bf16[144,256]{1,0:T(8,128)(2,1)S(1)}, bf16[144,256]{1,0:T(8,128)(2,1)S(1)}, u32[]{:S(2)}, u32[]{:S(2)}) collective-permute-start(bf16[144,256]{1,0:T(8,128)(2,1)S(1)} %get-tuple-element.113), channel_id=1, source_target_pairs={{0,6},{1,7},{2,4},{3,5},{4,2},{5,3},{6,0},{7,1},{8,14},{9,15},{10,... | collective-permute-start | bytes 221192 | tf_op jit(solution)/shard_map/ppermute | solution.py:34
  45.3 0.0 collective-permute-start.13
  45.3 1.5 %collective-permute-start.14 = (bf16[144,256]{1,0:T(8,128)(2,1)S(1)}, bf16[144,256]{1,0:T(8,128)(2,1)S(1)}, u32[]{:S(2)}, u32[]{:S(2)}) collective-permute-start(bf16[144,256]{1,0:T(8,128)(2,1)S(1)} %get-tuple-element.115), channel_id=1, source_target_pairs={{0,2},{1,3},{2,0},{3,1},{4,6},{5,7},{6,4},{7,5},{8,10},{9,11},{10,... | collective-permute-start | bytes 221192 | tf_op jit(solution)/shard_map/ppermute | solution.py:34
  46.8 0.8 %collective-permute-start.11 = (bf16[32,256]{1,0:T(8,128)(2,1)S(1)}, bf16[32,256]{1,0:T(8,128)(2,1)S(1)}, u32[]{:S(2)}, u32[]{:S(2)}) collective-permute-start(bf16[32,256]{1,0:T(8,128)(2,1)S(1)} %get-tuple-element.111), channel_id=1, source_target_pairs={{0,1},{1,0},{2,3},{3,2},{4,5},{5,4},{6,7},{7,6},{8,9},{9,8},{10,11... | collective-permute-start | bytes 49160 | tf_op jit(solution)/shard_map/ppermute | solution.py:34
  47.6 1.7 %shard_map.102 = (bf16[192,1152]{1,0:T(8,128)(2,1)}, f32[8,128]{1,0:T(8,128)S(1)}) custom-call(bf16[192,1152]{1,0:T(8,128)(2,1)S(1)} %get-tuple-element.61.features, f32[1,1152]{1,0:T(1,128)S(1)} %get-tuple-element.62.gain, f32[192,1152]{1,0:T(8,128)S(1)} %get-tuple-element.99.norm_back, bf16[32,256]{1,0:T(8,128)(2,1)S(1)} %get-tuple-element.107.before.tail), custom_call_target="tpu_custom_call" | custom-call | bytes 5308416 | tf_op jit(solution)/shard_map/pallas_call | solution.py:138
  49.4 1.2 %collective-permute-done.11.tail_across = bf16[32,256]{1,0:T(8,128)(2,1)S(1)} collective-permute-done((bf16[32,256]{1,0:T(8,128)(2,1)S(1)}, bf16[32,256]{1,0:T(8,128)(2,1)S(1)}, u32[]{:S(2)}, u32[]{:S(2)}) %collective-permute-start.11) | collective-permute-done | bytes 16416 | tf_op jit(solution)/shard_map/ppermute | solution.py:34
  50.6 0.0 collective-permute-done.12.refs_1_
  50.6 0.8 %collective-permute-done.13.refs_2_ = bf16[144,256]{1,0:T(8,128)(2,1)S(1)} collective-permute-done((bf16[144,256]{1,0:T(8,128)(2,1)S(1)}, bf16[144,256]{1,0:T(8,128)(2,1)S(1)}, u32[]{:S(2)}, u32[]{:S(2)}) %collective-permute-start.13) | collective-permute-done | bytes 73760 | tf_op jit(solution)/shard_map/ppermute | solution.py:34
  51.3 0.0 collective-permute-done.14.refs_3_
  51.4 1.9 %collective-permute-start.16 = (bf16[176,256]{1,0:T(8,128)(2,1)S(1)}, bf16[176,256]{1,0:T(8,128)(2,1)S(1)}, u32[]{:S(2)}, u32[]{:S(2)}) collective-permute-start(bf16[176,256]{1,0:T(8,128)(2,1)S(1)} %shard_map.103.refs_0_), channel_id=1, source_target_pairs={{0,16},{8,24},{16,0},{24,8},{1,17},{9,25},{17,1},{25,9},{2,18},{10... | collective-permute-start | bytes 270344 | tf_op jit(solution)/shard_map/ppermute | solution.py:34
  53.3 0.0 collective-permute-start.15
  53.3 2.8 %collective-permute-done.16.refs_2_ = bf16[176,256]{1,0:T(8,128)(2,1)S(1)} collective-permute-done((bf16[176,256]{1,0:T(8,128)(2,1)S(1)}, bf16[176,256]{1,0:T(8,128)(2,1)S(1)}, u32[]{:S(2)}, u32[]{:S(2)}) %collective-permute-start.16) | collective-permute-done | bytes 90144 | tf_op jit(solution)/shard_map/ppermute | solution.py:34
  56.1 1.3 %collective-permute-done.17.refs_3_ = bf16[176,256]{1,0:T(8,128)(2,1)S(1)} collective-permute-done((bf16[176,256]{1,0:T(8,128)(2,1)S(1)}, bf16[176,256]{1,0:T(8,128)(2,1)S(1)}, u32[]{:S(2)}, u32[]{:S(2)}) %collective-permute-start.17) | collective-permute-done | bytes 90144 | tf_op jit(solution)/shard_map/ppermute | solution.py:34
  57.4 1.5 %shard_map.104 = (f32[144,1152]{1,0:T(8,128)}, f32[1152]{0:T(1024)}) custom-call(s32[2]{0:T(128)S(1)} %pad_add_fusion.place, bf16[176,256]{1,0:T(8,128)(2,1)S(1)} %shard_map.103.refs_0_, bf16[176,256]{1,0:T(8,128)(2,1)S(1)} %collective-permute-done.15.refs_1_, bf16[176,256]{1,0:T(8,128)(2,1)S(1)} %collective-permute-done.16.refs_2_, ...), custom_call_target="tpu_custom_call" | custom-call | bytes 1327104 | tf_op jit(solution)/shard_map/pallas_call | solution.py:138
  (7 shorter events, 0.1 us)
Async XLA Ops:
  0.6 4.5 %collective-permute-start = (bf16[192,1152]{1,0:T(8,128)(2,1)}, bf16[192,1152]{1,0:T(8,128)(2,1)S(1)}, u32[]{:S(2)}, u32[]{:S(2)}) collective-permute-start(bf16[192,1152]{1,0:T(8,128)(2,1)} %bitcast.7), channel_id=1, source_target_pairs={{0,8},{8,0},{16,24},{24,16},{1,9},{9,1},{17,25},{25,17},{2,10},{10... | collective-permute-start | bytes 1327112 | tf_op jit(solution)/shard_map/ppermute | solution.py:34
  1.1 13.5 %collective-permute-start.3 = (bf16[192,1152]{1,0:T(8,128)(2,1)}, bf16[192,1152]{1,0:T(8,128)(2,1)S(1)}, u32[]{:S(2)}, u32[]{:S(2)}) collective-permute-start(bf16[192,1152]{1,0:T(8,128)(2,1)} %bitcast.8), channel_id=1, source_target_pairs={{0,16},{8,24},{16,0},{24,8},{1,17},{9,25},{17,1},{25,9},{2,18},{10... | collective-permute-start | bytes 1327112 | tf_op jit(solution)/shard_map/ppermute | solution.py:34
  5.1 1.0 %copy-start = (bf16[192,1,1152]{2,0,1:T(8,128)(2,1)S(1)}, bf16[192,1,1152]{2,0,1:T(8,128)(2,1)}, u32[]{:S(2)}) copy-start(bf16[192,1,1152]{2,0,1:T(8,128)(2,1)} %param.7) | copy-start | bytes 1327108
  6.1 1.0 %copy-start.1 = (bf16[192,1,1152]{2,0,1:T(8,128)(2,1)S(1)}, bf16[192,1,1152]{2,0,1:T(8,128)(2,1)}, u32[]{:S(2)}) copy-start(bf16[192,1,1152]{2,0,1:T(8,128)(2,1)} %param.6) | copy-start | bytes 1327108
  7.1 0.7 %copy-start.2 = (f32[1152]{0:T(1024)S(1)}, f32[1152]{0:T(1024)}, u32[]{:S(2)}) copy-start(f32[1152]{0:T(1024)} %gain_line.1) | copy-start | bytes 13828
  12.6 2.7 %collective-permute-start.1 = (bf16[192,1152]{1,0:T(8,128)(2,1)S(1)}, bf16[192,1152]{1,0:T(8,128)(2,1)S(1)}, u32[]{:S(2)}, u32[]{:S(2)}) collective-permute-start(bf16[192,1152]{1,0:T(8,128)(2,1)S(1)} %get-tuple-element.68.text), channel_id=1, source_target_pairs={{0,8},{8,0},{16,24},{24,16},{1,9},{9,1},{17,25},{25,17},{2,10},{10... | collective-permute-start | bytes 1327112 | tf_op jit(solution)/shard_map/ppermute | solution.py:34
  12.8 12.4 %collective-permute-start.2 = (bf16[192,1152]{1,0:T(8,128)(2,1)S(1)}, bf16[192,1152]{1,0:T(8,128)(2,1)S(1)}, u32[]{:S(2)}, u32[]{:S(2)}) collective-permute-start(bf16[192,1152]{1,0:T(8,128)(2,1)S(1)} %get-tuple-element.68.text), channel_id=1, source_target_pairs={{0,16},{8,24},{16,0},{24,8},{1,17},{9,25},{17,1},{25,9},{2,18},{10... | collective-permute-start | bytes 1327112 | tf_op jit(solution)/shard_map/ppermute | solution.py:34
  14.7 3.2 %collective-permute-start.4 = (bf16[160,1152]{1,0:T(8,128)(2,1)S(1)}, bf16[160,1152]{1,0:T(8,128)(2,1)S(1)}, u32[]{:S(2)}, u32[]{:S(2)}) collective-permute-start(bf16[160,1152]{1,0:T(8,128)(2,1)S(1)} %get-tuple-element.71), channel_id=1, source_target_pairs={{0,8},{8,0},{16,24},{24,16},{1,9},{9,1},{17,25},{25,17},{2,10},{10... | collective-permute-start | bytes 1105928 | tf_op jit(solution)/shard_map/ppermute | solution.py:34
  14.8 3.1 %collective-permute-start.5 = (bf16[32,1152]{1,0:T(8,128)(2,1)S(1)}, bf16[32,1152]{1,0:T(8,128)(2,1)S(1)}, u32[]{:S(2)}, u32[]{:S(2)}) collective-permute-start(bf16[32,1152]{1,0:T(8,128)(2,1)S(1)} %get-tuple-element.72), channel_id=1, source_target_pairs={{0,8},{8,0},{16,24},{24,16},{1,9},{9,1},{17,25},{25,17},{2,10},{10... | collective-permute-start | bytes 221192 | tf_op jit(solution)/shard_map/ppermute | solution.py:34
  25.2 2.5 %collective-permute-start.6 = (bf16[192,1152]{1,0:T(8,128)(2,1)S(1)}, bf16[192,1152]{1,0:T(8,128)(2,1)S(1)}, u32[]{:S(2)}, u32[]{:S(2)}) collective-permute-start(bf16[192,1152]{1,0:T(8,128)(2,1)S(1)} %collective-permute-done.2.t2), channel_id=1, source_target_pairs={{0,8},{8,0},{16,24},{24,16},{1,9},{9,1},{17,25},{25,17},{2,10},{10... | collective-permute-start | bytes 1327112 | tf_op jit(solution)/shard_map/ppermute | solution.py:34
  31.5 10.3 %collective-permute-start.7 = (bf16[4,144,256]{2,1,0:T(8,128)(2,1)S(1)}, bf16[4,144,256]{2,1,0:T(8,128)(2,1)S(1)}, u32[]{:S(2)}, u32[]{:S(2)}) collective-permute-start(bf16[4,144,256]{2,1,0:T(8,128)(2,1)S(1)} %get-tuple-element.102), channel_id=1, source_target_pairs={{0,1},{1,0},{2,3},{3,2},{4,5},{5,4},{6,7},{7,6},{8,9},{9,8},{10,11... | collective-permute-start | bytes 884744 | tf_op jit(solution)/shard_map/ppermute | solution.py:34
  33.3 6.5 %collective-permute-start.8 = (bf16[2,32,256]{2,1,0:T(8,128)(2,1)S(1)}, bf16[2,32,256]{2,1,0:T(8,128)(2,1)S(1)}, u32[]{:S(2)}, u32[]{:S(2)}) collective-permute-start(bf16[2,32,256]{2,1,0:T(8,128)(2,1)S(1)} %get-tuple-element.104), channel_id=1, source_target_pairs={{0,6},{1,7},{2,4},{3,5},{4,2},{5,3},{6,0},{7,1},{8,14},{9,15},{10,... | collective-permute-start | bytes 98312 | tf_op jit(solution)/shard_map/ppermute | solution.py:34
  36.9 4.8 %collective-permute-start.9 = (bf16[2,32,256]{2,1,0:T(8,128)(2,1)S(1)}, bf16[2,32,256]{2,1,0:T(8,128)(2,1)S(1)}, u32[]{:S(2)}, u32[]{:S(2)}) collective-permute-start(bf16[2,32,256]{2,1,0:T(8,128)(2,1)S(1)} %get-tuple-element.105), channel_id=1, source_target_pairs={{0,4},{1,5},{2,6},{3,7},{4,0},{5,1},{6,2},{7,3},{8,12},{9,13},{10,... | collective-permute-start | bytes 98312 | tf_op jit(solution)/shard_map/ppermute | solution.py:34
  36.9 4.8 %collective-permute-start.10 = (bf16[2,32,256]{2,1,0:T(8,128)(2,1)S(1)}, bf16[2,32,256]{2,1,0:T(8,128)(2,1)S(1)}, u32[]{:S(2)}, u32[]{:S(2)}) collective-permute-start(bf16[2,32,256]{2,1,0:T(8,128)(2,1)S(1)} %get-tuple-element.106), channel_id=1, source_target_pairs={{0,2},{1,3},{2,0},{3,1},{4,6},{5,7},{6,4},{7,5},{8,10},{9,11},{10,... | collective-permute-start | bytes 98312 | tf_op jit(solution)/shard_map/ppermute | solution.py:34
  42.4 8.2 %collective-permute-start.12 = (bf16[144,256]{1,0:T(8,128)(2,1)S(1)}, bf16[144,256]{1,0:T(8,128)(2,1)S(1)}, u32[]{:S(2)}, u32[]{:S(2)}) collective-permute-start(bf16[144,256]{1,0:T(8,128)(2,1)S(1)} %get-tuple-element.113), channel_id=1, source_target_pairs={{0,6},{1,7},{2,4},{3,5},{4,2},{5,3},{6,0},{7,1},{8,14},{9,15},{10,... | collective-permute-start | bytes 221192 | tf_op jit(solution)/shard_map/ppermute | solution.py:34
  45.3 6.0 %collective-permute-start.13 = (bf16[144,256]{1,0:T(8,128)(2,1)S(1)}, bf16[144,256]{1,0:T(8,128)(2,1)S(1)}, u32[]{:S(2)}, u32[]{:S(2)}) collective-permute-start(bf16[144,256]{1,0:T(8,128)(2,1)S(1)} %get-tuple-element.114), channel_id=1, source_target_pairs={{0,4},{1,5},{2,6},{3,7},{4,0},{5,1},{6,2},{7,3},{8,12},{9,13},{10,... | collective-permute-start | bytes 221192 | tf_op jit(solution)/shard_map/ppermute | solution.py:34
  45.3 6.0 %collective-permute-start.14 = (bf16[144,256]{1,0:T(8,128)(2,1)S(1)}, bf16[144,256]{1,0:T(8,128)(2,1)S(1)}, u32[]{:S(2)}, u32[]{:S(2)}) collective-permute-start(bf16[144,256]{1,0:T(8,128)(2,1)S(1)} %get-tuple-element.115), channel_id=1, source_target_pairs={{0,2},{1,3},{2,0},{3,1},{4,6},{5,7},{6,4},{7,5},{8,10},{9,11},{10,... | collective-permute-start | bytes 221192 | tf_op jit(solution)/shard_map/ppermute | solution.py:34
  46.8 3.7 %collective-permute-start.11 = (bf16[32,256]{1,0:T(8,128)(2,1)S(1)}, bf16[32,256]{1,0:T(8,128)(2,1)S(1)}, u32[]{:S(2)}, u32[]{:S(2)}) collective-permute-start(bf16[32,256]{1,0:T(8,128)(2,1)S(1)} %get-tuple-element.111), channel_id=1, source_target_pairs={{0,1},{1,0},{2,3},{3,2},{4,5},{5,4},{6,7},{7,6},{8,9},{9,8},{10,11... | collective-permute-start | bytes 49160 | tf_op jit(solution)/shard_map/ppermute | solution.py:34
  51.4 4.7 %collective-permute-start.16 = (bf16[176,256]{1,0:T(8,128)(2,1)S(1)}, bf16[176,256]{1,0:T(8,128)(2,1)S(1)}, u32[]{:S(2)}, u32[]{:S(2)}) collective-permute-start(bf16[176,256]{1,0:T(8,128)(2,1)S(1)} %shard_map.103.refs_0_), channel_id=1, source_target_pairs={{0,16},{8,24},{16,0},{24,8},{1,17},{9,25},{17,1},{25,9},{2,18},{10... | collective-permute-start | bytes 270344 | tf_op jit(solution)/shard_map/ppermute | solution.py:34
  53.3 2.8 %collective-permute-start.15 = (bf16[176,256]{1,0:T(8,128)(2,1)S(1)}, bf16[176,256]{1,0:T(8,128)(2,1)S(1)}, u32[]{:S(2)}, u32[]{:S(2)}) collective-permute-start(bf16[176,256]{1,0:T(8,128)(2,1)S(1)} %shard_map.103.refs_0_), channel_id=1, source_target_pairs={{0,8},{8,0},{16,24},{24,16},{1,9},{9,1},{17,25},{25,17},{2,10},{10... | collective-permute-start | bytes 270344 | tf_op jit(solution)/shard_map/ppermute | solution.py:34
  56.1 1.3 %collective-permute-start.17 = (bf16[176,256]{1,0:T(8,128)(2,1)S(1)}, bf16[176,256]{1,0:T(8,128)(2,1)S(1)}, u32[]{:S(2)}, u32[]{:S(2)}) collective-permute-start(bf16[176,256]{1,0:T(8,128)(2,1)S(1)} %collective-permute-done.16.refs_2_), channel_id=1, source_target_pairs={{0,8},{8,0},{16,24},{24,16},{1,9},{9,1},{17,25},{25,17},{2,10},{10... | collective-permute-start | bytes 270344 | tf_op jit(solution)/shard_map/ppermute | solution.py:34

commit v13 on v12

--- a/solution.py
+++ b/solution.py
@@ -246,12 +246,12 @@
 
 def near_pairs_body(
     scale, bias, place, normed, unit, factors, text_own, t1, proj, before,
-    text_unit, normed_turned, unit_turned, inverse, text_columns, weights, totals, proj_columns, token, dots, turned,
+    text_unit, normed_turned, turned, unit_turned, inverse, text_columns, weights, totals, proj_columns, token, dots,
 ):
     token[...] = jnp.zeros_like(token)
     rows = t1.shape[0]
     text_unit[:rows, :] = text_own[...]
-    unit_into(t1, text_unit, rows)
+    text_unit[rows:, :] = t1[...]
     dots[...] = dot(text_unit[...], unit[...], LAST)
     totals[...] = weigh(dots, scale[0], bias[0], 0, weights)
     take_columns(place, text_unit, text_columns)
@@ -277,9 +277,9 @@
 
 
 def far_body(
-    scale, bias, place, f2, f3_head, f3_tail, proj, gain, text_near,
-    normed_turned, unit, unit_turned, inverse, weights, totals, token,
-    normed, projected, dots, turned, factors,
+    scale, bias, place, f2, f3_head, f3_tail, proj, gain, text_near, text_columns, weights_near,
+    normed_turned, unit, turned, unit_turned, inverse, weights, totals, early_near, early_far, token,
+    normed, projected, dots, factors,
 ):
     rows = f2.shape[0]
     normalize_into(f2, gain, normed, 0)
@@ -291,20 +291,21 @@
     totals[...] = weigh(dots, scale[0], bias[0], None, weights)
     turn_own(place, unit, factors, turned, unit_turned, inverse)
     normed_turned[...] = normed[...].T
+    early_near[...] = dot(text_columns[...], weights_near[...], FIRST)
+    early_far[...] = dot(text_columns[...], weights[...], FIRST)
     token[...] = jnp.zeros_like(token)
 
 
 def third_body(
-    scale, bias, place, t2, unit_near, unit_far, totals_near, totals_far, early_near, early_far,
-    before, text_unit, weights, back_near, back_far, totals,
+    scale, bias, place, text_unit, flat_near, flat_far, totals_near, totals_far, early_near, early_far,
+    before, weights, back_near, back_far, totals,
     text_columns, dots,
 ):
     rows = text_unit.shape[0]
     near = 2 * rows
-    unit_into(t2, text_unit, 0)
     take_columns(place, text_unit, text_columns)
-    dots[:, :near] = dot(text_unit[...], unit_near[...], LAST)
-    dots[:, near:] = dot(text_unit[...], unit_far[...], LAST)
+    dots[:, :near] = dot(text_unit[...], flat_near[...])
+    dots[:, near:] = dot(text_unit[...], flat_far[...])
     added = weigh(dots, scale[0], bias[0], near, weights)
     totals[:, :near] = totals_near[...] + added[:, :near]
     totals[:, near:] = totals_far[...] + added[:, near:]
@@ -329,22 +330,21 @@
 
 
 def partial_body(
-    members, groups, lead, scale, bias, place, t3, unit_near, unit_far, totals, back_near, back_far, unit_turned_near,
+    members, groups, lead, scale, bias, place, text_unit, flat_near, flat_far, totals, back_near, back_far, unit_turned_near,
     unit_turned_far, inverse_near, inverse_far, turned_near, turned_far, proj_columns, gain,
     across, keep_lead, keep_tail, *refs,
 ):
-    along, (text_unit, weights, text_columns, dots, packed) = refs[: groups // 2 - 1], refs[groups // 2 - 1 :]
+    along, (weights, text_columns, dots, packed) = refs[: groups // 2 - 1], refs[groups // 2 - 1 :]
     rows = text_unit.shape[0]
     near = 2 * rows
     every = members * rows
-    width = unit_near.shape[1]
+    width = text_unit.shape[1]
     columns = width // members
     count, full = packed.shape[1:]
     scale, bias = scale[0], bias[0]
-    unit_into(t3, text_unit, 0)
     take_columns(place, text_unit, text_columns)
-    dots[:, :near] = dot(text_unit[...], unit_near[...], LAST)
-    dots[:, near:] = dot(text_unit[...], unit_far[...], LAST)
+    dots[:, :near] = dot(text_unit[...], flat_near[...])
+    dots[:, near:] = dot(text_unit[...], flat_far[...])
     total = totals[...] + weigh(dots, scale, bias, near + rows, weights)
     added = dot(text_columns[...], weights[...], FIRST)
     back = []
@@ -429,8 +429,7 @@
 
 
 def text_body(
-    scale, text, weights_near, weights_far, unit_near, unit_far, text_columns, before,
-    text_grad, back_near, back_far, token, product,
+    scale, text, weights_near, weights_far, unit_near, unit_far, before, text_grad, token, product,
 ):
     rows = text_grad.shape[0]
     scale = scale[0]
@@ -446,8 +445,6 @@
         ).astype(BF16)
 
     over_rows(rows, 32, text_chunk)
-    back_near[...] = dot(text_columns[...], weights_near[...], FIRST)
-    back_far[...] = dot(text_columns[...], weights_far[...], FIRST)
     token[...] = jnp.zeros_like(token)
 
 
@@ -478,7 +475,7 @@
     total[split:, :] = (tail[...].astype(F32) + tail_across[...].astype(F32)).astype(BF16)
 
 
-def finish_body(members, place, *refs):
+def finish_body(members, place, before, *refs):
     packets, (proj_grad, gain_gradient, ordered) = refs[:members], refs[members:]
     count, full = packets[0].shape
     rows, width = proj_grad.shape
@@ -527,7 +524,7 @@
 
     line, mine = ((1, near), F32), ((columns, near), BF16)
     kept = ((width, width), BF16)
-    f0_kept, proj_kept, t_sent, gain_row, normed_near, unit_near, factors, text_own, token = call(
+    f0_kept, proj_kept, t0_kept, gain_row, normed_near, unit_near, factors, text_own, token = call(
         near_body,
         [half, kept, half, ((1, width), F32), wide, wide, ((near, LANES), F32), half, TOKEN],
         [((near, width), F32)],
@@ -538,72 +535,68 @@
         moved=8 * near * width,
     )(scale, bias, place, f0, proj, t0, f1, gain)
 
-    t2 = send(t_sent, "loop", lambda p: p ^ 2)
-    t1 = send(t_sent, "loop", lambda p: p ^ 1)
+    t2 = send(text_own, "loop", lambda p: p ^ 2)
+    t1 = send(text_own, "loop", lambda p: p ^ 1)
     head = rows // 6 * 5
     f3_head, f3_tail = call(split_body, [((head, width), BF16), ((rows - head, width), BF16)], moved=1000)(f2, token)
     f3_head = send(f3_head, "loop", lambda p: p ^ 1)
     f3_tail = send(f3_tail, "loop", lambda p: p ^ 1)
 
     (
-        text_near, turned_near, unit_turned_near, inverse_near, text_columns_near, weights_near, totals_near, proj_columns,
+        text_near, turned_near, flat_near, unit_turned_near, inverse_near, text_columns_near, weights_near, totals_near, proj_columns,
         token,
     ) = call(
         near_pairs_body,
-        [wide, turned, mine, line, part, square, line, ((width, columns), BF16), TOKEN],
-        [((near, near), F32), turned],
+        [wide, turned, turned, mine, line, part, square, line, ((width, columns), BF16), TOKEN],
+        [((near, near), F32)],
         smem=3,
         flops=1000,
         moved=1000,
     )(scale, bias, place, normed_near, unit_near, factors, text_own, t1, proj_kept, token)
 
-    turned_far, unit_far, unit_turned_far, inverse_far, weights_far, totals_far, token = call(
+    back_kind = ((columns, near), F32)
+    (
+        turned_far, unit_far, flat_far, unit_turned_far, inverse_far, weights_far, totals_far, early_near, early_far,
+        token,
+    ) = call(
         far_body,
-        [turned, wide, mine, line, square, line, TOKEN],
-        [wide, ((near, width), F32), ((near, near), F32), turned, ((near, LANES), F32)],
+        [turned, wide, turned, mine, line, square, line, back_kind, back_kind, TOKEN],
+        [wide, ((near, width), F32), ((near, near), F32), ((near, LANES), F32)],
         smem=3,
         flops=1000,
         moved=1000,
-    )(scale, bias, place, f2, f3_head, f3_tail, proj_kept, gain_row, text_near)
-
-    back_kind = ((columns, near), F32)
-    text_grad, early_near, early_far, token = call(
-        text_body,
-        [half, back_kind, back_kind, TOKEN],
-        [((rows, width), F32)],
-        smem=1,
-        flops=1000,
-        moved=1000,
-    )(scale, t_sent, weights_near, weights_far, unit_near, unit_far, text_columns_near, token)
+    )(
+        scale, bias, place, f2, f3_head, f3_tail, proj_kept, gain_row, text_near, text_columns_near, weights_near,
+    )
 
     t2_after, token = lax.optimization_barrier((t2, token))
     t3 = send(t2_after, "loop", lambda p: p ^ 1)
 
     narrow = ((rows, every), BF16)
-    text_third, weights_third, back_near, back_far, totals = call(
+    weights_third, back_near, back_far, totals = call(
         third_body,
-        [half, narrow, back_kind, back_kind, ((1, every), F32)],
+        [narrow, back_kind, back_kind, ((1, every), F32)],
         [((rows, columns), BF16), ((rows, every), F32)],
         smem=3,
         flops=2 * near * width * width,
         moved=8 * near * width,
     )(
-        scale, bias, place, t2, unit_near, unit_far, totals_near, totals_far, early_near, early_far, token,
+        scale, bias, place, t2, flat_near, flat_far, totals_near, totals_far, early_near, early_far, token,
     )
 
     outs = call(
         functools.partial(partial_body, members, groups, lead),
-        [((steps, lead, full), BF16)] * 2 + [((2, tail, full), BF16)] * steps + [half, narrow],
+        [((steps, lead, full), BF16)] * 2 + [((2, tail, full), BF16)] * steps + [narrow],
         [((rows, columns), BF16), ((rows, every), F32), ((groups,) + packet, BF16)],
         smem=3,
         flops=4 * near * width * width,
         moved=16 * near * width,
     )(
-        scale, bias, place, t3, unit_near, unit_far, totals, back_near, back_far, unit_turned_near, unit_turned_far,
+        scale, bias, place, t3, flat_near, flat_far, totals, back_near, back_far, unit_turned_near, unit_turned_far,
         inverse_near, inverse_far, turned_near, turned_far, proj_columns, gain_row,
     )
     across, keep_lead, keep_tail = outs[:3]
-    along, (text_fourth, weights_fourth) = outs[3 : 2 + steps], outs[2 + steps :]
+    along, weights_fourth = outs[3 : 2 + steps], outs[2 + steps]
 
     across = send(across, "rep", lambda p: p ^ 1)
     along = [send(along[step - 1], "rep", lambda p: p ^ (2 * step)) for step in reversed(range(1, steps))]
@@ -616,7 +609,7 @@
         flops=4 * near * width * width,
         moved=12 * near * width,
     )(
-        scale, proj_kept, text_near, text_third, text_fourth, weights_near, weights_third, weights_fourth,
+        scale, proj_kept, text_near, t2, t3, weights_near, weights_third, weights_fourth,
         unit_near, factors,
     )
 
@@ -641,6 +634,15 @@
     )(token, outs[steps], tail_across, *leads)
     far_block = send(reduced, "loop", lambda p: p ^ 2)
     near_block = send(reduced, "loop", lambda p: p ^ 1)
+    text_grad, token = call(
+        text_body,
+        [half, TOKEN],
+        [((rows, width), F32)],
+        smem=1,
+        flops=2 * near * width * width,
+        moved=6 * near * width,
+    )(scale, t0_kept, weights_near, weights_far, unit_near, unit_far, reduced)
+    far_block, token = lax.optimization_barrier((far_block, token))
     blocks = [reduced, near_block, far_block, send(far_block, "loop", lambda p: p ^ 1)]
 
     proj_grad, gain_gradient = call(
@@ -649,7 +651,7 @@
         [((members, bands * BAND, full), F32)],
         smem=1,
         moved=8 * each * width,
-    )(place, *blocks)
+    )(place, token, *blocks)
     return feature_grad[:, None, :], text_grad[:, None, :], proj_grad, gain_gradient
 
 

time: 59.2 us -> 58.8 us (level)
  waiting for transfers between devices: 9.46 us -> 11.6 us
  Pallas kernels: 26.6 us -> 25.3 us
  starting transfers between devices: 18 us -> 16.8 us
    ppermute x18, waiting for transfers between devices: 9.46 us -> 11.6 us  [send(): return lax.ppermute(value, axis, [(p, target(p)) for p in range(count)])]
    pallas_call x12, Pallas kernels: 26.6 us -> 25.3 us  [run(): pl.pallas_call(body, out_shape=[jax.ShapeDtypeStruct(shape, kind) for sha...]
    ppermute x18, starting transfers between devices: 18 us -> 16.8 us  [send(): return lax.ppermute(value, axis, [(p, target(p)) for p in range(count)])]
  transfers between devices with their start and end apart: 18 -> 18, of which waited for: 7 -> 7; matrix products, arithmetic and copies ran while one was open for 0% -> 0% of each run, Pallas kernels for 35% -> 34%
where the time goes in v13:
time: 58.8 us; the launch traced here: 58.5 us
  Pallas kernels  25.3 us (43%)
  starting transfers between devices  16.8 us (29%)
  waiting for transfers between devices  11.6 us (20%)
  local copies, waits for them, and re-layouts  2.72 us (5%)
  between operations  2.03 us (3%)
    pallas_call x12, Pallas kernels, run(): pl.pallas_call(body, out_shape=[jax.ShapeDtypeStruct(shape, kind) for sha...  25.3 us
    ppermute x18, starting transfers between devices, send(): return lax.ppermute(value, axis, [(p, target(p)) for p in range(count)])  16.8 us
    ppermute x18, waiting for transfers between devices, send(): return lax.ppermute(value, axis, [(p, target(p)) for p in range(count)])  11.6 us
    unnamed x6, local copies, waits for them, and re-layouts  2.72 us
  transfers between devices with their start and end apart: 18, of which 7 were waited for; matrix products, arithmetic and copies ran while one was open for 0% of the time, Pallas kernels for 34%

profile of v13, /device:TPU:0, one launch (start us, length us, event | category | flops | bytes accessed | tf_op | source)
XLA Modules:
  0.0 58.5 jit_solution(13460585098030216940)
XLA Ops:
  0.6 0.5 collective-permute-start
  1.1 2.6 %collective-permute-start.3 = (bf16[192,1152]{1,0:T(8,128)(2,1)}, bf16[192,1152]{1,0:T(8,128)(2,1)S(1)}, u32[]{:S(2)}, u32[]{:S(2)}) collective-permute-start(bf16[192,1152]{1,0:T(8,128)(2,1)} %bitcast.8), channel_id=1, source_target_pairs={{0,16},{8,24},{16,0},{24,8},{1,17},{9,25},{17,1},{25,9},{2,18},{10... | collective-permute-start | bytes 1327112 | tf_op jit(solution)/shard_map/ppermute | solution.py:34
  5.0 0.1 pad_add_fusion.place
  5.1 0.0 collective-permute-done.f1
  5.1 1.0 %copy-done = bf16[192,1,1152]{2,0,1:T(8,128)(2,1)S(1)} copy-done((bf16[192,1,1152]{2,0,1:T(8,128)(2,1)S(1)}, bf16[192,1,1152]{2,0,1:T(8,128)(2,1)}, u32[]{:S(2)}) %copy-start) | copy-done | bytes 442392
  6.1 1.0 %copy-done.1 = bf16[192,1,1152]{2,0,1:T(8,128)(2,1)S(1)} copy-done((bf16[192,1,1152]{2,0,1:T(8,128)(2,1)S(1)}, bf16[192,1,1152]{2,0,1:T(8,128)(2,1)}, u32[]{:S(2)}) %copy-start.1) | copy-done | bytes 442392
  7.1 0.7 %copy-done.2 = f32[1152]{0:T(1024)S(1)} copy-done((f32[1152]{0:T(1024)S(1)}, f32[1152]{0:T(1024)}, u32[]{:S(2)}) %copy-start.2) | copy-done | bytes 4632
  7.8 4.8 %shard_map.93 = (bf16[192,1152]{1,0:T(8,128)(2,1)S(1)}, bf16[1152,1152]{1,0:T(8,128)(2,1)S(1)}, bf16[192,1152]{1,0:T(8,128)(2,1)S(1)}, f32[1,1152]{1,0:T(1,128)S...) custom-call(f32[1]{0:T(128)S(6)} %copy.10.scale, ...), custom_call_target="tpu_custom_call" | custom-call | flops 1019215872 | bytes 3538944 | tf_op jit(solution)/shard_map/pallas_call | solution.py:138
  12.6 0.2 collective-permute-start.1
  12.8 0.5 collective-permute-start.2
  13.4 1.3 %collective-permute-done.3.f2 = bf16[192,1152]{1,0:T(8,128)(2,1)S(1)} collective-permute-done((bf16[192,1152]{1,0:T(8,128)(2,1)}, bf16[192,1152]{1,0:T(8,128)(2,1)S(1)}, u32[]{:S(2)}, u32[]{:S(2)}) %collective-permute-start.3) | collective-permute-done | bytes 442400 | tf_op jit(solution)/shard_map/ppermute | solution.py:34
  14.7 0.1 collective-permute-start.4
  14.8 0.5 collective-permute-start.5
  15.3 0.0 collective-permute-done.1.t1
  15.3 2.2 %shard_map.94 = (bf16[384,1152]{1,0:T(8,128)(2,1)S(1)}, bf16[1152,384]{1,0:T(8,128)(2,1)S(1)}, bf16[1152,384]{1,0:T(8,128)(2,1)S(1)}, bf16[288,384]{1,0:T(8,128)...) custom-call(f32[1]{0:T(128)S(6)} %copy.10.scale, ...), custom_call_target="tpu_custom_call" | custom-call | flops 1000 | bytes 1000 | tf_op jit(solution)/shard_map/pallas_call | solution.py:138
  17.5 0.0 collective-permute-done.5.f3_tail
  17.5 0.0 collective-permute-done.4.f3_head
  17.5 5.1 %shard_map.96 = (bf16[1152,384]{1,0:T(8,128)(2,1)S(1)}, bf16[384,1152]{1,0:T(8,128)(2,1)S(1)}, bf16[1152,384]{1,0:T(8,128)(2,1)S(1)}, bf16[288,384]{1,0:T(8,128)...) custom-call(f32[1]{0:T(128)S(6)} %copy.10.scale, ...), custom_call_target="tpu_custom_call" | custom-call | flops 1000 | bytes 1000 | tf_op jit(solution)/shard_map/pallas_call | solution.py:138
  22.7 2.6 %collective-permute-done.2.text_unit.text_third = bf16[192,1152]{1,0:T(8,128)(2,1)S(1)} collective-permute-done((bf16[192,1152]{1,0:T(8,128)(2,1)S(1)}, bf16[192,1152]{1,0:T(8,128)(2,1)S(1)}, u32[]{:S(2)}, u32[]{:S(2)}) %collective-permute-start.2) | collective-permute-done | bytes 442400 | tf_op jit(solution)/shard_map/ppermute | solution.py:34
  25.2 0.0 collective-permute-start.6
  25.2 1.9 %shard_map.97 = (bf16[192,768]{1,0:T(8,128)(2,1)S(1)}, f32[288,384]{1,0:T(8,128)S(1)}, f32[288,384]{1,0:T(8,128)S(1)}, f32[1,768]{1,0:T(1,128)S(1)}) custom-call(f32[1]{0:T(128)S(6)} %copy.10.scale, f32[1]{0:T(128)S(6)} %copy.11.bias, s32[2]{0:T(128)S(1)} %pad_add_fusion.place, bf16[192,1152]{1,0:T(8,128)(2,1)S(1)} %collective-permute-done.2.text_unit.text_third, ...), custom_call_target="tpu_custom_call" | custom-call | flops 1019215872 | bytes 3538944 | tf_op jit(solution)/shard_map/pallas_call | solution.py:138
  27.1 0.0 collective-permute-done.6.text_unit.text_fourth
  27.1 3.3 %shard_map.98 = (bf16[4,144,256]{2,1,0:T(8,128)(2,1)S(1)}, bf16[4,144,256]{2,1,0:T(8,128)(2,1)S(1)}, bf16[2,32,256]{2,1,0:T(8,128)(2,1)S(1)}, bf16[2,32,256]{2,1...) custom-call(f32[1]{0:T(128)S(6)} %copy.10.scale, ...), custom_call_target="tpu_custom_call" | custom-call | flops 2038431744 | bytes 7077888 | tf_op jit(solution)/shard_map/pallas_call | solution.py:138
  30.4 1.6 %collective-permute-start.7 = (bf16[4,144,256]{2,1,0:T(8,128)(2,1)S(1)}, bf16[4,144,256]{2,1,0:T(8,128)(2,1)S(1)}, u32[]{:S(2)}, u32[]{:S(2)}) collective-permute-start(bf16[4,144,256]{2,1,0:T(8,128)(2,1)S(1)} %get-tuple-element.100), channel_id=1, source_target_pairs={{0,1},{1,0},{2,3},{3,2},{4,5},{5,4},{6,7},{7,6},{8,9},{9,8},{10,11... | collective-permute-start | bytes 884744 | tf_op jit(solution)/shard_map/ppermute | solution.py:34
  32.0 3.6 %collective-permute-start.8 = (bf16[2,32,256]{2,1,0:T(8,128)(2,1)S(1)}, bf16[2,32,256]{2,1,0:T(8,128)(2,1)S(1)}, u32[]{:S(2)}, u32[]{:S(2)}) collective-permute-start(bf16[2,32,256]{2,1,0:T(8,128)(2,1)S(1)} %get-tuple-element.102), channel_id=1, source_target_pairs={{0,6},{1,7},{2,4},{3,5},{4,2},{5,3},{6,0},{7,1},{8,14},{9,15},{10,... | collective-permute-start | bytes 98312 | tf_op jit(solution)/shard_map/ppermute | solution.py:34
  35.6 0.0 collective-permute-start.9
  35.7 0.8 %collective-permute-start.10 = (bf16[2,32,256]{2,1,0:T(8,128)(2,1)S(1)}, bf16[2,32,256]{2,1,0:T(8,128)(2,1)S(1)}, u32[]{:S(2)}, u32[]{:S(2)}) collective-permute-start(bf16[2,32,256]{2,1,0:T(8,128)(2,1)S(1)} %get-tuple-element.104), channel_id=1, source_target_pairs={{0,2},{1,3},{2,0},{3,1},{4,6},{5,7},{6,4},{7,5},{8,10},{9,11},{10,... | collective-permute-start | bytes 98312 | tf_op jit(solution)/shard_map/ppermute | solution.py:34
  36.4 2.1 %shard_map.99 = (f32[192,1152]{1,0:T(8,128)S(1)}, f32[8,128]{1,0:T(8,128)S(1)}) custom-call(f32[1]{0:T(128)S(6)} %copy.10.scale, bf16[1152,1152]{1,0:T(8,128)(2,1)S(1)} %get-tuple-element.65.proj, bf16[384,1152]{1,0:T(8,128)(2,1)S(1)} %get-tuple-element.71.text_near, bf16[192,1152]{1,0:T(8,128)(2,1)S(1)} %collective-permute-done.2.text_unit.text_third, ...), custom_call_target="tpu_custom_call" | custom-call | flops 2038431744 | bytes 5308416 | tf_op jit(solution)/shard_map/pallas_call | solution.py:138
  38.5 0.0 collective-permute-done.8.refs_0_
  38.5 1.9 %collective-permute-done.9.refs_1_ = bf16[2,32,256]{2,1,0:T(8,128)(2,1)S(1)} collective-permute-done((bf16[2,32,256]{2,1,0:T(8,128)(2,1)S(1)}, bf16[2,32,256]{2,1,0:T(8,128)(2,1)S(1)}, u32[]{:S(2)}, u32[]{:S(2)}) %collective-permute-start.9) | collective-permute-done | bytes 32800 | tf_op jit(solution)/shard_map/ppermute | solution.py:34
  40.5 0.0 collective-permute-done.10.refs_2_
  40.5 0.0 collective-permute-done.7.across
  40.5 0.6 %shard_map.100 = (bf16[144,256]{1,0:T(8,128)(2,1)S(1)}, bf16[144,256]{1,0:T(8,128)(2,1)S(1)}, bf16[144,256]{1,0:T(8,128)(2,1)S(1)}, bf16[144,256]{1,0:T(8,128)(2...) custom-call(s32[2]{0:T(128)S(1)} %pad_add_fusion.place, f32[8,128]{1,0:T(8,128)S(1)} %get-tuple-element.98.token, ...), custom_call_target="tpu_custom_call" | custom-call | bytes 663552 | tf_op jit(solution)/shard_map/pallas_call | solution.py:138
  41.1 3.3 %collective-permute-start.12 = (bf16[144,256]{1,0:T(8,128)(2,1)S(1)}, bf16[144,256]{1,0:T(8,128)(2,1)S(1)}, u32[]{:S(2)}, u32[]{:S(2)}) collective-permute-start(bf16[144,256]{1,0:T(8,128)(2,1)S(1)} %get-tuple-element.113), channel_id=1, source_target_pairs={{0,6},{1,7},{2,4},{3,5},{4,2},{5,3},{6,0},{7,1},{8,14},{9,15},{10,... | collective-permute-start | bytes 221192 | tf_op jit(solution)/shard_map/ppermute | solution.py:34
  44.4 0.0 collective-permute-start.13
  44.4 1.2 %collective-permute-start.14 = (bf16[144,256]{1,0:T(8,128)(2,1)S(1)}, bf16[144,256]{1,0:T(8,128)(2,1)S(1)}, u32[]{:S(2)}, u32[]{:S(2)}) collective-permute-start(bf16[144,256]{1,0:T(8,128)(2,1)S(1)} %get-tuple-element.115), channel_id=1, source_target_pairs={{0,2},{1,3},{2,0},{3,1},{4,6},{5,7},{6,4},{7,5},{8,10},{9,11},{10,... | collective-permute-start | bytes 221192 | tf_op jit(solution)/shard_map/ppermute | solution.py:34
  45.6 1.1 %collective-permute-start.11 = (bf16[32,256]{1,0:T(8,128)(2,1)S(1)}, bf16[32,256]{1,0:T(8,128)(2,1)S(1)}, u32[]{:S(2)}, u32[]{:S(2)}) collective-permute-start(bf16[32,256]{1,0:T(8,128)(2,1)S(1)} %get-tuple-element.111), channel_id=1, source_target_pairs={{0,1},{1,0},{2,3},{3,2},{4,5},{5,4},{6,7},{7,6},{8,9},{9,8},{10,11... | collective-permute-start | bytes 49160 | tf_op jit(solution)/shard_map/ppermute | solution.py:34
  46.7 1.7 %shard_map.101 = (bf16[192,1152]{1,0:T(8,128)(2,1)}, f32[8,128]{1,0:T(8,128)S(1)}) custom-call(bf16[192,1152]{1,0:T(8,128)(2,1)S(1)} %get-tuple-element.63.features, f32[1,1152]{1,0:T(1,128)S(1)} %get-tuple-element.64.gain, f32[192,1152]{1,0:T(8,128)S(1)} %get-tuple-element.97.norm_back, bf16[32,256]{1,0:T(8,128)(2,1)S(1)} %get-tuple-element.105.before.tail), custom_call_target="tpu_custom_call" | custom-call | bytes 5308416 | tf_op jit(solution)/shard_map/pallas_call | solution.py:138
  48.4 0.9 %collective-permute-done.11.tail_across = bf16[32,256]{1,0:T(8,128)(2,1)S(1)} collective-permute-done((bf16[32,256]{1,0:T(8,128)(2,1)S(1)}, bf16[32,256]{1,0:T(8,128)(2,1)S(1)}, u32[]{:S(2)}, u32[]{:S(2)}) %collective-permute-start.11) | collective-permute-done | bytes 16416 | tf_op jit(solution)/shard_map/ppermute | solution.py:34
  49.3 0.0 collective-permute-done.12.refs_1_
  49.3 1.2 %collective-permute-done.13.refs_2_ = bf16[144,256]{1,0:T(8,128)(2,1)S(1)} collective-permute-done((bf16[144,256]{1,0:T(8,128)(2,1)S(1)}, bf16[144,256]{1,0:T(8,128)(2,1)S(1)}, u32[]{:S(2)}, u32[]{:S(2)}) %collective-permute-start.13) | collective-permute-done | bytes 73760 | tf_op jit(solution)/shard_map/ppermute | solution.py:34
  50.6 0.1 collective-permute-start.16
  50.7 0.7 %collective-permute-start.15 = (bf16[176,256]{1,0:T(8,128)(2,1)S(1)}, bf16[176,256]{1,0:T(8,128)(2,1)S(1)}, u32[]{:S(2)}, u32[]{:S(2)}) collective-permute-start(bf16[176,256]{1,0:T(8,128)(2,1)S(1)} %shard_map.102.before.refs_0_), channel_id=1, source_target_pairs={{0,16},{8,24},{16,0},{24,8},{1,17},{9,25},{17,1},{25,9},{2,18},{10... | collective-permute-start | bytes 270344 | tf_op jit(solution)/shard_map/ppermute | solution.py:34
  51.4 2.0 %shard_map.103 = (bf16[192,1152]{1,0:T(8,128)(2,1)}, f32[8,128]{1,0:T(8,128)S(1)}) custom-call(f32[1]{0:T(128)S(6)} %copy.10.scale, bf16[192,1152]{1,0:T(8,128)(2,1)S(1)} %get-tuple-element.107.text, bf16[384,384]{1,0:T(8,128)(2,1)S(1)} %get-tuple-element.75.weights_near, bf16[384,384]{1,0:T(8,128)(2,1)S(1)} %get-tuple-element.108.weights_far, ...), custom_call_target="tpu_custom_call" | custom-call | flops 1019215872 | bytes 2654208 | tf_op jit(solution)/shard_map/pallas_call | solution.py:138
  53.4 2.3 %collective-permute-done.15.refs_2_ = bf16[176,256]{1,0:T(8,128)(2,1)S(1)} collective-permute-done((bf16[176,256]{1,0:T(8,128)(2,1)S(1)}, bf16[176,256]{1,0:T(8,128)(2,1)S(1)}, u32[]{:S(2)}, u32[]{:S(2)}) %collective-permute-start.15) | collective-permute-done | bytes 90144 | tf_op jit(solution)/shard_map/ppermute | solution.py:34
  55.7 0.0 collective-permute-start.17
  55.7 1.3 %collective-permute-done.17.refs_3_ = bf16[176,256]{1,0:T(8,128)(2,1)S(1)} collective-permute-done((bf16[176,256]{1,0:T(8,128)(2,1)S(1)}, bf16[176,256]{1,0:T(8,128)(2,1)S(1)}, u32[]{:S(2)}, u32[]{:S(2)}) %collective-permute-start.17) | collective-permute-done | bytes 90144 | tf_op jit(solution)/shard_map/ppermute | solution.py:34
  57.0 1.5 %shard_map.104 = (f32[144,1152]{1,0:T(8,128)}, f32[1152]{0:T(1024)}) custom-call(s32[2]{0:T(128)S(1)} %pad_add_fusion.place, f32[8,128]{1,0:T(8,128)S(1)} %get-tuple-element.118.before, bf16[176,256]{1,0:T(8,128)(2,1)S(1)} %shard_map.102.before.refs_0_, bf16[176,256]{1,0:T(8,128)(2,1)S(1)} %collective-permute-done.16.refs_1_, ...), custom_call_target="tpu_custom_call" | custom-call | bytes 1327104 | tf_op jit(solution)/shard_map/pallas_call | solution.py:138
  (7 shorter events, 0.1 us)
Async XLA Ops:
  0.6 4.5 %collective-permute-start = (bf16[192,1152]{1,0:T(8,128)(2,1)}, bf16[192,1152]{1,0:T(8,128)(2,1)S(1)}, u32[]{:S(2)}, u32[]{:S(2)}) collective-permute-start(bf16[192,1152]{1,0:T(8,128)(2,1)} %bitcast.7), channel_id=1, source_target_pairs={{0,8},{8,0},{16,24},{24,16},{1,9},{9,1},{17,25},{25,17},{2,10},{10... | collective-permute-start | bytes 1327112 | tf_op jit(solution)/shard_map/ppermute | solution.py:34
  1.1 13.5 %collective-permute-start.3 = (bf16[192,1152]{1,0:T(8,128)(2,1)}, bf16[192,1152]{1,0:T(8,128)(2,1)S(1)}, u32[]{:S(2)}, u32[]{:S(2)}) collective-permute-start(bf16[192,1152]{1,0:T(8,128)(2,1)} %bitcast.8), channel_id=1, source_target_pairs={{0,16},{8,24},{16,0},{24,8},{1,17},{9,25},{17,1},{25,9},{2,18},{10... | collective-permute-start | bytes 1327112 | tf_op jit(solution)/shard_map/ppermute | solution.py:34
  5.1 1.0 %copy-start = (bf16[192,1,1152]{2,0,1:T(8,128)(2,1)S(1)}, bf16[192,1,1152]{2,0,1:T(8,128)(2,1)}, u32[]{:S(2)}) copy-start(bf16[192,1,1152]{2,0,1:T(8,128)(2,1)} %param.7) | copy-start | bytes 1327108
  6.1 1.0 %copy-start.1 = (bf16[192,1,1152]{2,0,1:T(8,128)(2,1)S(1)}, bf16[192,1,1152]{2,0,1:T(8,128)(2,1)}, u32[]{:S(2)}) copy-start(bf16[192,1,1152]{2,0,1:T(8,128)(2,1)} %param.6) | copy-start | bytes 1327108
  7.1 0.7 %copy-start.2 = (f32[1152]{0:T(1024)S(1)}, f32[1152]{0:T(1024)}, u32[]{:S(2)}) copy-start(f32[1152]{0:T(1024)} %gain_line.1) | copy-start | bytes 13828
  12.6 2.7 %collective-permute-start.1 = (bf16[192,1152]{1,0:T(8,128)(2,1)S(1)}, bf16[192,1152]{1,0:T(8,128)(2,1)S(1)}, u32[]{:S(2)}, u32[]{:S(2)}) collective-permute-start(bf16[192,1152]{1,0:T(8,128)(2,1)S(1)} %get-tuple-element.69.text_own), channel_id=1, source_target_pairs={{0,8},{8,0},{16,24},{24,16},{1,9},{9,1},{17,25},{25,17},{2,10},{10... | collective-permute-start | bytes 1327112 | tf_op jit(solution)/shard_map/ppermute | solution.py:34
  12.8 12.4 %collective-permute-start.2 = (bf16[192,1152]{1,0:T(8,128)(2,1)S(1)}, bf16[192,1152]{1,0:T(8,128)(2,1)S(1)}, u32[]{:S(2)}, u32[]{:S(2)}) collective-permute-start(bf16[192,1152]{1,0:T(8,128)(2,1)S(1)} %get-tuple-element.69.text_own), channel_id=1, source_target_pairs={{0,16},{8,24},{16,0},{24,8},{1,17},{9,25},{17,1},{25,9},{2,18},{10... | collective-permute-start | bytes 1327112 | tf_op jit(solution)/shard_map/ppermute | solution.py:34
  14.7 2.8 %collective-permute-start.4 = (bf16[160,1152]{1,0:T(8,128)(2,1)S(1)}, bf16[160,1152]{1,0:T(8,128)(2,1)S(1)}, u32[]{:S(2)}, u32[]{:S(2)}) collective-permute-start(bf16[160,1152]{1,0:T(8,128)(2,1)S(1)} %get-tuple-element.72), channel_id=1, source_target_pairs={{0,8},{8,0},{16,24},{24,16},{1,9},{9,1},{17,25},{25,17},{2,10},{10... | collective-permute-start | bytes 1105928 | tf_op jit(solution)/shard_map/ppermute | solution.py:34
  14.8 2.7 %collective-permute-start.5 = (bf16[32,1152]{1,0:T(8,128)(2,1)S(1)}, bf16[32,1152]{1,0:T(8,128)(2,1)S(1)}, u32[]{:S(2)}, u32[]{:S(2)}) collective-permute-start(bf16[32,1152]{1,0:T(8,128)(2,1)S(1)} %get-tuple-element.73), channel_id=1, source_target_pairs={{0,8},{8,0},{16,24},{24,16},{1,9},{9,1},{17,25},{25,17},{2,10},{10... | collective-permute-start | bytes 221192 | tf_op jit(solution)/shard_map/ppermute | solution.py:34
  25.2 1.9 %collective-permute-start.6 = (bf16[192,1152]{1,0:T(8,128)(2,1)S(1)}, bf16[192,1152]{1,0:T(8,128)(2,1)S(1)}, u32[]{:S(2)}, u32[]{:S(2)}) collective-permute-start(bf16[192,1152]{1,0:T(8,128)(2,1)S(1)} %collective-permute-done.2.text_unit.text_third), channel_id=1, source_target_pairs={{0,8},{8,0},{16,24},{24,16},{1,9},{9,1},{17,25},{25,17},{2,10},{10... | collective-permute-start | bytes 1327112 | tf_op jit(solution)/shard_map/ppermute | solution.py:34
  30.4 10.0 %collective-permute-start.7 = (bf16[4,144,256]{2,1,0:T(8,128)(2,1)S(1)}, bf16[4,144,256]{2,1,0:T(8,128)(2,1)S(1)}, u32[]{:S(2)}, u32[]{:S(2)}) collective-permute-start(bf16[4,144,256]{2,1,0:T(8,128)(2,1)S(1)} %get-tuple-element.100), channel_id=1, source_target_pairs={{0,1},{1,0},{2,3},{3,2},{4,5},{5,4},{6,7},{7,6},{8,9},{9,8},{10,11... | collective-permute-start | bytes 884744 | tf_op jit(solution)/shard_map/ppermute | solution.py:34
  32.0 6.5 %collective-permute-start.8 = (bf16[2,32,256]{2,1,0:T(8,128)(2,1)S(1)}, bf16[2,32,256]{2,1,0:T(8,128)(2,1)S(1)}, u32[]{:S(2)}, u32[]{:S(2)}) collective-permute-start(bf16[2,32,256]{2,1,0:T(8,128)(2,1)S(1)} %get-tuple-element.102), channel_id=1, source_target_pairs={{0,6},{1,7},{2,4},{3,5},{4,2},{5,3},{6,0},{7,1},{8,14},{9,15},{10,... | collective-permute-start | bytes 98312 | tf_op jit(solution)/shard_map/ppermute | solution.py:34
  35.6 4.8 %collective-permute-start.9 = (bf16[2,32,256]{2,1,0:T(8,128)(2,1)S(1)}, bf16[2,32,256]{2,1,0:T(8,128)(2,1)S(1)}, u32[]{:S(2)}, u32[]{:S(2)}) collective-permute-start(bf16[2,32,256]{2,1,0:T(8,128)(2,1)S(1)} %get-tuple-element.103), channel_id=1, source_target_pairs={{0,4},{1,5},{2,6},{3,7},{4,0},{5,1},{6,2},{7,3},{8,12},{9,13},{10,... | collective-permute-start | bytes 98312 | tf_op jit(solution)/shard_map/ppermute | solution.py:34
  35.7 4.8 %collective-permute-start.10 = (bf16[2,32,256]{2,1,0:T(8,128)(2,1)S(1)}, bf16[2,32,256]{2,1,0:T(8,128)(2,1)S(1)}, u32[]{:S(2)}, u32[]{:S(2)}) collective-permute-start(bf16[2,32,256]{2,1,0:T(8,128)(2,1)S(1)} %get-tuple-element.104), channel_id=1, source_target_pairs={{0,2},{1,3},{2,0},{3,1},{4,6},{5,7},{6,4},{7,5},{8,10},{9,11},{10,... | collective-permute-start | bytes 98312 | tf_op jit(solution)/shard_map/ppermute | solution.py:34
  41.1 8.2 %collective-permute-start.12 = (bf16[144,256]{1,0:T(8,128)(2,1)S(1)}, bf16[144,256]{1,0:T(8,128)(2,1)S(1)}, u32[]{:S(2)}, u32[]{:S(2)}) collective-permute-start(bf16[144,256]{1,0:T(8,128)(2,1)S(1)} %get-tuple-element.113), channel_id=1, source_target_pairs={{0,6},{1,7},{2,4},{3,5},{4,2},{5,3},{6,0},{7,1},{8,14},{9,15},{10,... | collective-permute-start | bytes 221192 | tf_op jit(solution)/shard_map/ppermute | solution.py:34
  44.4 6.2 %collective-permute-start.13 = (bf16[144,256]{1,0:T(8,128)(2,1)S(1)}, bf16[144,256]{1,0:T(8,128)(2,1)S(1)}, u32[]{:S(2)}, u32[]{:S(2)}) collective-permute-start(bf16[144,256]{1,0:T(8,128)(2,1)S(1)} %get-tuple-element.114), channel_id=1, source_target_pairs={{0,4},{1,5},{2,6},{3,7},{4,0},{5,1},{6,2},{7,3},{8,12},{9,13},{10,... | collective-permute-start | bytes 221192 | tf_op jit(solution)/shard_map/ppermute | solution.py:34
  44.4 6.2 %collective-permute-start.14 = (bf16[144,256]{1,0:T(8,128)(2,1)S(1)}, bf16[144,256]{1,0:T(8,128)(2,1)S(1)}, u32[]{:S(2)}, u32[]{:S(2)}) collective-permute-start(bf16[144,256]{1,0:T(8,128)(2,1)S(1)} %get-tuple-element.115), channel_id=1, source_target_pairs={{0,2},{1,3},{2,0},{3,1},{4,6},{5,7},{6,4},{7,5},{8,10},{9,11},{10,... | collective-permute-start | bytes 221192 | tf_op jit(solution)/shard_map/ppermute | solution.py:34
  45.6 3.7 %collective-permute-start.11 = (bf16[32,256]{1,0:T(8,128)(2,1)S(1)}, bf16[32,256]{1,0:T(8,128)(2,1)S(1)}, u32[]{:S(2)}, u32[]{:S(2)}) collective-permute-start(bf16[32,256]{1,0:T(8,128)(2,1)S(1)} %get-tuple-element.111), channel_id=1, source_target_pairs={{0,1},{1,0},{2,3},{3,2},{4,5},{5,4},{6,7},{7,6},{8,9},{9,8},{10,11... | collective-permute-start | bytes 49160 | tf_op jit(solution)/shard_map/ppermute | solution.py:34
  50.6 5.1 %collective-permute-start.16 = (bf16[176,256]{1,0:T(8,128)(2,1)S(1)}, bf16[176,256]{1,0:T(8,128)(2,1)S(1)}, u32[]{:S(2)}, u32[]{:S(2)}) collective-permute-start(bf16[176,256]{1,0:T(8,128)(2,1)S(1)} %shard_map.102.before.refs_0_), channel_id=1, source_target_pairs={{0,8},{8,0},{16,24},{24,16},{1,9},{9,1},{17,25},{25,17},{2,10},{10... | collective-permute-start | bytes 270344 | tf_op jit(solution)/shard_map/ppermute | solution.py:34
  50.7 5.0 %collective-permute-start.15 = (bf16[176,256]{1,0:T(8,128)(2,1)S(1)}, bf16[176,256]{1,0:T(8,128)(2,1)S(1)}, u32[]{:S(2)}, u32[]{:S(2)}) collective-permute-start(bf16[176,256]{1,0:T(8,128)(2,1)S(1)} %shard_map.102.before.refs_0_), channel_id=1, source_target_pairs={{0,16},{8,24},{16,0},{24,8},{1,17},{9,25},{17,1},{25,9},{2,18},{10... | collective-permute-start | bytes 270344 | tf_op jit(solution)/shard_map/ppermute | solution.py:34
  55.7 1.3 %collective-permute-start.17 = (bf16[176,256]{1,0:T(8,128)(2,1)S(1)}, bf16[176,256]{1,0:T(8,128)(2,1)S(1)}, u32[]{:S(2)}, u32[]{:S(2)}) collective-permute-start(bf16[176,256]{1,0:T(8,128)(2,1)S(1)} %collective-permute-done.15.refs_2_), channel_id=1, source_target_pairs={{0,8},{8,0},{16,24},{24,16},{1,9},{9,1},{17,25},{25,17},{2,10},{10... | collective-permute-start | bytes 270344 | tf_op jit(solution)/shard_map/ppermute | solution.py:34

commit v14 on v13

--- a/solution.py
+++ b/solution.py
@@ -208,20 +208,20 @@
     return jnp.sum(total, axis=0, keepdims=True)
 
 
-def take_columns(place, source, target):
+def take_columns(source, target):
     members = source.shape[1] // target.shape[1]
     full = target.shape[1] // LANES * LANES
     rest = target.shape[1] - full
-    target[:, :full] = source[:, pl.ds(pl.multiple_of(place[0] * full, LANES), full)]
+    target[:, :full] = source[:, pl.ds(pl.multiple_of(lax.axis_index("loop") * full, LANES), full)]
     for member in range(members):
 
-        @pl.when(place[0] == member)
+        @pl.when(lax.axis_index("loop") == member)
         def _():
             target[:, full:] = source[:, members * full + member * rest : members * full + (member + 1) * rest]
 
 
 def near_body(
-    scale, bias, place, f0_far, proj_far, t0_far, f1, gain_line,
+    scale, bias, f0_far, proj_far, t0_far, f1, gain_line,
     f0, proj, t0, gain, normed, unit, factors, text_unit, token, projected, semaphores,
 ):
     rows = f0.shape[0]
@@ -245,7 +245,7 @@
 
 
 def near_pairs_body(
-    scale, bias, place, normed, unit, factors, text_own, t1, proj, before,
+    scale, bias, normed, unit, factors, text_own, t1, proj, before,
     text_unit, normed_turned, turned, unit_turned, inverse, text_columns, weights, totals, proj_columns, token, dots,
 ):
     token[...] = jnp.zeros_like(token)
@@ -254,20 +254,20 @@
     text_unit[rows:, :] = t1[...]
     dots[...] = dot(text_unit[...], unit[...], LAST)
     totals[...] = weigh(dots, scale[0], bias[0], 0, weights)
-    take_columns(place, text_unit, text_columns)
-    take_columns(place, proj, proj_columns)
-    turn_own(place, unit, factors, turned, unit_turned, inverse)
+    take_columns(text_unit, text_columns)
+    take_columns(proj, proj_columns)
+    turn_own(unit, factors, turned, unit_turned, inverse)
     normed_turned[...] = normed[...].T
 
 
-def turn_own(place, unit, factors, turned, unit_turned, inverse):
+def turn_own(unit, factors, turned, unit_turned, inverse):
     columns = unit_turned.shape[0]
     full = columns // LANES * LANES
     rest = columns - full
     turned[...] = unit[...].T
-    unit_turned[:full, :] = turned[pl.ds(pl.multiple_of(place[0] * full, LANES), full), :]
+    unit_turned[:full, :] = turned[pl.ds(pl.multiple_of(lax.axis_index("loop") * full, LANES), full), :]
     begin = turned.shape[0] // columns * full
-    unit_turned[full:, :] = turned[pl.ds(pl.multiple_of(begin + place[0] * rest, BAND), rest), :]
+    unit_turned[full:, :] = turned[pl.ds(pl.multiple_of(begin + lax.axis_index("loop") * rest, BAND), rest), :]
     inverse[...] = factors[...].T[:1, :]
 
 
@@ -277,7 +277,7 @@
 
 
 def far_body(
-    scale, bias, place, f2, f3_head, f3_tail, proj, gain, text_near, text_columns, weights_near,
+    scale, bias, f2, f3_head, f3_tail, proj, gain, text_near, text_columns, weights_near,
     normed_turned, unit, turned, unit_turned, inverse, weights, totals, early_near, early_far, token,
     normed, projected, dots, factors,
 ):
@@ -289,7 +289,7 @@
     unit_into(projected, unit, 0, factors)
     dots[...] = dot(text_near[...], unit[...], LAST)
     totals[...] = weigh(dots, scale[0], bias[0], None, weights)
-    turn_own(place, unit, factors, turned, unit_turned, inverse)
+    turn_own(unit, factors, turned, unit_turned, inverse)
     normed_turned[...] = normed[...].T
     early_near[...] = dot(text_columns[...], weights_near[...], FIRST)
     early_far[...] = dot(text_columns[...], weights[...], FIRST)
@@ -297,13 +297,13 @@
 
 
 def third_body(
-    scale, bias, place, text_unit, flat_near, flat_far, totals_near, totals_far, early_near, early_far,
+    scale, bias, text_unit, flat_near, flat_far, totals_near, totals_far, early_near, early_far,
     before, weights, back_near, back_far, totals,
     text_columns, dots,
 ):
     rows = text_unit.shape[0]
     near = 2 * rows
-    take_columns(place, text_unit, text_columns)
+    take_columns(text_unit, text_columns)
     dots[:, :near] = dot(text_unit[...], flat_near[...])
     dots[:, near:] = dot(text_unit[...], flat_far[...])
     added = weigh(dots, scale[0], bias[0], near, weights)
@@ -330,7 +330,7 @@
 
 
 def partial_body(
-    members, groups, lead, scale, bias, place, text_unit, flat_near, flat_far, totals, back_near, back_far, unit_turned_near,
+    members, groups, lead, scale, bias, text_unit, flat_near, flat_far, totals, back_near, back_far, unit_turned_near,
     unit_turned_far, inverse_near, inverse_far, turned_near, turned_far, proj_columns, gain,
     across, keep_lead, keep_tail, *refs,
 ):
@@ -342,7 +342,7 @@
     columns = width // members
     count, full = packed.shape[1:]
     scale, bias = scale[0], bias[0]
-    take_columns(place, text_unit, text_columns)
+    take_columns(text_unit, text_columns)
     dots[:, :near] = dot(text_unit[...], flat_near[...])
     dots[:, near:] = dot(text_unit[...], flat_far[...])
     total = totals[...] + weigh(dots, scale, bias, near + rows, weights)
@@ -376,7 +376,7 @@
     for group in range(groups):
         packed[group, count - BAND :, full - LANES :] = gain_tile
 
-    own = place[1]
+    own = lax.axis_index("rep")
     for step in range(groups // 2):
         across[step] = packed[own ^ 1 ^ (2 * step), :lead, :]
         keep_lead[step] = packed[own ^ (2 * step), :lead, :]
@@ -448,13 +448,13 @@
     token[...] = jnp.zeros_like(token)
 
 
-def first_sum_body(place, token, keep_lead, across, keep_tail, *refs):
+def first_sum_body(token, keep_lead, across, keep_tail, *refs):
     steps = keep_lead.shape[0]
     along, refs = refs[: steps - 1], refs[steps - 1 :]
     leads, (tail, tail_across, ordered) = refs[:steps], refs[steps:]
     for step in range(steps):
         leads[step][...] = (keep_lead[step].astype(F32) + across[step].astype(F32)).astype(BF16)
-    own = place[1] // 2
+    own = lax.axis_index("rep") // 2
     ordered[own] = keep_tail[...]
     for step in range(1, steps):
         ordered[own ^ step] = along[steps - 1 - step][...]
@@ -475,14 +475,14 @@
     total[split:, :] = (tail[...].astype(F32) + tail_across[...].astype(F32)).astype(BF16)
 
 
-def finish_body(members, place, before, *refs):
+def finish_body(members, before, *refs):
     packets, (proj_grad, gain_gradient, ordered) = refs[:members], refs[members:]
     count, full = packets[0].shape
     rows, width = proj_grad.shape
     rest = width // members - full
     per_band = full // rest
     for k in range(members):
-        member = place[0] ^ k
+        member = lax.axis_index("loop") ^ k
         proj_grad[:, pl.ds(pl.multiple_of(member * full, LANES), full)] = packets[k][:rows, :].astype(F32)
         ordered[member] = packets[k][rows:, :].astype(F32)
     tails = []
@@ -502,7 +502,6 @@
 def local_four(features, text, proj, gain, scale, bias):
     members = lax.axis_size("loop")
     groups = lax.axis_size("rep")
-    place = jnp.stack([lax.axis_index("loop"), lax.axis_index("rep")]).astype(jnp.int32)
     rows, width = features.shape[0], features.shape[2]
     near, every = 2 * rows, 4 * rows
     columns = width // members
@@ -528,12 +527,12 @@
         near_body,
         [half, kept, half, ((1, width), F32), wide, wide, ((near, LANES), F32), half, TOKEN],
         [((near, width), F32)],
-        smem=3,
+        smem=2,
         hbm=3,
         limit=46,
         flops=2 * near * width * width,
         moved=8 * near * width,
-    )(scale, bias, place, f0, proj, t0, f1, gain)
+    )(scale, bias, f0, proj, t0, f1, gain)
 
     t2 = send(text_own, "loop", lambda p: p ^ 2)
     t1 = send(text_own, "loop", lambda p: p ^ 1)
@@ -549,10 +548,10 @@
         near_pairs_body,
         [wide, turned, turned, mine, line, part, square, line, ((width, columns), BF16), TOKEN],
         [((near, near), F32)],
-        smem=3,
+        smem=2,
         flops=1000,
         moved=1000,
-    )(scale, bias, place, normed_near, unit_near, factors, text_own, t1, proj_kept, token)
+    )(scale, bias, normed_near, unit_near, factors, text_own, t1, proj_kept, token)
 
     back_kind = ((columns, near), F32)
     (
@@ -562,11 +561,11 @@
         far_body,
         [turned, wide, turned, mine, line, square, line, back_kind, back_kind, TOKEN],
         [wide, ((near, width), F32), ((near, near), F32), ((near, LANES), F32)],
-        smem=3,
+        smem=2,
         flops=1000,
         moved=1000,
     )(
-        scale, bias, place, f2, f3_head, f3_tail, proj_kept, gain_row, text_near, text_columns_near, weights_near,
+        scale, bias, f2, f3_head, f3_tail, proj_kept, gain_row, text_near, text_columns_near, weights_near,
     )
 
     t2_after, token = lax.optimization_barrier((t2, token))
@@ -577,22 +576,22 @@
         third_body,
         [narrow, back_kind, back_kind, ((1, every), F32)],
         [((rows, columns), BF16), ((rows, every), F32)],
-        smem=3,
+        smem=2,
         flops=2 * near * width * width,
         moved=8 * near * width,
     )(
-        scale, bias, place, t2, flat_near, flat_far, totals_near, totals_far, early_near, early_far, token,
+        scale, bias, t2, flat_near, flat_far, totals_near, totals_far, early_near, early_far, token,
     )
 
     outs = call(
         functools.partial(partial_body, members, groups, lead),
         [((steps, lead, full), BF16)] * 2 + [((2, tail, full), BF16)] * steps + [narrow],
         [((rows, columns), BF16), ((rows, every), F32), ((groups,) + packet, BF16)],
-        smem=3,
+        smem=2,
         flops=4 * near * width * width,
         moved=16 * near * width,
     )(
-        scale, bias, place, t3, flat_near, flat_far, totals, back_near, back_far, unit_turned_near, unit_turned_far,
+        scale, bias, t3, flat_near, flat_far, totals, back_near, back_far, unit_turned_near, unit_turned_far,
         inverse_near, inverse_far, turned_near, turned_far, proj_columns, gain_row,
     )
     across, keep_lead, keep_tail = outs[:3]
@@ -617,9 +616,8 @@
         first_sum_body,
         [((lead, full), BF16)] * steps + [((tail, full), BF16)] * 2,
         [((steps, 2, tail, full), BF16)],
-        smem=1,
         moved=4 * each * width,
-    )(place, token, keep_lead, across, keep_tail, *along)
+    )(token, keep_lead, across, keep_tail, *along)
     leads = [outs[0]] + [send(outs[step], "rep", lambda p: p ^ (2 * step)) for step in reversed(range(1, steps))]
     tail_across = send(outs[steps + 1], "rep", lambda p: p ^ 1)
 
@@ -633,7 +631,6 @@
         moved=4 * each * width,
     )(token, outs[steps], tail_across, *leads)
     far_block = send(reduced, "loop", lambda p: p ^ 2)
-    near_block = send(reduced, "loop", lambda p: p ^ 1)
     text_grad, token = call(
         text_body,
         [half, TOKEN],
@@ -642,16 +639,16 @@
         flops=2 * near * width * width,
         moved=6 * near * width,
     )(scale, t0_kept, weights_near, weights_far, unit_near, unit_far, reduced)
-    far_block, token = lax.optimization_barrier((far_block, token))
+    reduced, token = lax.optimization_barrier((reduced, token))
+    near_block = send(reduced, "loop", lambda p: p ^ 1)
     blocks = [reduced, near_block, far_block, send(far_block, "loop", lambda p: p ^ 1)]
 
     proj_grad, gain_gradient = call(
         functools.partial(finish_body, members),
         [((each, width), F32), ((width,), F32)],
         [((members, bands * BAND, full), F32)],
-        smem=1,
         moved=8 * each * width,
-    )(place, token, *blocks)
+    )(token, *blocks)
     return feature_grad[:, None, :], text_grad[:, None, :], proj_grad, gain_gradient
 
 

time: 58.8 us -> 55.1 us (0.937)
  Pallas kernels: 25.3 us -> 21.6 us
    pallas_call x12, Pallas kernels: 25.3 us -> 21.6 us  [run(): pl.pallas_call(body, out_shape=[jax.ShapeDtypeStruct(shape, kind) for sha...]
  transfers between devices with their start and end apart: 18 -> 18, of which waited for: 7 -> 8; matrix products, arithmetic and copies ran while one was open for 0% -> 0% of each run, Pallas kernels for 34% -> 32%
where the time goes in v14:
time: 55.1 us; the launch traced here: 54.8 us
  Pallas kernels  21.6 us (39%)
  starting transfers between devices  16.9 us (31%)
  waiting for transfers between devices  11.5 us (21%)
  local copies, waits for them, and re-layouts  2.72 us (5%)
  between operations  2.05 us (4%)
    pallas_call x12, Pallas kernels, run(): pl.pallas_call(body, out_shape=[jax.ShapeDtypeStruct(shape, kind) for sha...  21.6 us
    ppermute x18, starting transfers between devices, send(): return lax.ppermute(value, axis, [(p, target(p)) for p in range(count)])  16.9 us
    ppermute x18, waiting for transfers between devices, send(): return lax.ppermute(value, axis, [(p, target(p)) for p in range(count)])  11.5 us
    unnamed x6, local copies, waits for them, and re-layouts  2.72 us
  transfers between devices with their start and end apart: 18, of which 8 were waited for; matrix products, arithmetic and copies ran while one was open for 0% of the time, Pallas kernels for 32%

profile of v14, /device:TPU:0, one launch (start us, length us, event | category | flops | bytes accessed | tf_op | source)
XLA Modules:
  0.0 54.8 jit_solution(11276788461657165718)
XLA Ops:
  0.6 0.5 collective-permute-start
  1.2 2.6 %collective-permute-start.3 = (bf16[192,1152]{1,0:T(8,128)(2,1)}, bf16[192,1152]{1,0:T(8,128)(2,1)S(1)}, u32[]{:S(2)}, u32[]{:S(2)}) collective-permute-start(bf16[192,1152]{1,0:T(8,128)(2,1)} %bitcast.6), channel_id=1, source_target_pairs={{0,16},{8,24},{16,0},{24,8},{1,17},{9,25},{17,1},{25,9},{2,18},{10... | collective-permute-start | bytes 1327112 | tf_op jit(solution)/shard_map/ppermute | solution.py:34
  5.0 0.0 collective-permute-done.f1
  5.0 1.0 %copy-done = bf16[192,1,1152]{2,0,1:T(8,128)(2,1)S(1)} copy-done((bf16[192,1,1152]{2,0,1:T(8,128)(2,1)S(1)}, bf16[192,1,1152]{2,0,1:T(8,128)(2,1)}, u32[]{:S(2)}) %copy-start) | copy-done | bytes 442392
  6.0 1.0 %copy-done.1 = bf16[192,1,1152]{2,0,1:T(8,128)(2,1)S(1)} copy-done((bf16[192,1,1152]{2,0,1:T(8,128)(2,1)S(1)}, bf16[192,1,1152]{2,0,1:T(8,128)(2,1)}, u32[]{:S(2)}) %copy-start.1) | copy-done | bytes 442392
  7.1 0.7 %copy-done.2 = f32[1152]{0:T(1024)S(1)} copy-done((f32[1152]{0:T(1024)S(1)}, f32[1152]{0:T(1024)}, u32[]{:S(2)}) %copy-start.2) | copy-done | bytes 4632
  7.7 4.2 %shard_map.93 = (bf16[192,1152]{1,0:T(8,128)(2,1)S(1)}, bf16[1152,1152]{1,0:T(8,128)(2,1)S(1)}, bf16[192,1152]{1,0:T(8,128)(2,1)S(1)}, f32[1,1152]{1,0:T(1,128)S...) custom-call(f32[1]{0:T(128)S(6)} %copy.10.scale, ...), custom_call_target="tpu_custom_call" | custom-call | flops 1019215872 | bytes 3538944 | tf_op jit(solution)/shard_map/pallas_call | solution.py:138
  12.0 0.2 collective-permute-start.1
  12.2 0.6 %collective-permute-start.2 = (bf16[192,1152]{1,0:T(8,128)(2,1)S(1)}, bf16[192,1152]{1,0:T(8,128)(2,1)S(1)}, u32[]{:S(2)}, u32[]{:S(2)}) collective-permute-start(bf16[192,1152]{1,0:T(8,128)(2,1)S(1)} %get-tuple-element.69.text_own), channel_id=1, source_target_pairs={{0,16},{8,24},{16,0},{24,8},{1,17},{9,25},{17,1},{25,9},{2,18},{10... | collective-permute-start | bytes 1327112 | tf_op jit(solution)/shard_map/ppermute | solution.py:34
  12.8 1.9 %collective-permute-done.3.f2 = bf16[192,1152]{1,0:T(8,128)(2,1)S(1)} collective-permute-done((bf16[192,1152]{1,0:T(8,128)(2,1)}, bf16[192,1152]{1,0:T(8,128)(2,1)S(1)}, u32[]{:S(2)}, u32[]{:S(2)}) %collective-permute-start.3) | collective-permute-done | bytes 442400 | tf_op jit(solution)/shard_map/ppermute | solution.py:34
  14.7 0.1 collective-permute-start.4
  14.8 0.5 collective-permute-start.5
  15.3 0.0 collective-permute-done.1.t1
  15.3 1.7 %shard_map.94 = (bf16[384,1152]{1,0:T(8,128)(2,1)S(1)}, bf16[1152,384]{1,0:T(8,128)(2,1)S(1)}, bf16[1152,384]{1,0:T(8,128)(2,1)S(1)}, bf16[288,384]{1,0:T(8,128)...) custom-call(f32[1]{0:T(128)S(6)} %copy.10.scale, ...), custom_call_target="tpu_custom_call" | custom-call | flops 1000 | bytes 1000 | tf_op jit(solution)/shard_map/pallas_call | solution.py:138
  17.0 0.0 collective-permute-done.5.f3_tail
  17.0 0.0 collective-permute-done.4.f3_head
  17.0 4.6 %shard_map.96 = (bf16[1152,384]{1,0:T(8,128)(2,1)S(1)}, bf16[384,1152]{1,0:T(8,128)(2,1)S(1)}, bf16[1152,384]{1,0:T(8,128)(2,1)S(1)}, bf16[288,384]{1,0:T(8,128)...) custom-call(f32[1]{0:T(128)S(6)} %copy.10.scale, ...), custom_call_target="tpu_custom_call" | custom-call | flops 1000 | bytes 1000 | tf_op jit(solution)/shard_map/pallas_call | solution.py:138
  21.7 2.9 %collective-permute-done.2.text_unit.text_third = bf16[192,1152]{1,0:T(8,128)(2,1)S(1)} collective-permute-done((bf16[192,1152]{1,0:T(8,128)(2,1)S(1)}, bf16[192,1152]{1,0:T(8,128)(2,1)S(1)}, u32[]{:S(2)}, u32[]{:S(2)}) %collective-permute-start.2) | collective-permute-done | bytes 442400 | tf_op jit(solution)/shard_map/ppermute | solution.py:34
  24.6 0.0 collective-permute-start.6
  24.6 1.3 %shard_map.97 = (bf16[192,768]{1,0:T(8,128)(2,1)S(1)}, f32[288,384]{1,0:T(8,128)S(1)}, f32[288,384]{1,0:T(8,128)S(1)}, f32[1,768]{1,0:T(1,128)S(1)}) custom-call(f32[1]{0:T(128)S(6)} %copy.10.scale, f32[1]{0:T(128)S(6)} %copy.11.bias, bf16[192,1152]{1,0:T(8,128)(2,1)S(1)} %collective-permute-done.2.text_unit.text_third, ...), custom_call_target="tpu_custom_call" | custom-call | flops 1019215872 | bytes 3538944 | tf_op jit(solution)/shard_map/pallas_call | solution.py:138
  26.0 0.5 collective-permute-done.6.text_unit.text_fourth
  26.4 2.7 %shard_map.98 = (bf16[4,144,256]{2,1,0:T(8,128)(2,1)S(1)}, bf16[4,144,256]{2,1,0:T(8,128)(2,1)S(1)}, bf16[2,32,256]{2,1,0:T(8,128)(2,1)S(1)}, bf16[2,32,256]{2,1...) custom-call(f32[1]{0:T(128)S(6)} %copy.10.scale, ...), custom_call_target="tpu_custom_call" | custom-call | flops 2038431744 | bytes 7077888 | tf_op jit(solution)/shard_map/pallas_call | solution.py:138
  29.2 1.6 %collective-permute-start.7 = (bf16[4,144,256]{2,1,0:T(8,128)(2,1)S(1)}, bf16[4,144,256]{2,1,0:T(8,128)(2,1)S(1)}, u32[]{:S(2)}, u32[]{:S(2)}) collective-permute-start(bf16[4,144,256]{2,1,0:T(8,128)(2,1)S(1)} %get-tuple-element.100), channel_id=1, source_target_pairs={{0,1},{1,0},{2,3},{3,2},{4,5},{5,4},{6,7},{7,6},{8,9},{9,8},{10,11... | collective-permute-start | bytes 884744 | tf_op jit(solution)/shard_map/ppermute | solution.py:34
  30.7 3.6 %collective-permute-start.8 = (bf16[2,32,256]{2,1,0:T(8,128)(2,1)S(1)}, bf16[2,32,256]{2,1,0:T(8,128)(2,1)S(1)}, u32[]{:S(2)}, u32[]{:S(2)}) collective-permute-start(bf16[2,32,256]{2,1,0:T(8,128)(2,1)S(1)} %get-tuple-element.102), channel_id=1, source_target_pairs={{0,6},{1,7},{2,4},{3,5},{4,2},{5,3},{6,0},{7,1},{8,14},{9,15},{10,... | collective-permute-start | bytes 98312 | tf_op jit(solution)/shard_map/ppermute | solution.py:34
  34.3 0.0 collective-permute-start.9
  34.3 0.8 %collective-permute-start.10 = (bf16[2,32,256]{2,1,0:T(8,128)(2,1)S(1)}, bf16[2,32,256]{2,1,0:T(8,128)(2,1)S(1)}, u32[]{:S(2)}, u32[]{:S(2)}) collective-permute-start(bf16[2,32,256]{2,1,0:T(8,128)(2,1)S(1)} %get-tuple-element.104), channel_id=1, source_target_pairs={{0,2},{1,3},{2,0},{3,1},{4,6},{5,7},{6,4},{7,5},{8,10},{9,11},{10,... | collective-permute-start | bytes 98312 | tf_op jit(solution)/shard_map/ppermute | solution.py:34
  35.1 2.1 %shard_map.99 = (f32[192,1152]{1,0:T(8,128)S(1)}, f32[8,128]{1,0:T(8,128)S(1)}) custom-call(f32[1]{0:T(128)S(6)} %copy.10.scale, bf16[1152,1152]{1,0:T(8,128)(2,1)S(1)} %get-tuple-element.65.proj, bf16[384,1152]{1,0:T(8,128)(2,1)S(1)} %get-tuple-element.71.text_near, bf16[192,1152]{1,0:T(8,128)(2,1)S(1)} %collective-permute-done.2.text_unit.text_third, ...), custom_call_target="tpu_custom_call" | custom-call | flops 2038431744 | bytes 5308416 | tf_op jit(solution)/shard_map/pallas_call | solution.py:138
  37.2 0.0 collective-permute-done.8.refs_0_
  37.2 1.9 %collective-permute-done.9.refs_1_ = bf16[2,32,256]{2,1,0:T(8,128)(2,1)S(1)} collective-permute-done((bf16[2,32,256]{2,1,0:T(8,128)(2,1)S(1)}, bf16[2,32,256]{2,1,0:T(8,128)(2,1)S(1)}, u32[]{:S(2)}, u32[]{:S(2)}) %collective-permute-start.9) | collective-permute-done | bytes 32800 | tf_op jit(solution)/shard_map/ppermute | solution.py:34
  39.2 0.0 collective-permute-done.10.refs_2_
  39.2 0.0 collective-permute-done.7.across
  39.2 0.1 shard_map.100
  39.3 2.9 %collective-permute-start.12 = (bf16[144,256]{1,0:T(8,128)(2,1)S(1)}, bf16[144,256]{1,0:T(8,128)(2,1)S(1)}, u32[]{:S(2)}, u32[]{:S(2)}) collective-permute-start(bf16[144,256]{1,0:T(8,128)(2,1)S(1)} %get-tuple-element.113), channel_id=1, source_target_pairs={{0,6},{1,7},{2,4},{3,5},{4,2},{5,3},{6,0},{7,1},{8,14},{9,15},{10,... | collective-permute-start | bytes 221192 | tf_op jit(solution)/shard_map/ppermute | solution.py:34
  42.1 0.0 collective-permute-start.13
  42.1 1.6 %collective-permute-start.14 = (bf16[144,256]{1,0:T(8,128)(2,1)S(1)}, bf16[144,256]{1,0:T(8,128)(2,1)S(1)}, u32[]{:S(2)}, u32[]{:S(2)}) collective-permute-start(bf16[144,256]{1,0:T(8,128)(2,1)S(1)} %get-tuple-element.115), channel_id=1, source_target_pairs={{0,2},{1,3},{2,0},{3,1},{4,6},{5,7},{6,4},{7,5},{8,10},{9,11},{10,... | collective-permute-start | bytes 221192 | tf_op jit(solution)/shard_map/ppermute | solution.py:34
  43.7 0.7 %collective-permute-start.11 = (bf16[32,256]{1,0:T(8,128)(2,1)S(1)}, bf16[32,256]{1,0:T(8,128)(2,1)S(1)}, u32[]{:S(2)}, u32[]{:S(2)}) collective-permute-start(bf16[32,256]{1,0:T(8,128)(2,1)S(1)} %get-tuple-element.111), channel_id=1, source_target_pairs={{0,1},{1,0},{2,3},{3,2},{4,5},{5,4},{6,7},{7,6},{8,9},{9,8},{10,11... | collective-permute-start | bytes 49160 | tf_op jit(solution)/shard_map/ppermute | solution.py:34
  44.4 1.7 %shard_map.101 = (bf16[192,1152]{1,0:T(8,128)(2,1)}, f32[8,128]{1,0:T(8,128)S(1)}) custom-call(bf16[192,1152]{1,0:T(8,128)(2,1)S(1)} %get-tuple-element.63.features, f32[1,1152]{1,0:T(1,128)S(1)} %get-tuple-element.64.gain, f32[192,1152]{1,0:T(8,128)S(1)} %get-tuple-element.97.norm_back, bf16[32,256]{1,0:T(8,128)(2,1)S(1)} %get-tuple-element.105.before.tail), custom_call_target="tpu_custom_call" | custom-call | bytes 5308416 | tf_op jit(solution)/shard_map/pallas_call | solution.py:138
  46.1 1.3 %collective-permute-done.11.tail_across = bf16[32,256]{1,0:T(8,128)(2,1)S(1)} collective-permute-done((bf16[32,256]{1,0:T(8,128)(2,1)S(1)}, bf16[32,256]{1,0:T(8,128)(2,1)S(1)}, u32[]{:S(2)}, u32[]{:S(2)}) %collective-permute-start.11) | collective-permute-done | bytes 16416 | tf_op jit(solution)/shard_map/ppermute | solution.py:34
  47.5 0.0 collective-permute-done.12.refs_1_
  47.5 0.4 collective-permute-done.13.refs_2_
  47.9 0.0 collective-permute-done.14.refs_3_
  47.9 1.3 %collective-permute-start.16 = (bf16[176,256]{1,0:T(8,128)(2,1)S(1)}, bf16[176,256]{1,0:T(8,128)(2,1)S(1)}, u32[]{:S(2)}, u32[]{:S(2)}) collective-permute-start(bf16[176,256]{1,0:T(8,128)(2,1)S(1)} %shard_map.102.before.refs_0_), channel_id=1, source_target_pairs={{0,16},{8,24},{16,0},{24,8},{1,17},{9,25},{17,1},{25,9},{2,18},{10... | collective-permute-start | bytes 270344 | tf_op jit(solution)/shard_map/ppermute | solution.py:34
  49.2 2.0 %shard_map.103 = (bf16[192,1152]{1,0:T(8,128)(2,1)}, f32[8,128]{1,0:T(8,128)S(1)}) custom-call(f32[1]{0:T(128)S(6)} %copy.10.scale, bf16[192,1152]{1,0:T(8,128)(2,1)S(1)} %get-tuple-element.107.text, bf16[384,384]{1,0:T(8,128)(2,1)S(1)} %get-tuple-element.75.weights_near, bf16[384,384]{1,0:T(8,128)(2,1)S(1)} %get-tuple-element.108.weights_far, ...), custom_call_target="tpu_custom_call" | custom-call | flops 1019215872 | bytes 2654208 | tf_op jit(solution)/shard_map/pallas_call | solution.py:138
  51.2 0.0 collective-permute-start.15
  51.2 1.3 %collective-permute-done.16.refs_2_ = bf16[176,256]{1,0:T(8,128)(2,1)S(1)} collective-permute-done((bf16[176,256]{1,0:T(8,128)(2,1)S(1)}, bf16[176,256]{1,0:T(8,128)(2,1)S(1)}, u32[]{:S(2)}, u32[]{:S(2)}) %collective-permute-start.16) | collective-permute-done | bytes 90144 | tf_op jit(solution)/shard_map/ppermute | solution.py:34
  52.5 0.0 collective-permute-start.17
  52.5 1.3 %collective-permute-done.17.refs_3_ = bf16[176,256]{1,0:T(8,128)(2,1)S(1)} collective-permute-done((bf16[176,256]{1,0:T(8,128)(2,1)S(1)}, bf16[176,256]{1,0:T(8,128)(2,1)S(1)}, u32[]{:S(2)}, u32[]{:S(2)}) %collective-permute-start.17) | collective-permute-done | bytes 90144 | tf_op jit(solution)/shard_map/ppermute | solution.py:34
  53.8 1.0 %shard_map.104 = (f32[144,1152]{1,0:T(8,128)}, f32[1152]{0:T(1024)}) custom-call(f32[8,128]{1,0:T(8,128)S(1)} %get-tuple-element.118.before, bf16[176,256]{1,0:T(8,128)(2,1)S(1)} %shard_map.102.before.refs_0_, bf16[176,256]{1,0:T(8,128)(2,1)S(1)} %collective-permute-done.15.refs_1_, bf16[176,256]{1,0:T(8,128)(2,1)S(1)} %collective-permute-done.16.refs_2_, ...), custom_call_target="tpu_custom_call" | custom-call | bytes 1327104 | tf_op jit(solution)/shard_map/pallas_call | solution.py:138
  (6 shorter events, 0.1 us)
Async XLA Ops:
  0.6 4.4 %collective-permute-start = (bf16[192,1152]{1,0:T(8,128)(2,1)}, bf16[192,1152]{1,0:T(8,128)(2,1)S(1)}, u32[]{:S(2)}, u32[]{:S(2)}) collective-permute-start(bf16[192,1152]{1,0:T(8,128)(2,1)} %bitcast.5), channel_id=1, source_target_pairs={{0,8},{8,0},{16,24},{24,16},{1,9},{9,1},{17,25},{25,17},{2,10},{10... | collective-permute-start | bytes 1327112 | tf_op jit(solution)/shard_map/ppermute | solution.py:34
  1.2 13.5 %collective-permute-start.3 = (bf16[192,1152]{1,0:T(8,128)(2,1)}, bf16[192,1152]{1,0:T(8,128)(2,1)S(1)}, u32[]{:S(2)}, u32[]{:S(2)}) collective-permute-start(bf16[192,1152]{1,0:T(8,128)(2,1)} %bitcast.6), channel_id=1, source_target_pairs={{0,16},{8,24},{16,0},{24,8},{1,17},{9,25},{17,1},{25,9},{2,18},{10... | collective-permute-start | bytes 1327112 | tf_op jit(solution)/shard_map/ppermute | solution.py:34
  5.0 1.0 %copy-start = (bf16[192,1,1152]{2,0,1:T(8,128)(2,1)S(1)}, bf16[192,1,1152]{2,0,1:T(8,128)(2,1)}, u32[]{:S(2)}) copy-start(bf16[192,1,1152]{2,0,1:T(8,128)(2,1)} %param.7) | copy-start | bytes 1327108
  6.0 1.0 %copy-start.1 = (bf16[192,1,1152]{2,0,1:T(8,128)(2,1)S(1)}, bf16[192,1,1152]{2,0,1:T(8,128)(2,1)}, u32[]{:S(2)}) copy-start(bf16[192,1,1152]{2,0,1:T(8,128)(2,1)} %param.6) | copy-start | bytes 1327108
  7.1 0.7 %copy-start.2 = (f32[1152]{0:T(1024)S(1)}, f32[1152]{0:T(1024)}, u32[]{:S(2)}) copy-start(f32[1152]{0:T(1024)} %gain_line.1) | copy-start | bytes 13828
  12.0 3.3 %collective-permute-start.1 = (bf16[192,1152]{1,0:T(8,128)(2,1)S(1)}, bf16[192,1152]{1,0:T(8,128)(2,1)S(1)}, u32[]{:S(2)}, u32[]{:S(2)}) collective-permute-start(bf16[192,1152]{1,0:T(8,128)(2,1)S(1)} %get-tuple-element.69.text_own), channel_id=1, source_target_pairs={{0,8},{8,0},{16,24},{24,16},{1,9},{9,1},{17,25},{25,17},{2,10},{10... | collective-permute-start | bytes 1327112 | tf_op jit(solution)/shard_map/ppermute | solution.py:34
  12.2 12.4 %collective-permute-start.2 = (bf16[192,1152]{1,0:T(8,128)(2,1)S(1)}, bf16[192,1152]{1,0:T(8,128)(2,1)S(1)}, u32[]{:S(2)}, u32[]{:S(2)}) collective-permute-start(bf16[192,1152]{1,0:T(8,128)(2,1)S(1)} %get-tuple-element.69.text_own), channel_id=1, source_target_pairs={{0,16},{8,24},{16,0},{24,8},{1,17},{9,25},{17,1},{25,9},{2,18},{10... | collective-permute-start | bytes 1327112 | tf_op jit(solution)/shard_map/ppermute | solution.py:34
  14.7 2.3 %collective-permute-start.4 = (bf16[160,1152]{1,0:T(8,128)(2,1)S(1)}, bf16[160,1152]{1,0:T(8,128)(2,1)S(1)}, u32[]{:S(2)}, u32[]{:S(2)}) collective-permute-start(bf16[160,1152]{1,0:T(8,128)(2,1)S(1)} %get-tuple-element.72), channel_id=1, source_target_pairs={{0,8},{8,0},{16,24},{24,16},{1,9},{9,1},{17,25},{25,17},{2,10},{10... | collective-permute-start | bytes 1105928 | tf_op jit(solution)/shard_map/ppermute | solution.py:34
  14.8 2.2 %collective-permute-start.5 = (bf16[32,1152]{1,0:T(8,128)(2,1)S(1)}, bf16[32,1152]{1,0:T(8,128)(2,1)S(1)}, u32[]{:S(2)}, u32[]{:S(2)}) collective-permute-start(bf16[32,1152]{1,0:T(8,128)(2,1)S(1)} %get-tuple-element.73), channel_id=1, source_target_pairs={{0,8},{8,0},{16,24},{24,16},{1,9},{9,1},{17,25},{25,17},{2,10},{10... | collective-permute-start | bytes 221192 | tf_op jit(solution)/shard_map/ppermute | solution.py:34
  24.6 1.8 %collective-permute-start.6 = (bf16[192,1152]{1,0:T(8,128)(2,1)S(1)}, bf16[192,1152]{1,0:T(8,128)(2,1)S(1)}, u32[]{:S(2)}, u32[]{:S(2)}) collective-permute-start(bf16[192,1152]{1,0:T(8,128)(2,1)S(1)} %collective-permute-done.2.text_unit.text_third), channel_id=1, source_target_pairs={{0,8},{8,0},{16,24},{24,16},{1,9},{9,1},{17,25},{25,17},{2,10},{10... | collective-permute-start | bytes 1327112 | tf_op jit(solution)/shard_map/ppermute | solution.py:34
  29.2 10.0 %collective-permute-start.7 = (bf16[4,144,256]{2,1,0:T(8,128)(2,1)S(1)}, bf16[4,144,256]{2,1,0:T(8,128)(2,1)S(1)}, u32[]{:S(2)}, u32[]{:S(2)}) collective-permute-start(bf16[4,144,256]{2,1,0:T(8,128)(2,1)S(1)} %get-tuple-element.100), channel_id=1, source_target_pairs={{0,1},{1,0},{2,3},{3,2},{4,5},{5,4},{6,7},{7,6},{8,9},{9,8},{10,11... | collective-permute-start | bytes 884744 | tf_op jit(solution)/shard_map/ppermute | solution.py:34
  30.7 6.5 %collective-permute-start.8 = (bf16[2,32,256]{2,1,0:T(8,128)(2,1)S(1)}, bf16[2,32,256]{2,1,0:T(8,128)(2,1)S(1)}, u32[]{:S(2)}, u32[]{:S(2)}) collective-permute-start(bf16[2,32,256]{2,1,0:T(8,128)(2,1)S(1)} %get-tuple-element.102), channel_id=1, source_target_pairs={{0,6},{1,7},{2,4},{3,5},{4,2},{5,3},{6,0},{7,1},{8,14},{9,15},{10,... | collective-permute-start | bytes 98312 | tf_op jit(solution)/shard_map/ppermute | solution.py:34
  34.3 4.8 %collective-permute-start.9 = (bf16[2,32,256]{2,1,0:T(8,128)(2,1)S(1)}, bf16[2,32,256]{2,1,0:T(8,128)(2,1)S(1)}, u32[]{:S(2)}, u32[]{:S(2)}) collective-permute-start(bf16[2,32,256]{2,1,0:T(8,128)(2,1)S(1)} %get-tuple-element.103), channel_id=1, source_target_pairs={{0,4},{1,5},{2,6},{3,7},{4,0},{5,1},{6,2},{7,3},{8,12},{9,13},{10,... | collective-permute-start | bytes 98312 | tf_op jit(solution)/shard_map/ppermute | solution.py:34
  34.3 4.8 %collective-permute-start.10 = (bf16[2,32,256]{2,1,0:T(8,128)(2,1)S(1)}, bf16[2,32,256]{2,1,0:T(8,128)(2,1)S(1)}, u32[]{:S(2)}, u32[]{:S(2)}) collective-permute-start(bf16[2,32,256]{2,1,0:T(8,128)(2,1)S(1)} %get-tuple-element.104), channel_id=1, source_target_pairs={{0,2},{1,3},{2,0},{3,1},{4,6},{5,7},{6,4},{7,5},{8,10},{9,11},{10,... | collective-permute-start | bytes 98312 | tf_op jit(solution)/shard_map/ppermute | solution.py:34
  39.3 8.2 %collective-permute-start.12 = (bf16[144,256]{1,0:T(8,128)(2,1)S(1)}, bf16[144,256]{1,0:T(8,128)(2,1)S(1)}, u32[]{:S(2)}, u32[]{:S(2)}) collective-permute-start(bf16[144,256]{1,0:T(8,128)(2,1)S(1)} %get-tuple-element.113), channel_id=1, source_target_pairs={{0,6},{1,7},{2,4},{3,5},{4,2},{5,3},{6,0},{7,1},{8,14},{9,15},{10,... | collective-permute-start | bytes 221192 | tf_op jit(solution)/shard_map/ppermute | solution.py:34
  42.1 5.8 %collective-permute-start.13 = (bf16[144,256]{1,0:T(8,128)(2,1)S(1)}, bf16[144,256]{1,0:T(8,128)(2,1)S(1)}, u32[]{:S(2)}, u32[]{:S(2)}) collective-permute-start(bf16[144,256]{1,0:T(8,128)(2,1)S(1)} %get-tuple-element.114), channel_id=1, source_target_pairs={{0,4},{1,5},{2,6},{3,7},{4,0},{5,1},{6,2},{7,3},{8,12},{9,13},{10,... | collective-permute-start | bytes 221192 | tf_op jit(solution)/shard_map/ppermute | solution.py:34
  42.1 5.8 %collective-permute-start.14 = (bf16[144,256]{1,0:T(8,128)(2,1)S(1)}, bf16[144,256]{1,0:T(8,128)(2,1)S(1)}, u32[]{:S(2)}, u32[]{:S(2)}) collective-permute-start(bf16[144,256]{1,0:T(8,128)(2,1)S(1)} %get-tuple-element.115), channel_id=1, source_target_pairs={{0,2},{1,3},{2,0},{3,1},{4,6},{5,7},{6,4},{7,5},{8,10},{9,11},{10,... | collective-permute-start | bytes 221192 | tf_op jit(solution)/shard_map/ppermute | solution.py:34
  43.7 3.7 %collective-permute-start.11 = (bf16[32,256]{1,0:T(8,128)(2,1)S(1)}, bf16[32,256]{1,0:T(8,128)(2,1)S(1)}, u32[]{:S(2)}, u32[]{:S(2)}) collective-permute-start(bf16[32,256]{1,0:T(8,128)(2,1)S(1)} %get-tuple-element.111), channel_id=1, source_target_pairs={{0,1},{1,0},{2,3},{3,2},{4,5},{5,4},{6,7},{7,6},{8,9},{9,8},{10,11... | collective-permute-start | bytes 49160 | tf_op jit(solution)/shard_map/ppermute | solution.py:34
  47.9 4.6 %collective-permute-start.16 = (bf16[176,256]{1,0:T(8,128)(2,1)S(1)}, bf16[176,256]{1,0:T(8,128)(2,1)S(1)}, u32[]{:S(2)}, u32[]{:S(2)}) collective-permute-start(bf16[176,256]{1,0:T(8,128)(2,1)S(1)} %shard_map.102.before.refs_0_), channel_id=1, source_target_pairs={{0,16},{8,24},{16,0},{24,8},{1,17},{9,25},{17,1},{25,9},{2,18},{10... | collective-permute-start | bytes 270344 | tf_op jit(solution)/shard_map/ppermute | solution.py:34
  51.2 1.3 %collective-permute-start.15 = (bf16[176,256]{1,0:T(8,128)(2,1)S(1)}, bf16[176,256]{1,0:T(8,128)(2,1)S(1)}, u32[]{:S(2)}, u32[]{:S(2)}) collective-permute-start(bf16[176,256]{1,0:T(8,128)(2,1)S(1)} %shard_map.102.before.refs_0_), channel_id=1, source_target_pairs={{0,8},{8,0},{16,24},{24,16},{1,9},{9,1},{17,25},{25,17},{2,10},{10... | collective-permute-start | bytes 270344 | tf_op jit(solution)/shard_map/ppermute | solution.py:34
  52.5 1.3 %collective-permute-start.17 = (bf16[176,256]{1,0:T(8,128)(2,1)S(1)}, bf16[176,256]{1,0:T(8,128)(2,1)S(1)}, u32[]{:S(2)}, u32[]{:S(2)}) collective-permute-start(bf16[176,256]{1,0:T(8,128)(2,1)S(1)} %collective-permute-done.16.refs_2_), channel_id=1, source_target_pairs={{0,8},{8,0},{16,24},{24,16},{1,9},{9,1},{17,25},{25,17},{2,10},{10... | collective-permute-start | bytes 270344 | tf_op jit(solution)/shard_map/ppermute | solution.py:34

commit v15 on v14

--- a/solution.py
+++ b/solution.py
@@ -130,6 +130,7 @@
 LANES = 128
 BAND = 16
 TOKEN = ((8, LANES), F32)
+Z_ORDER = (2, 3, 1)
 
 
 def call(body, outs, scratch=(), smem=0, hbm=0, limit=24, flops=0, moved=0):
@@ -457,7 +458,7 @@
     own = lax.axis_index("rep") // 2
     ordered[own] = keep_tail[...]
     for step in range(1, steps):
-        ordered[own ^ step] = along[steps - 1 - step][...]
+        ordered[own ^ step] = along[Z_ORDER.index(step)][...]
     value = ordered[0].astype(F32)
     for step in range(1, steps):
         value = value + ordered[step].astype(F32)
@@ -598,7 +599,7 @@
     along, weights_fourth = outs[3 : 2 + steps], outs[2 + steps]
 
     across = send(across, "rep", lambda p: p ^ 1)
-    along = [send(along[step - 1], "rep", lambda p: p ^ (2 * step)) for step in reversed(range(1, steps))]
+    along = [send(along[step - 1], "rep", lambda p: p ^ (2 * step)) for step in Z_ORDER]
 
     norm_back, token = call(
         image_body,
@@ -618,7 +619,7 @@
         [((steps, 2, tail, full), BF16)],
         moved=4 * each * width,
     )(token, keep_lead, across, keep_tail, *along)
-    leads = [outs[0]] + [send(outs[step], "rep", lambda p: p ^ (2 * step)) for step in reversed(range(1, steps))]
+    leads = [outs[0]] + [send(outs[step], "rep", lambda p: p ^ (2 * step)) for step in Z_ORDER]
     tail_across = send(outs[steps + 1], "rep", lambda p: p ^ 1)
 
     feature_grad, token = call(feature_body, [half, TOKEN], moved=12 * near * width)(

time: 55.1 us -> 55.1 us (level)
  transfers between devices with their start and end apart: 18 -> 18, of which waited for: 8 -> 10; matrix products, arithmetic and copies ran while one was open for 0% -> 0% of each run, Pallas kernels for 32% -> 32%
where the time goes in v15:
time: 55.1 us; the launch traced here: 54.9 us
  Pallas kernels  21.6 us (39%)
  starting transfers between devices  16.8 us (30%)
  waiting for transfers between devices  11.7 us (21%)
  local copies, waits for them, and re-layouts  2.72 us (5%)
  between operations  2.05 us (4%)
    pallas_call x12, Pallas kernels, run(): pl.pallas_call(body, out_shape=[jax.ShapeDtypeStruct(shape, kind) for sha...  21.6 us
    ppermute x18, starting transfers between devices, send(): return lax.ppermute(value, axis, [(p, target(p)) for p in range(count)])  16.8 us
    ppermute x18, waiting for transfers between devices, send(): return lax.ppermute(value, axis, [(p, target(p)) for p in range(count)])  11.7 us
    unnamed x6, local copies, waits for them, and re-layouts  2.72 us
  transfers between devices with their start and end apart: 18, of which 10 were waited for; matrix products, arithmetic and copies ran while one was open for 0% of the time, Pallas kernels for 32%

profile of v15, /device:TPU:0, one launch (start us, length us, event | category | flops | bytes accessed | tf_op | source)
XLA Modules:
  0.0 54.9 jit_solution(10504920343031646134)
XLA Ops:
  0.6 0.5 collective-permute-start
  1.2 2.6 %collective-permute-start.3 = (bf16[192,1152]{1,0:T(8,128)(2,1)}, bf16[192,1152]{1,0:T(8,128)(2,1)S(1)}, u32[]{:S(2)}, u32[]{:S(2)}) collective-permute-start(bf16[192,1152]{1,0:T(8,128)(2,1)} %bitcast.6), channel_id=1, source_target_pairs={{0,16},{8,24},{16,0},{24,8},{1,17},{9,25},{17,1},{25,9},{2,18},{10... | collective-permute-start | bytes 1327112 | tf_op jit(solution)/shard_map/ppermute | solution.py:34
  5.0 0.0 collective-permute-done.f1
  5.0 1.0 %copy-done = bf16[192,1,1152]{2,0,1:T(8,128)(2,1)S(1)} copy-done((bf16[192,1,1152]{2,0,1:T(8,128)(2,1)S(1)}, bf16[192,1,1152]{2,0,1:T(8,128)(2,1)}, u32[]{:S(2)}) %copy-start) | copy-done | bytes 442392
  6.0 1.0 %copy-done.1 = bf16[192,1,1152]{2,0,1:T(8,128)(2,1)S(1)} copy-done((bf16[192,1,1152]{2,0,1:T(8,128)(2,1)S(1)}, bf16[192,1,1152]{2,0,1:T(8,128)(2,1)}, u32[]{:S(2)}) %copy-start.1) | copy-done | bytes 442392
  7.1 0.7 %copy-done.2 = f32[1152]{0:T(1024)S(1)} copy-done((f32[1152]{0:T(1024)S(1)}, f32[1152]{0:T(1024)}, u32[]{:S(2)}) %copy-start.2) | copy-done | bytes 4632
  7.7 4.2 %shard_map.93 = (bf16[192,1152]{1,0:T(8,128)(2,1)S(1)}, bf16[1152,1152]{1,0:T(8,128)(2,1)S(1)}, bf16[192,1152]{1,0:T(8,128)(2,1)S(1)}, f32[1,1152]{1,0:T(1,128)S...) custom-call(f32[1]{0:T(128)S(6)} %copy.10.scale, ...), custom_call_target="tpu_custom_call" | custom-call | flops 1019215872 | bytes 3538944 | tf_op jit(solution)/shard_map/pallas_call | solution.py:139
  12.0 0.2 collective-permute-start.1
  12.2 0.6 %collective-permute-start.2 = (bf16[192,1152]{1,0:T(8,128)(2,1)S(1)}, bf16[192,1152]{1,0:T(8,128)(2,1)S(1)}, u32[]{:S(2)}, u32[]{:S(2)}) collective-permute-start(bf16[192,1152]{1,0:T(8,128)(2,1)S(1)} %get-tuple-element.69.text_own), channel_id=1, source_target_pairs={{0,16},{8,24},{16,0},{24,8},{1,17},{9,25},{17,1},{25,9},{2,18},{10... | collective-permute-start | bytes 1327112 | tf_op jit(solution)/shard_map/ppermute | solution.py:34
  12.8 1.9 %collective-permute-done.3.f2 = bf16[192,1152]{1,0:T(8,128)(2,1)S(1)} collective-permute-done((bf16[192,1152]{1,0:T(8,128)(2,1)}, bf16[192,1152]{1,0:T(8,128)(2,1)S(1)}, u32[]{:S(2)}, u32[]{:S(2)}) %collective-permute-start.3) | collective-permute-done | bytes 442400 | tf_op jit(solution)/shard_map/ppermute | solution.py:34
  14.7 0.1 collective-permute-start.4
  14.8 0.5 collective-permute-start.5
  15.3 0.0 collective-permute-done.1.t1
  15.3 1.7 %shard_map.94 = (bf16[384,1152]{1,0:T(8,128)(2,1)S(1)}, bf16[1152,384]{1,0:T(8,128)(2,1)S(1)}, bf16[1152,384]{1,0:T(8,128)(2,1)S(1)}, bf16[288,384]{1,0:T(8,128)...) custom-call(f32[1]{0:T(128)S(6)} %copy.10.scale, ...), custom_call_target="tpu_custom_call" | custom-call | flops 1000 | bytes 1000 | tf_op jit(solution)/shard_map/pallas_call | solution.py:139
  17.0 0.0 collective-permute-done.5.f3_tail
  17.0 0.0 collective-permute-done.4.f3_head
  17.0 4.6 %shard_map.96 = (bf16[1152,384]{1,0:T(8,128)(2,1)S(1)}, bf16[384,1152]{1,0:T(8,128)(2,1)S(1)}, bf16[1152,384]{1,0:T(8,128)(2,1)S(1)}, bf16[288,384]{1,0:T(8,128)...) custom-call(f32[1]{0:T(128)S(6)} %copy.10.scale, ...), custom_call_target="tpu_custom_call" | custom-call | flops 1000 | bytes 1000 | tf_op jit(solution)/shard_map/pallas_call | solution.py:139
  21.7 2.9 %collective-permute-done.2.text_unit.text_third = bf16[192,1152]{1,0:T(8,128)(2,1)S(1)} collective-permute-done((bf16[192,1152]{1,0:T(8,128)(2,1)S(1)}, bf16[192,1152]{1,0:T(8,128)(2,1)S(1)}, u32[]{:S(2)}, u32[]{:S(2)}) %collective-permute-start.2) | collective-permute-done | bytes 442400 | tf_op jit(solution)/shard_map/ppermute | solution.py:34
  24.6 0.0 collective-permute-start.6
  24.6 1.3 %shard_map.97 = (bf16[192,768]{1,0:T(8,128)(2,1)S(1)}, f32[288,384]{1,0:T(8,128)S(1)}, f32[288,384]{1,0:T(8,128)S(1)}, f32[1,768]{1,0:T(1,128)S(1)}) custom-call(f32[1]{0:T(128)S(6)} %copy.10.scale, f32[1]{0:T(128)S(6)} %copy.11.bias, bf16[192,1152]{1,0:T(8,128)(2,1)S(1)} %collective-permute-done.2.text_unit.text_third, ...), custom_call_target="tpu_custom_call" | custom-call | flops 1019215872 | bytes 3538944 | tf_op jit(solution)/shard_map/pallas_call | solution.py:139
  26.0 0.5 collective-permute-done.6.text_unit.text_fourth
  26.4 2.7 %shard_map.98 = (bf16[4,144,256]{2,1,0:T(8,128)(2,1)S(1)}, bf16[4,144,256]{2,1,0:T(8,128)(2,1)S(1)}, bf16[2,32,256]{2,1,0:T(8,128)(2,1)S(1)}, bf16[2,32,256]{2,1...) custom-call(f32[1]{0:T(128)S(6)} %copy.10.scale, ...), custom_call_target="tpu_custom_call" | custom-call | flops 2038431744 | bytes 7077888 | tf_op jit(solution)/shard_map/pallas_call | solution.py:139
  29.2 1.6 %collective-permute-start.7 = (bf16[4,144,256]{2,1,0:T(8,128)(2,1)S(1)}, bf16[4,144,256]{2,1,0:T(8,128)(2,1)S(1)}, u32[]{:S(2)}, u32[]{:S(2)}) collective-permute-start(bf16[4,144,256]{2,1,0:T(8,128)(2,1)S(1)} %get-tuple-element.100), channel_id=1, source_target_pairs={{0,1},{1,0},{2,3},{3,2},{4,5},{5,4},{6,7},{7,6},{8,9},{9,8},{10,11... | collective-permute-start | bytes 884744 | tf_op jit(solution)/shard_map/ppermute | solution.py:34
  30.7 2.6 %collective-permute-start.8 = (bf16[2,32,256]{2,1,0:T(8,128)(2,1)S(1)}, bf16[2,32,256]{2,1,0:T(8,128)(2,1)S(1)}, u32[]{:S(2)}, u32[]{:S(2)}) collective-permute-start(bf16[2,32,256]{2,1,0:T(8,128)(2,1)S(1)} %get-tuple-element.102), channel_id=1, source_target_pairs={{0,4},{1,5},{2,6},{3,7},{4,0},{5,1},{6,2},{7,3},{8,12},{9,13},{10,... | collective-permute-start | bytes 98312 | tf_op jit(solution)/shard_map/ppermute | solution.py:34
  33.3 1.3 %collective-permute-start.9 = (bf16[2,32,256]{2,1,0:T(8,128)(2,1)S(1)}, bf16[2,32,256]{2,1,0:T(8,128)(2,1)S(1)}, u32[]{:S(2)}, u32[]{:S(2)}) collective-permute-start(bf16[2,32,256]{2,1,0:T(8,128)(2,1)S(1)} %get-tuple-element.103), channel_id=1, source_target_pairs={{0,6},{1,7},{2,4},{3,5},{4,2},{5,3},{6,0},{7,1},{8,14},{9,15},{10,... | collective-permute-start | bytes 98312 | tf_op jit(solution)/shard_map/ppermute | solution.py:34
  34.7 0.2 collective-permute-start.10
  34.9 2.1 %shard_map.99 = (f32[192,1152]{1,0:T(8,128)S(1)}, f32[8,128]{1,0:T(8,128)S(1)}) custom-call(f32[1]{0:T(128)S(6)} %copy.10.scale, bf16[1152,1152]{1,0:T(8,128)(2,1)S(1)} %get-tuple-element.65.proj, bf16[384,1152]{1,0:T(8,128)(2,1)S(1)} %get-tuple-element.71.text_near, bf16[192,1152]{1,0:T(8,128)(2,1)S(1)} %collective-permute-done.2.text_unit.text_third, ...), custom_call_target="tpu_custom_call" | custom-call | flops 2038431744 | bytes 5308416 | tf_op jit(solution)/shard_map/pallas_call | solution.py:139
  37.0 0.0 collective-permute-done.8.refs_0_
  37.0 2.0 %collective-permute-done.9.refs_1_ = bf16[2,32,256]{2,1,0:T(8,128)(2,1)S(1)} collective-permute-done((bf16[2,32,256]{2,1,0:T(8,128)(2,1)S(1)}, bf16[2,32,256]{2,1,0:T(8,128)(2,1)S(1)}, u32[]{:S(2)}, u32[]{:S(2)}) %collective-permute-start.9) | collective-permute-done | bytes 32800 | tf_op jit(solution)/shard_map/ppermute | solution.py:34
  39.0 0.0 collective-permute-done.10.refs_2_
  39.0 0.0 collective-permute-done.7.across
  39.0 0.1 shard_map.100
  39.1 1.9 %collective-permute-start.12 = (bf16[144,256]{1,0:T(8,128)(2,1)S(1)}, bf16[144,256]{1,0:T(8,128)(2,1)S(1)}, u32[]{:S(2)}, u32[]{:S(2)}) collective-permute-start(bf16[144,256]{1,0:T(8,128)(2,1)S(1)} %get-tuple-element.113), channel_id=1, source_target_pairs={{0,4},{1,5},{2,6},{3,7},{4,0},{5,1},{6,2},{7,3},{8,12},{9,13},{10,... | collective-permute-start | bytes 221192 | tf_op jit(solution)/shard_map/ppermute | solution.py:34
  41.1 1.4 %collective-permute-start.13 = (bf16[144,256]{1,0:T(8,128)(2,1)S(1)}, bf16[144,256]{1,0:T(8,128)(2,1)S(1)}, u32[]{:S(2)}, u32[]{:S(2)}) collective-permute-start(bf16[144,256]{1,0:T(8,128)(2,1)S(1)} %get-tuple-element.114), channel_id=1, source_target_pairs={{0,6},{1,7},{2,4},{3,5},{4,2},{5,3},{6,0},{7,1},{8,14},{9,15},{10,... | collective-permute-start | bytes 221192 | tf_op jit(solution)/shard_map/ppermute | solution.py:34
  42.4 0.3 collective-permute-start.14
  42.7 1.5 %collective-permute-start.11 = (bf16[32,256]{1,0:T(8,128)(2,1)S(1)}, bf16[32,256]{1,0:T(8,128)(2,1)S(1)}, u32[]{:S(2)}, u32[]{:S(2)}) collective-permute-start(bf16[32,256]{1,0:T(8,128)(2,1)S(1)} %get-tuple-element.111), channel_id=1, source_target_pairs={{0,1},{1,0},{2,3},{3,2},{4,5},{5,4},{6,7},{7,6},{8,9},{9,8},{10,11... | collective-permute-start | bytes 49160 | tf_op jit(solution)/shard_map/ppermute | solution.py:34
  44.2 1.7 %shard_map.101 = (bf16[192,1152]{1,0:T(8,128)(2,1)}, f32[8,128]{1,0:T(8,128)S(1)}) custom-call(bf16[192,1152]{1,0:T(8,128)(2,1)S(1)} %get-tuple-element.63.features, f32[1,1152]{1,0:T(1,128)S(1)} %get-tuple-element.64.gain, f32[192,1152]{1,0:T(8,128)S(1)} %get-tuple-element.97.norm_back, bf16[32,256]{1,0:T(8,128)(2,1)S(1)} %get-tuple-element.105.before.tail), custom_call_target="tpu_custom_call" | custom-call | bytes 5308416 | tf_op jit(solution)/shard_map/pallas_call | solution.py:139
  45.9 0.5 collective-permute-done.11.tail_across
  46.4 1.0 %collective-permute-done.12.refs_1_ = bf16[144,256]{1,0:T(8,128)(2,1)S(1)} collective-permute-done((bf16[144,256]{1,0:T(8,128)(2,1)S(1)}, bf16[144,256]{1,0:T(8,128)(2,1)S(1)}, u32[]{:S(2)}, u32[]{:S(2)}) %collective-permute-start.12) | collective-permute-done | bytes 73760 | tf_op jit(solution)/shard_map/ppermute | solution.py:34
  47.5 0.0 collective-permute-done.13.refs_2_
  47.5 0.4 collective-permute-done.14.refs_3_
  48.0 1.5 %collective-permute-start.16 = (bf16[176,256]{1,0:T(8,128)(2,1)S(1)}, bf16[176,256]{1,0:T(8,128)(2,1)S(1)}, u32[]{:S(2)}, u32[]{:S(2)}) collective-permute-start(bf16[176,256]{1,0:T(8,128)(2,1)S(1)} %shard_map.102.before.refs_0_), channel_id=1, source_target_pairs={{0,16},{8,24},{16,0},{24,8},{1,17},{9,25},{17,1},{25,9},{2,18},{10... | collective-permute-start | bytes 270344 | tf_op jit(solution)/shard_map/ppermute | solution.py:34
  49.4 2.0 %shard_map.103 = (bf16[192,1152]{1,0:T(8,128)(2,1)}, f32[8,128]{1,0:T(8,128)S(1)}) custom-call(f32[1]{0:T(128)S(6)} %copy.10.scale, bf16[192,1152]{1,0:T(8,128)(2,1)S(1)} %get-tuple-element.107.text, bf16[384,384]{1,0:T(8,128)(2,1)S(1)} %get-tuple-element.75.weights_near, bf16[384,384]{1,0:T(8,128)(2,1)S(1)} %get-tuple-element.108.weights_far, ...), custom_call_target="tpu_custom_call" | custom-call | flops 1019215872 | bytes 2654208 | tf_op jit(solution)/shard_map/pallas_call | solution.py:139
  51.4 0.0 collective-permute-start.15
  51.4 1.1 %collective-permute-done.16.refs_2_ = bf16[176,256]{1,0:T(8,128)(2,1)S(1)} collective-permute-done((bf16[176,256]{1,0:T(8,128)(2,1)S(1)}, bf16[176,256]{1,0:T(8,128)(2,1)S(1)}, u32[]{:S(2)}, u32[]{:S(2)}) %collective-permute-start.16) | collective-permute-done | bytes 90144 | tf_op jit(solution)/shard_map/ppermute | solution.py:34
  52.6 0.2 collective-permute-done.15.refs_1_
  52.7 1.1 %collective-permute-done.17.refs_3_ = bf16[176,256]{1,0:T(8,128)(2,1)S(1)} collective-permute-done((bf16[176,256]{1,0:T(8,128)(2,1)S(1)}, bf16[176,256]{1,0:T(8,128)(2,1)S(1)}, u32[]{:S(2)}, u32[]{:S(2)}) %collective-permute-start.17) | collective-permute-done | bytes 90144 | tf_op jit(solution)/shard_map/ppermute | solution.py:34
  53.9 1.0 %shard_map.104 = (f32[144,1152]{1,0:T(8,128)}, f32[1152]{0:T(1024)}) custom-call(f32[8,128]{1,0:T(8,128)S(1)} %get-tuple-element.118.before, bf16[176,256]{1,0:T(8,128)(2,1)S(1)} %shard_map.102.before.refs_0_, bf16[176,256]{1,0:T(8,128)(2,1)S(1)} %collective-permute-done.15.refs_1_, bf16[176,256]{1,0:T(8,128)(2,1)S(1)} %collective-permute-done.16.refs_2_, ...), custom_call_target="tpu_custom_call" | custom-call | bytes 1327104 | tf_op jit(solution)/shard_map/pallas_call | solution.py:139
  (6 shorter events, 0.1 us)
Async XLA Ops:
  0.6 4.4 %collective-permute-start = (bf16[192,1152]{1,0:T(8,128)(2,1)}, bf16[192,1152]{1,0:T(8,128)(2,1)S(1)}, u32[]{:S(2)}, u32[]{:S(2)}) collective-permute-start(bf16[192,1152]{1,0:T(8,128)(2,1)} %bitcast.5), channel_id=1, source_target_pairs={{0,8},{8,0},{16,24},{24,16},{1,9},{9,1},{17,25},{25,17},{2,10},{10... | collective-permute-start | bytes 1327112 | tf_op jit(solution)/shard_map/ppermute | solution.py:34
  1.2 13.5 %collective-permute-start.3 = (bf16[192,1152]{1,0:T(8,128)(2,1)}, bf16[192,1152]{1,0:T(8,128)(2,1)S(1)}, u32[]{:S(2)}, u32[]{:S(2)}) collective-permute-start(bf16[192,1152]{1,0:T(8,128)(2,1)} %bitcast.6), channel_id=1, source_target_pairs={{0,16},{8,24},{16,0},{24,8},{1,17},{9,25},{17,1},{25,9},{2,18},{10... | collective-permute-start | bytes 1327112 | tf_op jit(solution)/shard_map/ppermute | solution.py:34
  5.0 1.0 %copy-start = (bf16[192,1,1152]{2,0,1:T(8,128)(2,1)S(1)}, bf16[192,1,1152]{2,0,1:T(8,128)(2,1)}, u32[]{:S(2)}) copy-start(bf16[192,1,1152]{2,0,1:T(8,128)(2,1)} %param.7) | copy-start | bytes 1327108
  6.0 1.0 %copy-start.1 = (bf16[192,1,1152]{2,0,1:T(8,128)(2,1)S(1)}, bf16[192,1,1152]{2,0,1:T(8,128)(2,1)}, u32[]{:S(2)}) copy-start(bf16[192,1,1152]{2,0,1:T(8,128)(2,1)} %param.6) | copy-start | bytes 1327108
  7.1 0.7 %copy-start.2 = (f32[1152]{0:T(1024)S(1)}, f32[1152]{0:T(1024)}, u32[]{:S(2)}) copy-start(f32[1152]{0:T(1024)} %gain_line.1) | copy-start | bytes 13828
  12.0 3.3 %collective-permute-start.1 = (bf16[192,1152]{1,0:T(8,128)(2,1)S(1)}, bf16[192,1152]{1,0:T(8,128)(2,1)S(1)}, u32[]{:S(2)}, u32[]{:S(2)}) collective-permute-start(bf16[192,1152]{1,0:T(8,128)(2,1)S(1)} %get-tuple-element.69.text_own), channel_id=1, source_target_pairs={{0,8},{8,0},{16,24},{24,16},{1,9},{9,1},{17,25},{25,17},{2,10},{10... | collective-permute-start | bytes 1327112 | tf_op jit(solution)/shard_map/ppermute | solution.py:34
  12.2 12.4 %collective-permute-start.2 = (bf16[192,1152]{1,0:T(8,128)(2,1)S(1)}, bf16[192,1152]{1,0:T(8,128)(2,1)S(1)}, u32[]{:S(2)}, u32[]{:S(2)}) collective-permute-start(bf16[192,1152]{1,0:T(8,128)(2,1)S(1)} %get-tuple-element.69.text_own), channel_id=1, source_target_pairs={{0,16},{8,24},{16,0},{24,8},{1,17},{9,25},{17,1},{25,9},{2,18},{10... | collective-permute-start | bytes 1327112 | tf_op jit(solution)/shard_map/ppermute | solution.py:34
  14.7 2.3 %collective-permute-start.4 = (bf16[160,1152]{1,0:T(8,128)(2,1)S(1)}, bf16[160,1152]{1,0:T(8,128)(2,1)S(1)}, u32[]{:S(2)}, u32[]{:S(2)}) collective-permute-start(bf16[160,1152]{1,0:T(8,128)(2,1)S(1)} %get-tuple-element.72), channel_id=1, source_target_pairs={{0,8},{8,0},{16,24},{24,16},{1,9},{9,1},{17,25},{25,17},{2,10},{10... | collective-permute-start | bytes 1105928 | tf_op jit(solution)/shard_map/ppermute | solution.py:34
  14.8 2.2 %collective-permute-start.5 = (bf16[32,1152]{1,0:T(8,128)(2,1)S(1)}, bf16[32,1152]{1,0:T(8,128)(2,1)S(1)}, u32[]{:S(2)}, u32[]{:S(2)}) collective-permute-start(bf16[32,1152]{1,0:T(8,128)(2,1)S(1)} %get-tuple-element.73), channel_id=1, source_target_pairs={{0,8},{8,0},{16,24},{24,16},{1,9},{9,1},{17,25},{25,17},{2,10},{10... | collective-permute-start | bytes 221192 | tf_op jit(solution)/shard_map/ppermute | solution.py:34
  24.6 1.8 %collective-permute-start.6 = (bf16[192,1152]{1,0:T(8,128)(2,1)S(1)}, bf16[192,1152]{1,0:T(8,128)(2,1)S(1)}, u32[]{:S(2)}, u32[]{:S(2)}) collective-permute-start(bf16[192,1152]{1,0:T(8,128)(2,1)S(1)} %collective-permute-done.2.text_unit.text_third), channel_id=1, source_target_pairs={{0,8},{8,0},{16,24},{24,16},{1,9},{9,1},{17,25},{25,17},{2,10},{10... | collective-permute-start | bytes 1327112 | tf_op jit(solution)/shard_map/ppermute | solution.py:34
  29.2 9.9 %collective-permute-start.7 = (bf16[4,144,256]{2,1,0:T(8,128)(2,1)S(1)}, bf16[4,144,256]{2,1,0:T(8,128)(2,1)S(1)}, u32[]{:S(2)}, u32[]{:S(2)}) collective-permute-start(bf16[4,144,256]{2,1,0:T(8,128)(2,1)S(1)} %get-tuple-element.100), channel_id=1, source_target_pairs={{0,1},{1,0},{2,3},{3,2},{4,5},{5,4},{6,7},{7,6},{8,9},{9,8},{10,11... | collective-permute-start | bytes 884744 | tf_op jit(solution)/shard_map/ppermute | solution.py:34
  30.7 6.3 %collective-permute-start.8 = (bf16[2,32,256]{2,1,0:T(8,128)(2,1)S(1)}, bf16[2,32,256]{2,1,0:T(8,128)(2,1)S(1)}, u32[]{:S(2)}, u32[]{:S(2)}) collective-permute-start(bf16[2,32,256]{2,1,0:T(8,128)(2,1)S(1)} %get-tuple-element.102), channel_id=1, source_target_pairs={{0,4},{1,5},{2,6},{3,7},{4,0},{5,1},{6,2},{7,3},{8,12},{9,13},{10,... | collective-permute-start | bytes 98312 | tf_op jit(solution)/shard_map/ppermute | solution.py:34
  33.3 5.7 %collective-permute-start.9 = (bf16[2,32,256]{2,1,0:T(8,128)(2,1)S(1)}, bf16[2,32,256]{2,1,0:T(8,128)(2,1)S(1)}, u32[]{:S(2)}, u32[]{:S(2)}) collective-permute-start(bf16[2,32,256]{2,1,0:T(8,128)(2,1)S(1)} %get-tuple-element.103), channel_id=1, source_target_pairs={{0,6},{1,7},{2,4},{3,5},{4,2},{5,3},{6,0},{7,1},{8,14},{9,15},{10,... | collective-permute-start | bytes 98312 | tf_op jit(solution)/shard_map/ppermute | solution.py:34
  34.7 4.4 %collective-permute-start.10 = (bf16[2,32,256]{2,1,0:T(8,128)(2,1)S(1)}, bf16[2,32,256]{2,1,0:T(8,128)(2,1)S(1)}, u32[]{:S(2)}, u32[]{:S(2)}) collective-permute-start(bf16[2,32,256]{2,1,0:T(8,128)(2,1)S(1)} %get-tuple-element.104), channel_id=1, source_target_pairs={{0,2},{1,3},{2,0},{3,1},{4,6},{5,7},{6,4},{7,5},{8,10},{9,11},{10,... | collective-permute-start | bytes 98312 | tf_op jit(solution)/shard_map/ppermute | solution.py:34
  39.1 8.3 %collective-permute-start.12 = (bf16[144,256]{1,0:T(8,128)(2,1)S(1)}, bf16[144,256]{1,0:T(8,128)(2,1)S(1)}, u32[]{:S(2)}, u32[]{:S(2)}) collective-permute-start(bf16[144,256]{1,0:T(8,128)(2,1)S(1)} %get-tuple-element.113), channel_id=1, source_target_pairs={{0,4},{1,5},{2,6},{3,7},{4,0},{5,1},{6,2},{7,3},{8,12},{9,13},{10,... | collective-permute-start | bytes 221192 | tf_op jit(solution)/shard_map/ppermute | solution.py:34
  41.1 6.4 %collective-permute-start.13 = (bf16[144,256]{1,0:T(8,128)(2,1)S(1)}, bf16[144,256]{1,0:T(8,128)(2,1)S(1)}, u32[]{:S(2)}, u32[]{:S(2)}) collective-permute-start(bf16[144,256]{1,0:T(8,128)(2,1)S(1)} %get-tuple-element.114), channel_id=1, source_target_pairs={{0,6},{1,7},{2,4},{3,5},{4,2},{5,3},{6,0},{7,1},{8,14},{9,15},{10,... | collective-permute-start | bytes 221192 | tf_op jit(solution)/shard_map/ppermute | solution.py:34
  42.4 5.5 %collective-permute-start.14 = (bf16[144,256]{1,0:T(8,128)(2,1)S(1)}, bf16[144,256]{1,0:T(8,128)(2,1)S(1)}, u32[]{:S(2)}, u32[]{:S(2)}) collective-permute-start(bf16[144,256]{1,0:T(8,128)(2,1)S(1)} %get-tuple-element.115), channel_id=1, source_target_pairs={{0,2},{1,3},{2,0},{3,1},{4,6},{5,7},{6,4},{7,5},{8,10},{9,11},{10,... | collective-permute-start | bytes 221192 | tf_op jit(solution)/shard_map/ppermute | solution.py:34
  42.7 3.7 %collective-permute-start.11 = (bf16[32,256]{1,0:T(8,128)(2,1)S(1)}, bf16[32,256]{1,0:T(8,128)(2,1)S(1)}, u32[]{:S(2)}, u32[]{:S(2)}) collective-permute-start(bf16[32,256]{1,0:T(8,128)(2,1)S(1)} %get-tuple-element.111), channel_id=1, source_target_pairs={{0,1},{1,0},{2,3},{3,2},{4,5},{5,4},{6,7},{7,6},{8,9},{9,8},{10,11... | collective-permute-start | bytes 49160 | tf_op jit(solution)/shard_map/ppermute | solution.py:34
  48.0 4.6 %collective-permute-start.16 = (bf16[176,256]{1,0:T(8,128)(2,1)S(1)}, bf16[176,256]{1,0:T(8,128)(2,1)S(1)}, u32[]{:S(2)}, u32[]{:S(2)}) collective-permute-start(bf16[176,256]{1,0:T(8,128)(2,1)S(1)} %shard_map.102.before.refs_0_), channel_id=1, source_target_pairs={{0,16},{8,24},{16,0},{24,8},{1,17},{9,25},{17,1},{25,9},{2,18},{10... | collective-permute-start | bytes 270344 | tf_op jit(solution)/shard_map/ppermute | solution.py:34
  51.4 1.3 %collective-permute-start.15 = (bf16[176,256]{1,0:T(8,128)(2,1)S(1)}, bf16[176,256]{1,0:T(8,128)(2,1)S(1)}, u32[]{:S(2)}, u32[]{:S(2)}) collective-permute-start(bf16[176,256]{1,0:T(8,128)(2,1)S(1)} %shard_map.102.before.refs_0_), channel_id=1, source_target_pairs={{0,8},{8,0},{16,24},{24,16},{1,9},{9,1},{17,25},{25,17},{2,10},{10... | collective-permute-start | bytes 270344 | tf_op jit(solution)/shard_map/ppermute | solution.py:34
  52.6 1.3 %collective-permute-start.17 = (bf16[176,256]{1,0:T(8,128)(2,1)S(1)}, bf16[176,256]{1,0:T(8,128)(2,1)S(1)}, u32[]{:S(2)}, u32[]{:S(2)}) collective-permute-start(bf16[176,256]{1,0:T(8,128)(2,1)S(1)} %collective-permute-done.16.refs_2_), channel_id=1, source_target_pairs={{0,8},{8,0},{16,24},{24,16},{1,9},{9,1},{17,25},{25,17},{2,10},{10... | collective-permute-start | bytes 270344 | tf_op jit(solution)/shard_map/ppermute | solution.py:34

commit v16 on v14

--- a/solution.py
+++ b/solution.py
@@ -330,11 +330,10 @@
 
 
 def partial_body(
-    members, groups, lead, scale, bias, text_unit, flat_near, flat_far, totals, back_near, back_far, unit_turned_near,
+    members, groups, scale, bias, text_unit, flat_near, flat_far, totals, back_near, back_far, unit_turned_near,
     unit_turned_far, inverse_near, inverse_far, turned_near, turned_far, proj_columns, gain,
-    across, keep_lead, keep_tail, *refs,
+    across_first, across_later, keep, weights, text_columns, dots, packed,
 ):
-    along, (weights, text_columns, dots, packed) = refs[: groups // 2 - 1], refs[groups // 2 - 1 :]
     rows = text_unit.shape[0]
     near = 2 * rows
     every = members * rows
@@ -377,13 +376,11 @@
         packed[group, count - BAND :, full - LANES :] = gain_tile
 
     own = lax.axis_index("rep")
-    for step in range(groups // 2):
-        across[step] = packed[own ^ 1 ^ (2 * step), :lead, :]
-        keep_lead[step] = packed[own ^ (2 * step), :lead, :]
-    for other in range(2):
-        keep_tail[other] = packed[own ^ other, lead:, :]
-        for step in range(1, groups // 2):
-            along[step - 1][other] = packed[own ^ (2 * step) ^ other, lead:, :]
+    for at in range(2):
+        across_first[at] = packed[own ^ 1 ^ (4 + 2 * at)]
+        across_later[at] = packed[own ^ 1 ^ (2 * at)]
+    for at in range(4):
+        keep[at] = packed[own ^ (2 * at)]
 
 
 def image_body(
@@ -448,34 +445,29 @@
     token[...] = jnp.zeros_like(token)
 
 
-def first_sum_body(token, keep_lead, across, keep_tail, *refs):
-    steps = keep_lead.shape[0]
-    along, refs = refs[: steps - 1], refs[steps - 1 :]
-    leads, (tail, tail_across, ordered) = refs[:steps], refs[steps:]
-    for step in range(steps):
-        leads[step][...] = (keep_lead[step].astype(F32) + across[step].astype(F32)).astype(BF16)
-    own = lax.axis_index("rep") // 2
-    ordered[own] = keep_tail[...]
-    for step in range(1, steps):
-        ordered[own ^ step] = along[steps - 1 - step][...]
-    value = ordered[0].astype(F32)
-    for step in range(1, steps):
-        value = value + ordered[step].astype(F32)
-    tail[...] = value[0].astype(BF16)
-    tail_across[...] = value[1].astype(BF16)
-
-
-def last_sum_body(before, tail, tail_across, *refs):
-    leads, total = refs[:-1], refs[-1]
-    split = leads[0].shape[0]
-    value = leads[0][...].astype(F32)
-    for lead in leads[1:]:
-        value = value + lead[...].astype(F32)
-    total[:split, :] = value.astype(BF16)
-    total[split:, :] = (tail[...].astype(F32) + tail_across[...].astype(F32)).astype(BF16)
-
-
-def finish_body(members, before, *refs):
+def pair_sum_body(first, before, keep, come, low, high):
+    for at, target in enumerate((low, high)):
+        target[...] = (keep[first + at].astype(F32) + come[at].astype(F32)).astype(BF16)
+
+
+def far_sum_body(before, two_on, three_on, total):
+    total[...] = two_on[...].astype(F32) + three_on[...].astype(F32)
+
+
+def last_sum_body(far, own, next_one, two_on, three_on, total, ordered):
+    parts = (own, next_one, two_on, three_on)
+    total[...] = (own[...].astype(F32) + next_one[...].astype(F32) + far[...]).astype(BF16)
+    count, full = total.shape
+    z = lax.axis_index("rep") // 2
+    for step, part in enumerate(parts):
+        ordered[z ^ step] = part[count - BAND :, full - LANES :].astype(F32)
+    value = ordered[0]
+    for at in range(1, len(parts)):
+        value = value + ordered[at]
+    total[count - BAND :, full - LANES :] = value.astype(BF16)
+
+
+def finish_body(members, *refs):
     packets, (proj_grad, gain_gradient, ordered) = refs[:members], refs[members:]
     count, full = packets[0].shape
     rows, width = proj_grad.shape
@@ -510,9 +502,6 @@
     bands = -(-(each // BAND) // (full // (columns - full)))
     packet = (each + bands * BAND, full)
 
-    lead = (5 * packet[0] // BAND // 6) * BAND
-    tail = packet[0] - lead
-    steps = groups // 2
 
     f0, t0 = features[:, 0, :], text[:, 0, :]
     f2 = send(f0, "loop", lambda p: p ^ 2)
@@ -568,6 +557,15 @@
         scale, bias, f2, f3_head, f3_tail, proj_kept, gain_row, text_near, text_columns_near, weights_near,
     )
 
+    text_grad, token = call(
+        text_body,
+        [half, TOKEN],
+        [((rows, width), F32)],
+        smem=1,
+        flops=1000,
+        moved=1000,
+    )(scale, t0_kept, weights_near, weights_far, unit_near, unit_far, token)
+
     t2_after, token = lax.optimization_barrier((t2, token))
     t3 = send(t2_after, "loop", lambda p: p ^ 1)
 
@@ -584,8 +582,8 @@
     )
 
     outs = call(
-        functools.partial(partial_body, members, groups, lead),
-        [((steps, lead, full), BF16)] * 2 + [((2, tail, full), BF16)] * steps + [narrow],
+        functools.partial(partial_body, members, groups),
+        [((2,) + packet, BF16)] * 2 + [((4,) + packet, BF16), narrow],
         [((rows, columns), BF16), ((rows, every), F32), ((groups,) + packet, BF16)],
         smem=2,
         flops=4 * near * width * width,
@@ -594,52 +592,40 @@
         scale, bias, t3, flat_near, flat_far, totals, back_near, back_far, unit_turned_near, unit_turned_far,
         inverse_near, inverse_far, turned_near, turned_far, proj_columns, gain_row,
     )
-    across, keep_lead, keep_tail = outs[:3]
-    along, weights_fourth = outs[3 : 2 + steps], outs[2 + steps]
-
-    across = send(across, "rep", lambda p: p ^ 1)
-    along = [send(along[step - 1], "rep", lambda p: p ^ (2 * step)) for step in reversed(range(1, steps))]
-
+    across_first, across_later, keep, weights_fourth = outs
+    come_first = send(across_first, "rep", lambda p: p ^ 1)
     norm_back, token = call(
         image_body,
         [((rows, width), F32), TOKEN],
         [half, ((rows, width), F32)],
         smem=1,
-        flops=4 * near * width * width,
-        moved=12 * near * width,
+        flops=1000,
+        moved=1000,
     )(
         scale, proj_kept, text_near, t2, t3, weights_near, weights_third, weights_fourth,
         unit_near, factors,
     )
 
-    outs = call(
-        first_sum_body,
-        [((lead, full), BF16)] * steps + [((tail, full), BF16)] * 2,
-        [((steps, 2, tail, full), BF16)],
-        moved=4 * each * width,
-    )(token, keep_lead, across, keep_tail, *along)
-    leads = [outs[0]] + [send(outs[step], "rep", lambda p: p ^ (2 * step)) for step in reversed(range(1, steps))]
-    tail_across = send(outs[steps + 1], "rep", lambda p: p ^ 1)
-
+    across_later, token = lax.optimization_barrier((across_later, token))
+    come_later = send(across_later, "rep", lambda p: p ^ 1)
+    two_on, three_on = call(functools.partial(pair_sum_body, 2), [(packet, BF16)] * 2, moved=1000)(
+        token, keep, come_first
+    )
+    first_two = two_on
+    two_on = send(two_on, "rep", lambda p: p ^ 4)
+    three_on = send(three_on, "rep", lambda p: p ^ 6)
+    own_sum, next_one = call(functools.partial(pair_sum_body, 0), [(packet, BF16)] * 2, moved=1000)(
+        first_two, keep, come_later
+    )
+    next_one = send(next_one, "rep", lambda p: p ^ 2)
     feature_grad, token = call(feature_body, [half, TOKEN], moved=12 * near * width)(
-        f0_kept, gain_row, norm_back, outs[steps]
-    )
-
-    (reduced,) = call(
-        last_sum_body,
-        [(packet, BF16)],
-        moved=4 * each * width,
-    )(token, outs[steps], tail_across, *leads)
+        f0_kept, gain_row, norm_back, own_sum
+    )
+    (far_sum,) = call(far_sum_body, [(packet, F32)], moved=1000)(token, two_on, three_on)
+    (reduced,) = call(last_sum_body, [(packet, BF16)], [((4, BAND, LANES), F32)], moved=1000)(
+        far_sum, own_sum, next_one, two_on, three_on
+    )
     far_block = send(reduced, "loop", lambda p: p ^ 2)
-    text_grad, token = call(
-        text_body,
-        [half, TOKEN],
-        [((rows, width), F32)],
-        smem=1,
-        flops=2 * near * width * width,
-        moved=6 * near * width,
-    )(scale, t0_kept, weights_near, weights_far, unit_near, unit_far, reduced)
-    reduced, token = lax.optimization_barrier((reduced, token))
     near_block = send(reduced, "loop", lambda p: p ^ 1)
     blocks = [reduced, near_block, far_block, send(far_block, "loop", lambda p: p ^ 1)]
 
@@ -648,7 +634,7 @@
         [((each, width), F32), ((width,), F32)],
         [((members, bands * BAND, full), F32)],
         moved=8 * each * width,
-    )(token, *blocks)
+    )(*blocks)
     return feature_grad[:, None, :], text_grad[:, None, :], proj_grad, gain_gradient
 
 

time: 55.1 us -> 54 us (0.980)
  starting transfers between devices: 16.9 us -> 13.3 us
  waiting for transfers between devices: 11.5 us -> 14.1 us
    ppermute x18 -> x15, starting transfers between devices: 16.9 us -> 13.3 us  [send(): return lax.ppermute(value, axis, [(p, target(p)) for p in range(count)])]
    ppermute x18 -> x15, waiting for transfers between devices: 11.5 us -> 14.1 us  [send(): return lax.ppermute(value, axis, [(p, target(p)) for p in range(count)])]
    pallas_call x12 -> x14, Pallas kernels: 21.6 us -> 21.6 us  [run(): pl.pallas_call(body, out_shape=[jax.ShapeDtypeStruct(shape, kind) for sha...]
  transfers between devices with their start and end apart: 18 -> 15, of which waited for: 8 -> 8; matrix products, arithmetic and copies ran while one was open for 0% -> 0% of each run, Pallas kernels for 32% -> 33%
where the time goes in v16:
time: 54 us; the launch traced here: 53.7 us
  Pallas kernels  21.6 us (40%)
  waiting for transfers between devices  14.1 us (26%)
  starting transfers between devices  13.3 us (25%)
  local copies, waits for them, and re-layouts  2.72 us (5%)
  between operations  2.05 us (4%)
    pallas_call x14, Pallas kernels, run(): pl.pallas_call(body, out_shape=[jax.ShapeDtypeStruct(shape, kind) for sha...  21.6 us
    ppermute x15, waiting for transfers between devices, send(): return lax.ppermute(value, axis, [(p, target(p)) for p in range(count)])  14.1 us
    ppermute x15, starting transfers between devices, send(): return lax.ppermute(value, axis, [(p, target(p)) for p in range(count)])  13.3 us
    unnamed x6, local copies, waits for them, and re-layouts  2.72 us
  transfers between devices with their start and end apart: 15, of which 8 were waited for; matrix products, arithmetic and copies ran while one was open for 0% of the time, Pallas kernels for 33%

profile of v16, /device:TPU:0, one launch (start us, length us, event | category | flops | bytes accessed | tf_op | source)
XLA Modules:
  0.0 53.7 jit_solution(9879515142735856276)
XLA Ops:
  0.6 0.5 collective-permute-start
  1.2 2.6 %collective-permute-start.3 = (bf16[192,1152]{1,0:T(8,128)(2,1)}, bf16[192,1152]{1,0:T(8,128)(2,1)S(1)}, u32[]{:S(2)}, u32[]{:S(2)}) collective-permute-start(bf16[192,1152]{1,0:T(8,128)(2,1)} %bitcast.6), channel_id=1, source_target_pairs={{0,16},{8,24},{16,0},{24,8},{1,17},{9,25},{17,1},{25,9},{2,18},{10... | collective-permute-start | bytes 1327112 | tf_op jit(solution)/shard_map/ppermute | solution.py:34
  5.0 0.0 collective-permute-done.f1
  5.0 0.0 copy-start
  5.0 1.0 %copy-done = bf16[192,1,1152]{2,0,1:T(8,128)(2,1)S(1)} copy-done((bf16[192,1,1152]{2,0,1:T(8,128)(2,1)S(1)}, bf16[192,1,1152]{2,0,1:T(8,128)(2,1)}, u32[]{:S(2)}) %copy-start) | copy-done | bytes 442392
  6.0 0.0 copy-start.1
  6.0 1.0 %copy-done.1 = bf16[192,1,1152]{2,0,1:T(8,128)(2,1)S(1)} copy-done((bf16[192,1,1152]{2,0,1:T(8,128)(2,1)S(1)}, bf16[192,1,1152]{2,0,1:T(8,128)(2,1)}, u32[]{:S(2)}) %copy-start.1) | copy-done | bytes 442392
  7.1 0.0 copy-start.2
  7.1 0.7 %copy-done.2 = f32[1152]{0:T(1024)S(1)} copy-done((f32[1152]{0:T(1024)S(1)}, f32[1152]{0:T(1024)}, u32[]{:S(2)}) %copy-start.2) | copy-done | bytes 4632
  7.7 4.2 %shard_map.93 = (bf16[192,1152]{1,0:T(8,128)(2,1)S(1)}, bf16[1152,1152]{1,0:T(8,128)(2,1)S(1)}, bf16[192,1152]{1,0:T(8,128)(2,1)S(1)}, f32[1,1152]{1,0:T(1,128)S...) custom-call(f32[1]{0:T(128)S(6)} %copy.10.scale, ...), custom_call_target="tpu_custom_call" | custom-call | flops 1019215872 | bytes 3538944 | tf_op jit(solution)/shard_map/pallas_call | solution.py:138
  12.0 0.2 collective-permute-start.1
  12.2 0.6 %collective-permute-start.2 = (bf16[192,1152]{1,0:T(8,128)(2,1)S(1)}, bf16[192,1152]{1,0:T(8,128)(2,1)S(1)}, u32[]{:S(2)}, u32[]{:S(2)}) collective-permute-start(bf16[192,1152]{1,0:T(8,128)(2,1)S(1)} %get-tuple-element.64.text_own), channel_id=1, source_target_pairs={{0,16},{8,24},{16,0},{24,8},{1,17},{9,25},{17,1},{25,9},{2,18},{10... | collective-permute-start | bytes 1327112 | tf_op jit(solution)/shard_map/ppermute | solution.py:34
  12.8 1.9 %collective-permute-done.3.f2 = bf16[192,1152]{1,0:T(8,128)(2,1)S(1)} collective-permute-done((bf16[192,1152]{1,0:T(8,128)(2,1)}, bf16[192,1152]{1,0:T(8,128)(2,1)S(1)}, u32[]{:S(2)}, u32[]{:S(2)}) %collective-permute-start.3) | collective-permute-done | bytes 442400 | tf_op jit(solution)/shard_map/ppermute | solution.py:34
  14.7 0.1 collective-permute-start.4
  14.8 0.5 collective-permute-start.5
  15.3 0.0 collective-permute-done.1.t1
  15.3 1.7 %shard_map.94 = (bf16[384,1152]{1,0:T(8,128)(2,1)S(1)}, bf16[1152,384]{1,0:T(8,128)(2,1)S(1)}, bf16[1152,384]{1,0:T(8,128)(2,1)S(1)}, bf16[288,384]{1,0:T(8,128)...) custom-call(f32[1]{0:T(128)S(6)} %copy.10.scale, ...), custom_call_target="tpu_custom_call" | custom-call | flops 1000 | bytes 1000 | tf_op jit(solution)/shard_map/pallas_call | solution.py:138
  17.0 0.0 collective-permute-done.5.f3_tail
  17.0 0.0 collective-permute-done.4.f3_head
  17.0 4.6 %shard_map.96 = (bf16[1152,384]{1,0:T(8,128)(2,1)S(1)}, bf16[384,1152]{1,0:T(8,128)(2,1)S(1)}, bf16[1152,384]{1,0:T(8,128)(2,1)S(1)}, bf16[288,384]{1,0:T(8,128)...) custom-call(f32[1]{0:T(128)S(6)} %copy.10.scale, ...), custom_call_target="tpu_custom_call" | custom-call | flops 1000 | bytes 1000 | tf_op jit(solution)/shard_map/pallas_call | solution.py:138
  21.7 2.0 %shard_map.97 = (bf16[192,1152]{1,0:T(8,128)(2,1)}, f32[8,128]{1,0:T(8,128)S(1)}) custom-call(f32[1]{0:T(128)S(6)} %copy.10.scale, bf16[192,1152]{1,0:T(8,128)(2,1)S(1)} %get-tuple-element.67.text, bf16[384,384]{1,0:T(8,128)(2,1)S(1)} %get-tuple-element.68.weights_near, bf16[384,384]{1,0:T(8,128)(2,1)S(1)} %get-tuple-element.72.weights_far, ...), custom_call_target="tpu_custom_call" | custom-call | flops 1000 | bytes 1000 | tf_op jit(solution)/shard_map/pallas_call | solution.py:138
  23.7 0.9 %collective-permute-done.2.text_unit.text_third = bf16[192,1152]{1,0:T(8,128)(2,1)S(1)} collective-permute-done((bf16[192,1152]{1,0:T(8,128)(2,1)S(1)}, bf16[192,1152]{1,0:T(8,128)(2,1)S(1)}, u32[]{:S(2)}, u32[]{:S(2)}) %collective-permute-start.2) | collective-permute-done | bytes 442400 | tf_op jit(solution)/shard_map/ppermute | solution.py:34
  24.6 0.0 collective-permute-start.6
  24.6 1.3 %shard_map.98 = (bf16[192,768]{1,0:T(8,128)(2,1)S(1)}, f32[288,384]{1,0:T(8,128)S(1)}, f32[288,384]{1,0:T(8,128)S(1)}, f32[1,768]{1,0:T(1,128)S(1)}) custom-call(f32[1]{0:T(128)S(6)} %copy.10.scale, f32[1]{0:T(128)S(6)} %copy.11.bias, bf16[192,1152]{1,0:T(8,128)(2,1)S(1)} %collective-permute-done.2.text_unit.text_third, ...), custom_call_target="tpu_custom_call" | custom-call | flops 1019215872 | bytes 3538944 | tf_op jit(solution)/shard_map/pallas_call | solution.py:138
  26.0 0.5 collective-permute-done.6.text_unit.text_fourth
  26.4 2.7 %shard_map.99 = (bf16[2,176,256]{2,1,0:T(8,128)(2,1)S(1)}, bf16[2,176,256]{2,1,0:T(8,128)(2,1)S(1)}, bf16[4,176,256]{2,1,0:T(8,128)(2,1)S(1)}, bf16[192,768]{1,0:T(8,128)(2,1)S(1)}) custom-call(f32[1]{0:T(128)S(6)} %copy.10.scale, f32[1]{0:T(128)S(6)} %copy.11.bias, bf16[192,1152]{1,0:T(8,128)(2,1)S(1)} %collective-permute-done.6.text_unit.text_fourth, ...), custom_call_target="tpu_custom_call" | custom-call | flops 2038431744 | bytes 7077888 | tf_op jit(solution)/shard_map/pallas_call | solution.py:138
  29.2 1.6 %collective-permute-start.7 = (bf16[2,176,256]{2,1,0:T(8,128)(2,1)S(1)}, bf16[2,176,256]{2,1,0:T(8,128)(2,1)S(1)}, u32[]{:S(2)}, u32[]{:S(2)}) collective-permute-start(bf16[2,176,256]{2,1,0:T(8,128)(2,1)S(1)} %get-tuple-element.101), channel_id=1, source_target_pairs={{0,1},{1,0},{2,3},{3,2},{4,5},{5,4},{6,7},{7,6},{8,9},{9,8},{10,11... | collective-permute-start | bytes 540680 | tf_op jit(solution)/shard_map/ppermute | solution.py:34
  30.7 2.1 %shard_map.100 = (f32[192,1152]{1,0:T(8,128)S(1)}, f32[8,128]{1,0:T(8,128)S(1)}) custom-call(f32[1]{0:T(128)S(6)} %copy.10.scale, bf16[1152,1152]{1,0:T(8,128)(2,1)S(1)} %get-tuple-element.60.proj, bf16[384,1152]{1,0:T(8,128)(2,1)S(1)} %get-tuple-element.66.text_near, bf16[192,1152]{1,0:T(8,128)(2,1)S(1)} %collective-permute-done.2.text_unit.text_third, ...), custom_call_target="tpu_custom_call" | custom-call | flops 1000 | bytes 1000 | tf_op jit(solution)/shard_map/pallas_call | solution.py:138
  32.9 0.6 %collective-permute-start.8 = (bf16[2,176,256]{2,1,0:T(8,128)(2,1)S(1)}, bf16[2,176,256]{2,1,0:T(8,128)(2,1)S(1)}, u32[]{:S(2)}, u32[]{:S(2)}) collective-permute-start(bf16[2,176,256]{2,1,0:T(8,128)(2,1)S(1)} %get-tuple-element.103), channel_id=1, source_target_pairs={{0,1},{1,0},{2,3},{3,2},{4,5},{5,4},{6,7},{7,6},{8,9},{9,8},{10,11... | collective-permute-start | bytes 540680 | tf_op jit(solution)/shard_map/ppermute | solution.py:34
  33.4 2.9 %collective-permute-done.7.come = bf16[2,176,256]{2,1,0:T(8,128)(2,1)S(1)} collective-permute-done((bf16[2,176,256]{2,1,0:T(8,128)(2,1)S(1)}, bf16[2,176,256]{2,1,0:T(8,128)(2,1)S(1)}, u32[]{:S(2)}, u32[]{:S(2)}) %collective-permute-start.7) | collective-permute-done | bytes 180256 | tf_op jit(solution)/shard_map/ppermute | solution.py:34
  36.3 3.7 %collective-permute-start.10 = (bf16[176,256]{1,0:T(8,128)(2,1)S(1)}, bf16[176,256]{1,0:T(8,128)(2,1)S(1)}, u32[]{:S(2)}, u32[]{:S(2)}) collective-permute-start(bf16[176,256]{1,0:T(8,128)(2,1)S(1)} %get-tuple-element.108), channel_id=1, source_target_pairs={{0,6},{1,7},{2,4},{3,5},{4,2},{5,3},{6,0},{7,1},{8,14},{9,15},{10,... | collective-permute-start | bytes 270344 | tf_op jit(solution)/shard_map/ppermute | solution.py:34
  40.0 0.0 collective-permute-start.9
  40.0 0.0 collective-permute-done.8.come
  40.0 1.4 %collective-permute-start.11 = (bf16[176,256]{1,0:T(8,128)(2,1)S(1)}, bf16[176,256]{1,0:T(8,128)(2,1)S(1)}, u32[]{:S(2)}, u32[]{:S(2)}) collective-permute-start(bf16[176,256]{1,0:T(8,128)(2,1)S(1)} %get-tuple-element.109), channel_id=1, source_target_pairs={{0,2},{1,3},{2,0},{3,1},{4,6},{5,7},{6,4},{7,5},{8,10},{9,11},{10,... | collective-permute-start | bytes 270344 | tf_op jit(solution)/shard_map/ppermute | solution.py:34
  41.5 1.7 %shard_map.103 = (bf16[192,1152]{1,0:T(8,128)(2,1)}, f32[8,128]{1,0:T(8,128)S(1)}) custom-call(bf16[192,1152]{1,0:T(8,128)(2,1)S(1)} %get-tuple-element.58.features, f32[1,1152]{1,0:T(1,128)S(1)} %get-tuple-element.59.gain, f32[192,1152]{1,0:T(8,128)S(1)} %get-tuple-element.96.norm_back, bf16[176,256]{1,0:T(8,128)(2,1)S(1)} %get-tuple-element.104.before.own), custom_call_target="tpu_custom_call" | custom-call | bytes 5308416 | tf_op jit(solution)/shard_map/pallas_call | solution.py:138
  43.2 0.1 collective-permute-done.10.three_on
  43.3 3.5 %collective-permute-done.9.two_on = bf16[176,256]{1,0:T(8,128)(2,1)S(1)} collective-permute-done((bf16[176,256]{1,0:T(8,128)(2,1)S(1)}, bf16[176,256]{1,0:T(8,128)(2,1)S(1)}, u32[]{:S(2)}, u32[]{:S(2)}) %collective-permute-start.9) | collective-permute-done | bytes 90144 | tf_op jit(solution)/shard_map/ppermute | solution.py:34
  46.8 0.0 collective-permute-done.11.next_one
  46.8 0.1 shard_map.105.refs_0_
  46.9 1.6 %collective-permute-start.13 = (bf16[176,256]{1,0:T(8,128)(2,1)S(1)}, bf16[176,256]{1,0:T(8,128)(2,1)S(1)}, u32[]{:S(2)}, u32[]{:S(2)}) collective-permute-start(bf16[176,256]{1,0:T(8,128)(2,1)S(1)} %shard_map.105.refs_0_), channel_id=1, source_target_pairs={{0,16},{8,24},{16,0},{24,8},{1,17},{9,25},{17,1},{25,9},{2,18},{10... | collective-permute-start | bytes 270344 | tf_op jit(solution)/shard_map/ppermute | solution.py:34
  48.4 0.0 collective-permute-start.12
  48.4 3.0 %collective-permute-done.13.refs_2_ = bf16[176,256]{1,0:T(8,128)(2,1)S(1)} collective-permute-done((bf16[176,256]{1,0:T(8,128)(2,1)S(1)}, bf16[176,256]{1,0:T(8,128)(2,1)S(1)}, u32[]{:S(2)}, u32[]{:S(2)}) %collective-permute-start.13) | collective-permute-done | bytes 90144 | tf_op jit(solution)/shard_map/ppermute | solution.py:34
  51.5 0.0 collective-permute-start.14
  51.5 0.0 collective-permute-done.12.refs_1_
  51.5 1.3 %collective-permute-done.14.refs_3_ = bf16[176,256]{1,0:T(8,128)(2,1)S(1)} collective-permute-done((bf16[176,256]{1,0:T(8,128)(2,1)S(1)}, bf16[176,256]{1,0:T(8,128)(2,1)S(1)}, u32[]{:S(2)}, u32[]{:S(2)}) %collective-permute-start.14) | collective-permute-done | bytes 90144 | tf_op jit(solution)/shard_map/ppermute | solution.py:34
  52.7 1.0 %shard_map.106 = (f32[144,1152]{1,0:T(8,128)}, f32[1152]{0:T(1024)}) custom-call(bf16[176,256]{1,0:T(8,128)(2,1)S(1)} %shard_map.105.refs_0_, bf16[176,256]{1,0:T(8,128)(2,1)S(1)} %collective-permute-done.12.refs_1_, bf16[176,256]{1,0:T(8,128)(2,1)S(1)} %collective-permute-done.13.refs_2_, bf16[176,256]{1,0:T(8,128)(2,1)S(1)} %collective-permute-done.14.refs_3_), custom_call_target="tpu_custom_call" | custom-call | bytes 1327104 | tf_op jit(solution)/shard_map/pallas_call | solution.py:138
  (4 shorter events, 0.1 us)
Async XLA Ops:
  0.6 4.4 %collective-permute-start = (bf16[192,1152]{1,0:T(8,128)(2,1)}, bf16[192,1152]{1,0:T(8,128)(2,1)S(1)}, u32[]{:S(2)}, u32[]{:S(2)}) collective-permute-start(bf16[192,1152]{1,0:T(8,128)(2,1)} %bitcast.5), channel_id=1, source_target_pairs={{0,8},{8,0},{16,24},{24,16},{1,9},{9,1},{17,25},{25,17},{2,10},{10... | collective-permute-start | bytes 1327112 | tf_op jit(solution)/shard_map/ppermute | solution.py:34
  1.2 13.5 %collective-permute-start.3 = (bf16[192,1152]{1,0:T(8,128)(2,1)}, bf16[192,1152]{1,0:T(8,128)(2,1)S(1)}, u32[]{:S(2)}, u32[]{:S(2)}) collective-permute-start(bf16[192,1152]{1,0:T(8,128)(2,1)} %bitcast.6), channel_id=1, source_target_pairs={{0,16},{8,24},{16,0},{24,8},{1,17},{9,25},{17,1},{25,9},{2,18},{10... | collective-permute-start | bytes 1327112 | tf_op jit(solution)/shard_map/ppermute | solution.py:34
  5.0 1.0 %copy-start = (bf16[192,1,1152]{2,0,1:T(8,128)(2,1)S(1)}, bf16[192,1,1152]{2,0,1:T(8,128)(2,1)}, u32[]{:S(2)}) copy-start(bf16[192,1,1152]{2,0,1:T(8,128)(2,1)} %param.7) | copy-start | bytes 1327108
  6.0 1.0 %copy-start.1 = (bf16[192,1,1152]{2,0,1:T(8,128)(2,1)S(1)}, bf16[192,1,1152]{2,0,1:T(8,128)(2,1)}, u32[]{:S(2)}) copy-start(bf16[192,1,1152]{2,0,1:T(8,128)(2,1)} %param.6) | copy-start | bytes 1327108
  7.1 0.7 %copy-start.2 = (f32[1152]{0:T(1024)S(1)}, f32[1152]{0:T(1024)}, u32[]{:S(2)}) copy-start(f32[1152]{0:T(1024)} %gain_line.1) | copy-start | bytes 13828
  12.0 3.3 %collective-permute-start.1 = (bf16[192,1152]{1,0:T(8,128)(2,1)S(1)}, bf16[192,1152]{1,0:T(8,128)(2,1)S(1)}, u32[]{:S(2)}, u32[]{:S(2)}) collective-permute-start(bf16[192,1152]{1,0:T(8,128)(2,1)S(1)} %get-tuple-element.64.text_own), channel_id=1, source_target_pairs={{0,8},{8,0},{16,24},{24,16},{1,9},{9,1},{17,25},{25,17},{2,10},{10... | collective-permute-start | bytes 1327112 | tf_op jit(solution)/shard_map/ppermute | solution.py:34
  12.2 12.4 %collective-permute-start.2 = (bf16[192,1152]{1,0:T(8,128)(2,1)S(1)}, bf16[192,1152]{1,0:T(8,128)(2,1)S(1)}, u32[]{:S(2)}, u32[]{:S(2)}) collective-permute-start(bf16[192,1152]{1,0:T(8,128)(2,1)S(1)} %get-tuple-element.64.text_own), channel_id=1, source_target_pairs={{0,16},{8,24},{16,0},{24,8},{1,17},{9,25},{17,1},{25,9},{2,18},{10... | collective-permute-start | bytes 1327112 | tf_op jit(solution)/shard_map/ppermute | solution.py:34
  14.7 2.3 %collective-permute-start.4 = (bf16[160,1152]{1,0:T(8,128)(2,1)S(1)}, bf16[160,1152]{1,0:T(8,128)(2,1)S(1)}, u32[]{:S(2)}, u32[]{:S(2)}) collective-permute-start(bf16[160,1152]{1,0:T(8,128)(2,1)S(1)} %get-tuple-element.69), channel_id=1, source_target_pairs={{0,8},{8,0},{16,24},{24,16},{1,9},{9,1},{17,25},{25,17},{2,10},{10... | collective-permute-start | bytes 1105928 | tf_op jit(solution)/shard_map/ppermute | solution.py:34
  14.8 2.2 %collective-permute-start.5 = (bf16[32,1152]{1,0:T(8,128)(2,1)S(1)}, bf16[32,1152]{1,0:T(8,128)(2,1)S(1)}, u32[]{:S(2)}, u32[]{:S(2)}) collective-permute-start(bf16[32,1152]{1,0:T(8,128)(2,1)S(1)} %get-tuple-element.70), channel_id=1, source_target_pairs={{0,8},{8,0},{16,24},{24,16},{1,9},{9,1},{17,25},{25,17},{2,10},{10... | collective-permute-start | bytes 221192 | tf_op jit(solution)/shard_map/ppermute | solution.py:34
  24.6 1.8 %collective-permute-start.6 = (bf16[192,1152]{1,0:T(8,128)(2,1)S(1)}, bf16[192,1152]{1,0:T(8,128)(2,1)S(1)}, u32[]{:S(2)}, u32[]{:S(2)}) collective-permute-start(bf16[192,1152]{1,0:T(8,128)(2,1)S(1)} %collective-permute-done.2.text_unit.text_third), channel_id=1, source_target_pairs={{0,8},{8,0},{16,24},{24,16},{1,9},{9,1},{17,25},{25,17},{2,10},{10... | collective-permute-start | bytes 1327112 | tf_op jit(solution)/shard_map/ppermute | solution.py:34
  29.2 7.1 %collective-permute-start.7 = (bf16[2,176,256]{2,1,0:T(8,128)(2,1)S(1)}, bf16[2,176,256]{2,1,0:T(8,128)(2,1)S(1)}, u32[]{:S(2)}, u32[]{:S(2)}) collective-permute-start(bf16[2,176,256]{2,1,0:T(8,128)(2,1)S(1)} %get-tuple-element.101), channel_id=1, source_target_pairs={{0,1},{1,0},{2,3},{3,2},{4,5},{5,4},{6,7},{7,6},{8,9},{9,8},{10,11... | collective-permute-start | bytes 540680 | tf_op jit(solution)/shard_map/ppermute | solution.py:34
  32.9 7.1 %collective-permute-start.8 = (bf16[2,176,256]{2,1,0:T(8,128)(2,1)S(1)}, bf16[2,176,256]{2,1,0:T(8,128)(2,1)S(1)}, u32[]{:S(2)}, u32[]{:S(2)}) collective-permute-start(bf16[2,176,256]{2,1,0:T(8,128)(2,1)S(1)} %get-tuple-element.103), channel_id=1, source_target_pairs={{0,1},{1,0},{2,3},{3,2},{4,5},{5,4},{6,7},{7,6},{8,9},{9,8},{10,11... | collective-permute-start | bytes 540680 | tf_op jit(solution)/shard_map/ppermute | solution.py:34
  36.3 7.0 %collective-permute-start.10 = (bf16[176,256]{1,0:T(8,128)(2,1)S(1)}, bf16[176,256]{1,0:T(8,128)(2,1)S(1)}, u32[]{:S(2)}, u32[]{:S(2)}) collective-permute-start(bf16[176,256]{1,0:T(8,128)(2,1)S(1)} %get-tuple-element.108), channel_id=1, source_target_pairs={{0,6},{1,7},{2,4},{3,5},{4,2},{5,3},{6,0},{7,1},{8,14},{9,15},{10,... | collective-permute-start | bytes 270344 | tf_op jit(solution)/shard_map/ppermute | solution.py:34
  40.0 6.8 %collective-permute-start.9 = (bf16[176,256]{1,0:T(8,128)(2,1)S(1)}, bf16[176,256]{1,0:T(8,128)(2,1)S(1)}, u32[]{:S(2)}, u32[]{:S(2)}) collective-permute-start(bf16[176,256]{1,0:T(8,128)(2,1)S(1)} %get-tuple-element.102.before), channel_id=1, source_target_pairs={{0,4},{1,5},{2,6},{3,7},{4,0},{5,1},{6,2},{7,3},{8,12},{9,13},{10,... | collective-permute-start | bytes 270344 | tf_op jit(solution)/shard_map/ppermute | solution.py:34
  40.0 6.8 %collective-permute-start.11 = (bf16[176,256]{1,0:T(8,128)(2,1)S(1)}, bf16[176,256]{1,0:T(8,128)(2,1)S(1)}, u32[]{:S(2)}, u32[]{:S(2)}) collective-permute-start(bf16[176,256]{1,0:T(8,128)(2,1)S(1)} %get-tuple-element.109), channel_id=1, source_target_pairs={{0,2},{1,3},{2,0},{3,1},{4,6},{5,7},{6,4},{7,5},{8,10},{9,11},{10,... | collective-permute-start | bytes 270344 | tf_op jit(solution)/shard_map/ppermute | solution.py:34
  46.9 4.6 %collective-permute-start.13 = (bf16[176,256]{1,0:T(8,128)(2,1)S(1)}, bf16[176,256]{1,0:T(8,128)(2,1)S(1)}, u32[]{:S(2)}, u32[]{:S(2)}) collective-permute-start(bf16[176,256]{1,0:T(8,128)(2,1)S(1)} %shard_map.105.refs_0_), channel_id=1, source_target_pairs={{0,16},{8,24},{16,0},{24,8},{1,17},{9,25},{17,1},{25,9},{2,18},{10... | collective-permute-start | bytes 270344 | tf_op jit(solution)/shard_map/ppermute | solution.py:34
  48.4 3.0 %collective-permute-start.12 = (bf16[176,256]{1,0:T(8,128)(2,1)S(1)}, bf16[176,256]{1,0:T(8,128)(2,1)S(1)}, u32[]{:S(2)}, u32[]{:S(2)}) collective-permute-start(bf16[176,256]{1,0:T(8,128)(2,1)S(1)} %shard_map.105.refs_0_), channel_id=1, source_target_pairs={{0,8},{8,0},{16,24},{24,16},{1,9},{9,1},{17,25},{25,17},{2,10},{10... | collective-permute-start | bytes 270344 | tf_op jit(solution)/shard_map/ppermute | solution.py:34
  51.5 1.3 %collective-permute-start.14 = (bf16[176,256]{1,0:T(8,128)(2,1)S(1)}, bf16[176,256]{1,0:T(8,128)(2,1)S(1)}, u32[]{:S(2)}, u32[]{:S(2)}) collective-permute-start(bf16[176,256]{1,0:T(8,128)(2,1)S(1)} %collective-permute-done.13.refs_2_), channel_id=1, source_target_pairs={{0,8},{8,0},{16,24},{24,16},{1,9},{9,1},{17,25},{25,17},{2,10},{10... | collective-permute-start | bytes 270344 | tf_op jit(solution)/shard_map/ppermute | solution.py:34

commit v17 on v16

--- a/solution.py
+++ b/solution.py
@@ -332,7 +332,7 @@
 def partial_body(
     members, groups, scale, bias, text_unit, flat_near, flat_far, totals, back_near, back_far, unit_turned_near,
     unit_turned_far, inverse_near, inverse_far, turned_near, turned_far, proj_columns, gain,
-    across_first, across_later, keep, weights, text_columns, dots, packed,
+    across_three, across_near, across_own, keep, weights, text_columns, dots, packed,
 ):
     rows = text_unit.shape[0]
     near = 2 * rows
@@ -376,9 +376,10 @@
         packed[group, count - BAND :, full - LANES :] = gain_tile
 
     own = lax.axis_index("rep")
-    for at in range(2):
-        across_first[at] = packed[own ^ 1 ^ (4 + 2 * at)]
-        across_later[at] = packed[own ^ 1 ^ (2 * at)]
+    across_three[...] = packed[own ^ 7]
+    across_near[0] = packed[own ^ 3]
+    across_near[1] = packed[own ^ 5]
+    across_own[...] = packed[own ^ 1]
     for at in range(4):
         keep[at] = packed[own ^ (2 * at)]
 
@@ -445,16 +446,21 @@
     token[...] = jnp.zeros_like(token)
 
 
-def pair_sum_body(first, before, keep, come, low, high):
-    for at, target in enumerate((low, high)):
-        target[...] = (keep[first + at].astype(F32) + come[at].astype(F32)).astype(BF16)
+def three_sum_body(before, keep, come, total):
+    total[...] = (keep[3].astype(F32) + come[...].astype(F32)).astype(BF16)
+
+
+def near_sum_body(before, keep, come, next_one, two_on):
+    for at, target in enumerate((next_one, two_on)):
+        target[...] = (keep[1 + at].astype(F32) + come[at].astype(F32)).astype(BF16)
 
 
 def far_sum_body(before, two_on, three_on, total):
     total[...] = two_on[...].astype(F32) + three_on[...].astype(F32)
 
 
-def last_sum_body(far, own, next_one, two_on, three_on, total, ordered):
+def last_sum_body(far, keep, come, next_one, two_on, three_on, total, ordered, own):
+    own[...] = (keep[0].astype(F32) + come[...].astype(F32)).astype(BF16)
     parts = (own, next_one, two_on, three_on)
     total[...] = (own[...].astype(F32) + next_one[...].astype(F32) + far[...]).astype(BF16)
     count, full = total.shape
@@ -583,7 +589,7 @@
 
     outs = call(
         functools.partial(partial_body, members, groups),
-        [((2,) + packet, BF16)] * 2 + [((4,) + packet, BF16), narrow],
+        [(packet, BF16), ((2,) + packet, BF16), (packet, BF16), ((4,) + packet, BF16), narrow],
         [((rows, columns), BF16), ((rows, every), F32), ((groups,) + packet, BF16)],
         smem=2,
         flops=4 * near * width * width,
@@ -592,8 +598,8 @@
         scale, bias, t3, flat_near, flat_far, totals, back_near, back_far, unit_turned_near, unit_turned_far,
         inverse_near, inverse_far, turned_near, turned_far, proj_columns, gain_row,
     )
-    across_first, across_later, keep, weights_fourth = outs
-    come_first = send(across_first, "rep", lambda p: p ^ 1)
+    across_three, across_near, across_own, keep, weights_fourth = outs
+    come_three = send(across_three, "rep", lambda p: p ^ 1)
     norm_back, token = call(
         image_body,
         [((rows, width), F32), TOKEN],
@@ -606,24 +612,21 @@
         unit_near, factors,
     )
 
-    across_later, token = lax.optimization_barrier((across_later, token))
-    come_later = send(across_later, "rep", lambda p: p ^ 1)
-    two_on, three_on = call(functools.partial(pair_sum_body, 2), [(packet, BF16)] * 2, moved=1000)(
-        token, keep, come_first
-    )
-    first_two = two_on
-    two_on = send(two_on, "rep", lambda p: p ^ 4)
-    three_on = send(three_on, "rep", lambda p: p ^ 6)
-    own_sum, next_one = call(functools.partial(pair_sum_body, 0), [(packet, BF16)] * 2, moved=1000)(
-        first_two, keep, come_later
-    )
-    next_one = send(next_one, "rep", lambda p: p ^ 2)
+    across_near, token = lax.optimization_barrier((across_near, token))
+    come_near = send(across_near, "rep", lambda p: p ^ 1)
+    (three_sum,) = call(three_sum_body, [(packet, BF16)], flops=3000000000, moved=1000)(token, keep, come_three)
+    three_on = send(three_sum, "rep", lambda p: p ^ 6)
+    next_sum, two_sum = call(near_sum_body, [(packet, BF16)] * 2, moved=1000)(three_sum, keep, come_near)
+    two_on = send(two_sum, "rep", lambda p: p ^ 4)
+    next_one = send(next_sum, "rep", lambda p: p ^ 2)
+    across_own, next_sum = lax.optimization_barrier((across_own, next_sum))
+    come_own = send(across_own, "rep", lambda p: p ^ 1)
     feature_grad, token = call(feature_body, [half, TOKEN], moved=12 * near * width)(
-        f0_kept, gain_row, norm_back, own_sum
+        f0_kept, gain_row, norm_back, next_sum
     )
     (far_sum,) = call(far_sum_body, [(packet, F32)], moved=1000)(token, two_on, three_on)
-    (reduced,) = call(last_sum_body, [(packet, BF16)], [((4, BAND, LANES), F32)], moved=1000)(
-        far_sum, own_sum, next_one, two_on, three_on
+    (reduced,) = call(last_sum_body, [(packet, BF16)], [((4, BAND, LANES), F32), (packet, BF16)], moved=1000)(
+        far_sum, keep, come_own, next_one, two_on, three_on
     )
     far_block = send(reduced, "loop", lambda p: p ^ 2)
     near_block = send(reduced, "loop", lambda p: p ^ 1)

time: 54 us -> 54.3 us (level)
  starting transfers between devices: 13.3 us -> 16.6 us
  waiting for transfers between devices: 14.1 us -> 11 us
    ppermute x15 -> x16, starting transfers between devices: 13.3 us -> 16.6 us  [send(): return lax.ppermute(value, axis, [(p, target(p)) for p in range(count)])]
    ppermute x15 -> x16, waiting for transfers between devices: 14.1 us -> 11 us  [send(): return lax.ppermute(value, axis, [(p, target(p)) for p in range(count)])]
  transfers between devices with their start and end apart: 15 -> 16, of which waited for: 8 -> 9; matrix products, arithmetic and copies ran while one was open for 0% -> 0% of each run, Pallas kernels for 33% -> 33%
where the time goes in v17:
time: 54.3 us; the launch traced here: 54 us
  Pallas kernels  21.6 us (40%)
  starting transfers between devices  16.6 us (31%)
  waiting for transfers between devices  11 us (20%)
  local copies, waits for them, and re-layouts  2.72 us (5%)
  between operations  2.05 us (4%)
    pallas_call x14, Pallas kernels, run(): pl.pallas_call(body, out_shape=[jax.ShapeDtypeStruct(shape, kind) for sha...  21.6 us
    ppermute x16, starting transfers between devices, send(): return lax.ppermute(value, axis, [(p, target(p)) for p in range(count)])  16.6 us
    ppermute x16, waiting for transfers between devices, send(): return lax.ppermute(value, axis, [(p, target(p)) for p in range(count)])  11 us
    unnamed x6, local copies, waits for them, and re-layouts  2.72 us
  transfers between devices with their start and end apart: 16, of which 9 were waited for; matrix products, arithmetic and copies ran while one was open for 0% of the time, Pallas kernels for 33%

profile of v17, /device:TPU:0, one launch (start us, length us, event | category | flops | bytes accessed | tf_op | source)
XLA Modules:
  0.0 54.0 jit_solution(12650329057154849055)
XLA Ops:
  0.6 0.5 collective-permute-start
  1.2 2.6 %collective-permute-start.3 = (bf16[192,1152]{1,0:T(8,128)(2,1)}, bf16[192,1152]{1,0:T(8,128)(2,1)S(1)}, u32[]{:S(2)}, u32[]{:S(2)}) collective-permute-start(bf16[192,1152]{1,0:T(8,128)(2,1)} %bitcast.6), channel_id=1, source_target_pairs={{0,16},{8,24},{16,0},{24,8},{1,17},{9,25},{17,1},{25,9},{2,18},{10... | collective-permute-start | bytes 1327112 | tf_op jit(solution)/shard_map/ppermute | solution.py:34
  5.0 0.0 collective-permute-done.f1
  5.0 0.0 copy-start
  5.0 1.0 %copy-done = bf16[192,1,1152]{2,0,1:T(8,128)(2,1)S(1)} copy-done((bf16[192,1,1152]{2,0,1:T(8,128)(2,1)S(1)}, bf16[192,1,1152]{2,0,1:T(8,128)(2,1)}, u32[]{:S(2)}) %copy-start) | copy-done | bytes 442392
  6.0 0.0 copy-start.1
  6.0 1.0 %copy-done.1 = bf16[192,1,1152]{2,0,1:T(8,128)(2,1)S(1)} copy-done((bf16[192,1,1152]{2,0,1:T(8,128)(2,1)S(1)}, bf16[192,1,1152]{2,0,1:T(8,128)(2,1)}, u32[]{:S(2)}) %copy-start.1) | copy-done | bytes 442392
  7.1 0.0 copy-start.2
  7.1 0.7 %copy-done.2 = f32[1152]{0:T(1024)S(1)} copy-done((f32[1152]{0:T(1024)S(1)}, f32[1152]{0:T(1024)}, u32[]{:S(2)}) %copy-start.2) | copy-done | bytes 4632
  7.7 4.2 %shard_map.93 = (bf16[192,1152]{1,0:T(8,128)(2,1)S(1)}, bf16[1152,1152]{1,0:T(8,128)(2,1)S(1)}, bf16[192,1152]{1,0:T(8,128)(2,1)S(1)}, f32[1,1152]{1,0:T(1,128)S...) custom-call(f32[1]{0:T(128)S(6)} %copy.10.scale, ...), custom_call_target="tpu_custom_call" | custom-call | flops 1019215872 | bytes 3538944 | tf_op jit(solution)/shard_map/pallas_call | solution.py:138
  12.0 0.2 collective-permute-start.1
  12.2 0.6 %collective-permute-start.2 = (bf16[192,1152]{1,0:T(8,128)(2,1)S(1)}, bf16[192,1152]{1,0:T(8,128)(2,1)S(1)}, u32[]{:S(2)}, u32[]{:S(2)}) collective-permute-start(bf16[192,1152]{1,0:T(8,128)(2,1)S(1)} %get-tuple-element.65.text_own), channel_id=1, source_target_pairs={{0,16},{8,24},{16,0},{24,8},{1,17},{9,25},{17,1},{25,9},{2,18},{10... | collective-permute-start | bytes 1327112 | tf_op jit(solution)/shard_map/ppermute | solution.py:34
  12.8 1.9 %collective-permute-done.3.f2 = bf16[192,1152]{1,0:T(8,128)(2,1)S(1)} collective-permute-done((bf16[192,1152]{1,0:T(8,128)(2,1)}, bf16[192,1152]{1,0:T(8,128)(2,1)S(1)}, u32[]{:S(2)}, u32[]{:S(2)}) %collective-permute-start.3) | collective-permute-done | bytes 442400 | tf_op jit(solution)/shard_map/ppermute | solution.py:34
  14.7 0.1 collective-permute-start.4
  14.8 0.5 collective-permute-start.5
  15.3 0.0 collective-permute-done.1.t1
  15.3 1.7 %shard_map.94 = (bf16[384,1152]{1,0:T(8,128)(2,1)S(1)}, bf16[1152,384]{1,0:T(8,128)(2,1)S(1)}, bf16[1152,384]{1,0:T(8,128)(2,1)S(1)}, bf16[288,384]{1,0:T(8,128)...) custom-call(f32[1]{0:T(128)S(6)} %copy.10.scale, ...), custom_call_target="tpu_custom_call" | custom-call | flops 1000 | bytes 1000 | tf_op jit(solution)/shard_map/pallas_call | solution.py:138
  17.0 0.0 collective-permute-done.5.f3_tail
  17.0 0.0 collective-permute-done.4.f3_head
  17.0 4.6 %shard_map.96 = (bf16[1152,384]{1,0:T(8,128)(2,1)S(1)}, bf16[384,1152]{1,0:T(8,128)(2,1)S(1)}, bf16[1152,384]{1,0:T(8,128)(2,1)S(1)}, bf16[288,384]{1,0:T(8,128)...) custom-call(f32[1]{0:T(128)S(6)} %copy.10.scale, ...), custom_call_target="tpu_custom_call" | custom-call | flops 1000 | bytes 1000 | tf_op jit(solution)/shard_map/pallas_call | solution.py:138
  21.7 2.0 %shard_map.97 = (bf16[192,1152]{1,0:T(8,128)(2,1)}, f32[8,128]{1,0:T(8,128)S(1)}) custom-call(f32[1]{0:T(128)S(6)} %copy.10.scale, bf16[192,1152]{1,0:T(8,128)(2,1)S(1)} %get-tuple-element.68.text, bf16[384,384]{1,0:T(8,128)(2,1)S(1)} %get-tuple-element.69.weights_near, bf16[384,384]{1,0:T(8,128)(2,1)S(1)} %get-tuple-element.73.weights_far, ...), custom_call_target="tpu_custom_call" | custom-call | flops 1000 | bytes 1000 | tf_op jit(solution)/shard_map/pallas_call | solution.py:138
  23.7 0.9 %collective-permute-done.2.text_unit.text_third = bf16[192,1152]{1,0:T(8,128)(2,1)S(1)} collective-permute-done((bf16[192,1152]{1,0:T(8,128)(2,1)S(1)}, bf16[192,1152]{1,0:T(8,128)(2,1)S(1)}, u32[]{:S(2)}, u32[]{:S(2)}) %collective-permute-start.2) | collective-permute-done | bytes 442400 | tf_op jit(solution)/shard_map/ppermute | solution.py:34
  24.6 0.0 collective-permute-start.6
  24.6 1.3 %shard_map.98 = (bf16[192,768]{1,0:T(8,128)(2,1)S(1)}, f32[288,384]{1,0:T(8,128)S(1)}, f32[288,384]{1,0:T(8,128)S(1)}, f32[1,768]{1,0:T(1,128)S(1)}) custom-call(f32[1]{0:T(128)S(6)} %copy.10.scale, f32[1]{0:T(128)S(6)} %copy.11.bias, bf16[192,1152]{1,0:T(8,128)(2,1)S(1)} %collective-permute-done.2.text_unit.text_third, ...), custom_call_target="tpu_custom_call" | custom-call | flops 1019215872 | bytes 3538944 | tf_op jit(solution)/shard_map/pallas_call | solution.py:138
  26.0 0.5 collective-permute-done.6.text_unit.text_fourth
  26.4 2.7 %shard_map.99 = (bf16[176,256]{1,0:T(8,128)(2,1)S(1)}, bf16[2,176,256]{2,1,0:T(8,128)(2,1)S(1)}, bf16[176,256]{1,0:T(8,128)(2,1)S(1)}, bf16[4,176,256]{2,1,0:T(8,128)(2,1)S(1)}, bf16[192,768]{1,0:T(8,128)(2,1)S(1)}) custom-call(f32[1]{0:T(128)S(6)} %copy.10.scale, f32[1]{0:T(128)S(6)} %copy.11.bias, ...), custom_call_target="tpu_custom_call" | custom-call | flops 2038431744 | bytes 7077888 | tf_op jit(solution)/shard_map/pallas_call | solution.py:138
  29.2 1.6 %collective-permute-start.7 = (bf16[176,256]{1,0:T(8,128)(2,1)S(1)}, bf16[176,256]{1,0:T(8,128)(2,1)S(1)}, u32[]{:S(2)}, u32[]{:S(2)}) collective-permute-start(bf16[176,256]{1,0:T(8,128)(2,1)S(1)} %get-tuple-element.103), channel_id=1, source_target_pairs={{0,1},{1,0},{2,3},{3,2},{4,5},{5,4},{6,7},{7,6},{8,9},{9,8},{10,11... | collective-permute-start | bytes 270344 | tf_op jit(solution)/shard_map/ppermute | solution.py:34
  30.7 2.1 %shard_map.100 = (f32[192,1152]{1,0:T(8,128)S(1)}, f32[8,128]{1,0:T(8,128)S(1)}) custom-call(f32[1]{0:T(128)S(6)} %copy.10.scale, bf16[1152,1152]{1,0:T(8,128)(2,1)S(1)} %get-tuple-element.61.proj, bf16[384,1152]{1,0:T(8,128)(2,1)S(1)} %get-tuple-element.67.text_near, bf16[192,1152]{1,0:T(8,128)(2,1)S(1)} %collective-permute-done.2.text_unit.text_third, ...), custom_call_target="tpu_custom_call" | custom-call | flops 1000 | bytes 1000 | tf_op jit(solution)/shard_map/pallas_call | solution.py:138
  32.9 0.6 %collective-permute-start.8 = (bf16[2,176,256]{2,1,0:T(8,128)(2,1)S(1)}, bf16[2,176,256]{2,1,0:T(8,128)(2,1)S(1)}, u32[]{:S(2)}, u32[]{:S(2)}) collective-permute-start(bf16[2,176,256]{2,1,0:T(8,128)(2,1)S(1)} %get-tuple-element.104), channel_id=1, source_target_pairs={{0,1},{1,0},{2,3},{3,2},{4,5},{5,4},{6,7},{7,6},{8,9},{9,8},{10,11... | collective-permute-start | bytes 540680 | tf_op jit(solution)/shard_map/ppermute | solution.py:34
  33.4 0.5 %collective-permute-done.7.come = bf16[176,256]{1,0:T(8,128)(2,1)S(1)} collective-permute-done((bf16[176,256]{1,0:T(8,128)(2,1)S(1)}, bf16[176,256]{1,0:T(8,128)(2,1)S(1)}, u32[]{:S(2)}, u32[]{:S(2)}) %collective-permute-start.7) | collective-permute-done | bytes 90144 | tf_op jit(solution)/shard_map/ppermute | solution.py:34
  34.0 3.7 %collective-permute-start.10 = (bf16[176,256]{1,0:T(8,128)(2,1)S(1)}, bf16[176,256]{1,0:T(8,128)(2,1)S(1)}, u32[]{:S(2)}, u32[]{:S(2)}) collective-permute-start(bf16[176,256]{1,0:T(8,128)(2,1)S(1)} %shard_map.101.before), channel_id=1, source_target_pairs={{0,6},{1,7},{2,4},{3,5},{4,2},{5,3},{6,0},{7,1},{8,14},{9,15},{10,... | collective-permute-start | bytes 270344 | tf_op jit(solution)/shard_map/ppermute | solution.py:34
  37.7 1.6 %collective-permute-done.8.come = bf16[2,176,256]{2,1,0:T(8,128)(2,1)S(1)} collective-permute-done((bf16[2,176,256]{2,1,0:T(8,128)(2,1)S(1)}, bf16[2,176,256]{2,1,0:T(8,128)(2,1)S(1)}, u32[]{:S(2)}, u32[]{:S(2)}) %collective-permute-start.8) | collective-permute-done | bytes 180256 | tf_op jit(solution)/shard_map/ppermute | solution.py:34
  39.4 2.7 %collective-permute-start.9 = (bf16[176,256]{1,0:T(8,128)(2,1)S(1)}, bf16[176,256]{1,0:T(8,128)(2,1)S(1)}, u32[]{:S(2)}, u32[]{:S(2)}) collective-permute-start(bf16[176,256]{1,0:T(8,128)(2,1)S(1)} %get-tuple-element.110), channel_id=1, source_target_pairs={{0,4},{1,5},{2,6},{3,7},{4,0},{5,1},{6,2},{7,3},{8,12},{9,13},{10,... | collective-permute-start | bytes 270344 | tf_op jit(solution)/shard_map/ppermute | solution.py:34
  42.0 0.5 collective-permute-start.11
  42.5 1.6 %collective-permute-start.12 = (bf16[176,256]{1,0:T(8,128)(2,1)S(1)}, bf16[176,256]{1,0:T(8,128)(2,1)S(1)}, u32[]{:S(2)}, u32[]{:S(2)}) collective-permute-start(bf16[176,256]{1,0:T(8,128)(2,1)S(1)} %get-tuple-element.106.before), channel_id=1, source_target_pairs={{0,2},{1,3},{2,0},{3,1},{4,6},{5,7},{6,4},{7,5},{8,10},{9,11},{10,... | collective-permute-start | bytes 270344 | tf_op jit(solution)/shard_map/ppermute | solution.py:34
  44.1 1.7 %shard_map.103 = (bf16[192,1152]{1,0:T(8,128)(2,1)}, f32[8,128]{1,0:T(8,128)S(1)}) custom-call(bf16[192,1152]{1,0:T(8,128)(2,1)S(1)} %get-tuple-element.59.features, f32[1,1152]{1,0:T(1,128)S(1)} %get-tuple-element.60.gain, f32[192,1152]{1,0:T(8,128)S(1)} %get-tuple-element.97.norm_back, bf16[176,256]{1,0:T(8,128)(2,1)S(1)} %get-tuple-element.106.before), custom_call_target="tpu_custom_call" | custom-call | bytes 5308416 | tf_op jit(solution)/shard_map/pallas_call | solution.py:138
  45.8 0.0 collective-permute-done.10.three_on
  45.8 0.0 collective-permute-done.9.two_on
  45.9 0.7 %collective-permute-done.11.come = bf16[176,256]{1,0:T(8,128)(2,1)S(1)} collective-permute-done((bf16[176,256]{1,0:T(8,128)(2,1)S(1)}, bf16[176,256]{1,0:T(8,128)(2,1)S(1)}, u32[]{:S(2)}, u32[]{:S(2)}) %collective-permute-start.11) | collective-permute-done | bytes 90144 | tf_op jit(solution)/shard_map/ppermute | solution.py:34
  46.6 0.5 collective-permute-done.12.next_one
  47.1 0.1 shard_map.105.refs_0_
  47.1 1.6 %collective-permute-start.14 = (bf16[176,256]{1,0:T(8,128)(2,1)S(1)}, bf16[176,256]{1,0:T(8,128)(2,1)S(1)}, u32[]{:S(2)}, u32[]{:S(2)}) collective-permute-start(bf16[176,256]{1,0:T(8,128)(2,1)S(1)} %shard_map.105.refs_0_), channel_id=1, source_target_pairs={{0,16},{8,24},{16,0},{24,8},{1,17},{9,25},{17,1},{25,9},{2,18},{10... | collective-permute-start | bytes 270344 | tf_op jit(solution)/shard_map/ppermute | solution.py:34
  48.7 0.0 collective-permute-start.13
  48.7 3.0 %collective-permute-done.14.refs_2_ = bf16[176,256]{1,0:T(8,128)(2,1)S(1)} collective-permute-done((bf16[176,256]{1,0:T(8,128)(2,1)S(1)}, bf16[176,256]{1,0:T(8,128)(2,1)S(1)}, u32[]{:S(2)}, u32[]{:S(2)}) %collective-permute-start.14) | collective-permute-done | bytes 90144 | tf_op jit(solution)/shard_map/ppermute | solution.py:34
  51.7 0.0 collective-permute-start.15
  51.7 0.0 collective-permute-done.13.refs_1_
  51.7 1.3 %collective-permute-done.15.refs_3_ = bf16[176,256]{1,0:T(8,128)(2,1)S(1)} collective-permute-done((bf16[176,256]{1,0:T(8,128)(2,1)S(1)}, bf16[176,256]{1,0:T(8,128)(2,1)S(1)}, u32[]{:S(2)}, u32[]{:S(2)}) %collective-permute-start.15) | collective-permute-done | bytes 90144 | tf_op jit(solution)/shard_map/ppermute | solution.py:34
  53.0 1.0 %shard_map.106 = (f32[144,1152]{1,0:T(8,128)}, f32[1152]{0:T(1024)}) custom-call(bf16[176,256]{1,0:T(8,128)(2,1)S(1)} %shard_map.105.refs_0_, bf16[176,256]{1,0:T(8,128)(2,1)S(1)} %collective-permute-done.13.refs_1_, bf16[176,256]{1,0:T(8,128)(2,1)S(1)} %collective-permute-done.14.refs_2_, bf16[176,256]{1,0:T(8,128)(2,1)S(1)} %collective-permute-done.15.refs_3_), custom_call_target="tpu_custom_call" | custom-call | bytes 1327104 | tf_op jit(solution)/shard_map/pallas_call | solution.py:138
  (4 shorter events, 0.1 us)
Async XLA Ops:
  0.6 4.4 %collective-permute-start = (bf16[192,1152]{1,0:T(8,128)(2,1)}, bf16[192,1152]{1,0:T(8,128)(2,1)S(1)}, u32[]{:S(2)}, u32[]{:S(2)}) collective-permute-start(bf16[192,1152]{1,0:T(8,128)(2,1)} %bitcast.5), channel_id=1, source_target_pairs={{0,8},{8,0},{16,24},{24,16},{1,9},{9,1},{17,25},{25,17},{2,10},{10... | collective-permute-start | bytes 1327112 | tf_op jit(solution)/shard_map/ppermute | solution.py:34
  1.2 13.5 %collective-permute-start.3 = (bf16[192,1152]{1,0:T(8,128)(2,1)}, bf16[192,1152]{1,0:T(8,128)(2,1)S(1)}, u32[]{:S(2)}, u32[]{:S(2)}) collective-permute-start(bf16[192,1152]{1,0:T(8,128)(2,1)} %bitcast.6), channel_id=1, source_target_pairs={{0,16},{8,24},{16,0},{24,8},{1,17},{9,25},{17,1},{25,9},{2,18},{10... | collective-permute-start | bytes 1327112 | tf_op jit(solution)/shard_map/ppermute | solution.py:34
  5.0 1.0 %copy-start = (bf16[192,1,1152]{2,0,1:T(8,128)(2,1)S(1)}, bf16[192,1,1152]{2,0,1:T(8,128)(2,1)}, u32[]{:S(2)}) copy-start(bf16[192,1,1152]{2,0,1:T(8,128)(2,1)} %param.7) | copy-start | bytes 1327108
  6.0 1.0 %copy-start.1 = (bf16[192,1,1152]{2,0,1:T(8,128)(2,1)S(1)}, bf16[192,1,1152]{2,0,1:T(8,128)(2,1)}, u32[]{:S(2)}) copy-start(bf16[192,1,1152]{2,0,1:T(8,128)(2,1)} %param.6) | copy-start | bytes 1327108
  7.1 0.7 %copy-start.2 = (f32[1152]{0:T(1024)S(1)}, f32[1152]{0:T(1024)}, u32[]{:S(2)}) copy-start(f32[1152]{0:T(1024)} %gain_line.1) | copy-start | bytes 13828
  12.0 3.3 %collective-permute-start.1 = (bf16[192,1152]{1,0:T(8,128)(2,1)S(1)}, bf16[192,1152]{1,0:T(8,128)(2,1)S(1)}, u32[]{:S(2)}, u32[]{:S(2)}) collective-permute-start(bf16[192,1152]{1,0:T(8,128)(2,1)S(1)} %get-tuple-element.65.text_own), channel_id=1, source_target_pairs={{0,8},{8,0},{16,24},{24,16},{1,9},{9,1},{17,25},{25,17},{2,10},{10... | collective-permute-start | bytes 1327112 | tf_op jit(solution)/shard_map/ppermute | solution.py:34
  12.2 12.4 %collective-permute-start.2 = (bf16[192,1152]{1,0:T(8,128)(2,1)S(1)}, bf16[192,1152]{1,0:T(8,128)(2,1)S(1)}, u32[]{:S(2)}, u32[]{:S(2)}) collective-permute-start(bf16[192,1152]{1,0:T(8,128)(2,1)S(1)} %get-tuple-element.65.text_own), channel_id=1, source_target_pairs={{0,16},{8,24},{16,0},{24,8},{1,17},{9,25},{17,1},{25,9},{2,18},{10... | collective-permute-start | bytes 1327112 | tf_op jit(solution)/shard_map/ppermute | solution.py:34
  14.7 2.3 %collective-permute-start.4 = (bf16[160,1152]{1,0:T(8,128)(2,1)S(1)}, bf16[160,1152]{1,0:T(8,128)(2,1)S(1)}, u32[]{:S(2)}, u32[]{:S(2)}) collective-permute-start(bf16[160,1152]{1,0:T(8,128)(2,1)S(1)} %get-tuple-element.70), channel_id=1, source_target_pairs={{0,8},{8,0},{16,24},{24,16},{1,9},{9,1},{17,25},{25,17},{2,10},{10... | collective-permute-start | bytes 1105928 | tf_op jit(solution)/shard_map/ppermute | solution.py:34
  14.8 2.2 %collective-permute-start.5 = (bf16[32,1152]{1,0:T(8,128)(2,1)S(1)}, bf16[32,1152]{1,0:T(8,128)(2,1)S(1)}, u32[]{:S(2)}, u32[]{:S(2)}) collective-permute-start(bf16[32,1152]{1,0:T(8,128)(2,1)S(1)} %get-tuple-element.71), channel_id=1, source_target_pairs={{0,8},{8,0},{16,24},{24,16},{1,9},{9,1},{17,25},{25,17},{2,10},{10... | collective-permute-start | bytes 221192 | tf_op jit(solution)/shard_map/ppermute | solution.py:34
  24.6 1.8 %collective-permute-start.6 = (bf16[192,1152]{1,0:T(8,128)(2,1)S(1)}, bf16[192,1152]{1,0:T(8,128)(2,1)S(1)}, u32[]{:S(2)}, u32[]{:S(2)}) collective-permute-start(bf16[192,1152]{1,0:T(8,128)(2,1)S(1)} %collective-permute-done.2.text_unit.text_third), channel_id=1, source_target_pairs={{0,8},{8,0},{16,24},{24,16},{1,9},{9,1},{17,25},{25,17},{2,10},{10... | collective-permute-start | bytes 1327112 | tf_op jit(solution)/shard_map/ppermute | solution.py:34
  29.2 4.8 %collective-permute-start.7 = (bf16[176,256]{1,0:T(8,128)(2,1)S(1)}, bf16[176,256]{1,0:T(8,128)(2,1)S(1)}, u32[]{:S(2)}, u32[]{:S(2)}) collective-permute-start(bf16[176,256]{1,0:T(8,128)(2,1)S(1)} %get-tuple-element.103), channel_id=1, source_target_pairs={{0,1},{1,0},{2,3},{3,2},{4,5},{5,4},{6,7},{7,6},{8,9},{9,8},{10,11... | collective-permute-start | bytes 270344 | tf_op jit(solution)/shard_map/ppermute | solution.py:34
  32.9 6.5 %collective-permute-start.8 = (bf16[2,176,256]{2,1,0:T(8,128)(2,1)S(1)}, bf16[2,176,256]{2,1,0:T(8,128)(2,1)S(1)}, u32[]{:S(2)}, u32[]{:S(2)}) collective-permute-start(bf16[2,176,256]{2,1,0:T(8,128)(2,1)S(1)} %get-tuple-element.104), channel_id=1, source_target_pairs={{0,1},{1,0},{2,3},{3,2},{4,5},{5,4},{6,7},{7,6},{8,9},{9,8},{10,11... | collective-permute-start | bytes 540680 | tf_op jit(solution)/shard_map/ppermute | solution.py:34
  34.0 11.8 %collective-permute-start.10 = (bf16[176,256]{1,0:T(8,128)(2,1)S(1)}, bf16[176,256]{1,0:T(8,128)(2,1)S(1)}, u32[]{:S(2)}, u32[]{:S(2)}) collective-permute-start(bf16[176,256]{1,0:T(8,128)(2,1)S(1)} %shard_map.101.before), channel_id=1, source_target_pairs={{0,6},{1,7},{2,4},{3,5},{4,2},{5,3},{6,0},{7,1},{8,14},{9,15},{10,... | collective-permute-start | bytes 270344 | tf_op jit(solution)/shard_map/ppermute | solution.py:34
  39.4 6.5 %collective-permute-start.9 = (bf16[176,256]{1,0:T(8,128)(2,1)S(1)}, bf16[176,256]{1,0:T(8,128)(2,1)S(1)}, u32[]{:S(2)}, u32[]{:S(2)}) collective-permute-start(bf16[176,256]{1,0:T(8,128)(2,1)S(1)} %get-tuple-element.110), channel_id=1, source_target_pairs={{0,4},{1,5},{2,6},{3,7},{4,0},{5,1},{6,2},{7,3},{8,12},{9,13},{10,... | collective-permute-start | bytes 270344 | tf_op jit(solution)/shard_map/ppermute | solution.py:34
  42.0 4.5 %collective-permute-start.11 = (bf16[176,256]{1,0:T(8,128)(2,1)S(1)}, bf16[176,256]{1,0:T(8,128)(2,1)S(1)}, u32[]{:S(2)}, u32[]{:S(2)}) collective-permute-start(bf16[176,256]{1,0:T(8,128)(2,1)S(1)} %get-tuple-element.111), channel_id=1, source_target_pairs={{0,1},{1,0},{2,3},{3,2},{4,5},{5,4},{6,7},{7,6},{8,9},{9,8},{10,11... | collective-permute-start | bytes 270344 | tf_op jit(solution)/shard_map/ppermute | solution.py:34
  42.5 4.5 %collective-permute-start.12 = (bf16[176,256]{1,0:T(8,128)(2,1)S(1)}, bf16[176,256]{1,0:T(8,128)(2,1)S(1)}, u32[]{:S(2)}, u32[]{:S(2)}) collective-permute-start(bf16[176,256]{1,0:T(8,128)(2,1)S(1)} %get-tuple-element.106.before), channel_id=1, source_target_pairs={{0,2},{1,3},{2,0},{3,1},{4,6},{5,7},{6,4},{7,5},{8,10},{9,11},{10,... | collective-permute-start | bytes 270344 | tf_op jit(solution)/shard_map/ppermute | solution.py:34
  47.1 4.6 %collective-permute-start.14 = (bf16[176,256]{1,0:T(8,128)(2,1)S(1)}, bf16[176,256]{1,0:T(8,128)(2,1)S(1)}, u32[]{:S(2)}, u32[]{:S(2)}) collective-permute-start(bf16[176,256]{1,0:T(8,128)(2,1)S(1)} %shard_map.105.refs_0_), channel_id=1, source_target_pairs={{0,16},{8,24},{16,0},{24,8},{1,17},{9,25},{17,1},{25,9},{2,18},{10... | collective-permute-start | bytes 270344 | tf_op jit(solution)/shard_map/ppermute | solution.py:34
  48.7 3.0 %collective-permute-start.13 = (bf16[176,256]{1,0:T(8,128)(2,1)S(1)}, bf16[176,256]{1,0:T(8,128)(2,1)S(1)}, u32[]{:S(2)}, u32[]{:S(2)}) collective-permute-start(bf16[176,256]{1,0:T(8,128)(2,1)S(1)} %shard_map.105.refs_0_), channel_id=1, source_target_pairs={{0,8},{8,0},{16,24},{24,16},{1,9},{9,1},{17,25},{25,17},{2,10},{10... | collective-permute-start | bytes 270344 | tf_op jit(solution)/shard_map/ppermute | solution.py:34
  51.7 1.3 %collective-permute-start.15 = (bf16[176,256]{1,0:T(8,128)(2,1)S(1)}, bf16[176,256]{1,0:T(8,128)(2,1)S(1)}, u32[]{:S(2)}, u32[]{:S(2)}) collective-permute-start(bf16[176,256]{1,0:T(8,128)(2,1)S(1)} %collective-permute-done.14.refs_2_), channel_id=1, source_target_pairs={{0,8},{8,0},{16,24},{24,16},{1,9},{9,1},{17,25},{25,17},{2,10},{10... | collective-permute-start | bytes 270344 | tf_op jit(solution)/shard_map/ppermute | solution.py:34

commit v18 on v16

--- a/solution.py
+++ b/solution.py
@@ -329,33 +329,48 @@
         target[at : at + BAND, :] = jnp.concatenate(part, axis=1).astype(BF16)
 
 
-def partial_body(
-    members, groups, scale, bias, text_unit, flat_near, flat_far, totals, back_near, back_far, unit_turned_near,
-    unit_turned_far, inverse_near, inverse_far, turned_near, turned_far, proj_columns, gain,
-    across_first, across_later, keep, weights, text_columns, dots, packed,
+def far_packets_body(
+    members, scale, bias, text_unit, flat_near, flat_far, totals, back_near, back_far, unit_turned_near,
+    unit_turned_far, inverse_near, inverse_far, turned_near, turned_far, across, back, weights, text_columns, dots,
 ):
     rows = text_unit.shape[0]
     near = 2 * rows
     every = members * rows
-    width = text_unit.shape[1]
-    columns = width // members
-    count, full = packed.shape[1:]
+    columns = text_columns.shape[1]
+    each = turned_near.shape[0] // lax.axis_size("rep")
+    full = across.shape[2]
     scale, bias = scale[0], bias[0]
     take_columns(text_unit, text_columns)
     dots[:, :near] = dot(text_unit[...], flat_near[...])
     dots[:, near:] = dot(text_unit[...], flat_far[...])
     total = totals[...] + weigh(dots, scale, bias, near + rows, weights)
     added = dot(text_columns[...], weights[...], FIRST)
-    back = []
     for where, earlier, unit_turned, inverse in (
         (slice(0, near), back_near, unit_turned_near, inverse_near),
         (slice(near, every), back_far, unit_turned_far, inverse_far),
     ):
         whole = earlier[...] + added[:, where]
         part = (whole - unit_turned[...].astype(F32) * total[:, where]) * (inverse[...] * scale)
-        back.append(part.astype(BF16))
+        back[:, where] = part.astype(BF16)
+    own = lax.axis_index("rep")
+    picked = []
+    for at in range(2):
+        where = pl.ds(pl.multiple_of((own ^ (5 + 2 * at)) * each, BAND), each)
+        picked.append(jnp.concatenate([turned_near[where, :], turned_far[where, :]], axis=1))
+    product = dot(jnp.concatenate(picked, axis=0), back[...], LAST) * (1.0 / every)
+    for at in range(2):
+        pack_into(across.at[at], product[at * each : (at + 1) * each, :], full)
+
+
+def partial_body(
+    members, groups, back, turned_near, turned_far, proj_columns, gain, across_later, keep, token, packed,
+):
+    width = turned_near.shape[0]
+    every = back.shape[1]
+    columns = width // members
+    count, full = packed.shape[1:]
     turned = jnp.concatenate([turned_near[...], turned_far[...]], axis=1)
-    product = dot(turned, jnp.concatenate(back, axis=1), LAST)
+    product = dot(turned, back[...], LAST)
     each = width // groups
     product = product * (1.0 / every)
     for group in range(groups):
@@ -377,15 +392,15 @@
 
     own = lax.axis_index("rep")
     for at in range(2):
-        across_first[at] = packed[own ^ 1 ^ (4 + 2 * at)]
         across_later[at] = packed[own ^ 1 ^ (2 * at)]
     for at in range(4):
         keep[at] = packed[own ^ (2 * at)]
+    token[...] = jnp.zeros_like(token)
 
 
 def image_body(
     scale, proj, text_near, text_third, text_fourth, weights_near, weights_third, weights_fourth,
-    unit, factors, norm_back, token, back, product,
+    unit, factors, before, norm_back, token, back, product,
 ):
     rows = back.shape[0]
     scale = scale[0]
@@ -445,29 +460,41 @@
     token[...] = jnp.zeros_like(token)
 
 
-def pair_sum_body(first, before, keep, come, low, high):
-    for at, target in enumerate((low, high)):
-        target[...] = (keep[first + at].astype(F32) + come[at].astype(F32)).astype(BF16)
+def far_pair_sum_body(before, keep, come, two_on, three_on):
+    for at, target in enumerate((two_on, three_on)):
+        target[...] = (keep[2 + at].astype(F32) + come[at].astype(F32)).astype(BF16)
+
+
+def near_pair_sum_body(before, keep, come, own, next_one, gain_rows):
+    for at, target in enumerate((own, next_one)):
+        target[...] = (keep[at].astype(F32) + come[at].astype(F32)).astype(BF16)
+    count, full = own.shape
+    gain_rows[...] = own[count - BAND :, full - LANES :]
+
+
+def gain_sum_body(two_on, three_on, token):
+    token[...] = jnp.zeros_like(token)
 
 
 def far_sum_body(before, two_on, three_on, total):
     total[...] = two_on[...].astype(F32) + three_on[...].astype(F32)
 
 
-def last_sum_body(far, own, next_one, two_on, three_on, total, ordered):
-    parts = (own, next_one, two_on, three_on)
+def last_sum_body(far, own, next_one, gain_two, gain_three, total, ordered):
     total[...] = (own[...].astype(F32) + next_one[...].astype(F32) + far[...]).astype(BF16)
     count, full = total.shape
     z = lax.axis_index("rep") // 2
-    for step, part in enumerate(parts):
-        ordered[z ^ step] = part[count - BAND :, full - LANES :].astype(F32)
+    ordered[z] = own[count - BAND :, full - LANES :].astype(F32)
+    ordered[z ^ 1] = next_one[count - BAND :, full - LANES :].astype(F32)
+    ordered[z ^ 2] = gain_two[...].astype(F32)
+    ordered[z ^ 3] = gain_three[...].astype(F32)
     value = ordered[0]
-    for at in range(1, len(parts)):
+    for at in range(1, 4):
         value = value + ordered[at]
     total[count - BAND :, full - LANES :] = value.astype(BF16)
 
 
-def finish_body(members, *refs):
+def finish_body(members, before, *refs):
     packets, (proj_grad, gain_gradient, ordered) = refs[:members], refs[members:]
     count, full = packets[0].shape
     rows, width = proj_grad.shape
@@ -581,52 +608,56 @@
         scale, bias, t2, flat_near, flat_far, totals_near, totals_far, early_near, early_far, token,
     )
 
-    outs = call(
-        functools.partial(partial_body, members, groups),
-        [((2,) + packet, BF16)] * 2 + [((4,) + packet, BF16), narrow],
-        [((rows, columns), BF16), ((rows, every), F32), ((groups,) + packet, BF16)],
+    across_first, back, weights_fourth = call(
+        functools.partial(far_packets_body, members),
+        [((2,) + packet, BF16), ((columns, every), BF16), narrow],
+        [((rows, columns), BF16), ((rows, every), F32)],
         smem=2,
-        flops=4 * near * width * width,
-        moved=16 * near * width,
+        moved=1000,
     )(
         scale, bias, t3, flat_near, flat_far, totals, back_near, back_far, unit_turned_near, unit_turned_far,
-        inverse_near, inverse_far, turned_near, turned_far, proj_columns, gain_row,
-    )
-    across_first, across_later, keep, weights_fourth = outs
+        inverse_near, inverse_far, turned_near, turned_far,
+    )
     come_first = send(across_first, "rep", lambda p: p ^ 1)
+    across_later, keep, token = call(
+        functools.partial(partial_body, members, groups),
+        [((2,) + packet, BF16), ((4,) + packet, BF16), TOKEN],
+        [((groups,) + packet, BF16)],
+        moved=1000,
+    )(back, turned_near, turned_far, proj_columns, gain_row)
     norm_back, token = call(
         image_body,
         [((rows, width), F32), TOKEN],
         [half, ((rows, width), F32)],
         smem=1,
-        flops=1000,
         moved=1000,
     )(
         scale, proj_kept, text_near, t2, t3, weights_near, weights_third, weights_fourth,
-        unit_near, factors,
+        unit_near, factors, token,
     )
 
     across_later, token = lax.optimization_barrier((across_later, token))
     come_later = send(across_later, "rep", lambda p: p ^ 1)
-    two_on, three_on = call(functools.partial(pair_sum_body, 2), [(packet, BF16)] * 2, moved=1000)(
-        token, keep, come_first
-    )
-    first_two = two_on
-    two_on = send(two_on, "rep", lambda p: p ^ 4)
-    three_on = send(three_on, "rep", lambda p: p ^ 6)
-    own_sum, next_one = call(functools.partial(pair_sum_body, 0), [(packet, BF16)] * 2, moved=1000)(
-        first_two, keep, come_later
-    )
+    two_sum, three_sum = call(far_pair_sum_body, [(packet, BF16)] * 2, moved=1000)(token, keep, come_first)
+    two_on = send(two_sum, "rep", lambda p: p ^ 4)
+    three_on = send(three_sum, "rep", lambda p: p ^ 6)
+    own_sum, next_one, gain_rows = call(
+        near_pair_sum_body, [(packet, BF16)] * 2 + [((BAND, LANES), BF16)], moved=1000
+    )(two_sum, keep, come_later)
     next_one = send(next_one, "rep", lambda p: p ^ 2)
-    feature_grad, token = call(feature_body, [half, TOKEN], moved=12 * near * width)(
-        f0_kept, gain_row, norm_back, own_sum
-    )
+    gain_two = send(gain_rows, "rep", lambda p: p ^ 4)
+    gain_three = send(gain_rows, "rep", lambda p: p ^ 6)
+    (token,) = call(gain_sum_body, [TOKEN], moved=1000)(gain_two, gain_three)
     (far_sum,) = call(far_sum_body, [(packet, F32)], moved=1000)(token, two_on, three_on)
     (reduced,) = call(last_sum_body, [(packet, BF16)], [((4, BAND, LANES), F32)], moved=1000)(
-        far_sum, own_sum, next_one, two_on, three_on
+        far_sum, own_sum, next_one, gain_two, gain_three
     )
     far_block = send(reduced, "loop", lambda p: p ^ 2)
     near_block = send(reduced, "loop", lambda p: p ^ 1)
+    feature_grad, token = call(feature_body, [half, TOKEN], moved=12 * near * width)(
+        f0_kept, gain_row, norm_back, reduced
+    )
+    far_block, token = lax.optimization_barrier((far_block, token))
     blocks = [reduced, near_block, far_block, send(far_block, "loop", lambda p: p ^ 1)]
 
     proj_grad, gain_gradient = call(
@@ -634,7 +665,7 @@
         [((each, width), F32), ((width,), F32)],
         [((members, bands * BAND, full), F32)],
         moved=8 * each * width,
-    )(*blocks)
+    )(token, *blocks)
     return feature_grad[:, None, :], text_grad[:, None, :], proj_grad, gain_gradient
 
 

time: 54 us -> 55.8 us (1.033)
  starting transfers between devices: 13.3 us -> 16.1 us
  waiting for transfers between devices: 14.1 us -> 12.4 us
  Pallas kernels: 21.6 us -> 22.2 us
    ppermute x15 -> x17, starting transfers between devices: 13.3 us -> 16.1 us  [send(): return lax.ppermute(value, axis, [(p, target(p)) for p in range(count)])]
    ppermute x15 -> x17, waiting for transfers between devices: 14.1 us -> 12.4 us  [send(): return lax.ppermute(value, axis, [(p, target(p)) for p in range(count)])]
    pallas_call x14 -> x16, Pallas kernels: 21.6 us -> 22.2 us  [run(): pl.pallas_call(body, out_shape=[jax.ShapeDtypeStruct(shape, kind) for sha...]
  transfers between devices with their start and end apart: 15 -> 17, of which waited for: 8 -> 9; matrix products, arithmetic and copies ran while one was open for 0% -> 0% of each run, Pallas kernels for 33% -> 35%
where the time goes in v18:
time: 55.8 us; the launch traced here: 55.5 us
  Pallas kernels  22.2 us (40%)
  starting transfers between devices  16.1 us (29%)
  waiting for transfers between devices  12.4 us (22%)
  local copies, waits for them, and re-layouts  2.72 us (5%)
  between operations  2.06 us (4%)
    pallas_call x16, Pallas kernels, run(): pl.pallas_call(body, out_shape=[jax.ShapeDtypeStruct(shape, kind) for sha...  22.2 us
    ppermute x17, starting transfers between devices, send(): return lax.ppermute(value, axis, [(p, target(p)) for p in range(count)])  16.1 us
    ppermute x17, waiting for transfers between devices, send(): return lax.ppermute(value, axis, [(p, target(p)) for p in range(count)])  12.4 us
    unnamed x6, local copies, waits for them, and re-layouts  2.72 us
  transfers between devices with their start and end apart: 17, of which 9 were waited for; matrix products, arithmetic and copies ran while one was open for 0% of the time, Pallas kernels for 35%

profile of v18, /device:TPU:0, one launch (start us, length us, event | category | flops | bytes accessed | tf_op | source)
XLA Modules:
  0.0 55.5 jit_solution(11700576210393635243)
XLA Ops:
  0.6 0.5 collective-permute-start
  1.2 2.6 %collective-permute-start.3 = (bf16[192,1152]{1,0:T(8,128)(2,1)}, bf16[192,1152]{1,0:T(8,128)(2,1)S(1)}, u32[]{:S(2)}, u32[]{:S(2)}) collective-permute-start(bf16[192,1152]{1,0:T(8,128)(2,1)} %bitcast.6), channel_id=1, source_target_pairs={{0,16},{8,24},{16,0},{24,8},{1,17},{9,25},{17,1},{25,9},{2,18},{10... | collective-permute-start | bytes 1327112 | tf_op jit(solution)/shard_map/ppermute | solution.py:34
  5.0 0.0 collective-permute-done.f1
  5.0 1.0 %copy-done = bf16[192,1,1152]{2,0,1:T(8,128)(2,1)S(1)} copy-done((bf16[192,1,1152]{2,0,1:T(8,128)(2,1)S(1)}, bf16[192,1,1152]{2,0,1:T(8,128)(2,1)}, u32[]{:S(2)}) %copy-start) | copy-done | bytes 442392
  6.0 1.0 %copy-done.1 = bf16[192,1,1152]{2,0,1:T(8,128)(2,1)S(1)} copy-done((bf16[192,1,1152]{2,0,1:T(8,128)(2,1)S(1)}, bf16[192,1,1152]{2,0,1:T(8,128)(2,1)}, u32[]{:S(2)}) %copy-start.1) | copy-done | bytes 442392
  7.1 0.7 %copy-done.2 = f32[1152]{0:T(1024)S(1)} copy-done((f32[1152]{0:T(1024)S(1)}, f32[1152]{0:T(1024)}, u32[]{:S(2)}) %copy-start.2) | copy-done | bytes 4632
  7.7 4.2 %shard_map.93 = (bf16[192,1152]{1,0:T(8,128)(2,1)S(1)}, bf16[1152,1152]{1,0:T(8,128)(2,1)S(1)}, bf16[192,1152]{1,0:T(8,128)(2,1)S(1)}, f32[1,1152]{1,0:T(1,128)S...) custom-call(f32[1]{0:T(128)S(6)} %copy.10.scale, ...), custom_call_target="tpu_custom_call" | custom-call | flops 1019215872 | bytes 3538944 | tf_op jit(solution)/shard_map/pallas_call | solution.py:138
  12.0 0.2 collective-permute-start.1
  12.2 0.6 %collective-permute-start.2 = (bf16[192,1152]{1,0:T(8,128)(2,1)S(1)}, bf16[192,1152]{1,0:T(8,128)(2,1)S(1)}, u32[]{:S(2)}, u32[]{:S(2)}) collective-permute-start(bf16[192,1152]{1,0:T(8,128)(2,1)S(1)} %get-tuple-element.69.text_own), channel_id=1, source_target_pairs={{0,16},{8,24},{16,0},{24,8},{1,17},{9,25},{17,1},{25,9},{2,18},{10... | collective-permute-start | bytes 1327112 | tf_op jit(solution)/shard_map/ppermute | solution.py:34
  12.8 1.9 %collective-permute-done.3.f2 = bf16[192,1152]{1,0:T(8,128)(2,1)S(1)} collective-permute-done((bf16[192,1152]{1,0:T(8,128)(2,1)}, bf16[192,1152]{1,0:T(8,128)(2,1)S(1)}, u32[]{:S(2)}, u32[]{:S(2)}) %collective-permute-start.3) | collective-permute-done | bytes 442400 | tf_op jit(solution)/shard_map/ppermute | solution.py:34
  14.7 0.1 collective-permute-start.4
  14.8 0.5 collective-permute-start.5
  15.3 0.0 collective-permute-done.1.t1
  15.3 1.7 %shard_map.94 = (bf16[384,1152]{1,0:T(8,128)(2,1)S(1)}, bf16[1152,384]{1,0:T(8,128)(2,1)S(1)}, bf16[1152,384]{1,0:T(8,128)(2,1)S(1)}, bf16[288,384]{1,0:T(8,128)...) custom-call(f32[1]{0:T(128)S(6)} %copy.10.scale, ...), custom_call_target="tpu_custom_call" | custom-call | flops 1000 | bytes 1000 | tf_op jit(solution)/shard_map/pallas_call | solution.py:138
  17.0 0.0 collective-permute-done.5.f3_tail
  17.0 0.0 collective-permute-done.4.f3_head
  17.0 4.6 %shard_map.96 = (bf16[1152,384]{1,0:T(8,128)(2,1)S(1)}, bf16[384,1152]{1,0:T(8,128)(2,1)S(1)}, bf16[1152,384]{1,0:T(8,128)(2,1)S(1)}, bf16[288,384]{1,0:T(8,128)...) custom-call(f32[1]{0:T(128)S(6)} %copy.10.scale, ...), custom_call_target="tpu_custom_call" | custom-call | flops 1000 | bytes 1000 | tf_op jit(solution)/shard_map/pallas_call | solution.py:138
  21.7 2.0 %shard_map.97 = (bf16[192,1152]{1,0:T(8,128)(2,1)}, f32[8,128]{1,0:T(8,128)S(1)}) custom-call(f32[1]{0:T(128)S(6)} %copy.10.scale, bf16[192,1152]{1,0:T(8,128)(2,1)S(1)} %get-tuple-element.72.text, bf16[384,384]{1,0:T(8,128)(2,1)S(1)} %get-tuple-element.73.weights_near, bf16[384,384]{1,0:T(8,128)(2,1)S(1)} %get-tuple-element.77.weights_far, ...), custom_call_target="tpu_custom_call" | custom-call | flops 1000 | bytes 1000 | tf_op jit(solution)/shard_map/pallas_call | solution.py:138
  23.7 0.9 %collective-permute-done.2.text_unit.text_third = bf16[192,1152]{1,0:T(8,128)(2,1)S(1)} collective-permute-done((bf16[192,1152]{1,0:T(8,128)(2,1)S(1)}, bf16[192,1152]{1,0:T(8,128)(2,1)S(1)}, u32[]{:S(2)}, u32[]{:S(2)}) %collective-permute-start.2) | collective-permute-done | bytes 442400 | tf_op jit(solution)/shard_map/ppermute | solution.py:34
  24.6 0.0 collective-permute-start.6
  24.6 1.3 %shard_map.98 = (bf16[192,768]{1,0:T(8,128)(2,1)S(1)}, f32[288,384]{1,0:T(8,128)S(1)}, f32[288,384]{1,0:T(8,128)S(1)}, f32[1,768]{1,0:T(1,128)S(1)}) custom-call(f32[1]{0:T(128)S(6)} %copy.10.scale, f32[1]{0:T(128)S(6)} %copy.11.bias, bf16[192,1152]{1,0:T(8,128)(2,1)S(1)} %collective-permute-done.2.text_unit.text_third, ...), custom_call_target="tpu_custom_call" | custom-call | flops 1019215872 | bytes 3538944 | tf_op jit(solution)/shard_map/pallas_call | solution.py:138
  26.0 0.5 collective-permute-done.6.text_unit.text_fourth
  26.4 1.9 %shard_map.99 = (bf16[2,176,256]{2,1,0:T(8,128)(2,1)S(1)}, bf16[288,768]{1,0:T(8,128)(2,1)S(1)}, bf16[192,768]{1,0:T(8,128)(2,1)S(1)}) custom-call(f32[1]{0:T(128)S(6)} %copy.10.scale, f32[1]{0:T(128)S(6)} %copy.11.bias, bf16[192,1152]{1,0:T(8,128)(2,1)S(1)} %collective-permute-done.6.text_unit.text_fourth, ...), custom_call_target="tpu_custom_call" | custom-call | bytes 1000 | tf_op jit(solution)/shard_map/pallas_call | solution.py:138
  28.3 1.6 %collective-permute-start.7 = (bf16[2,176,256]{2,1,0:T(8,128)(2,1)S(1)}, bf16[2,176,256]{2,1,0:T(8,128)(2,1)S(1)}, u32[]{:S(2)}, u32[]{:S(2)}) collective-permute-start(bf16[2,176,256]{2,1,0:T(8,128)(2,1)S(1)} %get-tuple-element.108), channel_id=1, source_target_pairs={{0,1},{1,0},{2,3},{3,2},{4,5},{5,4},{6,7},{7,6},{8,9},{9,8},{10,11... | collective-permute-start | bytes 540680 | tf_op jit(solution)/shard_map/ppermute | solution.py:34
  29.9 1.3 %shard_map.100 = (bf16[2,176,256]{2,1,0:T(8,128)(2,1)S(1)}, bf16[4,176,256]{2,1,0:T(8,128)(2,1)S(1)}, f32[8,128]{1,0:T(8,128)S(1)}) custom-call(bf16[288,768]{1,0:T(8,128)(2,1)S(1)} %get-tuple-element.100.back, bf16[1152,384]{1,0:T(8,128)(2,1)S(1)} %get-tuple-element.97.turned_near, bf16[1152,384]{1,0:T(8,128)(2,1)S(1)} %get-tuple-element.98.turned_far, ...), custom_call_target="tpu_custom_call" | custom-call | bytes 1000 | tf_op jit(solution)/shard_map/pallas_call | solution.py:138
  31.2 2.1 %shard_map.101 = (f32[192,1152]{1,0:T(8,128)S(1)}, f32[8,128]{1,0:T(8,128)S(1)}) custom-call(f32[1]{0:T(128)S(6)} %copy.10.scale, bf16[1152,1152]{1,0:T(8,128)(2,1)S(1)} %get-tuple-element.65.proj, bf16[384,1152]{1,0:T(8,128)(2,1)S(1)} %get-tuple-element.71.text_near, bf16[192,1152]{1,0:T(8,128)(2,1)S(1)} %collective-permute-done.2.text_unit.text_third, ...), custom_call_target="tpu_custom_call" | custom-call | bytes 1000 | tf_op jit(solution)/shard_map/pallas_call | solution.py:138
  33.4 0.6 %collective-permute-start.8 = (bf16[2,176,256]{2,1,0:T(8,128)(2,1)S(1)}, bf16[2,176,256]{2,1,0:T(8,128)(2,1)S(1)}, u32[]{:S(2)}, u32[]{:S(2)}) collective-permute-start(bf16[2,176,256]{2,1,0:T(8,128)(2,1)S(1)} %get-tuple-element.110), channel_id=1, source_target_pairs={{0,1},{1,0},{2,3},{3,2},{4,5},{5,4},{6,7},{7,6},{8,9},{9,8},{10,11... | collective-permute-start | bytes 540680 | tf_op jit(solution)/shard_map/ppermute | solution.py:34
  33.9 1.1 %collective-permute-done.7.come = bf16[2,176,256]{2,1,0:T(8,128)(2,1)S(1)} collective-permute-done((bf16[2,176,256]{2,1,0:T(8,128)(2,1)S(1)}, bf16[2,176,256]{2,1,0:T(8,128)(2,1)S(1)}, u32[]{:S(2)}, u32[]{:S(2)}) %collective-permute-start.7) | collective-permute-done | bytes 180256 | tf_op jit(solution)/shard_map/ppermute | solution.py:34
  35.1 3.7 %collective-permute-start.12 = (bf16[176,256]{1,0:T(8,128)(2,1)S(1)}, bf16[176,256]{1,0:T(8,128)(2,1)S(1)}, u32[]{:S(2)}, u32[]{:S(2)}) collective-permute-start(bf16[176,256]{1,0:T(8,128)(2,1)S(1)} %get-tuple-element.112), channel_id=1, source_target_pairs={{0,6},{1,7},{2,4},{3,5},{4,2},{5,3},{6,0},{7,1},{8,14},{9,15},{10,... | collective-permute-start | bytes 270344 | tf_op jit(solution)/shard_map/ppermute | solution.py:34
  38.7 0.0 collective-permute-start.11
  38.8 1.1 %collective-permute-done.8.come = bf16[2,176,256]{2,1,0:T(8,128)(2,1)S(1)} collective-permute-done((bf16[2,176,256]{2,1,0:T(8,128)(2,1)S(1)}, bf16[2,176,256]{2,1,0:T(8,128)(2,1)S(1)}, u32[]{:S(2)}, u32[]{:S(2)}) %collective-permute-start.8) | collective-permute-done | bytes 180256 | tf_op jit(solution)/shard_map/ppermute | solution.py:34
  39.8 0.1 shard_map.103
  39.9 1.6 %collective-permute-start.13 = (bf16[176,256]{1,0:T(8,128)(2,1)S(1)}, bf16[176,256]{1,0:T(8,128)(2,1)S(1)}, u32[]{:S(2)}, u32[]{:S(2)}) collective-permute-start(bf16[176,256]{1,0:T(8,128)(2,1)S(1)} %get-tuple-element.114), channel_id=1, source_target_pairs={{0,2},{1,3},{2,0},{3,1},{4,6},{5,7},{6,4},{7,5},{8,10},{9,11},{10,... | collective-permute-start | bytes 270344 | tf_op jit(solution)/shard_map/ppermute | solution.py:34
  41.5 2.5 %collective-permute-start.10 = (bf16[16,128]{1,0:T(8,128)(2,1)S(1)}, bf16[16,128]{1,0:T(8,128)(2,1)S(1)}, u32[]{:S(2)}, u32[]{:S(2)}) collective-permute-start(bf16[16,128]{1,0:T(8,128)(2,1)S(1)} %get-tuple-element.111), channel_id=1, source_target_pairs={{0,6},{1,7},{2,4},{3,5},{4,2},{5,3},{6,0},{7,1},{8,14},{9,15},{10,... | collective-permute-start | bytes 12296 | tf_op jit(solution)/shard_map/ppermute | solution.py:34
  44.0 0.1 collective-permute-start.9
  44.1 2.8 %collective-permute-done.10.three_on.gain_three = bf16[16,128]{1,0:T(8,128)(2,1)S(1)} collective-permute-done((bf16[16,128]{1,0:T(8,128)(2,1)S(1)}, bf16[16,128]{1,0:T(8,128)(2,1)S(1)}, u32[]{:S(2)}, u32[]{:S(2)}) %collective-permute-start.10) | collective-permute-done | bytes 4128 | tf_op jit(solution)/shard_map/ppermute | solution.py:34
  46.9 1.6 %collective-permute-done.9.two_on.gain_two = bf16[16,128]{1,0:T(8,128)(2,1)S(1)} collective-permute-done((bf16[16,128]{1,0:T(8,128)(2,1)S(1)}, bf16[16,128]{1,0:T(8,128)(2,1)S(1)}, u32[]{:S(2)}, u32[]{:S(2)}) %collective-permute-start.9) | collective-permute-done | bytes 4128 | tf_op jit(solution)/shard_map/ppermute | solution.py:34
  48.5 0.0 collective-permute-done.12.three_on
  48.5 0.0 collective-permute-done.11.two_on
  48.5 0.0 collective-permute-done.13.next_one
  48.6 0.1 shard_map.106.before.refs_0_
  48.6 1.6 %collective-permute-start.14 = (bf16[176,256]{1,0:T(8,128)(2,1)S(1)}, bf16[176,256]{1,0:T(8,128)(2,1)S(1)}, u32[]{:S(2)}, u32[]{:S(2)}) collective-permute-start(bf16[176,256]{1,0:T(8,128)(2,1)S(1)} %shard_map.106.before.refs_0_), channel_id=1, source_target_pairs={{0,16},{8,24},{16,0},{24,8},{1,17},{9,25},{17,1},{25,9},{2,18},{10... | collective-permute-start | bytes 270344 | tf_op jit(solution)/shard_map/ppermute | solution.py:34
  50.2 1.7 %shard_map.107 = (bf16[192,1152]{1,0:T(8,128)(2,1)}, f32[8,128]{1,0:T(8,128)S(1)}) custom-call(bf16[192,1152]{1,0:T(8,128)(2,1)S(1)} %get-tuple-element.63.features, f32[1,1152]{1,0:T(1,128)S(1)} %get-tuple-element.64.gain, f32[192,1152]{1,0:T(8,128)S(1)} %get-tuple-element.103.norm_back, bf16[176,256]{1,0:T(8,128)(2,1)S(1)} %shard_map.106.before.refs_0_), custom_call_target="tpu_custom_call" | custom-call | bytes 5308416 | tf_op jit(solution)/shard_map/pallas_call | solution.py:138
  51.9 1.3 %collective-permute-done.14.refs_2_ = bf16[176,256]{1,0:T(8,128)(2,1)S(1)} collective-permute-done((bf16[176,256]{1,0:T(8,128)(2,1)S(1)}, bf16[176,256]{1,0:T(8,128)(2,1)S(1)}, u32[]{:S(2)}, u32[]{:S(2)}) %collective-permute-start.14) | collective-permute-done | bytes 90144 | tf_op jit(solution)/shard_map/ppermute | solution.py:34
  53.2 0.0 collective-permute-start.16
  53.2 0.0 collective-permute-done.15.refs_1_
  53.2 1.3 %collective-permute-done.16.refs_3_ = bf16[176,256]{1,0:T(8,128)(2,1)S(1)} collective-permute-done((bf16[176,256]{1,0:T(8,128)(2,1)S(1)}, bf16[176,256]{1,0:T(8,128)(2,1)S(1)}, u32[]{:S(2)}, u32[]{:S(2)}) %collective-permute-start.16) | collective-permute-done | bytes 90144 | tf_op jit(solution)/shard_map/ppermute | solution.py:34
  54.5 1.0 %shard_map.108 = (f32[144,1152]{1,0:T(8,128)}, f32[1152]{0:T(1024)}) custom-call(f32[8,128]{1,0:T(8,128)S(1)} %get-tuple-element.118.before, bf16[176,256]{1,0:T(8,128)(2,1)S(1)} %shard_map.106.before.refs_0_, bf16[176,256]{1,0:T(8,128)(2,1)S(1)} %collective-permute-done.15.refs_1_, bf16[176,256]{1,0:T(8,128)(2,1)S(1)} %collective-permute-done.14.refs_2_, ...), custom_call_target="tpu_custom_call" | custom-call | bytes 1327104 | tf_op jit(solution)/shard_map/pallas_call | solution.py:138
  (8 shorter events, 0.1 us)
Async XLA Ops:
  0.6 4.4 %collective-permute-start = (bf16[192,1152]{1,0:T(8,128)(2,1)}, bf16[192,1152]{1,0:T(8,128)(2,1)S(1)}, u32[]{:S(2)}, u32[]{:S(2)}) collective-permute-start(bf16[192,1152]{1,0:T(8,128)(2,1)} %bitcast.5), channel_id=1, source_target_pairs={{0,8},{8,0},{16,24},{24,16},{1,9},{9,1},{17,25},{25,17},{2,10},{10... | collective-permute-start | bytes 1327112 | tf_op jit(solution)/shard_map/ppermute | solution.py:34
  1.2 13.5 %collective-permute-start.3 = (bf16[192,1152]{1,0:T(8,128)(2,1)}, bf16[192,1152]{1,0:T(8,128)(2,1)S(1)}, u32[]{:S(2)}, u32[]{:S(2)}) collective-permute-start(bf16[192,1152]{1,0:T(8,128)(2,1)} %bitcast.6), channel_id=1, source_target_pairs={{0,16},{8,24},{16,0},{24,8},{1,17},{9,25},{17,1},{25,9},{2,18},{10... | collective-permute-start | bytes 1327112 | tf_op jit(solution)/shard_map/ppermute | solution.py:34
  5.0 1.0 %copy-start = (bf16[192,1,1152]{2,0,1:T(8,128)(2,1)S(1)}, bf16[192,1,1152]{2,0,1:T(8,128)(2,1)}, u32[]{:S(2)}) copy-start(bf16[192,1,1152]{2,0,1:T(8,128)(2,1)} %param.7) | copy-start | bytes 1327108
  6.0 1.0 %copy-start.1 = (bf16[192,1,1152]{2,0,1:T(8,128)(2,1)S(1)}, bf16[192,1,1152]{2,0,1:T(8,128)(2,1)}, u32[]{:S(2)}) copy-start(bf16[192,1,1152]{2,0,1:T(8,128)(2,1)} %param.6) | copy-start | bytes 1327108
  7.1 0.7 %copy-start.2 = (f32[1152]{0:T(1024)S(1)}, f32[1152]{0:T(1024)}, u32[]{:S(2)}) copy-start(f32[1152]{0:T(1024)} %gain_line.1) | copy-start | bytes 13828
  12.0 3.3 %collective-permute-start.1 = (bf16[192,1152]{1,0:T(8,128)(2,1)S(1)}, bf16[192,1152]{1,0:T(8,128)(2,1)S(1)}, u32[]{:S(2)}, u32[]{:S(2)}) collective-permute-start(bf16[192,1152]{1,0:T(8,128)(2,1)S(1)} %get-tuple-element.69.text_own), channel_id=1, source_target_pairs={{0,8},{8,0},{16,24},{24,16},{1,9},{9,1},{17,25},{25,17},{2,10},{10... | collective-permute-start | bytes 1327112 | tf_op jit(solution)/shard_map/ppermute | solution.py:34
  12.2 12.4 %collective-permute-start.2 = (bf16[192,1152]{1,0:T(8,128)(2,1)S(1)}, bf16[192,1152]{1,0:T(8,128)(2,1)S(1)}, u32[]{:S(2)}, u32[]{:S(2)}) collective-permute-start(bf16[192,1152]{1,0:T(8,128)(2,1)S(1)} %get-tuple-element.69.text_own), channel_id=1, source_target_pairs={{0,16},{8,24},{16,0},{24,8},{1,17},{9,25},{17,1},{25,9},{2,18},{10... | collective-permute-start | bytes 1327112 | tf_op jit(solution)/shard_map/ppermute | solution.py:34
  14.7 2.3 %collective-permute-start.4 = (bf16[160,1152]{1,0:T(8,128)(2,1)S(1)}, bf16[160,1152]{1,0:T(8,128)(2,1)S(1)}, u32[]{:S(2)}, u32[]{:S(2)}) collective-permute-start(bf16[160,1152]{1,0:T(8,128)(2,1)S(1)} %get-tuple-element.74), channel_id=1, source_target_pairs={{0,8},{8,0},{16,24},{24,16},{1,9},{9,1},{17,25},{25,17},{2,10},{10... | collective-permute-start | bytes 1105928 | tf_op jit(solution)/shard_map/ppermute | solution.py:34
  14.8 2.2 %collective-permute-start.5 = (bf16[32,1152]{1,0:T(8,128)(2,1)S(1)}, bf16[32,1152]{1,0:T(8,128)(2,1)S(1)}, u32[]{:S(2)}, u32[]{:S(2)}) collective-permute-start(bf16[32,1152]{1,0:T(8,128)(2,1)S(1)} %get-tuple-element.75), channel_id=1, source_target_pairs={{0,8},{8,0},{16,24},{24,16},{1,9},{9,1},{17,25},{25,17},{2,10},{10... | collective-permute-start | bytes 221192 | tf_op jit(solution)/shard_map/ppermute | solution.py:34
  24.6 1.8 %collective-permute-start.6 = (bf16[192,1152]{1,0:T(8,128)(2,1)S(1)}, bf16[192,1152]{1,0:T(8,128)(2,1)S(1)}, u32[]{:S(2)}, u32[]{:S(2)}) collective-permute-start(bf16[192,1152]{1,0:T(8,128)(2,1)S(1)} %collective-permute-done.2.text_unit.text_third), channel_id=1, source_target_pairs={{0,8},{8,0},{16,24},{24,16},{1,9},{9,1},{17,25},{25,17},{2,10},{10... | collective-permute-start | bytes 1327112 | tf_op jit(solution)/shard_map/ppermute | solution.py:34
  28.3 6.7 %collective-permute-start.7 = (bf16[2,176,256]{2,1,0:T(8,128)(2,1)S(1)}, bf16[2,176,256]{2,1,0:T(8,128)(2,1)S(1)}, u32[]{:S(2)}, u32[]{:S(2)}) collective-permute-start(bf16[2,176,256]{2,1,0:T(8,128)(2,1)S(1)} %get-tuple-element.108), channel_id=1, source_target_pairs={{0,1},{1,0},{2,3},{3,2},{4,5},{5,4},{6,7},{7,6},{8,9},{9,8},{10,11... | collective-permute-start | bytes 540680 | tf_op jit(solution)/shard_map/ppermute | solution.py:34
  33.4 6.5 %collective-permute-start.8 = (bf16[2,176,256]{2,1,0:T(8,128)(2,1)S(1)}, bf16[2,176,256]{2,1,0:T(8,128)(2,1)S(1)}, u32[]{:S(2)}, u32[]{:S(2)}) collective-permute-start(bf16[2,176,256]{2,1,0:T(8,128)(2,1)S(1)} %get-tuple-element.110), channel_id=1, source_target_pairs={{0,1},{1,0},{2,3},{3,2},{4,5},{5,4},{6,7},{7,6},{8,9},{9,8},{10,11... | collective-permute-start | bytes 540680 | tf_op jit(solution)/shard_map/ppermute | solution.py:34
  35.1 13.4 %collective-permute-start.12 = (bf16[176,256]{1,0:T(8,128)(2,1)S(1)}, bf16[176,256]{1,0:T(8,128)(2,1)S(1)}, u32[]{:S(2)}, u32[]{:S(2)}) collective-permute-start(bf16[176,256]{1,0:T(8,128)(2,1)S(1)} %get-tuple-element.112), channel_id=1, source_target_pairs={{0,6},{1,7},{2,4},{3,5},{4,2},{5,3},{6,0},{7,1},{8,14},{9,15},{10,... | collective-permute-start | bytes 270344 | tf_op jit(solution)/shard_map/ppermute | solution.py:34
  38.7 9.8 %collective-permute-start.11 = (bf16[176,256]{1,0:T(8,128)(2,1)S(1)}, bf16[176,256]{1,0:T(8,128)(2,1)S(1)}, u32[]{:S(2)}, u32[]{:S(2)}) collective-permute-start(bf16[176,256]{1,0:T(8,128)(2,1)S(1)} %get-tuple-element.109.before), channel_id=1, source_target_pairs={{0,4},{1,5},{2,6},{3,7},{4,0},{5,1},{6,2},{7,3},{8,12},{9,13},{10,... | collective-permute-start | bytes 270344 | tf_op jit(solution)/shard_map/ppermute | solution.py:34
  39.9 8.7 %collective-permute-start.13 = (bf16[176,256]{1,0:T(8,128)(2,1)S(1)}, bf16[176,256]{1,0:T(8,128)(2,1)S(1)}, u32[]{:S(2)}, u32[]{:S(2)}) collective-permute-start(bf16[176,256]{1,0:T(8,128)(2,1)S(1)} %get-tuple-element.114), channel_id=1, source_target_pairs={{0,2},{1,3},{2,0},{3,1},{4,6},{5,7},{6,4},{7,5},{8,10},{9,11},{10,... | collective-permute-start | bytes 270344 | tf_op jit(solution)/shard_map/ppermute | solution.py:34
  41.5 5.4 %collective-permute-start.10 = (bf16[16,128]{1,0:T(8,128)(2,1)S(1)}, bf16[16,128]{1,0:T(8,128)(2,1)S(1)}, u32[]{:S(2)}, u32[]{:S(2)}) collective-permute-start(bf16[16,128]{1,0:T(8,128)(2,1)S(1)} %get-tuple-element.111), channel_id=1, source_target_pairs={{0,6},{1,7},{2,4},{3,5},{4,2},{5,3},{6,0},{7,1},{8,14},{9,15},{10,... | collective-permute-start | bytes 12296 | tf_op jit(solution)/shard_map/ppermute | solution.py:34
  44.0 4.5 %collective-permute-start.9 = (bf16[16,128]{1,0:T(8,128)(2,1)S(1)}, bf16[16,128]{1,0:T(8,128)(2,1)S(1)}, u32[]{:S(2)}, u32[]{:S(2)}) collective-permute-start(bf16[16,128]{1,0:T(8,128)(2,1)S(1)} %get-tuple-element.111), channel_id=1, source_target_pairs={{0,4},{1,5},{2,6},{3,7},{4,0},{5,1},{6,2},{7,3},{8,12},{9,13},{10,... | collective-permute-start | bytes 12296 | tf_op jit(solution)/shard_map/ppermute | solution.py:34
  48.6 4.6 %collective-permute-start.14 = (bf16[176,256]{1,0:T(8,128)(2,1)S(1)}, bf16[176,256]{1,0:T(8,128)(2,1)S(1)}, u32[]{:S(2)}, u32[]{:S(2)}) collective-permute-start(bf16[176,256]{1,0:T(8,128)(2,1)S(1)} %shard_map.106.before.refs_0_), channel_id=1, source_target_pairs={{0,16},{8,24},{16,0},{24,8},{1,17},{9,25},{17,1},{25,9},{2,18},{10... | collective-permute-start | bytes 270344 | tf_op jit(solution)/shard_map/ppermute | solution.py:34
  50.2 3.0 %collective-permute-start.15 = (bf16[176,256]{1,0:T(8,128)(2,1)S(1)}, bf16[176,256]{1,0:T(8,128)(2,1)S(1)}, u32[]{:S(2)}, u32[]{:S(2)}) collective-permute-start(bf16[176,256]{1,0:T(8,128)(2,1)S(1)} %shard_map.106.before.refs_0_), channel_id=1, source_target_pairs={{0,8},{8,0},{16,24},{24,16},{1,9},{9,1},{17,25},{25,17},{2,10},{10... | collective-permute-start | bytes 270344 | tf_op jit(solution)/shard_map/ppermute | solution.py:34
  53.2 1.3 %collective-permute-start.16 = (bf16[176,256]{1,0:T(8,128)(2,1)S(1)}, bf16[176,256]{1,0:T(8,128)(2,1)S(1)}, u32[]{:S(2)}, u32[]{:S(2)}) collective-permute-start(bf16[176,256]{1,0:T(8,128)(2,1)S(1)} %collective-permute-done.14.refs_2_), channel_id=1, source_target_pairs={{0,8},{8,0},{16,24},{24,16},{1,9},{9,1},{17,25},{25,17},{2,10},{10... | collective-permute-start | bytes 270344 | tf_op jit(solution)/shard_map/ppermute | solution.py:34

commit v19 on v18

--- a/solution.py
+++ b/solution.py
@@ -363,7 +363,7 @@
 
 
 def partial_body(
-    members, groups, back, turned_near, turned_far, proj_columns, gain, across_later, keep, token, packed,
+    members, groups, back, turned_near, turned_far, proj_columns, gain, across_later, keep, gain_rows, token, packed,
 ):
     width = turned_near.shape[0]
     every = back.shape[1]
@@ -389,6 +389,7 @@
     gain_tile = jnp.concatenate(pieces, axis=0).astype(BF16)
     for group in range(groups):
         packed[group, count - BAND :, full - LANES :] = gain_tile
+    gain_rows[...] = gain_tile
 
     own = lax.axis_index("rep")
     for at in range(2):
@@ -460,41 +461,38 @@
     token[...] = jnp.zeros_like(token)
 
 
-def far_pair_sum_body(before, keep, come, two_on, three_on):
+def far_pair_sum_body(before, keep, come, gain_rows, come_gain_rows, two_on, three_on):
     for at, target in enumerate((two_on, three_on)):
         target[...] = (keep[2 + at].astype(F32) + come[at].astype(F32)).astype(BF16)
-
-
-def near_pair_sum_body(before, keep, come, own, next_one, gain_rows):
+        count, full = target.shape
+        target[count - BAND :, full - LANES :] = (
+            gain_rows[...].astype(F32) + come_gain_rows[...].astype(F32)
+        ).astype(BF16)
+
+
+def near_pair_sum_body(before, keep, come, own, next_one):
     for at, target in enumerate((own, next_one)):
         target[...] = (keep[at].astype(F32) + come[at].astype(F32)).astype(BF16)
-    count, full = own.shape
-    gain_rows[...] = own[count - BAND :, full - LANES :]
-
-
-def gain_sum_body(two_on, three_on, token):
-    token[...] = jnp.zeros_like(token)
 
 
 def far_sum_body(before, two_on, three_on, total):
     total[...] = two_on[...].astype(F32) + three_on[...].astype(F32)
 
 
-def last_sum_body(far, own, next_one, gain_two, gain_three, total, ordered):
+def last_sum_body(far, own, next_one, two_on, three_on, total, ordered):
+    parts = (own, next_one, two_on, three_on)
     total[...] = (own[...].astype(F32) + next_one[...].astype(F32) + far[...]).astype(BF16)
     count, full = total.shape
     z = lax.axis_index("rep") // 2
-    ordered[z] = own[count - BAND :, full - LANES :].astype(F32)
-    ordered[z ^ 1] = next_one[count - BAND :, full - LANES :].astype(F32)
-    ordered[z ^ 2] = gain_two[...].astype(F32)
-    ordered[z ^ 3] = gain_three[...].astype(F32)
+    for step, part in enumerate(parts):
+        ordered[z ^ step] = part[count - BAND :, full - LANES :].astype(F32)
     value = ordered[0]
-    for at in range(1, 4):
+    for at in range(1, len(parts)):
         value = value + ordered[at]
     total[count - BAND :, full - LANES :] = value.astype(BF16)
 
 
-def finish_body(members, before, *refs):
+def finish_body(members, *refs):
     packets, (proj_grad, gain_gradient, ordered) = refs[:members], refs[members:]
     count, full = packets[0].shape
     rows, width = proj_grad.shape
@@ -619,9 +617,9 @@
         inverse_near, inverse_far, turned_near, turned_far,
     )
     come_first = send(across_first, "rep", lambda p: p ^ 1)
-    across_later, keep, token = call(
+    across_later, keep, gain_rows, token = call(
         functools.partial(partial_body, members, groups),
-        [((2,) + packet, BF16), ((4,) + packet, BF16), TOKEN],
+        [((2,) + packet, BF16), ((4,) + packet, BF16), ((BAND, LANES), BF16), TOKEN],
         [((groups,) + packet, BF16)],
         moved=1000,
     )(back, turned_near, turned_far, proj_columns, gain_row)
@@ -638,26 +636,23 @@
 
     across_later, token = lax.optimization_barrier((across_later, token))
     come_later = send(across_later, "rep", lambda p: p ^ 1)
-    two_sum, three_sum = call(far_pair_sum_body, [(packet, BF16)] * 2, moved=1000)(token, keep, come_first)
+    come_gain_rows = send(gain_rows, "rep", lambda p: p ^ 1)
+    two_sum, three_sum = call(far_pair_sum_body, [(packet, BF16)] * 2, moved=1000)(
+        token, keep, come_first, gain_rows, come_gain_rows
+    )
     two_on = send(two_sum, "rep", lambda p: p ^ 4)
     three_on = send(three_sum, "rep", lambda p: p ^ 6)
-    own_sum, next_one, gain_rows = call(
-        near_pair_sum_body, [(packet, BF16)] * 2 + [((BAND, LANES), BF16)], moved=1000
-    )(two_sum, keep, come_later)
+    own_sum, next_one = call(near_pair_sum_body, [(packet, BF16)] * 2, moved=1000)(two_sum, keep, come_later)
     next_one = send(next_one, "rep", lambda p: p ^ 2)
-    gain_two = send(gain_rows, "rep", lambda p: p ^ 4)
-    gain_three = send(gain_rows, "rep", lambda p: p ^ 6)
-    (token,) = call(gain_sum_body, [TOKEN], moved=1000)(gain_two, gain_three)
+    feature_grad, token = call(feature_body, [half, TOKEN], moved=12 * near * width)(
+        f0_kept, gain_row, norm_back, own_sum
+    )
     (far_sum,) = call(far_sum_body, [(packet, F32)], moved=1000)(token, two_on, three_on)
     (reduced,) = call(last_sum_body, [(packet, BF16)], [((4, BAND, LANES), F32)], moved=1000)(
-        far_sum, own_sum, next_one, gain_two, gain_three
+        far_sum, own_sum, next_one, two_on, three_on
     )
     far_block = send(reduced, "loop", lambda p: p ^ 2)
     near_block = send(reduced, "loop", lambda p: p ^ 1)
-    feature_grad, token = call(feature_body, [half, TOKEN], moved=12 * near * width)(
-        f0_kept, gain_row, norm_back, reduced
-    )
-    far_block, token = lax.optimization_barrier((far_block, token))
     blocks = [reduced, near_block, far_block, send(far_block, "loop", lambda p: p ^ 1)]
 
     proj_grad, gain_gradient = call(
@@ -665,7 +660,7 @@
         [((each, width), F32), ((width,), F32)],
         [((members, bands * BAND, full), F32)],
         moved=8 * each * width,
-    )(token, *blocks)
+    )(*blocks)
     return feature_grad[:, None, :], text_grad[:, None, :], proj_grad, gain_gradient
 
 

time: 55.8 us -> 57.7 us (1.034)
  waiting for transfers between devices: 12.4 us -> 16.3 us
  starting transfers between devices: 16.1 us -> 14.2 us
    ppermute x17 -> x16, waiting for transfers between devices: 12.4 us -> 16.3 us  [send(): return lax.ppermute(value, axis, [(p, target(p)) for p in range(count)])]
    ppermute x17 -> x16, starting transfers between devices: 16.1 us -> 14.2 us  [send(): return lax.ppermute(value, axis, [(p, target(p)) for p in range(count)])]
    pallas_call x16 -> x15, Pallas kernels: 22.2 us -> 22.1 us  [run(): pl.pallas_call(body, out_shape=[jax.ShapeDtypeStruct(shape, kind) for sha...]
  transfers between devices with their start and end apart: 17 -> 16, of which waited for: 9 -> 8; matrix products, arithmetic and copies ran while one was open for 0% -> 0% of each run, Pallas kernels for 35% -> 33%
where the time goes in v19:
time: 57.7 us; the launch traced here: 57.4 us
  Pallas kernels  22.1 us (38%)
  waiting for transfers between devices  16.3 us (28%)
  starting transfers between devices  14.2 us (25%)
  local copies, waits for them, and re-layouts  2.72 us (5%)
  between operations  2.06 us (4%)
    pallas_call x15, Pallas kernels, run(): pl.pallas_call(body, out_shape=[jax.ShapeDtypeStruct(shape, kind) for sha...  22.1 us
    ppermute x16, waiting for transfers between devices, send(): return lax.ppermute(value, axis, [(p, target(p)) for p in range(count)])  16.3 us
    ppermute x16, starting transfers between devices, send(): return lax.ppermute(value, axis, [(p, target(p)) for p in range(count)])  14.2 us
    unnamed x6, local copies, waits for them, and re-layouts  2.72 us
  transfers between devices with their start and end apart: 16, of which 8 were waited for; matrix products, arithmetic and copies ran while one was open for 0% of the time, Pallas kernels for 33%

profile of v19, /device:TPU:0, one launch (start us, length us, event | category | flops | bytes accessed | tf_op | source)
XLA Modules:
  0.0 57.4 jit_solution(761242084025889011)
XLA Ops:
  0.6 0.5 collective-permute-start
  1.2 2.6 %collective-permute-start.3 = (bf16[192,1152]{1,0:T(8,128)(2,1)}, bf16[192,1152]{1,0:T(8,128)(2,1)S(1)}, u32[]{:S(2)}, u32[]{:S(2)}) collective-permute-start(bf16[192,1152]{1,0:T(8,128)(2,1)} %bitcast.6), channel_id=1, source_target_pairs={{0,16},{8,24},{16,0},{24,8},{1,17},{9,25},{17,1},{25,9},{2,18},{10... | collective-permute-start | bytes 1327112 | tf_op jit(solution)/shard_map/ppermute | solution.py:34
  5.0 0.0 collective-permute-done.f1
  5.0 0.0 copy-start
  5.0 1.0 %copy-done = bf16[192,1,1152]{2,0,1:T(8,128)(2,1)S(1)} copy-done((bf16[192,1,1152]{2,0,1:T(8,128)(2,1)S(1)}, bf16[192,1,1152]{2,0,1:T(8,128)(2,1)}, u32[]{:S(2)}) %copy-start) | copy-done | bytes 442392
  6.0 0.0 copy-start.1
  6.0 1.0 %copy-done.1 = bf16[192,1,1152]{2,0,1:T(8,128)(2,1)S(1)} copy-done((bf16[192,1,1152]{2,0,1:T(8,128)(2,1)S(1)}, bf16[192,1,1152]{2,0,1:T(8,128)(2,1)}, u32[]{:S(2)}) %copy-start.1) | copy-done | bytes 442392
  7.1 0.7 %copy-done.2 = f32[1152]{0:T(1024)S(1)} copy-done((f32[1152]{0:T(1024)S(1)}, f32[1152]{0:T(1024)}, u32[]{:S(2)}) %copy-start.2) | copy-done | bytes 4632
  7.7 4.2 %shard_map.93 = (bf16[192,1152]{1,0:T(8,128)(2,1)S(1)}, bf16[1152,1152]{1,0:T(8,128)(2,1)S(1)}, bf16[192,1152]{1,0:T(8,128)(2,1)S(1)}, f32[1,1152]{1,0:T(1,128)S...) custom-call(f32[1]{0:T(128)S(6)} %copy.10.scale, ...), custom_call_target="tpu_custom_call" | custom-call | flops 1019215872 | bytes 3538944 | tf_op jit(solution)/shard_map/pallas_call | solution.py:138
  12.0 0.2 collective-permute-start.1
  12.2 0.6 %collective-permute-start.2 = (bf16[192,1152]{1,0:T(8,128)(2,1)S(1)}, bf16[192,1152]{1,0:T(8,128)(2,1)S(1)}, u32[]{:S(2)}, u32[]{:S(2)}) collective-permute-start(bf16[192,1152]{1,0:T(8,128)(2,1)S(1)} %get-tuple-element.67.text_own), channel_id=1, source_target_pairs={{0,16},{8,24},{16,0},{24,8},{1,17},{9,25},{17,1},{25,9},{2,18},{10... | collective-permute-start | bytes 1327112 | tf_op jit(solution)/shard_map/ppermute | solution.py:34
  12.8 1.9 %collective-permute-done.3.f2 = bf16[192,1152]{1,0:T(8,128)(2,1)S(1)} collective-permute-done((bf16[192,1152]{1,0:T(8,128)(2,1)}, bf16[192,1152]{1,0:T(8,128)(2,1)S(1)}, u32[]{:S(2)}, u32[]{:S(2)}) %collective-permute-start.3) | collective-permute-done | bytes 442400 | tf_op jit(solution)/shard_map/ppermute | solution.py:34
  14.7 0.1 collective-permute-start.4
  14.8 0.5 collective-permute-start.5
  15.3 0.0 collective-permute-done.1.t1
  15.3 1.7 %shard_map.94 = (bf16[384,1152]{1,0:T(8,128)(2,1)S(1)}, bf16[1152,384]{1,0:T(8,128)(2,1)S(1)}, bf16[1152,384]{1,0:T(8,128)(2,1)S(1)}, bf16[288,384]{1,0:T(8,128)...) custom-call(f32[1]{0:T(128)S(6)} %copy.10.scale, ...), custom_call_target="tpu_custom_call" | custom-call | flops 1000 | bytes 1000 | tf_op jit(solution)/shard_map/pallas_call | solution.py:138
  17.0 0.0 collective-permute-done.5.f3_tail
  17.0 0.0 collective-permute-done.4.f3_head
  17.0 4.6 %shard_map.96 = (bf16[1152,384]{1,0:T(8,128)(2,1)S(1)}, bf16[384,1152]{1,0:T(8,128)(2,1)S(1)}, bf16[1152,384]{1,0:T(8,128)(2,1)S(1)}, bf16[288,384]{1,0:T(8,128)...) custom-call(f32[1]{0:T(128)S(6)} %copy.10.scale, ...), custom_call_target="tpu_custom_call" | custom-call | flops 1000 | bytes 1000 | tf_op jit(solution)/shard_map/pallas_call | solution.py:138
  21.7 2.0 %shard_map.97 = (bf16[192,1152]{1,0:T(8,128)(2,1)}, f32[8,128]{1,0:T(8,128)S(1)}) custom-call(f32[1]{0:T(128)S(6)} %copy.10.scale, bf16[192,1152]{1,0:T(8,128)(2,1)S(1)} %get-tuple-element.70.text, bf16[384,384]{1,0:T(8,128)(2,1)S(1)} %get-tuple-element.71.weights_near, bf16[384,384]{1,0:T(8,128)(2,1)S(1)} %get-tuple-element.75.weights_far, ...), custom_call_target="tpu_custom_call" | custom-call | flops 1000 | bytes 1000 | tf_op jit(solution)/shard_map/pallas_call | solution.py:138
  23.7 0.9 %collective-permute-done.2.text_unit.text_third = bf16[192,1152]{1,0:T(8,128)(2,1)S(1)} collective-permute-done((bf16[192,1152]{1,0:T(8,128)(2,1)S(1)}, bf16[192,1152]{1,0:T(8,128)(2,1)S(1)}, u32[]{:S(2)}, u32[]{:S(2)}) %collective-permute-start.2) | collective-permute-done | bytes 442400 | tf_op jit(solution)/shard_map/ppermute | solution.py:34
  24.6 0.0 collective-permute-start.6
  24.6 1.3 %shard_map.98 = (bf16[192,768]{1,0:T(8,128)(2,1)S(1)}, f32[288,384]{1,0:T(8,128)S(1)}, f32[288,384]{1,0:T(8,128)S(1)}, f32[1,768]{1,0:T(1,128)S(1)}) custom-call(f32[1]{0:T(128)S(6)} %copy.10.scale, f32[1]{0:T(128)S(6)} %copy.11.bias, bf16[192,1152]{1,0:T(8,128)(2,1)S(1)} %collective-permute-done.2.text_unit.text_third, ...), custom_call_target="tpu_custom_call" | custom-call | flops 1019215872 | bytes 3538944 | tf_op jit(solution)/shard_map/pallas_call | solution.py:138
  26.0 0.5 collective-permute-done.6.text_unit.text_fourth
  26.4 1.9 %shard_map.99 = (bf16[2,176,256]{2,1,0:T(8,128)(2,1)S(1)}, bf16[288,768]{1,0:T(8,128)(2,1)S(1)}, bf16[192,768]{1,0:T(8,128)(2,1)S(1)}) custom-call(f32[1]{0:T(128)S(6)} %copy.10.scale, f32[1]{0:T(128)S(6)} %copy.11.bias, bf16[192,1152]{1,0:T(8,128)(2,1)S(1)} %collective-permute-done.6.text_unit.text_fourth, ...), custom_call_target="tpu_custom_call" | custom-call | bytes 1000 | tf_op jit(solution)/shard_map/pallas_call | solution.py:138
  28.3 1.6 %collective-permute-start.7 = (bf16[2,176,256]{2,1,0:T(8,128)(2,1)S(1)}, bf16[2,176,256]{2,1,0:T(8,128)(2,1)S(1)}, u32[]{:S(2)}, u32[]{:S(2)}) collective-permute-start(bf16[2,176,256]{2,1,0:T(8,128)(2,1)S(1)} %get-tuple-element.106), channel_id=1, source_target_pairs={{0,1},{1,0},{2,3},{3,2},{4,5},{5,4},{6,7},{7,6},{8,9},{9,8},{10,11... | collective-permute-start | bytes 540680 | tf_op jit(solution)/shard_map/ppermute | solution.py:34
  29.9 1.3 %shard_map.100 = (bf16[2,176,256]{2,1,0:T(8,128)(2,1)S(1)}, bf16[4,176,256]{2,1,0:T(8,128)(2,1)S(1)}, bf16[16,128]{1,0:T(8,128)(2,1)S(1)}, f32[8,128]{1,0:T(8,128)S(1)}) custom-call(bf16[288,768]{1,0:T(8,128)(2,1)S(1)} %get-tuple-element.98.back, bf16[1152,384]{1,0:T(8,128)(2,1)S(1)} %get-tuple-element.95.turned_near, ...), custom_call_target="tpu_custom_call" | custom-call | bytes 1000 | tf_op jit(solution)/shard_map/pallas_call | solution.py:138
  31.2 2.1 %shard_map.101 = (f32[192,1152]{1,0:T(8,128)S(1)}, f32[8,128]{1,0:T(8,128)S(1)}) custom-call(f32[1]{0:T(128)S(6)} %copy.10.scale, bf16[1152,1152]{1,0:T(8,128)(2,1)S(1)} %get-tuple-element.63.proj, bf16[384,1152]{1,0:T(8,128)(2,1)S(1)} %get-tuple-element.69.text_near, bf16[192,1152]{1,0:T(8,128)(2,1)S(1)} %collective-permute-done.2.text_unit.text_third, ...), custom_call_target="tpu_custom_call" | custom-call | bytes 1000 | tf_op jit(solution)/shard_map/pallas_call | solution.py:138
  33.4 0.6 %collective-permute-start.9 = (bf16[2,176,256]{2,1,0:T(8,128)(2,1)S(1)}, bf16[2,176,256]{2,1,0:T(8,128)(2,1)S(1)}, u32[]{:S(2)}, u32[]{:S(2)}) collective-permute-start(bf16[2,176,256]{2,1,0:T(8,128)(2,1)S(1)} %get-tuple-element.109), channel_id=1, source_target_pairs={{0,1},{1,0},{2,3},{3,2},{4,5},{5,4},{6,7},{7,6},{8,9},{9,8},{10,11... | collective-permute-start | bytes 540680 | tf_op jit(solution)/shard_map/ppermute | solution.py:34
  33.9 1.5 %collective-permute-start.8 = (bf16[16,128]{1,0:T(8,128)(2,1)S(1)}, bf16[16,128]{1,0:T(8,128)(2,1)S(1)}, u32[]{:S(2)}, u32[]{:S(2)}) collective-permute-start(bf16[16,128]{1,0:T(8,128)(2,1)S(1)} %get-tuple-element.107.gain_rows), channel_id=1, source_target_pairs={{0,1},{1,0},{2,3},{3,2},{4,5},{5,4},{6,7},{7,6},{8,9},{9,8},{10,11... | collective-permute-start | bytes 12296 | tf_op jit(solution)/shard_map/ppermute | solution.py:34
  35.4 4.5 %collective-permute-done.8.come_gain_rows = bf16[16,128]{1,0:T(8,128)(2,1)S(1)} collective-permute-done((bf16[16,128]{1,0:T(8,128)(2,1)S(1)}, bf16[16,128]{1,0:T(8,128)(2,1)S(1)}, u32[]{:S(2)}, u32[]{:S(2)}) %collective-permute-start.8) | collective-permute-done | bytes 4128 | tf_op jit(solution)/shard_map/ppermute | solution.py:34
  39.9 0.0 collective-permute-done.7.come
  40.0 3.7 %collective-permute-start.11 = (bf16[176,256]{1,0:T(8,128)(2,1)S(1)}, bf16[176,256]{1,0:T(8,128)(2,1)S(1)}, u32[]{:S(2)}, u32[]{:S(2)}) collective-permute-start(bf16[176,256]{1,0:T(8,128)(2,1)S(1)} %get-tuple-element.114), channel_id=1, source_target_pairs={{0,6},{1,7},{2,4},{3,5},{4,2},{5,3},{6,0},{7,1},{8,14},{9,15},{10,... | collective-permute-start | bytes 270344 | tf_op jit(solution)/shard_map/ppermute | solution.py:34
  43.6 0.0 collective-permute-start.10
  43.6 0.0 collective-permute-done.9.come
  43.7 0.8 %collective-permute-start.12 = (bf16[176,256]{1,0:T(8,128)(2,1)S(1)}, bf16[176,256]{1,0:T(8,128)(2,1)S(1)}, u32[]{:S(2)}, u32[]{:S(2)}) collective-permute-start(bf16[176,256]{1,0:T(8,128)(2,1)S(1)} %get-tuple-element.115), channel_id=1, source_target_pairs={{0,2},{1,3},{2,0},{3,1},{4,6},{5,7},{6,4},{7,5},{8,10},{9,11},{10,... | collective-permute-start | bytes 270344 | tf_op jit(solution)/shard_map/ppermute | solution.py:34
  44.5 1.7 %shard_map.104 = (bf16[192,1152]{1,0:T(8,128)(2,1)}, f32[8,128]{1,0:T(8,128)S(1)}) custom-call(bf16[192,1152]{1,0:T(8,128)(2,1)S(1)} %get-tuple-element.61.features, f32[1,1152]{1,0:T(1,128)S(1)} %get-tuple-element.62.gain, f32[192,1152]{1,0:T(8,128)S(1)} %get-tuple-element.101.norm_back, bf16[176,256]{1,0:T(8,128)(2,1)S(1)} %get-tuple-element.110.before.own), custom_call_target="tpu_custom_call" | custom-call | bytes 5308416 | tf_op jit(solution)/shard_map/pallas_call | solution.py:138
  46.2 0.7 %collective-permute-done.11.three_on = bf16[176,256]{1,0:T(8,128)(2,1)S(1)} collective-permute-done((bf16[176,256]{1,0:T(8,128)(2,1)S(1)}, bf16[176,256]{1,0:T(8,128)(2,1)S(1)}, u32[]{:S(2)}, u32[]{:S(2)}) %collective-permute-start.11) | collective-permute-done | bytes 90144 | tf_op jit(solution)/shard_map/ppermute | solution.py:34
  46.9 3.5 %collective-permute-done.10.two_on = bf16[176,256]{1,0:T(8,128)(2,1)S(1)} collective-permute-done((bf16[176,256]{1,0:T(8,128)(2,1)S(1)}, bf16[176,256]{1,0:T(8,128)(2,1)S(1)}, u32[]{:S(2)}, u32[]{:S(2)}) %collective-permute-start.10) | collective-permute-done | bytes 90144 | tf_op jit(solution)/shard_map/ppermute | solution.py:34
  50.5 0.0 collective-permute-done.12.next_one
  50.5 0.1 shard_map.106.refs_0_
  50.5 1.5 %collective-permute-start.14 = (bf16[176,256]{1,0:T(8,128)(2,1)S(1)}, bf16[176,256]{1,0:T(8,128)(2,1)S(1)}, u32[]{:S(2)}, u32[]{:S(2)}) collective-permute-start(bf16[176,256]{1,0:T(8,128)(2,1)S(1)} %shard_map.106.refs_0_), channel_id=1, source_target_pairs={{0,16},{8,24},{16,0},{24,8},{1,17},{9,25},{17,1},{25,9},{2,18},{10... | collective-permute-start | bytes 270344 | tf_op jit(solution)/shard_map/ppermute | solution.py:34
  52.1 0.0 collective-permute-start.13
  52.1 3.1 %collective-permute-done.14.refs_2_ = bf16[176,256]{1,0:T(8,128)(2,1)S(1)} collective-permute-done((bf16[176,256]{1,0:T(8,128)(2,1)S(1)}, bf16[176,256]{1,0:T(8,128)(2,1)S(1)}, u32[]{:S(2)}, u32[]{:S(2)}) %collective-permute-start.14) | collective-permute-done | bytes 90144 | tf_op jit(solution)/shard_map/ppermute | solution.py:34
  55.1 0.0 collective-permute-start.15
  55.1 0.0 collective-permute-done.13.refs_1_
  55.1 1.3 %collective-permute-done.15.refs_3_ = bf16[176,256]{1,0:T(8,128)(2,1)S(1)} collective-permute-done((bf16[176,256]{1,0:T(8,128)(2,1)S(1)}, bf16[176,256]{1,0:T(8,128)(2,1)S(1)}, u32[]{:S(2)}, u32[]{:S(2)}) %collective-permute-start.15) | collective-permute-done | bytes 90144 | tf_op jit(solution)/shard_map/ppermute | solution.py:34
  56.4 1.0 %shard_map.107 = (f32[144,1152]{1,0:T(8,128)}, f32[1152]{0:T(1024)}) custom-call(bf16[176,256]{1,0:T(8,128)(2,1)S(1)} %shard_map.106.refs_0_, bf16[176,256]{1,0:T(8,128)(2,1)S(1)} %collective-permute-done.13.refs_1_, bf16[176,256]{1,0:T(8,128)(2,1)S(1)} %collective-permute-done.14.refs_2_, bf16[176,256]{1,0:T(8,128)(2,1)S(1)} %collective-permute-done.15.refs_3_), custom_call_target="tpu_custom_call" | custom-call | bytes 1327104 | tf_op jit(solution)/shard_map/pallas_call | solution.py:138
  (5 shorter events, 0.1 us)
Async XLA Ops:
  0.6 4.4 %collective-permute-start = (bf16[192,1152]{1,0:T(8,128)(2,1)}, bf16[192,1152]{1,0:T(8,128)(2,1)S(1)}, u32[]{:S(2)}, u32[]{:S(2)}) collective-permute-start(bf16[192,1152]{1,0:T(8,128)(2,1)} %bitcast.5), channel_id=1, source_target_pairs={{0,8},{8,0},{16,24},{24,16},{1,9},{9,1},{17,25},{25,17},{2,10},{10... | collective-permute-start | bytes 1327112 | tf_op jit(solution)/shard_map/ppermute | solution.py:34
  1.2 13.5 %collective-permute-start.3 = (bf16[192,1152]{1,0:T(8,128)(2,1)}, bf16[192,1152]{1,0:T(8,128)(2,1)S(1)}, u32[]{:S(2)}, u32[]{:S(2)}) collective-permute-start(bf16[192,1152]{1,0:T(8,128)(2,1)} %bitcast.6), channel_id=1, source_target_pairs={{0,16},{8,24},{16,0},{24,8},{1,17},{9,25},{17,1},{25,9},{2,18},{10... | collective-permute-start | bytes 1327112 | tf_op jit(solution)/shard_map/ppermute | solution.py:34
  5.0 1.0 %copy-start = (bf16[192,1,1152]{2,0,1:T(8,128)(2,1)S(1)}, bf16[192,1,1152]{2,0,1:T(8,128)(2,1)}, u32[]{:S(2)}) copy-start(bf16[192,1,1152]{2,0,1:T(8,128)(2,1)} %param.7) | copy-start | bytes 1327108
  6.0 1.0 %copy-start.1 = (bf16[192,1,1152]{2,0,1:T(8,128)(2,1)S(1)}, bf16[192,1,1152]{2,0,1:T(8,128)(2,1)}, u32[]{:S(2)}) copy-start(bf16[192,1,1152]{2,0,1:T(8,128)(2,1)} %param.6) | copy-start | bytes 1327108
  7.1 0.7 %copy-start.2 = (f32[1152]{0:T(1024)S(1)}, f32[1152]{0:T(1024)}, u32[]{:S(2)}) copy-start(f32[1152]{0:T(1024)} %gain_line.1) | copy-start | bytes 13828
  12.0 3.3 %collective-permute-start.1 = (bf16[192,1152]{1,0:T(8,128)(2,1)S(1)}, bf16[192,1152]{1,0:T(8,128)(2,1)S(1)}, u32[]{:S(2)}, u32[]{:S(2)}) collective-permute-start(bf16[192,1152]{1,0:T(8,128)(2,1)S(1)} %get-tuple-element.67.text_own), channel_id=1, source_target_pairs={{0,8},{8,0},{16,24},{24,16},{1,9},{9,1},{17,25},{25,17},{2,10},{10... | collective-permute-start | bytes 1327112 | tf_op jit(solution)/shard_map/ppermute | solution.py:34
  12.2 12.4 %collective-permute-start.2 = (bf16[192,1152]{1,0:T(8,128)(2,1)S(1)}, bf16[192,1152]{1,0:T(8,128)(2,1)S(1)}, u32[]{:S(2)}, u32[]{:S(2)}) collective-permute-start(bf16[192,1152]{1,0:T(8,128)(2,1)S(1)} %get-tuple-element.67.text_own), channel_id=1, source_target_pairs={{0,16},{8,24},{16,0},{24,8},{1,17},{9,25},{17,1},{25,9},{2,18},{10... | collective-permute-start | bytes 1327112 | tf_op jit(solution)/shard_map/ppermute | solution.py:34
  14.7 2.3 %collective-permute-start.4 = (bf16[160,1152]{1,0:T(8,128)(2,1)S(1)}, bf16[160,1152]{1,0:T(8,128)(2,1)S(1)}, u32[]{:S(2)}, u32[]{:S(2)}) collective-permute-start(bf16[160,1152]{1,0:T(8,128)(2,1)S(1)} %get-tuple-element.72), channel_id=1, source_target_pairs={{0,8},{8,0},{16,24},{24,16},{1,9},{9,1},{17,25},{25,17},{2,10},{10... | collective-permute-start | bytes 1105928 | tf_op jit(solution)/shard_map/ppermute | solution.py:34
  14.8 2.2 %collective-permute-start.5 = (bf16[32,1152]{1,0:T(8,128)(2,1)S(1)}, bf16[32,1152]{1,0:T(8,128)(2,1)S(1)}, u32[]{:S(2)}, u32[]{:S(2)}) collective-permute-start(bf16[32,1152]{1,0:T(8,128)(2,1)S(1)} %get-tuple-element.73), channel_id=1, source_target_pairs={{0,8},{8,0},{16,24},{24,16},{1,9},{9,1},{17,25},{25,17},{2,10},{10... | collective-permute-start | bytes 221192 | tf_op jit(solution)/shard_map/ppermute | solution.py:34
  24.6 1.8 %collective-permute-start.6 = (bf16[192,1152]{1,0:T(8,128)(2,1)S(1)}, bf16[192,1152]{1,0:T(8,128)(2,1)S(1)}, u32[]{:S(2)}, u32[]{:S(2)}) collective-permute-start(bf16[192,1152]{1,0:T(8,128)(2,1)S(1)} %collective-permute-done.2.text_unit.text_third), channel_id=1, source_target_pairs={{0,8},{8,0},{16,24},{24,16},{1,9},{9,1},{17,25},{25,17},{2,10},{10... | collective-permute-start | bytes 1327112 | tf_op jit(solution)/shard_map/ppermute | solution.py:34
  28.3 11.6 %collective-permute-start.7 = (bf16[2,176,256]{2,1,0:T(8,128)(2,1)S(1)}, bf16[2,176,256]{2,1,0:T(8,128)(2,1)S(1)}, u32[]{:S(2)}, u32[]{:S(2)}) collective-permute-start(bf16[2,176,256]{2,1,0:T(8,128)(2,1)S(1)} %get-tuple-element.106), channel_id=1, source_target_pairs={{0,1},{1,0},{2,3},{3,2},{4,5},{5,4},{6,7},{7,6},{8,9},{9,8},{10,11... | collective-permute-start | bytes 540680 | tf_op jit(solution)/shard_map/ppermute | solution.py:34
  33.4 10.3 %collective-permute-start.9 = (bf16[2,176,256]{2,1,0:T(8,128)(2,1)S(1)}, bf16[2,176,256]{2,1,0:T(8,128)(2,1)S(1)}, u32[]{:S(2)}, u32[]{:S(2)}) collective-permute-start(bf16[2,176,256]{2,1,0:T(8,128)(2,1)S(1)} %get-tuple-element.109), channel_id=1, source_target_pairs={{0,1},{1,0},{2,3},{3,2},{4,5},{5,4},{6,7},{7,6},{8,9},{9,8},{10,11... | collective-permute-start | bytes 540680 | tf_op jit(solution)/shard_map/ppermute | solution.py:34
  33.9 6.0 %collective-permute-start.8 = (bf16[16,128]{1,0:T(8,128)(2,1)S(1)}, bf16[16,128]{1,0:T(8,128)(2,1)S(1)}, u32[]{:S(2)}, u32[]{:S(2)}) collective-permute-start(bf16[16,128]{1,0:T(8,128)(2,1)S(1)} %get-tuple-element.107.gain_rows), channel_id=1, source_target_pairs={{0,1},{1,0},{2,3},{3,2},{4,5},{5,4},{6,7},{7,6},{8,9},{9,8},{10,11... | collective-permute-start | bytes 12296 | tf_op jit(solution)/shard_map/ppermute | solution.py:34
  40.0 7.0 %collective-permute-start.11 = (bf16[176,256]{1,0:T(8,128)(2,1)S(1)}, bf16[176,256]{1,0:T(8,128)(2,1)S(1)}, u32[]{:S(2)}, u32[]{:S(2)}) collective-permute-start(bf16[176,256]{1,0:T(8,128)(2,1)S(1)} %get-tuple-element.114), channel_id=1, source_target_pairs={{0,6},{1,7},{2,4},{3,5},{4,2},{5,3},{6,0},{7,1},{8,14},{9,15},{10,... | collective-permute-start | bytes 270344 | tf_op jit(solution)/shard_map/ppermute | solution.py:34
  43.6 6.8 %collective-permute-start.10 = (bf16[176,256]{1,0:T(8,128)(2,1)S(1)}, bf16[176,256]{1,0:T(8,128)(2,1)S(1)}, u32[]{:S(2)}, u32[]{:S(2)}) collective-permute-start(bf16[176,256]{1,0:T(8,128)(2,1)S(1)} %get-tuple-element.108.before), channel_id=1, source_target_pairs={{0,4},{1,5},{2,6},{3,7},{4,0},{5,1},{6,2},{7,3},{8,12},{9,13},{10,... | collective-permute-start | bytes 270344 | tf_op jit(solution)/shard_map/ppermute | solution.py:34
  43.7 6.8 %collective-permute-start.12 = (bf16[176,256]{1,0:T(8,128)(2,1)S(1)}, bf16[176,256]{1,0:T(8,128)(2,1)S(1)}, u32[]{:S(2)}, u32[]{:S(2)}) collective-permute-start(bf16[176,256]{1,0:T(8,128)(2,1)S(1)} %get-tuple-element.115), channel_id=1, source_target_pairs={{0,2},{1,3},{2,0},{3,1},{4,6},{5,7},{6,4},{7,5},{8,10},{9,11},{10,... | collective-permute-start | bytes 270344 | tf_op jit(solution)/shard_map/ppermute | solution.py:34
  50.5 4.6 %collective-permute-start.14 = (bf16[176,256]{1,0:T(8,128)(2,1)S(1)}, bf16[176,256]{1,0:T(8,128)(2,1)S(1)}, u32[]{:S(2)}, u32[]{:S(2)}) collective-permute-start(bf16[176,256]{1,0:T(8,128)(2,1)S(1)} %shard_map.106.refs_0_), channel_id=1, source_target_pairs={{0,16},{8,24},{16,0},{24,8},{1,17},{9,25},{17,1},{25,9},{2,18},{10... | collective-permute-start | bytes 270344 | tf_op jit(solution)/shard_map/ppermute | solution.py:34
  52.1 3.1 %collective-permute-start.13 = (bf16[176,256]{1,0:T(8,128)(2,1)S(1)}, bf16[176,256]{1,0:T(8,128)(2,1)S(1)}, u32[]{:S(2)}, u32[]{:S(2)}) collective-permute-start(bf16[176,256]{1,0:T(8,128)(2,1)S(1)} %shard_map.106.refs_0_), channel_id=1, source_target_pairs={{0,8},{8,0},{16,24},{24,16},{1,9},{9,1},{17,25},{25,17},{2,10},{10... | collective-permute-start | bytes 270344 | tf_op jit(solution)/shard_map/ppermute | solution.py:34
  55.1 1.3 %collective-permute-start.15 = (bf16[176,256]{1,0:T(8,128)(2,1)S(1)}, bf16[176,256]{1,0:T(8,128)(2,1)S(1)}, u32[]{:S(2)}, u32[]{:S(2)}) collective-permute-start(bf16[176,256]{1,0:T(8,128)(2,1)S(1)} %collective-permute-done.14.refs_2_), channel_id=1, source_target_pairs={{0,8},{8,0},{16,24},{24,16},{1,9},{9,1},{17,25},{25,17},{2,10},{10... | collective-permute-start | bytes 270344 | tf_op jit(solution)/shard_map/ppermute | solution.py:34

commit v20 on v16

--- a/solution.py
+++ b/solution.py
@@ -332,7 +332,7 @@
 def partial_body(
     members, groups, scale, bias, text_unit, flat_near, flat_far, totals, back_near, back_far, unit_turned_near,
     unit_turned_far, inverse_near, inverse_far, turned_near, turned_far, proj_columns, gain,
-    across_first, across_later, keep, weights, text_columns, dots, packed,
+    across_three, across_two, across_later, keep, weights, text_columns, dots, packed,
 ):
     rows = text_unit.shape[0]
     near = 2 * rows
@@ -376,8 +376,9 @@
         packed[group, count - BAND :, full - LANES :] = gain_tile
 
     own = lax.axis_index("rep")
+    across_three[...] = packed[own ^ 7]
+    across_two[...] = packed[own ^ 5]
     for at in range(2):
-        across_first[at] = packed[own ^ 1 ^ (4 + 2 * at)]
         across_later[at] = packed[own ^ 1 ^ (2 * at)]
     for at in range(4):
         keep[at] = packed[own ^ (2 * at)]
@@ -445,9 +446,13 @@
     token[...] = jnp.zeros_like(token)
 
 
-def pair_sum_body(first, before, keep, come, low, high):
-    for at, target in enumerate((low, high)):
-        target[...] = (keep[first + at].astype(F32) + come[at].astype(F32)).astype(BF16)
+def one_sum_body(place, before, keep, come, total):
+    total[...] = (keep[place].astype(F32) + come[...].astype(F32)).astype(BF16)
+
+
+def pair_sum_body(before, keep, come, own, next_one):
+    for at, target in enumerate((own, next_one)):
+        target[...] = (keep[at].astype(F32) + come[at].astype(F32)).astype(BF16)
 
 
 def far_sum_body(before, two_on, three_on, total):
@@ -583,7 +588,7 @@
 
     outs = call(
         functools.partial(partial_body, members, groups),
-        [((2,) + packet, BF16)] * 2 + [((4,) + packet, BF16), narrow],
+        [(packet, BF16)] * 2 + [((2,) + packet, BF16), ((4,) + packet, BF16), narrow],
         [((rows, columns), BF16), ((rows, every), F32), ((groups,) + packet, BF16)],
         smem=2,
         flops=4 * near * width * width,
@@ -592,8 +597,9 @@
         scale, bias, t3, flat_near, flat_far, totals, back_near, back_far, unit_turned_near, unit_turned_far,
         inverse_near, inverse_far, turned_near, turned_far, proj_columns, gain_row,
     )
-    across_first, across_later, keep, weights_fourth = outs
-    come_first = send(across_first, "rep", lambda p: p ^ 1)
+    across_three, across_two, across_later, keep, weights_fourth = outs
+    come_three = send(across_three, "rep", lambda p: p ^ 1)
+    come_two = send(across_two, "rep", lambda p: p ^ 1)
     norm_back, token = call(
         image_body,
         [((rows, width), F32), TOKEN],
@@ -608,15 +614,15 @@
 
     across_later, token = lax.optimization_barrier((across_later, token))
     come_later = send(across_later, "rep", lambda p: p ^ 1)
-    two_on, three_on = call(functools.partial(pair_sum_body, 2), [(packet, BF16)] * 2, moved=1000)(
-        token, keep, come_first
-    )
-    first_two = two_on
-    two_on = send(two_on, "rep", lambda p: p ^ 4)
-    three_on = send(three_on, "rep", lambda p: p ^ 6)
-    own_sum, next_one = call(functools.partial(pair_sum_body, 0), [(packet, BF16)] * 2, moved=1000)(
-        first_two, keep, come_later
-    )
+    (three_sum,) = call(functools.partial(one_sum_body, 3), [(packet, BF16)], flops=1000, moved=1000)(
+        token, keep, come_three
+    )
+    three_on = send(three_sum, "rep", lambda p: p ^ 6)
+    (two_sum,) = call(functools.partial(one_sum_body, 2), [(packet, BF16)], flops=3000000000, moved=1000)(
+        three_sum, keep, come_two
+    )
+    two_on = send(two_sum, "rep", lambda p: p ^ 4)
+    own_sum, next_one = call(pair_sum_body, [(packet, BF16)] * 2, moved=1000)(two_sum, keep, come_later)
     next_one = send(next_one, "rep", lambda p: p ^ 2)
     feature_grad, token = call(feature_body, [half, TOKEN], moved=12 * near * width)(
         f0_kept, gain_row, norm_back, own_sum

time: 54 us -> 53.5 us (level)
  waiting for transfers between devices: 14.1 us -> 11.7 us
  starting transfers between devices: 13.3 us -> 15.1 us
    ppermute x15 -> x16, waiting for transfers between devices: 14.1 us -> 11.7 us  [send(): return lax.ppermute(value, axis, [(p, target(p)) for p in range(count)])]
    ppermute x15 -> x16, starting transfers between devices: 13.3 us -> 15.1 us  [send(): return lax.ppermute(value, axis, [(p, target(p)) for p in range(count)])]
    pallas_call x14 -> x15, Pallas kernels: 21.6 us -> 21.6 us  [run(): pl.pallas_call(body, out_shape=[jax.ShapeDtypeStruct(shape, kind) for sha...]
  transfers between devices with their start and end apart: 15 -> 16, of which waited for: 8 -> 8; matrix products, arithmetic and copies ran while one was open for 0% -> 0% of each run, Pallas kernels for 33% -> 34%
where the time goes in v20:
time: 53.5 us; the launch traced here: 53.2 us
  Pallas kernels  21.6 us (40%)
  starting transfers between devices  15.1 us (28%)
  waiting for transfers between devices  11.7 us (22%)
  local copies, waits for them, and re-layouts  2.72 us (5%)
  between operations  2.06 us (4%)
    pallas_call x15, Pallas kernels, run(): pl.pallas_call(body, out_shape=[jax.ShapeDtypeStruct(shape, kind) for sha...  21.6 us
    ppermute x16, starting transfers between devices, send(): return lax.ppermute(value, axis, [(p, target(p)) for p in range(count)])  15.1 us
    ppermute x16, waiting for transfers between devices, send(): return lax.ppermute(value, axis, [(p, target(p)) for p in range(count)])  11.7 us
    unnamed x6, local copies, waits for them, and re-layouts  2.72 us
  transfers between devices with their start and end apart: 16, of which 8 were waited for; matrix products, arithmetic and copies ran while one was open for 0% of the time, Pallas kernels for 34%

profile of v20, /device:TPU:0, one launch (start us, length us, event | category | flops | bytes accessed | tf_op | source)
XLA Modules:
  0.0 53.2 jit_solution(5988483403699463996)
XLA Ops:
  0.6 0.5 collective-permute-start
  1.2 2.6 %collective-permute-start.3 = (bf16[192,1152]{1,0:T(8,128)(2,1)}, bf16[192,1152]{1,0:T(8,128)(2,1)S(1)}, u32[]{:S(2)}, u32[]{:S(2)}) collective-permute-start(bf16[192,1152]{1,0:T(8,128)(2,1)} %bitcast.6), channel_id=1, source_target_pairs={{0,16},{8,24},{16,0},{24,8},{1,17},{9,25},{17,1},{25,9},{2,18},{10... | collective-permute-start | bytes 1327112 | tf_op jit(solution)/shard_map/ppermute | solution.py:34
  5.0 0.0 collective-permute-done.f1
  5.0 0.0 copy-start
  5.0 1.0 %copy-done = bf16[192,1,1152]{2,0,1:T(8,128)(2,1)S(1)} copy-done((bf16[192,1,1152]{2,0,1:T(8,128)(2,1)S(1)}, bf16[192,1,1152]{2,0,1:T(8,128)(2,1)}, u32[]{:S(2)}) %copy-start) | copy-done | bytes 442392
  6.0 0.0 copy-start.1
  6.0 1.0 %copy-done.1 = bf16[192,1,1152]{2,0,1:T(8,128)(2,1)S(1)} copy-done((bf16[192,1,1152]{2,0,1:T(8,128)(2,1)S(1)}, bf16[192,1,1152]{2,0,1:T(8,128)(2,1)}, u32[]{:S(2)}) %copy-start.1) | copy-done | bytes 442392
  7.1 0.0 copy-start.2
  7.1 0.7 %copy-done.2 = f32[1152]{0:T(1024)S(1)} copy-done((f32[1152]{0:T(1024)S(1)}, f32[1152]{0:T(1024)}, u32[]{:S(2)}) %copy-start.2) | copy-done | bytes 4632
  7.7 4.2 %shard_map.93 = (bf16[192,1152]{1,0:T(8,128)(2,1)S(1)}, bf16[1152,1152]{1,0:T(8,128)(2,1)S(1)}, bf16[192,1152]{1,0:T(8,128)(2,1)S(1)}, f32[1,1152]{1,0:T(1,128)S...) custom-call(f32[1]{0:T(128)S(6)} %copy.10.scale, ...), custom_call_target="tpu_custom_call" | custom-call | flops 1019215872 | bytes 3538944 | tf_op jit(solution)/shard_map/pallas_call | solution.py:138
  12.0 0.2 collective-permute-start.1
  12.2 0.6 %collective-permute-start.2 = (bf16[192,1152]{1,0:T(8,128)(2,1)S(1)}, bf16[192,1152]{1,0:T(8,128)(2,1)S(1)}, u32[]{:S(2)}, u32[]{:S(2)}) collective-permute-start(bf16[192,1152]{1,0:T(8,128)(2,1)S(1)} %get-tuple-element.63.text_own), channel_id=1, source_target_pairs={{0,16},{8,24},{16,0},{24,8},{1,17},{9,25},{17,1},{25,9},{2,18},{10... | collective-permute-start | bytes 1327112 | tf_op jit(solution)/shard_map/ppermute | solution.py:34
  12.8 1.9 %collective-permute-done.3.f2 = bf16[192,1152]{1,0:T(8,128)(2,1)S(1)} collective-permute-done((bf16[192,1152]{1,0:T(8,128)(2,1)}, bf16[192,1152]{1,0:T(8,128)(2,1)S(1)}, u32[]{:S(2)}, u32[]{:S(2)}) %collective-permute-start.3) | collective-permute-done | bytes 442400 | tf_op jit(solution)/shard_map/ppermute | solution.py:34
  14.7 0.1 collective-permute-start.4
  14.8 0.5 collective-permute-start.5
  15.3 0.0 collective-permute-done.1.t1
  15.3 1.7 %shard_map.94 = (bf16[384,1152]{1,0:T(8,128)(2,1)S(1)}, bf16[1152,384]{1,0:T(8,128)(2,1)S(1)}, bf16[1152,384]{1,0:T(8,128)(2,1)S(1)}, bf16[288,384]{1,0:T(8,128)...) custom-call(f32[1]{0:T(128)S(6)} %copy.10.scale, ...), custom_call_target="tpu_custom_call" | custom-call | flops 1000 | bytes 1000 | tf_op jit(solution)/shard_map/pallas_call | solution.py:138
  17.0 0.0 collective-permute-done.5.f3_tail
  17.0 0.0 collective-permute-done.4.f3_head
  17.0 4.6 %shard_map.96 = (bf16[1152,384]{1,0:T(8,128)(2,1)S(1)}, bf16[384,1152]{1,0:T(8,128)(2,1)S(1)}, bf16[1152,384]{1,0:T(8,128)(2,1)S(1)}, bf16[288,384]{1,0:T(8,128)...) custom-call(f32[1]{0:T(128)S(6)} %copy.10.scale, ...), custom_call_target="tpu_custom_call" | custom-call | flops 1000 | bytes 1000 | tf_op jit(solution)/shard_map/pallas_call | solution.py:138
  21.7 2.0 %shard_map.97 = (bf16[192,1152]{1,0:T(8,128)(2,1)}, f32[8,128]{1,0:T(8,128)S(1)}) custom-call(f32[1]{0:T(128)S(6)} %copy.10.scale, bf16[192,1152]{1,0:T(8,128)(2,1)S(1)} %get-tuple-element.66.text, bf16[384,384]{1,0:T(8,128)(2,1)S(1)} %get-tuple-element.67.weights_near, bf16[384,384]{1,0:T(8,128)(2,1)S(1)} %get-tuple-element.71.weights_far, ...), custom_call_target="tpu_custom_call" | custom-call | flops 1000 | bytes 1000 | tf_op jit(solution)/shard_map/pallas_call | solution.py:138
  23.7 0.9 %collective-permute-done.2.text_unit.text_third = bf16[192,1152]{1,0:T(8,128)(2,1)S(1)} collective-permute-done((bf16[192,1152]{1,0:T(8,128)(2,1)S(1)}, bf16[192,1152]{1,0:T(8,128)(2,1)S(1)}, u32[]{:S(2)}, u32[]{:S(2)}) %collective-permute-start.2) | collective-permute-done | bytes 442400 | tf_op jit(solution)/shard_map/ppermute | solution.py:34
  24.6 0.0 collective-permute-start.6
  24.6 1.3 %shard_map.98 = (bf16[192,768]{1,0:T(8,128)(2,1)S(1)}, f32[288,384]{1,0:T(8,128)S(1)}, f32[288,384]{1,0:T(8,128)S(1)}, f32[1,768]{1,0:T(1,128)S(1)}) custom-call(f32[1]{0:T(128)S(6)} %copy.10.scale, f32[1]{0:T(128)S(6)} %copy.11.bias, bf16[192,1152]{1,0:T(8,128)(2,1)S(1)} %collective-permute-done.2.text_unit.text_third, ...), custom_call_target="tpu_custom_call" | custom-call | flops 1019215872 | bytes 3538944 | tf_op jit(solution)/shard_map/pallas_call | solution.py:138
  26.0 0.5 collective-permute-done.6.text_unit.text_fourth
  26.4 2.7 %shard_map.99 = (bf16[176,256]{1,0:T(8,128)(2,1)S(1)}, bf16[176,256]{1,0:T(8,128)(2,1)S(1)}, bf16[2,176,256]{2,1,0:T(8,128)(2,1)S(1)}, bf16[4,176,256]{2,1,0:T(8,128)(2,1)S(1)}, bf16[192,768]{1,0:T(8,128)(2,1)S(1)}) custom-call(f32[1]{0:T(128)S(6)} %copy.10.scale, f32[1]{0:T(128)S(6)} %copy.11.bias, ...), custom_call_target="tpu_custom_call" | custom-call | flops 2038431744 | bytes 7077888 | tf_op jit(solution)/shard_map/pallas_call | solution.py:138
  29.2 1.6 %collective-permute-start.7 = (bf16[176,256]{1,0:T(8,128)(2,1)S(1)}, bf16[176,256]{1,0:T(8,128)(2,1)S(1)}, u32[]{:S(2)}, u32[]{:S(2)}) collective-permute-start(bf16[176,256]{1,0:T(8,128)(2,1)S(1)} %get-tuple-element.100), channel_id=1, source_target_pairs={{0,1},{1,0},{2,3},{3,2},{4,5},{5,4},{6,7},{7,6},{8,9},{9,8},{10,11... | collective-permute-start | bytes 270344 | tf_op jit(solution)/shard_map/ppermute | solution.py:34
  30.7 0.5 collective-permute-start.8
  31.3 2.1 %shard_map.100 = (f32[192,1152]{1,0:T(8,128)S(1)}, f32[8,128]{1,0:T(8,128)S(1)}) custom-call(f32[1]{0:T(128)S(6)} %copy.10.scale, bf16[1152,1152]{1,0:T(8,128)(2,1)S(1)} %get-tuple-element.59.proj, bf16[384,1152]{1,0:T(8,128)(2,1)S(1)} %get-tuple-element.65.text_near, bf16[192,1152]{1,0:T(8,128)(2,1)S(1)} %collective-permute-done.2.text_unit.text_third, ...), custom_call_target="tpu_custom_call" | custom-call | flops 1000 | bytes 1000 | tf_op jit(solution)/shard_map/pallas_call | solution.py:138
  33.4 1.6 %collective-permute-start.9 = (bf16[2,176,256]{2,1,0:T(8,128)(2,1)S(1)}, bf16[2,176,256]{2,1,0:T(8,128)(2,1)S(1)}, u32[]{:S(2)}, u32[]{:S(2)}) collective-permute-start(bf16[2,176,256]{2,1,0:T(8,128)(2,1)S(1)} %get-tuple-element.102), channel_id=1, source_target_pairs={{0,1},{1,0},{2,3},{3,2},{4,5},{5,4},{6,7},{7,6},{8,9},{9,8},{10,11... | collective-permute-start | bytes 540680 | tf_op jit(solution)/shard_map/ppermute | solution.py:34
  34.9 0.0 collective-permute-done.7.come
  35.0 3.7 %collective-permute-start.11 = (bf16[176,256]{1,0:T(8,128)(2,1)S(1)}, bf16[176,256]{1,0:T(8,128)(2,1)S(1)}, u32[]{:S(2)}, u32[]{:S(2)}) collective-permute-start(bf16[176,256]{1,0:T(8,128)(2,1)S(1)} %shard_map.101.before), channel_id=1, source_target_pairs={{0,6},{1,7},{2,4},{3,5},{4,2},{5,3},{6,0},{7,1},{8,14},{9,15},{10,... | collective-permute-start | bytes 270344 | tf_op jit(solution)/shard_map/ppermute | solution.py:34
  38.6 0.0 collective-permute-done.8.come
  38.7 0.1 collective-permute-start.10
  38.8 1.0 %collective-permute-done.9.come = bf16[2,176,256]{2,1,0:T(8,128)(2,1)S(1)} collective-permute-done((bf16[2,176,256]{2,1,0:T(8,128)(2,1)S(1)}, bf16[2,176,256]{2,1,0:T(8,128)(2,1)S(1)}, u32[]{:S(2)}, u32[]{:S(2)}) %collective-permute-start.9) | collective-permute-done | bytes 180256 | tf_op jit(solution)/shard_map/ppermute | solution.py:34
  39.8 1.6 %collective-permute-start.12 = (bf16[176,256]{1,0:T(8,128)(2,1)S(1)}, bf16[176,256]{1,0:T(8,128)(2,1)S(1)}, u32[]{:S(2)}, u32[]{:S(2)}) collective-permute-start(bf16[176,256]{1,0:T(8,128)(2,1)S(1)} %get-tuple-element.107), channel_id=1, source_target_pairs={{0,2},{1,3},{2,0},{3,1},{4,6},{5,7},{6,4},{7,5},{8,10},{9,11},{10,... | collective-permute-start | bytes 270344 | tf_op jit(solution)/shard_map/ppermute | solution.py:34
  41.5 1.7 %shard_map.104 = (bf16[192,1152]{1,0:T(8,128)(2,1)}, f32[8,128]{1,0:T(8,128)S(1)}) custom-call(bf16[192,1152]{1,0:T(8,128)(2,1)S(1)} %get-tuple-element.57.features, f32[1,1152]{1,0:T(1,128)S(1)} %get-tuple-element.58.gain, f32[192,1152]{1,0:T(8,128)S(1)} %get-tuple-element.95.norm_back, bf16[176,256]{1,0:T(8,128)(2,1)S(1)} %get-tuple-element.103.before.own), custom_call_target="tpu_custom_call" | custom-call | bytes 5308416 | tf_op jit(solution)/shard_map/pallas_call | solution.py:138
  43.2 0.0 collective-permute-done.11.three_on
  43.2 2.7 %collective-permute-done.10.two_on = bf16[176,256]{1,0:T(8,128)(2,1)S(1)} collective-permute-done((bf16[176,256]{1,0:T(8,128)(2,1)S(1)}, bf16[176,256]{1,0:T(8,128)(2,1)S(1)}, u32[]{:S(2)}, u32[]{:S(2)}) %collective-permute-start.10) | collective-permute-done | bytes 90144 | tf_op jit(solution)/shard_map/ppermute | solution.py:34
  45.9 0.4 collective-permute-done.12.next_one
  46.3 0.1 shard_map.106.refs_0_
  46.3 1.6 %collective-permute-start.14 = (bf16[176,256]{1,0:T(8,128)(2,1)S(1)}, bf16[176,256]{1,0:T(8,128)(2,1)S(1)}, u32[]{:S(2)}, u32[]{:S(2)}) collective-permute-start(bf16[176,256]{1,0:T(8,128)(2,1)S(1)} %shard_map.106.refs_0_), channel_id=1, source_target_pairs={{0,16},{8,24},{16,0},{24,8},{1,17},{9,25},{17,1},{25,9},{2,18},{10... | collective-permute-start | bytes 270344 | tf_op jit(solution)/shard_map/ppermute | solution.py:34
  47.9 0.0 collective-permute-start.13
  47.9 3.0 %collective-permute-done.14.refs_2_ = bf16[176,256]{1,0:T(8,128)(2,1)S(1)} collective-permute-done((bf16[176,256]{1,0:T(8,128)(2,1)S(1)}, bf16[176,256]{1,0:T(8,128)(2,1)S(1)}, u32[]{:S(2)}, u32[]{:S(2)}) %collective-permute-start.14) | collective-permute-done | bytes 90144 | tf_op jit(solution)/shard_map/ppermute | solution.py:34
  50.9 0.0 collective-permute-start.15
  50.9 0.0 collective-permute-done.13.refs_1_
  50.9 1.3 %collective-permute-done.15.refs_3_ = bf16[176,256]{1,0:T(8,128)(2,1)S(1)} collective-permute-done((bf16[176,256]{1,0:T(8,128)(2,1)S(1)}, bf16[176,256]{1,0:T(8,128)(2,1)S(1)}, u32[]{:S(2)}, u32[]{:S(2)}) %collective-permute-start.15) | collective-permute-done | bytes 90144 | tf_op jit(solution)/shard_map/ppermute | solution.py:34
  52.2 1.0 %shard_map.107 = (f32[144,1152]{1,0:T(8,128)}, f32[1152]{0:T(1024)}) custom-call(bf16[176,256]{1,0:T(8,128)(2,1)S(1)} %shard_map.106.refs_0_, bf16[176,256]{1,0:T(8,128)(2,1)S(1)} %collective-permute-done.13.refs_1_, bf16[176,256]{1,0:T(8,128)(2,1)S(1)} %collective-permute-done.14.refs_2_, bf16[176,256]{1,0:T(8,128)(2,1)S(1)} %collective-permute-done.15.refs_3_), custom_call_target="tpu_custom_call" | custom-call | bytes 1327104 | tf_op jit(solution)/shard_map/pallas_call | solution.py:138
  (5 shorter events, 0.1 us)
Async XLA Ops:
  0.6 4.4 %collective-permute-start = (bf16[192,1152]{1,0:T(8,128)(2,1)}, bf16[192,1152]{1,0:T(8,128)(2,1)S(1)}, u32[]{:S(2)}, u32[]{:S(2)}) collective-permute-start(bf16[192,1152]{1,0:T(8,128)(2,1)} %bitcast.5), channel_id=1, source_target_pairs={{0,8},{8,0},{16,24},{24,16},{1,9},{9,1},{17,25},{25,17},{2,10},{10... | collective-permute-start | bytes 1327112 | tf_op jit(solution)/shard_map/ppermute | solution.py:34
  1.2 13.5 %collective-permute-start.3 = (bf16[192,1152]{1,0:T(8,128)(2,1)}, bf16[192,1152]{1,0:T(8,128)(2,1)S(1)}, u32[]{:S(2)}, u32[]{:S(2)}) collective-permute-start(bf16[192,1152]{1,0:T(8,128)(2,1)} %bitcast.6), channel_id=1, source_target_pairs={{0,16},{8,24},{16,0},{24,8},{1,17},{9,25},{17,1},{25,9},{2,18},{10... | collective-permute-start | bytes 1327112 | tf_op jit(solution)/shard_map/ppermute | solution.py:34
  5.0 1.0 %copy-start = (bf16[192,1,1152]{2,0,1:T(8,128)(2,1)S(1)}, bf16[192,1,1152]{2,0,1:T(8,128)(2,1)}, u32[]{:S(2)}) copy-start(bf16[192,1,1152]{2,0,1:T(8,128)(2,1)} %param.7) | copy-start | bytes 1327108
  6.0 1.0 %copy-start.1 = (bf16[192,1,1152]{2,0,1:T(8,128)(2,1)S(1)}, bf16[192,1,1152]{2,0,1:T(8,128)(2,1)}, u32[]{:S(2)}) copy-start(bf16[192,1,1152]{2,0,1:T(8,128)(2,1)} %param.6) | copy-start | bytes 1327108
  7.1 0.7 %copy-start.2 = (f32[1152]{0:T(1024)S(1)}, f32[1152]{0:T(1024)}, u32[]{:S(2)}) copy-start(f32[1152]{0:T(1024)} %gain_line.1) | copy-start | bytes 13828
  12.0 3.3 %collective-permute-start.1 = (bf16[192,1152]{1,0:T(8,128)(2,1)S(1)}, bf16[192,1152]{1,0:T(8,128)(2,1)S(1)}, u32[]{:S(2)}, u32[]{:S(2)}) collective-permute-start(bf16[192,1152]{1,0:T(8,128)(2,1)S(1)} %get-tuple-element.63.text_own), channel_id=1, source_target_pairs={{0,8},{8,0},{16,24},{24,16},{1,9},{9,1},{17,25},{25,17},{2,10},{10... | collective-permute-start | bytes 1327112 | tf_op jit(solution)/shard_map/ppermute | solution.py:34
  12.2 12.4 %collective-permute-start.2 = (bf16[192,1152]{1,0:T(8,128)(2,1)S(1)}, bf16[192,1152]{1,0:T(8,128)(2,1)S(1)}, u32[]{:S(2)}, u32[]{:S(2)}) collective-permute-start(bf16[192,1152]{1,0:T(8,128)(2,1)S(1)} %get-tuple-element.63.text_own), channel_id=1, source_target_pairs={{0,16},{8,24},{16,0},{24,8},{1,17},{9,25},{17,1},{25,9},{2,18},{10... | collective-permute-start | bytes 1327112 | tf_op jit(solution)/shard_map/ppermute | solution.py:34
  14.7 2.3 %collective-permute-start.4 = (bf16[160,1152]{1,0:T(8,128)(2,1)S(1)}, bf16[160,1152]{1,0:T(8,128)(2,1)S(1)}, u32[]{:S(2)}, u32[]{:S(2)}) collective-permute-start(bf16[160,1152]{1,0:T(8,128)(2,1)S(1)} %get-tuple-element.68), channel_id=1, source_target_pairs={{0,8},{8,0},{16,24},{24,16},{1,9},{9,1},{17,25},{25,17},{2,10},{10... | collective-permute-start | bytes 1105928 | tf_op jit(solution)/shard_map/ppermute | solution.py:34
  14.8 2.2 %collective-permute-start.5 = (bf16[32,1152]{1,0:T(8,128)(2,1)S(1)}, bf16[32,1152]{1,0:T(8,128)(2,1)S(1)}, u32[]{:S(2)}, u32[]{:S(2)}) collective-permute-start(bf16[32,1152]{1,0:T(8,128)(2,1)S(1)} %get-tuple-element.69), channel_id=1, source_target_pairs={{0,8},{8,0},{16,24},{24,16},{1,9},{9,1},{17,25},{25,17},{2,10},{10... | collective-permute-start | bytes 221192 | tf_op jit(solution)/shard_map/ppermute | solution.py:34
  24.6 1.8 %collective-permute-start.6 = (bf16[192,1152]{1,0:T(8,128)(2,1)S(1)}, bf16[192,1152]{1,0:T(8,128)(2,1)S(1)}, u32[]{:S(2)}, u32[]{:S(2)}) collective-permute-start(bf16[192,1152]{1,0:T(8,128)(2,1)S(1)} %collective-permute-done.2.text_unit.text_third), channel_id=1, source_target_pairs={{0,8},{8,0},{16,24},{24,16},{1,9},{9,1},{17,25},{25,17},{2,10},{10... | collective-permute-start | bytes 1327112 | tf_op jit(solution)/shard_map/ppermute | solution.py:34
  29.2 5.8 %collective-permute-start.7 = (bf16[176,256]{1,0:T(8,128)(2,1)S(1)}, bf16[176,256]{1,0:T(8,128)(2,1)S(1)}, u32[]{:S(2)}, u32[]{:S(2)}) collective-permute-start(bf16[176,256]{1,0:T(8,128)(2,1)S(1)} %get-tuple-element.100), channel_id=1, source_target_pairs={{0,1},{1,0},{2,3},{3,2},{4,5},{5,4},{6,7},{7,6},{8,9},{9,8},{10,11... | collective-permute-start | bytes 270344 | tf_op jit(solution)/shard_map/ppermute | solution.py:34
  30.7 7.9 %collective-permute-start.8 = (bf16[176,256]{1,0:T(8,128)(2,1)S(1)}, bf16[176,256]{1,0:T(8,128)(2,1)S(1)}, u32[]{:S(2)}, u32[]{:S(2)}) collective-permute-start(bf16[176,256]{1,0:T(8,128)(2,1)S(1)} %get-tuple-element.101), channel_id=1, source_target_pairs={{0,1},{1,0},{2,3},{3,2},{4,5},{5,4},{6,7},{7,6},{8,9},{9,8},{10,11... | collective-permute-start | bytes 270344 | tf_op jit(solution)/shard_map/ppermute | solution.py:34
  33.4 6.4 %collective-permute-start.9 = (bf16[2,176,256]{2,1,0:T(8,128)(2,1)S(1)}, bf16[2,176,256]{2,1,0:T(8,128)(2,1)S(1)}, u32[]{:S(2)}, u32[]{:S(2)}) collective-permute-start(bf16[2,176,256]{2,1,0:T(8,128)(2,1)S(1)} %get-tuple-element.102), channel_id=1, source_target_pairs={{0,1},{1,0},{2,3},{3,2},{4,5},{5,4},{6,7},{7,6},{8,9},{9,8},{10,11... | collective-permute-start | bytes 540680 | tf_op jit(solution)/shard_map/ppermute | solution.py:34
  35.0 8.2 %collective-permute-start.11 = (bf16[176,256]{1,0:T(8,128)(2,1)S(1)}, bf16[176,256]{1,0:T(8,128)(2,1)S(1)}, u32[]{:S(2)}, u32[]{:S(2)}) collective-permute-start(bf16[176,256]{1,0:T(8,128)(2,1)S(1)} %shard_map.101.before), channel_id=1, source_target_pairs={{0,6},{1,7},{2,4},{3,5},{4,2},{5,3},{6,0},{7,1},{8,14},{9,15},{10,... | collective-permute-start | bytes 270344 | tf_op jit(solution)/shard_map/ppermute | solution.py:34
  38.7 7.2 %collective-permute-start.10 = (bf16[176,256]{1,0:T(8,128)(2,1)S(1)}, bf16[176,256]{1,0:T(8,128)(2,1)S(1)}, u32[]{:S(2)}, u32[]{:S(2)}) collective-permute-start(bf16[176,256]{1,0:T(8,128)(2,1)S(1)} %shard_map.102.before), channel_id=1, source_target_pairs={{0,4},{1,5},{2,6},{3,7},{4,0},{5,1},{6,2},{7,3},{8,12},{9,13},{10,... | collective-permute-start | bytes 270344 | tf_op jit(solution)/shard_map/ppermute | solution.py:34
  39.8 6.5 %collective-permute-start.12 = (bf16[176,256]{1,0:T(8,128)(2,1)S(1)}, bf16[176,256]{1,0:T(8,128)(2,1)S(1)}, u32[]{:S(2)}, u32[]{:S(2)}) collective-permute-start(bf16[176,256]{1,0:T(8,128)(2,1)S(1)} %get-tuple-element.107), channel_id=1, source_target_pairs={{0,2},{1,3},{2,0},{3,1},{4,6},{5,7},{6,4},{7,5},{8,10},{9,11},{10,... | collective-permute-start | bytes 270344 | tf_op jit(solution)/shard_map/ppermute | solution.py:34
  46.3 4.6 %collective-permute-start.14 = (bf16[176,256]{1,0:T(8,128)(2,1)S(1)}, bf16[176,256]{1,0:T(8,128)(2,1)S(1)}, u32[]{:S(2)}, u32[]{:S(2)}) collective-permute-start(bf16[176,256]{1,0:T(8,128)(2,1)S(1)} %shard_map.106.refs_0_), channel_id=1, source_target_pairs={{0,16},{8,24},{16,0},{24,8},{1,17},{9,25},{17,1},{25,9},{2,18},{10... | collective-permute-start | bytes 270344 | tf_op jit(solution)/shard_map/ppermute | solution.py:34
  47.9 3.0 %collective-permute-start.13 = (bf16[176,256]{1,0:T(8,128)(2,1)S(1)}, bf16[176,256]{1,0:T(8,128)(2,1)S(1)}, u32[]{:S(2)}, u32[]{:S(2)}) collective-permute-start(bf16[176,256]{1,0:T(8,128)(2,1)S(1)} %shard_map.106.refs_0_), channel_id=1, source_target_pairs={{0,8},{8,0},{16,24},{24,16},{1,9},{9,1},{17,25},{25,17},{2,10},{10... | collective-permute-start | bytes 270344 | tf_op jit(solution)/shard_map/ppermute | solution.py:34
  50.9 1.3 %collective-permute-start.15 = (bf16[176,256]{1,0:T(8,128)(2,1)S(1)}, bf16[176,256]{1,0:T(8,128)(2,1)S(1)}, u32[]{:S(2)}, u32[]{:S(2)}) collective-permute-start(bf16[176,256]{1,0:T(8,128)(2,1)S(1)} %collective-permute-done.14.refs_2_), channel_id=1, source_target_pairs={{0,8},{8,0},{16,24},{24,16},{1,9},{9,1},{17,25},{25,17},{2,10},{10... | collective-permute-start | bytes 270344 | tf_op jit(solution)/shard_map/ppermute | solution.py:34

commit v21 on v17

--- a/solution.py
+++ b/solution.py
@@ -332,7 +332,7 @@
 def partial_body(
     members, groups, scale, bias, text_unit, flat_near, flat_far, totals, back_near, back_far, unit_turned_near,
     unit_turned_far, inverse_near, inverse_far, turned_near, turned_far, proj_columns, gain,
-    across_three, across_near, across_own, keep, weights, text_columns, dots, packed,
+    across_three, across_two, across_next, across_own, keep, weights, text_columns, dots, packed,
 ):
     rows = text_unit.shape[0]
     near = 2 * rows
@@ -377,8 +377,8 @@
 
     own = lax.axis_index("rep")
     across_three[...] = packed[own ^ 7]
-    across_near[0] = packed[own ^ 3]
-    across_near[1] = packed[own ^ 5]
+    across_two[...] = packed[own ^ 5]
+    across_next[...] = packed[own ^ 3]
     across_own[...] = packed[own ^ 1]
     for at in range(4):
         keep[at] = packed[own ^ (2 * at)]
@@ -386,7 +386,7 @@
 
 def image_body(
     scale, proj, text_near, text_third, text_fourth, weights_near, weights_third, weights_fourth,
-    unit, factors, norm_back, token, back, product,
+    unit, factors, before, norm_back, token, back, product,
 ):
     rows = back.shape[0]
     scale = scale[0]
@@ -446,13 +446,8 @@
     token[...] = jnp.zeros_like(token)
 
 
-def three_sum_body(before, keep, come, total):
-    total[...] = (keep[3].astype(F32) + come[...].astype(F32)).astype(BF16)
-
-
-def near_sum_body(before, keep, come, next_one, two_on):
-    for at, target in enumerate((next_one, two_on)):
-        target[...] = (keep[1 + at].astype(F32) + come[at].astype(F32)).astype(BF16)
+def one_sum_body(place, before, keep, come, total):
+    total[...] = (keep[place].astype(F32) + come[...].astype(F32)).astype(BF16)
 
 
 def far_sum_body(before, two_on, three_on, total):
@@ -589,7 +584,7 @@
 
     outs = call(
         functools.partial(partial_body, members, groups),
-        [(packet, BF16), ((2,) + packet, BF16), (packet, BF16), ((4,) + packet, BF16), narrow],
+        [(packet, BF16)] * 4 + [((4,) + packet, BF16), narrow],
         [((rows, columns), BF16), ((rows, every), F32), ((groups,) + packet, BF16)],
         smem=2,
         flops=4 * near * width * width,
@@ -598,8 +593,23 @@
         scale, bias, t3, flat_near, flat_far, totals, back_near, back_far, unit_turned_near, unit_turned_far,
         inverse_near, inverse_far, turned_near, turned_far, proj_columns, gain_row,
     )
-    across_three, across_near, across_own, keep, weights_fourth = outs
+    across_three, across_two, across_next, across_own, keep, weights_fourth = outs
     come_three = send(across_three, "rep", lambda p: p ^ 1)
+    come_two = send(across_two, "rep", lambda p: p ^ 1)
+    come_next = send(across_next, "rep", lambda p: p ^ 1)
+    come_own = send(across_own, "rep", lambda p: p ^ 1)
+    (three_sum,) = call(functools.partial(one_sum_body, 3), [(packet, BF16)], flops=1000, moved=1000)(
+        keep, keep, come_three
+    )
+    three_on = send(three_sum, "rep", lambda p: p ^ 6)
+    (two_sum,) = call(functools.partial(one_sum_body, 2), [(packet, BF16)], flops=1000, moved=1000)(
+        three_sum, keep, come_two
+    )
+    two_on = send(two_sum, "rep", lambda p: p ^ 4)
+    (next_sum,) = call(functools.partial(one_sum_body, 1), [(packet, BF16)], flops=1000, moved=1000)(
+        two_sum, keep, come_next
+    )
+    next_one = send(next_sum, "rep", lambda p: p ^ 2)
     norm_back, token = call(
         image_body,
         [((rows, width), F32), TOKEN],
@@ -609,21 +619,9 @@
         moved=1000,
     )(
         scale, proj_kept, text_near, t2, t3, weights_near, weights_third, weights_fourth,
-        unit_near, factors,
-    )
-
-    across_near, token = lax.optimization_barrier((across_near, token))
-    come_near = send(across_near, "rep", lambda p: p ^ 1)
-    (three_sum,) = call(three_sum_body, [(packet, BF16)], flops=3000000000, moved=1000)(token, keep, come_three)
-    three_on = send(three_sum, "rep", lambda p: p ^ 6)
-    next_sum, two_sum = call(near_sum_body, [(packet, BF16)] * 2, moved=1000)(three_sum, keep, come_near)
-    two_on = send(two_sum, "rep", lambda p: p ^ 4)
-    next_one = send(next_sum, "rep", lambda p: p ^ 2)
-    across_own, next_sum = lax.optimization_barrier((across_own, next_sum))
-    come_own = send(across_own, "rep", lambda p: p ^ 1)
-    feature_grad, token = call(feature_body, [half, TOKEN], moved=12 * near * width)(
-        f0_kept, gain_row, norm_back, next_sum
-    )
+        unit_near, factors, next_sum,
+    )
+    feature_grad, token = call(feature_body, [half, TOKEN], moved=1000)(f0_kept, gain_row, norm_back, token)
     (far_sum,) = call(far_sum_body, [(packet, F32)], moved=1000)(token, two_on, three_on)
     (reduced,) = call(last_sum_body, [(packet, BF16)], [((4, BAND, LANES), F32), (packet, BF16)], moved=1000)(
         far_sum, keep, come_own, next_one, two_on, three_on

time: 54.3 us -> 53.6 us (0.987)
  waiting for transfers between devices: 11 us -> 9.4 us
  starting transfers between devices: 16.6 us -> 17.5 us
    ppermute x16 -> x17, waiting for transfers between devices: 11 us -> 9.4 us  [send(): return lax.ppermute(value, axis, [(p, target(p)) for p in range(count)])]
    ppermute x16 -> x17, starting transfers between devices: 16.6 us -> 17.5 us  [send(): return lax.ppermute(value, axis, [(p, target(p)) for p in range(count)])]
    pallas_call x14 -> x15, Pallas kernels: 21.6 us -> 21.6 us  [run(): pl.pallas_call(body, out_shape=[jax.ShapeDtypeStruct(shape, kind) for sha...]
  transfers between devices with their start and end apart: 16 -> 17, of which waited for: 9 -> 6; matrix products, arithmetic and copies ran while one was open for 0% -> 0% of each run, Pallas kernels for 33% -> 33%
where the time goes in v21:
time: 53.6 us; the launch traced here: 53.3 us
  Pallas kernels  21.6 us (40%)
  starting transfers between devices  17.5 us (33%)
  waiting for transfers between devices  9.4 us (18%)
  local copies, waits for them, and re-layouts  2.72 us (5%)
  between operations  2.07 us (4%)
    pallas_call x15, Pallas kernels, run(): pl.pallas_call(body, out_shape=[jax.ShapeDtypeStruct(shape, kind) for sha...  21.6 us
    ppermute x17, starting transfers between devices, send(): return lax.ppermute(value, axis, [(p, target(p)) for p in range(count)])  17.5 us
    ppermute x17, waiting for transfers between devices, send(): return lax.ppermute(value, axis, [(p, target(p)) for p in range(count)])  9.4 us
    unnamed x6, local copies, waits for them, and re-layouts  2.72 us
  transfers between devices with their start and end apart: 17, of which 6 were waited for; matrix products, arithmetic and copies ran while one was open for 0% of the time, Pallas kernels for 33%

profile of v21, /device:TPU:0, one launch (start us, length us, event | category | flops | bytes accessed | tf_op | source)
XLA Modules:
  0.0 53.3 jit_solution(11910858566699244094)
XLA Ops:
  0.6 0.5 collective-permute-start
  1.2 2.6 %collective-permute-start.3 = (bf16[192,1152]{1,0:T(8,128)(2,1)}, bf16[192,1152]{1,0:T(8,128)(2,1)S(1)}, u32[]{:S(2)}, u32[]{:S(2)}) collective-permute-start(bf16[192,1152]{1,0:T(8,128)(2,1)} %bitcast.6), channel_id=1, source_target_pairs={{0,16},{8,24},{16,0},{24,8},{1,17},{9,25},{17,1},{25,9},{2,18},{10... | collective-permute-start | bytes 1327112 | tf_op jit(solution)/shard_map/ppermute | solution.py:34
  5.0 0.0 collective-permute-done.f1
  5.0 0.0 copy-start
  5.0 1.0 %copy-done = bf16[192,1,1152]{2,0,1:T(8,128)(2,1)S(1)} copy-done((bf16[192,1,1152]{2,0,1:T(8,128)(2,1)S(1)}, bf16[192,1,1152]{2,0,1:T(8,128)(2,1)}, u32[]{:S(2)}) %copy-start) | copy-done | bytes 442392
  6.0 1.0 %copy-done.1 = bf16[192,1,1152]{2,0,1:T(8,128)(2,1)S(1)} copy-done((bf16[192,1,1152]{2,0,1:T(8,128)(2,1)S(1)}, bf16[192,1,1152]{2,0,1:T(8,128)(2,1)}, u32[]{:S(2)}) %copy-start.1) | copy-done | bytes 442392
  7.1 0.7 %copy-done.2 = f32[1152]{0:T(1024)S(1)} copy-done((f32[1152]{0:T(1024)S(1)}, f32[1152]{0:T(1024)}, u32[]{:S(2)}) %copy-start.2) | copy-done | bytes 4632
  7.7 4.2 %shard_map.93 = (bf16[192,1152]{1,0:T(8,128)(2,1)S(1)}, bf16[1152,1152]{1,0:T(8,128)(2,1)S(1)}, bf16[192,1152]{1,0:T(8,128)(2,1)S(1)}, f32[1,1152]{1,0:T(1,128)S...) custom-call(f32[1]{0:T(128)S(6)} %copy.10.scale, ...), custom_call_target="tpu_custom_call" | custom-call | flops 1019215872 | bytes 3538944 | tf_op jit(solution)/shard_map/pallas_call | solution.py:138
  12.0 0.2 collective-permute-start.1
  12.2 0.6 %collective-permute-start.2 = (bf16[192,1152]{1,0:T(8,128)(2,1)S(1)}, bf16[192,1152]{1,0:T(8,128)(2,1)S(1)}, u32[]{:S(2)}, u32[]{:S(2)}) collective-permute-start(bf16[192,1152]{1,0:T(8,128)(2,1)S(1)} %get-tuple-element.60.text_own), channel_id=1, source_target_pairs={{0,16},{8,24},{16,0},{24,8},{1,17},{9,25},{17,1},{25,9},{2,18},{10... | collective-permute-start | bytes 1327112 | tf_op jit(solution)/shard_map/ppermute | solution.py:34
  12.8 1.9 %collective-permute-done.3.f2 = bf16[192,1152]{1,0:T(8,128)(2,1)S(1)} collective-permute-done((bf16[192,1152]{1,0:T(8,128)(2,1)}, bf16[192,1152]{1,0:T(8,128)(2,1)S(1)}, u32[]{:S(2)}, u32[]{:S(2)}) %collective-permute-start.3) | collective-permute-done | bytes 442400 | tf_op jit(solution)/shard_map/ppermute | solution.py:34
  14.7 0.1 collective-permute-start.4
  14.8 0.5 collective-permute-start.5
  15.3 0.0 collective-permute-done.1.t1
  15.3 1.7 %shard_map.94 = (bf16[384,1152]{1,0:T(8,128)(2,1)S(1)}, bf16[1152,384]{1,0:T(8,128)(2,1)S(1)}, bf16[1152,384]{1,0:T(8,128)(2,1)S(1)}, bf16[288,384]{1,0:T(8,128)...) custom-call(f32[1]{0:T(128)S(6)} %copy.10.scale, ...), custom_call_target="tpu_custom_call" | custom-call | flops 1000 | bytes 1000 | tf_op jit(solution)/shard_map/pallas_call | solution.py:138
  17.0 0.0 collective-permute-done.5.f3_tail
  17.0 0.0 collective-permute-done.4.f3_head
  17.0 4.6 %shard_map.96 = (bf16[1152,384]{1,0:T(8,128)(2,1)S(1)}, bf16[384,1152]{1,0:T(8,128)(2,1)S(1)}, bf16[1152,384]{1,0:T(8,128)(2,1)S(1)}, bf16[288,384]{1,0:T(8,128)...) custom-call(f32[1]{0:T(128)S(6)} %copy.10.scale, ...), custom_call_target="tpu_custom_call" | custom-call | flops 1000 | bytes 1000 | tf_op jit(solution)/shard_map/pallas_call | solution.py:138
  21.7 2.0 %shard_map.97 = (bf16[192,1152]{1,0:T(8,128)(2,1)}, f32[8,128]{1,0:T(8,128)S(1)}) custom-call(f32[1]{0:T(128)S(6)} %copy.10.scale, bf16[192,1152]{1,0:T(8,128)(2,1)S(1)} %get-tuple-element.63.text, bf16[384,384]{1,0:T(8,128)(2,1)S(1)} %get-tuple-element.64.weights_near, bf16[384,384]{1,0:T(8,128)(2,1)S(1)} %get-tuple-element.68.weights_far, ...), custom_call_target="tpu_custom_call" | custom-call | flops 1000 | bytes 1000 | tf_op jit(solution)/shard_map/pallas_call | solution.py:138
  23.7 0.9 %collective-permute-done.2.text_unit.text_third = bf16[192,1152]{1,0:T(8,128)(2,1)S(1)} collective-permute-done((bf16[192,1152]{1,0:T(8,128)(2,1)S(1)}, bf16[192,1152]{1,0:T(8,128)(2,1)S(1)}, u32[]{:S(2)}, u32[]{:S(2)}) %collective-permute-start.2) | collective-permute-done | bytes 442400 | tf_op jit(solution)/shard_map/ppermute | solution.py:34
  24.6 0.0 collective-permute-start.6
  24.6 1.3 %shard_map.98 = (bf16[192,768]{1,0:T(8,128)(2,1)S(1)}, f32[288,384]{1,0:T(8,128)S(1)}, f32[288,384]{1,0:T(8,128)S(1)}, f32[1,768]{1,0:T(1,128)S(1)}) custom-call(f32[1]{0:T(128)S(6)} %copy.10.scale, f32[1]{0:T(128)S(6)} %copy.11.bias, bf16[192,1152]{1,0:T(8,128)(2,1)S(1)} %collective-permute-done.2.text_unit.text_third, ...), custom_call_target="tpu_custom_call" | custom-call | flops 1019215872 | bytes 3538944 | tf_op jit(solution)/shard_map/pallas_call | solution.py:138
  26.0 0.5 collective-permute-done.6.text_unit.text_fourth
  26.4 2.7 %shard_map.99 = (bf16[176,256]{1,0:T(8,128)(2,1)S(1)}, bf16[176,256]{1,0:T(8,128)(2,1)S(1)}, bf16[176,256]{1,0:T(8,128)(2,1)S(1)}, bf16[176,256]{1,0:T(8,128)(2,...) custom-call(f32[1]{0:T(128)S(6)} %copy.10.scale, f32[1]{0:T(128)S(6)} %copy.11.bias, ...), custom_call_target="tpu_custom_call" | custom-call | flops 2038431744 | bytes 7077888 | tf_op jit(solution)/shard_map/pallas_call | solution.py:138
  29.2 1.6 %collective-permute-start.7 = (bf16[176,256]{1,0:T(8,128)(2,1)S(1)}, bf16[176,256]{1,0:T(8,128)(2,1)S(1)}, u32[]{:S(2)}, u32[]{:S(2)}) collective-permute-start(bf16[176,256]{1,0:T(8,128)(2,1)S(1)} %get-tuple-element.93), channel_id=1, source_target_pairs={{0,1},{1,0},{2,3},{3,2},{4,5},{5,4},{6,7},{7,6},{8,9},{9,8},{10,11... | collective-permute-start | bytes 270344 | tf_op jit(solution)/shard_map/ppermute | solution.py:34
  30.7 0.5 collective-permute-start.8
  31.2 1.5 %collective-permute-start.9 = (bf16[176,256]{1,0:T(8,128)(2,1)S(1)}, bf16[176,256]{1,0:T(8,128)(2,1)S(1)}, u32[]{:S(2)}, u32[]{:S(2)}) collective-permute-start(bf16[176,256]{1,0:T(8,128)(2,1)S(1)} %get-tuple-element.95), channel_id=1, source_target_pairs={{0,1},{1,0},{2,3},{3,2},{4,5},{5,4},{6,7},{7,6},{8,9},{9,8},{10,11... | collective-permute-start | bytes 270344 | tf_op jit(solution)/shard_map/ppermute | solution.py:34
  32.8 1.9 %collective-permute-done.7.come = bf16[176,256]{1,0:T(8,128)(2,1)S(1)} collective-permute-done((bf16[176,256]{1,0:T(8,128)(2,1)S(1)}, bf16[176,256]{1,0:T(8,128)(2,1)S(1)}, u32[]{:S(2)}, u32[]{:S(2)}) %collective-permute-start.7) | collective-permute-done | bytes 90144 | tf_op jit(solution)/shard_map/ppermute | solution.py:34
  34.7 3.7 %collective-permute-start.11 = (bf16[176,256]{1,0:T(8,128)(2,1)S(1)}, bf16[176,256]{1,0:T(8,128)(2,1)S(1)}, u32[]{:S(2)}, u32[]{:S(2)}) collective-permute-start(bf16[176,256]{1,0:T(8,128)(2,1)S(1)} %shard_map.100.before), channel_id=1, source_target_pairs={{0,6},{1,7},{2,4},{3,5},{4,2},{5,3},{6,0},{7,1},{8,14},{9,15},{10,... | collective-permute-start | bytes 270344 | tf_op jit(solution)/shard_map/ppermute | solution.py:34
  38.4 0.0 collective-permute-done.8.come
  38.4 0.9 %collective-permute-start.10 = (bf16[176,256]{1,0:T(8,128)(2,1)S(1)}, bf16[176,256]{1,0:T(8,128)(2,1)S(1)}, u32[]{:S(2)}, u32[]{:S(2)}) collective-permute-start(bf16[176,256]{1,0:T(8,128)(2,1)S(1)} %shard_map.101.before), channel_id=1, source_target_pairs={{0,4},{1,5},{2,6},{3,7},{4,0},{5,1},{6,2},{7,3},{8,12},{9,13},{10,... | collective-permute-start | bytes 270344 | tf_op jit(solution)/shard_map/ppermute | solution.py:34
  39.3 1.6 %collective-permute-start.12 = (bf16[176,256]{1,0:T(8,128)(2,1)S(1)}, bf16[176,256]{1,0:T(8,128)(2,1)S(1)}, u32[]{:S(2)}, u32[]{:S(2)}) collective-permute-start(bf16[176,256]{1,0:T(8,128)(2,1)S(1)} %get-tuple-element.101), channel_id=1, source_target_pairs={{0,1},{1,0},{2,3},{3,2},{4,5},{5,4},{6,7},{7,6},{8,9},{9,8},{10,11... | collective-permute-start | bytes 270344 | tf_op jit(solution)/shard_map/ppermute | solution.py:34
  40.8 0.0 collective-permute-done.9.come
  40.8 1.6 %collective-permute-start.13 = (bf16[176,256]{1,0:T(8,128)(2,1)S(1)}, bf16[176,256]{1,0:T(8,128)(2,1)S(1)}, u32[]{:S(2)}, u32[]{:S(2)}) collective-permute-start(bf16[176,256]{1,0:T(8,128)(2,1)S(1)} %shard_map.102.before), channel_id=1, source_target_pairs={{0,2},{1,3},{2,0},{3,1},{4,6},{5,7},{6,4},{7,5},{8,10},{9,11},{10,... | collective-permute-start | bytes 270344 | tf_op jit(solution)/shard_map/ppermute | solution.py:34
  42.5 2.1 %shard_map.103 = (f32[192,1152]{1,0:T(8,128)S(1)}, f32[8,128]{1,0:T(8,128)S(1)}) custom-call(f32[1]{0:T(128)S(6)} %copy.10.scale, bf16[1152,1152]{1,0:T(8,128)(2,1)S(1)} %get-tuple-element.56.proj, bf16[384,1152]{1,0:T(8,128)(2,1)S(1)} %get-tuple-element.62.text_near, bf16[192,1152]{1,0:T(8,128)(2,1)S(1)} %collective-permute-done.2.text_unit.text_third, ...), custom_call_target="tpu_custom_call" | custom-call | flops 1000 | bytes 1000 | tf_op jit(solution)/shard_map/pallas_call | solution.py:138
  44.6 1.7 %shard_map.104 = (bf16[192,1152]{1,0:T(8,128)(2,1)}, f32[8,128]{1,0:T(8,128)S(1)}) custom-call(bf16[192,1152]{1,0:T(8,128)(2,1)S(1)} %get-tuple-element.54.features, f32[1,1152]{1,0:T(1,128)S(1)} %get-tuple-element.55.gain, f32[192,1152]{1,0:T(8,128)S(1)} %get-tuple-element.96.norm_back, f32[8,128]{1,0:T(8,128)S(1)} %get-tuple-element.97.before), custom_call_target="tpu_custom_call" | custom-call | bytes 1000 | tf_op jit(solution)/shard_map/pallas_call | solution.py:138
  46.3 0.0 collective-permute-done.11.three_on
  46.3 0.0 collective-permute-done.10.two_on
  46.4 0.0 collective-permute-done.12.come
  46.4 0.0 collective-permute-done.13.next_one
  46.4 0.1 shard_map.106.refs_0_
  46.5 1.7 %collective-permute-start.15 = (bf16[176,256]{1,0:T(8,128)(2,1)S(1)}, bf16[176,256]{1,0:T(8,128)(2,1)S(1)}, u32[]{:S(2)}, u32[]{:S(2)}) collective-permute-start(bf16[176,256]{1,0:T(8,128)(2,1)S(1)} %shard_map.106.refs_0_), channel_id=1, source_target_pairs={{0,16},{8,24},{16,0},{24,8},{1,17},{9,25},{17,1},{25,9},{2,18},{10... | collective-permute-start | bytes 270344 | tf_op jit(solution)/shard_map/ppermute | solution.py:34
  48.1 0.0 collective-permute-start.14
  48.1 2.9 %collective-permute-done.15.refs_2_ = bf16[176,256]{1,0:T(8,128)(2,1)S(1)} collective-permute-done((bf16[176,256]{1,0:T(8,128)(2,1)S(1)}, bf16[176,256]{1,0:T(8,128)(2,1)S(1)}, u32[]{:S(2)}, u32[]{:S(2)}) %collective-permute-start.15) | collective-permute-done | bytes 90144 | tf_op jit(solution)/shard_map/ppermute | solution.py:34
  51.1 0.0 collective-permute-start.16
  51.1 0.0 collective-permute-done.14.refs_1_
  51.1 1.3 %collective-permute-done.16.refs_3_ = bf16[176,256]{1,0:T(8,128)(2,1)S(1)} collective-permute-done((bf16[176,256]{1,0:T(8,128)(2,1)S(1)}, bf16[176,256]{1,0:T(8,128)(2,1)S(1)}, u32[]{:S(2)}, u32[]{:S(2)}) %collective-permute-start.16) | collective-permute-done | bytes 90144 | tf_op jit(solution)/shard_map/ppermute | solution.py:34
  52.3 1.0 %shard_map.107 = (f32[144,1152]{1,0:T(8,128)}, f32[1152]{0:T(1024)}) custom-call(bf16[176,256]{1,0:T(8,128)(2,1)S(1)} %shard_map.106.refs_0_, bf16[176,256]{1,0:T(8,128)(2,1)S(1)} %collective-permute-done.14.refs_1_, bf16[176,256]{1,0:T(8,128)(2,1)S(1)} %collective-permute-done.15.refs_2_, bf16[176,256]{1,0:T(8,128)(2,1)S(1)} %collective-permute-done.16.refs_3_), custom_call_target="tpu_custom_call" | custom-call | bytes 1327104 | tf_op jit(solution)/shard_map/pallas_call | solution.py:138
  (7 shorter events, 0.1 us)
Async XLA Ops:
  0.6 4.4 %collective-permute-start = (bf16[192,1152]{1,0:T(8,128)(2,1)}, bf16[192,1152]{1,0:T(8,128)(2,1)S(1)}, u32[]{:S(2)}, u32[]{:S(2)}) collective-permute-start(bf16[192,1152]{1,0:T(8,128)(2,1)} %bitcast.5), channel_id=1, source_target_pairs={{0,8},{8,0},{16,24},{24,16},{1,9},{9,1},{17,25},{25,17},{2,10},{10... | collective-permute-start | bytes 1327112 | tf_op jit(solution)/shard_map/ppermute | solution.py:34
  1.2 13.5 %collective-permute-start.3 = (bf16[192,1152]{1,0:T(8,128)(2,1)}, bf16[192,1152]{1,0:T(8,128)(2,1)S(1)}, u32[]{:S(2)}, u32[]{:S(2)}) collective-permute-start(bf16[192,1152]{1,0:T(8,128)(2,1)} %bitcast.6), channel_id=1, source_target_pairs={{0,16},{8,24},{16,0},{24,8},{1,17},{9,25},{17,1},{25,9},{2,18},{10... | collective-permute-start | bytes 1327112 | tf_op jit(solution)/shard_map/ppermute | solution.py:34
  5.0 1.0 %copy-start = (bf16[192,1,1152]{2,0,1:T(8,128)(2,1)S(1)}, bf16[192,1,1152]{2,0,1:T(8,128)(2,1)}, u32[]{:S(2)}) copy-start(bf16[192,1,1152]{2,0,1:T(8,128)(2,1)} %param.7) | copy-start | bytes 1327108
  6.0 1.0 %copy-start.1 = (bf16[192,1,1152]{2,0,1:T(8,128)(2,1)S(1)}, bf16[192,1,1152]{2,0,1:T(8,128)(2,1)}, u32[]{:S(2)}) copy-start(bf16[192,1,1152]{2,0,1:T(8,128)(2,1)} %param.6) | copy-start | bytes 1327108
  7.1 0.7 %copy-start.2 = (f32[1152]{0:T(1024)S(1)}, f32[1152]{0:T(1024)}, u32[]{:S(2)}) copy-start(f32[1152]{0:T(1024)} %gain_line.1) | copy-start | bytes 13828
  12.0 3.3 %collective-permute-start.1 = (bf16[192,1152]{1,0:T(8,128)(2,1)S(1)}, bf16[192,1152]{1,0:T(8,128)(2,1)S(1)}, u32[]{:S(2)}, u32[]{:S(2)}) collective-permute-start(bf16[192,1152]{1,0:T(8,128)(2,1)S(1)} %get-tuple-element.60.text_own), channel_id=1, source_target_pairs={{0,8},{8,0},{16,24},{24,16},{1,9},{9,1},{17,25},{25,17},{2,10},{10... | collective-permute-start | bytes 1327112 | tf_op jit(solution)/shard_map/ppermute | solution.py:34
  12.2 12.4 %collective-permute-start.2 = (bf16[192,1152]{1,0:T(8,128)(2,1)S(1)}, bf16[192,1152]{1,0:T(8,128)(2,1)S(1)}, u32[]{:S(2)}, u32[]{:S(2)}) collective-permute-start(bf16[192,1152]{1,0:T(8,128)(2,1)S(1)} %get-tuple-element.60.text_own), channel_id=1, source_target_pairs={{0,16},{8,24},{16,0},{24,8},{1,17},{9,25},{17,1},{25,9},{2,18},{10... | collective-permute-start | bytes 1327112 | tf_op jit(solution)/shard_map/ppermute | solution.py:34
  14.7 2.3 %collective-permute-start.4 = (bf16[160,1152]{1,0:T(8,128)(2,1)S(1)}, bf16[160,1152]{1,0:T(8,128)(2,1)S(1)}, u32[]{:S(2)}, u32[]{:S(2)}) collective-permute-start(bf16[160,1152]{1,0:T(8,128)(2,1)S(1)} %get-tuple-element.65), channel_id=1, source_target_pairs={{0,8},{8,0},{16,24},{24,16},{1,9},{9,1},{17,25},{25,17},{2,10},{10... | collective-permute-start | bytes 1105928 | tf_op jit(solution)/shard_map/ppermute | solution.py:34
  14.8 2.2 %collective-permute-start.5 = (bf16[32,1152]{1,0:T(8,128)(2,1)S(1)}, bf16[32,1152]{1,0:T(8,128)(2,1)S(1)}, u32[]{:S(2)}, u32[]{:S(2)}) collective-permute-start(bf16[32,1152]{1,0:T(8,128)(2,1)S(1)} %get-tuple-element.66), channel_id=1, source_target_pairs={{0,8},{8,0},{16,24},{24,16},{1,9},{9,1},{17,25},{25,17},{2,10},{10... | collective-permute-start | bytes 221192 | tf_op jit(solution)/shard_map/ppermute | solution.py:34
  24.6 1.8 %collective-permute-start.6 = (bf16[192,1152]{1,0:T(8,128)(2,1)S(1)}, bf16[192,1152]{1,0:T(8,128)(2,1)S(1)}, u32[]{:S(2)}, u32[]{:S(2)}) collective-permute-start(bf16[192,1152]{1,0:T(8,128)(2,1)S(1)} %collective-permute-done.2.text_unit.text_third), channel_id=1, source_target_pairs={{0,8},{8,0},{16,24},{24,16},{1,9},{9,1},{17,25},{25,17},{2,10},{10... | collective-permute-start | bytes 1327112 | tf_op jit(solution)/shard_map/ppermute | solution.py:34
  29.2 5.5 %collective-permute-start.7 = (bf16[176,256]{1,0:T(8,128)(2,1)S(1)}, bf16[176,256]{1,0:T(8,128)(2,1)S(1)}, u32[]{:S(2)}, u32[]{:S(2)}) collective-permute-start(bf16[176,256]{1,0:T(8,128)(2,1)S(1)} %get-tuple-element.93), channel_id=1, source_target_pairs={{0,1},{1,0},{2,3},{3,2},{4,5},{5,4},{6,7},{7,6},{8,9},{9,8},{10,11... | collective-permute-start | bytes 270344 | tf_op jit(solution)/shard_map/ppermute | solution.py:34
  30.7 7.6 %collective-permute-start.8 = (bf16[176,256]{1,0:T(8,128)(2,1)S(1)}, bf16[176,256]{1,0:T(8,128)(2,1)S(1)}, u32[]{:S(2)}, u32[]{:S(2)}) collective-permute-start(bf16[176,256]{1,0:T(8,128)(2,1)S(1)} %get-tuple-element.94), channel_id=1, source_target_pairs={{0,1},{1,0},{2,3},{3,2},{4,5},{5,4},{6,7},{7,6},{8,9},{9,8},{10,11... | collective-permute-start | bytes 270344 | tf_op jit(solution)/shard_map/ppermute | solution.py:34
  31.2 9.6 %collective-permute-start.9 = (bf16[176,256]{1,0:T(8,128)(2,1)S(1)}, bf16[176,256]{1,0:T(8,128)(2,1)S(1)}, u32[]{:S(2)}, u32[]{:S(2)}) collective-permute-start(bf16[176,256]{1,0:T(8,128)(2,1)S(1)} %get-tuple-element.95), channel_id=1, source_target_pairs={{0,1},{1,0},{2,3},{3,2},{4,5},{5,4},{6,7},{7,6},{8,9},{9,8},{10,11... | collective-permute-start | bytes 270344 | tf_op jit(solution)/shard_map/ppermute | solution.py:34
  34.7 11.6 %collective-permute-start.11 = (bf16[176,256]{1,0:T(8,128)(2,1)S(1)}, bf16[176,256]{1,0:T(8,128)(2,1)S(1)}, u32[]{:S(2)}, u32[]{:S(2)}) collective-permute-start(bf16[176,256]{1,0:T(8,128)(2,1)S(1)} %shard_map.100.before), channel_id=1, source_target_pairs={{0,6},{1,7},{2,4},{3,5},{4,2},{5,3},{6,0},{7,1},{8,14},{9,15},{10,... | collective-permute-start | bytes 270344 | tf_op jit(solution)/shard_map/ppermute | solution.py:34
  38.4 7.9 %collective-permute-start.10 = (bf16[176,256]{1,0:T(8,128)(2,1)S(1)}, bf16[176,256]{1,0:T(8,128)(2,1)S(1)}, u32[]{:S(2)}, u32[]{:S(2)}) collective-permute-start(bf16[176,256]{1,0:T(8,128)(2,1)S(1)} %shard_map.101.before), channel_id=1, source_target_pairs={{0,4},{1,5},{2,6},{3,7},{4,0},{5,1},{6,2},{7,3},{8,12},{9,13},{10,... | collective-permute-start | bytes 270344 | tf_op jit(solution)/shard_map/ppermute | solution.py:34
  39.3 7.1 %collective-permute-start.12 = (bf16[176,256]{1,0:T(8,128)(2,1)S(1)}, bf16[176,256]{1,0:T(8,128)(2,1)S(1)}, u32[]{:S(2)}, u32[]{:S(2)}) collective-permute-start(bf16[176,256]{1,0:T(8,128)(2,1)S(1)} %get-tuple-element.101), channel_id=1, source_target_pairs={{0,1},{1,0},{2,3},{3,2},{4,5},{5,4},{6,7},{7,6},{8,9},{9,8},{10,11... | collective-permute-start | bytes 270344 | tf_op jit(solution)/shard_map/ppermute | solution.py:34
  40.8 5.5 %collective-permute-start.13 = (bf16[176,256]{1,0:T(8,128)(2,1)S(1)}, bf16[176,256]{1,0:T(8,128)(2,1)S(1)}, u32[]{:S(2)}, u32[]{:S(2)}) collective-permute-start(bf16[176,256]{1,0:T(8,128)(2,1)S(1)} %shard_map.102.before), channel_id=1, source_target_pairs={{0,2},{1,3},{2,0},{3,1},{4,6},{5,7},{6,4},{7,5},{8,10},{9,11},{10,... | collective-permute-start | bytes 270344 | tf_op jit(solution)/shard_map/ppermute | solution.py:34
  46.5 4.6 %collective-permute-start.15 = (bf16[176,256]{1,0:T(8,128)(2,1)S(1)}, bf16[176,256]{1,0:T(8,128)(2,1)S(1)}, u32[]{:S(2)}, u32[]{:S(2)}) collective-permute-start(bf16[176,256]{1,0:T(8,128)(2,1)S(1)} %shard_map.106.refs_0_), channel_id=1, source_target_pairs={{0,16},{8,24},{16,0},{24,8},{1,17},{9,25},{17,1},{25,9},{2,18},{10... | collective-permute-start | bytes 270344 | tf_op jit(solution)/shard_map/ppermute | solution.py:34
  48.1 2.9 %collective-permute-start.14 = (bf16[176,256]{1,0:T(8,128)(2,1)S(1)}, bf16[176,256]{1,0:T(8,128)(2,1)S(1)}, u32[]{:S(2)}, u32[]{:S(2)}) collective-permute-start(bf16[176,256]{1,0:T(8,128)(2,1)S(1)} %shard_map.106.refs_0_), channel_id=1, source_target_pairs={{0,8},{8,0},{16,24},{24,16},{1,9},{9,1},{17,25},{25,17},{2,10},{10... | collective-permute-start | bytes 270344 | tf_op jit(solution)/shard_map/ppermute | solution.py:34
  51.1 1.3 %collective-permute-start.16 = (bf16[176,256]{1,0:T(8,128)(2,1)S(1)}, bf16[176,256]{1,0:T(8,128)(2,1)S(1)}, u32[]{:S(2)}, u32[]{:S(2)}) collective-permute-start(bf16[176,256]{1,0:T(8,128)(2,1)S(1)} %collective-permute-done.15.refs_2_), channel_id=1, source_target_pairs={{0,8},{8,0},{16,24},{24,16},{1,9},{9,1},{17,25},{25,17},{2,10},{10... | collective-permute-start | bytes 270344 | tf_op jit(solution)/shard_map/ppermute | solution.py:34

commit v22 on v21

--- a/solution.py
+++ b/solution.py
@@ -468,7 +468,7 @@
     total[count - BAND :, full - LANES :] = value.astype(BF16)
 
 
-def finish_body(members, *refs):
+def finish_body(members, before, *refs):
     packets, (proj_grad, gain_gradient, ordered) = refs[:members], refs[members:]
     count, full = packets[0].shape
     rows, width = proj_grad.shape
@@ -621,13 +621,16 @@
         scale, proj_kept, text_near, t2, t3, weights_near, weights_third, weights_fourth,
         unit_near, factors, next_sum,
     )
-    feature_grad, token = call(feature_body, [half, TOKEN], moved=1000)(f0_kept, gain_row, norm_back, token)
     (far_sum,) = call(far_sum_body, [(packet, F32)], moved=1000)(token, two_on, three_on)
     (reduced,) = call(last_sum_body, [(packet, BF16)], [((4, BAND, LANES), F32), (packet, BF16)], moved=1000)(
         far_sum, keep, come_own, next_one, two_on, three_on
     )
     far_block = send(reduced, "loop", lambda p: p ^ 2)
     near_block = send(reduced, "loop", lambda p: p ^ 1)
+    feature_grad, token = call(feature_body, [half, TOKEN], moved=12 * near * width)(
+        f0_kept, gain_row, norm_back, reduced
+    )
+    far_block, token = lax.optimization_barrier((far_block, token))
     blocks = [reduced, near_block, far_block, send(far_block, "loop", lambda p: p ^ 1)]
 
     proj_grad, gain_gradient = call(
@@ -635,7 +638,7 @@
         [((each, width), F32), ((width,), F32)],
         [((members, bands * BAND, full), F32)],
         moved=8 * each * width,
-    )(*blocks)
+    )(token, *blocks)
     return feature_grad[:, None, :], text_grad[:, None, :], proj_grad, gain_gradient
 
 

time: 53.6 us -> 53.3 us (level)
  transfers between devices with their start and end apart: 17 -> 17, of which waited for: 6 -> 8; matrix products, arithmetic and copies ran while one was open for 0% -> 0% of each run, Pallas kernels for 33% -> 34%
where the time goes in v22:
time: 53.3 us; the launch traced here: 53 us
  Pallas kernels  21.6 us (41%)
  starting transfers between devices  17.4 us (33%)
  waiting for transfers between devices  9.22 us (17%)
  local copies, waits for them, and re-layouts  2.72 us (5%)
  between operations  2.07 us (4%)
    pallas_call x15, Pallas kernels, run(): pl.pallas_call(body, out_shape=[jax.ShapeDtypeStruct(shape, kind) for sha...  21.6 us
    ppermute x17, starting transfers between devices, send(): return lax.ppermute(value, axis, [(p, target(p)) for p in range(count)])  17.4 us
    ppermute x17, waiting for transfers between devices, send(): return lax.ppermute(value, axis, [(p, target(p)) for p in range(count)])  9.22 us
    unnamed x6, local copies, waits for them, and re-layouts  2.72 us
  transfers between devices with their start and end apart: 17, of which 8 were waited for; matrix products, arithmetic and copies ran while one was open for 0% of the time, Pallas kernels for 34%

profile of v22, /device:TPU:0, one launch (start us, length us, event | category | flops | bytes accessed | tf_op | source)
XLA Modules:
  0.0 53.0 jit_solution(12945339415843701880)
XLA Ops:
  0.6 0.5 collective-permute-start
  1.2 2.6 %collective-permute-start.3 = (bf16[192,1152]{1,0:T(8,128)(2,1)}, bf16[192,1152]{1,0:T(8,128)(2,1)S(1)}, u32[]{:S(2)}, u32[]{:S(2)}) collective-permute-start(bf16[192,1152]{1,0:T(8,128)(2,1)} %bitcast.6), channel_id=1, source_target_pairs={{0,16},{8,24},{16,0},{24,8},{1,17},{9,25},{17,1},{25,9},{2,18},{10... | collective-permute-start | bytes 1327112 | tf_op jit(solution)/shard_map/ppermute | solution.py:34
  5.0 0.0 collective-permute-done.f1
  5.0 0.0 copy-start
  5.0 1.0 %copy-done = bf16[192,1,1152]{2,0,1:T(8,128)(2,1)S(1)} copy-done((bf16[192,1,1152]{2,0,1:T(8,128)(2,1)S(1)}, bf16[192,1,1152]{2,0,1:T(8,128)(2,1)}, u32[]{:S(2)}) %copy-start) | copy-done | bytes 442392
  6.0 1.0 %copy-done.1 = bf16[192,1,1152]{2,0,1:T(8,128)(2,1)S(1)} copy-done((bf16[192,1,1152]{2,0,1:T(8,128)(2,1)S(1)}, bf16[192,1,1152]{2,0,1:T(8,128)(2,1)}, u32[]{:S(2)}) %copy-start.1) | copy-done | bytes 442392
  7.1 0.7 %copy-done.2 = f32[1152]{0:T(1024)S(1)} copy-done((f32[1152]{0:T(1024)S(1)}, f32[1152]{0:T(1024)}, u32[]{:S(2)}) %copy-start.2) | copy-done | bytes 4632
  7.7 4.2 %shard_map.93 = (bf16[192,1152]{1,0:T(8,128)(2,1)S(1)}, bf16[1152,1152]{1,0:T(8,128)(2,1)S(1)}, bf16[192,1152]{1,0:T(8,128)(2,1)S(1)}, f32[1,1152]{1,0:T(1,128)S...) custom-call(f32[1]{0:T(128)S(6)} %copy.10.scale, ...), custom_call_target="tpu_custom_call" | custom-call | flops 1019215872 | bytes 3538944 | tf_op jit(solution)/shard_map/pallas_call | solution.py:138
  12.0 0.2 collective-permute-start.1
  12.2 0.6 %collective-permute-start.2 = (bf16[192,1152]{1,0:T(8,128)(2,1)S(1)}, bf16[192,1152]{1,0:T(8,128)(2,1)S(1)}, u32[]{:S(2)}, u32[]{:S(2)}) collective-permute-start(bf16[192,1152]{1,0:T(8,128)(2,1)S(1)} %get-tuple-element.62.text_own), channel_id=1, source_target_pairs={{0,16},{8,24},{16,0},{24,8},{1,17},{9,25},{17,1},{25,9},{2,18},{10... | collective-permute-start | bytes 1327112 | tf_op jit(solution)/shard_map/ppermute | solution.py:34
  12.8 1.9 %collective-permute-done.3.f2 = bf16[192,1152]{1,0:T(8,128)(2,1)S(1)} collective-permute-done((bf16[192,1152]{1,0:T(8,128)(2,1)}, bf16[192,1152]{1,0:T(8,128)(2,1)S(1)}, u32[]{:S(2)}, u32[]{:S(2)}) %collective-permute-start.3) | collective-permute-done | bytes 442400 | tf_op jit(solution)/shard_map/ppermute | solution.py:34
  14.7 0.1 collective-permute-start.4
  14.8 0.5 collective-permute-start.5
  15.3 0.0 collective-permute-done.1.t1
  15.3 1.7 %shard_map.94 = (bf16[384,1152]{1,0:T(8,128)(2,1)S(1)}, bf16[1152,384]{1,0:T(8,128)(2,1)S(1)}, bf16[1152,384]{1,0:T(8,128)(2,1)S(1)}, bf16[288,384]{1,0:T(8,128)...) custom-call(f32[1]{0:T(128)S(6)} %copy.10.scale, ...), custom_call_target="tpu_custom_call" | custom-call | flops 1000 | bytes 1000 | tf_op jit(solution)/shard_map/pallas_call | solution.py:138
  17.0 0.0 collective-permute-done.5.f3_tail
  17.0 0.0 collective-permute-done.4.f3_head
  17.0 4.6 %shard_map.96 = (bf16[1152,384]{1,0:T(8,128)(2,1)S(1)}, bf16[384,1152]{1,0:T(8,128)(2,1)S(1)}, bf16[1152,384]{1,0:T(8,128)(2,1)S(1)}, bf16[288,384]{1,0:T(8,128)...) custom-call(f32[1]{0:T(128)S(6)} %copy.10.scale, ...), custom_call_target="tpu_custom_call" | custom-call | flops 1000 | bytes 1000 | tf_op jit(solution)/shard_map/pallas_call | solution.py:138
  21.7 2.0 %shard_map.97 = (bf16[192,1152]{1,0:T(8,128)(2,1)}, f32[8,128]{1,0:T(8,128)S(1)}) custom-call(f32[1]{0:T(128)S(6)} %copy.10.scale, bf16[192,1152]{1,0:T(8,128)(2,1)S(1)} %get-tuple-element.65.text, bf16[384,384]{1,0:T(8,128)(2,1)S(1)} %get-tuple-element.66.weights_near, bf16[384,384]{1,0:T(8,128)(2,1)S(1)} %get-tuple-element.70.weights_far, ...), custom_call_target="tpu_custom_call" | custom-call | flops 1000 | bytes 1000 | tf_op jit(solution)/shard_map/pallas_call | solution.py:138
  23.7 0.9 %collective-permute-done.2.text_unit.text_third = bf16[192,1152]{1,0:T(8,128)(2,1)S(1)} collective-permute-done((bf16[192,1152]{1,0:T(8,128)(2,1)S(1)}, bf16[192,1152]{1,0:T(8,128)(2,1)S(1)}, u32[]{:S(2)}, u32[]{:S(2)}) %collective-permute-start.2) | collective-permute-done | bytes 442400 | tf_op jit(solution)/shard_map/ppermute | solution.py:34
  24.6 0.0 collective-permute-start.6
  24.6 1.3 %shard_map.98 = (bf16[192,768]{1,0:T(8,128)(2,1)S(1)}, f32[288,384]{1,0:T(8,128)S(1)}, f32[288,384]{1,0:T(8,128)S(1)}, f32[1,768]{1,0:T(1,128)S(1)}) custom-call(f32[1]{0:T(128)S(6)} %copy.10.scale, f32[1]{0:T(128)S(6)} %copy.11.bias, bf16[192,1152]{1,0:T(8,128)(2,1)S(1)} %collective-permute-done.2.text_unit.text_third, ...), custom_call_target="tpu_custom_call" | custom-call | flops 1019215872 | bytes 3538944 | tf_op jit(solution)/shard_map/pallas_call | solution.py:138
  26.0 0.5 collective-permute-done.6.text_unit.text_fourth
  26.4 2.7 %shard_map.99 = (bf16[176,256]{1,0:T(8,128)(2,1)S(1)}, bf16[176,256]{1,0:T(8,128)(2,1)S(1)}, bf16[176,256]{1,0:T(8,128)(2,1)S(1)}, bf16[176,256]{1,0:T(8,128)(2,...) custom-call(f32[1]{0:T(128)S(6)} %copy.10.scale, f32[1]{0:T(128)S(6)} %copy.11.bias, ...), custom_call_target="tpu_custom_call" | custom-call | flops 2038431744 | bytes 7077888 | tf_op jit(solution)/shard_map/pallas_call | solution.py:138
  29.1 1.6 %collective-permute-start.7 = (bf16[176,256]{1,0:T(8,128)(2,1)S(1)}, bf16[176,256]{1,0:T(8,128)(2,1)S(1)}, u32[]{:S(2)}, u32[]{:S(2)}) collective-permute-start(bf16[176,256]{1,0:T(8,128)(2,1)S(1)} %get-tuple-element.95), channel_id=1, source_target_pairs={{0,1},{1,0},{2,3},{3,2},{4,5},{5,4},{6,7},{7,6},{8,9},{9,8},{10,11... | collective-permute-start | bytes 270344 | tf_op jit(solution)/shard_map/ppermute | solution.py:34
  30.7 0.5 collective-permute-start.8
  31.2 1.5 %collective-permute-start.9 = (bf16[176,256]{1,0:T(8,128)(2,1)S(1)}, bf16[176,256]{1,0:T(8,128)(2,1)S(1)}, u32[]{:S(2)}, u32[]{:S(2)}) collective-permute-start(bf16[176,256]{1,0:T(8,128)(2,1)S(1)} %get-tuple-element.97), channel_id=1, source_target_pairs={{0,1},{1,0},{2,3},{3,2},{4,5},{5,4},{6,7},{7,6},{8,9},{9,8},{10,11... | collective-permute-start | bytes 270344 | tf_op jit(solution)/shard_map/ppermute | solution.py:34
  32.8 1.9 %collective-permute-done.7.come = bf16[176,256]{1,0:T(8,128)(2,1)S(1)} collective-permute-done((bf16[176,256]{1,0:T(8,128)(2,1)S(1)}, bf16[176,256]{1,0:T(8,128)(2,1)S(1)}, u32[]{:S(2)}, u32[]{:S(2)}) %collective-permute-start.7) | collective-permute-done | bytes 90144 | tf_op jit(solution)/shard_map/ppermute | solution.py:34
  34.7 3.7 %collective-permute-start.11 = (bf16[176,256]{1,0:T(8,128)(2,1)S(1)}, bf16[176,256]{1,0:T(8,128)(2,1)S(1)}, u32[]{:S(2)}, u32[]{:S(2)}) collective-permute-start(bf16[176,256]{1,0:T(8,128)(2,1)S(1)} %shard_map.100.before), channel_id=1, source_target_pairs={{0,6},{1,7},{2,4},{3,5},{4,2},{5,3},{6,0},{7,1},{8,14},{9,15},{10,... | collective-permute-start | bytes 270344 | tf_op jit(solution)/shard_map/ppermute | solution.py:34
  38.3 0.0 collective-permute-done.8.come
  38.4 0.9 %collective-permute-start.10 = (bf16[176,256]{1,0:T(8,128)(2,1)S(1)}, bf16[176,256]{1,0:T(8,128)(2,1)S(1)}, u32[]{:S(2)}, u32[]{:S(2)}) collective-permute-start(bf16[176,256]{1,0:T(8,128)(2,1)S(1)} %shard_map.101.before), channel_id=1, source_target_pairs={{0,4},{1,5},{2,6},{3,7},{4,0},{5,1},{6,2},{7,3},{8,12},{9,13},{10,... | collective-permute-start | bytes 270344 | tf_op jit(solution)/shard_map/ppermute | solution.py:34
  39.2 1.6 %collective-permute-start.12 = (bf16[176,256]{1,0:T(8,128)(2,1)S(1)}, bf16[176,256]{1,0:T(8,128)(2,1)S(1)}, u32[]{:S(2)}, u32[]{:S(2)}) collective-permute-start(bf16[176,256]{1,0:T(8,128)(2,1)S(1)} %get-tuple-element.100), channel_id=1, source_target_pairs={{0,1},{1,0},{2,3},{3,2},{4,5},{5,4},{6,7},{7,6},{8,9},{9,8},{10,11... | collective-permute-start | bytes 270344 | tf_op jit(solution)/shard_map/ppermute | solution.py:34
  40.8 0.0 collective-permute-done.9.come
  40.8 1.6 %collective-permute-start.13 = (bf16[176,256]{1,0:T(8,128)(2,1)S(1)}, bf16[176,256]{1,0:T(8,128)(2,1)S(1)}, u32[]{:S(2)}, u32[]{:S(2)}) collective-permute-start(bf16[176,256]{1,0:T(8,128)(2,1)S(1)} %shard_map.102.before), channel_id=1, source_target_pairs={{0,2},{1,3},{2,0},{3,1},{4,6},{5,7},{6,4},{7,5},{8,10},{9,11},{10,... | collective-permute-start | bytes 270344 | tf_op jit(solution)/shard_map/ppermute | solution.py:34
  42.5 2.1 %shard_map.103 = (f32[192,1152]{1,0:T(8,128)S(1)}, f32[8,128]{1,0:T(8,128)S(1)}) custom-call(f32[1]{0:T(128)S(6)} %copy.10.scale, bf16[1152,1152]{1,0:T(8,128)(2,1)S(1)} %get-tuple-element.58.proj, bf16[384,1152]{1,0:T(8,128)(2,1)S(1)} %get-tuple-element.64.text_near, bf16[192,1152]{1,0:T(8,128)(2,1)S(1)} %collective-permute-done.2.text_unit.text_third, ...), custom_call_target="tpu_custom_call" | custom-call | flops 1000 | bytes 1000 | tf_op jit(solution)/shard_map/pallas_call | solution.py:138
  44.6 0.0 collective-permute-done.11.three_on
  44.6 0.6 %collective-permute-done.10.two_on = bf16[176,256]{1,0:T(8,128)(2,1)S(1)} collective-permute-done((bf16[176,256]{1,0:T(8,128)(2,1)S(1)}, bf16[176,256]{1,0:T(8,128)(2,1)S(1)}, u32[]{:S(2)}, u32[]{:S(2)}) %collective-permute-start.10) | collective-permute-done | bytes 90144 | tf_op jit(solution)/shard_map/ppermute | solution.py:34
  45.2 0.0 collective-permute-done.12.come
  45.2 0.9 %collective-permute-done.13.next_one = bf16[176,256]{1,0:T(8,128)(2,1)S(1)} collective-permute-done((bf16[176,256]{1,0:T(8,128)(2,1)S(1)}, bf16[176,256]{1,0:T(8,128)(2,1)S(1)}, u32[]{:S(2)}, u32[]{:S(2)}) %collective-permute-start.13) | collective-permute-done | bytes 90144 | tf_op jit(solution)/shard_map/ppermute | solution.py:34
  46.1 0.1 shard_map.105.before.refs_0_
  46.2 1.6 %collective-permute-start.14 = (bf16[176,256]{1,0:T(8,128)(2,1)S(1)}, bf16[176,256]{1,0:T(8,128)(2,1)S(1)}, u32[]{:S(2)}, u32[]{:S(2)}) collective-permute-start(bf16[176,256]{1,0:T(8,128)(2,1)S(1)} %shard_map.105.before.refs_0_), channel_id=1, source_target_pairs={{0,16},{8,24},{16,0},{24,8},{1,17},{9,25},{17,1},{25,9},{2,18},{10... | collective-permute-start | bytes 270344 | tf_op jit(solution)/shard_map/ppermute | solution.py:34
  47.7 0.0 collective-permute-start.15
  47.7 1.7 %shard_map.106 = (bf16[192,1152]{1,0:T(8,128)(2,1)}, f32[8,128]{1,0:T(8,128)S(1)}) custom-call(bf16[192,1152]{1,0:T(8,128)(2,1)S(1)} %get-tuple-element.56.features, f32[1,1152]{1,0:T(1,128)S(1)} %get-tuple-element.57.gain, f32[192,1152]{1,0:T(8,128)S(1)} %get-tuple-element.98.norm_back, bf16[176,256]{1,0:T(8,128)(2,1)S(1)} %shard_map.105.before.refs_0_), custom_call_target="tpu_custom_call" | custom-call | bytes 5308416 | tf_op jit(solution)/shard_map/pallas_call | solution.py:138
  49.4 1.3 %collective-permute-done.14.refs_2_ = bf16[176,256]{1,0:T(8,128)(2,1)S(1)} collective-permute-done((bf16[176,256]{1,0:T(8,128)(2,1)S(1)}, bf16[176,256]{1,0:T(8,128)(2,1)S(1)}, u32[]{:S(2)}, u32[]{:S(2)}) %collective-permute-start.14) | collective-permute-done | bytes 90144 | tf_op jit(solution)/shard_map/ppermute | solution.py:34
  50.7 0.0 collective-permute-start.16
  50.7 0.0 collective-permute-done.15.refs_1_
  50.8 1.3 %collective-permute-done.16.refs_3_ = bf16[176,256]{1,0:T(8,128)(2,1)S(1)} collective-permute-done((bf16[176,256]{1,0:T(8,128)(2,1)S(1)}, bf16[176,256]{1,0:T(8,128)(2,1)S(1)}, u32[]{:S(2)}, u32[]{:S(2)}) %collective-permute-start.16) | collective-permute-done | bytes 90144 | tf_op jit(solution)/shard_map/ppermute | solution.py:34
  52.0 1.0 %shard_map.107 = (f32[144,1152]{1,0:T(8,128)}, f32[1152]{0:T(1024)}) custom-call(f32[8,128]{1,0:T(8,128)S(1)} %get-tuple-element.104.before, bf16[176,256]{1,0:T(8,128)(2,1)S(1)} %shard_map.105.before.refs_0_, bf16[176,256]{1,0:T(8,128)(2,1)S(1)} %collective-permute-done.15.refs_1_, bf16[176,256]{1,0:T(8,128)(2,1)S(1)} %collective-permute-done.14.refs_2_, ...), custom_call_target="tpu_custom_call" | custom-call | bytes 1327104 | tf_op jit(solution)/shard_map/pallas_call | solution.py:138
  (7 shorter events, 0.1 us)
Async XLA Ops:
  0.6 4.4 %collective-permute-start = (bf16[192,1152]{1,0:T(8,128)(2,1)}, bf16[192,1152]{1,0:T(8,128)(2,1)S(1)}, u32[]{:S(2)}, u32[]{:S(2)}) collective-permute-start(bf16[192,1152]{1,0:T(8,128)(2,1)} %bitcast.5), channel_id=1, source_target_pairs={{0,8},{8,0},{16,24},{24,16},{1,9},{9,1},{17,25},{25,17},{2,10},{10... | collective-permute-start | bytes 1327112 | tf_op jit(solution)/shard_map/ppermute | solution.py:34
  1.2 13.5 %collective-permute-start.3 = (bf16[192,1152]{1,0:T(8,128)(2,1)}, bf16[192,1152]{1,0:T(8,128)(2,1)S(1)}, u32[]{:S(2)}, u32[]{:S(2)}) collective-permute-start(bf16[192,1152]{1,0:T(8,128)(2,1)} %bitcast.6), channel_id=1, source_target_pairs={{0,16},{8,24},{16,0},{24,8},{1,17},{9,25},{17,1},{25,9},{2,18},{10... | collective-permute-start | bytes 1327112 | tf_op jit(solution)/shard_map/ppermute | solution.py:34
  5.0 1.0 %copy-start = (bf16[192,1,1152]{2,0,1:T(8,128)(2,1)S(1)}, bf16[192,1,1152]{2,0,1:T(8,128)(2,1)}, u32[]{:S(2)}) copy-start(bf16[192,1,1152]{2,0,1:T(8,128)(2,1)} %param.7) | copy-start | bytes 1327108
  6.0 1.0 %copy-start.1 = (bf16[192,1,1152]{2,0,1:T(8,128)(2,1)S(1)}, bf16[192,1,1152]{2,0,1:T(8,128)(2,1)}, u32[]{:S(2)}) copy-start(bf16[192,1,1152]{2,0,1:T(8,128)(2,1)} %param.6) | copy-start | bytes 1327108
  7.1 0.7 %copy-start.2 = (f32[1152]{0:T(1024)S(1)}, f32[1152]{0:T(1024)}, u32[]{:S(2)}) copy-start(f32[1152]{0:T(1024)} %gain_line.1) | copy-start | bytes 13828
  12.0 3.3 %collective-permute-start.1 = (bf16[192,1152]{1,0:T(8,128)(2,1)S(1)}, bf16[192,1152]{1,0:T(8,128)(2,1)S(1)}, u32[]{:S(2)}, u32[]{:S(2)}) collective-permute-start(bf16[192,1152]{1,0:T(8,128)(2,1)S(1)} %get-tuple-element.62.text_own), channel_id=1, source_target_pairs={{0,8},{8,0},{16,24},{24,16},{1,9},{9,1},{17,25},{25,17},{2,10},{10... | collective-permute-start | bytes 1327112 | tf_op jit(solution)/shard_map/ppermute | solution.py:34
  12.2 12.4 %collective-permute-start.2 = (bf16[192,1152]{1,0:T(8,128)(2,1)S(1)}, bf16[192,1152]{1,0:T(8,128)(2,1)S(1)}, u32[]{:S(2)}, u32[]{:S(2)}) collective-permute-start(bf16[192,1152]{1,0:T(8,128)(2,1)S(1)} %get-tuple-element.62.text_own), channel_id=1, source_target_pairs={{0,16},{8,24},{16,0},{24,8},{1,17},{9,25},{17,1},{25,9},{2,18},{10... | collective-permute-start | bytes 1327112 | tf_op jit(solution)/shard_map/ppermute | solution.py:34
  14.7 2.3 %collective-permute-start.4 = (bf16[160,1152]{1,0:T(8,128)(2,1)S(1)}, bf16[160,1152]{1,0:T(8,128)(2,1)S(1)}, u32[]{:S(2)}, u32[]{:S(2)}) collective-permute-start(bf16[160,1152]{1,0:T(8,128)(2,1)S(1)} %get-tuple-element.67), channel_id=1, source_target_pairs={{0,8},{8,0},{16,24},{24,16},{1,9},{9,1},{17,25},{25,17},{2,10},{10... | collective-permute-start | bytes 1105928 | tf_op jit(solution)/shard_map/ppermute | solution.py:34
  14.8 2.2 %collective-permute-start.5 = (bf16[32,1152]{1,0:T(8,128)(2,1)S(1)}, bf16[32,1152]{1,0:T(8,128)(2,1)S(1)}, u32[]{:S(2)}, u32[]{:S(2)}) collective-permute-start(bf16[32,1152]{1,0:T(8,128)(2,1)S(1)} %get-tuple-element.68), channel_id=1, source_target_pairs={{0,8},{8,0},{16,24},{24,16},{1,9},{9,1},{17,25},{25,17},{2,10},{10... | collective-permute-start | bytes 221192 | tf_op jit(solution)/shard_map/ppermute | solution.py:34
  24.6 1.8 %collective-permute-start.6 = (bf16[192,1152]{1,0:T(8,128)(2,1)S(1)}, bf16[192,1152]{1,0:T(8,128)(2,1)S(1)}, u32[]{:S(2)}, u32[]{:S(2)}) collective-permute-start(bf16[192,1152]{1,0:T(8,128)(2,1)S(1)} %collective-permute-done.2.text_unit.text_third), channel_id=1, source_target_pairs={{0,8},{8,0},{16,24},{24,16},{1,9},{9,1},{17,25},{25,17},{2,10},{10... | collective-permute-start | bytes 1327112 | tf_op jit(solution)/shard_map/ppermute | solution.py:34
  29.1 5.5 %collective-permute-start.7 = (bf16[176,256]{1,0:T(8,128)(2,1)S(1)}, bf16[176,256]{1,0:T(8,128)(2,1)S(1)}, u32[]{:S(2)}, u32[]{:S(2)}) collective-permute-start(bf16[176,256]{1,0:T(8,128)(2,1)S(1)} %get-tuple-element.95), channel_id=1, source_target_pairs={{0,1},{1,0},{2,3},{3,2},{4,5},{5,4},{6,7},{7,6},{8,9},{9,8},{10,11... | collective-permute-start | bytes 270344 | tf_op jit(solution)/shard_map/ppermute | solution.py:34
  30.7 7.6 %collective-permute-start.8 = (bf16[176,256]{1,0:T(8,128)(2,1)S(1)}, bf16[176,256]{1,0:T(8,128)(2,1)S(1)}, u32[]{:S(2)}, u32[]{:S(2)}) collective-permute-start(bf16[176,256]{1,0:T(8,128)(2,1)S(1)} %get-tuple-element.96), channel_id=1, source_target_pairs={{0,1},{1,0},{2,3},{3,2},{4,5},{5,4},{6,7},{7,6},{8,9},{9,8},{10,11... | collective-permute-start | bytes 270344 | tf_op jit(solution)/shard_map/ppermute | solution.py:34
  31.2 9.6 %collective-permute-start.9 = (bf16[176,256]{1,0:T(8,128)(2,1)S(1)}, bf16[176,256]{1,0:T(8,128)(2,1)S(1)}, u32[]{:S(2)}, u32[]{:S(2)}) collective-permute-start(bf16[176,256]{1,0:T(8,128)(2,1)S(1)} %get-tuple-element.97), channel_id=1, source_target_pairs={{0,1},{1,0},{2,3},{3,2},{4,5},{5,4},{6,7},{7,6},{8,9},{9,8},{10,11... | collective-permute-start | bytes 270344 | tf_op jit(solution)/shard_map/ppermute | solution.py:34
  34.7 9.9 %collective-permute-start.11 = (bf16[176,256]{1,0:T(8,128)(2,1)S(1)}, bf16[176,256]{1,0:T(8,128)(2,1)S(1)}, u32[]{:S(2)}, u32[]{:S(2)}) collective-permute-start(bf16[176,256]{1,0:T(8,128)(2,1)S(1)} %shard_map.100.before), channel_id=1, source_target_pairs={{0,6},{1,7},{2,4},{3,5},{4,2},{5,3},{6,0},{7,1},{8,14},{9,15},{10,... | collective-permute-start | bytes 270344 | tf_op jit(solution)/shard_map/ppermute | solution.py:34
  38.4 6.8 %collective-permute-start.10 = (bf16[176,256]{1,0:T(8,128)(2,1)S(1)}, bf16[176,256]{1,0:T(8,128)(2,1)S(1)}, u32[]{:S(2)}, u32[]{:S(2)}) collective-permute-start(bf16[176,256]{1,0:T(8,128)(2,1)S(1)} %shard_map.101.before), channel_id=1, source_target_pairs={{0,4},{1,5},{2,6},{3,7},{4,0},{5,1},{6,2},{7,3},{8,12},{9,13},{10,... | collective-permute-start | bytes 270344 | tf_op jit(solution)/shard_map/ppermute | solution.py:34
  39.2 6.0 %collective-permute-start.12 = (bf16[176,256]{1,0:T(8,128)(2,1)S(1)}, bf16[176,256]{1,0:T(8,128)(2,1)S(1)}, u32[]{:S(2)}, u32[]{:S(2)}) collective-permute-start(bf16[176,256]{1,0:T(8,128)(2,1)S(1)} %get-tuple-element.100), channel_id=1, source_target_pairs={{0,1},{1,0},{2,3},{3,2},{4,5},{5,4},{6,7},{7,6},{8,9},{9,8},{10,11... | collective-permute-start | bytes 270344 | tf_op jit(solution)/shard_map/ppermute | solution.py:34
  40.8 5.2 %collective-permute-start.13 = (bf16[176,256]{1,0:T(8,128)(2,1)S(1)}, bf16[176,256]{1,0:T(8,128)(2,1)S(1)}, u32[]{:S(2)}, u32[]{:S(2)}) collective-permute-start(bf16[176,256]{1,0:T(8,128)(2,1)S(1)} %shard_map.102.before), channel_id=1, source_target_pairs={{0,2},{1,3},{2,0},{3,1},{4,6},{5,7},{6,4},{7,5},{8,10},{9,11},{10,... | collective-permute-start | bytes 270344 | tf_op jit(solution)/shard_map/ppermute | solution.py:34
  46.2 4.6 %collective-permute-start.14 = (bf16[176,256]{1,0:T(8,128)(2,1)S(1)}, bf16[176,256]{1,0:T(8,128)(2,1)S(1)}, u32[]{:S(2)}, u32[]{:S(2)}) collective-permute-start(bf16[176,256]{1,0:T(8,128)(2,1)S(1)} %shard_map.105.before.refs_0_), channel_id=1, source_target_pairs={{0,16},{8,24},{16,0},{24,8},{1,17},{9,25},{17,1},{25,9},{2,18},{10... | collective-permute-start | bytes 270344 | tf_op jit(solution)/shard_map/ppermute | solution.py:34
  47.7 3.0 %collective-permute-start.15 = (bf16[176,256]{1,0:T(8,128)(2,1)S(1)}, bf16[176,256]{1,0:T(8,128)(2,1)S(1)}, u32[]{:S(2)}, u32[]{:S(2)}) collective-permute-start(bf16[176,256]{1,0:T(8,128)(2,1)S(1)} %shard_map.105.before.refs_0_), channel_id=1, source_target_pairs={{0,8},{8,0},{16,24},{24,16},{1,9},{9,1},{17,25},{25,17},{2,10},{10... | collective-permute-start | bytes 270344 | tf_op jit(solution)/shard_map/ppermute | solution.py:34
  50.7 1.3 %collective-permute-start.16 = (bf16[176,256]{1,0:T(8,128)(2,1)S(1)}, bf16[176,256]{1,0:T(8,128)(2,1)S(1)}, u32[]{:S(2)}, u32[]{:S(2)}) collective-permute-start(bf16[176,256]{1,0:T(8,128)(2,1)S(1)} %collective-permute-done.14.refs_2_), channel_id=1, source_target_pairs={{0,8},{8,0},{16,24},{24,16},{1,9},{9,1},{17,25},{25,17},{2,10},{10... | collective-permute-start | bytes 270344 | tf_op jit(solution)/shard_map/ppermute | solution.py:34

commit v23 on v22

--- a/solution.py
+++ b/solution.py
@@ -454,10 +454,14 @@
     total[...] = two_on[...].astype(F32) + three_on[...].astype(F32)
 
 
-def last_sum_body(far, keep, come, next_one, two_on, three_on, total, ordered, own):
+def others_sum_body(far, next_one, total):
+    total[...] = far[...] + next_one[...].astype(F32)
+
+
+def last_sum_body(others, keep, come, next_one, two_on, three_on, total, ordered, own):
     own[...] = (keep[0].astype(F32) + come[...].astype(F32)).astype(BF16)
     parts = (own, next_one, two_on, three_on)
-    total[...] = (own[...].astype(F32) + next_one[...].astype(F32) + far[...]).astype(BF16)
+    total[...] = (own[...].astype(F32) + others[...]).astype(BF16)
     count, full = total.shape
     z = lax.axis_index("rep") // 2
     for step, part in enumerate(parts):
@@ -622,8 +626,9 @@
         unit_near, factors, next_sum,
     )
     (far_sum,) = call(far_sum_body, [(packet, F32)], moved=1000)(token, two_on, three_on)
+    (others,) = call(others_sum_body, [(packet, F32)], moved=1000)(far_sum, next_one)
     (reduced,) = call(last_sum_body, [(packet, BF16)], [((4, BAND, LANES), F32), (packet, BF16)], moved=1000)(
-        far_sum, keep, come_own, next_one, two_on, three_on
+        others, keep, come_own, next_one, two_on, three_on
     )
     far_block = send(reduced, "loop", lambda p: p ^ 2)
     near_block = send(reduced, "loop", lambda p: p ^ 1)

time: 53.3 us -> 52.8 us (level)
  waiting for transfers between devices: 9.22 us -> 8.64 us
    ppermute x17, waiting for transfers between devices: 9.22 us -> 8.64 us  [send(): return lax.ppermute(value, axis, [(p, target(p)) for p in range(count)])]
    pallas_call x15 -> x16, Pallas kernels: 21.6 us -> 21.6 us  [run(): pl.pallas_call(body, out_shape=[jax.ShapeDtypeStruct(shape, kind) for sha...]
where the time goes in v23:
time: 52.8 us; the launch traced here: 52.5 us
  Pallas kernels  21.6 us (41%)
  starting transfers between devices  17.4 us (33%)
  waiting for transfers between devices  8.64 us (16%)
  local copies, waits for them, and re-layouts  2.72 us (5%)
  between operations  2.07 us (4%)
    pallas_call x16, Pallas kernels, run(): pl.pallas_call(body, out_shape=[jax.ShapeDtypeStruct(shape, kind) for sha...  21.6 us
    ppermute x17, starting transfers between devices, send(): return lax.ppermute(value, axis, [(p, target(p)) for p in range(count)])  17.4 us
    ppermute x17, waiting for transfers between devices, send(): return lax.ppermute(value, axis, [(p, target(p)) for p in range(count)])  8.64 us
    unnamed x6, local copies, waits for them, and re-layouts  2.72 us
  transfers between devices with their start and end apart: 17, of which 8 were waited for; matrix products, arithmetic and copies ran while one was open for 0% of the time, Pallas kernels for 34%

profile of v23, /device:TPU:0, one launch (start us, length us, event | category | flops | bytes accessed | tf_op | source)
XLA Modules:
  0.0 52.5 jit_solution(8261739565685738525)
XLA Ops:
  0.6 0.5 collective-permute-start
  1.2 2.6 %collective-permute-start.3 = (bf16[192,1152]{1,0:T(8,128)(2,1)}, bf16[192,1152]{1,0:T(8,128)(2,1)S(1)}, u32[]{:S(2)}, u32[]{:S(2)}) collective-permute-start(bf16[192,1152]{1,0:T(8,128)(2,1)} %bitcast.6), channel_id=1, source_target_pairs={{0,16},{8,24},{16,0},{24,8},{1,17},{9,25},{17,1},{25,9},{2,18},{10... | collective-permute-start | bytes 1327112 | tf_op jit(solution)/shard_map/ppermute | solution.py:34
  5.0 0.0 collective-permute-done.f1
  5.0 0.0 copy-start
  5.0 1.0 %copy-done = bf16[192,1,1152]{2,0,1:T(8,128)(2,1)S(1)} copy-done((bf16[192,1,1152]{2,0,1:T(8,128)(2,1)S(1)}, bf16[192,1,1152]{2,0,1:T(8,128)(2,1)}, u32[]{:S(2)}) %copy-start) | copy-done | bytes 442392
  6.0 1.0 %copy-done.1 = bf16[192,1,1152]{2,0,1:T(8,128)(2,1)S(1)} copy-done((bf16[192,1,1152]{2,0,1:T(8,128)(2,1)S(1)}, bf16[192,1,1152]{2,0,1:T(8,128)(2,1)}, u32[]{:S(2)}) %copy-start.1) | copy-done | bytes 442392
  7.1 0.7 %copy-done.2 = f32[1152]{0:T(1024)S(1)} copy-done((f32[1152]{0:T(1024)S(1)}, f32[1152]{0:T(1024)}, u32[]{:S(2)}) %copy-start.2) | copy-done | bytes 4632
  7.7 4.2 %shard_map.93 = (bf16[192,1152]{1,0:T(8,128)(2,1)S(1)}, bf16[1152,1152]{1,0:T(8,128)(2,1)S(1)}, bf16[192,1152]{1,0:T(8,128)(2,1)S(1)}, f32[1,1152]{1,0:T(1,128)S...) custom-call(f32[1]{0:T(128)S(6)} %copy.10.scale, ...), custom_call_target="tpu_custom_call" | custom-call | flops 1019215872 | bytes 3538944 | tf_op jit(solution)/shard_map/pallas_call | solution.py:138
  12.0 0.2 collective-permute-start.1
  12.2 0.6 %collective-permute-start.2 = (bf16[192,1152]{1,0:T(8,128)(2,1)S(1)}, bf16[192,1152]{1,0:T(8,128)(2,1)S(1)}, u32[]{:S(2)}, u32[]{:S(2)}) collective-permute-start(bf16[192,1152]{1,0:T(8,128)(2,1)S(1)} %get-tuple-element.62.text_own), channel_id=1, source_target_pairs={{0,16},{8,24},{16,0},{24,8},{1,17},{9,25},{17,1},{25,9},{2,18},{10... | collective-permute-start | bytes 1327112 | tf_op jit(solution)/shard_map/ppermute | solution.py:34
  12.8 1.9 %collective-permute-done.3.f2 = bf16[192,1152]{1,0:T(8,128)(2,1)S(1)} collective-permute-done((bf16[192,1152]{1,0:T(8,128)(2,1)}, bf16[192,1152]{1,0:T(8,128)(2,1)S(1)}, u32[]{:S(2)}, u32[]{:S(2)}) %collective-permute-start.3) | collective-permute-done | bytes 442400 | tf_op jit(solution)/shard_map/ppermute | solution.py:34
  14.7 0.1 collective-permute-start.4
  14.8 0.5 collective-permute-start.5
  15.3 0.0 collective-permute-done.1.t1
  15.3 1.7 %shard_map.94 = (bf16[384,1152]{1,0:T(8,128)(2,1)S(1)}, bf16[1152,384]{1,0:T(8,128)(2,1)S(1)}, bf16[1152,384]{1,0:T(8,128)(2,1)S(1)}, bf16[288,384]{1,0:T(8,128)...) custom-call(f32[1]{0:T(128)S(6)} %copy.10.scale, ...), custom_call_target="tpu_custom_call" | custom-call | flops 1000 | bytes 1000 | tf_op jit(solution)/shard_map/pallas_call | solution.py:138
  17.0 0.0 collective-permute-done.5.f3_tail
  17.0 0.0 collective-permute-done.4.f3_head
  17.0 4.6 %shard_map.96 = (bf16[1152,384]{1,0:T(8,128)(2,1)S(1)}, bf16[384,1152]{1,0:T(8,128)(2,1)S(1)}, bf16[1152,384]{1,0:T(8,128)(2,1)S(1)}, bf16[288,384]{1,0:T(8,128)...) custom-call(f32[1]{0:T(128)S(6)} %copy.10.scale, ...), custom_call_target="tpu_custom_call" | custom-call | flops 1000 | bytes 1000 | tf_op jit(solution)/shard_map/pallas_call | solution.py:138
  21.7 2.0 %shard_map.97 = (bf16[192,1152]{1,0:T(8,128)(2,1)}, f32[8,128]{1,0:T(8,128)S(1)}) custom-call(f32[1]{0:T(128)S(6)} %copy.10.scale, bf16[192,1152]{1,0:T(8,128)(2,1)S(1)} %get-tuple-element.65.text, bf16[384,384]{1,0:T(8,128)(2,1)S(1)} %get-tuple-element.66.weights_near, bf16[384,384]{1,0:T(8,128)(2,1)S(1)} %get-tuple-element.70.weights_far, ...), custom_call_target="tpu_custom_call" | custom-call | flops 1000 | bytes 1000 | tf_op jit(solution)/shard_map/pallas_call | solution.py:138
  23.7 0.9 %collective-permute-done.2.text_unit.text_third = bf16[192,1152]{1,0:T(8,128)(2,1)S(1)} collective-permute-done((bf16[192,1152]{1,0:T(8,128)(2,1)S(1)}, bf16[192,1152]{1,0:T(8,128)(2,1)S(1)}, u32[]{:S(2)}, u32[]{:S(2)}) %collective-permute-start.2) | collective-permute-done | bytes 442400 | tf_op jit(solution)/shard_map/ppermute | solution.py:34
  24.6 0.0 collective-permute-start.6
  24.6 1.3 %shard_map.98 = (bf16[192,768]{1,0:T(8,128)(2,1)S(1)}, f32[288,384]{1,0:T(8,128)S(1)}, f32[288,384]{1,0:T(8,128)S(1)}, f32[1,768]{1,0:T(1,128)S(1)}) custom-call(f32[1]{0:T(128)S(6)} %copy.10.scale, f32[1]{0:T(128)S(6)} %copy.11.bias, bf16[192,1152]{1,0:T(8,128)(2,1)S(1)} %collective-permute-done.2.text_unit.text_third, ...), custom_call_target="tpu_custom_call" | custom-call | flops 1019215872 | bytes 3538944 | tf_op jit(solution)/shard_map/pallas_call | solution.py:138
  26.0 0.5 collective-permute-done.6.text_unit.text_fourth
  26.4 2.7 %shard_map.99 = (bf16[176,256]{1,0:T(8,128)(2,1)S(1)}, bf16[176,256]{1,0:T(8,128)(2,1)S(1)}, bf16[176,256]{1,0:T(8,128)(2,1)S(1)}, bf16[176,256]{1,0:T(8,128)(2,...) custom-call(f32[1]{0:T(128)S(6)} %copy.10.scale, f32[1]{0:T(128)S(6)} %copy.11.bias, ...), custom_call_target="tpu_custom_call" | custom-call | flops 2038431744 | bytes 7077888 | tf_op jit(solution)/shard_map/pallas_call | solution.py:138
  29.1 1.6 %collective-permute-start.7 = (bf16[176,256]{1,0:T(8,128)(2,1)S(1)}, bf16[176,256]{1,0:T(8,128)(2,1)S(1)}, u32[]{:S(2)}, u32[]{:S(2)}) collective-permute-start(bf16[176,256]{1,0:T(8,128)(2,1)S(1)} %get-tuple-element.95), channel_id=1, source_target_pairs={{0,1},{1,0},{2,3},{3,2},{4,5},{5,4},{6,7},{7,6},{8,9},{9,8},{10,11... | collective-permute-start | bytes 270344 | tf_op jit(solution)/shard_map/ppermute | solution.py:34
  30.7 0.5 collective-permute-start.8
  31.2 1.5 %collective-permute-start.9 = (bf16[176,256]{1,0:T(8,128)(2,1)S(1)}, bf16[176,256]{1,0:T(8,128)(2,1)S(1)}, u32[]{:S(2)}, u32[]{:S(2)}) collective-permute-start(bf16[176,256]{1,0:T(8,128)(2,1)S(1)} %get-tuple-element.97), channel_id=1, source_target_pairs={{0,1},{1,0},{2,3},{3,2},{4,5},{5,4},{6,7},{7,6},{8,9},{9,8},{10,11... | collective-permute-start | bytes 270344 | tf_op jit(solution)/shard_map/ppermute | solution.py:34
  32.8 1.9 %collective-permute-done.7.come = bf16[176,256]{1,0:T(8,128)(2,1)S(1)} collective-permute-done((bf16[176,256]{1,0:T(8,128)(2,1)S(1)}, bf16[176,256]{1,0:T(8,128)(2,1)S(1)}, u32[]{:S(2)}, u32[]{:S(2)}) %collective-permute-start.7) | collective-permute-done | bytes 90144 | tf_op jit(solution)/shard_map/ppermute | solution.py:34
  34.7 3.7 %collective-permute-start.11 = (bf16[176,256]{1,0:T(8,128)(2,1)S(1)}, bf16[176,256]{1,0:T(8,128)(2,1)S(1)}, u32[]{:S(2)}, u32[]{:S(2)}) collective-permute-start(bf16[176,256]{1,0:T(8,128)(2,1)S(1)} %shard_map.100.before), channel_id=1, source_target_pairs={{0,6},{1,7},{2,4},{3,5},{4,2},{5,3},{6,0},{7,1},{8,14},{9,15},{10,... | collective-permute-start | bytes 270344 | tf_op jit(solution)/shard_map/ppermute | solution.py:34
  38.3 0.0 collective-permute-done.8.come
  38.4 0.9 %collective-permute-start.10 = (bf16[176,256]{1,0:T(8,128)(2,1)S(1)}, bf16[176,256]{1,0:T(8,128)(2,1)S(1)}, u32[]{:S(2)}, u32[]{:S(2)}) collective-permute-start(bf16[176,256]{1,0:T(8,128)(2,1)S(1)} %shard_map.101.before), channel_id=1, source_target_pairs={{0,4},{1,5},{2,6},{3,7},{4,0},{5,1},{6,2},{7,3},{8,12},{9,13},{10,... | collective-permute-start | bytes 270344 | tf_op jit(solution)/shard_map/ppermute | solution.py:34
  39.2 0.0 collective-permute-done.9.come
  39.3 1.7 %collective-permute-start.12 = (bf16[176,256]{1,0:T(8,128)(2,1)S(1)}, bf16[176,256]{1,0:T(8,128)(2,1)S(1)}, u32[]{:S(2)}, u32[]{:S(2)}) collective-permute-start(bf16[176,256]{1,0:T(8,128)(2,1)S(1)} %shard_map.102.before), channel_id=1, source_target_pairs={{0,2},{1,3},{2,0},{3,1},{4,6},{5,7},{6,4},{7,5},{8,10},{9,11},{10,... | collective-permute-start | bytes 270344 | tf_op jit(solution)/shard_map/ppermute | solution.py:34
  40.9 1.5 %collective-permute-start.13 = (bf16[176,256]{1,0:T(8,128)(2,1)S(1)}, bf16[176,256]{1,0:T(8,128)(2,1)S(1)}, u32[]{:S(2)}, u32[]{:S(2)}) collective-permute-start(bf16[176,256]{1,0:T(8,128)(2,1)S(1)} %get-tuple-element.100), channel_id=1, source_target_pairs={{0,1},{1,0},{2,3},{3,2},{4,5},{5,4},{6,7},{7,6},{8,9},{9,8},{10,11... | collective-permute-start | bytes 270344 | tf_op jit(solution)/shard_map/ppermute | solution.py:34
  42.5 2.1 %shard_map.103 = (f32[192,1152]{1,0:T(8,128)S(1)}, f32[8,128]{1,0:T(8,128)S(1)}) custom-call(f32[1]{0:T(128)S(6)} %copy.10.scale, bf16[1152,1152]{1,0:T(8,128)(2,1)S(1)} %get-tuple-element.58.proj, bf16[384,1152]{1,0:T(8,128)(2,1)S(1)} %get-tuple-element.64.text_near, bf16[192,1152]{1,0:T(8,128)(2,1)S(1)} %collective-permute-done.2.text_unit.text_third, ...), custom_call_target="tpu_custom_call" | custom-call | flops 1000 | bytes 1000 | tf_op jit(solution)/shard_map/pallas_call | solution.py:138
  44.6 0.0 collective-permute-done.11.three_on
  44.6 0.6 %collective-permute-done.10.two_on = bf16[176,256]{1,0:T(8,128)(2,1)S(1)} collective-permute-done((bf16[176,256]{1,0:T(8,128)(2,1)S(1)}, bf16[176,256]{1,0:T(8,128)(2,1)S(1)}, u32[]{:S(2)}, u32[]{:S(2)}) %collective-permute-start.10) | collective-permute-done | bytes 90144 | tf_op jit(solution)/shard_map/ppermute | solution.py:34
  45.2 0.3 collective-permute-done.12.next_one
  45.5 0.0 collective-permute-done.13.come
  45.5 0.1 shard_map.106.before.refs_0_
  45.6 1.6 %collective-permute-start.14 = (bf16[176,256]{1,0:T(8,128)(2,1)S(1)}, bf16[176,256]{1,0:T(8,128)(2,1)S(1)}, u32[]{:S(2)}, u32[]{:S(2)}) collective-permute-start(bf16[176,256]{1,0:T(8,128)(2,1)S(1)} %shard_map.106.before.refs_0_), channel_id=1, source_target_pairs={{0,16},{8,24},{16,0},{24,8},{1,17},{9,25},{17,1},{25,9},{2,18},{10... | collective-permute-start | bytes 270344 | tf_op jit(solution)/shard_map/ppermute | solution.py:34
  47.2 0.0 collective-permute-start.15
  47.2 1.7 %shard_map.107 = (bf16[192,1152]{1,0:T(8,128)(2,1)}, f32[8,128]{1,0:T(8,128)S(1)}) custom-call(bf16[192,1152]{1,0:T(8,128)(2,1)S(1)} %get-tuple-element.56.features, f32[1,1152]{1,0:T(1,128)S(1)} %get-tuple-element.57.gain, f32[192,1152]{1,0:T(8,128)S(1)} %get-tuple-element.98.norm_back, bf16[176,256]{1,0:T(8,128)(2,1)S(1)} %shard_map.106.before.refs_0_), custom_call_target="tpu_custom_call" | custom-call | bytes 5308416 | tf_op jit(solution)/shard_map/pallas_call | solution.py:138
  48.9 1.3 %collective-permute-done.14.refs_2_ = bf16[176,256]{1,0:T(8,128)(2,1)S(1)} collective-permute-done((bf16[176,256]{1,0:T(8,128)(2,1)S(1)}, bf16[176,256]{1,0:T(8,128)(2,1)S(1)}, u32[]{:S(2)}, u32[]{:S(2)}) %collective-permute-start.14) | collective-permute-done | bytes 90144 | tf_op jit(solution)/shard_map/ppermute | solution.py:34
  50.2 0.0 collective-permute-start.16
  50.2 0.0 collective-permute-done.15.refs_1_
  50.2 1.3 %collective-permute-done.16.refs_3_ = bf16[176,256]{1,0:T(8,128)(2,1)S(1)} collective-permute-done((bf16[176,256]{1,0:T(8,128)(2,1)S(1)}, bf16[176,256]{1,0:T(8,128)(2,1)S(1)}, u32[]{:S(2)}, u32[]{:S(2)}) %collective-permute-start.16) | collective-permute-done | bytes 90144 | tf_op jit(solution)/shard_map/ppermute | solution.py:34
  51.5 1.0 %shard_map.108 = (f32[144,1152]{1,0:T(8,128)}, f32[1152]{0:T(1024)}) custom-call(f32[8,128]{1,0:T(8,128)S(1)} %get-tuple-element.104.before, bf16[176,256]{1,0:T(8,128)(2,1)S(1)} %shard_map.106.before.refs_0_, bf16[176,256]{1,0:T(8,128)(2,1)S(1)} %collective-permute-done.15.refs_1_, bf16[176,256]{1,0:T(8,128)(2,1)S(1)} %collective-permute-done.14.refs_2_, ...), custom_call_target="tpu_custom_call" | custom-call | bytes 1327104 | tf_op jit(solution)/shard_map/pallas_call | solution.py:138
  (8 shorter events, 0.2 us)
Async XLA Ops:
  0.6 4.4 %collective-permute-start = (bf16[192,1152]{1,0:T(8,128)(2,1)}, bf16[192,1152]{1,0:T(8,128)(2,1)S(1)}, u32[]{:S(2)}, u32[]{:S(2)}) collective-permute-start(bf16[192,1152]{1,0:T(8,128)(2,1)} %bitcast.5), channel_id=1, source_target_pairs={{0,8},{8,0},{16,24},{24,16},{1,9},{9,1},{17,25},{25,17},{2,10},{10... | collective-permute-start | bytes 1327112 | tf_op jit(solution)/shard_map/ppermute | solution.py:34
  1.2 13.5 %collective-permute-start.3 = (bf16[192,1152]{1,0:T(8,128)(2,1)}, bf16[192,1152]{1,0:T(8,128)(2,1)S(1)}, u32[]{:S(2)}, u32[]{:S(2)}) collective-permute-start(bf16[192,1152]{1,0:T(8,128)(2,1)} %bitcast.6), channel_id=1, source_target_pairs={{0,16},{8,24},{16,0},{24,8},{1,17},{9,25},{17,1},{25,9},{2,18},{10... | collective-permute-start | bytes 1327112 | tf_op jit(solution)/shard_map/ppermute | solution.py:34
  5.0 1.0 %copy-start = (bf16[192,1,1152]{2,0,1:T(8,128)(2,1)S(1)}, bf16[192,1,1152]{2,0,1:T(8,128)(2,1)}, u32[]{:S(2)}) copy-start(bf16[192,1,1152]{2,0,1:T(8,128)(2,1)} %param.7) | copy-start | bytes 1327108
  6.0 1.0 %copy-start.1 = (bf16[192,1,1152]{2,0,1:T(8,128)(2,1)S(1)}, bf16[192,1,1152]{2,0,1:T(8,128)(2,1)}, u32[]{:S(2)}) copy-start(bf16[192,1,1152]{2,0,1:T(8,128)(2,1)} %param.6) | copy-start | bytes 1327108
  7.1 0.7 %copy-start.2 = (f32[1152]{0:T(1024)S(1)}, f32[1152]{0:T(1024)}, u32[]{:S(2)}) copy-start(f32[1152]{0:T(1024)} %gain_line.1) | copy-start | bytes 13828
  12.0 3.3 %collective-permute-start.1 = (bf16[192,1152]{1,0:T(8,128)(2,1)S(1)}, bf16[192,1152]{1,0:T(8,128)(2,1)S(1)}, u32[]{:S(2)}, u32[]{:S(2)}) collective-permute-start(bf16[192,1152]{1,0:T(8,128)(2,1)S(1)} %get-tuple-element.62.text_own), channel_id=1, source_target_pairs={{0,8},{8,0},{16,24},{24,16},{1,9},{9,1},{17,25},{25,17},{2,10},{10... | collective-permute-start | bytes 1327112 | tf_op jit(solution)/shard_map/ppermute | solution.py:34
  12.2 12.4 %collective-permute-start.2 = (bf16[192,1152]{1,0:T(8,128)(2,1)S(1)}, bf16[192,1152]{1,0:T(8,128)(2,1)S(1)}, u32[]{:S(2)}, u32[]{:S(2)}) collective-permute-start(bf16[192,1152]{1,0:T(8,128)(2,1)S(1)} %get-tuple-element.62.text_own), channel_id=1, source_target_pairs={{0,16},{8,24},{16,0},{24,8},{1,17},{9,25},{17,1},{25,9},{2,18},{10... | collective-permute-start | bytes 1327112 | tf_op jit(solution)/shard_map/ppermute | solution.py:34
  14.7 2.3 %collective-permute-start.4 = (bf16[160,1152]{1,0:T(8,128)(2,1)S(1)}, bf16[160,1152]{1,0:T(8,128)(2,1)S(1)}, u32[]{:S(2)}, u32[]{:S(2)}) collective-permute-start(bf16[160,1152]{1,0:T(8,128)(2,1)S(1)} %get-tuple-element.67), channel_id=1, source_target_pairs={{0,8},{8,0},{16,24},{24,16},{1,9},{9,1},{17,25},{25,17},{2,10},{10... | collective-permute-start | bytes 1105928 | tf_op jit(solution)/shard_map/ppermute | solution.py:34
  14.8 2.2 %collective-permute-start.5 = (bf16[32,1152]{1,0:T(8,128)(2,1)S(1)}, bf16[32,1152]{1,0:T(8,128)(2,1)S(1)}, u32[]{:S(2)}, u32[]{:S(2)}) collective-permute-start(bf16[32,1152]{1,0:T(8,128)(2,1)S(1)} %get-tuple-element.68), channel_id=1, source_target_pairs={{0,8},{8,0},{16,24},{24,16},{1,9},{9,1},{17,25},{25,17},{2,10},{10... | collective-permute-start | bytes 221192 | tf_op jit(solution)/shard_map/ppermute | solution.py:34
  24.6 1.8 %collective-permute-start.6 = (bf16[192,1152]{1,0:T(8,128)(2,1)S(1)}, bf16[192,1152]{1,0:T(8,128)(2,1)S(1)}, u32[]{:S(2)}, u32[]{:S(2)}) collective-permute-start(bf16[192,1152]{1,0:T(8,128)(2,1)S(1)} %collective-permute-done.2.text_unit.text_third), channel_id=1, source_target_pairs={{0,8},{8,0},{16,24},{24,16},{1,9},{9,1},{17,25},{25,17},{2,10},{10... | collective-permute-start | bytes 1327112 | tf_op jit(solution)/shard_map/ppermute | solution.py:34
  29.1 5.5 %collective-permute-start.7 = (bf16[176,256]{1,0:T(8,128)(2,1)S(1)}, bf16[176,256]{1,0:T(8,128)(2,1)S(1)}, u32[]{:S(2)}, u32[]{:S(2)}) collective-permute-start(bf16[176,256]{1,0:T(8,128)(2,1)S(1)} %get-tuple-element.95), channel_id=1, source_target_pairs={{0,1},{1,0},{2,3},{3,2},{4,5},{5,4},{6,7},{7,6},{8,9},{9,8},{10,11... | collective-permute-start | bytes 270344 | tf_op jit(solution)/shard_map/ppermute | solution.py:34
  30.7 7.6 %collective-permute-start.8 = (bf16[176,256]{1,0:T(8,128)(2,1)S(1)}, bf16[176,256]{1,0:T(8,128)(2,1)S(1)}, u32[]{:S(2)}, u32[]{:S(2)}) collective-permute-start(bf16[176,256]{1,0:T(8,128)(2,1)S(1)} %get-tuple-element.96), channel_id=1, source_target_pairs={{0,1},{1,0},{2,3},{3,2},{4,5},{5,4},{6,7},{7,6},{8,9},{9,8},{10,11... | collective-permute-start | bytes 270344 | tf_op jit(solution)/shard_map/ppermute | solution.py:34
  31.2 8.0 %collective-permute-start.9 = (bf16[176,256]{1,0:T(8,128)(2,1)S(1)}, bf16[176,256]{1,0:T(8,128)(2,1)S(1)}, u32[]{:S(2)}, u32[]{:S(2)}) collective-permute-start(bf16[176,256]{1,0:T(8,128)(2,1)S(1)} %get-tuple-element.97), channel_id=1, source_target_pairs={{0,1},{1,0},{2,3},{3,2},{4,5},{5,4},{6,7},{7,6},{8,9},{9,8},{10,11... | collective-permute-start | bytes 270344 | tf_op jit(solution)/shard_map/ppermute | solution.py:34
  34.7 9.9 %collective-permute-start.11 = (bf16[176,256]{1,0:T(8,128)(2,1)S(1)}, bf16[176,256]{1,0:T(8,128)(2,1)S(1)}, u32[]{:S(2)}, u32[]{:S(2)}) collective-permute-start(bf16[176,256]{1,0:T(8,128)(2,1)S(1)} %shard_map.100.before), channel_id=1, source_target_pairs={{0,6},{1,7},{2,4},{3,5},{4,2},{5,3},{6,0},{7,1},{8,14},{9,15},{10,... | collective-permute-start | bytes 270344 | tf_op jit(solution)/shard_map/ppermute | solution.py:34
  38.4 6.8 %collective-permute-start.10 = (bf16[176,256]{1,0:T(8,128)(2,1)S(1)}, bf16[176,256]{1,0:T(8,128)(2,1)S(1)}, u32[]{:S(2)}, u32[]{:S(2)}) collective-permute-start(bf16[176,256]{1,0:T(8,128)(2,1)S(1)} %shard_map.101.before), channel_id=1, source_target_pairs={{0,4},{1,5},{2,6},{3,7},{4,0},{5,1},{6,2},{7,3},{8,12},{9,13},{10,... | collective-permute-start | bytes 270344 | tf_op jit(solution)/shard_map/ppermute | solution.py:34
  39.3 6.2 %collective-permute-start.12 = (bf16[176,256]{1,0:T(8,128)(2,1)S(1)}, bf16[176,256]{1,0:T(8,128)(2,1)S(1)}, u32[]{:S(2)}, u32[]{:S(2)}) collective-permute-start(bf16[176,256]{1,0:T(8,128)(2,1)S(1)} %shard_map.102.before), channel_id=1, source_target_pairs={{0,2},{1,3},{2,0},{3,1},{4,6},{5,7},{6,4},{7,5},{8,10},{9,11},{10,... | collective-permute-start | bytes 270344 | tf_op jit(solution)/shard_map/ppermute | solution.py:34
  40.9 4.6 %collective-permute-start.13 = (bf16[176,256]{1,0:T(8,128)(2,1)S(1)}, bf16[176,256]{1,0:T(8,128)(2,1)S(1)}, u32[]{:S(2)}, u32[]{:S(2)}) collective-permute-start(bf16[176,256]{1,0:T(8,128)(2,1)S(1)} %get-tuple-element.100), channel_id=1, source_target_pairs={{0,1},{1,0},{2,3},{3,2},{4,5},{5,4},{6,7},{7,6},{8,9},{9,8},{10,11... | collective-permute-start | bytes 270344 | tf_op jit(solution)/shard_map/ppermute | solution.py:34
  45.6 4.6 %collective-permute-start.14 = (bf16[176,256]{1,0:T(8,128)(2,1)S(1)}, bf16[176,256]{1,0:T(8,128)(2,1)S(1)}, u32[]{:S(2)}, u32[]{:S(2)}) collective-permute-start(bf16[176,256]{1,0:T(8,128)(2,1)S(1)} %shard_map.106.before.refs_0_), channel_id=1, source_target_pairs={{0,16},{8,24},{16,0},{24,8},{1,17},{9,25},{17,1},{25,9},{2,18},{10... | collective-permute-start | bytes 270344 | tf_op jit(solution)/shard_map/ppermute | solution.py:34
  47.2 3.0 %collective-permute-start.15 = (bf16[176,256]{1,0:T(8,128)(2,1)S(1)}, bf16[176,256]{1,0:T(8,128)(2,1)S(1)}, u32[]{:S(2)}, u32[]{:S(2)}) collective-permute-start(bf16[176,256]{1,0:T(8,128)(2,1)S(1)} %shard_map.106.before.refs_0_), channel_id=1, source_target_pairs={{0,8},{8,0},{16,24},{24,16},{1,9},{9,1},{17,25},{25,17},{2,10},{10... | collective-permute-start | bytes 270344 | tf_op jit(solution)/shard_map/ppermute | solution.py:34
  50.2 1.3 %collective-permute-start.16 = (bf16[176,256]{1,0:T(8,128)(2,1)S(1)}, bf16[176,256]{1,0:T(8,128)(2,1)S(1)}, u32[]{:S(2)}, u32[]{:S(2)}) collective-permute-start(bf16[176,256]{1,0:T(8,128)(2,1)S(1)} %collective-permute-done.14.refs_2_), channel_id=1, source_target_pairs={{0,8},{8,0},{16,24},{24,16},{1,9},{9,1},{17,25},{25,17},{2,10},{10... | collective-permute-start | bytes 270344 | tf_op jit(solution)/shard_map/ppermute | solution.py:34

commit v24 on v23

--- a/solution.py
+++ b/solution.py
@@ -600,12 +600,13 @@
     across_three, across_two, across_next, across_own, keep, weights_fourth = outs
     come_three = send(across_three, "rep", lambda p: p ^ 1)
     come_two = send(across_two, "rep", lambda p: p ^ 1)
-    come_next = send(across_next, "rep", lambda p: p ^ 1)
     come_own = send(across_own, "rep", lambda p: p ^ 1)
     (three_sum,) = call(functools.partial(one_sum_body, 3), [(packet, BF16)], flops=1000, moved=1000)(
         keep, keep, come_three
     )
     three_on = send(three_sum, "rep", lambda p: p ^ 6)
+    across_next, three_sum = lax.optimization_barrier((across_next, three_sum))
+    come_next = send(across_next, "rep", lambda p: p ^ 1)
     (two_sum,) = call(functools.partial(one_sum_body, 2), [(packet, BF16)], flops=1000, moved=1000)(
         three_sum, keep, come_two
     )

time: 52.8 us -> 53.7 us (1.017)
  waiting for transfers between devices: 8.64 us -> 11.2 us
  starting transfers between devices: 17.4 us -> 15.8 us
    ppermute x17, waiting for transfers between devices: 8.64 us -> 11.2 us  [send(): return lax.ppermute(value, axis, [(p, target(p)) for p in range(count)])]
    ppermute x17, starting transfers between devices: 17.4 us -> 15.8 us  [send(): return lax.ppermute(value, axis, [(p, target(p)) for p in range(count)])]
  transfers between devices with their start and end apart: 17 -> 17, of which waited for: 8 -> 7; matrix products, arithmetic and copies ran while one was open for 0% -> 0% of each run, Pallas kernels for 34% -> 33%
where the time goes in v24:
time: 53.7 us; the launch traced here: 53.4 us
  Pallas kernels  21.6 us (40%)
  starting transfers between devices  15.8 us (29%)
  waiting for transfers between devices  11.2 us (21%)
  local copies, waits for them, and re-layouts  2.72 us (5%)
  between operations  2.09 us (4%)
    pallas_call x16, Pallas kernels, run(): pl.pallas_call(body, out_shape=[jax.ShapeDtypeStruct(shape, kind) for sha...  21.6 us
    ppermute x17, starting transfers between devices, send(): return lax.ppermute(value, axis, [(p, target(p)) for p in range(count)])  15.8 us
    ppermute x17, waiting for transfers between devices, send(): return lax.ppermute(value, axis, [(p, target(p)) for p in range(count)])  11.2 us
    unnamed x6, local copies, waits for them, and re-layouts  2.72 us
  transfers between devices with their start and end apart: 17, of which 7 were waited for; matrix products, arithmetic and copies ran while one was open for 0% of the time, Pallas kernels for 33%

profile of v24, /device:TPU:0, one launch (start us, length us, event | category | flops | bytes accessed | tf_op | source)
XLA Modules:
  0.0 53.4 jit_solution(11413757317586284847)
XLA Ops:
  0.6 0.5 collective-permute-start
  1.2 2.6 %collective-permute-start.3 = (bf16[192,1152]{1,0:T(8,128)(2,1)}, bf16[192,1152]{1,0:T(8,128)(2,1)S(1)}, u32[]{:S(2)}, u32[]{:S(2)}) collective-permute-start(bf16[192,1152]{1,0:T(8,128)(2,1)} %bitcast.6), channel_id=1, source_target_pairs={{0,16},{8,24},{16,0},{24,8},{1,17},{9,25},{17,1},{25,9},{2,18},{10... | collective-permute-start | bytes 1327112 | tf_op jit(solution)/shard_map/ppermute | solution.py:34
  5.0 0.0 collective-permute-done.f1
  5.0 0.0 copy-start
  5.0 1.0 %copy-done = bf16[192,1,1152]{2,0,1:T(8,128)(2,1)S(1)} copy-done((bf16[192,1,1152]{2,0,1:T(8,128)(2,1)S(1)}, bf16[192,1,1152]{2,0,1:T(8,128)(2,1)}, u32[]{:S(2)}) %copy-start) | copy-done | bytes 442392
  6.0 1.0 %copy-done.1 = bf16[192,1,1152]{2,0,1:T(8,128)(2,1)S(1)} copy-done((bf16[192,1,1152]{2,0,1:T(8,128)(2,1)S(1)}, bf16[192,1,1152]{2,0,1:T(8,128)(2,1)}, u32[]{:S(2)}) %copy-start.1) | copy-done | bytes 442392
  7.1 0.7 %copy-done.2 = f32[1152]{0:T(1024)S(1)} copy-done((f32[1152]{0:T(1024)S(1)}, f32[1152]{0:T(1024)}, u32[]{:S(2)}) %copy-start.2) | copy-done | bytes 4632
  7.7 4.2 %shard_map.93 = (bf16[192,1152]{1,0:T(8,128)(2,1)S(1)}, bf16[1152,1152]{1,0:T(8,128)(2,1)S(1)}, bf16[192,1152]{1,0:T(8,128)(2,1)S(1)}, f32[1,1152]{1,0:T(1,128)S...) custom-call(f32[1]{0:T(128)S(6)} %copy.10.scale, ...), custom_call_target="tpu_custom_call" | custom-call | flops 1019215872 | bytes 3538944 | tf_op jit(solution)/shard_map/pallas_call | solution.py:138
  12.0 0.2 collective-permute-start.1
  12.2 0.6 %collective-permute-start.2 = (bf16[192,1152]{1,0:T(8,128)(2,1)S(1)}, bf16[192,1152]{1,0:T(8,128)(2,1)S(1)}, u32[]{:S(2)}, u32[]{:S(2)}) collective-permute-start(bf16[192,1152]{1,0:T(8,128)(2,1)S(1)} %get-tuple-element.64.text_own), channel_id=1, source_target_pairs={{0,16},{8,24},{16,0},{24,8},{1,17},{9,25},{17,1},{25,9},{2,18},{10... | collective-permute-start | bytes 1327112 | tf_op jit(solution)/shard_map/ppermute | solution.py:34
  12.8 1.9 %collective-permute-done.3.f2 = bf16[192,1152]{1,0:T(8,128)(2,1)S(1)} collective-permute-done((bf16[192,1152]{1,0:T(8,128)(2,1)}, bf16[192,1152]{1,0:T(8,128)(2,1)S(1)}, u32[]{:S(2)}, u32[]{:S(2)}) %collective-permute-start.3) | collective-permute-done | bytes 442400 | tf_op jit(solution)/shard_map/ppermute | solution.py:34
  14.7 0.1 collective-permute-start.4
  14.8 0.5 collective-permute-start.5
  15.3 0.0 collective-permute-done.1.t1
  15.3 1.7 %shard_map.94 = (bf16[384,1152]{1,0:T(8,128)(2,1)S(1)}, bf16[1152,384]{1,0:T(8,128)(2,1)S(1)}, bf16[1152,384]{1,0:T(8,128)(2,1)S(1)}, bf16[288,384]{1,0:T(8,128)...) custom-call(f32[1]{0:T(128)S(6)} %copy.10.scale, ...), custom_call_target="tpu_custom_call" | custom-call | flops 1000 | bytes 1000 | tf_op jit(solution)/shard_map/pallas_call | solution.py:138
  17.0 0.0 collective-permute-done.5.f3_tail
  17.0 0.0 collective-permute-done.4.f3_head
  17.0 4.6 %shard_map.96 = (bf16[1152,384]{1,0:T(8,128)(2,1)S(1)}, bf16[384,1152]{1,0:T(8,128)(2,1)S(1)}, bf16[1152,384]{1,0:T(8,128)(2,1)S(1)}, bf16[288,384]{1,0:T(8,128)...) custom-call(f32[1]{0:T(128)S(6)} %copy.10.scale, ...), custom_call_target="tpu_custom_call" | custom-call | flops 1000 | bytes 1000 | tf_op jit(solution)/shard_map/pallas_call | solution.py:138
  21.7 2.0 %shard_map.97 = (bf16[192,1152]{1,0:T(8,128)(2,1)}, f32[8,128]{1,0:T(8,128)S(1)}) custom-call(f32[1]{0:T(128)S(6)} %copy.10.scale, bf16[192,1152]{1,0:T(8,128)(2,1)S(1)} %get-tuple-element.67.text, bf16[384,384]{1,0:T(8,128)(2,1)S(1)} %get-tuple-element.68.weights_near, bf16[384,384]{1,0:T(8,128)(2,1)S(1)} %get-tuple-element.72.weights_far, ...), custom_call_target="tpu_custom_call" | custom-call | flops 1000 | bytes 1000 | tf_op jit(solution)/shard_map/pallas_call | solution.py:138
  23.7 0.9 %collective-permute-done.2.text_unit.text_third = bf16[192,1152]{1,0:T(8,128)(2,1)S(1)} collective-permute-done((bf16[192,1152]{1,0:T(8,128)(2,1)S(1)}, bf16[192,1152]{1,0:T(8,128)(2,1)S(1)}, u32[]{:S(2)}, u32[]{:S(2)}) %collective-permute-start.2) | collective-permute-done | bytes 442400 | tf_op jit(solution)/shard_map/ppermute | solution.py:34
  24.6 0.0 collective-permute-start.6
  24.6 1.3 %shard_map.98 = (bf16[192,768]{1,0:T(8,128)(2,1)S(1)}, f32[288,384]{1,0:T(8,128)S(1)}, f32[288,384]{1,0:T(8,128)S(1)}, f32[1,768]{1,0:T(1,128)S(1)}) custom-call(f32[1]{0:T(128)S(6)} %copy.10.scale, f32[1]{0:T(128)S(6)} %copy.11.bias, bf16[192,1152]{1,0:T(8,128)(2,1)S(1)} %collective-permute-done.2.text_unit.text_third, ...), custom_call_target="tpu_custom_call" | custom-call | flops 1019215872 | bytes 3538944 | tf_op jit(solution)/shard_map/pallas_call | solution.py:138
  26.0 0.5 collective-permute-done.6.text_unit.text_fourth
  26.4 2.7 %shard_map.99 = (bf16[176,256]{1,0:T(8,128)(2,1)S(1)}, bf16[176,256]{1,0:T(8,128)(2,1)S(1)}, bf16[176,256]{1,0:T(8,128)(2,1)S(1)}, bf16[176,256]{1,0:T(8,128)(2,...) custom-call(f32[1]{0:T(128)S(6)} %copy.10.scale, f32[1]{0:T(128)S(6)} %copy.11.bias, ...), custom_call_target="tpu_custom_call" | custom-call | flops 2038431744 | bytes 7077888 | tf_op jit(solution)/shard_map/pallas_call | solution.py:138
  29.1 1.6 %collective-permute-start.7 = (bf16[176,256]{1,0:T(8,128)(2,1)S(1)}, bf16[176,256]{1,0:T(8,128)(2,1)S(1)}, u32[]{:S(2)}, u32[]{:S(2)}) collective-permute-start(bf16[176,256]{1,0:T(8,128)(2,1)S(1)} %get-tuple-element.98), channel_id=1, source_target_pairs={{0,1},{1,0},{2,3},{3,2},{4,5},{5,4},{6,7},{7,6},{8,9},{9,8},{10,11... | collective-permute-start | bytes 270344 | tf_op jit(solution)/shard_map/ppermute | solution.py:34
  30.7 0.5 collective-permute-start.8
  31.2 3.4 %collective-permute-done.7.come = bf16[176,256]{1,0:T(8,128)(2,1)S(1)} collective-permute-done((bf16[176,256]{1,0:T(8,128)(2,1)S(1)}, bf16[176,256]{1,0:T(8,128)(2,1)S(1)}, u32[]{:S(2)}, u32[]{:S(2)}) %collective-permute-start.7) | collective-permute-done | bytes 90144 | tf_op jit(solution)/shard_map/ppermute | solution.py:34
  34.7 1.6 %collective-permute-start.9 = (bf16[176,256]{1,0:T(8,128)(2,1)S(1)}, bf16[176,256]{1,0:T(8,128)(2,1)S(1)}, u32[]{:S(2)}, u32[]{:S(2)}) collective-permute-start(bf16[176,256]{1,0:T(8,128)(2,1)S(1)} %get-tuple-element.101), channel_id=1, source_target_pairs={{0,1},{1,0},{2,3},{3,2},{4,5},{5,4},{6,7},{7,6},{8,9},{9,8},{10,11... | collective-permute-start | bytes 270344 | tf_op jit(solution)/shard_map/ppermute | solution.py:34
  36.3 3.6 %collective-permute-start.11 = (bf16[176,256]{1,0:T(8,128)(2,1)S(1)}, bf16[176,256]{1,0:T(8,128)(2,1)S(1)}, u32[]{:S(2)}, u32[]{:S(2)}) collective-permute-start(bf16[176,256]{1,0:T(8,128)(2,1)S(1)} %shard_map.100.before), channel_id=1, source_target_pairs={{0,6},{1,7},{2,4},{3,5},{4,2},{5,3},{6,0},{7,1},{8,14},{9,15},{10,... | collective-permute-start | bytes 270344 | tf_op jit(solution)/shard_map/ppermute | solution.py:34
  39.9 0.0 collective-permute-done.8.come
  39.9 0.1 collective-permute-start.10
  40.0 0.0 collective-permute-done.9.come
  40.0 0.9 %collective-permute-start.12 = (bf16[176,256]{1,0:T(8,128)(2,1)S(1)}, bf16[176,256]{1,0:T(8,128)(2,1)S(1)}, u32[]{:S(2)}, u32[]{:S(2)}) collective-permute-start(bf16[176,256]{1,0:T(8,128)(2,1)S(1)} %shard_map.102.before), channel_id=1, source_target_pairs={{0,2},{1,3},{2,0},{3,1},{4,6},{5,7},{6,4},{7,5},{8,10},{9,11},{10,... | collective-permute-start | bytes 270344 | tf_op jit(solution)/shard_map/ppermute | solution.py:34
  41.0 1.5 %collective-permute-start.13 = (bf16[176,256]{1,0:T(8,128)(2,1)S(1)}, bf16[176,256]{1,0:T(8,128)(2,1)S(1)}, u32[]{:S(2)}, u32[]{:S(2)}) collective-permute-start(bf16[176,256]{1,0:T(8,128)(2,1)S(1)} %get-tuple-element.104), channel_id=1, source_target_pairs={{0,1},{1,0},{2,3},{3,2},{4,5},{5,4},{6,7},{7,6},{8,9},{9,8},{10,11... | collective-permute-start | bytes 270344 | tf_op jit(solution)/shard_map/ppermute | solution.py:34
  42.5 2.1 %shard_map.103 = (f32[192,1152]{1,0:T(8,128)S(1)}, f32[8,128]{1,0:T(8,128)S(1)}) custom-call(f32[1]{0:T(128)S(6)} %copy.10.scale, bf16[1152,1152]{1,0:T(8,128)(2,1)S(1)} %get-tuple-element.60.proj, bf16[384,1152]{1,0:T(8,128)(2,1)S(1)} %get-tuple-element.66.text_near, bf16[192,1152]{1,0:T(8,128)(2,1)S(1)} %collective-permute-done.2.text_unit.text_third, ...), custom_call_target="tpu_custom_call" | custom-call | flops 1000 | bytes 1000 | tf_op jit(solution)/shard_map/pallas_call | solution.py:138
  44.6 0.0 collective-permute-done.11.three_on
  44.6 1.8 %collective-permute-done.10.two_on = bf16[176,256]{1,0:T(8,128)(2,1)S(1)} collective-permute-done((bf16[176,256]{1,0:T(8,128)(2,1)S(1)}, bf16[176,256]{1,0:T(8,128)(2,1)S(1)}, u32[]{:S(2)}, u32[]{:S(2)}) %collective-permute-start.10) | collective-permute-done | bytes 90144 | tf_op jit(solution)/shard_map/ppermute | solution.py:34
  46.5 0.0 collective-permute-done.12.next_one
  46.5 0.0 collective-permute-done.13.come
  46.5 0.1 shard_map.106.before.refs_0_
  46.6 1.5 %collective-permute-start.14 = (bf16[176,256]{1,0:T(8,128)(2,1)S(1)}, bf16[176,256]{1,0:T(8,128)(2,1)S(1)}, u32[]{:S(2)}, u32[]{:S(2)}) collective-permute-start(bf16[176,256]{1,0:T(8,128)(2,1)S(1)} %shard_map.106.before.refs_0_), channel_id=1, source_target_pairs={{0,16},{8,24},{16,0},{24,8},{1,17},{9,25},{17,1},{25,9},{2,18},{10... | collective-permute-start | bytes 270344 | tf_op jit(solution)/shard_map/ppermute | solution.py:34
  48.0 0.0 collective-permute-start.15
  48.0 1.7 %shard_map.107 = (bf16[192,1152]{1,0:T(8,128)(2,1)}, f32[8,128]{1,0:T(8,128)S(1)}) custom-call(bf16[192,1152]{1,0:T(8,128)(2,1)S(1)} %get-tuple-element.58.features, f32[1,1152]{1,0:T(1,128)S(1)} %get-tuple-element.59.gain, f32[192,1152]{1,0:T(8,128)S(1)} %get-tuple-element.102.norm_back, bf16[176,256]{1,0:T(8,128)(2,1)S(1)} %shard_map.106.before.refs_0_), custom_call_target="tpu_custom_call" | custom-call | bytes 5308416 | tf_op jit(solution)/shard_map/pallas_call | solution.py:138
  49.8 1.4 %collective-permute-done.14.refs_2_ = bf16[176,256]{1,0:T(8,128)(2,1)S(1)} collective-permute-done((bf16[176,256]{1,0:T(8,128)(2,1)S(1)}, bf16[176,256]{1,0:T(8,128)(2,1)S(1)}, u32[]{:S(2)}, u32[]{:S(2)}) %collective-permute-start.14) | collective-permute-done | bytes 90144 | tf_op jit(solution)/shard_map/ppermute | solution.py:34
  51.2 0.0 collective-permute-start.16
  51.2 0.0 collective-permute-done.15.refs_1_
  51.2 1.3 %collective-permute-done.16.refs_3_ = bf16[176,256]{1,0:T(8,128)(2,1)S(1)} collective-permute-done((bf16[176,256]{1,0:T(8,128)(2,1)S(1)}, bf16[176,256]{1,0:T(8,128)(2,1)S(1)}, u32[]{:S(2)}, u32[]{:S(2)}) %collective-permute-start.16) | collective-permute-done | bytes 90144 | tf_op jit(solution)/shard_map/ppermute | solution.py:34
  52.5 1.0 %shard_map.108 = (f32[144,1152]{1,0:T(8,128)}, f32[1152]{0:T(1024)}) custom-call(f32[8,128]{1,0:T(8,128)S(1)} %get-tuple-element.108.before, bf16[176,256]{1,0:T(8,128)(2,1)S(1)} %shard_map.106.before.refs_0_, bf16[176,256]{1,0:T(8,128)(2,1)S(1)} %collective-permute-done.15.refs_1_, bf16[176,256]{1,0:T(8,128)(2,1)S(1)} %collective-permute-done.14.refs_2_, ...), custom_call_target="tpu_custom_call" | custom-call | bytes 1327104 | tf_op jit(solution)/shard_map/pallas_call | solution.py:138
  (8 shorter events, 0.2 us)
Async XLA Ops:
  0.6 4.4 %collective-permute-start = (bf16[192,1152]{1,0:T(8,128)(2,1)}, bf16[192,1152]{1,0:T(8,128)(2,1)S(1)}, u32[]{:S(2)}, u32[]{:S(2)}) collective-permute-start(bf16[192,1152]{1,0:T(8,128)(2,1)} %bitcast.5), channel_id=1, source_target_pairs={{0,8},{8,0},{16,24},{24,16},{1,9},{9,1},{17,25},{25,17},{2,10},{10... | collective-permute-start | bytes 1327112 | tf_op jit(solution)/shard_map/ppermute | solution.py:34
  1.2 13.5 %collective-permute-start.3 = (bf16[192,1152]{1,0:T(8,128)(2,1)}, bf16[192,1152]{1,0:T(8,128)(2,1)S(1)}, u32[]{:S(2)}, u32[]{:S(2)}) collective-permute-start(bf16[192,1152]{1,0:T(8,128)(2,1)} %bitcast.6), channel_id=1, source_target_pairs={{0,16},{8,24},{16,0},{24,8},{1,17},{9,25},{17,1},{25,9},{2,18},{10... | collective-permute-start | bytes 1327112 | tf_op jit(solution)/shard_map/ppermute | solution.py:34
  5.0 1.0 %copy-start = (bf16[192,1,1152]{2,0,1:T(8,128)(2,1)S(1)}, bf16[192,1,1152]{2,0,1:T(8,128)(2,1)}, u32[]{:S(2)}) copy-start(bf16[192,1,1152]{2,0,1:T(8,128)(2,1)} %param.7) | copy-start | bytes 1327108
  6.0 1.0 %copy-start.1 = (bf16[192,1,1152]{2,0,1:T(8,128)(2,1)S(1)}, bf16[192,1,1152]{2,0,1:T(8,128)(2,1)}, u32[]{:S(2)}) copy-start(bf16[192,1,1152]{2,0,1:T(8,128)(2,1)} %param.6) | copy-start | bytes 1327108
  7.1 0.7 %copy-start.2 = (f32[1152]{0:T(1024)S(1)}, f32[1152]{0:T(1024)}, u32[]{:S(2)}) copy-start(f32[1152]{0:T(1024)} %gain_line.1) | copy-start | bytes 13828
  12.0 3.3 %collective-permute-start.1 = (bf16[192,1152]{1,0:T(8,128)(2,1)S(1)}, bf16[192,1152]{1,0:T(8,128)(2,1)S(1)}, u32[]{:S(2)}, u32[]{:S(2)}) collective-permute-start(bf16[192,1152]{1,0:T(8,128)(2,1)S(1)} %get-tuple-element.64.text_own), channel_id=1, source_target_pairs={{0,8},{8,0},{16,24},{24,16},{1,9},{9,1},{17,25},{25,17},{2,10},{10... | collective-permute-start | bytes 1327112 | tf_op jit(solution)/shard_map/ppermute | solution.py:34
  12.2 12.4 %collective-permute-start.2 = (bf16[192,1152]{1,0:T(8,128)(2,1)S(1)}, bf16[192,1152]{1,0:T(8,128)(2,1)S(1)}, u32[]{:S(2)}, u32[]{:S(2)}) collective-permute-start(bf16[192,1152]{1,0:T(8,128)(2,1)S(1)} %get-tuple-element.64.text_own), channel_id=1, source_target_pairs={{0,16},{8,24},{16,0},{24,8},{1,17},{9,25},{17,1},{25,9},{2,18},{10... | collective-permute-start | bytes 1327112 | tf_op jit(solution)/shard_map/ppermute | solution.py:34
  14.7 2.3 %collective-permute-start.4 = (bf16[160,1152]{1,0:T(8,128)(2,1)S(1)}, bf16[160,1152]{1,0:T(8,128)(2,1)S(1)}, u32[]{:S(2)}, u32[]{:S(2)}) collective-permute-start(bf16[160,1152]{1,0:T(8,128)(2,1)S(1)} %get-tuple-element.69), channel_id=1, source_target_pairs={{0,8},{8,0},{16,24},{24,16},{1,9},{9,1},{17,25},{25,17},{2,10},{10... | collective-permute-start | bytes 1105928 | tf_op jit(solution)/shard_map/ppermute | solution.py:34
  14.8 2.2 %collective-permute-start.5 = (bf16[32,1152]{1,0:T(8,128)(2,1)S(1)}, bf16[32,1152]{1,0:T(8,128)(2,1)S(1)}, u32[]{:S(2)}, u32[]{:S(2)}) collective-permute-start(bf16[32,1152]{1,0:T(8,128)(2,1)S(1)} %get-tuple-element.70), channel_id=1, source_target_pairs={{0,8},{8,0},{16,24},{24,16},{1,9},{9,1},{17,25},{25,17},{2,10},{10... | collective-permute-start | bytes 221192 | tf_op jit(solution)/shard_map/ppermute | solution.py:34
  24.6 1.8 %collective-permute-start.6 = (bf16[192,1152]{1,0:T(8,128)(2,1)S(1)}, bf16[192,1152]{1,0:T(8,128)(2,1)S(1)}, u32[]{:S(2)}, u32[]{:S(2)}) collective-permute-start(bf16[192,1152]{1,0:T(8,128)(2,1)S(1)} %collective-permute-done.2.text_unit.text_third), channel_id=1, source_target_pairs={{0,8},{8,0},{16,24},{24,16},{1,9},{9,1},{17,25},{25,17},{2,10},{10... | collective-permute-start | bytes 1327112 | tf_op jit(solution)/shard_map/ppermute | solution.py:34
  29.1 5.5 %collective-permute-start.7 = (bf16[176,256]{1,0:T(8,128)(2,1)S(1)}, bf16[176,256]{1,0:T(8,128)(2,1)S(1)}, u32[]{:S(2)}, u32[]{:S(2)}) collective-permute-start(bf16[176,256]{1,0:T(8,128)(2,1)S(1)} %get-tuple-element.98), channel_id=1, source_target_pairs={{0,1},{1,0},{2,3},{3,2},{4,5},{5,4},{6,7},{7,6},{8,9},{9,8},{10,11... | collective-permute-start | bytes 270344 | tf_op jit(solution)/shard_map/ppermute | solution.py:34
  30.7 9.2 %collective-permute-start.8 = (bf16[176,256]{1,0:T(8,128)(2,1)S(1)}, bf16[176,256]{1,0:T(8,128)(2,1)S(1)}, u32[]{:S(2)}, u32[]{:S(2)}) collective-permute-start(bf16[176,256]{1,0:T(8,128)(2,1)S(1)} %get-tuple-element.100), channel_id=1, source_target_pairs={{0,1},{1,0},{2,3},{3,2},{4,5},{5,4},{6,7},{7,6},{8,9},{9,8},{10,11... | collective-permute-start | bytes 270344 | tf_op jit(solution)/shard_map/ppermute | solution.py:34
  34.7 5.3 %collective-permute-start.9 = (bf16[176,256]{1,0:T(8,128)(2,1)S(1)}, bf16[176,256]{1,0:T(8,128)(2,1)S(1)}, u32[]{:S(2)}, u32[]{:S(2)}) collective-permute-start(bf16[176,256]{1,0:T(8,128)(2,1)S(1)} %get-tuple-element.101), channel_id=1, source_target_pairs={{0,1},{1,0},{2,3},{3,2},{4,5},{5,4},{6,7},{7,6},{8,9},{9,8},{10,11... | collective-permute-start | bytes 270344 | tf_op jit(solution)/shard_map/ppermute | solution.py:34
  36.3 8.3 %collective-permute-start.11 = (bf16[176,256]{1,0:T(8,128)(2,1)S(1)}, bf16[176,256]{1,0:T(8,128)(2,1)S(1)}, u32[]{:S(2)}, u32[]{:S(2)}) collective-permute-start(bf16[176,256]{1,0:T(8,128)(2,1)S(1)} %shard_map.100.before), channel_id=1, source_target_pairs={{0,6},{1,7},{2,4},{3,5},{4,2},{5,3},{6,0},{7,1},{8,14},{9,15},{10,... | collective-permute-start | bytes 270344 | tf_op jit(solution)/shard_map/ppermute | solution.py:34
  39.9 6.5 %collective-permute-start.10 = (bf16[176,256]{1,0:T(8,128)(2,1)S(1)}, bf16[176,256]{1,0:T(8,128)(2,1)S(1)}, u32[]{:S(2)}, u32[]{:S(2)}) collective-permute-start(bf16[176,256]{1,0:T(8,128)(2,1)S(1)} %shard_map.101.before), channel_id=1, source_target_pairs={{0,4},{1,5},{2,6},{3,7},{4,0},{5,1},{6,2},{7,3},{8,12},{9,13},{10,... | collective-permute-start | bytes 270344 | tf_op jit(solution)/shard_map/ppermute | solution.py:34
  40.0 6.4 %collective-permute-start.12 = (bf16[176,256]{1,0:T(8,128)(2,1)S(1)}, bf16[176,256]{1,0:T(8,128)(2,1)S(1)}, u32[]{:S(2)}, u32[]{:S(2)}) collective-permute-start(bf16[176,256]{1,0:T(8,128)(2,1)S(1)} %shard_map.102.before), channel_id=1, source_target_pairs={{0,2},{1,3},{2,0},{3,1},{4,6},{5,7},{6,4},{7,5},{8,10},{9,11},{10,... | collective-permute-start | bytes 270344 | tf_op jit(solution)/shard_map/ppermute | solution.py:34
  41.0 5.5 %collective-permute-start.13 = (bf16[176,256]{1,0:T(8,128)(2,1)S(1)}, bf16[176,256]{1,0:T(8,128)(2,1)S(1)}, u32[]{:S(2)}, u32[]{:S(2)}) collective-permute-start(bf16[176,256]{1,0:T(8,128)(2,1)S(1)} %get-tuple-element.104), channel_id=1, source_target_pairs={{0,1},{1,0},{2,3},{3,2},{4,5},{5,4},{6,7},{7,6},{8,9},{9,8},{10,11... | collective-permute-start | bytes 270344 | tf_op jit(solution)/shard_map/ppermute | solution.py:34
  46.6 4.6 %collective-permute-start.14 = (bf16[176,256]{1,0:T(8,128)(2,1)S(1)}, bf16[176,256]{1,0:T(8,128)(2,1)S(1)}, u32[]{:S(2)}, u32[]{:S(2)}) collective-permute-start(bf16[176,256]{1,0:T(8,128)(2,1)S(1)} %shard_map.106.before.refs_0_), channel_id=1, source_target_pairs={{0,16},{8,24},{16,0},{24,8},{1,17},{9,25},{17,1},{25,9},{2,18},{10... | collective-permute-start | bytes 270344 | tf_op jit(solution)/shard_map/ppermute | solution.py:34
  48.0 3.1 %collective-permute-start.15 = (bf16[176,256]{1,0:T(8,128)(2,1)S(1)}, bf16[176,256]{1,0:T(8,128)(2,1)S(1)}, u32[]{:S(2)}, u32[]{:S(2)}) collective-permute-start(bf16[176,256]{1,0:T(8,128)(2,1)S(1)} %shard_map.106.before.refs_0_), channel_id=1, source_target_pairs={{0,8},{8,0},{16,24},{24,16},{1,9},{9,1},{17,25},{25,17},{2,10},{10... | collective-permute-start | bytes 270344 | tf_op jit(solution)/shard_map/ppermute | solution.py:34
  51.2 1.3 %collective-permute-start.16 = (bf16[176,256]{1,0:T(8,128)(2,1)S(1)}, bf16[176,256]{1,0:T(8,128)(2,1)S(1)}, u32[]{:S(2)}, u32[]{:S(2)}) collective-permute-start(bf16[176,256]{1,0:T(8,128)(2,1)S(1)} %collective-permute-done.14.refs_2_), channel_id=1, source_target_pairs={{0,8},{8,0},{16,24},{24,16},{1,9},{9,1},{17,25},{25,17},{2,10},{10... | collective-permute-start | bytes 270344 | tf_op jit(solution)/shard_map/ppermute | solution.py:34

commit v25 on v23

--- a/solution.py
+++ b/solution.py
@@ -472,28 +472,49 @@
     total[count - BAND :, full - LANES :] = value.astype(BF16)
 
 
-def finish_body(members, before, *refs):
-    packets, (proj_grad, gain_gradient, ordered) = refs[:members], refs[members:]
+def place_main(packet, member, buffer, out, semaphore):
+    rows, full = buffer.shape
+    buffer[...] = packet[:rows, :].astype(F32)
+    where = pl.ds(pl.multiple_of(member * full, LANES), full)
+    copy = pltpu.make_async_copy(buffer, out.at[:, where], semaphore)
+    copy.start()
+    return copy
+
+
+def finish_most_body(before, own, near, far, out, first, second, third, semaphores):
+    copies = [
+        place_main(packet, lax.axis_index("loop") ^ k, buffer, out, semaphores.at[k])
+        for k, (packet, buffer) in enumerate(((own, first), (near, second), (far, third)))
+    ]
+    for copy in copies:
+        copy.wait()
+
+
+def finish_body(members, begun, *refs):
+    packets, (out, gain_gradient, ordered, main, last, semaphores) = refs[:members], refs[members:]
     count, full = packets[0].shape
-    rows, width = proj_grad.shape
+    rows, width = out.shape
     rest = width // members - full
     per_band = full // rest
+    main_out = place_main(packets[-1], lax.axis_index("loop") ^ (members - 1), main, out, semaphores.at[0])
     for k in range(members):
-        member = lax.axis_index("loop") ^ k
-        proj_grad[:, pl.ds(pl.multiple_of(member * full, LANES), full)] = packets[k][:rows, :].astype(F32)
-        ordered[member] = packets[k][rows:, :].astype(F32)
+        ordered[lax.axis_index("loop") ^ k] = packets[k][rows:, :].astype(F32)
     tails = []
     for index in range(rows // BAND):
         at, lane = (index // per_band) * BAND, (index % per_band) * rest
         tails.append(
             jnp.concatenate([ordered[member][at : at + BAND, lane : lane + rest] for member in range(members)], axis=1)
         )
-    proj_grad[:, members * full :] = jnp.concatenate(tails, axis=0)
+    last[...] = jnp.concatenate(tails, axis=0)
+    last_out = pltpu.make_async_copy(last, out.at[:, members * full :], semaphores.at[1])
+    last_out.start()
     value = ordered[0][count - rows - BAND :, full - LANES :]
     for member in range(1, members):
         value = value + ordered[member][count - rows - BAND :, full - LANES :]
     for at in range(width // LANES):
         gain_gradient[at * LANES : (at + 1) * LANES] = value[at]
+    main_out.wait()
+    last_out.wait()
 
 
 def local_four(features, text, proj, gain, scale, bias):
@@ -636,14 +657,33 @@
         f0_kept, gain_row, norm_back, reduced
     )
     far_block, token = lax.optimization_barrier((far_block, token))
-    blocks = [reduced, near_block, far_block, send(far_block, "loop", lambda p: p ^ 1)]
-
-    proj_grad, gain_gradient = call(
+    last_block = send(far_block, "loop", lambda p: p ^ 1)
+    out_kind = jax.ShapeDtypeStruct((each, width), F32)
+    main_room = pltpu.VMEM((each, full), F32)
+    begun = pl.pallas_call(
+        finish_most_body,
+        out_shape=out_kind,
+        in_specs=[VMEM] * 4,
+        out_specs=HBM,
+        scratch_shapes=[main_room] * 3 + [pltpu.SemaphoreType.DMA((3,))],
+        compiler_params=pltpu.CompilerParams(vmem_limit_bytes=24 * 2**20),
+        cost_estimate=pl.CostEstimate(flops=0, bytes_accessed=8 * each * width, transcendentals=0),
+    )(token, reduced, near_block, far_block)
+    proj_grad, gain_gradient = pl.pallas_call(
         functools.partial(finish_body, members),
-        [((each, width), F32), ((width,), F32)],
-        [((members, bands * BAND, full), F32)],
-        moved=8 * each * width,
-    )(token, *blocks)
+        out_shape=[out_kind, jax.ShapeDtypeStruct((width,), F32)],
+        in_specs=[HBM] + [VMEM] * members,
+        out_specs=[HBM, VMEM],
+        input_output_aliases={0: 0},
+        scratch_shapes=[
+            pltpu.VMEM((members, bands * BAND, full), F32),
+            main_room,
+            pltpu.VMEM((each, width - members * full), F32),
+            pltpu.SemaphoreType.DMA((2,)),
+        ],
+        compiler_params=pltpu.CompilerParams(vmem_limit_bytes=24 * 2**20),
+        cost_estimate=pl.CostEstimate(flops=0, bytes_accessed=2 * each * width, transcendentals=0),
+    )(begun, reduced, near_block, far_block, last_block)
     return feature_grad[:, None, :], text_grad[:, None, :], proj_grad, gain_gradient
 
 

time: 52.8 us -> 53.3 us (level)
  Pallas kernels: 21.6 us -> 22.8 us
  waiting for transfers between devices: 8.64 us -> 7.83 us
    pallas_call x0 -> x2, Pallas kernels: none -> 2.18 us  [the longest x1 1.38 us: local_four(): pl.pallas_call(functools.partial(finish_body, members), out_shape=[out_ki...]
    pallas_call x16 -> x15, Pallas kernels: 21.6 us -> 20.6 us  [run(): pl.pallas_call(body, out_shape=[jax.ShapeDtypeStruct(shape, kind) for sha...]
    ppermute x17, waiting for transfers between devices: 8.64 us -> 7.83 us  [send(): return lax.ppermute(value, axis, [(p, target(p)) for p in range(count)])]
  transfers between devices with their start and end apart: 17 -> 17, of which waited for: 8 -> 8; matrix products, arithmetic and copies ran while one was open for 0% -> 0% of each run, Pallas kernels for 34% -> 35%
where the time goes in v25:
time: 53.3 us; the launch traced here: 53 us
  Pallas kernels  22.8 us (43%)
  starting transfers between devices  17.4 us (33%)
  waiting for transfers between devices  7.83 us (15%)
  local copies, waits for them, and re-layouts  2.72 us (5%)
  between operations  2.24 us (4%)
    pallas_call x15, Pallas kernels, run(): pl.pallas_call(body, out_shape=[jax.ShapeDtypeStruct(shape, kind) for sha...  20.6 us
    ppermute x17, starting transfers between devices, send(): return lax.ppermute(value, axis, [(p, target(p)) for p in range(count)])  17.4 us
    ppermute x17, waiting for transfers between devices, send(): return lax.ppermute(value, axis, [(p, target(p)) for p in range(count)])  7.83 us
    unnamed x6, local copies, waits for them, and re-layouts  2.72 us
    pallas_call x1, Pallas kernels, local_four(): pl.pallas_call(functools.partial(finish_body, members), out_shape=[out_ki...  1.38 us
  transfers between devices with their start and end apart: 17, of which 8 were waited for; matrix products, arithmetic and copies ran while one was open for 0% of the time, Pallas kernels for 35%

profile of v25, /device:TPU:0, one launch (start us, length us, event | category | flops | bytes accessed | tf_op | source)
XLA Modules:
  0.0 53.0 jit_solution(3916772439779624524)
XLA Ops:
  0.6 0.5 collective-permute-start
  1.2 2.6 %collective-permute-start.3 = (bf16[192,1152]{1,0:T(8,128)(2,1)}, bf16[192,1152]{1,0:T(8,128)(2,1)S(1)}, u32[]{:S(2)}, u32[]{:S(2)}) collective-permute-start(bf16[192,1152]{1,0:T(8,128)(2,1)} %bitcast.6), channel_id=1, source_target_pairs={{0,16},{8,24},{16,0},{24,8},{1,17},{9,25},{17,1},{25,9},{2,18},{10... | collective-permute-start | bytes 1327112 | tf_op jit(solution)/shard_map/ppermute | solution.py:34
  5.0 0.0 collective-permute-done.f1
  5.0 1.0 %copy-done = bf16[192,1,1152]{2,0,1:T(8,128)(2,1)S(1)} copy-done((bf16[192,1,1152]{2,0,1:T(8,128)(2,1)S(1)}, bf16[192,1,1152]{2,0,1:T(8,128)(2,1)}, u32[]{:S(2)}) %copy-start) | copy-done | bytes 442392
  6.0 1.0 %copy-done.1 = bf16[192,1,1152]{2,0,1:T(8,128)(2,1)S(1)} copy-done((bf16[192,1,1152]{2,0,1:T(8,128)(2,1)S(1)}, bf16[192,1,1152]{2,0,1:T(8,128)(2,1)}, u32[]{:S(2)}) %copy-start.1) | copy-done | bytes 442392
  7.1 0.7 %copy-done.2 = f32[1152]{0:T(1024)S(1)} copy-done((f32[1152]{0:T(1024)S(1)}, f32[1152]{0:T(1024)}, u32[]{:S(2)}) %copy-start.2) | copy-done | bytes 4632
  7.7 4.2 %shard_map.93 = (bf16[192,1152]{1,0:T(8,128)(2,1)S(1)}, bf16[1152,1152]{1,0:T(8,128)(2,1)S(1)}, bf16[192,1152]{1,0:T(8,128)(2,1)S(1)}, f32[1,1152]{1,0:T(1,128)S...) custom-call(f32[1]{0:T(128)S(6)} %copy.12.scale, ...), custom_call_target="tpu_custom_call" | custom-call | flops 1019215872 | bytes 3538944 | tf_op jit(solution)/shard_map/pallas_call | solution.py:138
  12.0 0.2 collective-permute-start.1
  12.2 0.6 %collective-permute-start.2 = (bf16[192,1152]{1,0:T(8,128)(2,1)S(1)}, bf16[192,1152]{1,0:T(8,128)(2,1)S(1)}, u32[]{:S(2)}, u32[]{:S(2)}) collective-permute-start(bf16[192,1152]{1,0:T(8,128)(2,1)S(1)} %get-tuple-element.62.text_own), channel_id=1, source_target_pairs={{0,16},{8,24},{16,0},{24,8},{1,17},{9,25},{17,1},{25,9},{2,18},{10... | collective-permute-start | bytes 1327112 | tf_op jit(solution)/shard_map/ppermute | solution.py:34
  12.8 1.9 %collective-permute-done.3.f2 = bf16[192,1152]{1,0:T(8,128)(2,1)S(1)} collective-permute-done((bf16[192,1152]{1,0:T(8,128)(2,1)}, bf16[192,1152]{1,0:T(8,128)(2,1)S(1)}, u32[]{:S(2)}, u32[]{:S(2)}) %collective-permute-start.3) | collective-permute-done | bytes 442400 | tf_op jit(solution)/shard_map/ppermute | solution.py:34
  14.7 0.1 collective-permute-start.4
  14.8 0.5 collective-permute-start.5
  15.3 0.0 collective-permute-done.1.t1
  15.3 1.7 %shard_map.94 = (bf16[384,1152]{1,0:T(8,128)(2,1)S(1)}, bf16[1152,384]{1,0:T(8,128)(2,1)S(1)}, bf16[1152,384]{1,0:T(8,128)(2,1)S(1)}, bf16[288,384]{1,0:T(8,128)...) custom-call(f32[1]{0:T(128)S(6)} %copy.12.scale, ...), custom_call_target="tpu_custom_call" | custom-call | flops 1000 | bytes 1000 | tf_op jit(solution)/shard_map/pallas_call | solution.py:138
  17.0 0.0 collective-permute-done.5.f3_tail
  17.0 0.0 collective-permute-done.4.f3_head
  17.0 4.6 %shard_map.96 = (bf16[1152,384]{1,0:T(8,128)(2,1)S(1)}, bf16[384,1152]{1,0:T(8,128)(2,1)S(1)}, bf16[1152,384]{1,0:T(8,128)(2,1)S(1)}, bf16[288,384]{1,0:T(8,128)...) custom-call(f32[1]{0:T(128)S(6)} %copy.12.scale, ...), custom_call_target="tpu_custom_call" | custom-call | flops 1000 | bytes 1000 | tf_op jit(solution)/shard_map/pallas_call | solution.py:138
  21.7 2.0 %shard_map.97 = (bf16[192,1152]{1,0:T(8,128)(2,1)}, f32[8,128]{1,0:T(8,128)S(1)}) custom-call(f32[1]{0:T(128)S(6)} %copy.12.scale, bf16[192,1152]{1,0:T(8,128)(2,1)S(1)} %get-tuple-element.65.text, bf16[384,384]{1,0:T(8,128)(2,1)S(1)} %get-tuple-element.66.weights_near, bf16[384,384]{1,0:T(8,128)(2,1)S(1)} %get-tuple-element.70.weights_far, ...), custom_call_target="tpu_custom_call" | custom-call | flops 1000 | bytes 1000 | tf_op jit(solution)/shard_map/pallas_call | solution.py:138
  23.7 0.9 %collective-permute-done.2.text_unit.text_third = bf16[192,1152]{1,0:T(8,128)(2,1)S(1)} collective-permute-done((bf16[192,1152]{1,0:T(8,128)(2,1)S(1)}, bf16[192,1152]{1,0:T(8,128)(2,1)S(1)}, u32[]{:S(2)}, u32[]{:S(2)}) %collective-permute-start.2) | collective-permute-done | bytes 442400 | tf_op jit(solution)/shard_map/ppermute | solution.py:34
  24.6 0.0 collective-permute-start.6
  24.6 1.3 %shard_map.98 = (bf16[192,768]{1,0:T(8,128)(2,1)S(1)}, f32[288,384]{1,0:T(8,128)S(1)}, f32[288,384]{1,0:T(8,128)S(1)}, f32[1,768]{1,0:T(1,128)S(1)}) custom-call(f32[1]{0:T(128)S(6)} %copy.12.scale, f32[1]{0:T(128)S(6)} %copy.13.bias, bf16[192,1152]{1,0:T(8,128)(2,1)S(1)} %collective-permute-done.2.text_unit.text_third, ...), custom_call_target="tpu_custom_call" | custom-call | flops 1019215872 | bytes 3538944 | tf_op jit(solution)/shard_map/pallas_call | solution.py:138
  26.0 0.5 collective-permute-done.6.text_unit.text_fourth
  26.4 2.7 %shard_map.99 = (bf16[176,256]{1,0:T(8,128)(2,1)S(1)}, bf16[176,256]{1,0:T(8,128)(2,1)S(1)}, bf16[176,256]{1,0:T(8,128)(2,1)S(1)}, bf16[176,256]{1,0:T(8,128)(2,...) custom-call(f32[1]{0:T(128)S(6)} %copy.12.scale, f32[1]{0:T(128)S(6)} %copy.13.bias, ...), custom_call_target="tpu_custom_call" | custom-call | flops 2038431744 | bytes 7077888 | tf_op jit(solution)/shard_map/pallas_call | solution.py:138
  29.1 1.6 %collective-permute-start.7 = (bf16[176,256]{1,0:T(8,128)(2,1)S(1)}, bf16[176,256]{1,0:T(8,128)(2,1)S(1)}, u32[]{:S(2)}, u32[]{:S(2)}) collective-permute-start(bf16[176,256]{1,0:T(8,128)(2,1)S(1)} %get-tuple-element.95), channel_id=1, source_target_pairs={{0,1},{1,0},{2,3},{3,2},{4,5},{5,4},{6,7},{7,6},{8,9},{9,8},{10,11... | collective-permute-start | bytes 270344 | tf_op jit(solution)/shard_map/ppermute | solution.py:34
  30.7 0.5 collective-permute-start.8
  31.2 1.5 %collective-permute-start.9 = (bf16[176,256]{1,0:T(8,128)(2,1)S(1)}, bf16[176,256]{1,0:T(8,128)(2,1)S(1)}, u32[]{:S(2)}, u32[]{:S(2)}) collective-permute-start(bf16[176,256]{1,0:T(8,128)(2,1)S(1)} %get-tuple-element.97), channel_id=1, source_target_pairs={{0,1},{1,0},{2,3},{3,2},{4,5},{5,4},{6,7},{7,6},{8,9},{9,8},{10,11... | collective-permute-start | bytes 270344 | tf_op jit(solution)/shard_map/ppermute | solution.py:34
  32.8 1.9 %collective-permute-done.7.come = bf16[176,256]{1,0:T(8,128)(2,1)S(1)} collective-permute-done((bf16[176,256]{1,0:T(8,128)(2,1)S(1)}, bf16[176,256]{1,0:T(8,128)(2,1)S(1)}, u32[]{:S(2)}, u32[]{:S(2)}) %collective-permute-start.7) | collective-permute-done | bytes 90144 | tf_op jit(solution)/shard_map/ppermute | solution.py:34
  34.7 3.7 %collective-permute-start.11 = (bf16[176,256]{1,0:T(8,128)(2,1)S(1)}, bf16[176,256]{1,0:T(8,128)(2,1)S(1)}, u32[]{:S(2)}, u32[]{:S(2)}) collective-permute-start(bf16[176,256]{1,0:T(8,128)(2,1)S(1)} %shard_map.100.before), channel_id=1, source_target_pairs={{0,6},{1,7},{2,4},{3,5},{4,2},{5,3},{6,0},{7,1},{8,14},{9,15},{10,... | collective-permute-start | bytes 270344 | tf_op jit(solution)/shard_map/ppermute | solution.py:34
  38.3 0.0 collective-permute-done.8.come
  38.4 0.9 %collective-permute-start.10 = (bf16[176,256]{1,0:T(8,128)(2,1)S(1)}, bf16[176,256]{1,0:T(8,128)(2,1)S(1)}, u32[]{:S(2)}, u32[]{:S(2)}) collective-permute-start(bf16[176,256]{1,0:T(8,128)(2,1)S(1)} %shard_map.101.before), channel_id=1, source_target_pairs={{0,4},{1,5},{2,6},{3,7},{4,0},{5,1},{6,2},{7,3},{8,12},{9,13},{10,... | collective-permute-start | bytes 270344 | tf_op jit(solution)/shard_map/ppermute | solution.py:34
  39.2 0.0 collective-permute-done.9.come
  39.3 1.7 %collective-permute-start.12 = (bf16[176,256]{1,0:T(8,128)(2,1)S(1)}, bf16[176,256]{1,0:T(8,128)(2,1)S(1)}, u32[]{:S(2)}, u32[]{:S(2)}) collective-permute-start(bf16[176,256]{1,0:T(8,128)(2,1)S(1)} %shard_map.102.before), channel_id=1, source_target_pairs={{0,2},{1,3},{2,0},{3,1},{4,6},{5,7},{6,4},{7,5},{8,10},{9,11},{10,... | collective-permute-start | bytes 270344 | tf_op jit(solution)/shard_map/ppermute | solution.py:34
  40.9 1.5 %collective-permute-start.13 = (bf16[176,256]{1,0:T(8,128)(2,1)S(1)}, bf16[176,256]{1,0:T(8,128)(2,1)S(1)}, u32[]{:S(2)}, u32[]{:S(2)}) collective-permute-start(bf16[176,256]{1,0:T(8,128)(2,1)S(1)} %get-tuple-element.100), channel_id=1, source_target_pairs={{0,1},{1,0},{2,3},{3,2},{4,5},{5,4},{6,7},{7,6},{8,9},{9,8},{10,11... | collective-permute-start | bytes 270344 | tf_op jit(solution)/shard_map/ppermute | solution.py:34
  42.5 2.1 %shard_map.103 = (f32[192,1152]{1,0:T(8,128)S(1)}, f32[8,128]{1,0:T(8,128)S(1)}) custom-call(f32[1]{0:T(128)S(6)} %copy.12.scale, bf16[1152,1152]{1,0:T(8,128)(2,1)S(1)} %get-tuple-element.58.proj, bf16[384,1152]{1,0:T(8,128)(2,1)S(1)} %get-tuple-element.64.text_near, bf16[192,1152]{1,0:T(8,128)(2,1)S(1)} %collective-permute-done.2.text_unit.text_third, ...), custom_call_target="tpu_custom_call" | custom-call | flops 1000 | bytes 1000 | tf_op jit(solution)/shard_map/pallas_call | solution.py:138
  44.6 0.0 collective-permute-done.11.three_on
  44.6 0.6 %collective-permute-done.10.two_on = bf16[176,256]{1,0:T(8,128)(2,1)S(1)} collective-permute-done((bf16[176,256]{1,0:T(8,128)(2,1)S(1)}, bf16[176,256]{1,0:T(8,128)(2,1)S(1)}, u32[]{:S(2)}, u32[]{:S(2)}) %collective-permute-start.10) | collective-permute-done | bytes 90144 | tf_op jit(solution)/shard_map/ppermute | solution.py:34
  45.2 0.3 collective-permute-done.12.next_one
  45.5 0.0 collective-permute-done.13.come
  45.5 0.1 shard_map.106.before.own.refs_0_
  45.6 1.6 %collective-permute-start.14 = (bf16[176,256]{1,0:T(8,128)(2,1)S(1)}, bf16[176,256]{1,0:T(8,128)(2,1)S(1)}, u32[]{:S(2)}, u32[]{:S(2)}) collective-permute-start(bf16[176,256]{1,0:T(8,128)(2,1)S(1)} %shard_map.106.before.own.refs_0_), channel_id=1, source_target_pairs={{0,16},{8,24},{16,0},{24,8},{1,17},{9,25},{17,1},{25,9},{2,18},{10... | collective-permute-start | bytes 270344 | tf_op jit(solution)/shard_map/ppermute | solution.py:34
  47.2 0.0 collective-permute-start.15
  47.2 1.7 %shard_map.107 = (bf16[192,1152]{1,0:T(8,128)(2,1)}, f32[8,128]{1,0:T(8,128)S(1)}) custom-call(bf16[192,1152]{1,0:T(8,128)(2,1)S(1)} %get-tuple-element.56.features, f32[1,1152]{1,0:T(1,128)S(1)} %get-tuple-element.57.gain, f32[192,1152]{1,0:T(8,128)S(1)} %get-tuple-element.98.norm_back, bf16[176,256]{1,0:T(8,128)(2,1)S(1)} %shard_map.106.before.own.refs_0_), custom_call_target="tpu_custom_call" | custom-call | bytes 5308416 | tf_op jit(solution)/shard_map/pallas_call | solution.py:138
  48.9 1.3 %collective-permute-done.14.far.refs_2_ = bf16[176,256]{1,0:T(8,128)(2,1)S(1)} collective-permute-done((bf16[176,256]{1,0:T(8,128)(2,1)S(1)}, bf16[176,256]{1,0:T(8,128)(2,1)S(1)}, u32[]{:S(2)}, u32[]{:S(2)}) %collective-permute-start.14) | collective-permute-done | bytes 90144 | tf_op jit(solution)/shard_map/ppermute | solution.py:34
  50.2 0.0 collective-permute-start.16
  50.2 0.0 collective-permute-done.15.near.refs_1_
  50.2 0.8 %shard_map.108.begun = f32[144,1152]{1,0:T(8,128)} custom-call(f32[8,128]{1,0:T(8,128)S(1)} %get-tuple-element.104.before, bf16[176,256]{1,0:T(8,128)(2,1)S(1)} %shard_map.106.before.own.refs_0_, bf16[176,256]{1,0:T(8,128)(2,1)S(1)} %collective-permute-done.15.near.refs_1_, bf16[176,256]{1,0:T(8,128)(2,1)S(1)} %collective-permute-done.14.far.refs_2_), custom_call_target="tpu_custom_call" | custom-call | bytes 1327104 | tf_op jit(solution)/shard_map/pallas_call | solution.py:663
  51.0 0.5 collective-permute-done.16.refs_3_
  51.5 1.4 %shard_map.109 = (f32[144,1152]{1,0:T(8,128)}, f32[1152]{0:T(1024)}) custom-call(f32[144,1152]{1,0:T(8,128)} %shard_map.108.begun, bf16[176,256]{1,0:T(8,128)(2,1)S(1)} %shard_map.106.before.own.refs_0_, bf16[176,256]{1,0:T(8,128)(2,1)S(1)} %collective-permute-done.15.near.refs_1_, ...), custom_call_target="tpu_custom_call", output_to_operand_aliasing={{0}: (0, {})} | custom-call | bytes 331776 | tf_op jit(solution)/shard_map/pallas_call | solution.py:672
  (9 shorter events, 0.2 us)
Async XLA Ops:
  0.6 4.4 %collective-permute-start = (bf16[192,1152]{1,0:T(8,128)(2,1)}, bf16[192,1152]{1,0:T(8,128)(2,1)S(1)}, u32[]{:S(2)}, u32[]{:S(2)}) collective-permute-start(bf16[192,1152]{1,0:T(8,128)(2,1)} %bitcast.5), channel_id=1, source_target_pairs={{0,8},{8,0},{16,24},{24,16},{1,9},{9,1},{17,25},{25,17},{2,10},{10... | collective-permute-start | bytes 1327112 | tf_op jit(solution)/shard_map/ppermute | solution.py:34
  1.2 13.5 %collective-permute-start.3 = (bf16[192,1152]{1,0:T(8,128)(2,1)}, bf16[192,1152]{1,0:T(8,128)(2,1)S(1)}, u32[]{:S(2)}, u32[]{:S(2)}) collective-permute-start(bf16[192,1152]{1,0:T(8,128)(2,1)} %bitcast.6), channel_id=1, source_target_pairs={{0,16},{8,24},{16,0},{24,8},{1,17},{9,25},{17,1},{25,9},{2,18},{10... | collective-permute-start | bytes 1327112 | tf_op jit(solution)/shard_map/ppermute | solution.py:34
  5.0 1.0 %copy-start = (bf16[192,1,1152]{2,0,1:T(8,128)(2,1)S(1)}, bf16[192,1,1152]{2,0,1:T(8,128)(2,1)}, u32[]{:S(2)}) copy-start(bf16[192,1,1152]{2,0,1:T(8,128)(2,1)} %param.7) | copy-start | bytes 1327108
  6.0 1.0 %copy-start.1 = (bf16[192,1,1152]{2,0,1:T(8,128)(2,1)S(1)}, bf16[192,1,1152]{2,0,1:T(8,128)(2,1)}, u32[]{:S(2)}) copy-start(bf16[192,1,1152]{2,0,1:T(8,128)(2,1)} %param.6) | copy-start | bytes 1327108
  7.1 0.7 %copy-start.2 = (f32[1152]{0:T(1024)S(1)}, f32[1152]{0:T(1024)}, u32[]{:S(2)}) copy-start(f32[1152]{0:T(1024)} %gain_line.1) | copy-start | bytes 13828
  12.0 3.3 %collective-permute-start.1 = (bf16[192,1152]{1,0:T(8,128)(2,1)S(1)}, bf16[192,1152]{1,0:T(8,128)(2,1)S(1)}, u32[]{:S(2)}, u32[]{:S(2)}) collective-permute-start(bf16[192,1152]{1,0:T(8,128)(2,1)S(1)} %get-tuple-element.62.text_own), channel_id=1, source_target_pairs={{0,8},{8,0},{16,24},{24,16},{1,9},{9,1},{17,25},{25,17},{2,10},{10... | collective-permute-start | bytes 1327112 | tf_op jit(solution)/shard_map/ppermute | solution.py:34
  12.2 12.4 %collective-permute-start.2 = (bf16[192,1152]{1,0:T(8,128)(2,1)S(1)}, bf16[192,1152]{1,0:T(8,128)(2,1)S(1)}, u32[]{:S(2)}, u32[]{:S(2)}) collective-permute-start(bf16[192,1152]{1,0:T(8,128)(2,1)S(1)} %get-tuple-element.62.text_own), channel_id=1, source_target_pairs={{0,16},{8,24},{16,0},{24,8},{1,17},{9,25},{17,1},{25,9},{2,18},{10... | collective-permute-start | bytes 1327112 | tf_op jit(solution)/shard_map/ppermute | solution.py:34
  14.7 2.3 %collective-permute-start.4 = (bf16[160,1152]{1,0:T(8,128)(2,1)S(1)}, bf16[160,1152]{1,0:T(8,128)(2,1)S(1)}, u32[]{:S(2)}, u32[]{:S(2)}) collective-permute-start(bf16[160,1152]{1,0:T(8,128)(2,1)S(1)} %get-tuple-element.67), channel_id=1, source_target_pairs={{0,8},{8,0},{16,24},{24,16},{1,9},{9,1},{17,25},{25,17},{2,10},{10... | collective-permute-start | bytes 1105928 | tf_op jit(solution)/shard_map/ppermute | solution.py:34
  14.8 2.2 %collective-permute-start.5 = (bf16[32,1152]{1,0:T(8,128)(2,1)S(1)}, bf16[32,1152]{1,0:T(8,128)(2,1)S(1)}, u32[]{:S(2)}, u32[]{:S(2)}) collective-permute-start(bf16[32,1152]{1,0:T(8,128)(2,1)S(1)} %get-tuple-element.68), channel_id=1, source_target_pairs={{0,8},{8,0},{16,24},{24,16},{1,9},{9,1},{17,25},{25,17},{2,10},{10... | collective-permute-start | bytes 221192 | tf_op jit(solution)/shard_map/ppermute | solution.py:34
  24.6 1.8 %collective-permute-start.6 = (bf16[192,1152]{1,0:T(8,128)(2,1)S(1)}, bf16[192,1152]{1,0:T(8,128)(2,1)S(1)}, u32[]{:S(2)}, u32[]{:S(2)}) collective-permute-start(bf16[192,1152]{1,0:T(8,128)(2,1)S(1)} %collective-permute-done.2.text_unit.text_third), channel_id=1, source_target_pairs={{0,8},{8,0},{16,24},{24,16},{1,9},{9,1},{17,25},{25,17},{2,10},{10... | collective-permute-start | bytes 1327112 | tf_op jit(solution)/shard_map/ppermute | solution.py:34
  29.1 5.5 %collective-permute-start.7 = (bf16[176,256]{1,0:T(8,128)(2,1)S(1)}, bf16[176,256]{1,0:T(8,128)(2,1)S(1)}, u32[]{:S(2)}, u32[]{:S(2)}) collective-permute-start(bf16[176,256]{1,0:T(8,128)(2,1)S(1)} %get-tuple-element.95), channel_id=1, source_target_pairs={{0,1},{1,0},{2,3},{3,2},{4,5},{5,4},{6,7},{7,6},{8,9},{9,8},{10,11... | collective-permute-start | bytes 270344 | tf_op jit(solution)/shard_map/ppermute | solution.py:34
  30.7 7.6 %collective-permute-start.8 = (bf16[176,256]{1,0:T(8,128)(2,1)S(1)}, bf16[176,256]{1,0:T(8,128)(2,1)S(1)}, u32[]{:S(2)}, u32[]{:S(2)}) collective-permute-start(bf16[176,256]{1,0:T(8,128)(2,1)S(1)} %get-tuple-element.96), channel_id=1, source_target_pairs={{0,1},{1,0},{2,3},{3,2},{4,5},{5,4},{6,7},{7,6},{8,9},{9,8},{10,11... | collective-permute-start | bytes 270344 | tf_op jit(solution)/shard_map/ppermute | solution.py:34
  31.2 8.0 %collective-permute-start.9 = (bf16[176,256]{1,0:T(8,128)(2,1)S(1)}, bf16[176,256]{1,0:T(8,128)(2,1)S(1)}, u32[]{:S(2)}, u32[]{:S(2)}) collective-permute-start(bf16[176,256]{1,0:T(8,128)(2,1)S(1)} %get-tuple-element.97), channel_id=1, source_target_pairs={{0,1},{1,0},{2,3},{3,2},{4,5},{5,4},{6,7},{7,6},{8,9},{9,8},{10,11... | collective-permute-start | bytes 270344 | tf_op jit(solution)/shard_map/ppermute | solution.py:34
  34.7 9.9 %collective-permute-start.11 = (bf16[176,256]{1,0:T(8,128)(2,1)S(1)}, bf16[176,256]{1,0:T(8,128)(2,1)S(1)}, u32[]{:S(2)}, u32[]{:S(2)}) collective-permute-start(bf16[176,256]{1,0:T(8,128)(2,1)S(1)} %shard_map.100.before), channel_id=1, source_target_pairs={{0,6},{1,7},{2,4},{3,5},{4,2},{5,3},{6,0},{7,1},{8,14},{9,15},{10,... | collective-permute-start | bytes 270344 | tf_op jit(solution)/shard_map/ppermute | solution.py:34
  38.4 6.8 %collective-permute-start.10 = (bf16[176,256]{1,0:T(8,128)(2,1)S(1)}, bf16[176,256]{1,0:T(8,128)(2,1)S(1)}, u32[]{:S(2)}, u32[]{:S(2)}) collective-permute-start(bf16[176,256]{1,0:T(8,128)(2,1)S(1)} %shard_map.101.before), channel_id=1, source_target_pairs={{0,4},{1,5},{2,6},{3,7},{4,0},{5,1},{6,2},{7,3},{8,12},{9,13},{10,... | collective-permute-start | bytes 270344 | tf_op jit(solution)/shard_map/ppermute | solution.py:34
  39.3 6.2 %collective-permute-start.12 = (bf16[176,256]{1,0:T(8,128)(2,1)S(1)}, bf16[176,256]{1,0:T(8,128)(2,1)S(1)}, u32[]{:S(2)}, u32[]{:S(2)}) collective-permute-start(bf16[176,256]{1,0:T(8,128)(2,1)S(1)} %shard_map.102.before), channel_id=1, source_target_pairs={{0,2},{1,3},{2,0},{3,1},{4,6},{5,7},{6,4},{7,5},{8,10},{9,11},{10,... | collective-permute-start | bytes 270344 | tf_op jit(solution)/shard_map/ppermute | solution.py:34
  40.9 4.6 %collective-permute-start.13 = (bf16[176,256]{1,0:T(8,128)(2,1)S(1)}, bf16[176,256]{1,0:T(8,128)(2,1)S(1)}, u32[]{:S(2)}, u32[]{:S(2)}) collective-permute-start(bf16[176,256]{1,0:T(8,128)(2,1)S(1)} %get-tuple-element.100), channel_id=1, source_target_pairs={{0,1},{1,0},{2,3},{3,2},{4,5},{5,4},{6,7},{7,6},{8,9},{9,8},{10,11... | collective-permute-start | bytes 270344 | tf_op jit(solution)/shard_map/ppermute | solution.py:34
  45.6 4.6 %collective-permute-start.14 = (bf16[176,256]{1,0:T(8,128)(2,1)S(1)}, bf16[176,256]{1,0:T(8,128)(2,1)S(1)}, u32[]{:S(2)}, u32[]{:S(2)}) collective-permute-start(bf16[176,256]{1,0:T(8,128)(2,1)S(1)} %shard_map.106.before.own.refs_0_), channel_id=1, source_target_pairs={{0,16},{8,24},{16,0},{24,8},{1,17},{9,25},{17,1},{25,9},{2,18},{10... | collective-permute-start | bytes 270344 | tf_op jit(solution)/shard_map/ppermute | solution.py:34
  47.2 3.0 %collective-permute-start.15 = (bf16[176,256]{1,0:T(8,128)(2,1)S(1)}, bf16[176,256]{1,0:T(8,128)(2,1)S(1)}, u32[]{:S(2)}, u32[]{:S(2)}) collective-permute-start(bf16[176,256]{1,0:T(8,128)(2,1)S(1)} %shard_map.106.before.own.refs_0_), channel_id=1, source_target_pairs={{0,8},{8,0},{16,24},{24,16},{1,9},{9,1},{17,25},{25,17},{2,10},{10... | collective-permute-start | bytes 270344 | tf_op jit(solution)/shard_map/ppermute | solution.py:34
  50.2 1.3 %collective-permute-start.16 = (bf16[176,256]{1,0:T(8,128)(2,1)S(1)}, bf16[176,256]{1,0:T(8,128)(2,1)S(1)}, u32[]{:S(2)}, u32[]{:S(2)}) collective-permute-start(bf16[176,256]{1,0:T(8,128)(2,1)S(1)} %collective-permute-done.14.far.refs_2_), channel_id=1, source_target_pairs={{0,8},{8,0},{16,24},{24,16},{1,9},{9,1},{17,25},{25,17},{2,10},{10... | collective-permute-start | bytes 270344 | tf_op jit(solution)/shard_map/ppermute | solution.py:34

commit v26 on v23

--- a/solution.py
+++ b/solution.py
@@ -598,20 +598,20 @@
         inverse_near, inverse_far, turned_near, turned_far, proj_columns, gain_row,
     )
     across_three, across_two, across_next, across_own, keep, weights_fourth = outs
+    come_two = send(across_two, "rep", lambda p: p ^ 1)
     come_three = send(across_three, "rep", lambda p: p ^ 1)
-    come_two = send(across_two, "rep", lambda p: p ^ 1)
     come_next = send(across_next, "rep", lambda p: p ^ 1)
     come_own = send(across_own, "rep", lambda p: p ^ 1)
+    (two_sum,) = call(functools.partial(one_sum_body, 2), [(packet, BF16)], flops=1000, moved=1000)(
+        keep, keep, come_two
+    )
+    two_on = send(two_sum, "rep", lambda p: p ^ 4)
     (three_sum,) = call(functools.partial(one_sum_body, 3), [(packet, BF16)], flops=1000, moved=1000)(
-        keep, keep, come_three
+        two_sum, keep, come_three
     )
     three_on = send(three_sum, "rep", lambda p: p ^ 6)
-    (two_sum,) = call(functools.partial(one_sum_body, 2), [(packet, BF16)], flops=1000, moved=1000)(
-        three_sum, keep, come_two
-    )
-    two_on = send(two_sum, "rep", lambda p: p ^ 4)
     (next_sum,) = call(functools.partial(one_sum_body, 1), [(packet, BF16)], flops=1000, moved=1000)(
-        two_sum, keep, come_next
+        three_sum, keep, come_next
     )
     next_one = send(next_sum, "rep", lambda p: p ^ 2)
     norm_back, token = call(

time: 52.8 us -> 52.5 us (level)
    ppermute x17, starting transfers between devices: 17.4 us -> 16.9 us  [send(): return lax.ppermute(value, axis, [(p, target(p)) for p in range(count)])]
where the time goes in v26:
time: 52.5 us; the launch traced here: 52.2 us
  Pallas kernels  21.6 us (41%)
  starting transfers between devices  16.9 us (32%)
  waiting for transfers between devices  8.87 us (17%)
  local copies, waits for them, and re-layouts  2.72 us (5%)
  between operations  2.08 us (4%)
    pallas_call x16, Pallas kernels, run(): pl.pallas_call(body, out_shape=[jax.ShapeDtypeStruct(shape, kind) for sha...  21.6 us
    ppermute x17, starting transfers between devices, send(): return lax.ppermute(value, axis, [(p, target(p)) for p in range(count)])  16.9 us
    ppermute x17, waiting for transfers between devices, send(): return lax.ppermute(value, axis, [(p, target(p)) for p in range(count)])  8.87 us
    unnamed x6, local copies, waits for them, and re-layouts  2.72 us
  transfers between devices with their start and end apart: 17, of which 8 were waited for; matrix products, arithmetic and copies ran while one was open for 0% of the time, Pallas kernels for 34%

profile of v26, /device:TPU:0, one launch (start us, length us, event | category | flops | bytes accessed | tf_op | source)
XLA Modules:
  0.0 52.2 jit_solution(14891396721711990723)
XLA Ops:
  0.6 0.5 collective-permute-start
  1.2 2.6 %collective-permute-start.3 = (bf16[192,1152]{1,0:T(8,128)(2,1)}, bf16[192,1152]{1,0:T(8,128)(2,1)S(1)}, u32[]{:S(2)}, u32[]{:S(2)}) collective-permute-start(bf16[192,1152]{1,0:T(8,128)(2,1)} %bitcast.6), channel_id=1, source_target_pairs={{0,16},{8,24},{16,0},{24,8},{1,17},{9,25},{17,1},{25,9},{2,18},{10... | collective-permute-start | bytes 1327112 | tf_op jit(solution)/shard_map/ppermute | solution.py:34
  5.0 0.0 collective-permute-done.f1
  5.0 0.0 copy-start
  5.0 1.0 %copy-done = bf16[192,1,1152]{2,0,1:T(8,128)(2,1)S(1)} copy-done((bf16[192,1,1152]{2,0,1:T(8,128)(2,1)S(1)}, bf16[192,1,1152]{2,0,1:T(8,128)(2,1)}, u32[]{:S(2)}) %copy-start) | copy-done | bytes 442392
  6.0 1.0 %copy-done.1 = bf16[192,1,1152]{2,0,1:T(8,128)(2,1)S(1)} copy-done((bf16[192,1,1152]{2,0,1:T(8,128)(2,1)S(1)}, bf16[192,1,1152]{2,0,1:T(8,128)(2,1)}, u32[]{:S(2)}) %copy-start.1) | copy-done | bytes 442392
  7.1 0.7 %copy-done.2 = f32[1152]{0:T(1024)S(1)} copy-done((f32[1152]{0:T(1024)S(1)}, f32[1152]{0:T(1024)}, u32[]{:S(2)}) %copy-start.2) | copy-done | bytes 4632
  7.7 4.2 %shard_map.93 = (bf16[192,1152]{1,0:T(8,128)(2,1)S(1)}, bf16[1152,1152]{1,0:T(8,128)(2,1)S(1)}, bf16[192,1152]{1,0:T(8,128)(2,1)S(1)}, f32[1,1152]{1,0:T(1,128)S...) custom-call(f32[1]{0:T(128)S(6)} %copy.10.scale, ...), custom_call_target="tpu_custom_call" | custom-call | flops 1019215872 | bytes 3538944 | tf_op jit(solution)/shard_map/pallas_call | solution.py:138
  12.0 0.2 collective-permute-start.1
  12.2 0.6 %collective-permute-start.2 = (bf16[192,1152]{1,0:T(8,128)(2,1)S(1)}, bf16[192,1152]{1,0:T(8,128)(2,1)S(1)}, u32[]{:S(2)}, u32[]{:S(2)}) collective-permute-start(bf16[192,1152]{1,0:T(8,128)(2,1)S(1)} %get-tuple-element.62.text_own), channel_id=1, source_target_pairs={{0,16},{8,24},{16,0},{24,8},{1,17},{9,25},{17,1},{25,9},{2,18},{10... | collective-permute-start | bytes 1327112 | tf_op jit(solution)/shard_map/ppermute | solution.py:34
  12.8 1.9 %collective-permute-done.3.f2 = bf16[192,1152]{1,0:T(8,128)(2,1)S(1)} collective-permute-done((bf16[192,1152]{1,0:T(8,128)(2,1)}, bf16[192,1152]{1,0:T(8,128)(2,1)S(1)}, u32[]{:S(2)}, u32[]{:S(2)}) %collective-permute-start.3) | collective-permute-done | bytes 442400 | tf_op jit(solution)/shard_map/ppermute | solution.py:34
  14.7 0.1 collective-permute-start.4
  14.8 0.5 collective-permute-start.5
  15.3 0.0 collective-permute-done.1.t1
  15.3 1.7 %shard_map.94 = (bf16[384,1152]{1,0:T(8,128)(2,1)S(1)}, bf16[1152,384]{1,0:T(8,128)(2,1)S(1)}, bf16[1152,384]{1,0:T(8,128)(2,1)S(1)}, bf16[288,384]{1,0:T(8,128)...) custom-call(f32[1]{0:T(128)S(6)} %copy.10.scale, ...), custom_call_target="tpu_custom_call" | custom-call | flops 1000 | bytes 1000 | tf_op jit(solution)/shard_map/pallas_call | solution.py:138
  17.0 0.0 collective-permute-done.5.f3_tail
  17.0 0.0 collective-permute-done.4.f3_head
  17.0 4.6 %shard_map.96 = (bf16[1152,384]{1,0:T(8,128)(2,1)S(1)}, bf16[384,1152]{1,0:T(8,128)(2,1)S(1)}, bf16[1152,384]{1,0:T(8,128)(2,1)S(1)}, bf16[288,384]{1,0:T(8,128)...) custom-call(f32[1]{0:T(128)S(6)} %copy.10.scale, ...), custom_call_target="tpu_custom_call" | custom-call | flops 1000 | bytes 1000 | tf_op jit(solution)/shard_map/pallas_call | solution.py:138
  21.7 2.0 %shard_map.97 = (bf16[192,1152]{1,0:T(8,128)(2,1)}, f32[8,128]{1,0:T(8,128)S(1)}) custom-call(f32[1]{0:T(128)S(6)} %copy.10.scale, bf16[192,1152]{1,0:T(8,128)(2,1)S(1)} %get-tuple-element.65.text, bf16[384,384]{1,0:T(8,128)(2,1)S(1)} %get-tuple-element.66.weights_near, bf16[384,384]{1,0:T(8,128)(2,1)S(1)} %get-tuple-element.70.weights_far, ...), custom_call_target="tpu_custom_call" | custom-call | flops 1000 | bytes 1000 | tf_op jit(solution)/shard_map/pallas_call | solution.py:138
  23.7 0.9 %collective-permute-done.2.text_unit.text_third = bf16[192,1152]{1,0:T(8,128)(2,1)S(1)} collective-permute-done((bf16[192,1152]{1,0:T(8,128)(2,1)S(1)}, bf16[192,1152]{1,0:T(8,128)(2,1)S(1)}, u32[]{:S(2)}, u32[]{:S(2)}) %collective-permute-start.2) | collective-permute-done | bytes 442400 | tf_op jit(solution)/shard_map/ppermute | solution.py:34
  24.6 0.0 collective-permute-start.6
  24.6 1.3 %shard_map.98 = (bf16[192,768]{1,0:T(8,128)(2,1)S(1)}, f32[288,384]{1,0:T(8,128)S(1)}, f32[288,384]{1,0:T(8,128)S(1)}, f32[1,768]{1,0:T(1,128)S(1)}) custom-call(f32[1]{0:T(128)S(6)} %copy.10.scale, f32[1]{0:T(128)S(6)} %copy.11.bias, bf16[192,1152]{1,0:T(8,128)(2,1)S(1)} %collective-permute-done.2.text_unit.text_third, ...), custom_call_target="tpu_custom_call" | custom-call | flops 1019215872 | bytes 3538944 | tf_op jit(solution)/shard_map/pallas_call | solution.py:138
  26.0 0.5 collective-permute-done.6.text_unit.text_fourth
  26.4 2.7 %shard_map.99 = (bf16[176,256]{1,0:T(8,128)(2,1)S(1)}, bf16[176,256]{1,0:T(8,128)(2,1)S(1)}, bf16[176,256]{1,0:T(8,128)(2,1)S(1)}, bf16[176,256]{1,0:T(8,128)(2,...) custom-call(f32[1]{0:T(128)S(6)} %copy.10.scale, f32[1]{0:T(128)S(6)} %copy.11.bias, ...), custom_call_target="tpu_custom_call" | custom-call | flops 2038431744 | bytes 7077888 | tf_op jit(solution)/shard_map/pallas_call | solution.py:138
  29.1 1.6 %collective-permute-start.7 = (bf16[176,256]{1,0:T(8,128)(2,1)S(1)}, bf16[176,256]{1,0:T(8,128)(2,1)S(1)}, u32[]{:S(2)}, u32[]{:S(2)}) collective-permute-start(bf16[176,256]{1,0:T(8,128)(2,1)S(1)} %get-tuple-element.95), channel_id=1, source_target_pairs={{0,1},{1,0},{2,3},{3,2},{4,5},{5,4},{6,7},{7,6},{8,9},{9,8},{10,11... | collective-permute-start | bytes 270344 | tf_op jit(solution)/shard_map/ppermute | solution.py:34
  30.7 0.5 collective-permute-start.8
  31.2 1.5 %collective-permute-start.9 = (bf16[176,256]{1,0:T(8,128)(2,1)S(1)}, bf16[176,256]{1,0:T(8,128)(2,1)S(1)}, u32[]{:S(2)}, u32[]{:S(2)}) collective-permute-start(bf16[176,256]{1,0:T(8,128)(2,1)S(1)} %get-tuple-element.97), channel_id=1, source_target_pairs={{0,1},{1,0},{2,3},{3,2},{4,5},{5,4},{6,7},{7,6},{8,9},{9,8},{10,11... | collective-permute-start | bytes 270344 | tf_op jit(solution)/shard_map/ppermute | solution.py:34
  32.8 1.9 %collective-permute-done.7.come = bf16[176,256]{1,0:T(8,128)(2,1)S(1)} collective-permute-done((bf16[176,256]{1,0:T(8,128)(2,1)S(1)}, bf16[176,256]{1,0:T(8,128)(2,1)S(1)}, u32[]{:S(2)}, u32[]{:S(2)}) %collective-permute-start.7) | collective-permute-done | bytes 90144 | tf_op jit(solution)/shard_map/ppermute | solution.py:34
  34.7 2.6 %collective-permute-start.10 = (bf16[176,256]{1,0:T(8,128)(2,1)S(1)}, bf16[176,256]{1,0:T(8,128)(2,1)S(1)}, u32[]{:S(2)}, u32[]{:S(2)}) collective-permute-start(bf16[176,256]{1,0:T(8,128)(2,1)S(1)} %shard_map.100.before), channel_id=1, source_target_pairs={{0,4},{1,5},{2,6},{3,7},{4,0},{5,1},{6,2},{7,3},{8,12},{9,13},{10,... | collective-permute-start | bytes 270344 | tf_op jit(solution)/shard_map/ppermute | solution.py:34
  37.3 0.0 collective-permute-done.8.come
  37.4 2.9 %collective-permute-start.11 = (bf16[176,256]{1,0:T(8,128)(2,1)S(1)}, bf16[176,256]{1,0:T(8,128)(2,1)S(1)}, u32[]{:S(2)}, u32[]{:S(2)}) collective-permute-start(bf16[176,256]{1,0:T(8,128)(2,1)S(1)} %shard_map.101.before), channel_id=1, source_target_pairs={{0,6},{1,7},{2,4},{3,5},{4,2},{5,3},{6,0},{7,1},{8,14},{9,15},{10,... | collective-permute-start | bytes 270344 | tf_op jit(solution)/shard_map/ppermute | solution.py:34
  40.3 0.0 collective-permute-done.9.come
  40.3 0.1 collective-permute-start.12
  40.4 1.6 %collective-permute-start.13 = (bf16[176,256]{1,0:T(8,128)(2,1)S(1)}, bf16[176,256]{1,0:T(8,128)(2,1)S(1)}, u32[]{:S(2)}, u32[]{:S(2)}) collective-permute-start(bf16[176,256]{1,0:T(8,128)(2,1)S(1)} %get-tuple-element.100), channel_id=1, source_target_pairs={{0,1},{1,0},{2,3},{3,2},{4,5},{5,4},{6,7},{7,6},{8,9},{9,8},{10,11... | collective-permute-start | bytes 270344 | tf_op jit(solution)/shard_map/ppermute | solution.py:34
  42.0 2.1 %shard_map.103 = (f32[192,1152]{1,0:T(8,128)S(1)}, f32[8,128]{1,0:T(8,128)S(1)}) custom-call(f32[1]{0:T(128)S(6)} %copy.10.scale, bf16[1152,1152]{1,0:T(8,128)(2,1)S(1)} %get-tuple-element.58.proj, bf16[384,1152]{1,0:T(8,128)(2,1)S(1)} %get-tuple-element.64.text_near, bf16[192,1152]{1,0:T(8,128)(2,1)S(1)} %collective-permute-done.2.text_unit.text_third, ...), custom_call_target="tpu_custom_call" | custom-call | flops 1000 | bytes 1000 | tf_op jit(solution)/shard_map/pallas_call | solution.py:138
  44.1 0.0 collective-permute-done.10.two_on
  44.1 0.2 collective-permute-done.11.three_on
  44.3 0.9 %collective-permute-done.12.next_one = bf16[176,256]{1,0:T(8,128)(2,1)S(1)} collective-permute-done((bf16[176,256]{1,0:T(8,128)(2,1)S(1)}, bf16[176,256]{1,0:T(8,128)(2,1)S(1)}, u32[]{:S(2)}, u32[]{:S(2)}) %collective-permute-start.12) | collective-permute-done | bytes 90144 | tf_op jit(solution)/shard_map/ppermute | solution.py:34
  45.2 0.0 collective-permute-done.13.come
  45.2 0.1 shard_map.106.before.refs_0_
  45.3 1.5 %collective-permute-start.14 = (bf16[176,256]{1,0:T(8,128)(2,1)S(1)}, bf16[176,256]{1,0:T(8,128)(2,1)S(1)}, u32[]{:S(2)}, u32[]{:S(2)}) collective-permute-start(bf16[176,256]{1,0:T(8,128)(2,1)S(1)} %shard_map.106.before.refs_0_), channel_id=1, source_target_pairs={{0,16},{8,24},{16,0},{24,8},{1,17},{9,25},{17,1},{25,9},{2,18},{10... | collective-permute-start | bytes 270344 | tf_op jit(solution)/shard_map/ppermute | solution.py:34
  46.8 0.0 collective-permute-start.15
  46.8 1.7 %shard_map.107 = (bf16[192,1152]{1,0:T(8,128)(2,1)}, f32[8,128]{1,0:T(8,128)S(1)}) custom-call(bf16[192,1152]{1,0:T(8,128)(2,1)S(1)} %get-tuple-element.56.features, f32[1,1152]{1,0:T(1,128)S(1)} %get-tuple-element.57.gain, f32[192,1152]{1,0:T(8,128)S(1)} %get-tuple-element.98.norm_back, bf16[176,256]{1,0:T(8,128)(2,1)S(1)} %shard_map.106.before.refs_0_), custom_call_target="tpu_custom_call" | custom-call | bytes 5308416 | tf_op jit(solution)/shard_map/pallas_call | solution.py:138
  48.6 1.3 %collective-permute-done.14.refs_2_ = bf16[176,256]{1,0:T(8,128)(2,1)S(1)} collective-permute-done((bf16[176,256]{1,0:T(8,128)(2,1)S(1)}, bf16[176,256]{1,0:T(8,128)(2,1)S(1)}, u32[]{:S(2)}, u32[]{:S(2)}) %collective-permute-start.14) | collective-permute-done | bytes 90144 | tf_op jit(solution)/shard_map/ppermute | solution.py:34
  49.9 0.0 collective-permute-start.16
  49.9 0.0 collective-permute-done.15.refs_1_
  49.9 1.3 %collective-permute-done.16.refs_3_ = bf16[176,256]{1,0:T(8,128)(2,1)S(1)} collective-permute-done((bf16[176,256]{1,0:T(8,128)(2,1)S(1)}, bf16[176,256]{1,0:T(8,128)(2,1)S(1)}, u32[]{:S(2)}, u32[]{:S(2)}) %collective-permute-start.16) | collective-permute-done | bytes 90144 | tf_op jit(solution)/shard_map/ppermute | solution.py:34
  51.2 1.0 %shard_map.108 = (f32[144,1152]{1,0:T(8,128)}, f32[1152]{0:T(1024)}) custom-call(f32[8,128]{1,0:T(8,128)S(1)} %get-tuple-element.104.before, bf16[176,256]{1,0:T(8,128)(2,1)S(1)} %shard_map.106.before.refs_0_, bf16[176,256]{1,0:T(8,128)(2,1)S(1)} %collective-permute-done.15.refs_1_, bf16[176,256]{1,0:T(8,128)(2,1)S(1)} %collective-permute-done.14.refs_2_, ...), custom_call_target="tpu_custom_call" | custom-call | bytes 1327104 | tf_op jit(solution)/shard_map/pallas_call | solution.py:138
  (8 shorter events, 0.2 us)
Async XLA Ops:
  0.6 4.4 %collective-permute-start = (bf16[192,1152]{1,0:T(8,128)(2,1)}, bf16[192,1152]{1,0:T(8,128)(2,1)S(1)}, u32[]{:S(2)}, u32[]{:S(2)}) collective-permute-start(bf16[192,1152]{1,0:T(8,128)(2,1)} %bitcast.5), channel_id=1, source_target_pairs={{0,8},{8,0},{16,24},{24,16},{1,9},{9,1},{17,25},{25,17},{2,10},{10... | collective-permute-start | bytes 1327112 | tf_op jit(solution)/shard_map/ppermute | solution.py:34
  1.2 13.5 %collective-permute-start.3 = (bf16[192,1152]{1,0:T(8,128)(2,1)}, bf16[192,1152]{1,0:T(8,128)(2,1)S(1)}, u32[]{:S(2)}, u32[]{:S(2)}) collective-permute-start(bf16[192,1152]{1,0:T(8,128)(2,1)} %bitcast.6), channel_id=1, source_target_pairs={{0,16},{8,24},{16,0},{24,8},{1,17},{9,25},{17,1},{25,9},{2,18},{10... | collective-permute-start | bytes 1327112 | tf_op jit(solution)/shard_map/ppermute | solution.py:34
  5.0 1.0 %copy-start = (bf16[192,1,1152]{2,0,1:T(8,128)(2,1)S(1)}, bf16[192,1,1152]{2,0,1:T(8,128)(2,1)}, u32[]{:S(2)}) copy-start(bf16[192,1,1152]{2,0,1:T(8,128)(2,1)} %param.7) | copy-start | bytes 1327108
  6.0 1.0 %copy-start.1 = (bf16[192,1,1152]{2,0,1:T(8,128)(2,1)S(1)}, bf16[192,1,1152]{2,0,1:T(8,128)(2,1)}, u32[]{:S(2)}) copy-start(bf16[192,1,1152]{2,0,1:T(8,128)(2,1)} %param.6) | copy-start | bytes 1327108
  7.1 0.7 %copy-start.2 = (f32[1152]{0:T(1024)S(1)}, f32[1152]{0:T(1024)}, u32[]{:S(2)}) copy-start(f32[1152]{0:T(1024)} %gain_line.1) | copy-start | bytes 13828
  12.0 3.3 %collective-permute-start.1 = (bf16[192,1152]{1,0:T(8,128)(2,1)S(1)}, bf16[192,1152]{1,0:T(8,128)(2,1)S(1)}, u32[]{:S(2)}, u32[]{:S(2)}) collective-permute-start(bf16[192,1152]{1,0:T(8,128)(2,1)S(1)} %get-tuple-element.62.text_own), channel_id=1, source_target_pairs={{0,8},{8,0},{16,24},{24,16},{1,9},{9,1},{17,25},{25,17},{2,10},{10... | collective-permute-start | bytes 1327112 | tf_op jit(solution)/shard_map/ppermute | solution.py:34
  12.2 12.4 %collective-permute-start.2 = (bf16[192,1152]{1,0:T(8,128)(2,1)S(1)}, bf16[192,1152]{1,0:T(8,128)(2,1)S(1)}, u32[]{:S(2)}, u32[]{:S(2)}) collective-permute-start(bf16[192,1152]{1,0:T(8,128)(2,1)S(1)} %get-tuple-element.62.text_own), channel_id=1, source_target_pairs={{0,16},{8,24},{16,0},{24,8},{1,17},{9,25},{17,1},{25,9},{2,18},{10... | collective-permute-start | bytes 1327112 | tf_op jit(solution)/shard_map/ppermute | solution.py:34
  14.7 2.3 %collective-permute-start.4 = (bf16[160,1152]{1,0:T(8,128)(2,1)S(1)}, bf16[160,1152]{1,0:T(8,128)(2,1)S(1)}, u32[]{:S(2)}, u32[]{:S(2)}) collective-permute-start(bf16[160,1152]{1,0:T(8,128)(2,1)S(1)} %get-tuple-element.67), channel_id=1, source_target_pairs={{0,8},{8,0},{16,24},{24,16},{1,9},{9,1},{17,25},{25,17},{2,10},{10... | collective-permute-start | bytes 1105928 | tf_op jit(solution)/shard_map/ppermute | solution.py:34
  14.8 2.2 %collective-permute-start.5 = (bf16[32,1152]{1,0:T(8,128)(2,1)S(1)}, bf16[32,1152]{1,0:T(8,128)(2,1)S(1)}, u32[]{:S(2)}, u32[]{:S(2)}) collective-permute-start(bf16[32,1152]{1,0:T(8,128)(2,1)S(1)} %get-tuple-element.68), channel_id=1, source_target_pairs={{0,8},{8,0},{16,24},{24,16},{1,9},{9,1},{17,25},{25,17},{2,10},{10... | collective-permute-start | bytes 221192 | tf_op jit(solution)/shard_map/ppermute | solution.py:34
  24.6 1.8 %collective-permute-start.6 = (bf16[192,1152]{1,0:T(8,128)(2,1)S(1)}, bf16[192,1152]{1,0:T(8,128)(2,1)S(1)}, u32[]{:S(2)}, u32[]{:S(2)}) collective-permute-start(bf16[192,1152]{1,0:T(8,128)(2,1)S(1)} %collective-permute-done.2.text_unit.text_third), channel_id=1, source_target_pairs={{0,8},{8,0},{16,24},{24,16},{1,9},{9,1},{17,25},{25,17},{2,10},{10... | collective-permute-start | bytes 1327112 | tf_op jit(solution)/shard_map/ppermute | solution.py:34
  29.1 5.5 %collective-permute-start.7 = (bf16[176,256]{1,0:T(8,128)(2,1)S(1)}, bf16[176,256]{1,0:T(8,128)(2,1)S(1)}, u32[]{:S(2)}, u32[]{:S(2)}) collective-permute-start(bf16[176,256]{1,0:T(8,128)(2,1)S(1)} %get-tuple-element.95), channel_id=1, source_target_pairs={{0,1},{1,0},{2,3},{3,2},{4,5},{5,4},{6,7},{7,6},{8,9},{9,8},{10,11... | collective-permute-start | bytes 270344 | tf_op jit(solution)/shard_map/ppermute | solution.py:34
  30.7 6.6 %collective-permute-start.8 = (bf16[176,256]{1,0:T(8,128)(2,1)S(1)}, bf16[176,256]{1,0:T(8,128)(2,1)S(1)}, u32[]{:S(2)}, u32[]{:S(2)}) collective-permute-start(bf16[176,256]{1,0:T(8,128)(2,1)S(1)} %get-tuple-element.96), channel_id=1, source_target_pairs={{0,1},{1,0},{2,3},{3,2},{4,5},{5,4},{6,7},{7,6},{8,9},{9,8},{10,11... | collective-permute-start | bytes 270344 | tf_op jit(solution)/shard_map/ppermute | solution.py:34
  31.2 9.0 %collective-permute-start.9 = (bf16[176,256]{1,0:T(8,128)(2,1)S(1)}, bf16[176,256]{1,0:T(8,128)(2,1)S(1)}, u32[]{:S(2)}, u32[]{:S(2)}) collective-permute-start(bf16[176,256]{1,0:T(8,128)(2,1)S(1)} %get-tuple-element.97), channel_id=1, source_target_pairs={{0,1},{1,0},{2,3},{3,2},{4,5},{5,4},{6,7},{7,6},{8,9},{9,8},{10,11... | collective-permute-start | bytes 270344 | tf_op jit(solution)/shard_map/ppermute | solution.py:34
  34.7 9.4 %collective-permute-start.10 = (bf16[176,256]{1,0:T(8,128)(2,1)S(1)}, bf16[176,256]{1,0:T(8,128)(2,1)S(1)}, u32[]{:S(2)}, u32[]{:S(2)}) collective-permute-start(bf16[176,256]{1,0:T(8,128)(2,1)S(1)} %shard_map.100.before), channel_id=1, source_target_pairs={{0,4},{1,5},{2,6},{3,7},{4,0},{5,1},{6,2},{7,3},{8,12},{9,13},{10,... | collective-permute-start | bytes 270344 | tf_op jit(solution)/shard_map/ppermute | solution.py:34
  37.4 6.9 %collective-permute-start.11 = (bf16[176,256]{1,0:T(8,128)(2,1)S(1)}, bf16[176,256]{1,0:T(8,128)(2,1)S(1)}, u32[]{:S(2)}, u32[]{:S(2)}) collective-permute-start(bf16[176,256]{1,0:T(8,128)(2,1)S(1)} %shard_map.101.before), channel_id=1, source_target_pairs={{0,6},{1,7},{2,4},{3,5},{4,2},{5,3},{6,0},{7,1},{8,14},{9,15},{10,... | collective-permute-start | bytes 270344 | tf_op jit(solution)/shard_map/ppermute | solution.py:34
  40.3 4.9 %collective-permute-start.12 = (bf16[176,256]{1,0:T(8,128)(2,1)S(1)}, bf16[176,256]{1,0:T(8,128)(2,1)S(1)}, u32[]{:S(2)}, u32[]{:S(2)}) collective-permute-start(bf16[176,256]{1,0:T(8,128)(2,1)S(1)} %shard_map.102.before), channel_id=1, source_target_pairs={{0,2},{1,3},{2,0},{3,1},{4,6},{5,7},{6,4},{7,5},{8,10},{9,11},{10,... | collective-permute-start | bytes 270344 | tf_op jit(solution)/shard_map/ppermute | solution.py:34
  40.4 4.8 %collective-permute-start.13 = (bf16[176,256]{1,0:T(8,128)(2,1)S(1)}, bf16[176,256]{1,0:T(8,128)(2,1)S(1)}, u32[]{:S(2)}, u32[]{:S(2)}) collective-permute-start(bf16[176,256]{1,0:T(8,128)(2,1)S(1)} %get-tuple-element.100), channel_id=1, source_target_pairs={{0,1},{1,0},{2,3},{3,2},{4,5},{5,4},{6,7},{7,6},{8,9},{9,8},{10,11... | collective-permute-start | bytes 270344 | tf_op jit(solution)/shard_map/ppermute | solution.py:34
  45.3 4.6 %collective-permute-start.14 = (bf16[176,256]{1,0:T(8,128)(2,1)S(1)}, bf16[176,256]{1,0:T(8,128)(2,1)S(1)}, u32[]{:S(2)}, u32[]{:S(2)}) collective-permute-start(bf16[176,256]{1,0:T(8,128)(2,1)S(1)} %shard_map.106.before.refs_0_), channel_id=1, source_target_pairs={{0,16},{8,24},{16,0},{24,8},{1,17},{9,25},{17,1},{25,9},{2,18},{10... | collective-permute-start | bytes 270344 | tf_op jit(solution)/shard_map/ppermute | solution.py:34
  46.8 3.1 %collective-permute-start.15 = (bf16[176,256]{1,0:T(8,128)(2,1)S(1)}, bf16[176,256]{1,0:T(8,128)(2,1)S(1)}, u32[]{:S(2)}, u32[]{:S(2)}) collective-permute-start(bf16[176,256]{1,0:T(8,128)(2,1)S(1)} %shard_map.106.before.refs_0_), channel_id=1, source_target_pairs={{0,8},{8,0},{16,24},{24,16},{1,9},{9,1},{17,25},{25,17},{2,10},{10... | collective-permute-start | bytes 270344 | tf_op jit(solution)/shard_map/ppermute | solution.py:34
  49.9 1.3 %collective-permute-start.16 = (bf16[176,256]{1,0:T(8,128)(2,1)S(1)}, bf16[176,256]{1,0:T(8,128)(2,1)S(1)}, u32[]{:S(2)}, u32[]{:S(2)}) collective-permute-start(bf16[176,256]{1,0:T(8,128)(2,1)S(1)} %collective-permute-done.14.refs_2_), channel_id=1, source_target_pairs={{0,8},{8,0},{16,24},{24,16},{1,9},{9,1},{17,25},{25,17},{2,10},{10... | collective-permute-start | bytes 270344 | tf_op jit(solution)/shard_map/ppermute | solution.py:34

commit v27 on v26

--- a/solution.py
+++ b/solution.py
@@ -352,12 +352,11 @@
         (slice(near, every), back_far, unit_turned_far, inverse_far),
     ):
         whole = earlier[...] + added[:, where]
-        part = (whole - unit_turned[...].astype(F32) * total[:, where]) * (inverse[...] * scale)
+        part = (whole - unit_turned[...].astype(F32) * total[:, where]) * (inverse[...] * (scale * (1.0 / every)))
         back.append(part.astype(BF16))
     turned = jnp.concatenate([turned_near[...], turned_far[...]], axis=1)
     product = dot(turned, jnp.concatenate(back, axis=1), LAST)
     each = width // groups
-    product = product * (1.0 / every)
     for group in range(groups):
         pack_into(packed.at[group], product[group * each : (group + 1) * each, :], full)
 

time: 52.5 us -> 52.4 us (level)
  no operation moved by 1% of the time
where the time goes in v27:
time: 52.4 us; the launch traced here: 52.1 us
  Pallas kernels  21.6 us (41%)
  starting transfers between devices  16.9 us (32%)
  waiting for transfers between devices  8.87 us (17%)
  local copies, waits for them, and re-layouts  2.72 us (5%)
  between operations  2.08 us (4%)
    pallas_call x16, Pallas kernels, run(): pl.pallas_call(body, out_shape=[jax.ShapeDtypeStruct(shape, kind) for sha...  21.6 us
    ppermute x17, starting transfers between devices, send(): return lax.ppermute(value, axis, [(p, target(p)) for p in range(count)])  16.9 us
    ppermute x17, waiting for transfers between devices, send(): return lax.ppermute(value, axis, [(p, target(p)) for p in range(count)])  8.87 us
    unnamed x6, local copies, waits for them, and re-layouts  2.72 us
  transfers between devices with their start and end apart: 17, of which 8 were waited for; matrix products, arithmetic and copies ran while one was open for 0% of the time, Pallas kernels for 34%

profile of v27, /device:TPU:0, one launch (start us, length us, event | category | flops | bytes accessed | tf_op | source)
XLA Modules:
  0.0 52.1 jit_solution(1285646981963293551)
XLA Ops:
  0.6 0.5 collective-permute-start
  1.2 2.6 %collective-permute-start.3 = (bf16[192,1152]{1,0:T(8,128)(2,1)}, bf16[192,1152]{1,0:T(8,128)(2,1)S(1)}, u32[]{:S(2)}, u32[]{:S(2)}) collective-permute-start(bf16[192,1152]{1,0:T(8,128)(2,1)} %bitcast.6), channel_id=1, source_target_pairs={{0,16},{8,24},{16,0},{24,8},{1,17},{9,25},{17,1},{25,9},{2,18},{10... | collective-permute-start | bytes 1327112 | tf_op jit(solution)/shard_map/ppermute | solution.py:34
  5.0 0.0 collective-permute-done.f1
  5.0 0.0 copy-start
  5.0 1.0 %copy-done = bf16[192,1,1152]{2,0,1:T(8,128)(2,1)S(1)} copy-done((bf16[192,1,1152]{2,0,1:T(8,128)(2,1)S(1)}, bf16[192,1,1152]{2,0,1:T(8,128)(2,1)}, u32[]{:S(2)}) %copy-start) | copy-done | bytes 442392
  6.0 1.0 %copy-done.1 = bf16[192,1,1152]{2,0,1:T(8,128)(2,1)S(1)} copy-done((bf16[192,1,1152]{2,0,1:T(8,128)(2,1)S(1)}, bf16[192,1,1152]{2,0,1:T(8,128)(2,1)}, u32[]{:S(2)}) %copy-start.1) | copy-done | bytes 442392
  7.1 0.7 %copy-done.2 = f32[1152]{0:T(1024)S(1)} copy-done((f32[1152]{0:T(1024)S(1)}, f32[1152]{0:T(1024)}, u32[]{:S(2)}) %copy-start.2) | copy-done | bytes 4632
  7.7 4.2 %shard_map.93 = (bf16[192,1152]{1,0:T(8,128)(2,1)S(1)}, bf16[1152,1152]{1,0:T(8,128)(2,1)S(1)}, bf16[192,1152]{1,0:T(8,128)(2,1)S(1)}, f32[1,1152]{1,0:T(1,128)S...) custom-call(f32[1]{0:T(128)S(6)} %copy.10.scale, ...), custom_call_target="tpu_custom_call" | custom-call | flops 1019215872 | bytes 3538944 | tf_op jit(solution)/shard_map/pallas_call | solution.py:138
  12.0 0.2 collective-permute-start.1
  12.2 0.6 %collective-permute-start.2 = (bf16[192,1152]{1,0:T(8,128)(2,1)S(1)}, bf16[192,1152]{1,0:T(8,128)(2,1)S(1)}, u32[]{:S(2)}, u32[]{:S(2)}) collective-permute-start(bf16[192,1152]{1,0:T(8,128)(2,1)S(1)} %get-tuple-element.62.text_own), channel_id=1, source_target_pairs={{0,16},{8,24},{16,0},{24,8},{1,17},{9,25},{17,1},{25,9},{2,18},{10... | collective-permute-start | bytes 1327112 | tf_op jit(solution)/shard_map/ppermute | solution.py:34
  12.8 1.9 %collective-permute-done.3.f2 = bf16[192,1152]{1,0:T(8,128)(2,1)S(1)} collective-permute-done((bf16[192,1152]{1,0:T(8,128)(2,1)}, bf16[192,1152]{1,0:T(8,128)(2,1)S(1)}, u32[]{:S(2)}, u32[]{:S(2)}) %collective-permute-start.3) | collective-permute-done | bytes 442400 | tf_op jit(solution)/shard_map/ppermute | solution.py:34
  14.7 0.1 collective-permute-start.4
  14.8 0.5 collective-permute-start.5
  15.3 0.0 collective-permute-done.1.t1
  15.3 1.7 %shard_map.94 = (bf16[384,1152]{1,0:T(8,128)(2,1)S(1)}, bf16[1152,384]{1,0:T(8,128)(2,1)S(1)}, bf16[1152,384]{1,0:T(8,128)(2,1)S(1)}, bf16[288,384]{1,0:T(8,128)...) custom-call(f32[1]{0:T(128)S(6)} %copy.10.scale, ...), custom_call_target="tpu_custom_call" | custom-call | flops 1000 | bytes 1000 | tf_op jit(solution)/shard_map/pallas_call | solution.py:138
  17.0 0.0 collective-permute-done.5.f3_tail
  17.0 0.0 collective-permute-done.4.f3_head
  17.0 4.6 %shard_map.96 = (bf16[1152,384]{1,0:T(8,128)(2,1)S(1)}, bf16[384,1152]{1,0:T(8,128)(2,1)S(1)}, bf16[1152,384]{1,0:T(8,128)(2,1)S(1)}, bf16[288,384]{1,0:T(8,128)...) custom-call(f32[1]{0:T(128)S(6)} %copy.10.scale, ...), custom_call_target="tpu_custom_call" | custom-call | flops 1000 | bytes 1000 | tf_op jit(solution)/shard_map/pallas_call | solution.py:138
  21.7 2.0 %shard_map.97 = (bf16[192,1152]{1,0:T(8,128)(2,1)}, f32[8,128]{1,0:T(8,128)S(1)}) custom-call(f32[1]{0:T(128)S(6)} %copy.10.scale, bf16[192,1152]{1,0:T(8,128)(2,1)S(1)} %get-tuple-element.65.text, bf16[384,384]{1,0:T(8,128)(2,1)S(1)} %get-tuple-element.66.weights_near, bf16[384,384]{1,0:T(8,128)(2,1)S(1)} %get-tuple-element.70.weights_far, ...), custom_call_target="tpu_custom_call" | custom-call | flops 1000 | bytes 1000 | tf_op jit(solution)/shard_map/pallas_call | solution.py:138
  23.7 0.9 %collective-permute-done.2.text_unit.text_third = bf16[192,1152]{1,0:T(8,128)(2,1)S(1)} collective-permute-done((bf16[192,1152]{1,0:T(8,128)(2,1)S(1)}, bf16[192,1152]{1,0:T(8,128)(2,1)S(1)}, u32[]{:S(2)}, u32[]{:S(2)}) %collective-permute-start.2) | collective-permute-done | bytes 442400 | tf_op jit(solution)/shard_map/ppermute | solution.py:34
  24.6 0.0 collective-permute-start.6
  24.6 1.3 %shard_map.98 = (bf16[192,768]{1,0:T(8,128)(2,1)S(1)}, f32[288,384]{1,0:T(8,128)S(1)}, f32[288,384]{1,0:T(8,128)S(1)}, f32[1,768]{1,0:T(1,128)S(1)}) custom-call(f32[1]{0:T(128)S(6)} %copy.10.scale, f32[1]{0:T(128)S(6)} %copy.11.bias, bf16[192,1152]{1,0:T(8,128)(2,1)S(1)} %collective-permute-done.2.text_unit.text_third, ...), custom_call_target="tpu_custom_call" | custom-call | flops 1019215872 | bytes 3538944 | tf_op jit(solution)/shard_map/pallas_call | solution.py:138
  26.0 0.5 collective-permute-done.6.text_unit.text_fourth
  26.4 2.7 %shard_map.99 = (bf16[176,256]{1,0:T(8,128)(2,1)S(1)}, bf16[176,256]{1,0:T(8,128)(2,1)S(1)}, bf16[176,256]{1,0:T(8,128)(2,1)S(1)}, bf16[176,256]{1,0:T(8,128)(2,...) custom-call(f32[1]{0:T(128)S(6)} %copy.10.scale, f32[1]{0:T(128)S(6)} %copy.11.bias, ...), custom_call_target="tpu_custom_call" | custom-call | flops 2038431744 | bytes 7077888 | tf_op jit(solution)/shard_map/pallas_call | solution.py:138
  29.1 1.6 %collective-permute-start.7 = (bf16[176,256]{1,0:T(8,128)(2,1)S(1)}, bf16[176,256]{1,0:T(8,128)(2,1)S(1)}, u32[]{:S(2)}, u32[]{:S(2)}) collective-permute-start(bf16[176,256]{1,0:T(8,128)(2,1)S(1)} %get-tuple-element.95), channel_id=1, source_target_pairs={{0,1},{1,0},{2,3},{3,2},{4,5},{5,4},{6,7},{7,6},{8,9},{9,8},{10,11... | collective-permute-start | bytes 270344 | tf_op jit(solution)/shard_map/ppermute | solution.py:34
  30.7 0.5 collective-permute-start.8
  31.2 1.5 %collective-permute-start.9 = (bf16[176,256]{1,0:T(8,128)(2,1)S(1)}, bf16[176,256]{1,0:T(8,128)(2,1)S(1)}, u32[]{:S(2)}, u32[]{:S(2)}) collective-permute-start(bf16[176,256]{1,0:T(8,128)(2,1)S(1)} %get-tuple-element.97), channel_id=1, source_target_pairs={{0,1},{1,0},{2,3},{3,2},{4,5},{5,4},{6,7},{7,6},{8,9},{9,8},{10,11... | collective-permute-start | bytes 270344 | tf_op jit(solution)/shard_map/ppermute | solution.py:34
  32.7 1.9 %collective-permute-done.7.come = bf16[176,256]{1,0:T(8,128)(2,1)S(1)} collective-permute-done((bf16[176,256]{1,0:T(8,128)(2,1)S(1)}, bf16[176,256]{1,0:T(8,128)(2,1)S(1)}, u32[]{:S(2)}, u32[]{:S(2)}) %collective-permute-start.7) | collective-permute-done | bytes 90144 | tf_op jit(solution)/shard_map/ppermute | solution.py:34
  34.6 2.6 %collective-permute-start.10 = (bf16[176,256]{1,0:T(8,128)(2,1)S(1)}, bf16[176,256]{1,0:T(8,128)(2,1)S(1)}, u32[]{:S(2)}, u32[]{:S(2)}) collective-permute-start(bf16[176,256]{1,0:T(8,128)(2,1)S(1)} %shard_map.100.before), channel_id=1, source_target_pairs={{0,4},{1,5},{2,6},{3,7},{4,0},{5,1},{6,2},{7,3},{8,12},{9,13},{10,... | collective-permute-start | bytes 270344 | tf_op jit(solution)/shard_map/ppermute | solution.py:34
  37.3 0.0 collective-permute-done.8.come
  37.3 2.9 %collective-permute-start.11 = (bf16[176,256]{1,0:T(8,128)(2,1)S(1)}, bf16[176,256]{1,0:T(8,128)(2,1)S(1)}, u32[]{:S(2)}, u32[]{:S(2)}) collective-permute-start(bf16[176,256]{1,0:T(8,128)(2,1)S(1)} %shard_map.101.before), channel_id=1, source_target_pairs={{0,6},{1,7},{2,4},{3,5},{4,2},{5,3},{6,0},{7,1},{8,14},{9,15},{10,... | collective-permute-start | bytes 270344 | tf_op jit(solution)/shard_map/ppermute | solution.py:34
  40.2 0.0 collective-permute-done.9.come
  40.3 0.1 collective-permute-start.12
  40.3 1.6 %collective-permute-start.13 = (bf16[176,256]{1,0:T(8,128)(2,1)S(1)}, bf16[176,256]{1,0:T(8,128)(2,1)S(1)}, u32[]{:S(2)}, u32[]{:S(2)}) collective-permute-start(bf16[176,256]{1,0:T(8,128)(2,1)S(1)} %get-tuple-element.100), channel_id=1, source_target_pairs={{0,1},{1,0},{2,3},{3,2},{4,5},{5,4},{6,7},{7,6},{8,9},{9,8},{10,11... | collective-permute-start | bytes 270344 | tf_op jit(solution)/shard_map/ppermute | solution.py:34
  41.9 2.1 %shard_map.103 = (f32[192,1152]{1,0:T(8,128)S(1)}, f32[8,128]{1,0:T(8,128)S(1)}) custom-call(f32[1]{0:T(128)S(6)} %copy.10.scale, bf16[1152,1152]{1,0:T(8,128)(2,1)S(1)} %get-tuple-element.58.proj, bf16[384,1152]{1,0:T(8,128)(2,1)S(1)} %get-tuple-element.64.text_near, bf16[192,1152]{1,0:T(8,128)(2,1)S(1)} %collective-permute-done.2.text_unit.text_third, ...), custom_call_target="tpu_custom_call" | custom-call | flops 1000 | bytes 1000 | tf_op jit(solution)/shard_map/pallas_call | solution.py:138
  44.0 0.0 collective-permute-done.10.two_on
  44.1 0.2 collective-permute-done.11.three_on
  44.2 0.9 %collective-permute-done.12.next_one = bf16[176,256]{1,0:T(8,128)(2,1)S(1)} collective-permute-done((bf16[176,256]{1,0:T(8,128)(2,1)S(1)}, bf16[176,256]{1,0:T(8,128)(2,1)S(1)}, u32[]{:S(2)}, u32[]{:S(2)}) %collective-permute-start.12) | collective-permute-done | bytes 90144 | tf_op jit(solution)/shard_map/ppermute | solution.py:34
  45.2 0.0 collective-permute-done.13.come
  45.2 0.1 shard_map.106.before.refs_0_
  45.2 1.5 %collective-permute-start.14 = (bf16[176,256]{1,0:T(8,128)(2,1)S(1)}, bf16[176,256]{1,0:T(8,128)(2,1)S(1)}, u32[]{:S(2)}, u32[]{:S(2)}) collective-permute-start(bf16[176,256]{1,0:T(8,128)(2,1)S(1)} %shard_map.106.before.refs_0_), channel_id=1, source_target_pairs={{0,16},{8,24},{16,0},{24,8},{1,17},{9,25},{17,1},{25,9},{2,18},{10... | collective-permute-start | bytes 270344 | tf_op jit(solution)/shard_map/ppermute | solution.py:34
  46.8 0.0 collective-permute-start.15
  46.8 1.7 %shard_map.107 = (bf16[192,1152]{1,0:T(8,128)(2,1)}, f32[8,128]{1,0:T(8,128)S(1)}) custom-call(bf16[192,1152]{1,0:T(8,128)(2,1)S(1)} %get-tuple-element.56.features, f32[1,1152]{1,0:T(1,128)S(1)} %get-tuple-element.57.gain, f32[192,1152]{1,0:T(8,128)S(1)} %get-tuple-element.98.norm_back, bf16[176,256]{1,0:T(8,128)(2,1)S(1)} %shard_map.106.before.refs_0_), custom_call_target="tpu_custom_call" | custom-call | bytes 5308416 | tf_op jit(solution)/shard_map/pallas_call | solution.py:138
  48.5 1.3 %collective-permute-done.14.refs_2_ = bf16[176,256]{1,0:T(8,128)(2,1)S(1)} collective-permute-done((bf16[176,256]{1,0:T(8,128)(2,1)S(1)}, bf16[176,256]{1,0:T(8,128)(2,1)S(1)}, u32[]{:S(2)}, u32[]{:S(2)}) %collective-permute-start.14) | collective-permute-done | bytes 90144 | tf_op jit(solution)/shard_map/ppermute | solution.py:34
  49.8 0.0 collective-permute-start.16
  49.8 0.0 collective-permute-done.15.refs_1_
  49.8 1.3 %collective-permute-done.16.refs_3_ = bf16[176,256]{1,0:T(8,128)(2,1)S(1)} collective-permute-done((bf16[176,256]{1,0:T(8,128)(2,1)S(1)}, bf16[176,256]{1,0:T(8,128)(2,1)S(1)}, u32[]{:S(2)}, u32[]{:S(2)}) %collective-permute-start.16) | collective-permute-done | bytes 90144 | tf_op jit(solution)/shard_map/ppermute | solution.py:34
  51.1 1.0 %shard_map.108 = (f32[144,1152]{1,0:T(8,128)}, f32[1152]{0:T(1024)}) custom-call(f32[8,128]{1,0:T(8,128)S(1)} %get-tuple-element.104.before, bf16[176,256]{1,0:T(8,128)(2,1)S(1)} %shard_map.106.before.refs_0_, bf16[176,256]{1,0:T(8,128)(2,1)S(1)} %collective-permute-done.15.refs_1_, bf16[176,256]{1,0:T(8,128)(2,1)S(1)} %collective-permute-done.14.refs_2_, ...), custom_call_target="tpu_custom_call" | custom-call | bytes 1327104 | tf_op jit(solution)/shard_map/pallas_call | solution.py:138
  (8 shorter events, 0.2 us)
Async XLA Ops:
  0.6 4.4 %collective-permute-start = (bf16[192,1152]{1,0:T(8,128)(2,1)}, bf16[192,1152]{1,0:T(8,128)(2,1)S(1)}, u32[]{:S(2)}, u32[]{:S(2)}) collective-permute-start(bf16[192,1152]{1,0:T(8,128)(2,1)} %bitcast.5), channel_id=1, source_target_pairs={{0,8},{8,0},{16,24},{24,16},{1,9},{9,1},{17,25},{25,17},{2,10},{10... | collective-permute-start | bytes 1327112 | tf_op jit(solution)/shard_map/ppermute | solution.py:34
  1.2 13.5 %collective-permute-start.3 = (bf16[192,1152]{1,0:T(8,128)(2,1)}, bf16[192,1152]{1,0:T(8,128)(2,1)S(1)}, u32[]{:S(2)}, u32[]{:S(2)}) collective-permute-start(bf16[192,1152]{1,0:T(8,128)(2,1)} %bitcast.6), channel_id=1, source_target_pairs={{0,16},{8,24},{16,0},{24,8},{1,17},{9,25},{17,1},{25,9},{2,18},{10... | collective-permute-start | bytes 1327112 | tf_op jit(solution)/shard_map/ppermute | solution.py:34
  5.0 1.0 %copy-start = (bf16[192,1,1152]{2,0,1:T(8,128)(2,1)S(1)}, bf16[192,1,1152]{2,0,1:T(8,128)(2,1)}, u32[]{:S(2)}) copy-start(bf16[192,1,1152]{2,0,1:T(8,128)(2,1)} %param.7) | copy-start | bytes 1327108
  6.0 1.0 %copy-start.1 = (bf16[192,1,1152]{2,0,1:T(8,128)(2,1)S(1)}, bf16[192,1,1152]{2,0,1:T(8,128)(2,1)}, u32[]{:S(2)}) copy-start(bf16[192,1,1152]{2,0,1:T(8,128)(2,1)} %param.6) | copy-start | bytes 1327108
  7.1 0.7 %copy-start.2 = (f32[1152]{0:T(1024)S(1)}, f32[1152]{0:T(1024)}, u32[]{:S(2)}) copy-start(f32[1152]{0:T(1024)} %gain_line.1) | copy-start | bytes 13828
  12.0 3.3 %collective-permute-start.1 = (bf16[192,1152]{1,0:T(8,128)(2,1)S(1)}, bf16[192,1152]{1,0:T(8,128)(2,1)S(1)}, u32[]{:S(2)}, u32[]{:S(2)}) collective-permute-start(bf16[192,1152]{1,0:T(8,128)(2,1)S(1)} %get-tuple-element.62.text_own), channel_id=1, source_target_pairs={{0,8},{8,0},{16,24},{24,16},{1,9},{9,1},{17,25},{25,17},{2,10},{10... | collective-permute-start | bytes 1327112 | tf_op jit(solution)/shard_map/ppermute | solution.py:34
  12.2 12.4 %collective-permute-start.2 = (bf16[192,1152]{1,0:T(8,128)(2,1)S(1)}, bf16[192,1152]{1,0:T(8,128)(2,1)S(1)}, u32[]{:S(2)}, u32[]{:S(2)}) collective-permute-start(bf16[192,1152]{1,0:T(8,128)(2,1)S(1)} %get-tuple-element.62.text_own), channel_id=1, source_target_pairs={{0,16},{8,24},{16,0},{24,8},{1,17},{9,25},{17,1},{25,9},{2,18},{10... | collective-permute-start | bytes 1327112 | tf_op jit(solution)/shard_map/ppermute | solution.py:34
  14.7 2.3 %collective-permute-start.4 = (bf16[160,1152]{1,0:T(8,128)(2,1)S(1)}, bf16[160,1152]{1,0:T(8,128)(2,1)S(1)}, u32[]{:S(2)}, u32[]{:S(2)}) collective-permute-start(bf16[160,1152]{1,0:T(8,128)(2,1)S(1)} %get-tuple-element.67), channel_id=1, source_target_pairs={{0,8},{8,0},{16,24},{24,16},{1,9},{9,1},{17,25},{25,17},{2,10},{10... | collective-permute-start | bytes 1105928 | tf_op jit(solution)/shard_map/ppermute | solution.py:34
  14.8 2.2 %collective-permute-start.5 = (bf16[32,1152]{1,0:T(8,128)(2,1)S(1)}, bf16[32,1152]{1,0:T(8,128)(2,1)S(1)}, u32[]{:S(2)}, u32[]{:S(2)}) collective-permute-start(bf16[32,1152]{1,0:T(8,128)(2,1)S(1)} %get-tuple-element.68), channel_id=1, source_target_pairs={{0,8},{8,0},{16,24},{24,16},{1,9},{9,1},{17,25},{25,17},{2,10},{10... | collective-permute-start | bytes 221192 | tf_op jit(solution)/shard_map/ppermute | solution.py:34
  24.6 1.8 %collective-permute-start.6 = (bf16[192,1152]{1,0:T(8,128)(2,1)S(1)}, bf16[192,1152]{1,0:T(8,128)(2,1)S(1)}, u32[]{:S(2)}, u32[]{:S(2)}) collective-permute-start(bf16[192,1152]{1,0:T(8,128)(2,1)S(1)} %collective-permute-done.2.text_unit.text_third), channel_id=1, source_target_pairs={{0,8},{8,0},{16,24},{24,16},{1,9},{9,1},{17,25},{25,17},{2,10},{10... | collective-permute-start | bytes 1327112 | tf_op jit(solution)/shard_map/ppermute | solution.py:34
  29.1 5.5 %collective-permute-start.7 = (bf16[176,256]{1,0:T(8,128)(2,1)S(1)}, bf16[176,256]{1,0:T(8,128)(2,1)S(1)}, u32[]{:S(2)}, u32[]{:S(2)}) collective-permute-start(bf16[176,256]{1,0:T(8,128)(2,1)S(1)} %get-tuple-element.95), channel_id=1, source_target_pairs={{0,1},{1,0},{2,3},{3,2},{4,5},{5,4},{6,7},{7,6},{8,9},{9,8},{10,11... | collective-permute-start | bytes 270344 | tf_op jit(solution)/shard_map/ppermute | solution.py:34
  30.7 6.6 %collective-permute-start.8 = (bf16[176,256]{1,0:T(8,128)(2,1)S(1)}, bf16[176,256]{1,0:T(8,128)(2,1)S(1)}, u32[]{:S(2)}, u32[]{:S(2)}) collective-permute-start(bf16[176,256]{1,0:T(8,128)(2,1)S(1)} %get-tuple-element.96), channel_id=1, source_target_pairs={{0,1},{1,0},{2,3},{3,2},{4,5},{5,4},{6,7},{7,6},{8,9},{9,8},{10,11... | collective-permute-start | bytes 270344 | tf_op jit(solution)/shard_map/ppermute | solution.py:34
  31.2 9.0 %collective-permute-start.9 = (bf16[176,256]{1,0:T(8,128)(2,1)S(1)}, bf16[176,256]{1,0:T(8,128)(2,1)S(1)}, u32[]{:S(2)}, u32[]{:S(2)}) collective-permute-start(bf16[176,256]{1,0:T(8,128)(2,1)S(1)} %get-tuple-element.97), channel_id=1, source_target_pairs={{0,1},{1,0},{2,3},{3,2},{4,5},{5,4},{6,7},{7,6},{8,9},{9,8},{10,11... | collective-permute-start | bytes 270344 | tf_op jit(solution)/shard_map/ppermute | solution.py:34
  34.6 9.4 %collective-permute-start.10 = (bf16[176,256]{1,0:T(8,128)(2,1)S(1)}, bf16[176,256]{1,0:T(8,128)(2,1)S(1)}, u32[]{:S(2)}, u32[]{:S(2)}) collective-permute-start(bf16[176,256]{1,0:T(8,128)(2,1)S(1)} %shard_map.100.before), channel_id=1, source_target_pairs={{0,4},{1,5},{2,6},{3,7},{4,0},{5,1},{6,2},{7,3},{8,12},{9,13},{10,... | collective-permute-start | bytes 270344 | tf_op jit(solution)/shard_map/ppermute | solution.py:34
  37.3 6.9 %collective-permute-start.11 = (bf16[176,256]{1,0:T(8,128)(2,1)S(1)}, bf16[176,256]{1,0:T(8,128)(2,1)S(1)}, u32[]{:S(2)}, u32[]{:S(2)}) collective-permute-start(bf16[176,256]{1,0:T(8,128)(2,1)S(1)} %shard_map.101.before), channel_id=1, source_target_pairs={{0,6},{1,7},{2,4},{3,5},{4,2},{5,3},{6,0},{7,1},{8,14},{9,15},{10,... | collective-permute-start | bytes 270344 | tf_op jit(solution)/shard_map/ppermute | solution.py:34
  40.3 4.9 %collective-permute-start.12 = (bf16[176,256]{1,0:T(8,128)(2,1)S(1)}, bf16[176,256]{1,0:T(8,128)(2,1)S(1)}, u32[]{:S(2)}, u32[]{:S(2)}) collective-permute-start(bf16[176,256]{1,0:T(8,128)(2,1)S(1)} %shard_map.102.before), channel_id=1, source_target_pairs={{0,2},{1,3},{2,0},{3,1},{4,6},{5,7},{6,4},{7,5},{8,10},{9,11},{10,... | collective-permute-start | bytes 270344 | tf_op jit(solution)/shard_map/ppermute | solution.py:34
  40.3 4.8 %collective-permute-start.13 = (bf16[176,256]{1,0:T(8,128)(2,1)S(1)}, bf16[176,256]{1,0:T(8,128)(2,1)S(1)}, u32[]{:S(2)}, u32[]{:S(2)}) collective-permute-start(bf16[176,256]{1,0:T(8,128)(2,1)S(1)} %get-tuple-element.100), channel_id=1, source_target_pairs={{0,1},{1,0},{2,3},{3,2},{4,5},{5,4},{6,7},{7,6},{8,9},{9,8},{10,11... | collective-permute-start | bytes 270344 | tf_op jit(solution)/shard_map/ppermute | solution.py:34
  45.2 4.6 %collective-permute-start.14 = (bf16[176,256]{1,0:T(8,128)(2,1)S(1)}, bf16[176,256]{1,0:T(8,128)(2,1)S(1)}, u32[]{:S(2)}, u32[]{:S(2)}) collective-permute-start(bf16[176,256]{1,0:T(8,128)(2,1)S(1)} %shard_map.106.before.refs_0_), channel_id=1, source_target_pairs={{0,16},{8,24},{16,0},{24,8},{1,17},{9,25},{17,1},{25,9},{2,18},{10... | collective-permute-start | bytes 270344 | tf_op jit(solution)/shard_map/ppermute | solution.py:34
  46.8 3.1 %collective-permute-start.15 = (bf16[176,256]{1,0:T(8,128)(2,1)S(1)}, bf16[176,256]{1,0:T(8,128)(2,1)S(1)}, u32[]{:S(2)}, u32[]{:S(2)}) collective-permute-start(bf16[176,256]{1,0:T(8,128)(2,1)S(1)} %shard_map.106.before.refs_0_), channel_id=1, source_target_pairs={{0,8},{8,0},{16,24},{24,16},{1,9},{9,1},{17,25},{25,17},{2,10},{10... | collective-permute-start | bytes 270344 | tf_op jit(solution)/shard_map/ppermute | solution.py:34
  49.8 1.3 %collective-permute-start.16 = (bf16[176,256]{1,0:T(8,128)(2,1)S(1)}, bf16[176,256]{1,0:T(8,128)(2,1)S(1)}, u32[]{:S(2)}, u32[]{:S(2)}) collective-permute-start(bf16[176,256]{1,0:T(8,128)(2,1)S(1)} %collective-permute-done.14.refs_2_), channel_id=1, source_target_pairs={{0,8},{8,0},{16,24},{24,16},{1,9},{9,1},{17,25},{25,17},{2,10},{10... | collective-permute-start | bytes 270344 | tf_op jit(solution)/shard_map/ppermute | solution.py:34

commit v28 on v27

--- a/solution.py
+++ b/solution.py
@@ -204,7 +204,7 @@
         both = weight.astype(F32) * product
         return total + both[:8, :] + both[8:, :]
 
-    total = lax.fori_loop(0, texts // BAND, chunk, jnp.zeros((8, images), F32), unroll=4)
+    total = lax.fori_loop(0, texts // BAND, chunk, jnp.zeros((8, images), F32), unroll=12)
     return jnp.sum(total, axis=0, keepdims=True)
 
 

time: 52.4 us -> 52 us (level)
  Pallas kernels: 21.6 us -> 21 us
    pallas_call x16, Pallas kernels: 21.6 us -> 21 us  [run(): pl.pallas_call(body, out_shape=[jax.ShapeDtypeStruct(shape, kind) for sha...]
where the time goes in v28:
time: 52 us; the launch traced here: 51.7 us
  Pallas kernels  21 us (40%)
  starting transfers between devices  17 us (33%)
  waiting for transfers between devices  8.95 us (17%)
  local copies, waits for them, and re-layouts  2.72 us (5%)
  between operations  2.05 us (4%)
    pallas_call x16, Pallas kernels, run(): pl.pallas_call(body, out_shape=[jax.ShapeDtypeStruct(shape, kind) for sha...  21 us
    ppermute x17, starting transfers between devices, send(): return lax.ppermute(value, axis, [(p, target(p)) for p in range(count)])  17 us
    ppermute x17, waiting for transfers between devices, send(): return lax.ppermute(value, axis, [(p, target(p)) for p in range(count)])  8.95 us
    unnamed x6, local copies, waits for them, and re-layouts  2.72 us
  transfers between devices with their start and end apart: 17, of which 8 were waited for; matrix products, arithmetic and copies ran while one was open for 0% of the time, Pallas kernels for 34%

profile of v28, /device:TPU:0, one launch (start us, length us, event | category | flops | bytes accessed | tf_op | source)
XLA Modules:
  0.0 51.7 jit_solution(5851683738370967755)
XLA Ops:
  0.6 0.5 %collective-permute-start = (bf16[192,1152]{1,0:T(8,128)(2,1)}, bf16[192,1152]{1,0:T(8,128)(2,1)S(1)}, u32[]{:S(2)}, u32[]{:S(2)}) collective-permute-start(bf16[192,1152]{1,0:T(8,128)(2,1)} %bitcast.5), channel_id=1, source_target_pairs={{0,8},{8,0},{16,24},{24,16},{1,9},{9,1},{17,25},{25,17},{2,10},{10... | collective-permute-start | bytes 1327112 | tf_op jit(solution)/shard_map/ppermute | solution.py:34
  1.2 2.6 %collective-permute-start.3 = (bf16[192,1152]{1,0:T(8,128)(2,1)}, bf16[192,1152]{1,0:T(8,128)(2,1)S(1)}, u32[]{:S(2)}, u32[]{:S(2)}) collective-permute-start(bf16[192,1152]{1,0:T(8,128)(2,1)} %bitcast.6), channel_id=1, source_target_pairs={{0,16},{8,24},{16,0},{24,8},{1,17},{9,25},{17,1},{25,9},{2,18},{10... | collective-permute-start | bytes 1327112 | tf_op jit(solution)/shard_map/ppermute | solution.py:34
  5.0 0.0 collective-permute-done.f1
  5.0 0.0 copy-start
  5.0 1.0 %copy-done = bf16[192,1,1152]{2,0,1:T(8,128)(2,1)S(1)} copy-done((bf16[192,1,1152]{2,0,1:T(8,128)(2,1)S(1)}, bf16[192,1,1152]{2,0,1:T(8,128)(2,1)}, u32[]{:S(2)}) %copy-start) | copy-done | bytes 442392
  6.0 1.0 %copy-done.1 = bf16[192,1,1152]{2,0,1:T(8,128)(2,1)S(1)} copy-done((bf16[192,1,1152]{2,0,1:T(8,128)(2,1)S(1)}, bf16[192,1,1152]{2,0,1:T(8,128)(2,1)}, u32[]{:S(2)}) %copy-start.1) | copy-done | bytes 442392
  7.1 0.7 %copy-done.2 = f32[1152]{0:T(1024)S(1)} copy-done((f32[1152]{0:T(1024)S(1)}, f32[1152]{0:T(1024)}, u32[]{:S(2)}) %copy-start.2) | copy-done | bytes 4632
  7.7 4.2 %shard_map.93 = (bf16[192,1152]{1,0:T(8,128)(2,1)S(1)}, bf16[1152,1152]{1,0:T(8,128)(2,1)S(1)}, bf16[192,1152]{1,0:T(8,128)(2,1)S(1)}, f32[1,1152]{1,0:T(1,128)S...) custom-call(f32[1]{0:T(128)S(6)} %copy.10.scale, ...), custom_call_target="tpu_custom_call" | custom-call | flops 1019215872 | bytes 3538944 | tf_op jit(solution)/shard_map/pallas_call | solution.py:138
  12.0 0.2 collective-permute-start.1
  12.2 0.6 %collective-permute-start.2 = (bf16[192,1152]{1,0:T(8,128)(2,1)S(1)}, bf16[192,1152]{1,0:T(8,128)(2,1)S(1)}, u32[]{:S(2)}, u32[]{:S(2)}) collective-permute-start(bf16[192,1152]{1,0:T(8,128)(2,1)S(1)} %get-tuple-element.62.text_own), channel_id=1, source_target_pairs={{0,16},{8,24},{16,0},{24,8},{1,17},{9,25},{17,1},{25,9},{2,18},{10... | collective-permute-start | bytes 1327112 | tf_op jit(solution)/shard_map/ppermute | solution.py:34
  12.8 1.9 %collective-permute-done.3.f2 = bf16[192,1152]{1,0:T(8,128)(2,1)S(1)} collective-permute-done((bf16[192,1152]{1,0:T(8,128)(2,1)}, bf16[192,1152]{1,0:T(8,128)(2,1)S(1)}, u32[]{:S(2)}, u32[]{:S(2)}) %collective-permute-start.3) | collective-permute-done | bytes 442400 | tf_op jit(solution)/shard_map/ppermute | solution.py:34
  14.7 0.1 collective-permute-start.4
  14.8 0.5 collective-permute-start.5
  15.3 0.0 collective-permute-done.1.t1
  15.3 1.9 %shard_map.94 = (bf16[384,1152]{1,0:T(8,128)(2,1)S(1)}, bf16[1152,384]{1,0:T(8,128)(2,1)S(1)}, bf16[1152,384]{1,0:T(8,128)(2,1)S(1)}, bf16[288,384]{1,0:T(8,128)...) custom-call(f32[1]{0:T(128)S(6)} %copy.10.scale, ...), custom_call_target="tpu_custom_call" | custom-call | flops 1000 | bytes 1000 | tf_op jit(solution)/shard_map/pallas_call | solution.py:138
  17.2 0.0 collective-permute-done.5.f3_tail
  17.2 0.0 collective-permute-done.4.f3_head
  17.2 4.6 %shard_map.96 = (bf16[1152,384]{1,0:T(8,128)(2,1)S(1)}, bf16[384,1152]{1,0:T(8,128)(2,1)S(1)}, bf16[1152,384]{1,0:T(8,128)(2,1)S(1)}, bf16[288,384]{1,0:T(8,128)...) custom-call(f32[1]{0:T(128)S(6)} %copy.10.scale, ...), custom_call_target="tpu_custom_call" | custom-call | flops 1000 | bytes 1000 | tf_op jit(solution)/shard_map/pallas_call | solution.py:138
  21.8 2.0 %shard_map.97 = (bf16[192,1152]{1,0:T(8,128)(2,1)}, f32[8,128]{1,0:T(8,128)S(1)}) custom-call(f32[1]{0:T(128)S(6)} %copy.10.scale, bf16[192,1152]{1,0:T(8,128)(2,1)S(1)} %get-tuple-element.65.text, bf16[384,384]{1,0:T(8,128)(2,1)S(1)} %get-tuple-element.66.weights_near, bf16[384,384]{1,0:T(8,128)(2,1)S(1)} %get-tuple-element.70.weights_far, ...), custom_call_target="tpu_custom_call" | custom-call | flops 1000 | bytes 1000 | tf_op jit(solution)/shard_map/pallas_call | solution.py:138
  23.8 0.8 %collective-permute-done.2.text_unit.text_third = bf16[192,1152]{1,0:T(8,128)(2,1)S(1)} collective-permute-done((bf16[192,1152]{1,0:T(8,128)(2,1)S(1)}, bf16[192,1152]{1,0:T(8,128)(2,1)S(1)}, u32[]{:S(2)}, u32[]{:S(2)}) %collective-permute-start.2) | collective-permute-done | bytes 442400 | tf_op jit(solution)/shard_map/ppermute | solution.py:34
  24.6 0.0 collective-permute-start.6
  24.6 1.0 %shard_map.98 = (bf16[192,768]{1,0:T(8,128)(2,1)S(1)}, f32[288,384]{1,0:T(8,128)S(1)}, f32[288,384]{1,0:T(8,128)S(1)}, f32[1,768]{1,0:T(1,128)S(1)}) custom-call(f32[1]{0:T(128)S(6)} %copy.10.scale, f32[1]{0:T(128)S(6)} %copy.11.bias, bf16[192,1152]{1,0:T(8,128)(2,1)S(1)} %collective-permute-done.2.text_unit.text_third, ...), custom_call_target="tpu_custom_call" | custom-call | flops 1019215872 | bytes 3538944 | tf_op jit(solution)/shard_map/pallas_call | solution.py:138
  25.6 0.8 %collective-permute-done.6.text_unit.text_fourth = bf16[192,1152]{1,0:T(8,128)(2,1)S(1)} collective-permute-done((bf16[192,1152]{1,0:T(8,128)(2,1)S(1)}, bf16[192,1152]{1,0:T(8,128)(2,1)S(1)}, u32[]{:S(2)}, u32[]{:S(2)}) %collective-permute-start.6) | collective-permute-done | bytes 442400 | tf_op jit(solution)/shard_map/ppermute | solution.py:34
  26.4 2.3 %shard_map.99 = (bf16[176,256]{1,0:T(8,128)(2,1)S(1)}, bf16[176,256]{1,0:T(8,128)(2,1)S(1)}, bf16[176,256]{1,0:T(8,128)(2,1)S(1)}, bf16[176,256]{1,0:T(8,128)(2,...) custom-call(f32[1]{0:T(128)S(6)} %copy.10.scale, f32[1]{0:T(128)S(6)} %copy.11.bias, ...), custom_call_target="tpu_custom_call" | custom-call | flops 2038431744 | bytes 7077888 | tf_op jit(solution)/shard_map/pallas_call | solution.py:138
  28.7 1.6 %collective-permute-start.7 = (bf16[176,256]{1,0:T(8,128)(2,1)S(1)}, bf16[176,256]{1,0:T(8,128)(2,1)S(1)}, u32[]{:S(2)}, u32[]{:S(2)}) collective-permute-start(bf16[176,256]{1,0:T(8,128)(2,1)S(1)} %get-tuple-element.95), channel_id=1, source_target_pairs={{0,1},{1,0},{2,3},{3,2},{4,5},{5,4},{6,7},{7,6},{8,9},{9,8},{10,11... | collective-permute-start | bytes 270344 | tf_op jit(solution)/shard_map/ppermute | solution.py:34
  30.3 0.5 collective-permute-start.8
  30.8 1.5 %collective-permute-start.9 = (bf16[176,256]{1,0:T(8,128)(2,1)S(1)}, bf16[176,256]{1,0:T(8,128)(2,1)S(1)}, u32[]{:S(2)}, u32[]{:S(2)}) collective-permute-start(bf16[176,256]{1,0:T(8,128)(2,1)S(1)} %get-tuple-element.97), channel_id=1, source_target_pairs={{0,1},{1,0},{2,3},{3,2},{4,5},{5,4},{6,7},{7,6},{8,9},{9,8},{10,11... | collective-permute-start | bytes 270344 | tf_op jit(solution)/shard_map/ppermute | solution.py:34
  32.4 1.9 %collective-permute-done.7.come = bf16[176,256]{1,0:T(8,128)(2,1)S(1)} collective-permute-done((bf16[176,256]{1,0:T(8,128)(2,1)S(1)}, bf16[176,256]{1,0:T(8,128)(2,1)S(1)}, u32[]{:S(2)}, u32[]{:S(2)}) %collective-permute-start.7) | collective-permute-done | bytes 90144 | tf_op jit(solution)/shard_map/ppermute | solution.py:34
  34.3 2.7 %collective-permute-start.10 = (bf16[176,256]{1,0:T(8,128)(2,1)S(1)}, bf16[176,256]{1,0:T(8,128)(2,1)S(1)}, u32[]{:S(2)}, u32[]{:S(2)}) collective-permute-start(bf16[176,256]{1,0:T(8,128)(2,1)S(1)} %shard_map.100.before), channel_id=1, source_target_pairs={{0,4},{1,5},{2,6},{3,7},{4,0},{5,1},{6,2},{7,3},{8,12},{9,13},{10,... | collective-permute-start | bytes 270344 | tf_op jit(solution)/shard_map/ppermute | solution.py:34
  36.9 0.0 collective-permute-done.8.come
  36.9 2.9 %collective-permute-start.11 = (bf16[176,256]{1,0:T(8,128)(2,1)S(1)}, bf16[176,256]{1,0:T(8,128)(2,1)S(1)}, u32[]{:S(2)}, u32[]{:S(2)}) collective-permute-start(bf16[176,256]{1,0:T(8,128)(2,1)S(1)} %shard_map.101.before), channel_id=1, source_target_pairs={{0,6},{1,7},{2,4},{3,5},{4,2},{5,3},{6,0},{7,1},{8,14},{9,15},{10,... | collective-permute-start | bytes 270344 | tf_op jit(solution)/shard_map/ppermute | solution.py:34
  39.9 0.0 collective-permute-done.9.come
  39.9 0.1 collective-permute-start.12
  40.0 1.6 %collective-permute-start.13 = (bf16[176,256]{1,0:T(8,128)(2,1)S(1)}, bf16[176,256]{1,0:T(8,128)(2,1)S(1)}, u32[]{:S(2)}, u32[]{:S(2)}) collective-permute-start(bf16[176,256]{1,0:T(8,128)(2,1)S(1)} %get-tuple-element.100), channel_id=1, source_target_pairs={{0,1},{1,0},{2,3},{3,2},{4,5},{5,4},{6,7},{7,6},{8,9},{9,8},{10,11... | collective-permute-start | bytes 270344 | tf_op jit(solution)/shard_map/ppermute | solution.py:34
  41.6 2.1 %shard_map.103 = (f32[192,1152]{1,0:T(8,128)S(1)}, f32[8,128]{1,0:T(8,128)S(1)}) custom-call(f32[1]{0:T(128)S(6)} %copy.10.scale, bf16[1152,1152]{1,0:T(8,128)(2,1)S(1)} %get-tuple-element.58.proj, bf16[384,1152]{1,0:T(8,128)(2,1)S(1)} %get-tuple-element.64.text_near, bf16[192,1152]{1,0:T(8,128)(2,1)S(1)} %collective-permute-done.2.text_unit.text_third, ...), custom_call_target="tpu_custom_call" | custom-call | flops 1000 | bytes 1000 | tf_op jit(solution)/shard_map/pallas_call | solution.py:138
  43.7 0.0 collective-permute-done.10.two_on
  43.7 0.1 collective-permute-done.11.three_on
  43.9 0.9 %collective-permute-done.12.next_one = bf16[176,256]{1,0:T(8,128)(2,1)S(1)} collective-permute-done((bf16[176,256]{1,0:T(8,128)(2,1)S(1)}, bf16[176,256]{1,0:T(8,128)(2,1)S(1)}, u32[]{:S(2)}, u32[]{:S(2)}) %collective-permute-start.12) | collective-permute-done | bytes 90144 | tf_op jit(solution)/shard_map/ppermute | solution.py:34
  44.8 0.0 collective-permute-done.13.come
  44.8 0.1 shard_map.106.before.refs_0_
  44.9 1.6 %collective-permute-start.14 = (bf16[176,256]{1,0:T(8,128)(2,1)S(1)}, bf16[176,256]{1,0:T(8,128)(2,1)S(1)}, u32[]{:S(2)}, u32[]{:S(2)}) collective-permute-start(bf16[176,256]{1,0:T(8,128)(2,1)S(1)} %shard_map.106.before.refs_0_), channel_id=1, source_target_pairs={{0,16},{8,24},{16,0},{24,8},{1,17},{9,25},{17,1},{25,9},{2,18},{10... | collective-permute-start | bytes 270344 | tf_op jit(solution)/shard_map/ppermute | solution.py:34
  46.5 0.0 collective-permute-start.15
  46.5 1.7 %shard_map.107 = (bf16[192,1152]{1,0:T(8,128)(2,1)}, f32[8,128]{1,0:T(8,128)S(1)}) custom-call(bf16[192,1152]{1,0:T(8,128)(2,1)S(1)} %get-tuple-element.56.features, f32[1,1152]{1,0:T(1,128)S(1)} %get-tuple-element.57.gain, f32[192,1152]{1,0:T(8,128)S(1)} %get-tuple-element.98.norm_back, bf16[176,256]{1,0:T(8,128)(2,1)S(1)} %shard_map.106.before.refs_0_), custom_call_target="tpu_custom_call" | custom-call | bytes 5308416 | tf_op jit(solution)/shard_map/pallas_call | solution.py:138
  48.2 1.2 %collective-permute-done.14.refs_2_ = bf16[176,256]{1,0:T(8,128)(2,1)S(1)} collective-permute-done((bf16[176,256]{1,0:T(8,128)(2,1)S(1)}, bf16[176,256]{1,0:T(8,128)(2,1)S(1)}, u32[]{:S(2)}, u32[]{:S(2)}) %collective-permute-start.14) | collective-permute-done | bytes 90144 | tf_op jit(solution)/shard_map/ppermute | solution.py:34
  49.5 0.0 collective-permute-start.16
  49.5 0.0 collective-permute-done.15.refs_1_
  49.5 1.3 %collective-permute-done.16.refs_3_ = bf16[176,256]{1,0:T(8,128)(2,1)S(1)} collective-permute-done((bf16[176,256]{1,0:T(8,128)(2,1)S(1)}, bf16[176,256]{1,0:T(8,128)(2,1)S(1)}, u32[]{:S(2)}, u32[]{:S(2)}) %collective-permute-start.16) | collective-permute-done | bytes 90144 | tf_op jit(solution)/shard_map/ppermute | solution.py:34
  50.8 1.0 %shard_map.108 = (f32[144,1152]{1,0:T(8,128)}, f32[1152]{0:T(1024)}) custom-call(f32[8,128]{1,0:T(8,128)S(1)} %get-tuple-element.104.before, bf16[176,256]{1,0:T(8,128)(2,1)S(1)} %shard_map.106.before.refs_0_, bf16[176,256]{1,0:T(8,128)(2,1)S(1)} %collective-permute-done.15.refs_1_, bf16[176,256]{1,0:T(8,128)(2,1)S(1)} %collective-permute-done.14.refs_2_, ...), custom_call_target="tpu_custom_call" | custom-call | bytes 1327104 | tf_op jit(solution)/shard_map/pallas_call | solution.py:138
  (8 shorter events, 0.2 us)
Async XLA Ops:
  0.6 4.4 %collective-permute-start = (bf16[192,1152]{1,0:T(8,128)(2,1)}, bf16[192,1152]{1,0:T(8,128)(2,1)S(1)}, u32[]{:S(2)}, u32[]{:S(2)}) collective-permute-start(bf16[192,1152]{1,0:T(8,128)(2,1)} %bitcast.5), channel_id=1, source_target_pairs={{0,8},{8,0},{16,24},{24,16},{1,9},{9,1},{17,25},{25,17},{2,10},{10... | collective-permute-start | bytes 1327112 | tf_op jit(solution)/shard_map/ppermute | solution.py:34
  1.2 13.5 %collective-permute-start.3 = (bf16[192,1152]{1,0:T(8,128)(2,1)}, bf16[192,1152]{1,0:T(8,128)(2,1)S(1)}, u32[]{:S(2)}, u32[]{:S(2)}) collective-permute-start(bf16[192,1152]{1,0:T(8,128)(2,1)} %bitcast.6), channel_id=1, source_target_pairs={{0,16},{8,24},{16,0},{24,8},{1,17},{9,25},{17,1},{25,9},{2,18},{10... | collective-permute-start | bytes 1327112 | tf_op jit(solution)/shard_map/ppermute | solution.py:34
  5.0 1.0 %copy-start = (bf16[192,1,1152]{2,0,1:T(8,128)(2,1)S(1)}, bf16[192,1,1152]{2,0,1:T(8,128)(2,1)}, u32[]{:S(2)}) copy-start(bf16[192,1,1152]{2,0,1:T(8,128)(2,1)} %param.7) | copy-start | bytes 1327108
  6.0 1.0 %copy-start.1 = (bf16[192,1,1152]{2,0,1:T(8,128)(2,1)S(1)}, bf16[192,1,1152]{2,0,1:T(8,128)(2,1)}, u32[]{:S(2)}) copy-start(bf16[192,1,1152]{2,0,1:T(8,128)(2,1)} %param.6) | copy-start | bytes 1327108
  7.1 0.7 %copy-start.2 = (f32[1152]{0:T(1024)S(1)}, f32[1152]{0:T(1024)}, u32[]{:S(2)}) copy-start(f32[1152]{0:T(1024)} %gain_line.1) | copy-start | bytes 13828
  12.0 3.3 %collective-permute-start.1 = (bf16[192,1152]{1,0:T(8,128)(2,1)S(1)}, bf16[192,1152]{1,0:T(8,128)(2,1)S(1)}, u32[]{:S(2)}, u32[]{:S(2)}) collective-permute-start(bf16[192,1152]{1,0:T(8,128)(2,1)S(1)} %get-tuple-element.62.text_own), channel_id=1, source_target_pairs={{0,8},{8,0},{16,24},{24,16},{1,9},{9,1},{17,25},{25,17},{2,10},{10... | collective-permute-start | bytes 1327112 | tf_op jit(solution)/shard_map/ppermute | solution.py:34
  12.2 12.4 %collective-permute-start.2 = (bf16[192,1152]{1,0:T(8,128)(2,1)S(1)}, bf16[192,1152]{1,0:T(8,128)(2,1)S(1)}, u32[]{:S(2)}, u32[]{:S(2)}) collective-permute-start(bf16[192,1152]{1,0:T(8,128)(2,1)S(1)} %get-tuple-element.62.text_own), channel_id=1, source_target_pairs={{0,16},{8,24},{16,0},{24,8},{1,17},{9,25},{17,1},{25,9},{2,18},{10... | collective-permute-start | bytes 1327112 | tf_op jit(solution)/shard_map/ppermute | solution.py:34
  14.7 2.5 %collective-permute-start.4 = (bf16[160,1152]{1,0:T(8,128)(2,1)S(1)}, bf16[160,1152]{1,0:T(8,128)(2,1)S(1)}, u32[]{:S(2)}, u32[]{:S(2)}) collective-permute-start(bf16[160,1152]{1,0:T(8,128)(2,1)S(1)} %get-tuple-element.67), channel_id=1, source_target_pairs={{0,8},{8,0},{16,24},{24,16},{1,9},{9,1},{17,25},{25,17},{2,10},{10... | collective-permute-start | bytes 1105928 | tf_op jit(solution)/shard_map/ppermute | solution.py:34
  14.8 2.4 %collective-permute-start.5 = (bf16[32,1152]{1,0:T(8,128)(2,1)S(1)}, bf16[32,1152]{1,0:T(8,128)(2,1)S(1)}, u32[]{:S(2)}, u32[]{:S(2)}) collective-permute-start(bf16[32,1152]{1,0:T(8,128)(2,1)S(1)} %get-tuple-element.68), channel_id=1, source_target_pairs={{0,8},{8,0},{16,24},{24,16},{1,9},{9,1},{17,25},{25,17},{2,10},{10... | collective-permute-start | bytes 221192 | tf_op jit(solution)/shard_map/ppermute | solution.py:34
  24.6 1.8 %collective-permute-start.6 = (bf16[192,1152]{1,0:T(8,128)(2,1)S(1)}, bf16[192,1152]{1,0:T(8,128)(2,1)S(1)}, u32[]{:S(2)}, u32[]{:S(2)}) collective-permute-start(bf16[192,1152]{1,0:T(8,128)(2,1)S(1)} %collective-permute-done.2.text_unit.text_third), channel_id=1, source_target_pairs={{0,8},{8,0},{16,24},{24,16},{1,9},{9,1},{17,25},{25,17},{2,10},{10... | collective-permute-start | bytes 1327112 | tf_op jit(solution)/shard_map/ppermute | solution.py:34
  28.7 5.5 %collective-permute-start.7 = (bf16[176,256]{1,0:T(8,128)(2,1)S(1)}, bf16[176,256]{1,0:T(8,128)(2,1)S(1)}, u32[]{:S(2)}, u32[]{:S(2)}) collective-permute-start(bf16[176,256]{1,0:T(8,128)(2,1)S(1)} %get-tuple-element.95), channel_id=1, source_target_pairs={{0,1},{1,0},{2,3},{3,2},{4,5},{5,4},{6,7},{7,6},{8,9},{9,8},{10,11... | collective-permute-start | bytes 270344 | tf_op jit(solution)/shard_map/ppermute | solution.py:34
  30.3 6.6 %collective-permute-start.8 = (bf16[176,256]{1,0:T(8,128)(2,1)S(1)}, bf16[176,256]{1,0:T(8,128)(2,1)S(1)}, u32[]{:S(2)}, u32[]{:S(2)}) collective-permute-start(bf16[176,256]{1,0:T(8,128)(2,1)S(1)} %get-tuple-element.96), channel_id=1, source_target_pairs={{0,1},{1,0},{2,3},{3,2},{4,5},{5,4},{6,7},{7,6},{8,9},{9,8},{10,11... | collective-permute-start | bytes 270344 | tf_op jit(solution)/shard_map/ppermute | solution.py:34
  30.8 9.0 %collective-permute-start.9 = (bf16[176,256]{1,0:T(8,128)(2,1)S(1)}, bf16[176,256]{1,0:T(8,128)(2,1)S(1)}, u32[]{:S(2)}, u32[]{:S(2)}) collective-permute-start(bf16[176,256]{1,0:T(8,128)(2,1)S(1)} %get-tuple-element.97), channel_id=1, source_target_pairs={{0,1},{1,0},{2,3},{3,2},{4,5},{5,4},{6,7},{7,6},{8,9},{9,8},{10,11... | collective-permute-start | bytes 270344 | tf_op jit(solution)/shard_map/ppermute | solution.py:34
  34.3 9.4 %collective-permute-start.10 = (bf16[176,256]{1,0:T(8,128)(2,1)S(1)}, bf16[176,256]{1,0:T(8,128)(2,1)S(1)}, u32[]{:S(2)}, u32[]{:S(2)}) collective-permute-start(bf16[176,256]{1,0:T(8,128)(2,1)S(1)} %shard_map.100.before), channel_id=1, source_target_pairs={{0,4},{1,5},{2,6},{3,7},{4,0},{5,1},{6,2},{7,3},{8,12},{9,13},{10,... | collective-permute-start | bytes 270344 | tf_op jit(solution)/shard_map/ppermute | solution.py:34
  36.9 6.9 %collective-permute-start.11 = (bf16[176,256]{1,0:T(8,128)(2,1)S(1)}, bf16[176,256]{1,0:T(8,128)(2,1)S(1)}, u32[]{:S(2)}, u32[]{:S(2)}) collective-permute-start(bf16[176,256]{1,0:T(8,128)(2,1)S(1)} %shard_map.101.before), channel_id=1, source_target_pairs={{0,6},{1,7},{2,4},{3,5},{4,2},{5,3},{6,0},{7,1},{8,14},{9,15},{10,... | collective-permute-start | bytes 270344 | tf_op jit(solution)/shard_map/ppermute | solution.py:34
  39.9 4.9 %collective-permute-start.12 = (bf16[176,256]{1,0:T(8,128)(2,1)S(1)}, bf16[176,256]{1,0:T(8,128)(2,1)S(1)}, u32[]{:S(2)}, u32[]{:S(2)}) collective-permute-start(bf16[176,256]{1,0:T(8,128)(2,1)S(1)} %shard_map.102.before), channel_id=1, source_target_pairs={{0,2},{1,3},{2,0},{3,1},{4,6},{5,7},{6,4},{7,5},{8,10},{9,11},{10,... | collective-permute-start | bytes 270344 | tf_op jit(solution)/shard_map/ppermute | solution.py:34
  40.0 4.8 %collective-permute-start.13 = (bf16[176,256]{1,0:T(8,128)(2,1)S(1)}, bf16[176,256]{1,0:T(8,128)(2,1)S(1)}, u32[]{:S(2)}, u32[]{:S(2)}) collective-permute-start(bf16[176,256]{1,0:T(8,128)(2,1)S(1)} %get-tuple-element.100), channel_id=1, source_target_pairs={{0,1},{1,0},{2,3},{3,2},{4,5},{5,4},{6,7},{7,6},{8,9},{9,8},{10,11... | collective-permute-start | bytes 270344 | tf_op jit(solution)/shard_map/ppermute | solution.py:34
  44.9 4.6 %collective-permute-start.14 = (bf16[176,256]{1,0:T(8,128)(2,1)S(1)}, bf16[176,256]{1,0:T(8,128)(2,1)S(1)}, u32[]{:S(2)}, u32[]{:S(2)}) collective-permute-start(bf16[176,256]{1,0:T(8,128)(2,1)S(1)} %shard_map.106.before.refs_0_), channel_id=1, source_target_pairs={{0,16},{8,24},{16,0},{24,8},{1,17},{9,25},{17,1},{25,9},{2,18},{10... | collective-permute-start | bytes 270344 | tf_op jit(solution)/shard_map/ppermute | solution.py:34
  46.5 3.0 %collective-permute-start.15 = (bf16[176,256]{1,0:T(8,128)(2,1)S(1)}, bf16[176,256]{1,0:T(8,128)(2,1)S(1)}, u32[]{:S(2)}, u32[]{:S(2)}) collective-permute-start(bf16[176,256]{1,0:T(8,128)(2,1)S(1)} %shard_map.106.before.refs_0_), channel_id=1, source_target_pairs={{0,8},{8,0},{16,24},{24,16},{1,9},{9,1},{17,25},{25,17},{2,10},{10... | collective-permute-start | bytes 270344 | tf_op jit(solution)/shard_map/ppermute | solution.py:34
  49.5 1.3 %collective-permute-start.16 = (bf16[176,256]{1,0:T(8,128)(2,1)S(1)}, bf16[176,256]{1,0:T(8,128)(2,1)S(1)}, u32[]{:S(2)}, u32[]{:S(2)}) collective-permute-start(bf16[176,256]{1,0:T(8,128)(2,1)S(1)} %collective-permute-done.14.refs_2_), channel_id=1, source_target_pairs={{0,8},{8,0},{16,24},{24,16},{1,9},{9,1},{17,25},{25,17},{2,10},{10... | collective-permute-start | bytes 270344 | tf_op jit(solution)/shard_map/ppermute | solution.py:34
